TPU v7x, 32 devices: a whole 2x2x4 slice. The times are simulated.
32 devices in a mesh: seq: 8 (over y, x, core), head: 4 (over z).
Axes of the slice: x: 2, y: 2, z: 4, core: 2. Of those that a mesh axis runs over, the one named last changes fastest.
Arguments:
- query_rows: bfloat16 [4096, 64, 128], P('seq', 'head'), may hold values from -3 to 3
- key_rows: bfloat16 [4096, 64, 128], P('seq', 'head'), may hold values from -0.59765625 to 0.59765625
- value_rows: bfloat16 [4096, 64, 128], P('seq', 'head'), may hold values from -18 to 18
- output_grad: bfloat16 [4096, 64, 128], P('seq', 'head'), may hold values from -1.796875 to 1.796875
- norm_gain: float32 [64, 128], P('head'), may hold values from 0.1 to 1.9
- log_decay: float32 [64, 4096], P('head', 'seq'), may hold values from -0.6932 to 0, as said below
Outputs:
- normed: bfloat16 [4096, 64, 128], P('seq', 'head')
- grad_q: bfloat16 [4096, 64, 128], P('seq', 'head')
- grad_k: bfloat16 [4096, 64, 128], P('seq', 'head')
- grad_v: bfloat16 [4096, 64, 128], P('seq', 'head')
Inputs may be any that keep to these rules, and one draw needn't show every extreme that they name: `log_decay`: never positive.
All inputs are finite; a program needn't handle non-finite values.
Results may differ from a plain program's by a relative error of at most 0.0051.
Values sent between devices are 32-bit elements; how exact they have to be, the bound alone decides.
No kernel may reach another device: no remote copies, remote signals or barrier semaphores. Data moves between devices by JAX's collectives and lax.ppermute only.
A program may use at most 192 MiB of HBM per device.

v0:
```python
import functools

import jax
import jax.numpy as jnp
from jax import lax
from jax.experimental import pallas as pl
from jax.experimental.pallas import tpu as pltpu
from jax.sharding import PartitionSpec as P

HEAD_TOTAL = 64
HD = 128
BLOCK = 256
GROUP = 4
STEP_TOK = 128
F32 = jnp.float32
BF16 = jnp.bfloat16
VMEM_LIMIT = 40 * 1024 * 1024


def params():
    return pltpu.CompilerParams(
        dimension_semantics=("arbitrary",), vmem_limit_bytes=VMEM_LIMIT
    )


def cost(flops, moved, exps=0):
    return pl.CostEstimate(flops=flops, bytes_accessed=moved, transcendentals=exps)


def block_cum(log_decay):
    size = log_decay.shape[1]
    upper = lax.broadcasted_iota(jnp.int32, (size, size), 0) <= lax.broadcasted_iota(
        jnp.int32, (size, size), 1
    )
    return jnp.dot(
        log_decay,
        jnp.where(upper, 1.0, 0.0).astype(F32),
        precision=lax.Precision.HIGHEST,
        preferred_element_type=F32,
    )


def as_columns(row):
    return jnp.broadcast_to(row, (HD, row.shape[1])).T


def dot(a, b):
    return jnp.dot(a, b, preferred_element_type=F32)


def dot_rows(a, b):
    return lax.dot_general(a, b, (((1,), (1,)), ((), ())), preferred_element_type=F32)


def two_parts(matrix):
    high = matrix.astype(BF16)
    return high, (matrix - high.astype(F32)).astype(BF16)


def decay_matrix(row, columns):
    size = row.shape[1]
    lower = lax.broadcasted_iota(jnp.int32, (size, size), 0) >= lax.broadcasted_iota(
        jnp.int32, (size, size), 1
    )
    both = jnp.concatenate([columns] * (size // HD), axis=1)
    return jnp.exp(jnp.where(lower, both - row, -jnp.inf))


def to_rows(dst, block):
    tok, heads, dim = block.shape
    dst[...] = block[...].astype(F32).reshape(tok * heads, dim)


def head_rows(ref, head, heads, tok):
    return ref[pl.ds(head, tok, stride=heads), :]


def state_kernel(core_ref, ld_ref, k_ref, v_ref, own_ref, send_ref, first_ref, kx, vx, cum, acc):
    heads = ld_ref.shape[0]
    step = pl.program_id(0)
    per_block = BLOCK // STEP_TOK
    half = heads // 2

    @pl.when(step == 0)
    def _():
        for b in range(2):
            cum[b] = block_cum(ld_ref[:, b * BLOCK : (b + 1) * BLOCK])
        acc[...] = jnp.zeros_like(acc)

    to_rows(kx, k_ref)
    to_rows(vx, v_ref)
    b = step // per_block
    at = pl.multiple_of((step % per_block) * STEP_TOK, STEP_TOK)
    ends = cum[b, :, BLOCK - 1 : BLOCK]
    scale = jnp.exp(ends - cum[b, :, pl.ds(at, STEP_TOK)])
    for h in range(heads):
        keys = head_rows(kx, h, heads, STEP_TOK).T * scale[h : h + 1]
        values = head_rows(vx, h, heads, STEP_TOK).astype(BF16)
        acc[b, h] += dot(keys.astype(BF16), values)

    @pl.when(step == 2 * per_block - 1)
    def _():
        first_ref[...] = acc[0]
        last = jnp.exp(cum[1, :, BLOCK - 1 : BLOCK])
        for h in range(heads):
            acc[1, h] += last[h : h + 1, :] * acc[0, h]
        core = core_ref[0]
        own_ref[...] = acc[1, pl.ds(core * half, half)]
        send_ref[...] = acc[1, pl.ds((1 - core) * half, half)]


def local_state(core, log_decay, key_rows, value_rows):
    tok, heads, dim = key_rows.shape
    half = heads // 2
    raw = pl.BlockSpec((STEP_TOK, heads, dim), lambda i: (i, 0, 0))
    whole = lambda *shape: pl.BlockSpec(shape, lambda i: (0,) * len(shape))
    return pl.pallas_call(
        state_kernel,
        grid=(tok // STEP_TOK,),
        in_specs=[pl.BlockSpec(memory_space=pltpu.SMEM), whole(heads, tok), raw, raw],
        out_specs=[whole(half, dim, dim), whole(half, dim, dim), whole(heads, dim, dim)],
        out_shape=[
            jax.ShapeDtypeStruct((half, dim, dim), F32),
            jax.ShapeDtypeStruct((half, dim, dim), F32),
            jax.ShapeDtypeStruct((heads, dim, dim), F32),
        ],
        scratch_shapes=[
            pltpu.VMEM((STEP_TOK * heads, dim), F32),
            pltpu.VMEM((STEP_TOK * heads, dim), F32),
            pltpu.VMEM((2, heads, BLOCK), F32),
            pltpu.VMEM((2, heads, dim, dim), F32),
        ],
        compiler_params=params(),
        cost_estimate=cost(2 * tok * heads * dim * dim, 4 * tok * heads * dim),
        name="local_state",
    )(core, log_decay, key_rows, value_rows)


def intra_kernel(
    second, ld_ref, q_ref, k_ref, v_ref, o_ref, first_ref,
    qh_ref, kh_ref, vh_ref, oh_ref, w_ref, inner_ref, qx, kx, vx, ox, cum,
):
    heads = ld_ref.shape[0]
    step = pl.program_id(0)

    @pl.when(step == 0)
    def _():
        cum[...] = block_cum(ld_ref[...])
        to_rows(qx, q_ref)
        to_rows(kx, k_ref)
        to_rows(vx, v_ref)
        to_rows(ox, o_ref)

    for i in range(GROUP):
        h = step * GROUP + i
        query = head_rows(qx, h, heads, BLOCK).astype(BF16)
        key = head_rows(kx, h, heads, BLOCK).astype(BF16)
        value = head_rows(vx, h, heads, BLOCK).astype(BF16)
        qh_ref[i] = query
        kh_ref[i] = key
        vh_ref[i] = value
        oh_ref[i] = head_rows(ox, h, heads, BLOCK).astype(BF16)
        row = cum[pl.ds(h, 1), :]
        columns = as_columns(row)
        weights = (dot_rows(query, key) * decay_matrix(row, columns)).astype(BF16)
        w_ref[i] = weights
        inner = dot(weights, value)
        if second:
            high, low = two_parts(first_ref[i])
            inner += jnp.exp(columns) * (dot(query, high) + dot(query, low))
        inner_ref[i] = inner


def intra(index, log_decay, query_rows, key_rows, value_rows, output_grad, first):
    tok, heads, dim = key_rows.shape
    raw = pl.BlockSpec((BLOCK, heads, dim), lambda i: (index, 0, 0))
    by_head = pl.BlockSpec((GROUP, BLOCK, dim), lambda i: (i, 0, 0))
    head_shape = jax.ShapeDtypeStruct((heads, BLOCK, dim), BF16)
    return pl.pallas_call(
        functools.partial(intra_kernel, index > 0),
        grid=(heads // GROUP,),
        in_specs=[
            pl.BlockSpec((heads, BLOCK), lambda i: (0, index)),
            raw, raw, raw, raw,
            pl.BlockSpec((GROUP, dim, dim), lambda i: (i, 0, 0)),
        ],
        out_specs=[by_head] * 4 + [pl.BlockSpec((GROUP, BLOCK, BLOCK), lambda i: (i, 0, 0)), by_head],
        out_shape=[head_shape] * 4 + [
            jax.ShapeDtypeStruct((heads, BLOCK, BLOCK), BF16),
            jax.ShapeDtypeStruct((heads, BLOCK, dim), F32),
        ],
        scratch_shapes=[pltpu.VMEM((BLOCK * heads, dim), F32)] * 4 + [pltpu.VMEM((heads, BLOCK), F32)],
        compiler_params=params(),
        cost_estimate=cost(
            2 * heads * BLOCK * BLOCK * dim * 4, 20 * heads * BLOCK * dim, heads * BLOCK * BLOCK
        ),
        name=f"intra_{index}",
    )(log_decay, query_rows, key_rows, value_rows, output_grad, first)


def whole_state(core, keep_ref, recv_ref, group, i):
    half = keep_ref.shape[0]
    head = group * GROUP + i
    mine = (head // half) == core
    return jnp.where(mine, keep_ref[head % half], recv_ref[head % half])


def attend_kernel(
    core_ref, ld_ref, gain_ref, keep_ref, recv_ref, q0, q1, o0, o1, inner0, inner1,
    att0, att1, sums_ref, cum, squares, products,
):
    step = pl.program_id(0)
    steps = pl.num_programs(0)

    @pl.when(step == 0)
    def _():
        cum[0] = block_cum(ld_ref[:, :BLOCK])
        cum[1] = cum[0, :, BLOCK - 1 : BLOCK] + block_cum(ld_ref[:, BLOCK:])
        squares[...] = jnp.zeros_like(squares)
        products[...] = jnp.zeros_like(products)

    for i in range(GROUP):
        h = step * GROUP + i
        high, low = two_parts(whole_state(core_ref[0], keep_ref, recv_ref, step, i))
        gain = gain_ref[pl.ds(h, 1), :]
        for b, (q, o, inner, att) in enumerate(((q0, o0, inner0, att0), (q1, o1, inner1, att1))):
            columns = jnp.exp(as_columns(cum[b, pl.ds(h, 1), :]))
            attended = inner[i] + columns * (dot(q[i], high) + dot(q[i], low))
            att[i] = attended
            squares[b] += attended * attended
            products[b] += gain * o[i].astype(F32) * attended

    @pl.when(step == steps - 1)
    def _():
        ones = jnp.ones((8, HD), F32)
        for b in range(2):
            for at, total in enumerate((squares, products)):
                line = lax.dot_general(
                    ones, total[b], (((1,), (1,)), ((), ())),
                    precision=lax.Precision.HIGHEST, preferred_element_type=F32,
                )
                sums_ref[at : at + 1, b * BLOCK : (b + 1) * BLOCK] = line[:1]


def attend(core, log_decay, gain, keep, recv, parts):
    heads, tok = log_decay.shape
    dim = HD
    whole = lambda *shape: pl.BlockSpec(shape, lambda i: (0,) * len(shape))
    by_head = pl.BlockSpec((GROUP, BLOCK, dim), lambda i: (i, 0, 0))
    head_shape = jax.ShapeDtypeStruct((heads, BLOCK, dim), F32)
    return pl.pallas_call(
        attend_kernel,
        grid=(heads // GROUP,),
        in_specs=[pl.BlockSpec(memory_space=pltpu.SMEM), whole(heads, tok), whole(heads, dim)]
        + [whole(heads // 2, dim, dim)] * 2 + [by_head] * 6,
        out_specs=[by_head, by_head, whole(2, tok)],
        out_shape=[head_shape, head_shape, jax.ShapeDtypeStruct((2, tok), F32)],
        scratch_shapes=[
            pltpu.VMEM((2, heads, BLOCK), F32),
            pltpu.VMEM((2, BLOCK, dim), F32),
            pltpu.VMEM((2, BLOCK, dim), F32),
        ],
        compiler_params=params(),
        cost_estimate=cost(4 * heads * tok * dim * dim, 16 * heads * tok * dim),
        name="attend",
    )(core, log_decay, gain, keep, recv, *parts)


def inverse_rms(sums_ref, b):
    at = slice(b * BLOCK, (b + 1) * BLOCK)
    inv = lax.rsqrt(sums_ref[0:1, at] / (HEAD_TOTAL * HD) + 1e-06)
    mean = sums_ref[1:2, at] * inv / (HEAD_TOTAL * HD)
    return inv, mean


def norm_grad_kernel(
    core_ref, ld_ref, gain_ref, sums_ref, q0, q1, o0, o1, att0, att1,
    g0, g1, own_ref, send_ref, second_ref, cum, scales, acc,
):
    heads = ld_ref.shape[0]
    half = heads // 2
    step = pl.program_id(0)

    @pl.when(step == 0)
    def _():
        for b in range(2):
            cum[b] = block_cum(ld_ref[:, b * BLOCK : (b + 1) * BLOCK])
            inv, mean = inverse_rms(sums_ref, b)
            scales[b, 0] = as_columns(inv)
            scales[b, 1] = as_columns(inv * inv * mean)

    for i in range(GROUP):
        h = step * GROUP + i
        gain = gain_ref[pl.ds(h, 1), :]
        ends = []
        for b, (q, o, att, g) in enumerate(((q0, o0, att0, g0), (q1, o1, att1, g1))):
            grad = gain * o[i].astype(F32) * scales[b, 0] - att[i] * scales[b, 1]
            grad = grad.astype(BF16)
            g[i] = grad
            queries = q[i].astype(F32).T * jnp.exp(cum[b, pl.ds(h, 1), :])
            ends.append(dot(queries.astype(BF16), grad))
        second_ref[i] = ends[1]
        first_decay = jnp.exp(cum[0, pl.ds(h, 1), :][:, BLOCK - 1 :])
        acc[h] = ends[0] + first_decay * ends[1]

    @pl.when(step == pl.num_programs(0) - 1)
    def _():
        core = core_ref[0]
        own_ref[...] = acc[pl.ds(core * half, half)]
        send_ref[...] = acc[pl.ds((1 - core) * half, half)]


def norm_grad(core, log_decay, gain, sums, parts):
    heads, tok = log_decay.shape
    dim = HD
    half = heads // 2
    whole = lambda *shape: pl.BlockSpec(shape, lambda i: (0,) * len(shape))
    by_head = pl.BlockSpec((GROUP, BLOCK, dim), lambda i: (i, 0, 0))
    head_shape = jax.ShapeDtypeStruct((heads, BLOCK, dim), BF16)
    return pl.pallas_call(
        norm_grad_kernel,
        grid=(heads // GROUP,),
        in_specs=[
            pl.BlockSpec(memory_space=pltpu.SMEM), whole(heads, tok), whole(heads, dim), whole(2, tok),
        ] + [by_head] * 6,
        out_specs=[
            by_head, by_head, whole(half, dim, dim), whole(half, dim, dim),
            pl.BlockSpec((GROUP, dim, dim), lambda i: (i, 0, 0)),
        ],
        out_shape=[
            head_shape, head_shape,
            jax.ShapeDtypeStruct((half, dim, dim), F32),
            jax.ShapeDtypeStruct((half, dim, dim), F32),
            jax.ShapeDtypeStruct((heads, dim, dim), F32),
        ],
        scratch_shapes=[
            pltpu.VMEM((2, heads, BLOCK), F32),
            pltpu.VMEM((2, 2, BLOCK, dim), F32),
            pltpu.VMEM((heads, dim, dim), F32),
        ],
        compiler_params=params(),
        cost_estimate=cost(2 * heads * tok * dim * dim, 14 * heads * tok * dim),
        name="norm_grad",
    )(core, log_decay, gain, sums, *parts)


def normed_kernel(gain_ref, sums_ref, att0, att1, out_ref, rows):
    heads = gain_ref.shape[0]
    b = pl.program_id(0)
    at = pl.multiple_of(b * BLOCK, BLOCK)
    inv = as_columns(lax.rsqrt(sums_ref[0:1, pl.ds(at, BLOCK)] / (HEAD_TOTAL * HD) + 1e-06))
    for index, att in enumerate((att0, att1)):

        @pl.when(b == index)
        def _():
            for h in range(heads):
                rows[pl.ds(h, BLOCK, stride=heads), :] = att[h] * inv * gain_ref[h : h + 1, :]

    out_ref[...] = rows[...].reshape(BLOCK, heads, HD).astype(BF16)


def normed_rows(gain, sums, att0, att1):
    heads, _, dim = att0.shape
    tok = 2 * BLOCK
    whole = lambda *shape: pl.BlockSpec(shape, lambda i: (0,) * len(shape))
    return pl.pallas_call(
        normed_kernel,
        grid=(2,),
        in_specs=[whole(heads, dim), whole(2, tok), whole(heads, BLOCK, dim), whole(heads, BLOCK, dim)],
        out_specs=pl.BlockSpec((BLOCK, heads, dim), lambda i: (i, 0, 0)),
        out_shape=jax.ShapeDtypeStruct((tok, heads, dim), BF16),
        scratch_shapes=[pltpu.VMEM((BLOCK * heads, dim), F32)],
        compiler_params=params(),
        cost_estimate=cost(3 * heads * tok * dim, 6 * heads * tok * dim),
        name="normed_rows",
    )(gain, sums, att0, att1)


def grad_q_kernel(
    core_ref, ld_ref, keep_ref, recv_ref, first_ref, k_ref0, k_ref1, v_ref0, v_ref1, g_ref0, g_ref1,
    out_ref, gs_ref, cum, rows,
):
    heads = ld_ref.shape[0]
    b, group = pl.program_id(0), pl.program_id(1)

    @pl.when((b == 0) & (group == 0))
    def _():
        for x in range(2):
            cum[x] = block_cum(ld_ref[:, x * BLOCK : (x + 1) * BLOCK])

    def work(second, k, v, g):
        for i in range(GROUP):
            h = group * GROUP + i
            row = cum[second, pl.ds(h, 1), :]
            columns = as_columns(row)
            scores = (dot_rows(g[i], v[i]) * decay_matrix(row, columns)).astype(BF16)
            gs_ref[0, i] = scores
            state = whole_state(core_ref[0], keep_ref, recv_ref, group, i)
            if second:
                state = jnp.exp(cum[0, pl.ds(h, 1), :][:, BLOCK - 1 :]) * state + first_ref[i]
            high, low = two_parts(state)
            grad = dot(scores, k[i]) + jnp.exp(columns) * (dot_rows(g[i], high) + dot_rows(g[i], low))
            rows[pl.ds(h, BLOCK, stride=heads), :] = grad

    @pl.when(b == 0)
    def _():
        work(0, k_ref0, v_ref0, g_ref0)

    @pl.when(b == 1)
    def _():
        work(1, k_ref1, v_ref1, g_ref1)

    @pl.when(group == pl.num_programs(1) - 1)
    def _():
        out_ref[...] = rows[...].reshape(BLOCK, heads, HD).astype(BF16)


def two_level():
    return pltpu.CompilerParams(
        dimension_semantics=("arbitrary", "arbitrary"), vmem_limit_bytes=VMEM_LIMIT
    )


def grad_query(core, log_decay, keep, recv, first, k0, k1, v0, v1, g0, g1):
    heads, tok = log_decay.shape
    dim = HD
    groups = heads // GROUP
    whole = lambda *shape: pl.BlockSpec(shape, lambda b, i: (0,) * len(shape))
    head0 = pl.BlockSpec((GROUP, BLOCK, dim), lambda b, i: (jnp.where(b == 0, i, groups - 1), 0, 0))
    head1 = pl.BlockSpec((GROUP, BLOCK, dim), lambda b, i: (jnp.where(b == 0, 0, i), 0, 0))
    return pl.pallas_call(
        grad_q_kernel,
        grid=(2, groups),
        in_specs=[
            pl.BlockSpec(memory_space=pltpu.SMEM), whole(heads, tok),
            whole(heads // 2, dim, dim), whole(heads // 2, dim, dim),
            pl.BlockSpec((GROUP, dim, dim), lambda b, i: (i, 0, 0)),
        ] + [head0, head1] * 3,
        out_specs=[
            pl.BlockSpec((BLOCK, heads, dim), lambda b, i: (b, 0, 0)),
            pl.BlockSpec((1, GROUP, BLOCK, BLOCK), lambda b, i: (b, i, 0, 0)),
        ],
        out_shape=[
            jax.ShapeDtypeStruct((tok, heads, dim), BF16),
            jax.ShapeDtypeStruct((2, heads, BLOCK, BLOCK), BF16),
        ],
        scratch_shapes=[pltpu.VMEM((2, heads, BLOCK), F32), pltpu.VMEM((BLOCK * heads, dim), F32)],
        compiler_params=two_level(),
        cost_estimate=cost(
            4 * heads * tok * dim * (BLOCK + dim), 12 * heads * tok * dim, heads * tok * BLOCK
        ),
        name="grad_query",
    )(core, log_decay, keep, recv, first, k0, k1, v0, v1, g0, g1)


def transposed_dot(a, b):
    return lax.dot_general(a, b, (((0,), (0,)), ((), ())), preferred_element_type=F32)


def grad_kv_kernel(
    ld_ref, gs_ref, w0, w1, q0, q1, k0, v0, g0, g1, second_ref, dk0, dv0, dk1, dv1, cum,
):
    group = pl.program_id(0)

    @pl.when(group == 0)
    def _():
        cum[...] = block_cum(ld_ref[...])

    for i in range(GROUP):
        h = group * GROUP + i
        row = cum[pl.ds(h, 1), :]
        columns = as_columns(jnp.exp(row[:, BLOCK - 1 :] - row))
        high, low = two_parts(second_ref[i])
        dk0[i] = transposed_dot(gs_ref[0, i], q0[i]) + columns * (
            dot_rows(v0[i], high) + dot_rows(v0[i], low)
        )
        dv0[i] = transposed_dot(w0[i], g0[i]) + columns * (dot(k0[i], high) + dot(k0[i], low))
        dk1[i] = transposed_dot(gs_ref[1, i], q1[i])
        dv1[i] = transposed_dot(w1[i], g1[i])


def grad_key_value(log_decay, gs, w0, w1, q0, q1, k0, v0, g0, g1, second):
    heads, tok = log_decay.shape
    dim = HD
    by_head = pl.BlockSpec((GROUP, BLOCK, dim), lambda i: (i, 0, 0))
    square = pl.BlockSpec((GROUP, BLOCK, BLOCK), lambda i: (i, 0, 0))
    return pl.pallas_call(
        grad_kv_kernel,
        grid=(heads // GROUP,),
        in_specs=[
            pl.BlockSpec((heads, BLOCK), lambda i: (0, 0)),
            pl.BlockSpec((2, GROUP, BLOCK, BLOCK), lambda i: (0, i, 0, 0)),
            square, square, by_head, by_head, by_head, by_head, by_head, by_head,
            pl.BlockSpec((GROUP, dim, dim), lambda i: (i, 0, 0)),
        ],
        out_specs=[by_head] * 4,
        out_shape=[jax.ShapeDtypeStruct((heads, BLOCK, dim), F32)] * 4,
        scratch_shapes=[pltpu.VMEM((heads, BLOCK), F32)],
        compiler_params=params(),
        cost_estimate=cost(4 * heads * tok * dim * (BLOCK + dim), 30 * heads * tok * dim),
        name="grad_key_value",
    )(log_decay, gs, w0, w1, q0, q1, k0, v0, g0, g1, second)


def finish_kernel(
    core_ref, ld_ref, keep_ref, recv_ref, k_ref0, k_ref1, v_ref0, v_ref1, dk0, dk1, dv0, dv1,
    out_k, out_v, cum, rows_k, rows_v,
):
    heads = ld_ref.shape[0]
    b, group = pl.program_id(0), pl.program_id(1)

    @pl.when((b == 0) & (group == 0))
    def _():
        for x in range(2):
            cum[x] = block_cum(ld_ref[:, x * BLOCK : (x + 1) * BLOCK])

    def work(second, k, v, dk, dv):
        for i in range(GROUP):
            h = group * GROUP + i
            row = cum[second, pl.ds(h, 1), :]
            left = row[:, BLOCK - 1 :] - row
            if not second:
                left = left + cum[1, pl.ds(h, 1), :][:, BLOCK - 1 :]
            columns = as_columns(jnp.exp(left))
            high, low = two_parts(whole_state(core_ref[0], keep_ref, recv_ref, group, i))
            rows_k[pl.ds(h, BLOCK, stride=heads), :] = dk[i] + columns * (
                dot_rows(v[i], high) + dot_rows(v[i], low)
            )
            rows_v[pl.ds(h, BLOCK, stride=heads), :] = dv[i] + columns * (
                dot(k[i], high) + dot(k[i], low)
            )

    @pl.when(b == 0)
    def _():
        work(0, k_ref0, v_ref0, dk0, dv0)

    @pl.when(b == 1)
    def _():
        work(1, k_ref1, v_ref1, dk1, dv1)

    @pl.when(group == pl.num_programs(1) - 1)
    def _():
        out_k[...] = rows_k[...].reshape(BLOCK, heads, HD).astype(BF16)
        out_v[...] = rows_v[...].reshape(BLOCK, heads, HD).astype(BF16)


def finish(core, log_decay, keep, recv, k0, k1, v0, v1, dk0, dk1, dv0, dv1):
    heads, tok = log_decay.shape
    dim = HD
    groups = heads // GROUP
    whole = lambda *shape: pl.BlockSpec(shape, lambda b, i: (0,) * len(shape))
    head0 = pl.BlockSpec((GROUP, BLOCK, dim), lambda b, i: (jnp.where(b == 0, i, groups - 1), 0, 0))
    head1 = pl.BlockSpec((GROUP, BLOCK, dim), lambda b, i: (jnp.where(b == 0, 0, i), 0, 0))
    raw = pl.BlockSpec((BLOCK, heads, dim), lambda b, i: (b, 0, 0))
    out = jax.ShapeDtypeStruct((tok, heads, dim), BF16)
    return pl.pallas_call(
        finish_kernel,
        grid=(2, groups),
        in_specs=[
            pl.BlockSpec(memory_space=pltpu.SMEM), whole(heads, tok),
            whole(heads // 2, dim, dim), whole(heads // 2, dim, dim),
        ] + [head0, head1] * 4,
        out_specs=[raw, raw],
        out_shape=[out, out],
        scratch_shapes=[
            pltpu.VMEM((2, heads, BLOCK), F32),
            pltpu.VMEM((BLOCK * heads, dim), F32),
            pltpu.VMEM((BLOCK * heads, dim), F32),
        ],
        compiler_params=two_level(),
        cost_estimate=cost(8 * heads * tok * dim * dim, 16 * heads * tok * dim),
        name="finish",
    )(core, log_decay, keep, recv, k0, k1, v0, v1, dk0, dk1, dv0, dv1)


def swap(value, axis, bit):
    count = lax.axis_size(axis)
    return lax.ppermute(value, axis, [(i, i ^ bit) for i in range(count)])


def quad_decays(log_total):
    partner, row_same, row_other = (swap(log_total, "seq", bit) for bit in (1, 2, 3))
    return (
        jnp.exp(log_total), jnp.exp(partner), jnp.exp(log_total + partner),
        jnp.exp(row_same + row_other),
    )


def entering_quad(own, send, decays, backward):
    mine = lax.axis_index("seq")
    core = mine % 2
    half = own.shape[0]
    quarter = half // 2
    bits = [(mine >> at) % 2 for at in range(3)]
    if backward:
        bits = [1 - bit for bit in bits]
    late, right, low = (bit == 1 for bit in bits)
    d_own, d_partner, d_chip, d_row = (
        lax.dynamic_slice_in_dim(part, core * half, half) for part in decays
    )
    one, zero = jnp.ones((quarter,), F32), jnp.zeros((quarter,), F32)
    wide = lambda scale: scale[:, None, None]
    whole_one = jnp.ones((half,), F32)

    got = swap(send, "seq", 1)
    total = wide(jnp.where(late, whole_one, d_partner)) * own + wide(
        jnp.where(late, d_own, whole_one)
    ) * got
    first_total, second_total = total[:quarter], total[quarter:]
    chip_a, chip_b = d_chip[:quarter], d_chip[quarter:]
    row_a, row_b = d_row[:quarter], d_row[quarter:]

    a1 = swap(first_total, "seq", 2)
    b1 = swap(wide(jnp.where(right, one, row_b)) * second_total, "seq", 4)
    a2 = swap(
        wide(jnp.where(right, one, row_a)) * first_total + wide(jnp.where(right, chip_a, one)) * a1,
        "seq", 4,
    )
    b2 = swap(
        wide(jnp.where(low & right, zero, one)) * second_total
        + wide(jnp.where(low, jnp.where(right, one, chip_b), zero)) * b1,
        "seq", 2,
    )
    enter_a = (
        wide(jnp.where(low, jnp.where(right, row_a, one), zero)) * a2
        + wide(jnp.where(right, one, zero)) * a1
    )
    enter_b = (
        wide(jnp.where(low, jnp.where(right, row_b, one), zero)) * b1
        + wide(jnp.where(low | right, one, zero)) * b2
    )
    enter = jnp.concatenate([enter_a, enter_b], axis=0)
    after = wide(jnp.where(late, d_partner, d_own)) * enter + jnp.where(late, got, own)
    kept = jnp.where(late, after, enter)
    sent = jnp.where(late, enter, after)
    return kept, swap(sent, "seq", 1)


def entering_any(own, send, log_total, backward):
    count, mine = lax.axis_size("seq"), lax.axis_index("seq")
    core = mine % 2
    half = own.shape[0]
    in_order = jnp.where(
        core == 0, jnp.concatenate([own, send], axis=0), jnp.concatenate([send, own], axis=0)
    )
    states = lax.all_gather(in_order, "seq")
    decays = jnp.exp(lax.all_gather(log_total, "seq"))
    place = mine
    if backward:
        states, decays, place = states[::-1], decays[::-1], count - 1 - mine

    def step(at, total):
        longer = decays[at][:, None, None] * total + states[at]
        return jnp.where(at < place, longer, total)

    total = lax.fori_loop(0, count - 1, step, jnp.zeros_like(in_order))
    kept = lax.dynamic_slice_in_dim(total, core * half, half)
    return kept, lax.dynamic_slice_in_dim(total, (1 - core) * half, half)


def sum_over_heads(value):
    count = lax.axis_size("head")
    total = value
    for shift in range(1, count):
        total = total + lax.ppermute(
            value, "head", [(i, (i + shift) % count) for i in range(count)]
        )
    return total


def on_device(query_rows, key_rows, value_rows, output_grad, norm_gain, log_decay):
    core = (lax.axis_index("seq") % 2).astype(jnp.int32).reshape(1)
    log_total = jnp.sum(log_decay, axis=1)
    if lax.axis_size("seq") == 8:
        decays = quad_decays(log_total)
        entering = lambda own, send, backward: entering_quad(own, send, decays, backward)
    else:
        entering = lambda own, send, backward: entering_any(own, send, log_total, backward)

    own, send, first = local_state(core, log_decay, key_rows, value_rows)
    keep, recv = entering(own, send, False)
    q0, k0, v0, o0, w0, inner0 = intra(
        0, log_decay, query_rows, key_rows, value_rows, output_grad, first
    )
    q1, k1, v1, o1, w1, inner1 = intra(
        1, log_decay, query_rows, key_rows, value_rows, output_grad, first
    )
    att0, att1, sums = attend(
        core, log_decay, norm_gain, keep, recv, (q0, q1, o0, o1, inner0, inner1)
    )
    sums = sum_over_heads(sums)
    g0, g1, grad_own, grad_send, second = norm_grad(
        core, log_decay, norm_gain, sums, (q0, q1, o0, o1, att0, att1)
    )
    grad_keep, grad_recv = entering(grad_own, grad_send, True)
    normed = normed_rows(norm_gain, sums, att0, att1)
    grad_q, scores = grad_query(core, log_decay, keep, recv, first, k0, k1, v0, v1, g0, g1)
    dk0, dv0, dk1, dv1 = grad_key_value(
        log_decay, scores, w0, w1, q0, q1, k0, v0, g0, g1, second
    )
    grad_k, grad_v = finish(
        core, log_decay, grad_keep, grad_recv, k0, k1, v0, v1, dk0, dk1, dv0, dv1
    )
    return normed, grad_q, grad_k, grad_v


def solution(mesh):
    rows = P("seq", "head", None)
    return jax.shard_map(
        on_device,
        mesh=mesh,
        in_specs=(rows, rows, rows, rows, P("head", None), P("head", "seq")),
        out_specs=(rows, rows, rows, rows),
        check_vma=False,
    )
```

profile of v0, /device:TPU:0, one launch (start us, length us, event | category | flops | bytes accessed | tf_op | source)
XLA Modules:
  0.0 136.6 jit_solution(17439938055013457714)
XLA Ops:
  2.0 2.6 %collective-permute-start.1 = (f32[16]{0:T(128)S(1)}, f32[16]{0:T(128)S(1)}, u32[]{:S(2)}, u32[]{:S(2)}) collective-permute-start(f32[16]{0:T(128)S(1)} %reduce_sum.9), channel_id=1, source_target_pairs={{0,8},{4,12},{8,0},{12,4},{16,24},{20,28},{24,16},{28,20},{1,9},{5... | collective-permute-start | bytes 200 | tf_op jit(solution)/shard_map/ppermute | solution.py:578
  4.7 1.6 %copy-done = bf16[512,16,128]{2,1,0:T(8,128)(2,1)S(1)} copy-done((bf16[512,16,128]{2,1,0:T(8,128)(2,1)S(1)}, bf16[512,16,128]{2,1,0:T(8,128)(2,1)}, u32[]{:S(2)}) %copy-start) | copy-done | bytes 2097176
  6.2 1.6 %copy-done.2 = bf16[512,16,128]{2,1,0:T(8,128)(2,1)S(1)} copy-done((bf16[512,16,128]{2,1,0:T(8,128)(2,1)S(1)}, bf16[512,16,128]{2,1,0:T(8,128)(2,1)}, u32[]{:S(2)}) %copy-start.2) | copy-done | bytes 2097176
  8.6 4.5 %local_state.1 = (f32[8,128,128]{2,1,0:T(8,128)S(1)}, f32[8,128,128]{2,1,0:T(8,128)S(1)}, f32[16,128,128]{2,1,0:T(8,128)S(1)}) custom-call(s32[1]{0:T(128)} %bitcast.core_ref, f32[16,512]{1,0:T(8,128)S(1)} %copy-done.23, bf16[512,16,128]{2,1,0:T(8,128)(2,1)S(1)} %copy-done, bf16[512,16,128]{2,1,0:T(8,128)(2,1)S(1)} %copy-done.2), custom_call_target="tpu_custom_call" | custom-call | flops 268435456 | bytes 4194304 | tf_op jit(solution)/shard_map/local_state/pallas_call | solution.py:117
  13.6 1.5 %collective-permute-done.3 = f32[8,128,128]{2,1,0:T(8,128)S(1)} collective-permute-done((f32[8,128,128]{2,1,0:T(8,128)S(1)}, f32[8,128,128]{2,1,0:T(8,128)S(1)}, u32[]{:S(2)}, u32[]{:S(2)}) %collective-permute-start.3) | collective-permute-done | bytes 524320 | tf_op jit(solution)/shard_map/ppermute | solution.py:578
  15.9 1.7 %collective-permute-start.4 = (f32[4,128,128]{2,1,0:T(8,128)}, f32[4,128,128]{2,1,0:T(8,128)S(1)}, u32[]{:S(2)}, u32[]{:S(2)}) collective-permute-start(f32[4,128,128]{2,1,0:T(8,128)} %get-tuple-element.79), channel_id=1, source_target_pairs={{0,8},{4,12},{8,0},{12,4},{16,24},{20,28},{24,16},{28,20},{1,9},{5... | collective-permute-start | bytes 786440 | tf_op jit(solution)/shard_map/ppermute | solution.py:578
  17.6 1.5 %collective-permute-start.6 = (f32[4,128,128]{2,1,0:T(8,128)S(1)}, f32[4,128,128]{2,1,0:T(8,128)S(1)}, u32[]{:S(2)}, u32[]{:S(2)}) collective-permute-start(f32[4,128,128]{2,1,0:T(8,128)S(1)} %get-tuple-element.80), channel_id=1, source_target_pairs={{0,16},{4,20},{8,24},{12,28},{16,0},{20,4},{24,8},{28,12},{1,17},{... | collective-permute-start | bytes 786440 | tf_op jit(solution)/shard_map/ppermute | solution.py:578
  19.3 5.4 %collective-permute-done.4 = f32[4,128,128]{2,1,0:T(8,128)S(1)} collective-permute-done((f32[4,128,128]{2,1,0:T(8,128)}, f32[4,128,128]{2,1,0:T(8,128)S(1)}, u32[]{:S(2)}, u32[]{:S(2)}) %collective-permute-start.4) | collective-permute-done | bytes 262176 | tf_op jit(solution)/shard_map/ppermute | solution.py:578
  27.2 1.6 %collective-permute-start.5 = (f32[4,128,128]{2,1,0:T(8,128)S(1)}, f32[4,128,128]{2,1,0:T(8,128)S(1)}, u32[]{:S(2)}, u32[]{:S(2)}) collective-permute-start(f32[4,128,128]{2,1,0:T(8,128)S(1)} %get-tuple-element.77), channel_id=1, source_target_pairs={{0,16},{4,20},{8,24},{12,28},{16,0},{20,4},{24,8},{28,12},{1,17},{... | collective-permute-start | bytes 786440 | tf_op jit(solution)/shard_map/ppermute | solution.py:578
  28.8 5.6 %collective-permute-done.7 = f32[4,128,128]{2,1,0:T(8,128)S(1)} collective-permute-done((f32[4,128,128]{2,1,0:T(8,128)}, f32[4,128,128]{2,1,0:T(8,128)S(1)}, u32[]{:S(2)}, u32[]{:S(2)}) %collective-permute-start.7) | collective-permute-done | bytes 262176 | tf_op jit(solution)/shard_map/ppermute | solution.py:578
  36.8 6.7 %intra_0.1 = (bf16[16,256,128]{2,1,0:T(8,128)(2,1)S(1)}, bf16[16,256,128]{2,1,0:T(8,128)(2,1)S(1)}, bf16[16,256,128]{2,1,0:T(8,128)(2,1)S(1)}, bf16[16,256,128]{...) custom-call(f32[16,512]{1,0:T(8,128)S(1)} %copy-done.24, ...), custom_call_target="tpu_custom_call" | custom-call | flops 1073741824 | bytes 10485760 | tf_op jit(solution)/shard_map/intra_0/pallas_call | solution.py:179
  43.5 1.4 copy-done.25
  44.8 7.8 %intra_1.1 = (bf16[16,256,128]{2,1,0:T(8,128)(2,1)S(1)}, bf16[16,256,128]{2,1,0:T(8,128)(2,1)S(1)}, bf16[16,256,128]{2,1,0:T(8,128)(2,1)S(1)}, bf16[16,256,128]{...) custom-call(f32[16,512]{1,0:T(8,128)S(1)} %copy-done.24, ...), custom_call_target="tpu_custom_call" | custom-call | flops 1073741824 | bytes 10485760 | tf_op jit(solution)/shard_map/intra_1/pallas_call | solution.py:179
  54.7 1.4 %copy-done.26 = bf16[16,256,256]{2,1,0:T(8,128)(2,1)} copy-done((bf16[16,256,256]{2,1,0:T(8,128)(2,1)}, bf16[16,256,256]{2,1,0:T(8,128)(2,1)S(1)}, u32[]{:S(2)}) %copy-start.26) | copy-done | bytes 2097176
  56.1 3.2 %attend.1 = (f32[16,256,128]{2,1,0:T(8,128)S(1)}, f32[16,256,128]{2,1,0:T(8,128)S(1)}, f32[2,512]{1,0:T(2,128)S(1)}) custom-call(s32[1]{0:T(128)} %bitcast.core_ref, f32[16,512]{1,0:T(8,128)S(1)} %copy-done.24, f32[16,128]{1,0:T(8,128)S(1)} %copy-done.32, f32[8,128,128]{2,1,0:T(8,128)S(1)} %get-tuple-element.72.keep_ref, ...), custom_call_target="tpu_custom_call" | custom-call | flops 536870912 | bytes 16777216 | tf_op jit(solution)/shard_map/attend/pallas_call | solution.py:251
  59.3 3.7 %collective-permute-start.11 = (f32[2,512]{1,0:T(2,128)S(1)}, f32[2,512]{1,0:T(2,128)S(1)}, u32[]{:S(2)}, u32[]{:S(2)}) collective-permute-start(f32[2,512]{1,0:T(2,128)S(1)} %get-tuple-element.44), channel_id=1, source_target_pairs={{0,3},{1,0},{2,1},{3,2},{4,7},{5,4},{6,5},{7,6},{8,11},{9,8},{10,9... | collective-permute-start | bytes 12296 | tf_op jit(solution)/shard_map/ppermute | solution.py:665
  64.3 3.2 %collective-permute-done.10 = f32[2,512]{1,0:T(2,128)S(1)} collective-permute-done((f32[2,512]{1,0:T(2,128)S(1)}, f32[2,512]{1,0:T(2,128)S(1)}, u32[]{:S(2)}, u32[]{:S(2)}) %collective-permute-start.10) | collective-permute-done | bytes 4128 | tf_op jit(solution)/shard_map/ppermute | solution.py:665
  68.4 3.4 %norm_grad.1 = (bf16[16,256,128]{2,1,0:T(8,128)(2,1)S(1)}, bf16[16,256,128]{2,1,0:T(8,128)(2,1)S(1)}, f32[8,128,128]{2,1,0:T(8,128)}, f32[8,128,128]{2,1,0:T(8,128)S(1)}, f32[16,128,128]{2,1,0:T(8,128)S(1)}) custom-call(s32[1]{0:T(128)} %bitcast.core_ref, f32[16,512]{1,0:T(8,128)S(1)} %copy-done.24, f32[16,128]{1,0:T(8,128)S(1)} %copy-done.32, ...), custom_call_target="tpu_custom_call" | custom-call | flops 268435456 | bytes 14680064 | tf_op jit(solution)/shard_map/norm_grad/pallas_call | solution.py:320
  74.8 1.9 %collective-permute-done.12 = f32[8,128,128]{2,1,0:T(8,128)S(1)} collective-permute-done((f32[8,128,128]{2,1,0:T(8,128)S(1)}, f32[8,128,128]{2,1,0:T(8,128)S(1)}, u32[]{:S(2)}, u32[]{:S(2)}) %collective-permute-start.12) | collective-permute-done | bytes 524320 | tf_op jit(solution)/shard_map/ppermute | solution.py:578
  77.5 2.0 %multiply_add_fusion = f32[8,128,128]{2,1,0:T(8,128)} fusion(f32[8,128,128]{2,1,0:T(8,128)S(1)} %collective-permute-done.12, f32[8,128,128]{2,1,0:T(8,128)} %get-tuple-element.54, f32[8]{0:T(128)S(1)} %get-tuple-element.96, f32[8]{0:T(128)S(1)} %get-tuple-element.93), kind=kLoop, calls=%fused_computation.3 | loop fusion | flops 393216 | bytes 1572928 | tf_op jit(solution)/shard_map/add | solution.py:606
  79.5 1.9 %fusion.4 = (f32[4,128,128]{2,1,0:T(8,128)}, f32[4,128,128]{2,1,0:T(8,128)}) fusion(f32[8,128,128]{2,1,0:T(8,128)} %multiply_add_fusion, f32[4]{0:T(128)S(1)} %get-tuple-element.87), kind=kLoop, calls=%fused_computation.47 | loop fusion | flops 65536 | bytes 1048592 | tf_op jit(solution)/shard_map/slice | solution.py:609
  82.2 1.5 %collective-permute-start.15 = (f32[4,128,128]{2,1,0:T(8,128)}, f32[4,128,128]{2,1,0:T(8,128)}, u32[]{:S(2)}, u32[]{:S(2)}) collective-permute-start(f32[4,128,128]{2,1,0:T(8,128)} %get-tuple-element.76), channel_id=1, source_target_pairs={{0,16},{4,20},{8,24},{12,28},{16,0},{20,4},{24,8},{28,12},{1,17},{... | collective-permute-start | bytes 786440 | tf_op jit(solution)/shard_map/ppermute | solution.py:578
  83.7 6.2 %collective-permute-done.13 = f32[4,128,128]{2,1,0:T(8,128)S(1)} collective-permute-done((f32[4,128,128]{2,1,0:T(8,128)}, f32[4,128,128]{2,1,0:T(8,128)S(1)}, u32[]{:S(2)}, u32[]{:S(2)}) %collective-permute-start.13) | collective-permute-done | bytes 262176 | tf_op jit(solution)/shard_map/ppermute | solution.py:578
  90.5 2.0 %multiply_add_fusion.5 = (f32[4,128,128]{2,1,0:T(8,128)}, f32[4,128,128]{2,1,0:T(8,128)}) fusion(f32[4,128,128]{2,1,0:T(8,128)S(1)} %collective-permute-done.13, f32[4]{0:T(128)S(1)} %get-tuple-element.89, f32[4]{0:T(128)S(1)} %get-tuple-element.86, f32[8,128,128]{2,1,0:T(8,128)} %multiply_add_fusion, f32[4,128,128]{2,1,0:T(8,128)} %collective-permute-done.15, ...), kind=kLoop, calls=%fused_computation.13 | loop fusion | flops 393216 | bytes 1572916 | tf_op jit(solution)/shard_map/add | solution.py:616
  93.8 1.5 %collective-permute-start.14 = (f32[4,128,128]{2,1,0:T(8,128)}, f32[4,128,128]{2,1,0:T(8,128)}, u32[]{:S(2)}, u32[]{:S(2)}) collective-permute-start(f32[4,128,128]{2,1,0:T(8,128)} %get-tuple-element.73), channel_id=1, source_target_pairs={{0,16},{4,20},{8,24},{12,28},{16,0},{20,4},{24,8},{28,12},{1,17},{... | collective-permute-start | bytes 786440 | tf_op jit(solution)/shard_map/ppermute | solution.py:578
  95.3 4.8 %collective-permute-done.16 = f32[4,128,128]{2,1,0:T(8,128)} collective-permute-done((f32[4,128,128]{2,1,0:T(8,128)}, f32[4,128,128]{2,1,0:T(8,128)}, u32[]{:S(2)}, u32[]{:S(2)}) %collective-permute-start.16) | collective-permute-done | bytes 262176 | tf_op jit(solution)/shard_map/ppermute | solution.py:578
  103.9 3.7 %normed_rows.1 = bf16[512,16,128]{2,1,0:T(8,128)(2,1)} custom-call(f32[16,128]{1,0:T(8,128)S(1)} %copy-done.32, f32[2,512]{1,0:T(2,128)S(1)} %add_add_fusion.sums_ref, f32[16,256,128]{2,1,0:T(8,128)S(1)} %copy-done.8, f32[16,256,128]{2,1,0:T(8,128)S(1)} %copy-done.10), custom_call_target="tpu_custom_call" | custom-call | flops 3145728 | bytes 6291456 | tf_op jit(solution)/shard_map/normed_rows/pallas_call | solution.py:366
  107.7 8.8 %grad_query.1 = (bf16[512,16,128]{2,1,0:T(8,128)(2,1)}, bf16[2,16,256,256]{3,2,1,0:T(8,128)(2,1)S(1)}) custom-call(s32[1]{0:T(128)} %bitcast.core_ref, f32[16,512]{1,0:T(8,128)S(1)} %copy-done.24, f32[8,128,128]{2,1,0:T(8,128)S(1)} %copy-done.13, f32[8,128,128]{2,1,0:T(8,128)S(1)} %copy-done.28, f32[16,128,128]{2,1,0:T(8,128)S(1)} %get-tuple-element.37.first_ref, ...), custom_call_target="tpu_custom_call" | custom-call | flops 1610612736 | bytes 12582912 | tf_op jit(solution)/shard_map/grad_query/pallas_call | solution.py:431
  116.4 2.0 %copy-done.14 = bf16[2,16,256,256]{3,2,1,0:T(8,128)(2,1)} copy-done((bf16[2,16,256,256]{3,2,1,0:T(8,128)(2,1)}, bf16[2,16,256,256]{3,2,1,0:T(8,128)(2,1)S(1)}, u32[]{:S(2)}) %copy-start.14) | copy-done | bytes 4194328
  118.4 7.5 %grad_key_value.1 = (f32[16,256,128]{2,1,0:T(8,128)S(1)}, f32[16,256,128]{2,1,0:T(8,128)S(1)}, f32[16,256,128]{2,1,0:T(8,128)S(1)}, f32[16,256,128]{2,1,0:T(8,128)}) custom-call(f32[16,512]{1,0:T(8,128)S(1)} %copy-done.24, bf16[2,16,256,256]{3,2,1,0:T(8,128)(2,1)} %copy-done.14, bf16[16,256,256]{2,1,0:T(8,128)(2,1)} %copy-done.25, ...), custom_call_target="tpu_custom_call" | custom-call | flops 1610612736 | bytes 31457280 | tf_op jit(solution)/shard_map/grad_key_value/pallas_call | solution.py:487
  126.0 1.6 %copy-done.29 = f32[16,256,128]{2,1,0:T(8,128)S(1)} copy-done((f32[16,256,128]{2,1,0:T(8,128)S(1)}, f32[16,256,128]{2,1,0:T(8,128)}, u32[]{:S(2)}) %copy-start.29) | copy-done | bytes 2097176
  127.5 9.1 %finish.1 = (bf16[512,16,128]{2,1,0:T(8,128)(2,1)}, bf16[512,16,128]{2,1,0:T(8,128)(2,1)}) custom-call(s32[1]{0:T(128)} %bitcast.core_ref, f32[16,512]{1,0:T(8,128)S(1)} %copy-done.24, f32[8,128,128]{2,1,0:T(8,128)S(1)} %get-tuple-element.70.keep_ref, f32[8,128,128]{2,1,0:T(8,128)S(1)} %collective-permute-done.17.recv_ref, ...), custom_call_target="tpu_custom_call" | custom-call | flops 1073741824 | bytes 16777216 | tf_op jit(solution)/shard_map/finish/pallas_call | solution.py:556
  (103 shorter events, 23.1 us)
Async XLA Ops:
  1.5 11.9 %collective-permute-start = (f32[16]{0:T(128)S(1)}, f32[16]{0:T(128)S(1)}, u32[]{:S(2)}, u32[]{:S(2)}) collective-permute-start(f32[16]{0:T(128)S(1)} %reduce_sum.9), channel_id=1, source_target_pairs={{0,4},{4,0},{8,12},{12,8},{16,20},{20,16},{24,28},{28,24},{1,5},{5... | collective-permute-start | bytes 200 | tf_op jit(solution)/shard_map/ppermute | solution.py:578
  2.0 11.3 %collective-permute-start.1 = (f32[16]{0:T(128)S(1)}, f32[16]{0:T(128)S(1)}, u32[]{:S(2)}, u32[]{:S(2)}) collective-permute-start(f32[16]{0:T(128)S(1)} %reduce_sum.9), channel_id=1, source_target_pairs={{0,8},{4,12},{8,0},{12,4},{16,24},{20,28},{24,16},{28,20},{1,9},{5... | collective-permute-start | bytes 200 | tf_op jit(solution)/shard_map/ppermute | solution.py:578
  4.6 8.7 %collective-permute-start.2 = (f32[16]{0:T(128)S(1)}, f32[16]{0:T(128)S(1)}, u32[]{:S(2)}, u32[]{:S(2)}) collective-permute-start(f32[16]{0:T(128)S(1)} %reduce_sum.9), channel_id=1, source_target_pairs={{0,12},{4,8},{8,4},{12,0},{16,28},{20,24},{24,20},{28,16},{1,13},{... | collective-permute-start | bytes 200 | tf_op jit(solution)/shard_map/ppermute | solution.py:578
  13.1 2.0 %collective-permute-start.3 = (f32[8,128,128]{2,1,0:T(8,128)S(1)}, f32[8,128,128]{2,1,0:T(8,128)S(1)}, u32[]{:S(2)}, u32[]{:S(2)}) collective-permute-start(f32[8,128,128]{2,1,0:T(8,128)S(1)} %get-tuple-element.36), channel_id=1, source_target_pairs={{0,4},{4,0},{8,12},{12,8},{16,20},{20,16},{24,28},{28,24},{1,5},{5... | collective-permute-start | bytes 1572872 | tf_op jit(solution)/shard_map/ppermute | solution.py:578
  15.9 8.7 %collective-permute-start.4 = (f32[4,128,128]{2,1,0:T(8,128)}, f32[4,128,128]{2,1,0:T(8,128)S(1)}, u32[]{:S(2)}, u32[]{:S(2)}) collective-permute-start(f32[4,128,128]{2,1,0:T(8,128)} %get-tuple-element.79), channel_id=1, source_target_pairs={{0,8},{4,12},{8,0},{12,4},{16,24},{20,28},{24,16},{28,20},{1,9},{5... | collective-permute-start | bytes 786440 | tf_op jit(solution)/shard_map/ppermute | solution.py:578
  17.6 8.3 %collective-permute-start.6 = (f32[4,128,128]{2,1,0:T(8,128)S(1)}, f32[4,128,128]{2,1,0:T(8,128)S(1)}, u32[]{:S(2)}, u32[]{:S(2)}) collective-permute-start(f32[4,128,128]{2,1,0:T(8,128)S(1)} %get-tuple-element.80), channel_id=1, source_target_pairs={{0,16},{4,20},{8,24},{12,28},{16,0},{20,4},{24,8},{28,12},{1,17},{... | collective-permute-start | bytes 786440 | tf_op jit(solution)/shard_map/ppermute | solution.py:578
  25.9 9.1 %copy-start.24 = (f32[16,512]{1,0:T(8,128)S(1)}, f32[16,512]{1,0:T(8,128)}, u32[]{:S(2)}) copy-start(f32[16,512]{1,0:T(8,128)} %ld_ref.15) | copy-start | bytes 98308
  26.7 7.6 %collective-permute-start.7 = (f32[4,128,128]{2,1,0:T(8,128)}, f32[4,128,128]{2,1,0:T(8,128)S(1)}, u32[]{:S(2)}, u32[]{:S(2)}) collective-permute-start(f32[4,128,128]{2,1,0:T(8,128)} %get-tuple-element.78), channel_id=1, source_target_pairs={{0,8},{4,12},{8,0},{12,4},{16,24},{20,28},{24,16},{28,20},{1,9},{5... | collective-permute-start | bytes 786440 | tf_op jit(solution)/shard_map/ppermute | solution.py:578
  27.2 7.5 %collective-permute-start.5 = (f32[4,128,128]{2,1,0:T(8,128)S(1)}, f32[4,128,128]{2,1,0:T(8,128)S(1)}, u32[]{:S(2)}, u32[]{:S(2)}) collective-permute-start(f32[4,128,128]{2,1,0:T(8,128)S(1)} %get-tuple-element.77), channel_id=1, source_target_pairs={{0,16},{4,20},{8,24},{12,28},{16,0},{20,4},{24,8},{28,12},{1,17},{... | collective-permute-start | bytes 786440 | tf_op jit(solution)/shard_map/ppermute | solution.py:578
  35.0 21.1 %copy-start.12 = (f32[8,128,128]{2,1,0:T(8,128)}, f32[8,128,128]{2,1,0:T(8,128)S(1)}, u32[]{:S(2)}) copy-start(f32[8,128,128]{2,1,0:T(8,128)S(1)} %get-tuple-element.72.keep_ref) | copy-start | bytes 1572868
  35.0 21.1 %collective-permute-start.8 = (f32[8,128,128]{2,1,0:T(8,128)S(1)}, f32[8,128,128]{2,1,0:T(8,128)S(1)}, u32[]{:S(2)}, u32[]{:S(2)}) collective-permute-start(f32[8,128,128]{2,1,0:T(8,128)S(1)} %get-tuple-element.71), channel_id=1, source_target_pairs={{0,4},{4,0},{8,12},{12,8},{16,20},{20,16},{24,28},{28,24},{1,5},{5... | collective-permute-start | bytes 1572872 | tf_op jit(solution)/shard_map/ppermute | solution.py:578
  44.8 23.6 %copy-start.3 = (bf16[16,256,128]{2,1,0:T(8,128)(2,1)}, bf16[16,256,128]{2,1,0:T(8,128)(2,1)S(1)}, u32[]{:S(2)}) copy-start(bf16[16,256,128]{2,1,0:T(8,128)(2,1)S(1)} %get-tuple-element.38.q0) | copy-start | bytes 3145732
  44.8 11.2 %copy-start.32 = (f32[16,128]{1,0:T(8,128)S(1)}, f32[16,128]{1,0:T(8,128)}, u32[]{:S(2)}) copy-start(f32[16,128]{1,0:T(8,128)} %gain_ref.5) | copy-start | bytes 24580
  56.0 12.4 %copy-start.5 = (bf16[16,256,128]{2,1,0:T(8,128)(2,1)}, bf16[16,256,128]{2,1,0:T(8,128)(2,1)S(1)}, u32[]{:S(2)}) copy-start(bf16[16,256,128]{2,1,0:T(8,128)(2,1)S(1)} %get-tuple-element.39.q1) | copy-start | bytes 3145732
  59.3 12.5 %copy-start.7 = (f32[16,256,128]{2,1,0:T(8,128)}, f32[16,256,128]{2,1,0:T(8,128)S(1)}, u32[]{:S(2)}) copy-start(f32[16,256,128]{2,1,0:T(8,128)S(1)} %get-tuple-element.45.att0) | copy-start | bytes 6291460
  59.3 12.5 %copy-start.9 = (f32[16,256,128]{2,1,0:T(8,128)}, f32[16,256,128]{2,1,0:T(8,128)S(1)}, u32[]{:S(2)}) copy-start(f32[16,256,128]{2,1,0:T(8,128)S(1)} %get-tuple-element.46.att1) | copy-start | bytes 6291460
  59.3 5.0 %collective-permute-start.11 = (f32[2,512]{1,0:T(2,128)S(1)}, f32[2,512]{1,0:T(2,128)S(1)}, u32[]{:S(2)}, u32[]{:S(2)}) collective-permute-start(f32[2,512]{1,0:T(2,128)S(1)} %get-tuple-element.44), channel_id=1, source_target_pairs={{0,3},{1,0},{2,1},{3,2},{4,7},{5,4},{6,5},{7,6},{8,11},{9,8},{10,9... | collective-permute-start | bytes 12296 | tf_op jit(solution)/shard_map/ppermute | solution.py:665
  63.0 4.5 %collective-permute-start.10 = (f32[2,512]{1,0:T(2,128)S(1)}, f32[2,512]{1,0:T(2,128)S(1)}, u32[]{:S(2)}, u32[]{:S(2)}) collective-permute-start(f32[2,512]{1,0:T(2,128)S(1)} %get-tuple-element.44), channel_id=1, source_target_pairs={{0,2},{1,3},{2,0},{3,1},{4,6},{5,7},{6,4},{7,5},{8,10},{9,11},{10,... | collective-permute-start | bytes 12296 | tf_op jit(solution)/shard_map/ppermute | solution.py:665
  63.0 5.4 %collective-permute-start.9 = (f32[2,512]{1,0:T(2,128)S(1)}, f32[2,512]{1,0:T(2,128)S(1)}, u32[]{:S(2)}, u32[]{:S(2)}) collective-permute-start(f32[2,512]{1,0:T(2,128)S(1)} %get-tuple-element.44), channel_id=1, source_target_pairs={{0,1},{1,2},{2,3},{3,0},{4,5},{5,6},{6,7},{7,4},{8,9},{9,10},{10,1... | collective-permute-start | bytes 12296 | tf_op jit(solution)/shard_map/ppermute | solution.py:665
  74.8 1.9 %collective-permute-start.12 = (f32[8,128,128]{2,1,0:T(8,128)S(1)}, f32[8,128,128]{2,1,0:T(8,128)S(1)}, u32[]{:S(2)}, u32[]{:S(2)}) collective-permute-start(f32[8,128,128]{2,1,0:T(8,128)S(1)} %get-tuple-element.55), channel_id=1, source_target_pairs={{0,4},{4,0},{8,12},{12,8},{16,20},{20,16},{24,28},{28,24},{1,5},{5... | collective-permute-start | bytes 1572872 | tf_op jit(solution)/shard_map/ppermute | solution.py:578
  81.3 8.6 %collective-permute-start.13 = (f32[4,128,128]{2,1,0:T(8,128)}, f32[4,128,128]{2,1,0:T(8,128)S(1)}, u32[]{:S(2)}, u32[]{:S(2)}) collective-permute-start(f32[4,128,128]{2,1,0:T(8,128)} %get-tuple-element.75), channel_id=1, source_target_pairs={{0,8},{4,12},{8,0},{12,4},{16,24},{20,28},{24,16},{28,20},{1,9},{5... | collective-permute-start | bytes 786440 | tf_op jit(solution)/shard_map/ppermute | solution.py:578
  82.2 8.4 %collective-permute-start.15 = (f32[4,128,128]{2,1,0:T(8,128)}, f32[4,128,128]{2,1,0:T(8,128)}, u32[]{:S(2)}, u32[]{:S(2)}) collective-permute-start(f32[4,128,128]{2,1,0:T(8,128)} %get-tuple-element.76), channel_id=1, source_target_pairs={{0,16},{4,20},{8,24},{12,28},{16,0},{20,4},{24,8},{28,12},{1,17},{... | collective-permute-start | bytes 786440 | tf_op jit(solution)/shard_map/ppermute | solution.py:578
  92.6 7.5 %collective-permute-start.16 = (f32[4,128,128]{2,1,0:T(8,128)}, f32[4,128,128]{2,1,0:T(8,128)}, u32[]{:S(2)}, u32[]{:S(2)}) collective-permute-start(f32[4,128,128]{2,1,0:T(8,128)} %get-tuple-element.74), channel_id=1, source_target_pairs={{0,8},{4,12},{8,0},{12,4},{16,24},{20,28},{24,16},{28,20},{1,9},{5... | collective-permute-start | bytes 786440 | tf_op jit(solution)/shard_map/ppermute | solution.py:578
  93.8 7.6 %collective-permute-start.14 = (f32[4,128,128]{2,1,0:T(8,128)}, f32[4,128,128]{2,1,0:T(8,128)}, u32[]{:S(2)}, u32[]{:S(2)}) collective-permute-start(f32[4,128,128]{2,1,0:T(8,128)} %get-tuple-element.73), channel_id=1, source_target_pairs={{0,16},{4,20},{8,24},{12,28},{16,0},{20,4},{24,8},{28,12},{1,17},{... | collective-permute-start | bytes 786440 | tf_op jit(solution)/shard_map/ppermute | solution.py:578
  100.1 3.8 %copy-start.8 = (f32[16,256,128]{2,1,0:T(8,128)S(1)}, f32[16,256,128]{2,1,0:T(8,128)}, u32[]{:S(2)}) copy-start(f32[16,256,128]{2,1,0:T(8,128)} %copy-done.7) | copy-start | bytes 6291460
  100.1 3.8 %copy-start.10 = (f32[16,256,128]{2,1,0:T(8,128)S(1)}, f32[16,256,128]{2,1,0:T(8,128)}, u32[]{:S(2)}) copy-start(f32[16,256,128]{2,1,0:T(8,128)} %copy-done.9) | copy-start | bytes 6291460
  103.8 3.8 %copy-start.13 = (f32[8,128,128]{2,1,0:T(8,128)S(1)}, f32[8,128,128]{2,1,0:T(8,128)}, u32[]{:S(2)}) copy-start(f32[8,128,128]{2,1,0:T(8,128)} %copy-done.12) | copy-start | bytes 1572868
  103.8 3.8 %copy-start.16 = (bf16[16,256,128]{2,1,0:T(8,128)(2,1)S(1)}, bf16[16,256,128]{2,1,0:T(8,128)(2,1)}, u32[]{:S(2)}) copy-start(bf16[16,256,128]{2,1,0:T(8,128)(2,1)} %copy-done.15) | copy-start | bytes 3145732
  103.8 22.1 %collective-permute-start.17 = (f32[8,128,128]{2,1,0:T(8,128)S(1)}, f32[8,128,128]{2,1,0:T(8,128)S(1)}, u32[]{:S(2)}, u32[]{:S(2)}) collective-permute-start(f32[8,128,128]{2,1,0:T(8,128)S(1)} %get-tuple-element.69), channel_id=1, source_target_pairs={{0,4},{4,0},{8,12},{12,8},{16,20},{20,16},{24,28},{28,24},{1,5},{5... | collective-permute-start | bytes 1572872 | tf_op jit(solution)/shard_map/ppermute | solution.py:578
  107.6 10.8 %copy-start.4 = (bf16[16,256,128]{2,1,0:T(8,128)(2,1)S(1)}, bf16[16,256,128]{2,1,0:T(8,128)(2,1)}, u32[]{:S(2)}) copy-start(bf16[16,256,128]{2,1,0:T(8,128)(2,1)} %copy-done.3) | copy-start | bytes 3145732
  107.7 10.8 %copy-start.6 = (bf16[16,256,128]{2,1,0:T(8,128)(2,1)S(1)}, bf16[16,256,128]{2,1,0:T(8,128)(2,1)}, u32[]{:S(2)}) copy-start(bf16[16,256,128]{2,1,0:T(8,128)(2,1)} %copy-done.5) | copy-start | bytes 3145732
  107.7 10.8 %copy-start.31 = (f32[16,128,128]{2,1,0:T(8,128)S(1)}, f32[16,128,128]{2,1,0:T(8,128)}, u32[]{:S(2)}) copy-start(f32[16,128,128]{2,1,0:T(8,128)} %copy-done.30) | copy-start | bytes 3145732
  (20 other events, 38.6 us)
where the time goes:
time: 137 us
  Pallas kernels  54.6 us (40%)
  waiting for transfers between devices  31.9 us (23%)
  starting transfers between devices  18.5 us (14%)
  local copies, waits for them, and re-layouts  17.9 us (13%)
  other arithmetic  12.7 us (9%)
    ppermute x15, waiting for transfers between devices, swap(): return lax.ppermute(value, axis, [(i, i ^ bit) for i in range(count)])  27.5 us
    unnamed x68, local copies, waits for them, and re-layouts  17.8 us
    pallas_call x2, Pallas kernels, intra(): pl.pallas_call(functools.partial(intra_kernel, index > 0), grid=(heads //...  14.5 us
    ppermute x15, starting transfers between devices, swap(): return lax.ppermute(value, axis, [(i, i ^ bit) for i in range(count)])  13.9 us
    pallas_call x1, Pallas kernels, finish(): pl.pallas_call(finish_kernel, grid=(2, groups), in_specs=[pl.BlockSpec(me...  9.06 us
    pallas_call x1, Pallas kernels, grad_query(): pl.pallas_call(grad_q_kernel, grid=(2, groups), in_specs=[pl.BlockSpec(me...  8.76 us
    pallas_call x1, Pallas kernels, grad_key_value(): pl.pallas_call(grad_kv_kernel, grid=(heads // GROUP,), in_specs=[pl.Block...  7.53 us
    ppermute x3, starting transfers between devices, sum_over_heads(): lax.ppermute(value, 'head', [(i, (i + shift) % count) for i in range(coun...  4.67 us
  transfers between devices with their start and end apart: 18, of which 12 were waited for; matrix products, arithmetic and copies ran while one was open for 1% of the time, Pallas kernels for 29%

commit v1 on v0

--- a/solution.py
+++ b/solution.py
@@ -14,13 +14,11 @@
 STEP_TOK = 128
 F32 = jnp.float32
 BF16 = jnp.bfloat16
-VMEM_LIMIT = 40 * 1024 * 1024
-
-
-def params():
-    return pltpu.CompilerParams(
-        dimension_semantics=("arbitrary",), vmem_limit_bytes=VMEM_LIMIT
-    )
+MIB = 1024 * 1024
+
+
+def params(mib):
+    return pltpu.CompilerParams(dimension_semantics=("arbitrary",), vmem_limit_bytes=mib * MIB)
 
 
 def cost(flops, moved, exps=0):
@@ -130,7 +128,7 @@
             pltpu.VMEM((2, heads, BLOCK), F32),
             pltpu.VMEM((2, heads, dim, dim), F32),
         ],
-        compiler_params=params(),
+        compiler_params=params(16),
         cost_estimate=cost(2 * tok * heads * dim * dim, 4 * tok * heads * dim),
         name="local_state",
     )(core, log_decay, key_rows, value_rows)
@@ -190,7 +188,7 @@
             jax.ShapeDtypeStruct((heads, BLOCK, dim), F32),
         ],
         scratch_shapes=[pltpu.VMEM((BLOCK * heads, dim), F32)] * 4 + [pltpu.VMEM((heads, BLOCK), F32)],
-        compiler_params=params(),
+        compiler_params=params(24),
         cost_estimate=cost(
             2 * heads * BLOCK * BLOCK * dim * 4, 20 * heads * BLOCK * dim, heads * BLOCK * BLOCK
         ),
@@ -260,7 +258,7 @@
             pltpu.VMEM((2, BLOCK, dim), F32),
             pltpu.VMEM((2, BLOCK, dim), F32),
         ],
-        compiler_params=params(),
+        compiler_params=params(16),
         cost_estimate=cost(4 * heads * tok * dim * dim, 16 * heads * tok * dim),
         name="attend",
     )(core, log_decay, gain, keep, recv, *parts)
@@ -338,7 +336,7 @@
             pltpu.VMEM((2, 2, BLOCK, dim), F32),
             pltpu.VMEM((heads, dim, dim), F32),
         ],
-        compiler_params=params(),
+        compiler_params=params(16),
         cost_estimate=cost(2 * heads * tok * dim * dim, 14 * heads * tok * dim),
         name="norm_grad",
     )(core, log_decay, gain, sums, *parts)
@@ -370,7 +368,7 @@
         out_specs=pl.BlockSpec((BLOCK, heads, dim), lambda i: (i, 0, 0)),
         out_shape=jax.ShapeDtypeStruct((tok, heads, dim), BF16),
         scratch_shapes=[pltpu.VMEM((BLOCK * heads, dim), F32)],
-        compiler_params=params(),
+        compiler_params=params(16),
         cost_estimate=cost(3 * heads * tok * dim, 6 * heads * tok * dim),
         name="normed_rows",
     )(gain, sums, att0, att1)
@@ -415,9 +413,9 @@
         out_ref[...] = rows[...].reshape(BLOCK, heads, HD).astype(BF16)
 
 
-def two_level():
+def two_level(mib):
     return pltpu.CompilerParams(
-        dimension_semantics=("arbitrary", "arbitrary"), vmem_limit_bytes=VMEM_LIMIT
+        dimension_semantics=("arbitrary", "arbitrary"), vmem_limit_bytes=mib * MIB
     )
 
 
@@ -445,7 +443,7 @@
             jax.ShapeDtypeStruct((2, heads, BLOCK, BLOCK), BF16),
         ],
         scratch_shapes=[pltpu.VMEM((2, heads, BLOCK), F32), pltpu.VMEM((BLOCK * heads, dim), F32)],
-        compiler_params=two_level(),
+        compiler_params=two_level(16),
         cost_estimate=cost(
             4 * heads * tok * dim * (BLOCK + dim), 12 * heads * tok * dim, heads * tok * BLOCK
         ),
@@ -496,7 +494,7 @@
         out_specs=[by_head] * 4,
         out_shape=[jax.ShapeDtypeStruct((heads, BLOCK, dim), F32)] * 4,
         scratch_shapes=[pltpu.VMEM((heads, BLOCK), F32)],
-        compiler_params=params(),
+        compiler_params=params(16),
         cost_estimate=cost(4 * heads * tok * dim * (BLOCK + dim), 30 * heads * tok * dim),
         name="grad_key_value",
     )(log_decay, gs, w0, w1, q0, q1, k0, v0, g0, g1, second)
@@ -567,7 +565,7 @@
             pltpu.VMEM((BLOCK * heads, dim), F32),
             pltpu.VMEM((BLOCK * heads, dim), F32),
         ],
-        compiler_params=two_level(),
+        compiler_params=two_level(16),
         cost_estimate=cost(8 * heads * tok * dim * dim, 16 * heads * tok * dim),
         name="finish",
     )(core, log_decay, keep, recv, k0, k1, v0, v1, dk0, dk1, dv0, dv1)
@@ -586,7 +584,14 @@
     )
 
 
-def entering_quad(own, send, decays, backward):
+def entering_quad(own, send, decays, backward, tasks):
+    def work(stage, after, before=()):
+        if stage not in tasks:
+            return before
+        run, outputs = tasks[stage]
+        outputs.extend(run(after))
+        return lax.optimization_barrier((before, outputs[-1]))[0]
+
     mine = lax.axis_index("seq")
     core = mine % 2
     half = own.shape[0]
@@ -603,6 +608,7 @@
     whole_one = jnp.ones((half,), F32)
 
     got = swap(send, "seq", 1)
+    work(0, got)
     total = wide(jnp.where(late, whole_one, d_partner)) * own + wide(
         jnp.where(late, d_own, whole_one)
     ) * got
@@ -610,17 +616,21 @@
     chip_a, chip_b = d_chip[:quarter], d_chip[quarter:]
     row_a, row_b = d_row[:quarter], d_row[quarter:]
 
-    a1 = swap(first_total, "seq", 2)
-    b1 = swap(wide(jnp.where(right, one, row_b)) * second_total, "seq", 4)
-    a2 = swap(
-        wide(jnp.where(right, one, row_a)) * first_total + wide(jnp.where(right, chip_a, one)) * a1,
-        "seq", 4,
-    )
-    b2 = swap(
+    b0 = wide(jnp.where(right, one, row_b)) * second_total
+    a0, b0, total, = lax.optimization_barrier((first_total, b0, total))
+    a1 = swap(a0, "seq", 2)
+    b1 = swap(b0, "seq", 4)
+    a1, b1 = work(1, total, (a1, b1))
+    a2 = wide(jnp.where(right, one, row_a)) * first_total + wide(jnp.where(right, chip_a, one)) * a1
+    b2 = (
         wide(jnp.where(low & right, zero, one)) * second_total
-        + wide(jnp.where(low, jnp.where(right, one, chip_b), zero)) * b1,
-        "seq", 2,
-    )
+        + wide(jnp.where(low, jnp.where(right, one, chip_b), zero)) * b1
+    )
+    a2, b2 = lax.optimization_barrier((a2, b2))
+    sent = a2
+    a2 = swap(a2, "seq", 4)
+    b2 = swap(b2, "seq", 2)
+    a2, b2 = work(2, sent, (a2, b2))
     enter_a = (
         wide(jnp.where(low, jnp.where(right, row_a, one), zero)) * a2
         + wide(jnp.where(right, one, zero)) * a1
@@ -633,10 +643,14 @@
     after = wide(jnp.where(late, d_partner, d_own)) * enter + jnp.where(late, got, own)
     kept = jnp.where(late, after, enter)
     sent = jnp.where(late, enter, after)
-    return kept, swap(sent, "seq", 1)
-
-
-def entering_any(own, send, log_total, backward):
+    received = swap(sent, "seq", 1)
+    work(3, sent)
+    return kept, received
+
+
+def entering_any(own, send, log_total, backward, tasks):
+    for run, outputs in tasks.values():
+        outputs.extend(run(send))
     count, mine = lax.axis_size("seq"), lax.axis_index("seq")
     core = mine % 2
     half = own.shape[0]
@@ -660,12 +674,20 @@
 
 def sum_over_heads(value):
     count = lax.axis_size("head")
-    total = value
-    for shift in range(1, count):
-        total = total + lax.ppermute(
-            value, "head", [(i, (i + shift) % count) for i in range(count)]
+    reach = 1
+    while 2 * reach <= count and count % (2 * reach) == 0:
+        value = value + swap(value, "head", reach)
+        reach *= 2
+    part = value
+    for shift in range(1, count // reach):
+        value = value + lax.ppermute(
+            part, "head", [(i, (i + shift * reach) % count) for i in range(count)]
         )
-    return total
+    return value
+
+
+def follows(value, earlier):
+    return lax.optimization_barrier((value, earlier))[0]
 
 
 def on_device(query_rows, key_rows, value_rows, output_grad, norm_gain, log_decay):
@@ -673,18 +695,33 @@
     log_total = jnp.sum(log_decay, axis=1)
     if lax.axis_size("seq") == 8:
         decays = quad_decays(log_total)
-        entering = lambda own, send, backward: entering_quad(own, send, decays, backward)
+        entering = lambda own, send, backward, tasks: entering_quad(
+            own, send, decays, backward, tasks
+        )
     else:
-        entering = lambda own, send, backward: entering_any(own, send, log_total, backward)
-
-    own, send, first = local_state(core, log_decay, key_rows, value_rows)
-    keep, recv = entering(own, send, False)
-    q0, k0, v0, o0, w0, inner0 = intra(
-        0, log_decay, query_rows, key_rows, value_rows, output_grad, first
-    )
-    q1, k1, v1, o1, w1, inner1 = intra(
-        1, log_decay, query_rows, key_rows, value_rows, output_grad, first
-    )
+        entering = lambda own, send, backward, tasks: entering_any(
+            own, send, log_total, backward, tasks
+        )
+
+    query_rows, key_rows, value_rows, output_grad = (
+        pltpu.with_memory_space_constraint(rows, pltpu.HBM)
+        for rows in (query_rows, key_rows, value_rows, output_grad)
+    )
+    own, send, first = local_state(
+        core, pltpu.with_memory_space_constraint(log_decay, pltpu.HBM), key_rows, value_rows
+    )
+
+    def forward_task(index):
+        return lambda earlier: intra(
+            index, log_decay, query_rows, key_rows, value_rows, output_grad, follows(first, earlier)
+        )
+
+    in_0, in_1 = [], []
+    keep, recv = entering(
+        own, send, False, {1: (forward_task(0), in_0), 2: (forward_task(1), in_1)}
+    )
+    q0, k0, v0, o0, w0, inner0 = in_0
+    q1, k1, v1, o1, w1, inner1 = in_1
     att0, att1, sums = attend(
         core, log_decay, norm_gain, keep, recv, (q0, q1, o0, o1, inner0, inner1)
     )
@@ -692,16 +729,29 @@
     g0, g1, grad_own, grad_send, second = norm_grad(
         core, log_decay, norm_gain, sums, (q0, q1, o0, o1, att0, att1)
     )
-    grad_keep, grad_recv = entering(grad_own, grad_send, True)
-    normed = normed_rows(norm_gain, sums, att0, att1)
-    grad_q, scores = grad_query(core, log_decay, keep, recv, first, k0, k1, v0, v1, g0, g1)
-    dk0, dv0, dk1, dv1 = grad_key_value(
-        log_decay, scores, w0, w1, q0, q1, k0, v0, g0, g1, second
-    )
+    queries, keys, norms = [], [], []
+
+    def query_task(earlier):
+        return grad_query(
+            core, log_decay, keep, recv, follows(first, earlier), k0, k1, v0, v1, g0, g1
+        )
+
+    def key_task(earlier):
+        return grad_key_value(
+            log_decay, queries[1], w0, w1, q0, q1, k0, v0, g0, g1, follows(second, earlier)
+        )
+
+    def norm_task(earlier):
+        return [normed_rows(follows(norm_gain, earlier), sums, att0, att1)]
+
+    grad_keep, grad_recv = entering(
+        grad_own, grad_send, True, {1: (query_task, queries), 2: (key_task, keys), 3: (norm_task, norms)}
+    )
+    dk0, dv0, dk1, dv1 = keys
     grad_k, grad_v = finish(
         core, log_decay, grad_keep, grad_recv, k0, k1, v0, v1, dk0, dk1, dv0, dv1
     )
-    return normed, grad_q, grad_k, grad_v
+    return norms[0], queries[0], grad_k, grad_v
 
 
 def solution(mesh):

time: 137 us -> 122 us (0.89)
  waiting for transfers between devices: 31.9 us -> 8.55 us
  local copies, waits for them, and re-layouts: 17.9 us -> 28.8 us
  starting transfers between devices: 18.5 us -> 16.8 us
    ppermute x15 -> x17, waiting for transfers between devices: 27.5 us -> 8.55 us  [swap(): return lax.ppermute(value, axis, [(i, i ^ bit) for i in range(count)])]
    unnamed x68 -> x100, local copies, waits for them, and re-layouts: 17.8 us -> 28.6 us
    ppermute x3 -> x0, starting transfers between devices: 4.67 us -> none  [sum_over_heads(): lax.ppermute(value, 'head', [(i, (i + shift) % count) for i in range(coun...]
    ppermute x3 -> x0, waiting for transfers between devices: 4.39 us -> none  [sum_over_heads(): lax.ppermute(value, 'head', [(i, (i + shift) % count) for i in range(coun...]
    ppermute x15 -> x17, starting transfers between devices: 13.9 us -> 16.8 us  [swap(): return lax.ppermute(value, axis, [(i, i ^ bit) for i in range(count)])]
    pallas_call x1, Pallas kernels: 7.53 us -> 4.7 us  [grad_key_value(): pl.pallas_call(grad_kv_kernel, grid=(heads // GROUP,), in_specs=[pl.Block...]
    slice x2 -> x0, other arithmetic: 2.58 us -> none  [entering_quad(): first_total, second_total = (total[:quarter], total[quarter:])]
    add x2, other arithmetic: 2.13 us -> 0.25 us  [entering_quad(): wide(jnp.where(late, whole_one, d_partner)) * own]
  transfers between devices with their start and end apart: 18 -> 17, of which waited for: 12 -> 5; matrix products, arithmetic and copies ran while one was open for 1% -> 0% of each run, Pallas kernels for 29% -> 32%
where the time goes in v1:
time: 122 us; the launch traced here: 121 us
  Pallas kernels  53.5 us (44%)
  local copies, waits for them, and re-layouts  28.8 us (24%)
  starting transfers between devices  16.8 us (14%)
  other arithmetic  12.7 us (10%)
  waiting for transfers between devices  8.55 us (7%)
    unnamed x100, local copies, waits for them, and re-layouts  28.6 us
    ppermute x17, starting transfers between devices, swap(): return lax.ppermute(value, axis, [(i, i ^ bit) for i in range(count)])  16.8 us
    pallas_call x2, Pallas kernels, intra(): pl.pallas_call(functools.partial(intra_kernel, index > 0), grid=(heads //...  15.5 us
    pallas_call x1, Pallas kernels, finish(): pl.pallas_call(finish_kernel, grid=(2, groups), in_specs=[pl.BlockSpec(me...  9.09 us
    pallas_call x1, Pallas kernels, grad_query(): pl.pallas_call(grad_q_kernel, grid=(2, groups), in_specs=[pl.BlockSpec(me...  8.7 us
    ppermute x17, waiting for transfers between devices, swap(): return lax.ppermute(value, axis, [(i, i ^ bit) for i in range(count)])  8.55 us
    pallas_call x1, Pallas kernels, local_state(): pl.pallas_call(state_kernel, grid=(tok // STEP_TOK,), in_specs=[pl.BlockS...  6.03 us
    pallas_call x1, Pallas kernels, grad_key_value(): pl.pallas_call(grad_kv_kernel, grid=(heads // GROUP,), in_specs=[pl.Block...  4.7 us
  transfers between devices with their start and end apart: 17, of which 5 were waited for; matrix products, arithmetic and copies ran while one was open for 0% of the time, Pallas kernels for 32%

profile of v1, /device:TPU:0, one launch (start us, length us, event | category | flops | bytes accessed | tf_op | source)
XLA Modules:
  0.0 121.4 jit_solution(13302070205513213140)
XLA Ops:
  2.0 2.6 %collective-permute-start.1 = (f32[16]{0:T(128)S(1)}, f32[16]{0:T(128)S(1)}, u32[]{:S(2)}, u32[]{:S(2)}) collective-permute-start(f32[16]{0:T(128)S(1)} %reduce_sum.9), channel_id=1, source_target_pairs={{0,12},{4,8},{8,4},{12,0},{16,28},{20,24},{24,20},{28,16},{1,13},{... | collective-permute-start | bytes 200 | tf_op jit(solution)/shard_map/ppermute | solution.py:576
  4.7 6.0 %local_state.1 = (f32[8,128,128]{2,1,0:T(8,128)S(1)}, f32[8,128,128]{2,1,0:T(8,128)S(1)}, f32[16,128,128]{2,1,0:T(8,128)S(1)}) custom-call(s32[1]{0:T(128)} %bitcast.core_ref, f32[16,512]{1,0:T(8,128)} %ld_ref.15, bf16[512,16,128]{2,1,0:T(8,128)(2,1)} %k_ref.5, bf16[512,16,128]{2,1,0:T(8,128)(2,1)} %v_ref.5), custom_call_target="tpu_custom_call" | custom-call | flops 268435456 | bytes 4194304 | tf_op jit(solution)/shard_map/local_state/pallas_call | solution.py:115
  11.2 1.5 %collective-permute-done.3 = f32[8,128,128]{2,1,0:T(8,128)S(1)} collective-permute-done((f32[8,128,128]{2,1,0:T(8,128)S(1)}, f32[8,128,128]{2,1,0:T(8,128)S(1)}, u32[]{:S(2)}, u32[]{:S(2)}) %collective-permute-start.3) | collective-permute-done | bytes 524320 | tf_op jit(solution)/shard_map/ppermute | solution.py:576
  13.9 2.0 %collective-permute-start.4 = (f32[4,128,128]{2,1,0:T(8,128)}, f32[4,128,128]{2,1,0:T(8,128)S(1)}, u32[]{:S(2)}, u32[]{:S(2)}) collective-permute-start(f32[4,128,128]{2,1,0:T(8,128)} %get-tuple-element.56), channel_id=1, source_target_pairs={{0,8},{4,12},{8,0},{12,4},{16,24},{20,28},{24,16},{28,20},{1,9},{5... | collective-permute-start | bytes 786440 | tf_op jit(solution)/shard_map/ppermute | solution.py:576
  15.9 1.6 %collective-permute-start.5 = (f32[4,128,128]{2,1,0:T(8,128)}, f32[4,128,128]{2,1,0:T(8,128)}, u32[]{:S(2)}, u32[]{:S(2)}) collective-permute-start(f32[4,128,128]{2,1,0:T(8,128)} %get-tuple-element.57), channel_id=1, source_target_pairs={{0,16},{4,20},{8,24},{12,28},{16,0},{20,4},{24,8},{28,12},{1,17},{... | collective-permute-start | bytes 786440 | tf_op jit(solution)/shard_map/ppermute | solution.py:576
  17.4 7.3 %intra_0.1 = (bf16[16,256,128]{2,1,0:T(8,128)(2,1)S(1)}, bf16[16,256,128]{2,1,0:T(8,128)(2,1)S(1)}, bf16[16,256,128]{2,1,0:T(8,128)(2,1)S(1)}, bf16[16,256,128]{...) custom-call(f32[16,512]{1,0:T(8,128)S(1)} %copy-done.27, ...), custom_call_target="tpu_custom_call" | custom-call | flops 1073741824 | bytes 10485760 | tf_op jit(solution)/shard_map/intra_0/pallas_call | solution.py:177
  26.7 1.3 %copy-done.28 = bf16[16,256,256]{2,1,0:T(8,128)(2,1)} copy-done((bf16[16,256,256]{2,1,0:T(8,128)(2,1)}, bf16[16,256,256]{2,1,0:T(8,128)(2,1)S(1)}, u32[]{:S(2)}) %copy-start.28) | copy-done | bytes 2097176
  28.1 1.3 %copy-done.38 = f32[16,256,128]{2,1,0:T(8,128)} copy-done((f32[16,256,128]{2,1,0:T(8,128)}, f32[16,256,128]{2,1,0:T(8,128)S(1)}, u32[]{:S(2)}) %copy-start.38) | copy-done | bytes 2097176
  29.5 2.0 %multiply_add_fusion.8 = (f32[4,128,128]{2,1,0:T(8,128)}, f32[4,128,128]{2,1,0:T(8,128)}) fusion(f32[4,128,128]{2,1,0:T(8,128)} %collective-permute-done.5, f32[8,128,128]{2,1,0:T(8,128)} %copy-done.43, f32[4]{0:T(128)S(1)} %get-tuple-element.128, f32[]{:T(128)S(6)} %select_n.236, f32[4,128,128]{2,1,0:T(8,128)S(1)} %collective-permute-done.4, ...), kind=kLoop, calls=%fused_computation.16 | loop fusion | flops 393216 | bytes 1572916 | tf_op jit(solution)/shard_map/add | solution.py:626
  32.2 8.2 %intra_1.1 = (bf16[16,256,128]{2,1,0:T(8,128)(2,1)S(1)}, bf16[16,256,128]{2,1,0:T(8,128)(2,1)S(1)}, bf16[16,256,128]{2,1,0:T(8,128)(2,1)S(1)}, bf16[16,256,128]{...) custom-call(f32[16,512]{1,0:T(8,128)S(1)} %copy-done.27, ...), custom_call_target="tpu_custom_call" | custom-call | flops 1073741824 | bytes 10485760 | tf_op jit(solution)/shard_map/intra_1/pallas_call | solution.py:177
  41.4 1.7 %multiply_add_fusion.6 = f32[4,128,128]{2,1,0:T(8,128)S(1)} fusion(f32[4,128,128]{2,1,0:T(8,128)} %collective-permute-done.7, f32[4,128,128]{2,1,0:T(8,128)} %collective-permute-done.5, f32[]{:T(128)S(6)} %select_n.242, f32[4]{0:T(128)S(1)} %get-tuple-element.122), kind=kLoop, calls=%fused_computation.14 | loop fusion | flops 196608 | bytes 786452 | tf_op jit(solution)/shard_map/add | solution.py:639
  43.2 2.1 %multiply_add_fusion.7 = f32[4,128,128]{2,1,0:T(8,128)S(1)} fusion(f32[4,128,128]{2,1,0:T(8,128)S(1)} %collective-permute-done.4, f32[4,128,128]{2,1,0:T(8,128)} %collective-permute-done.6, f32[]{:T(128)S(6)} %select_n.239, f32[4]{0:T(128)S(1)} %get-tuple-element.120), kind=kLoop, calls=%fused_computation.15 | loop fusion | flops 196608 | bytes 786452 | tf_op jit(solution)/shard_map/add | solution.py:635
  45.6 1.9 %collective-permute-done.8.recv_ref = f32[8,128,128]{2,1,0:T(8,128)S(1)} collective-permute-done((f32[8,128,128]{2,1,0:T(8,128)S(1)}, f32[8,128,128]{2,1,0:T(8,128)S(1)}, u32[]{:S(2)}, u32[]{:S(2)}) %collective-permute-start.8) | collective-permute-done | bytes 524320 | tf_op jit(solution)/shard_map/ppermute | solution.py:576
  47.5 3.3 %attend.1 = (f32[16,256,128]{2,1,0:T(8,128)S(1)}, f32[16,256,128]{2,1,0:T(8,128)S(1)}, f32[2,512]{1,0:T(2,128)S(1)}) custom-call(s32[1]{0:T(128)} %bitcast.core_ref, f32[16,512]{1,0:T(8,128)S(1)} %copy-done.27, f32[16,128]{1,0:T(8,128)S(1)} %copy-done.42, f32[8,128,128]{2,1,0:T(8,128)S(1)} %get-tuple-element.110.keep_ref, ...), custom_call_target="tpu_custom_call" | custom-call | flops 536870912 | bytes 16777216 | tf_op jit(solution)/shard_map/attend/pallas_call | solution.py:249
  50.8 2.1 %collective-permute-start.9 = (f32[2,512]{1,0:T(2,128)S(1)}, f32[2,512]{1,0:T(2,128)S(1)}, u32[]{:S(2)}, u32[]{:S(2)}) collective-permute-start(f32[2,512]{1,0:T(2,128)S(1)} %get-tuple-element.72), channel_id=1, source_target_pairs={{0,1},{1,0},{2,3},{3,2},{4,5},{5,4},{6,7},{7,6},{8,9},{9,8},{10,11... | collective-permute-start | bytes 12296 | tf_op jit(solution)/shard_map/ppermute | solution.py:576
  52.9 1.6 %collective-permute-done.9 = f32[2,512]{1,0:T(2,128)S(1)} collective-permute-done((f32[2,512]{1,0:T(2,128)S(1)}, f32[2,512]{1,0:T(2,128)S(1)}, u32[]{:S(2)}, u32[]{:S(2)}) %collective-permute-start.9) | collective-permute-done | bytes 4128 | tf_op jit(solution)/shard_map/ppermute | solution.py:576
  54.5 3.0 %collective-permute-start.10 = (f32[2,512]{1,0:T(2,128)S(1)}, f32[2,512]{1,0:T(2,128)S(1)}, u32[]{:S(2)}, u32[]{:S(2)}) collective-permute-start(f32[2,512]{1,0:T(2,128)S(1)} %add.89), channel_id=1, source_target_pairs={{0,2},{1,3},{2,0},{3,1},{4,6},{5,7},{6,4},{7,5},{8,10},{9,11},{10,... | collective-permute-start | bytes 12296 | tf_op jit(solution)/shard_map/ppermute | solution.py:576
  57.5 1.6 %collective-permute-done.10 = f32[2,512]{1,0:T(2,128)S(1)} collective-permute-done((f32[2,512]{1,0:T(2,128)S(1)}, f32[2,512]{1,0:T(2,128)S(1)}, u32[]{:S(2)}, u32[]{:S(2)}) %collective-permute-start.10) | collective-permute-done | bytes 4128 | tf_op jit(solution)/shard_map/ppermute | solution.py:576
  59.1 2.6 %norm_grad.1 = (bf16[16,256,128]{2,1,0:T(8,128)(2,1)S(1)}, bf16[16,256,128]{2,1,0:T(8,128)(2,1)S(1)}, f32[8,128,128]{2,1,0:T(8,128)S(1)}, f32[8,128,128]{2,1,0:T(8,128)S(1)}, f32[16,128,128]{2,1,0:T(8,128)S(1)}) custom-call(s32[1]{0:T(128)} %bitcast.core_ref, f32[16,512]{1,0:T(8,128)S(1)} %copy-done.27, f32[16,128]{1,0:T(8,128)S(1)} %copy-done.42, ...), custom_call_target="tpu_custom_call" | custom-call | flops 268435456 | bytes 14680064 | tf_op jit(solution)/shard_map/norm_grad/pallas_call | solution.py:318
  63.8 1.9 %collective-permute-done.11 = f32[8,128,128]{2,1,0:T(8,128)S(1)} collective-permute-done((f32[8,128,128]{2,1,0:T(8,128)S(1)}, f32[8,128,128]{2,1,0:T(8,128)S(1)}, u32[]{:S(2)}, u32[]{:S(2)}) %collective-permute-start.11) | collective-permute-done | bytes 524320 | tf_op jit(solution)/shard_map/ppermute | solution.py:576
  67.5 1.8 %collective-permute-start.12 = (f32[4,128,128]{2,1,0:T(8,128)}, f32[4,128,128]{2,1,0:T(8,128)S(1)}, u32[]{:S(2)}, u32[]{:S(2)}) collective-permute-start(f32[4,128,128]{2,1,0:T(8,128)} %get-tuple-element.77), channel_id=1, source_target_pairs={{0,8},{4,12},{8,0},{12,4},{16,24},{20,28},{24,16},{28,20},{1,9},{5... | collective-permute-start | bytes 786440 | tf_op jit(solution)/shard_map/ppermute | solution.py:576
  69.3 1.5 %collective-permute-start.13 = (f32[4,128,128]{2,1,0:T(8,128)}, f32[4,128,128]{2,1,0:T(8,128)}, u32[]{:S(2)}, u32[]{:S(2)}) collective-permute-start(f32[4,128,128]{2,1,0:T(8,128)} %get-tuple-element.78), channel_id=1, source_target_pairs={{0,16},{4,20},{8,24},{12,28},{16,0},{20,4},{24,8},{28,12},{1,17},{... | collective-permute-start | bytes 786440 | tf_op jit(solution)/shard_map/ppermute | solution.py:576
  77.8 8.7 %grad_query.1 = (bf16[512,16,128]{2,1,0:T(8,128)(2,1)}, bf16[2,16,256,256]{3,2,1,0:T(8,128)(2,1)S(1)}) custom-call(s32[1]{0:T(128)} %bitcast.core_ref, f32[16,512]{1,0:T(8,128)S(1)} %copy-done.27, f32[8,128,128]{2,1,0:T(8,128)S(1)} %copy-done.10, f32[8,128,128]{2,1,0:T(8,128)S(1)} %copy-done.33, f32[16,128,128]{2,1,0:T(8,128)S(1)} %get-tuple-element.64.first_ref, ...), custom_call_target="tpu_custom_call" | custom-call | flops 1610612736 | bytes 12582912 | tf_op jit(solution)/shard_map/grad_query/pallas_call | solution.py:429
  86.5 2.0 %copy-done.11 = bf16[2,16,256,256]{3,2,1,0:T(8,128)(2,1)} copy-done((bf16[2,16,256,256]{3,2,1,0:T(8,128)(2,1)}, bf16[2,16,256,256]{3,2,1,0:T(8,128)(2,1)S(1)}, u32[]{:S(2)}) %copy-start.11) | copy-done | bytes 4194328
  88.6 1.9 %multiply_add_fusion.4 = (f32[4,128,128]{2,1,0:T(8,128)}, f32[4,128,128]{2,1,0:T(8,128)}) fusion(f32[4,128,128]{2,1,0:T(8,128)} %collective-permute-done.13, f32[8,128,128]{2,1,0:T(8,128)S(1)} %copy-done.45, f32[4]{0:T(128)S(1)} %get-tuple-element.127, f32[]{:T(128)S(6)} %select_n.249, f32[4,128,128]{2,1,0:T(8,128)S(1)} %collective-permute-done.12, ...), kind=kLoop, calls=%fused_computation.12 | loop fusion | flops 393216 | bytes 1572916 | tf_op jit(solution)/shard_map/add | solution.py:626
  92.4 2.2 %copy-done.12 = bf16[2,16,256,256]{3,2,1,0:T(8,128)(2,1)S(1)} copy-done((bf16[2,16,256,256]{3,2,1,0:T(8,128)(2,1)S(1)}, bf16[2,16,256,256]{3,2,1,0:T(8,128)(2,1)}, u32[]{:S(2)}) %copy-start.12) | copy-done | bytes 4194328
  97.1 1.6 %copy-done.29 = bf16[16,256,256]{2,1,0:T(8,128)(2,1)S(1)} copy-done((bf16[16,256,256]{2,1,0:T(8,128)(2,1)S(1)}, bf16[16,256,256]{2,1,0:T(8,128)(2,1)}, u32[]{:S(2)}) %copy-start.29) | copy-done | bytes 2097176
  98.7 1.6 %copy-done.31 = bf16[16,256,256]{2,1,0:T(8,128)(2,1)S(1)} copy-done((bf16[16,256,256]{2,1,0:T(8,128)(2,1)S(1)}, bf16[16,256,256]{2,1,0:T(8,128)(2,1)}, u32[]{:S(2)}) %copy-start.31) | copy-done | bytes 2097176
  101.5 4.7 %grad_key_value.1 = (f32[16,256,128]{2,1,0:T(8,128)S(1)}, f32[16,256,128]{2,1,0:T(8,128)S(1)}, f32[16,256,128]{2,1,0:T(8,128)S(1)}, f32[16,256,128]{2,1,0:T(8,128)S(1)}) custom-call(f32[16,512]{1,0:T(8,128)S(1)} %copy-done.27, bf16[2,16,256,256]{3,2,1,0:T(8,128)(2,1)S(1)} %copy-done.12, bf16[16,256,256]{2,1,0:T(8,128)(2,1)S(1)} %copy-done.29, ...), custom_call_target="tpu_custom_call" | custom-call | flops 1610612736 | bytes 31457280 | tf_op jit(solution)/shard_map/grad_key_value/pallas_call | solution.py:485
  106.2 1.4 %multiply_add_fusion.2 = (f32[4,128,128]{2,1,0:T(8,128)S(1)}, f32[4,128,128]{2,1,0:T(8,128)S(1)}) fusion(f32[4,128,128]{2,1,0:T(8,128)} %collective-permute-done.15, f32[4,128,128]{2,1,0:T(8,128)} %collective-permute-done.13, f32[]{:T(128)S(6)} %select_n.255, f32[4]{0:T(128)S(1)} %get-tuple-element.126, f32[4,128,128]{2,1,0:T(8,128)S(1)} %collective-permute-done.12, ...), kind=kLoop, calls=%fused_computation.10 | loop fusion | flops 393216 | bytes 1572904 | tf_op jit(solution)/shard_map/add | solution.py:639
  108.7 3.6 %normed_rows.1 = bf16[512,16,128]{2,1,0:T(8,128)(2,1)} custom-call(f32[16,128]{1,0:T(8,128)S(1)} %copy-done.42, f32[2,512]{1,0:T(2,128)S(1)} %add.90.sums_ref, f32[16,256,128]{2,1,0:T(8,128)S(1)} %copy-done.6, f32[16,256,128]{2,1,0:T(8,128)S(1)} %copy-done.8), custom_call_target="tpu_custom_call" | custom-call | flops 3145728 | bytes 6291456 | tf_op jit(solution)/shard_map/normed_rows/pallas_call | solution.py:364
  112.3 9.1 %finish.1 = (bf16[512,16,128]{2,1,0:T(8,128)(2,1)}, bf16[512,16,128]{2,1,0:T(8,128)(2,1)}) custom-call(s32[1]{0:T(128)} %bitcast.core_ref, f32[16,512]{1,0:T(8,128)S(1)} %copy-done.27, f32[8,128,128]{2,1,0:T(8,128)S(1)} %get-tuple-element.107.keep_ref, f32[8,128,128]{2,1,0:T(8,128)S(1)} %collective-permute-done.16.recv_ref, ...), custom_call_target="tpu_custom_call" | custom-call | flops 1073741824 | bytes 16777216 | tf_op jit(solution)/shard_map/finish/pallas_call | solution.py:554
  (133 shorter events, 24.5 us)
Async XLA Ops:
  1.5 9.5 %collective-permute-start.2 = (f32[16]{0:T(128)S(1)}, f32[16]{0:T(128)S(1)}, u32[]{:S(2)}, u32[]{:S(2)}) collective-permute-start(f32[16]{0:T(128)S(1)} %reduce_sum.9), channel_id=1, source_target_pairs={{0,4},{4,0},{8,12},{12,8},{16,20},{20,16},{24,28},{28,24},{1,5},{5... | collective-permute-start | bytes 200 | tf_op jit(solution)/shard_map/ppermute | solution.py:576
  2.0 8.9 %collective-permute-start.1 = (f32[16]{0:T(128)S(1)}, f32[16]{0:T(128)S(1)}, u32[]{:S(2)}, u32[]{:S(2)}) collective-permute-start(f32[16]{0:T(128)S(1)} %reduce_sum.9), channel_id=1, source_target_pairs={{0,12},{4,8},{8,4},{12,0},{16,28},{20,24},{24,20},{28,16},{1,13},{... | collective-permute-start | bytes 200 | tf_op jit(solution)/shard_map/ppermute | solution.py:576
  4.6 6.3 %collective-permute-start = (f32[16]{0:T(128)S(1)}, f32[16]{0:T(128)S(1)}, u32[]{:S(2)}, u32[]{:S(2)}) collective-permute-start(f32[16]{0:T(128)S(1)} %reduce_sum.9), channel_id=1, source_target_pairs={{0,8},{4,12},{8,0},{12,4},{16,24},{20,28},{24,16},{28,20},{1,9},{5... | collective-permute-start | bytes 200 | tf_op jit(solution)/shard_map/ppermute | solution.py:576
  10.7 5.1 %copy-start.34 = (f32[8,128,128]{2,1,0:T(8,128)}, f32[8,128,128]{2,1,0:T(8,128)S(1)}, u32[]{:S(2)}) copy-start(f32[8,128,128]{2,1,0:T(8,128)S(1)} %get-tuple-element.54) | copy-start | bytes 1572868
  10.7 6.7 %copy-start.27 = (f32[16,512]{1,0:T(8,128)S(1)}, f32[16,512]{1,0:T(8,128)}, u32[]{:S(2)}) copy-start(f32[16,512]{1,0:T(8,128)} %ld_ref.15) | copy-start | bytes 98308
  10.7 2.0 %collective-permute-start.3 = (f32[8,128,128]{2,1,0:T(8,128)S(1)}, f32[8,128,128]{2,1,0:T(8,128)S(1)}, u32[]{:S(2)}, u32[]{:S(2)}) collective-permute-start(f32[8,128,128]{2,1,0:T(8,128)S(1)} %get-tuple-element.55), channel_id=1, source_target_pairs={{0,4},{4,0},{8,12},{12,8},{16,20},{20,16},{24,28},{28,24},{1,5},{5... | collective-permute-start | bytes 1572872 | tf_op jit(solution)/shard_map/ppermute | solution.py:576
  13.9 15.7 %collective-permute-start.4 = (f32[4,128,128]{2,1,0:T(8,128)}, f32[4,128,128]{2,1,0:T(8,128)S(1)}, u32[]{:S(2)}, u32[]{:S(2)}) collective-permute-start(f32[4,128,128]{2,1,0:T(8,128)} %get-tuple-element.56), channel_id=1, source_target_pairs={{0,8},{4,12},{8,0},{12,4},{16,24},{20,28},{24,16},{28,20},{1,9},{5... | collective-permute-start | bytes 786440 | tf_op jit(solution)/shard_map/ppermute | solution.py:576
  15.9 13.7 %collective-permute-start.5 = (f32[4,128,128]{2,1,0:T(8,128)}, f32[4,128,128]{2,1,0:T(8,128)}, u32[]{:S(2)}, u32[]{:S(2)}) collective-permute-start(f32[4,128,128]{2,1,0:T(8,128)} %get-tuple-element.57), channel_id=1, source_target_pairs={{0,16},{4,20},{8,24},{12,28},{16,0},{20,4},{24,8},{28,12},{1,17},{... | collective-permute-start | bytes 786440 | tf_op jit(solution)/shard_map/ppermute | solution.py:576
  31.6 9.8 %collective-permute-start.7 = (f32[4,128,128]{2,1,0:T(8,128)}, f32[4,128,128]{2,1,0:T(8,128)}, u32[]{:S(2)}, u32[]{:S(2)}) collective-permute-start(f32[4,128,128]{2,1,0:T(8,128)} %get-tuple-element.63), channel_id=1, source_target_pairs={{0,8},{4,12},{8,0},{12,4},{16,24},{20,28},{24,16},{28,20},{1,9},{5... | collective-permute-start | bytes 786440 | tf_op jit(solution)/shard_map/ppermute | solution.py:576
  32.1 9.3 %collective-permute-start.6 = (f32[4,128,128]{2,1,0:T(8,128)}, f32[4,128,128]{2,1,0:T(8,128)}, u32[]{:S(2)}, u32[]{:S(2)}) collective-permute-start(f32[4,128,128]{2,1,0:T(8,128)} %get-tuple-element.62), channel_id=1, source_target_pairs={{0,16},{4,20},{8,24},{12,28},{16,0},{20,4},{24,8},{28,12},{1,17},{... | collective-permute-start | bytes 786440 | tf_op jit(solution)/shard_map/ppermute | solution.py:576
  32.1 13.1 %copy-start.35 = (f32[8,128,128]{2,1,0:T(8,128)S(1)}, f32[8,128,128]{2,1,0:T(8,128)}, u32[]{:S(2)}) copy-start(f32[8,128,128]{2,1,0:T(8,128)} %copy-done.34) | copy-start | bytes 1572868
  32.1 13.1 %copy-start.47 = (f32[8,128,128]{2,1,0:T(8,128)S(1)}, f32[8,128,128]{2,1,0:T(8,128)}, u32[]{:S(2)}) copy-start(f32[8,128,128]{2,1,0:T(8,128)} %copy-done.46) | copy-start | bytes 1572868
  41.4 17.7 %copy-start.3 = (bf16[16,256,128]{2,1,0:T(8,128)(2,1)}, bf16[16,256,128]{2,1,0:T(8,128)(2,1)S(1)}, u32[]{:S(2)}) copy-start(bf16[16,256,128]{2,1,0:T(8,128)(2,1)S(1)} %get-tuple-element.69.q1) | copy-start | bytes 3145732
  41.4 6.1 %copy-start.1 = (bf16[16,256,128]{2,1,0:T(8,128)(2,1)S(1)}, bf16[16,256,128]{2,1,0:T(8,128)(2,1)}, u32[]{:S(2)}) copy-start(bf16[16,256,128]{2,1,0:T(8,128)(2,1)} %copy-done) | copy-start | bytes 3145732
  41.4 6.1 %copy-start.20 = (bf16[16,256,128]{2,1,0:T(8,128)(2,1)S(1)}, bf16[16,256,128]{2,1,0:T(8,128)(2,1)}, u32[]{:S(2)}) copy-start(bf16[16,256,128]{2,1,0:T(8,128)(2,1)} %copy-done.19) | copy-start | bytes 3145732
  41.4 6.1 %copy-start.39 = (f32[16,256,128]{2,1,0:T(8,128)S(1)}, f32[16,256,128]{2,1,0:T(8,128)}, u32[]{:S(2)}) copy-start(f32[16,256,128]{2,1,0:T(8,128)} %copy-done.38) | copy-start | bytes 6291460
  41.4 6.1 %copy-start.42 = (f32[16,128]{1,0:T(8,128)S(1)}, f32[16,128]{1,0:T(8,128)}, u32[]{:S(2)}) copy-start(f32[16,128]{1,0:T(8,128)} %gain_ref.4) | copy-start | bytes 24580
  45.5 5.3 %copy-start.9 = (f32[8,128,128]{2,1,0:T(8,128)}, f32[8,128,128]{2,1,0:T(8,128)S(1)}, u32[]{:S(2)}) copy-start(f32[8,128,128]{2,1,0:T(8,128)S(1)} %get-tuple-element.110.keep_ref) | copy-start | bytes 1572868
  45.5 2.0 %collective-permute-start.8 = (f32[8,128,128]{2,1,0:T(8,128)S(1)}, f32[8,128,128]{2,1,0:T(8,128)S(1)}, u32[]{:S(2)}, u32[]{:S(2)}) collective-permute-start(f32[8,128,128]{2,1,0:T(8,128)S(1)} %get-tuple-element.109), channel_id=1, source_target_pairs={{0,4},{4,0},{8,12},{12,8},{16,20},{20,16},{24,28},{28,24},{1,5},{5... | collective-permute-start | bytes 1572872 | tf_op jit(solution)/shard_map/ppermute | solution.py:576
  50.8 10.9 %copy-start.5 = (f32[16,256,128]{2,1,0:T(8,128)}, f32[16,256,128]{2,1,0:T(8,128)S(1)}, u32[]{:S(2)}) copy-start(f32[16,256,128]{2,1,0:T(8,128)S(1)} %get-tuple-element.73.att0) | copy-start | bytes 6291460
  50.8 10.9 %copy-start.7 = (f32[16,256,128]{2,1,0:T(8,128)}, f32[16,256,128]{2,1,0:T(8,128)S(1)}, u32[]{:S(2)}) copy-start(f32[16,256,128]{2,1,0:T(8,128)S(1)} %get-tuple-element.74.att1) | copy-start | bytes 6291460
  50.8 3.7 %collective-permute-start.9 = (f32[2,512]{1,0:T(2,128)S(1)}, f32[2,512]{1,0:T(2,128)S(1)}, u32[]{:S(2)}, u32[]{:S(2)}) collective-permute-start(f32[2,512]{1,0:T(2,128)S(1)} %get-tuple-element.72), channel_id=1, source_target_pairs={{0,1},{1,0},{2,3},{3,2},{4,5},{5,4},{6,7},{7,6},{8,9},{9,8},{10,11... | collective-permute-start | bytes 12296 | tf_op jit(solution)/shard_map/ppermute | solution.py:576
  54.5 4.6 %collective-permute-start.10 = (f32[2,512]{1,0:T(2,128)S(1)}, f32[2,512]{1,0:T(2,128)S(1)}, u32[]{:S(2)}, u32[]{:S(2)}) collective-permute-start(f32[2,512]{1,0:T(2,128)S(1)} %add.89), channel_id=1, source_target_pairs={{0,2},{1,3},{2,0},{3,1},{4,6},{5,7},{6,4},{7,5},{8,10},{9,11},{10,... | collective-permute-start | bytes 12296 | tf_op jit(solution)/shard_map/ppermute | solution.py:576
  63.8 1.9 %collective-permute-start.11 = (f32[8,128,128]{2,1,0:T(8,128)S(1)}, f32[8,128,128]{2,1,0:T(8,128)S(1)}, u32[]{:S(2)}, u32[]{:S(2)}) collective-permute-start(f32[8,128,128]{2,1,0:T(8,128)S(1)} %get-tuple-element.76), channel_id=1, source_target_pairs={{0,4},{4,0},{8,12},{12,8},{16,20},{20,16},{24,28},{28,24},{1,5},{5... | collective-permute-start | bytes 1572872 | tf_op jit(solution)/shard_map/ppermute | solution.py:576
  67.5 21.0 %collective-permute-start.12 = (f32[4,128,128]{2,1,0:T(8,128)}, f32[4,128,128]{2,1,0:T(8,128)S(1)}, u32[]{:S(2)}, u32[]{:S(2)}) collective-permute-start(f32[4,128,128]{2,1,0:T(8,128)} %get-tuple-element.77), channel_id=1, source_target_pairs={{0,8},{4,12},{8,0},{12,4},{16,24},{20,28},{24,16},{28,20},{1,9},{5... | collective-permute-start | bytes 786440 | tf_op jit(solution)/shard_map/ppermute | solution.py:576
  69.3 19.2 %collective-permute-start.13 = (f32[4,128,128]{2,1,0:T(8,128)}, f32[4,128,128]{2,1,0:T(8,128)}, u32[]{:S(2)}, u32[]{:S(2)}) collective-permute-start(f32[4,128,128]{2,1,0:T(8,128)} %get-tuple-element.78), channel_id=1, source_target_pairs={{0,16},{4,20},{8,24},{12,28},{16,0},{20,4},{24,8},{28,12},{1,17},{... | collective-permute-start | bytes 786440 | tf_op jit(solution)/shard_map/ppermute | solution.py:576
  77.8 10.7 %copy-start.45 = (f32[8,128,128]{2,1,0:T(8,128)S(1)}, f32[8,128,128]{2,1,0:T(8,128)}, u32[]{:S(2)}) copy-start(f32[8,128,128]{2,1,0:T(8,128)} %copy-done.44) | copy-start | bytes 1572868
  90.5 15.7 %collective-permute-start.15 = (f32[4,128,128]{2,1,0:T(8,128)}, f32[4,128,128]{2,1,0:T(8,128)}, u32[]{:S(2)}, u32[]{:S(2)}) collective-permute-start(f32[4,128,128]{2,1,0:T(8,128)} %get-tuple-element.89), channel_id=1, source_target_pairs={{0,8},{4,12},{8,0},{12,4},{16,24},{20,28},{24,16},{28,20},{1,9},{5... | collective-permute-start | bytes 786440 | tf_op jit(solution)/shard_map/ppermute | solution.py:576
  91.0 15.2 %collective-permute-start.14 = (f32[4,128,128]{2,1,0:T(8,128)}, f32[4,128,128]{2,1,0:T(8,128)}, u32[]{:S(2)}, u32[]{:S(2)}) collective-permute-start(f32[4,128,128]{2,1,0:T(8,128)} %get-tuple-element.88), channel_id=1, source_target_pairs={{0,16},{4,20},{8,24},{12,28},{16,0},{20,4},{24,8},{28,12},{1,17},{... | collective-permute-start | bytes 786440 | tf_op jit(solution)/shard_map/ppermute | solution.py:576
  101.5 6.1 %copy-start.37 = (f32[8,128,128]{2,1,0:T(8,128)S(1)}, f32[8,128,128]{2,1,0:T(8,128)}, u32[]{:S(2)}) copy-start(f32[8,128,128]{2,1,0:T(8,128)} %copy-done.36) | copy-start | bytes 1572868
  101.5 6.2 %copy-start.49 = (f32[8,128,128]{2,1,0:T(8,128)S(1)}, f32[8,128,128]{2,1,0:T(8,128)}, u32[]{:S(2)}) copy-start(f32[8,128,128]{2,1,0:T(8,128)} %copy-done.48) | copy-start | bytes 1572868
  107.9 4.5 %collective-permute-start.16 = (f32[8,128,128]{2,1,0:T(8,128)S(1)}, f32[8,128,128]{2,1,0:T(8,128)S(1)}, u32[]{:S(2)}, u32[]{:S(2)}) collective-permute-start(f32[8,128,128]{2,1,0:T(8,128)S(1)} %get-tuple-element.108), channel_id=1, source_target_pairs={{0,4},{4,0},{8,12},{12,8},{16,20},{20,16},{24,28},{28,24},{1,5},{5... | collective-permute-start | bytes 1572872 | tf_op jit(solution)/shard_map/ppermute | solution.py:576
  (35 other events, 67.2 us)

commit v2 on v1

--- a/solution.py
+++ b/solution.py
@@ -21,6 +21,18 @@
     return pltpu.CompilerParams(dimension_semantics=("arbitrary",), vmem_limit_bytes=mib * MIB)
 
 
+def in_vmem(*shape, kind=F32):
+    return pltpu.VMEM(shape, kind)
+
+
+def in_hbm(*shape, kind=F32):
+    return pltpu.HBM(shape, kind)
+
+
+def stay(*arrays):
+    return [pltpu.with_memory_space_constraint(array, pltpu.HBM) for array in arrays]
+
+
 def cost(flops, moved, exps=0):
     return pl.CostEstimate(flops=flops, bytes_accessed=moved, transcendentals=exps)
 
@@ -55,6 +67,16 @@
     return high, (matrix - high.astype(F32)).astype(BF16)
 
 
+def times_state(rows, state):
+    return dot(jnp.concatenate([rows, rows], axis=1), jnp.concatenate(two_parts(state), axis=0))
+
+
+def times_state_t(rows, state):
+    return dot_rows(
+        jnp.concatenate([rows, rows], axis=1), jnp.concatenate(two_parts(state), axis=1)
+    )
+
+
 def decay_matrix(row, columns):
     size = row.shape[1]
     lower = lax.broadcasted_iota(jnp.int32, (size, size), 0) >= lax.broadcasted_iota(
@@ -73,7 +95,9 @@
     return ref[pl.ds(head, tok, stride=heads), :]
 
 
-def state_kernel(core_ref, ld_ref, k_ref, v_ref, own_ref, send_ref, first_ref, kx, vx, cum, acc):
+def state_kernel(
+    core_ref, ld_ref, k_ref, v_ref, own_ref, send_ref, first_ref, log_ref, kx, vx, cum, acc
+):
     heads = ld_ref.shape[0]
     step = pl.program_id(0)
     per_block = BLOCK // STEP_TOK
@@ -83,28 +107,32 @@
     def _():
         for b in range(2):
             cum[b] = block_cum(ld_ref[:, b * BLOCK : (b + 1) * BLOCK])
-        acc[...] = jnp.zeros_like(acc)
-
-    to_rows(kx, k_ref)
-    to_rows(vx, v_ref)
-    b = step // per_block
-    at = pl.multiple_of((step % per_block) * STEP_TOK, STEP_TOK)
-    ends = cum[b, :, BLOCK - 1 : BLOCK]
-    scale = jnp.exp(ends - cum[b, :, pl.ds(at, STEP_TOK)])
-    for h in range(heads):
-        keys = head_rows(kx, h, heads, STEP_TOK).T * scale[h : h + 1]
-        values = head_rows(vx, h, heads, STEP_TOK).astype(BF16)
-        acc[b, h] += dot(keys.astype(BF16), values)
+        ends = cum[0, :, BLOCK - 1 :] + cum[1, :, BLOCK - 1 :]
+        log_ref[...] = jnp.broadcast_to(ends, log_ref.shape)
+
+    at = pl.multiple_of((step % per_block) * STEP_TOK * heads, STEP_TOK * heads)
+    to_rows(kx.at[pl.ds(at, STEP_TOK * heads)], k_ref)
+    to_rows(vx.at[pl.ds(at, STEP_TOK * heads)], v_ref)
+
+    def block_state(b, h):
+        row = cum[b, h : h + 1, :]
+        scale = jnp.exp(row[:, BLOCK - 1 :] - row)
+        keys = head_rows(kx, h, heads, BLOCK).T * scale
+        return dot(keys.astype(BF16), head_rows(vx, h, heads, BLOCK).astype(BF16))
+
+    @pl.when(step == per_block - 1)
+    def _():
+        for h in range(heads):
+            first_ref[h] = block_state(0, h)
 
     @pl.when(step == 2 * per_block - 1)
     def _():
-        first_ref[...] = acc[0]
         last = jnp.exp(cum[1, :, BLOCK - 1 : BLOCK])
         for h in range(heads):
-            acc[1, h] += last[h : h + 1, :] * acc[0, h]
+            acc[h] = block_state(1, h) + last[h : h + 1, :] * first_ref[h]
         core = core_ref[0]
-        own_ref[...] = acc[1, pl.ds(core * half, half)]
-        send_ref[...] = acc[1, pl.ds((1 - core) * half, half)]
+        own_ref[...] = acc[pl.ds(core * half, half)]
+        send_ref[...] = acc[pl.ds((1 - core) * half, half)]
 
 
 def local_state(core, log_decay, key_rows, value_rows):
@@ -116,22 +144,25 @@
         state_kernel,
         grid=(tok // STEP_TOK,),
         in_specs=[pl.BlockSpec(memory_space=pltpu.SMEM), whole(heads, tok), raw, raw],
-        out_specs=[whole(half, dim, dim), whole(half, dim, dim), whole(heads, dim, dim)],
+        out_specs=[
+            whole(half, dim, dim), whole(half, dim, dim), whole(heads, dim, dim), whole(heads, dim),
+        ],
         out_shape=[
-            jax.ShapeDtypeStruct((half, dim, dim), F32),
-            jax.ShapeDtypeStruct((half, dim, dim), F32),
-            jax.ShapeDtypeStruct((heads, dim, dim), F32),
+            in_vmem(half, dim, dim),
+            in_vmem(half, dim, dim),
+            in_hbm(heads, dim, dim),
+            in_vmem(heads, dim),
         ],
         scratch_shapes=[
-            pltpu.VMEM((STEP_TOK * heads, dim), F32),
-            pltpu.VMEM((STEP_TOK * heads, dim), F32),
+            pltpu.VMEM((BLOCK * heads, dim), F32),
+            pltpu.VMEM((BLOCK * heads, dim), F32),
             pltpu.VMEM((2, heads, BLOCK), F32),
-            pltpu.VMEM((2, heads, dim, dim), F32),
+            pltpu.VMEM((heads, dim, dim), F32),
         ],
         compiler_params=params(16),
         cost_estimate=cost(2 * tok * heads * dim * dim, 4 * tok * heads * dim),
         name="local_state",
-    )(core, log_decay, key_rows, value_rows)
+    )(core, *stay(log_decay, key_rows, value_rows))
 
 
 def intra_kernel(
@@ -164,16 +195,18 @@
         w_ref[i] = weights
         inner = dot(weights, value)
         if second:
-            high, low = two_parts(first_ref[i])
-            inner += jnp.exp(columns) * (dot(query, high) + dot(query, low))
+            inner += jnp.exp(columns) * times_state(query, first_ref[i])
         inner_ref[i] = inner
 
 
 def intra(index, log_decay, query_rows, key_rows, value_rows, output_grad, first):
     tok, heads, dim = key_rows.shape
-    raw = pl.BlockSpec((BLOCK, heads, dim), lambda i: (index, 0, 0))
+    raw = pl.BlockSpec(
+        (BLOCK, heads, dim), lambda i: (index, 0, 0), pipeline_mode=pl.Buffered(1)
+    )
     by_head = pl.BlockSpec((GROUP, BLOCK, dim), lambda i: (i, 0, 0))
-    head_shape = jax.ShapeDtypeStruct((heads, BLOCK, dim), BF16)
+    near = in_vmem(heads, BLOCK, dim, kind=BF16)
+    far = in_hbm(heads, BLOCK, dim, kind=BF16)
     return pl.pallas_call(
         functools.partial(intra_kernel, index > 0),
         grid=(heads // GROUP,),
@@ -183,17 +216,17 @@
             pl.BlockSpec((GROUP, dim, dim), lambda i: (i, 0, 0)),
         ],
         out_specs=[by_head] * 4 + [pl.BlockSpec((GROUP, BLOCK, BLOCK), lambda i: (i, 0, 0)), by_head],
-        out_shape=[head_shape] * 4 + [
-            jax.ShapeDtypeStruct((heads, BLOCK, BLOCK), BF16),
-            jax.ShapeDtypeStruct((heads, BLOCK, dim), F32),
+        out_shape=[near, far, far, near] + [
+            in_hbm(heads, BLOCK, BLOCK, kind=BF16),
+            in_vmem(heads, BLOCK, dim),
         ],
         scratch_shapes=[pltpu.VMEM((BLOCK * heads, dim), F32)] * 4 + [pltpu.VMEM((heads, BLOCK), F32)],
-        compiler_params=params(24),
+        compiler_params=params(20),
         cost_estimate=cost(
             2 * heads * BLOCK * BLOCK * dim * 4, 20 * heads * BLOCK * dim, heads * BLOCK * BLOCK
         ),
         name=f"intra_{index}",
-    )(log_decay, query_rows, key_rows, value_rows, output_grad, first)
+    )(log_decay, *stay(query_rows, key_rows, value_rows, output_grad, first))
 
 
 def whole_state(core, keep_ref, recv_ref, group, i):
@@ -219,11 +252,11 @@
 
     for i in range(GROUP):
         h = step * GROUP + i
-        high, low = two_parts(whole_state(core_ref[0], keep_ref, recv_ref, step, i))
+        state = whole_state(core_ref[0], keep_ref, recv_ref, step, i)
         gain = gain_ref[pl.ds(h, 1), :]
         for b, (q, o, inner, att) in enumerate(((q0, o0, inner0, att0), (q1, o1, inner1, att1))):
             columns = jnp.exp(as_columns(cum[b, pl.ds(h, 1), :]))
-            attended = inner[i] + columns * (dot(q[i], high) + dot(q[i], low))
+            attended = inner[i] + columns * times_state(q[i], state)
             att[i] = attended
             squares[b] += attended * attended
             products[b] += gain * o[i].astype(F32) * attended
@@ -245,14 +278,14 @@
     dim = HD
     whole = lambda *shape: pl.BlockSpec(shape, lambda i: (0,) * len(shape))
     by_head = pl.BlockSpec((GROUP, BLOCK, dim), lambda i: (i, 0, 0))
-    head_shape = jax.ShapeDtypeStruct((heads, BLOCK, dim), F32)
+    head_shape = in_vmem(heads, BLOCK, dim)
     return pl.pallas_call(
         attend_kernel,
         grid=(heads // GROUP,),
         in_specs=[pl.BlockSpec(memory_space=pltpu.SMEM), whole(heads, tok), whole(heads, dim)]
         + [whole(heads // 2, dim, dim)] * 2 + [by_head] * 6,
         out_specs=[by_head, by_head, whole(2, tok)],
-        out_shape=[head_shape, head_shape, jax.ShapeDtypeStruct((2, tok), F32)],
+        out_shape=[head_shape, head_shape, in_vmem(2, tok)],
         scratch_shapes=[
             pltpu.VMEM((2, heads, BLOCK), F32),
             pltpu.VMEM((2, BLOCK, dim), F32),
@@ -314,7 +347,7 @@
     half = heads // 2
     whole = lambda *shape: pl.BlockSpec(shape, lambda i: (0,) * len(shape))
     by_head = pl.BlockSpec((GROUP, BLOCK, dim), lambda i: (i, 0, 0))
-    head_shape = jax.ShapeDtypeStruct((heads, BLOCK, dim), BF16)
+    head_shape = in_hbm(heads, BLOCK, dim, kind=BF16)
     return pl.pallas_call(
         norm_grad_kernel,
         grid=(heads // GROUP,),
@@ -327,9 +360,9 @@
         ],
         out_shape=[
             head_shape, head_shape,
-            jax.ShapeDtypeStruct((half, dim, dim), F32),
-            jax.ShapeDtypeStruct((half, dim, dim), F32),
-            jax.ShapeDtypeStruct((heads, dim, dim), F32),
+            in_vmem(half, dim, dim),
+            in_vmem(half, dim, dim),
+            in_hbm(heads, dim, dim),
         ],
         scratch_shapes=[
             pltpu.VMEM((2, heads, BLOCK), F32),
@@ -396,8 +429,7 @@
             state = whole_state(core_ref[0], keep_ref, recv_ref, group, i)
             if second:
                 state = jnp.exp(cum[0, pl.ds(h, 1), :][:, BLOCK - 1 :]) * state + first_ref[i]
-            high, low = two_parts(state)
-            grad = dot(scores, k[i]) + jnp.exp(columns) * (dot_rows(g[i], high) + dot_rows(g[i], low))
+            grad = dot(scores, k[i]) + jnp.exp(columns) * times_state_t(g[i], state)
             rows[pl.ds(h, BLOCK, stride=heads), :] = grad
 
     @pl.when(b == 0)
@@ -440,7 +472,7 @@
         ],
         out_shape=[
             jax.ShapeDtypeStruct((tok, heads, dim), BF16),
-            jax.ShapeDtypeStruct((2, heads, BLOCK, BLOCK), BF16),
+            in_hbm(2, heads, BLOCK, BLOCK, kind=BF16),
         ],
         scratch_shapes=[pltpu.VMEM((2, heads, BLOCK), F32), pltpu.VMEM((BLOCK * heads, dim), F32)],
         compiler_params=two_level(16),
@@ -448,7 +480,7 @@
             4 * heads * tok * dim * (BLOCK + dim), 12 * heads * tok * dim, heads * tok * BLOCK
         ),
         name="grad_query",
-    )(core, log_decay, keep, recv, first, k0, k1, v0, v1, g0, g1)
+    )(core, log_decay, keep, recv, *stay(first, k0, k1, v0, v1, g0, g1))
 
 
 def transposed_dot(a, b):
@@ -468,11 +500,9 @@
         h = group * GROUP + i
         row = cum[pl.ds(h, 1), :]
         columns = as_columns(jnp.exp(row[:, BLOCK - 1 :] - row))
-        high, low = two_parts(second_ref[i])
-        dk0[i] = transposed_dot(gs_ref[0, i], q0[i]) + columns * (
-            dot_rows(v0[i], high) + dot_rows(v0[i], low)
-        )
-        dv0[i] = transposed_dot(w0[i], g0[i]) + columns * (dot(k0[i], high) + dot(k0[i], low))
+        state = second_ref[i]
+        dk0[i] = transposed_dot(gs_ref[0, i], q0[i]) + columns * times_state_t(v0[i], state)
+        dv0[i] = transposed_dot(w0[i], g0[i]) + columns * times_state(k0[i], state)
         dk1[i] = transposed_dot(gs_ref[1, i], q1[i])
         dv1[i] = transposed_dot(w1[i], g1[i])
 
@@ -492,12 +522,12 @@
             pl.BlockSpec((GROUP, dim, dim), lambda i: (i, 0, 0)),
         ],
         out_specs=[by_head] * 4,
-        out_shape=[jax.ShapeDtypeStruct((heads, BLOCK, dim), F32)] * 4,
+        out_shape=[in_hbm(heads, BLOCK, dim)] * 4,
         scratch_shapes=[pltpu.VMEM((heads, BLOCK), F32)],
         compiler_params=params(16),
         cost_estimate=cost(4 * heads * tok * dim * (BLOCK + dim), 30 * heads * tok * dim),
         name="grad_key_value",
-    )(log_decay, gs, w0, w1, q0, q1, k0, v0, g0, g1, second)
+    )(log_decay, *stay(gs, w0, w1), q0, q1, *stay(k0, v0, g0, g1, second))
 
 
 def finish_kernel(
@@ -520,13 +550,9 @@
             if not second:
                 left = left + cum[1, pl.ds(h, 1), :][:, BLOCK - 1 :]
             columns = as_columns(jnp.exp(left))
-            high, low = two_parts(whole_state(core_ref[0], keep_ref, recv_ref, group, i))
-            rows_k[pl.ds(h, BLOCK, stride=heads), :] = dk[i] + columns * (
-                dot_rows(v[i], high) + dot_rows(v[i], low)
-            )
-            rows_v[pl.ds(h, BLOCK, stride=heads), :] = dv[i] + columns * (
-                dot(k[i], high) + dot(k[i], low)
-            )
+            state = whole_state(core_ref[0], keep_ref, recv_ref, group, i)
+            rows_k[pl.ds(h, BLOCK, stride=heads), :] = dk[i] + columns * times_state_t(v[i], state)
+            rows_v[pl.ds(h, BLOCK, stride=heads), :] = dv[i] + columns * times_state(k[i], state)
 
     @pl.when(b == 0)
     def _():
@@ -568,7 +594,7 @@
         compiler_params=two_level(16),
         cost_estimate=cost(8 * heads * tok * dim * dim, 16 * heads * tok * dim),
         name="finish",
-    )(core, log_decay, keep, recv, k0, k1, v0, v1, dk0, dk1, dv0, dv1)
+    )(core, log_decay, keep, recv, *stay(k0, k1, v0, v1, dk0, dk1, dv0, dv1))
 
 
 def swap(value, axis, bit):
@@ -576,15 +602,93 @@
     return lax.ppermute(value, axis, [(i, i ^ bit) for i in range(count)])
 
 
-def quad_decays(log_total):
-    partner, row_same, row_other = (swap(log_total, "seq", bit) for bit in (1, 2, 3))
-    return (
-        jnp.exp(log_total), jnp.exp(partner), jnp.exp(log_total + partner),
-        jnp.exp(row_same + row_other),
-    )
-
-
-def entering_quad(own, send, decays, backward, tasks):
+def quad_scales(logs, backward):
+    log_total, log_partner, log_row_same, log_row_other = logs
+    mine = lax.axis_index("seq")
+    core = mine % 2
+    half = log_total.shape[0] // 2
+    bits = [(mine >> at) % 2 for at in range(3)]
+    if backward:
+        bits = [1 - bit for bit in bits]
+    late, right, low = (bit == 1 for bit in bits)
+    own, partner, chip, row = (
+        lax.dynamic_slice_in_dim(jnp.exp(part[:, 0]), core * half, half)
+        for part in (log_total, log_partner, log_total + log_partner, log_row_same + log_row_other)
+    )
+    one, zero = jnp.ones((half,), F32), jnp.zeros((half,), F32)
+    first = jnp.arange(half) < half // 2
+    pick = jnp.where
+    rows = [
+        pick(late, one, partner),
+        pick(late, own, one),
+        pick(right, one, row),
+        pick(first, pick(right, one, row), pick(low & right, zero, one)),
+        pick(first, pick(right, chip, one), pick(low, pick(right, one, chip), zero)),
+        pick(first, pick(right, one, zero), pick(low, pick(right, row, one), zero)),
+        pick(first, pick(low, pick(right, row, one), zero), pick(low | right, one, zero)),
+        pick(late, partner, one),
+        pick(late, one, zero),
+        pick(late, one, own),
+        pick(late, zero, one),
+    ]
+    table = jnp.stack(rows)[:, :, None]
+    return jnp.broadcast_to(table, table.shape[:2] + (HD,))
+
+
+def mix(body, scales, arrays, heads_out, name):
+    dim = HD
+
+    def kernel(scales_ref, *refs):
+        scale = lambda row, head: scales_ref[row, head : head + 1, :]
+        body(scale, refs[: len(arrays)], refs[len(arrays) :])
+
+    return pl.pallas_call(
+        kernel,
+        in_specs=[pl.BlockSpec(memory_space=pltpu.VMEM)] * (1 + len(arrays)),
+        out_specs=[pl.BlockSpec(memory_space=pltpu.VMEM)] * len(heads_out),
+        out_shape=[in_vmem(heads, dim, dim) for heads in heads_out],
+        compiler_params=pltpu.CompilerParams(vmem_limit_bytes=8 * MIB),
+        cost_estimate=cost(4 * 8 * dim * dim, 16 * 8 * dim * dim),
+        name=name,
+    )(scales, *arrays)
+
+
+def mix_total(scale, arrays, outputs):
+    own, got = arrays
+    first, second, second_scaled = outputs
+    quarter = first.shape[0]
+    for h in range(2 * quarter):
+        total = scale(0, h) * own[h] + scale(1, h) * got[h]
+        if h < quarter:
+            first[h] = total
+        else:
+            second[h - quarter] = total
+            second_scaled[h - quarter] = scale(2, h) * total
+
+
+def mix_next(scale, arrays, outputs):
+    quarter = arrays[0].shape[0]
+    for part in range(2):
+        total, got, out = arrays[part], arrays[2 + part], outputs[part]
+        for i in range(quarter):
+            h = part * quarter + i
+            out[i] = scale(3, h) * total[i] + scale(4, h) * got[i]
+
+
+def mix_enter(scale, arrays, outputs):
+    own, got = arrays[:2]
+    kept, sent = outputs
+    quarter = own.shape[0] // 2
+    for part in range(2):
+        one, two = arrays[2 + part], arrays[4 + part]
+        for i in range(quarter):
+            h = part * quarter + i
+            enter = scale(5, h) * one[i] + scale(6, h) * two[i]
+            kept[h] = scale(7, h) * enter + scale(8, h) * got[h]
+            sent[h] = scale(9, h) * enter + scale(10, h) * own[h]
+
+
+def entering_quad(own, send, scales, tasks, name):
     def work(stage, after, before=()):
         if stage not in tasks:
             return before
@@ -592,57 +696,23 @@
         outputs.extend(run(after))
         return lax.optimization_barrier((before, outputs[-1]))[0]
 
-    mine = lax.axis_index("seq")
-    core = mine % 2
     half = own.shape[0]
     quarter = half // 2
-    bits = [(mine >> at) % 2 for at in range(3)]
-    if backward:
-        bits = [1 - bit for bit in bits]
-    late, right, low = (bit == 1 for bit in bits)
-    d_own, d_partner, d_chip, d_row = (
-        lax.dynamic_slice_in_dim(part, core * half, half) for part in decays
-    )
-    one, zero = jnp.ones((quarter,), F32), jnp.zeros((quarter,), F32)
-    wide = lambda scale: scale[:, None, None]
-    whole_one = jnp.ones((half,), F32)
-
     got = swap(send, "seq", 1)
-    work(0, got)
-    total = wide(jnp.where(late, whole_one, d_partner)) * own + wide(
-        jnp.where(late, d_own, whole_one)
-    ) * got
-    first_total, second_total = total[:quarter], total[quarter:]
-    chip_a, chip_b = d_chip[:quarter], d_chip[quarter:]
-    row_a, row_b = d_row[:quarter], d_row[quarter:]
-
-    b0 = wide(jnp.where(right, one, row_b)) * second_total
-    a0, b0, total, = lax.optimization_barrier((first_total, b0, total))
-    a1 = swap(a0, "seq", 2)
-    b1 = swap(b0, "seq", 4)
-    a1, b1 = work(1, total, (a1, b1))
-    a2 = wide(jnp.where(right, one, row_a)) * first_total + wide(jnp.where(right, chip_a, one)) * a1
-    b2 = (
-        wide(jnp.where(low & right, zero, one)) * second_total
-        + wide(jnp.where(low, jnp.where(right, one, chip_b), zero)) * b1
-    )
-    a2, b2 = lax.optimization_barrier((a2, b2))
-    sent = a2
-    a2 = swap(a2, "seq", 4)
-    b2 = swap(b2, "seq", 2)
-    a2, b2 = work(2, sent, (a2, b2))
-    enter_a = (
-        wide(jnp.where(low, jnp.where(right, row_a, one), zero)) * a2
-        + wide(jnp.where(right, one, zero)) * a1
-    )
-    enter_b = (
-        wide(jnp.where(low, jnp.where(right, row_b, one), zero)) * b1
-        + wide(jnp.where(low | right, one, zero)) * b2
-    )
-    enter = jnp.concatenate([enter_a, enter_b], axis=0)
-    after = wide(jnp.where(late, d_partner, d_own)) * enter + jnp.where(late, got, own)
-    kept = jnp.where(late, after, enter)
-    sent = jnp.where(late, enter, after)
+    scales = scales()
+    first, second, scaled = mix(
+        mix_total, scales, (own, got), (quarter,) * 3, name + "_total"
+    )
+    one_a, one_b = swap(first, "seq", 2), swap(scaled, "seq", 4)
+    one_a, one_b = work(1, scaled, (one_a, one_b))
+    next_a, next_b = mix(
+        mix_next, scales, (first, second, one_a, one_b), (quarter,) * 2, name + "_next"
+    )
+    two_a, two_b = swap(next_a, "seq", 4), swap(next_b, "seq", 2)
+    two_a, two_b = work(2, next_b, (two_a, two_b))
+    kept, sent = mix(
+        mix_enter, scales, (own, got, one_a, one_b, two_a, two_b), (half,) * 2, name + "_enter"
+    )
     received = swap(sent, "seq", 1)
     work(3, sent)
     return kept, received
@@ -692,24 +762,23 @@
 
 def on_device(query_rows, key_rows, value_rows, output_grad, norm_gain, log_decay):
     core = (lax.axis_index("seq") % 2).astype(jnp.int32).reshape(1)
-    log_total = jnp.sum(log_decay, axis=1)
+    own, send, first, log_total = local_state(core, log_decay, key_rows, value_rows)
     if lax.axis_size("seq") == 8:
-        decays = quad_decays(log_total)
+        logs = []
+
+        def scales(backward):
+            if not logs:
+                logs.append(log_total)
+                logs.extend(swap(log_total, "seq", bit) for bit in (1, 2, 3))
+            return lambda: quad_scales(logs, backward)
+
         entering = lambda own, send, backward, tasks: entering_quad(
-            own, send, decays, backward, tasks
+            own, send, scales(backward), tasks, "later" if backward else "earlier"
         )
     else:
         entering = lambda own, send, backward, tasks: entering_any(
-            own, send, log_total, backward, tasks
+            own, send, log_total[:, 0], backward, tasks
         )
-
-    query_rows, key_rows, value_rows, output_grad = (
-        pltpu.with_memory_space_constraint(rows, pltpu.HBM)
-        for rows in (query_rows, key_rows, value_rows, output_grad)
-    )
-    own, send, first = local_state(
-        core, pltpu.with_memory_space_constraint(log_decay, pltpu.HBM), key_rows, value_rows
-    )
 
     def forward_task(index):
         return lambda earlier: intra(

time: 122 us -> 113 us (0.926)
  Pallas kernels: 53.5 us -> 71.5 us
  local copies, waits for them, and re-layouts: 28.8 us -> 12.6 us
  other arithmetic: 12.7 us -> 0.58 us
  waiting for transfers between devices: 8.55 us -> 11.1 us
    unnamed x100 -> x42, local copies, waits for them, and re-layouts: 28.6 us -> 12.3 us
    add x7 -> x0, other arithmetic: 9.43 us -> none  [the longest x2 3.97 us: entering_quad(): wide(jnp.where(low & right, zero, one)) * second_total]
    pallas_call x1, Pallas kernels: 4.7 us -> 9.85 us  [grad_key_value(): pl.pallas_call(grad_kv_kernel, grid=(heads // GROUP,), in_specs=[pl.Block...]
    pallas_call x1, Pallas kernels: 9.09 us -> 12.8 us  [finish(): pl.pallas_call(finish_kernel, grid=(2, groups), in_specs=[pl.BlockSpec(me...]
    pallas_call x1, Pallas kernels: 8.7 us -> 12 us  [grad_query(): pl.pallas_call(grad_q_kernel, grid=(2, groups), in_specs=[pl.BlockSpec(me...]
    ppermute x17, waiting for transfers between devices: 8.55 us -> 11.1 us  [swap(): return lax.ppermute(value, axis, [(i, i ^ bit) for i in range(count)])]
    mul x2 -> x0, other arithmetic: 1.82 us -> none  [entering_quad(): b0 = wide(jnp.where(right, one, row_b)) * second_total]
    pallas_call x1, Pallas kernels: 6.03 us -> 7.83 us  [local_state(): pl.pallas_call(state_kernel, grid=(tok // STEP_TOK,), in_specs=[pl.BlockS...]
  transfers between devices with their start and end apart: 17 -> 17, of which waited for: 5 -> 6; matrix products, arithmetic and copies ran while one was open for 0% -> 1% of each run, Pallas kernels for 32% -> 38%
where the time goes in v2:
time: 113 us
  Pallas kernels  71.5 us (63%)
  starting transfers between devices  15.9 us (14%)
  local copies, waits for them, and re-layouts  12.6 us (11%)
  waiting for transfers between devices  11.1 us (10%)
    pallas_call x2, Pallas kernels, intra(): pl.pallas_call(functools.partial(intra_kernel, index > 0), grid=(heads //...  17.1 us
    ppermute x17, starting transfers between devices, swap(): return lax.ppermute(value, axis, [(i, i ^ bit) for i in range(count)])  15.9 us
    pallas_call x1, Pallas kernels, finish(): pl.pallas_call(finish_kernel, grid=(2, groups), in_specs=[pl.BlockSpec(me...  12.8 us
    unnamed x42, local copies, waits for them, and re-layouts  12.3 us
    pallas_call x1, Pallas kernels, grad_query(): pl.pallas_call(grad_q_kernel, grid=(2, groups), in_specs=[pl.BlockSpec(me...  12 us
    ppermute x17, waiting for transfers between devices, swap(): return lax.ppermute(value, axis, [(i, i ^ bit) for i in range(count)])  11.1 us
    pallas_call x1, Pallas kernels, grad_key_value(): pl.pallas_call(grad_kv_kernel, grid=(heads // GROUP,), in_specs=[pl.Block...  9.85 us
    pallas_call x1, Pallas kernels, local_state(): pl.pallas_call(state_kernel, grid=(tok // STEP_TOK,), in_specs=[pl.BlockS...  7.83 us
  transfers between devices with their start and end apart: 17, of which 6 were waited for; matrix products, arithmetic and copies ran while one was open for 1% of the time, Pallas kernels for 38%

profile of v2, /device:TPU:0, one launch (start us, length us, event | category | flops | bytes accessed | tf_op | source)
XLA Modules:
  0.0 112.6 jit_solution(1949209628421278224)
XLA Ops:
  0.7 7.8 %local_state.1 = (f32[8,128,128]{2,1,0:T(8,128)S(1)}, f32[8,128,128]{2,1,0:T(8,128)S(1)}, f32[16,128,128]{2,1,0:T(8,128)}, f32[16,128]{1,0:T(8,128)S(1)}) custom-call(s32[1]{0:T(128)} %bitcast.core_ref, f32[16,512]{1,0:T(8,128)} %ld_ref.15, bf16[512,16,128]{2,1,0:T(8,128)(2,1)} %k_ref.5, bf16[512,16,128]{2,1,0:T(8,128)(2,1)} %v_ref.5), custom_call_target="tpu_custom_call" | custom-call | flops 268435456 | bytes 4194304 | tf_op jit(solution)/shard_map/local_state/pallas_call | solution.py:143
  8.9 2.6 %collective-permute-start.2 = (f32[16,128]{1,0:T(8,128)S(1)}, f32[16,128]{1,0:T(8,128)S(1)}, u32[]{:S(2)}, u32[]{:S(2)}) collective-permute-start(f32[16,128]{1,0:T(8,128)S(1)} %get-tuple-element.63), channel_id=1, source_target_pairs={{0,12},{4,8},{8,4},{12,0},{16,28},{20,24},{24,20},{28,16},{1,13},{... | collective-permute-start | bytes 24584 | tf_op jit(solution)/shard_map/ppermute | solution.py:602
  12.0 0.9 collective-permute-done.2
  12.9 2.3 %collective-permute-done.1 = f32[16,128]{1,0:T(8,128)S(1)} collective-permute-done((f32[16,128]{1,0:T(8,128)S(1)}, f32[16,128]{1,0:T(8,128)S(1)}, u32[]{:S(2)}, u32[]{:S(2)}) %collective-permute-start.1) | collective-permute-done | bytes 8224 | tf_op jit(solution)/shard_map/ppermute | solution.py:602
  15.9 2.0 %collective-permute-start.5 = (f32[4,128,128]{2,1,0:T(8,128)S(1)}, f32[4,128,128]{2,1,0:T(8,128)S(1)}, u32[]{:S(2)}, u32[]{:S(2)}) collective-permute-start(f32[4,128,128]{2,1,0:T(8,128)S(1)} %get-tuple-element.67), channel_id=1, source_target_pairs={{0,16},{4,20},{8,24},{12,28},{16,0},{20,4},{24,8},{28,12},{1,17},{... | collective-permute-start | bytes 786440 | tf_op jit(solution)/shard_map/ppermute | solution.py:602
  17.8 8.4 %intra_0.1 = (bf16[16,256,128]{2,1,0:T(8,128)(2,1)S(1)}, bf16[16,256,128]{2,1,0:T(8,128)(2,1)}, bf16[16,256,128]{2,1,0:T(8,128)(2,1)}, bf16[16,256,128]{2,1,0:T(...) custom-call(f32[16,512]{1,0:T(8,128)S(1)} %copy-done.8, bf16[512,16,128]{2,1,0:T(8,128)(2,1)} %q_ref.3, ...), custom_call_target="tpu_custom_call" | custom-call | flops 1073741824 | bytes 10485760 | tf_op jit(solution)/shard_map/intra_0/pallas_call | solution.py:210
  26.4 1.9 %collective-permute-start.7 = (f32[4,128,128]{2,1,0:T(8,128)S(1)}, f32[4,128,128]{2,1,0:T(8,128)S(1)}, u32[]{:S(2)}, u32[]{:S(2)}) collective-permute-start(f32[4,128,128]{2,1,0:T(8,128)S(1)} %get-tuple-element.75), channel_id=1, source_target_pairs={{0,8},{4,12},{8,0},{12,4},{16,24},{20,28},{24,16},{28,20},{1,9},{5... | collective-permute-start | bytes 786440 | tf_op jit(solution)/shard_map/ppermute | solution.py:602
  28.4 8.8 %intra_1.1 = (bf16[16,256,128]{2,1,0:T(8,128)(2,1)S(1)}, bf16[16,256,128]{2,1,0:T(8,128)(2,1)}, bf16[16,256,128]{2,1,0:T(8,128)(2,1)}, bf16[16,256,128]{2,1,0:T(...) custom-call(f32[16,512]{1,0:T(8,128)S(1)} %copy-done.8, bf16[512,16,128]{2,1,0:T(8,128)(2,1)} %q_ref.3, ...), custom_call_target="tpu_custom_call" | custom-call | flops 1073741824 | bytes 10485760 | tf_op jit(solution)/shard_map/intra_1/pallas_call | solution.py:210
  37.5 1.9 %collective-permute-done.8.recv_ref = f32[8,128,128]{2,1,0:T(8,128)S(1)} collective-permute-done((f32[8,128,128]{2,1,0:T(8,128)S(1)}, f32[8,128,128]{2,1,0:T(8,128)S(1)}, u32[]{:S(2)}, u32[]{:S(2)}) %collective-permute-start.8) | collective-permute-done | bytes 524320 | tf_op jit(solution)/shard_map/ppermute | solution.py:602
  39.4 3.4 %attend.1 = (f32[16,256,128]{2,1,0:T(8,128)S(1)}, f32[16,256,128]{2,1,0:T(8,128)S(1)}, f32[2,512]{1,0:T(2,128)S(1)}) custom-call(s32[1]{0:T(128)} %bitcast.core_ref, f32[16,512]{1,0:T(8,128)S(1)} %copy-done.8, f32[16,128]{1,0:T(8,128)S(1)} %copy-done.20, f32[8,128,128]{2,1,0:T(8,128)S(1)} %get-tuple-element.80.keep_ref, ...), custom_call_target="tpu_custom_call" | custom-call | flops 536870912 | bytes 16777216 | tf_op jit(solution)/shard_map/attend/pallas_call | solution.py:282
  42.8 1.3 %copy-done = f32[16,256,128]{2,1,0:T(8,128)} copy-done((f32[16,256,128]{2,1,0:T(8,128)}, f32[16,256,128]{2,1,0:T(8,128)S(1)}, u32[]{:S(2)}) %copy-start) | copy-done | bytes 2097176
  44.2 1.3 %copy-done.3 = f32[16,256,128]{2,1,0:T(8,128)} copy-done((f32[16,256,128]{2,1,0:T(8,128)}, f32[16,256,128]{2,1,0:T(8,128)S(1)}, u32[]{:S(2)}) %copy-start.3) | copy-done | bytes 2097176
  45.5 1.6 %collective-permute-start.9 = (f32[2,512]{1,0:T(2,128)S(1)}, f32[2,512]{1,0:T(2,128)S(1)}, u32[]{:S(2)}, u32[]{:S(2)}) collective-permute-start(f32[2,512]{1,0:T(2,128)S(1)} %get-tuple-element.86), channel_id=1, source_target_pairs={{0,1},{1,0},{2,3},{3,2},{4,5},{5,4},{6,7},{7,6},{8,9},{9,8},{10,11... | collective-permute-start | bytes 12296 | tf_op jit(solution)/shard_map/ppermute | solution.py:602
  47.0 2.0 %collective-permute-done.9 = f32[2,512]{1,0:T(2,128)S(1)} collective-permute-done((f32[2,512]{1,0:T(2,128)S(1)}, f32[2,512]{1,0:T(2,128)S(1)}, u32[]{:S(2)}, u32[]{:S(2)}) %collective-permute-start.9) | collective-permute-done | bytes 4128 | tf_op jit(solution)/shard_map/ppermute | solution.py:602
  49.1 2.6 %collective-permute-start.10 = (f32[2,512]{1,0:T(2,128)S(1)}, f32[2,512]{1,0:T(2,128)S(1)}, u32[]{:S(2)}, u32[]{:S(2)}) collective-permute-start(f32[2,512]{1,0:T(2,128)S(1)} %add.49), channel_id=1, source_target_pairs={{0,2},{1,3},{2,0},{3,1},{4,6},{5,7},{6,4},{7,5},{8,10},{9,11},{10,... | collective-permute-start | bytes 12296 | tf_op jit(solution)/shard_map/ppermute | solution.py:602
  51.7 1.9 %collective-permute-done.10 = f32[2,512]{1,0:T(2,128)S(1)} collective-permute-done((f32[2,512]{1,0:T(2,128)S(1)}, f32[2,512]{1,0:T(2,128)S(1)}, u32[]{:S(2)}, u32[]{:S(2)}) %collective-permute-start.10) | collective-permute-done | bytes 4128 | tf_op jit(solution)/shard_map/ppermute | solution.py:602
  53.6 1.6 %copy-done.1 = f32[16,256,128]{2,1,0:T(8,128)S(1)} copy-done((f32[16,256,128]{2,1,0:T(8,128)S(1)}, f32[16,256,128]{2,1,0:T(8,128)}, u32[]{:S(2)}) %copy-start.1) | copy-done | bytes 2097176
  55.2 1.6 %copy-done.4 = f32[16,256,128]{2,1,0:T(8,128)S(1)} copy-done((f32[16,256,128]{2,1,0:T(8,128)S(1)}, f32[16,256,128]{2,1,0:T(8,128)}, u32[]{:S(2)}) %copy-start.4) | copy-done | bytes 2097176
  56.8 1.2 %copy-done.7 = bf16[16,256,128]{2,1,0:T(8,128)(2,1)S(1)} copy-done((bf16[16,256,128]{2,1,0:T(8,128)(2,1)S(1)}, bf16[16,256,128]{2,1,0:T(8,128)(2,1)}, u32[]{:S(2)}) %copy-start.7) | copy-done | bytes 1048600
  58.0 4.1 %norm_grad.1 = (bf16[16,256,128]{2,1,0:T(8,128)(2,1)}, bf16[16,256,128]{2,1,0:T(8,128)(2,1)}, f32[8,128,128]{2,1,0:T(8,128)S(1)}, f32[8,128,128]{2,1,0:T(8,128)}, f32[16,128,128]{2,1,0:T(8,128)}) custom-call(s32[1]{0:T(128)} %bitcast.core_ref, f32[16,512]{1,0:T(8,128)S(1)} %copy-done.8, f32[16,128]{1,0:T(8,128)S(1)} %copy-done.20, ...), custom_call_target="tpu_custom_call" | custom-call | flops 268435456 | bytes 14680064 | tf_op jit(solution)/shard_map/norm_grad/pallas_call | solution.py:351
  62.2 0.8 copy-done.17
  63.1 2.0 %collective-permute-done.11.refs_1_ = f32[8,128,128]{2,1,0:T(8,128)S(1)} collective-permute-done((f32[8,128,128]{2,1,0:T(8,128)}, f32[8,128,128]{2,1,0:T(8,128)S(1)}, u32[]{:S(2)}, u32[]{:S(2)}) %collective-permute-start.11) | collective-permute-done | bytes 524320 | tf_op jit(solution)/shard_map/ppermute | solution.py:602
  65.2 1.0 copy-done.18
  66.5 1.9 %collective-permute-start.13 = (f32[4,128,128]{2,1,0:T(8,128)S(1)}, f32[4,128,128]{2,1,0:T(8,128)S(1)}, u32[]{:S(2)}, u32[]{:S(2)}) collective-permute-start(f32[4,128,128]{2,1,0:T(8,128)S(1)} %get-tuple-element.92), channel_id=1, source_target_pairs={{0,16},{4,20},{8,24},{12,28},{16,0},{20,4},{24,8},{28,12},{1,17},{... | collective-permute-start | bytes 786440 | tf_op jit(solution)/shard_map/ppermute | solution.py:602
  68.4 1.0 copy-done.10
  69.5 1.0 copy-done.12
  70.5 12.0 %grad_query.1 = (bf16[512,16,128]{2,1,0:T(8,128)(2,1)}, bf16[2,16,256,256]{3,2,1,0:T(8,128)(2,1)}) custom-call(s32[1]{0:T(128)} %bitcast.core_ref, f32[16,512]{1,0:T(8,128)S(1)} %copy-done.8, f32[8,128,128]{2,1,0:T(8,128)S(1)} %copy-done.10, f32[8,128,128]{2,1,0:T(8,128)S(1)} %copy-done.12, f32[16,128,128]{2,1,0:T(8,128)} %get-tuple-element.93.first_ref, ...), custom_call_target="tpu_custom_call" | custom-call | flops 1610612736 | bytes 12582912 | tf_op jit(solution)/shard_map/grad_query/pallas_call | solution.py:461
  82.8 1.8 %collective-permute-start.15 = (f32[4,128,128]{2,1,0:T(8,128)S(1)}, f32[4,128,128]{2,1,0:T(8,128)S(1)}, u32[]{:S(2)}, u32[]{:S(2)}) collective-permute-start(f32[4,128,128]{2,1,0:T(8,128)S(1)} %get-tuple-element.105), channel_id=1, source_target_pairs={{0,8},{4,12},{8,0},{12,4},{16,24},{20,28},{24,16},{28,20},{1,9},{5... | collective-permute-start | bytes 786440 | tf_op jit(solution)/shard_map/ppermute | solution.py:602
  84.7 9.8 %grad_key_value.1 = (f32[16,256,128]{2,1,0:T(8,128)}, f32[16,256,128]{2,1,0:T(8,128)}, f32[16,256,128]{2,1,0:T(8,128)}, f32[16,256,128]{2,1,0:T(8,128)}) custom-call(f32[16,512]{1,0:T(8,128)S(1)} %copy-done.8, bf16[2,16,256,256]{3,2,1,0:T(8,128)(2,1)} %get-tuple-element.100.gs_ref, bf16[16,256,256]{2,1,0:T(8,128)(2,1)} %get-tuple-element.106.w0, ...), custom_call_target="tpu_custom_call" | custom-call | flops 1610612736 | bytes 31457280 | tf_op jit(solution)/shard_map/grad_key_value/pallas_call | solution.py:515
  94.8 1.3 %copy-done.2 = f32[16,256,128]{2,1,0:T(8,128)S(1)} copy-done((f32[16,256,128]{2,1,0:T(8,128)S(1)}, f32[16,256,128]{2,1,0:T(8,128)}, u32[]{:S(2)}) %copy-start.2) | copy-done | bytes 2097176
  96.1 3.6 %normed_rows.1 = bf16[512,16,128]{2,1,0:T(8,128)(2,1)} custom-call(f32[16,128]{1,0:T(8,128)S(1)} %copy-done.20, f32[2,512]{1,0:T(2,128)S(1)} %add.50.sums_ref, f32[16,256,128]{2,1,0:T(8,128)S(1)} %copy-done.2, f32[16,256,128]{2,1,0:T(8,128)S(1)} %copy-done.5), custom_call_target="tpu_custom_call" | custom-call | flops 3145728 | bytes 6291456 | tf_op jit(solution)/shard_map/normed_rows/pallas_call | solution.py:397
  99.8 12.8 %finish.1 = (bf16[512,16,128]{2,1,0:T(8,128)(2,1)}, bf16[512,16,128]{2,1,0:T(8,128)(2,1)}) custom-call(s32[1]{0:T(128)} %bitcast.core_ref, f32[16,512]{1,0:T(8,128)S(1)} %copy-done.8, f32[8,128,128]{2,1,0:T(8,128)S(1)} %get-tuple-element.116.keep_ref, f32[8,128,128]{2,1,0:T(8,128)S(1)} %collective-permute-done.16.recv_ref, ...), custom_call_target="tpu_custom_call" | custom-call | flops 1073741824 | bytes 16777216 | tf_op jit(solution)/shard_map/finish/pallas_call | solution.py:580
  (78 shorter events, 3.1 us)
Async XLA Ops:
  0.6 17.2 %copy-start.8 = (f32[16,512]{1,0:T(8,128)S(1)}, f32[16,512]{1,0:T(8,128)}, u32[]{:S(2)}) copy-start(f32[16,512]{1,0:T(8,128)} %ld_ref.15) | copy-start | bytes 98308
  8.5 9.4 %copy-start.13 = (f32[8,128,128]{2,1,0:T(8,128)}, f32[8,128,128]{2,1,0:T(8,128)S(1)}, u32[]{:S(2)}) copy-start(f32[8,128,128]{2,1,0:T(8,128)S(1)} %get-tuple-element.64.refs_0_) | copy-start | bytes 1572868
  8.5 3.4 %collective-permute-start = (f32[16,128]{1,0:T(8,128)S(1)}, f32[16,128]{1,0:T(8,128)S(1)}, u32[]{:S(2)}, u32[]{:S(2)}) collective-permute-start(f32[16,128]{1,0:T(8,128)S(1)} %get-tuple-element.63), channel_id=1, source_target_pairs={{0,4},{4,0},{8,12},{12,8},{16,20},{20,16},{24,28},{28,24},{1,5},{5... | collective-permute-start | bytes 24584 | tf_op jit(solution)/shard_map/ppermute | solution.py:602
  8.9 4.0 %collective-permute-start.2 = (f32[16,128]{1,0:T(8,128)S(1)}, f32[16,128]{1,0:T(8,128)S(1)}, u32[]{:S(2)}, u32[]{:S(2)}) collective-permute-start(f32[16,128]{1,0:T(8,128)S(1)} %get-tuple-element.63), channel_id=1, source_target_pairs={{0,12},{4,8},{8,4},{12,0},{16,28},{20,24},{24,20},{28,16},{1,13},{... | collective-permute-start | bytes 24584 | tf_op jit(solution)/shard_map/ppermute | solution.py:602
  11.5 3.7 %collective-permute-start.1 = (f32[16,128]{1,0:T(8,128)S(1)}, f32[16,128]{1,0:T(8,128)S(1)}, u32[]{:S(2)}, u32[]{:S(2)}) collective-permute-start(f32[16,128]{1,0:T(8,128)S(1)} %get-tuple-element.63), channel_id=1, source_target_pairs={{0,8},{4,12},{8,0},{12,4},{16,24},{20,28},{24,16},{28,20},{1,9},{5... | collective-permute-start | bytes 24584 | tf_op jit(solution)/shard_map/ppermute | solution.py:602
  11.6 4.0 %collective-permute-start.3 = (f32[8,128,128]{2,1,0:T(8,128)S(1)}, f32[8,128,128]{2,1,0:T(8,128)S(1)}, u32[]{:S(2)}, u32[]{:S(2)}) collective-permute-start(f32[8,128,128]{2,1,0:T(8,128)S(1)} %get-tuple-element.65), channel_id=1, source_target_pairs={{0,4},{4,0},{8,12},{12,8},{16,20},{20,16},{24,28},{28,24},{1,5},{5... | collective-permute-start | bytes 1572872 | tf_op jit(solution)/shard_map/ppermute | solution.py:602
  15.5 2.3 %copy-start.15 = (f32[8,128,128]{2,1,0:T(8,128)}, f32[8,128,128]{2,1,0:T(8,128)S(1)}, u32[]{:S(2)}) copy-start(f32[8,128,128]{2,1,0:T(8,128)S(1)} %collective-permute-done.3.refs_1_) | copy-start | bytes 1572868
  15.7 10.5 %collective-permute-start.4 = (f32[4,128,128]{2,1,0:T(8,128)S(1)}, f32[4,128,128]{2,1,0:T(8,128)S(1)}, u32[]{:S(2)}, u32[]{:S(2)}) collective-permute-start(f32[4,128,128]{2,1,0:T(8,128)S(1)} %get-tuple-element.66.refs_0_), channel_id=1, source_target_pairs={{0,8},{4,12},{8,0},{12,4},{16,24},{20,28},{24,16},{28,20},{1,9},{5... | collective-permute-start | bytes 786440 | tf_op jit(solution)/shard_map/ppermute | solution.py:602
  15.9 10.4 %collective-permute-start.5 = (f32[4,128,128]{2,1,0:T(8,128)S(1)}, f32[4,128,128]{2,1,0:T(8,128)S(1)}, u32[]{:S(2)}, u32[]{:S(2)}) collective-permute-start(f32[4,128,128]{2,1,0:T(8,128)S(1)} %get-tuple-element.67), channel_id=1, source_target_pairs={{0,16},{4,20},{8,24},{12,28},{16,0},{20,4},{24,8},{28,12},{1,17},{... | collective-permute-start | bytes 786440 | tf_op jit(solution)/shard_map/ppermute | solution.py:602
  26.3 10.8 %collective-permute-start.6 = (f32[4,128,128]{2,1,0:T(8,128)S(1)}, f32[4,128,128]{2,1,0:T(8,128)S(1)}, u32[]{:S(2)}, u32[]{:S(2)}) collective-permute-start(f32[4,128,128]{2,1,0:T(8,128)S(1)} %get-tuple-element.74), channel_id=1, source_target_pairs={{0,16},{4,20},{8,24},{12,28},{16,0},{20,4},{24,8},{28,12},{1,17},{... | collective-permute-start | bytes 786440 | tf_op jit(solution)/shard_map/ppermute | solution.py:602
  26.4 10.7 %copy-start.14 = (f32[8,128,128]{2,1,0:T(8,128)S(1)}, f32[8,128,128]{2,1,0:T(8,128)}, u32[]{:S(2)}) copy-start(f32[8,128,128]{2,1,0:T(8,128)} %copy-done.13) | copy-start | bytes 1572868
  26.4 10.7 %copy-start.16 = (f32[8,128,128]{2,1,0:T(8,128)S(1)}, f32[8,128,128]{2,1,0:T(8,128)}, u32[]{:S(2)}) copy-start(f32[8,128,128]{2,1,0:T(8,128)} %copy-done.15) | copy-start | bytes 1572868
  26.4 10.7 %collective-permute-start.7 = (f32[4,128,128]{2,1,0:T(8,128)S(1)}, f32[4,128,128]{2,1,0:T(8,128)S(1)}, u32[]{:S(2)}, u32[]{:S(2)}) collective-permute-start(f32[4,128,128]{2,1,0:T(8,128)S(1)} %get-tuple-element.75), channel_id=1, source_target_pairs={{0,8},{4,12},{8,0},{12,4},{16,24},{20,28},{24,16},{28,20},{1,9},{5... | collective-permute-start | bytes 786440 | tf_op jit(solution)/shard_map/ppermute | solution.py:602
  37.1 5.7 %copy-start.6 = (bf16[16,256,128]{2,1,0:T(8,128)(2,1)}, bf16[16,256,128]{2,1,0:T(8,128)(2,1)S(1)}, u32[]{:S(2)}) copy-start(bf16[16,256,128]{2,1,0:T(8,128)(2,1)S(1)} %get-tuple-element.85.o1) | copy-start | bytes 3145732
  37.1 2.2 %copy-start.20 = (f32[16,128]{1,0:T(8,128)S(1)}, f32[16,128]{1,0:T(8,128)}, u32[]{:S(2)}) copy-start(f32[16,128]{1,0:T(8,128)} %gain_ref.4) | copy-start | bytes 24580
  37.4 5.4 %copy-start.9 = (f32[8,128,128]{2,1,0:T(8,128)}, f32[8,128,128]{2,1,0:T(8,128)S(1)}, u32[]{:S(2)}) copy-start(f32[8,128,128]{2,1,0:T(8,128)S(1)} %get-tuple-element.80.keep_ref) | copy-start | bytes 1572868
  37.4 2.0 %collective-permute-start.8 = (f32[8,128,128]{2,1,0:T(8,128)S(1)}, f32[8,128,128]{2,1,0:T(8,128)S(1)}, u32[]{:S(2)}, u32[]{:S(2)}) collective-permute-start(f32[8,128,128]{2,1,0:T(8,128)S(1)} %get-tuple-element.81), channel_id=1, source_target_pairs={{0,4},{4,0},{8,12},{12,8},{16,20},{20,16},{24,28},{28,24},{1,5},{5... | collective-permute-start | bytes 1572872 | tf_op jit(solution)/shard_map/ppermute | solution.py:602
  39.4 3.5 %copy-start.11 = (f32[8,128,128]{2,1,0:T(8,128)}, f32[8,128,128]{2,1,0:T(8,128)S(1)}, u32[]{:S(2)}) copy-start(f32[8,128,128]{2,1,0:T(8,128)S(1)} %collective-permute-done.8.recv_ref) | copy-start | bytes 1572868
  42.8 1.3 %copy-start = (f32[16,256,128]{2,1,0:T(8,128)}, f32[16,256,128]{2,1,0:T(8,128)S(1)}, u32[]{:S(2)}) copy-start(f32[16,256,128]{2,1,0:T(8,128)S(1)} %get-tuple-element.87.att0) | copy-start | bytes 6291460
  45.5 3.6 %collective-permute-start.9 = (f32[2,512]{1,0:T(2,128)S(1)}, f32[2,512]{1,0:T(2,128)S(1)}, u32[]{:S(2)}, u32[]{:S(2)}) collective-permute-start(f32[2,512]{1,0:T(2,128)S(1)} %get-tuple-element.86), channel_id=1, source_target_pairs={{0,1},{1,0},{2,3},{3,2},{4,5},{5,4},{6,7},{7,6},{8,9},{9,8},{10,11... | collective-permute-start | bytes 12296 | tf_op jit(solution)/shard_map/ppermute | solution.py:602
  49.1 4.5 %collective-permute-start.10 = (f32[2,512]{1,0:T(2,128)S(1)}, f32[2,512]{1,0:T(2,128)S(1)}, u32[]{:S(2)}, u32[]{:S(2)}) collective-permute-start(f32[2,512]{1,0:T(2,128)S(1)} %add.49), channel_id=1, source_target_pairs={{0,2},{1,3},{2,0},{3,1},{4,6},{5,7},{6,4},{7,5},{8,10},{9,11},{10,... | collective-permute-start | bytes 12296 | tf_op jit(solution)/shard_map/ppermute | solution.py:602
  53.6 1.6 %copy-start.1 = (f32[16,256,128]{2,1,0:T(8,128)S(1)}, f32[16,256,128]{2,1,0:T(8,128)}, u32[]{:S(2)}) copy-start(f32[16,256,128]{2,1,0:T(8,128)} %copy-done) | copy-start | bytes 6291460
  55.2 1.6 %copy-start.4 = (f32[16,256,128]{2,1,0:T(8,128)S(1)}, f32[16,256,128]{2,1,0:T(8,128)}, u32[]{:S(2)}) copy-start(f32[16,256,128]{2,1,0:T(8,128)} %copy-done.3) | copy-start | bytes 6291460
  63.0 2.1 %collective-permute-start.11 = (f32[8,128,128]{2,1,0:T(8,128)}, f32[8,128,128]{2,1,0:T(8,128)S(1)}, u32[]{:S(2)}, u32[]{:S(2)}) collective-permute-start(f32[8,128,128]{2,1,0:T(8,128)} %get-tuple-element.90), channel_id=1, source_target_pairs={{0,4},{4,0},{8,12},{12,8},{16,20},{20,16},{24,28},{28,24},{1,5},{5... | collective-permute-start | bytes 1572872 | tf_op jit(solution)/shard_map/ppermute | solution.py:602
  66.3 16.2 %collective-permute-start.12 = (f32[4,128,128]{2,1,0:T(8,128)S(1)}, f32[4,128,128]{2,1,0:T(8,128)S(1)}, u32[]{:S(2)}, u32[]{:S(2)}) collective-permute-start(f32[4,128,128]{2,1,0:T(8,128)S(1)} %get-tuple-element.91.refs_0_), channel_id=1, source_target_pairs={{0,8},{4,12},{8,0},{12,4},{16,24},{20,28},{24,16},{28,20},{1,9},{5... | collective-permute-start | bytes 786440 | tf_op jit(solution)/shard_map/ppermute | solution.py:602
  66.5 16.0 %collective-permute-start.13 = (f32[4,128,128]{2,1,0:T(8,128)S(1)}, f32[4,128,128]{2,1,0:T(8,128)S(1)}, u32[]{:S(2)}, u32[]{:S(2)}) collective-permute-start(f32[4,128,128]{2,1,0:T(8,128)S(1)} %get-tuple-element.92), channel_id=1, source_target_pairs={{0,16},{4,20},{8,24},{12,28},{16,0},{20,4},{24,8},{28,12},{1,17},{... | collective-permute-start | bytes 786440 | tf_op jit(solution)/shard_map/ppermute | solution.py:602
  82.6 11.9 %collective-permute-start.14 = (f32[4,128,128]{2,1,0:T(8,128)S(1)}, f32[4,128,128]{2,1,0:T(8,128)S(1)}, u32[]{:S(2)}, u32[]{:S(2)}) collective-permute-start(f32[4,128,128]{2,1,0:T(8,128)S(1)} %get-tuple-element.104), channel_id=1, source_target_pairs={{0,16},{4,20},{8,24},{12,28},{16,0},{20,4},{24,8},{28,12},{1,17},{... | collective-permute-start | bytes 786440 | tf_op jit(solution)/shard_map/ppermute | solution.py:602
  82.8 11.7 %collective-permute-start.15 = (f32[4,128,128]{2,1,0:T(8,128)S(1)}, f32[4,128,128]{2,1,0:T(8,128)S(1)}, u32[]{:S(2)}, u32[]{:S(2)}) collective-permute-start(f32[4,128,128]{2,1,0:T(8,128)S(1)} %get-tuple-element.105), channel_id=1, source_target_pairs={{0,8},{4,12},{8,0},{12,4},{16,24},{20,28},{24,16},{28,20},{1,9},{5... | collective-permute-start | bytes 786440 | tf_op jit(solution)/shard_map/ppermute | solution.py:602
  84.7 9.9 %copy-start.19 = (f32[8,128,128]{2,1,0:T(8,128)S(1)}, f32[8,128,128]{2,1,0:T(8,128)}, u32[]{:S(2)}) copy-start(f32[8,128,128]{2,1,0:T(8,128)} %copy-done.17) | copy-start | bytes 1572868
  84.7 10.2 %copy-start.5 = (f32[16,256,128]{2,1,0:T(8,128)S(1)}, f32[16,256,128]{2,1,0:T(8,128)}, u32[]{:S(2)}) copy-start(f32[16,256,128]{2,1,0:T(8,128)} %copy-done.3) | copy-start | bytes 6291460
  94.5 1.6 %copy-start.2 = (f32[16,256,128]{2,1,0:T(8,128)S(1)}, f32[16,256,128]{2,1,0:T(8,128)}, u32[]{:S(2)}) copy-start(f32[16,256,128]{2,1,0:T(8,128)} %copy-done) | copy-start | bytes 6291460
  94.7 5.0 %collective-permute-start.16 = (f32[8,128,128]{2,1,0:T(8,128)S(1)}, f32[8,128,128]{2,1,0:T(8,128)S(1)}, u32[]{:S(2)}, u32[]{:S(2)}) collective-permute-start(f32[8,128,128]{2,1,0:T(8,128)S(1)} %get-tuple-element.113), channel_id=1, source_target_pairs={{0,4},{4,0},{8,12},{12,8},{16,20},{20,16},{24,28},{28,24},{1,5},{5... | collective-permute-start | bytes 1572872 | tf_op jit(solution)/shard_map/ppermute | solution.py:602
  (6 other events, 6.5 us)

commit v3 on v2

v3 whole, which is shorter than its diff:
```python
import jax
import jax.numpy as jnp
from jax import lax
from jax.experimental import pallas as pl
from jax.experimental.pallas import tpu as pltpu
from jax.sharding import PartitionSpec as P

HEAD_TOTAL = 64
HD = 128
BLOCK = 256
CHUNK = 128
TILE = 8
F32 = jnp.float32
BF16 = jnp.bfloat16
MIB = 1024 * 1024
NEAR = pl.BlockSpec(memory_space=pltpu.VMEM)
FAR = pl.BlockSpec(memory_space=pl.ANY)
SCALARS = pl.BlockSpec(memory_space=pltpu.SMEM)


def in_vmem(*shape, kind=F32):
    return pltpu.VMEM(shape, kind)


def near(*arrays):
    return [pltpu.with_memory_space_constraint(array, pltpu.VMEM) for array in arrays]


def far(*arrays):
    return [pltpu.with_memory_space_constraint(array, pltpu.HBM) for array in arrays]


def params(mib):
    return pltpu.CompilerParams(vmem_limit_bytes=mib * MIB)


def cost(flops, moved, exps=0):
    return pl.CostEstimate(flops=flops, bytes_accessed=moved, transcendentals=exps)


def block_cum(log_decay):
    size = log_decay.shape[1]
    upper = lax.broadcasted_iota(jnp.int32, (size, size), 0) <= lax.broadcasted_iota(
        jnp.int32, (size, size), 1
    )
    return jnp.dot(
        log_decay,
        jnp.where(upper, 1.0, 0.0).astype(F32),
        precision=lax.Precision.HIGHEST,
        preferred_element_type=F32,
    )


def as_columns(row):
    return jnp.broadcast_to(row, (HD, row.shape[1])).T


def dot(a, b):
    return jnp.dot(a, b, preferred_element_type=F32)


def dot_rows(a, b):
    return lax.dot_general(a, b, (((1,), (1,)), ((), ())), preferred_element_type=F32)


def two_parts(matrix):
    high = matrix.astype(BF16)
    return high, (matrix - high.astype(F32)).astype(BF16)


def times_state(rows, state):
    return dot(jnp.concatenate([rows, rows], axis=1), jnp.concatenate(two_parts(state), axis=0))


def times_state_t(rows, state):
    return dot_rows(
        jnp.concatenate([rows, rows], axis=1), jnp.concatenate(two_parts(state), axis=1)
    )


def decay_matrix(row, columns):
    size = row.shape[1]
    lower = lax.broadcasted_iota(jnp.int32, (size, size), 0) >= lax.broadcasted_iota(
        jnp.int32, (size, size), 1
    )
    both = jnp.concatenate([columns] * (size // HD), axis=1)
    return jnp.exp(jnp.where(lower, both - row, -jnp.inf))


def to_rows(dst, block):
    tok, heads, dim = block.shape
    dst[...] = block[...].astype(F32).reshape(tok * heads, dim)


def from_rows(rows, block):
    tok, heads, dim = block.shape
    block[...] = rows[...].reshape(tok, heads, dim).astype(BF16)


def transposed_dot(a, b):
    return lax.dot_general(a, b, (((0,), (0,)), ((), ())), preferred_element_type=F32)


def each_head(heads, unroll, body):
    def step(h, carry):
        body(h)
        return carry

    lax.fori_loop(0, heads, step, 0, unroll=unroll)


def head_rows(ref, head, heads, tok):
    return ref[pl.ds(head, tok, stride=heads), :]


def state_kernel(
    place_ref, ld_hbm, k_hbm, v_hbm, own_ref, send_ref, first_ref, kh, vh,
    ld_ref, k_raw, v_raw, kx, vx, cum, acc, decay, sems,
):
    heads, tok = ld_ref.shape
    half = heads // 2
    per_block = BLOCK // CHUNK
    copies = [pltpu.make_async_copy(ld_hbm, ld_ref, sems.at[0])]
    for c in range(tok // CHUNK):
        at = pl.ds(c * CHUNK, CHUNK)
        copies.append(pltpu.make_async_copy(k_hbm.at[at], k_raw.at[at], sems.at[2 * c + 1]))
        copies.append(pltpu.make_async_copy(v_hbm.at[at], v_raw.at[at], sems.at[2 * c + 2]))
    for copy in copies:
        copy.start()
    copies[0].wait()
    for b in range(2):
        cum[b] = block_cum(ld_ref[:, b * BLOCK : (b + 1) * BLOCK])
    ends = cum[0, :, BLOCK - 1 :] + cum[1, :, BLOCK - 1 :]
    decay[...] = jnp.broadcast_to(jnp.exp(ends), decay.shape)

    for b in range(2):
        for c in range(per_block):
            at = pl.ds((b * per_block + c) * CHUNK, CHUNK)
            rows = pl.ds(c * CHUNK * heads, CHUNK * heads)
            which = 2 * (b * per_block + c) + 1
            copies[which].wait()
            to_rows(kx.at[rows], k_raw.at[at])
            copies[which + 1].wait()
            to_rows(vx.at[rows], v_raw.at[at])

        def one(h, b=b):
            row = cum[b, pl.ds(h, 1), :]
            scale = jnp.exp(row[:, BLOCK - 1 :] - row)
            key = head_rows(kx, h, heads, BLOCK)
            value = head_rows(vx, h, heads, BLOCK).astype(BF16)
            kh[b, h] = key.astype(BF16)
            vh[b, h] = value
            state = dot((key.T * scale).astype(BF16), value)
            if b == 0:
                first_ref[h] = state
            else:
                acc[h] = state + jnp.exp(row[:, BLOCK - 1 :]) * first_ref[h]

        each_head(heads, 4, one)

    core = place_ref[0]
    own_ref[:, :HD] = acc[pl.ds(core * half, half)]
    send_ref[:, :HD] = acc[pl.ds((1 - core) * half, half)]
    for i in range(half):
        for ref, base in ((own_ref, core * half), (send_ref, (1 - core) * half)):
            ref[i, HD:] = jnp.broadcast_to(decay[pl.ds(base + i, 1), :], (TILE, HD))


def local_state(place, log_decay, key_rows, value_rows):
    tok, heads, dim = key_rows.shape
    half = heads // 2
    by_head = in_vmem(2, heads, BLOCK, dim, kind=BF16)
    return pl.pallas_call(
        state_kernel,
        in_specs=[SCALARS, FAR, FAR, FAR],
        out_specs=[NEAR] * 5,
        out_shape=[
            in_vmem(half, dim + TILE, dim), in_vmem(half, dim + TILE, dim),
            in_vmem(heads, dim, dim), by_head, by_head,
        ],
        scratch_shapes=[
            pltpu.VMEM((heads, tok), F32),
            pltpu.VMEM((tok, heads, dim), BF16),
            pltpu.VMEM((tok, heads, dim), BF16),
            pltpu.VMEM((BLOCK * heads, dim), F32),
            pltpu.VMEM((BLOCK * heads, dim), F32),
            pltpu.VMEM((2, heads, BLOCK), F32),
            pltpu.VMEM((heads, dim, dim), F32),
            pltpu.VMEM((heads, dim), F32),
            pltpu.SemaphoreType.DMA((2 * (tok // CHUNK) + 1,)),
        ],
        compiler_params=params(16),
        cost_estimate=cost(2 * tok * heads * dim * dim, 8 * tok * heads * dim),
        name="local_state",
    )(place, *far(log_decay, key_rows, value_rows))


def intra(index, log_decay, kh, vh, first, query_rows, output_grad):
    tok, heads, dim = query_rows.shape

    def kernel(ld_ref, kh, vh, first_ref, q_hbm, o_hbm, qh, oh, w_ref, inner_ref,
               q_raw, o_raw, qx, ox, cum, sems):
        at = pl.ds(index * BLOCK, BLOCK)
        copy_q = pltpu.make_async_copy(q_hbm.at[at], q_raw, sems.at[0])
        copy_o = pltpu.make_async_copy(o_hbm.at[at], o_raw, sems.at[1])
        copy_q.start()
        copy_o.start()
        cum[...] = block_cum(ld_ref[:, index * BLOCK : (index + 1) * BLOCK])
        copy_q.wait()
        to_rows(qx, q_raw)
        copy_o.wait()
        to_rows(ox, o_raw)

        def one(h):
            query = head_rows(qx, h, heads, BLOCK).astype(BF16)
            qh[h] = query
            oh[h] = head_rows(ox, h, heads, BLOCK).astype(BF16)
            row = cum[pl.ds(h, 1), :]
            columns = as_columns(row)
            weights = (dot_rows(query, kh[index, h]) * decay_matrix(row, columns)).astype(BF16)
            w_ref[h] = weights
            inner = dot(weights, vh[index, h])
            if index:
                inner += jnp.exp(columns) * times_state(query, first_ref[h])
            inner_ref[h] = inner

        each_head(heads, 2, one)

    by_head = in_vmem(heads, BLOCK, dim, kind=BF16)
    return pl.pallas_call(
        kernel,
        in_specs=[NEAR] * 4 + [FAR, FAR],
        out_specs=[NEAR] * 4,
        out_shape=[
            by_head, by_head, in_vmem(heads, BLOCK, BLOCK, kind=BF16), in_vmem(heads, BLOCK, dim),
        ],
        scratch_shapes=[
            pltpu.VMEM((BLOCK, heads, dim), BF16),
            pltpu.VMEM((BLOCK, heads, dim), BF16),
            pltpu.VMEM((BLOCK * heads, dim), F32),
            pltpu.VMEM((BLOCK * heads, dim), F32),
            pltpu.VMEM((heads, BLOCK), F32),
            pltpu.SemaphoreType.DMA((2,)),
        ],
        compiler_params=params(10),
        cost_estimate=cost(
            2 * heads * BLOCK * BLOCK * dim * 4, 20 * heads * BLOCK * dim, heads * BLOCK * BLOCK
        ),
        name=f"intra_{index}",
    )(log_decay, *near(kh, vh, first), *far(query_rows, output_grad))


def whole_state(core, keep_ref, recv_ref, head):
    half = keep_ref.shape[0]
    mine = (head // half) == core
    return jnp.where(mine, keep_ref[head % half], recv_ref[head % half])


def attend_kernel(
    place_ref, ld_ref, gain_ref, keep_ref, recv_ref, q0, q1, o0, o1, inner0, inner1,
    att0, att1, sums_ref, cum, squares, products,
):
    cum[0] = block_cum(ld_ref[:, :BLOCK])
    cum[1] = cum[0, :, BLOCK - 1 :] + block_cum(ld_ref[:, BLOCK:])
    squares[...] = jnp.zeros_like(squares)
    products[...] = jnp.zeros_like(products)

    def one(h):
        state = whole_state(place_ref[0], keep_ref, recv_ref, h)
        gain = gain_ref[pl.ds(h, 1), :]
        for b, (q, o, inner, att) in enumerate(((q0, o0, inner0, att0), (q1, o1, inner1, att1))):
            columns = jnp.exp(as_columns(cum[b, pl.ds(h, 1), :]))
            attended = inner[h] + columns * times_state(q[h], state)
            att[h] = attended
            squares[b] += attended * attended
            products[b] += gain * o[h].astype(F32) * attended

    each_head(ld_ref.shape[0], 2, one)
    ones = jnp.ones((8, HD), F32)
    for b in range(2):
        for at, total in enumerate((squares, products)):
            line = lax.dot_general(
                ones, total[b], (((1,), (1,)), ((), ())),
                precision=lax.Precision.HIGHEST, preferred_element_type=F32,
            )
            sums_ref[at : at + 1, b * BLOCK : (b + 1) * BLOCK] = line[:1]


def attend(place, log_decay, gain, keep, recv, parts):
    heads, tok = log_decay.shape
    dim = HD
    by_head = in_vmem(heads, BLOCK, dim)
    return pl.pallas_call(
        attend_kernel,
        in_specs=[SCALARS] + [NEAR] * 10,
        out_specs=[NEAR] * 3,
        out_shape=[by_head, by_head, in_vmem(2, tok)],
        scratch_shapes=[
            pltpu.VMEM((2, heads, BLOCK), F32),
            pltpu.VMEM((2, BLOCK, dim), F32),
            pltpu.VMEM((2, BLOCK, dim), F32),
        ],
        compiler_params=params(6),
        cost_estimate=cost(4 * heads * tok * dim * dim, 16 * heads * tok * dim),
        name="attend",
    )(place, log_decay, gain, *near(keep, recv, *parts))


def inverse_rms(sums_ref, b):
    at = slice(b * BLOCK, (b + 1) * BLOCK)
    inv = lax.rsqrt(sums_ref[0:1, at] / (HEAD_TOTAL * HD) + 1e-06)
    mean = sums_ref[1:2, at] * inv / (HEAD_TOTAL * HD)
    return inv, mean


def norm_grad_kernel(
    place_ref, ld_ref, gain_ref, sums_ref, q0, q1, o0, o1, att0, att1,
    g0, g1, own_ref, send_ref, second_ref, cum, scales, acc,
):
    heads = ld_ref.shape[0]
    half = heads // 2
    for b in range(2):
        cum[b] = block_cum(ld_ref[:, b * BLOCK : (b + 1) * BLOCK])
        inv, mean = inverse_rms(sums_ref, b)
        scales[b, 0] = as_columns(inv)
        scales[b, 1] = as_columns(inv * inv * mean)

    def one(h):
        gain = gain_ref[pl.ds(h, 1), :]
        ends = []
        for b, (q, o, att, g) in enumerate(((q0, o0, att0, g0), (q1, o1, att1, g1))):
            grad = gain * o[h].astype(F32) * scales[b, 0] - att[h] * scales[b, 1]
            grad = grad.astype(BF16)
            g[h] = grad
            queries = q[h].astype(F32).T * jnp.exp(cum[b, pl.ds(h, 1), :])
            ends.append(dot(queries.astype(BF16), grad))
        second_ref[h] = ends[1]
        first_decay = jnp.exp(cum[0, pl.ds(h, 1), :][:, BLOCK - 1 :])
        acc[h] = ends[0] + first_decay * ends[1]

    each_head(heads, 2, one)
    core = place_ref[0]
    own_ref[...] = acc[pl.ds(core * half, half)]
    send_ref[...] = acc[pl.ds((1 - core) * half, half)]


def norm_grad(place, log_decay, gain, sums, parts):
    heads, tok = log_decay.shape
    dim = HD
    half = heads // 2
    by_head = in_vmem(heads, BLOCK, dim, kind=BF16)
    return pl.pallas_call(
        norm_grad_kernel,
        in_specs=[SCALARS] + [NEAR] * 9,
        out_specs=[NEAR] * 5,
        out_shape=[
            by_head, by_head, in_vmem(half, dim, dim), in_vmem(half, dim, dim),
            in_vmem(heads, dim, dim),
        ],
        scratch_shapes=[
            pltpu.VMEM((2, heads, BLOCK), F32),
            pltpu.VMEM((2, 2, BLOCK, dim), F32),
            pltpu.VMEM((heads, dim, dim), F32),
        ],
        compiler_params=params(6),
        cost_estimate=cost(2 * heads * tok * dim * dim, 14 * heads * tok * dim),
        name="norm_grad",
    )(place, log_decay, gain, sums, *near(*parts))


def on_block(work):
    for index in range(2):
        pl.when(pl.program_id(0) == index)(lambda index=index: work(index))


def raw_output(heads, tok):
    spec = pl.BlockSpec((BLOCK, heads, HD), lambda i: (i, 0, 0))
    return spec, jax.ShapeDtypeStruct((tok, heads, HD), BF16)


def normed_kernel(gain_ref, sums_ref, att0, att1, out_ref, rows):
    heads = gain_ref.shape[0]

    def work(b):
        inv = as_columns(inverse_rms(sums_ref, b)[0])
        att = (att0, att1)[b]

        def one(h):
            rows[pl.ds(h, BLOCK, stride=heads), :] = att[h] * inv * gain_ref[pl.ds(h, 1), :]

        each_head(heads, 2, one)

    on_block(work)
    from_rows(rows, out_ref)


def normed_rows(gain, sums, att0, att1):
    heads, _, dim = att0.shape
    tok = 2 * BLOCK
    spec, shape = raw_output(heads, tok)
    return pl.pallas_call(
        normed_kernel,
        grid=(2,),
        in_specs=[NEAR] * 4,
        out_specs=spec,
        out_shape=shape,
        scratch_shapes=[pltpu.VMEM((BLOCK * heads, dim), F32)],
        compiler_params=params(7),
        cost_estimate=cost(3 * heads * tok * dim, 6 * heads * tok * dim),
        name="normed_rows",
    )(gain, sums, *near(att0, att1))


def grad_q_kernel(
    place_ref, ld_ref, keep_ref, recv_ref, first_ref, kh, vh, g0, g1, out_ref, gs_ref, cum, rows,
):
    heads = ld_ref.shape[0]

    def work(b):
        g = (g0, g1)[b]
        for x in range(2):
            cum[x] = block_cum(ld_ref[:, x * BLOCK : (x + 1) * BLOCK])

        def one(h):
            row = cum[b, pl.ds(h, 1), :]
            columns = as_columns(row)
            scores = (dot_rows(g[h], vh[b, h]) * decay_matrix(row, columns)).astype(BF16)
            gs_ref[b, h] = scores
            state = whole_state(place_ref[0], keep_ref, recv_ref, h)
            if b:
                state = jnp.exp(cum[0, pl.ds(h, 1), :][:, BLOCK - 1 :]) * state + first_ref[h]
            grad = dot(scores, kh[b, h]) + jnp.exp(columns) * times_state_t(g[h], state)
            rows[pl.ds(h, BLOCK, stride=heads), :] = grad

        each_head(heads, 2, one)

    on_block(work)
    from_rows(rows, out_ref)


def grad_query(place, log_decay, keep, recv, first, kh, vh, g0, g1):
    heads, tok = log_decay.shape
    dim = HD
    spec, shape = raw_output(heads, tok)
    return pl.pallas_call(
        grad_q_kernel,
        grid=(2,),
        in_specs=[SCALARS] + [NEAR] * 8,
        out_specs=[spec, NEAR],
        out_shape=[shape, in_vmem(2, heads, BLOCK, BLOCK, kind=BF16)],
        scratch_shapes=[pltpu.VMEM((2, heads, BLOCK), F32), pltpu.VMEM((BLOCK * heads, dim), F32)],
        compiler_params=params(8),
        cost_estimate=cost(
            4 * heads * tok * dim * (BLOCK + dim), 12 * heads * tok * dim, heads * tok * BLOCK
        ),
        name="grad_query",
    )(place, log_decay, *near(keep, recv, first, kh, vh, g0, g1))


def grad_kv_kernel(
    ld_ref, gs_ref, w0, w1, q0, q1, kh, vh, g0, g1, second_ref, dk, dv, cum,
):
    cum[...] = block_cum(ld_ref[:, :BLOCK])

    def one(h):
        row = cum[pl.ds(h, 1), :]
        columns = as_columns(jnp.exp(row[:, BLOCK - 1 :] - row))
        state = second_ref[h]
        dk[0, h] = transposed_dot(gs_ref[0, h], q0[h]) + columns * times_state_t(vh[0, h], state)
        dv[0, h] = transposed_dot(w0[h], g0[h]) + columns * times_state(kh[0, h], state)
        dk[1, h] = transposed_dot(gs_ref[1, h], q1[h])
        dv[1, h] = transposed_dot(w1[h], g1[h])

    each_head(ld_ref.shape[0], 2, one)


def grad_key_value(log_decay, gs, w0, w1, q0, q1, kh, vh, g0, g1, second):
    heads, tok = log_decay.shape
    dim = HD
    return pl.pallas_call(
        grad_kv_kernel,
        in_specs=[NEAR] * 11,
        out_specs=[NEAR] * 2,
        out_shape=[in_vmem(2, heads, BLOCK, dim)] * 2,
        scratch_shapes=[pltpu.VMEM((heads, BLOCK), F32)],
        compiler_params=params(4),
        cost_estimate=cost(4 * heads * tok * dim * (BLOCK + dim), 30 * heads * tok * dim),
        name="grad_key_value",
    )(log_decay, *near(gs, w0, w1, q0, q1, kh, vh, g0, g1, second))


def finish_kernel(
    place_ref, ld_ref, keep_ref, recv_ref, kh, vh, dk, dv, out_k, out_v, cum, rows_k, rows_v,
):
    heads = ld_ref.shape[0]

    def work(b):
        for x in range(2):
            cum[x] = block_cum(ld_ref[:, x * BLOCK : (x + 1) * BLOCK])

        def one(h):
            row = cum[b, pl.ds(h, 1), :]
            left = row[:, BLOCK - 1 :] - row
            if b == 0:
                left = left + cum[1, pl.ds(h, 1), :][:, BLOCK - 1 :]
            columns = as_columns(jnp.exp(left))
            state = whole_state(place_ref[0], keep_ref, recv_ref, h)
            at = pl.ds(h, BLOCK, stride=heads)
            rows_k[at, :] = dk[b, h] + columns * times_state_t(vh[b, h], state)
            rows_v[at, :] = dv[b, h] + columns * times_state(kh[b, h], state)

        each_head(heads, 2, one)

    on_block(work)
    from_rows(rows_k, out_k)
    from_rows(rows_v, out_v)


def finish(place, log_decay, keep, recv, kh, vh, dk, dv):
    heads, tok = log_decay.shape
    dim = HD
    spec, shape = raw_output(heads, tok)
    return pl.pallas_call(
        finish_kernel,
        grid=(2,),
        in_specs=[SCALARS] + [NEAR] * 7,
        out_specs=[spec, spec],
        out_shape=[shape, shape],
        scratch_shapes=[
            pltpu.VMEM((2, heads, BLOCK), F32),
            pltpu.VMEM((BLOCK * heads, dim), F32),
            pltpu.VMEM((BLOCK * heads, dim), F32),
        ],
        compiler_params=params(12),
        cost_estimate=cost(8 * heads * tok * dim * dim, 16 * heads * tok * dim),
        name="finish",
    )(place, log_decay, *near(keep, recv, kh, vh, dk, dv))


def swap(value, axis, bit):
    count = lax.axis_size(axis)
    return lax.ppermute(value, axis, [(i, i ^ bit) for i in range(count)])


def mix(body, place, arrays, shapes, name):
    def kernel(place_ref, *refs):
        bits = [place_ref[at] == 1 for at in range(1, 4)]
        body(bits, refs[: len(arrays)], refs[len(arrays) :])

    return pl.pallas_call(
        kernel,
        in_specs=[SCALARS] + [NEAR] * len(arrays),
        out_specs=[NEAR] * len(shapes),
        out_shape=[in_vmem(*shape) for shape in shapes],
        compiler_params=params(4),
        cost_estimate=cost(4 * 8 * HD * HD, 16 * 8 * HD * HD),
        name=name,
    )(place, *arrays)


OWN, PARTNER, CHIP, ROW, CORNER = range(5)


def mix_total(bits, own, got, d_own, d_got, first, second):
    late = bits[0]
    quarter = first.shape[0]
    for h in range(2 * quarter):
        total = jnp.where(late, 1.0, d_got(h)) * own[h, :HD] + jnp.where(late, d_own(h), 1.0) * got[h, :HD]
        if h < quarter:
            first[h, :HD] = total
        else:
            second[h - quarter] = total


def mix_total_first(bits, arrays, outputs):
    own, got = arrays
    first, second, chip = outputs
    quarter = first.shape[0]
    d_own = lambda h: own[h, HD : HD + 1]
    d_got = lambda h: got[h, HD : HD + 1]
    mix_total(bits, own, got, d_own, d_got, first, second)
    for h in range(2 * quarter):
        whole = d_own(h) * d_got(h)
        chip[h : h + 1] = whole
        place = HD + (TILE // 2) * (h // quarter)
        first[h % quarter, place : place + TILE // 2] = jnp.broadcast_to(whole, (TILE // 2, HD))


def mix_total_again(bits, arrays, outputs):
    table, own, got = arrays
    decay = lambda which: lambda h: table[which, h : h + 1]
    mix_total(bits, own, got, decay(OWN), decay(PARTNER), *outputs)


def mix_next(bits, decay, totals, gots, outputs):
    _, right, low = bits
    quarter = totals[1].shape[0]
    for i in range(quarter):
        h = i
        scale_total = jnp.where(right, 1.0, decay(ROW, h))
        scale_got = jnp.where(right, decay(CHIP, h), 1.0)
        outputs[0][i] = scale_total * totals[0][i, :HD] + scale_got * gots[0][i, :HD]
        h = quarter + i
        scale_total = jnp.where(low & right, 0.0, 1.0)
        corner = jnp.where(right, 1.0, decay(CHIP, h) * decay(CORNER, h))
        scale_got = jnp.where(low, corner, 0.0)
        outputs[1][i] = scale_total * totals[1][i] + scale_got * gots[1][i]


def mix_next_first(bits, arrays, outputs):
    own, got, chip, corner, first, second, one_a, one_b = arrays
    table = outputs[2]
    quarter = second.shape[0]
    for h in range(2 * quarter):
        place = HD + (TILE // 2) * (h // quarter)
        table[OWN, h : h + 1] = own[h, HD : HD + 1]
        table[PARTNER, h : h + 1] = got[h, HD : HD + 1]
        table[ROW, h : h + 1] = one_a[h % quarter, place : place + 1]
    table[CHIP] = chip[...]
    table[CORNER] = corner[...]
    decay = lambda which, h: table[which, h : h + 1]
    mix_next(bits, decay, (first, second), (one_a, one_b), outputs[:2])


def mix_next_again(bits, arrays, outputs):
    table, first, second, one_a, one_b = arrays
    decay = lambda which, h: table[which, h : h + 1]
    mix_next(bits, decay, (first, second), (one_a, one_b), outputs)


def mix_enter(bits, arrays, outputs):
    table, own, got, one_a, one_b, two_a, two_b = arrays
    kept, sent = outputs
    late, right, low = bits
    quarter = one_b.shape[0]
    decay = lambda which, h: table[which, h : h + 1]
    for h in range(2 * quarter):
        i = h % quarter
        row = jnp.where(right, decay(ROW, h), 1.0)
        if h < quarter:
            one, two = one_a[i, :HD], two_a[i]
            scale_one = jnp.where(right, 1.0, 0.0)
            scale_two = jnp.where(low, row, 0.0)
        else:
            one, two = one_b[i], two_b[i]
            scale_one = jnp.where(low, jnp.where(right, row, decay(CORNER, h)), 0.0)
            scale_two = jnp.where(low | right, 1.0, 0.0)
        enter = scale_one * one + scale_two * two
        after = jnp.where(late, decay(PARTNER, h), decay(OWN, h)) * enter
        after += jnp.where(late, got[h, :HD], own[h, :HD])
        kept[h] = jnp.where(late, after, enter)
        sent[h] = jnp.where(late, enter, after)


def entering_quad(own, send, table, place, tasks, name):
    def work(stage, after, before=()):
        if stage not in tasks:
            return before
        run, outputs = tasks[stage]
        outputs.extend(run(after))
        return lax.optimization_barrier((before, outputs[-1]))[0]

    half = own.shape[0]
    quarter = half // 2
    states, wide = (quarter, HD, HD), (quarter, HD + TILE, HD)
    got = swap(send, "seq", 1)
    if table is None:
        first, second, chip = mix(
            mix_total_first, place, (own, got), (wide, states, (half, HD)), name + "_total"
        )
    else:
        first, second = mix(
            mix_total_again, place, (table, own, got), (states, states), name + "_total"
        )
    one_a, one_b = swap(first, "seq", 2), swap(second, "seq", 4)
    if table is None:
        corner = swap(chip, "seq", 6)
        one_a, one_b, corner = work(1, second, (one_a, one_b, corner))
        next_a, next_b, table = mix(
            mix_next_first, place, (own, got, chip, corner, first, second, one_a, one_b),
            (states, states, (5, half, HD)), name + "_next",
        )
    else:
        one_a, one_b = work(1, second, (one_a, one_b))
        next_a, next_b = mix(
            mix_next_again, place, (table, first, second, one_a, one_b), (states, states),
            name + "_next",
        )
    two_a, two_b = swap(next_a, "seq", 4), swap(next_b, "seq", 2)
    two_a, two_b = work(2, next_b, (two_a, two_b))
    kept, sent = mix(
        mix_enter, place, (table, own, got, one_a, one_b, two_a, two_b),
        ((half, HD, HD), (half, HD, HD)), name + "_enter",
    )
    received = swap(sent, "seq", 1)
    work(3, sent)
    return kept, received, table


def entering_any(own, send, log_total, backward, tasks):
    for run, outputs in tasks.values():
        outputs.extend(run(send))
    count, mine = lax.axis_size("seq"), lax.axis_index("seq")
    core = mine % 2
    own, send = own[:, :HD], send[:, :HD]
    half = own.shape[0]
    in_order = jnp.where(
        core == 0, jnp.concatenate([own, send], axis=0), jnp.concatenate([send, own], axis=0)
    )
    states = lax.all_gather(in_order, "seq")
    decays = jnp.exp(lax.all_gather(log_total, "seq"))
    place = mine
    if backward:
        states, decays, place = states[::-1], decays[::-1], count - 1 - mine

    def step(at, total):
        longer = decays[at][:, None, None] * total + states[at]
        return jnp.where(at < place, longer, total)

    total = lax.fori_loop(0, count - 1, step, jnp.zeros_like(in_order))
    kept = lax.dynamic_slice_in_dim(total, core * half, half)
    return kept, lax.dynamic_slice_in_dim(total, (1 - core) * half, half)


def sum_over_heads(value):
    count = lax.axis_size("head")
    reach = 1
    while 2 * reach <= count and count % (2 * reach) == 0:
        value = value + swap(value, "head", reach)
        reach *= 2
    part = value
    for shift in range(1, count // reach):
        value = value + lax.ppermute(
            part, "head", [(i, (i + shift * reach) % count) for i in range(count)]
        )
    return value


def follows(value, earlier):
    return lax.optimization_barrier((value, earlier))[0]


def on_device(query_rows, key_rows, value_rows, output_grad, norm_gain, log_decay):
    mine = lax.axis_index("seq")
    bits = jnp.stack([(mine >> at) % 2 for at in range(3)])
    core = bits[:1]
    ahead = jnp.concatenate([core, bits]).astype(jnp.int32)
    behind = jnp.concatenate([core, 1 - bits]).astype(jnp.int32)
    table = [None]

    def entering(own, send, backward, tasks):
        if lax.axis_size("seq") != 8:
            return entering_any(own, send, jnp.sum(log_decay, axis=1), backward, tasks)
        kept, received, table[0] = entering_quad(
            own, send, table[0], behind if backward else ahead, tasks,
            "later" if backward else "earlier",
        )
        return kept, received

    own, send, first, kh, vh = local_state(ahead, log_decay, key_rows, value_rows)

    def forward_task(index):
        return lambda earlier: intra(
            index, log_decay, kh, vh, follows(first, earlier), query_rows, output_grad
        )

    in_0, in_1 = [], []
    keep, recv = entering(
        own, send, False, {1: (forward_task(0), in_0), 2: (forward_task(1), in_1)}
    )
    q0, o0, w0, inner0 = in_0
    q1, o1, w1, inner1 = in_1
    att0, att1, sums = attend(
        ahead, log_decay, norm_gain, keep, recv, (q0, q1, o0, o1, inner0, inner1)
    )
    sums = sum_over_heads(sums)
    g0, g1, grad_own, grad_send, second = norm_grad(
        ahead, log_decay, norm_gain, sums, (q0, q1, o0, o1, att0, att1)
    )
    queries, pairs, norms = [], [], []

    def query_task(earlier):
        return grad_query(
            ahead, log_decay, keep, recv, follows(first, earlier), kh, vh, g0, g1
        )

    def pair_task(earlier):
        return grad_key_value(
            log_decay, queries[1], w0, w1, q0, q1, kh, vh, g0, g1, follows(second, earlier)
        )

    def norm_task(earlier):
        return [normed_rows(follows(norm_gain, earlier), sums, att0, att1)]

    grad_keep, grad_recv = entering(
        grad_own, grad_send, True, {1: (query_task, queries), 2: (pair_task, pairs), 3: (norm_task, norms)}
    )
    grad_k, grad_v = finish(ahead, log_decay, grad_keep, grad_recv, kh, vh, *pairs)
    return norms[0], queries[0], grad_k, grad_v


def solution(mesh):
    rows = P("seq", "head", None)
    return jax.shard_map(
        on_device,
        mesh=mesh,
        in_specs=(rows, rows, rows, rows, P("head", None), P("head", "seq")),
        out_specs=(rows, rows, rows, rows),
        check_vma=False,
    )
```

time: 113 us -> 89.6 us (0.79)
  local copies, waits for them, and re-layouts: 12.6 us -> 0.01 us
  Pallas kernels: 71.5 us -> 60.7 us
    unnamed x42 -> x4, local copies, waits for them, and re-layouts: 12.3 us -> 0.01 us
    pallas_call x15, Pallas kernels: 71.5 us -> 60.7 us  [the longest x2 12.8 us: intra(): pl.pallas_call(kernel, in_specs=[NEAR] * 4 + [FAR, FAR], out_specs=[NEAR]...]
    ppermute x17 -> x15, starting transfers between devices: 15.9 us -> 17 us  [swap(): return lax.ppermute(value, axis, [(i, i ^ bit) for i in range(count)])]
    ppermute x17 -> x15, waiting for transfers between devices: 11.1 us -> 10.7 us  [swap(): return lax.ppermute(value, axis, [(i, i ^ bit) for i in range(count)])]
  transfers between devices with their start and end apart: 17 -> 15, of which waited for: 6 -> 8; matrix products, arithmetic and copies ran while one was open for 1% -> 0% of each run, Pallas kernels for 38% -> 36%
where the time goes in v3:
time: 89.6 us; the launch traced here: 89.4 us
  Pallas kernels  60.7 us (68%)
  starting transfers between devices  17 us (19%)
  waiting for transfers between devices  10.7 us (12%)
    ppermute x15, starting transfers between devices, swap(): return lax.ppermute(value, axis, [(i, i ^ bit) for i in range(count)])  17 us
    pallas_call x2, Pallas kernels, intra(): pl.pallas_call(kernel, in_specs=[NEAR] * 4 + [FAR, FAR], out_specs=[NEAR]...  12.8 us
    pallas_call x1, Pallas kernels, grad_query(): pl.pallas_call(grad_q_kernel, grid=(2,), in_specs=[SCALARS] + [NEAR] * 8,...  10.8 us
    ppermute x15, waiting for transfers between devices, swap(): return lax.ppermute(value, axis, [(i, i ^ bit) for i in range(count)])  10.7 us
    pallas_call x1, Pallas kernels, finish(): pl.pallas_call(finish_kernel, grid=(2,), in_specs=[SCALARS] + [NEAR] * 7,...  10.1 us
    pallas_call x1, Pallas kernels, local_state(): pl.pallas_call(state_kernel, in_specs=[SCALARS, FAR, FAR, FAR], out_specs...  6.63 us
    pallas_call x1, Pallas kernels, grad_key_value(): pl.pallas_call(grad_kv_kernel, in_specs=[NEAR] * 11, out_specs=[NEAR] * 2...  5.02 us
    pallas_call x1, Pallas kernels, attend(): pl.pallas_call(attend_kernel, in_specs=[SCALARS] + [NEAR] * 10, out_specs...  4.27 us
  transfers between devices with their start and end apart: 15, of which 8 were waited for; matrix products, arithmetic and copies ran while one was open for 0% of the time, Pallas kernels for 36%

profile of v3, /device:TPU:0, one launch (start us, length us, event | category | flops | bytes accessed | tf_op | source)
XLA Modules:
  0.0 89.4 jit_solution(6063426215927710771)
XLA Ops:
  0.7 6.6 %local_state.1 = (f32[8,136,128]{2,1,0:T(8,128)S(1)}, f32[8,136,128]{2,1,0:T(8,128)S(1)}, f32[16,128,128]{2,1,0:T(8,128)S(1)}, bf16[2,16,256,128]{3,2,1,0:T(8,128)(2,1)S(1)}, bf16[2,16,256,128]{3,2,1,0:T(8,128)(2,1)S(1)}) custom-call(s32[4]{0:T(128)S(1)} %pad_add_fusion.1.place_ref, f32[16,512]{1,0:T(8,128)} %ld_ref.13, bf16[512,16,128]{2,1,0:T(8,128)(2,1)} %k_hbm.1, ...), custom_call_target="tpu_custom_call" | custom-call | flops 268435456 | bytes 8388608 | tf_op jit(solution)/shard_map/local_state/pallas_call | solution.py:173
  7.4 0.5 collective-permute-start
  7.9 1.6 %collective-permute-done.refs_1_.refs_2_ = f32[8,136,128]{2,1,0:T(8,128)S(1)} collective-permute-done((f32[8,136,128]{2,1,0:T(8,128)S(1)}, f32[8,136,128]{2,1,0:T(8,128)S(1)}, u32[]{:S(2)}, u32[]{:S(2)}) %collective-permute-start) | collective-permute-done | bytes 557088 | tf_op jit(solution)/shard_map/ppermute | solution.py:542
  9.5 0.6 earlier_total.1
  10.1 2.9 %collective-permute-start.1 = (f32[4,136,128]{2,1,0:T(8,128)S(1)}, f32[4,136,128]{2,1,0:T(8,128)S(1)}, u32[]{:S(2)}, u32[]{:S(2)}) collective-permute-start(f32[4,136,128]{2,1,0:T(8,128)S(1)} %get-tuple-element.62.refs_4_), channel_id=1, source_target_pairs={{0,8},{4,12},{8,0},{12,4},{16,24},{20,28},{24,16},{28,20},{1,9},{5... | collective-permute-start | bytes 835592 | tf_op jit(solution)/shard_map/ppermute | solution.py:542
  13.0 1.5 %collective-permute-start.2 = (f32[4,128,128]{2,1,0:T(8,128)S(1)}, f32[4,128,128]{2,1,0:T(8,128)S(1)}, u32[]{:S(2)}, u32[]{:S(2)}) collective-permute-start(f32[4,128,128]{2,1,0:T(8,128)S(1)} %get-tuple-element.63.refs_5_), channel_id=1, source_target_pairs={{0,16},{4,20},{8,24},{12,28},{16,0},{20,4},{24,8},{28,12},{1,17},{... | collective-permute-start | bytes 786440 | tf_op jit(solution)/shard_map/ppermute | solution.py:542
  14.6 6.6 %intra_0.1 = (bf16[16,256,128]{2,1,0:T(8,128)(2,1)S(1)}, bf16[16,256,128]{2,1,0:T(8,128)(2,1)S(1)}, bf16[16,256,256]{2,1,0:T(8,128)(2,1)S(1)}, f32[16,256,128]{2,1,0:T(8,128)S(1)}) custom-call(f32[16,512]{1,0:T(8,128)S(1)} %copy-done, bf16[2,16,256,128]{3,2,1,0:T(8,128)(2,1)S(1)} %get-tuple-element.64.kh, ...), custom_call_target="tpu_custom_call" | custom-call | flops 1073741824 | bytes 10485760 | tf_op jit(solution)/shard_map/intra_0/pallas_call | solution.py:230
  21.3 0.6 earlier_next.1
  21.9 1.9 %collective-permute-start.4 = (f32[4,128,128]{2,1,0:T(8,128)S(1)}, f32[4,128,128]{2,1,0:T(8,128)S(1)}, u32[]{:S(2)}, u32[]{:S(2)}) collective-permute-start(f32[4,128,128]{2,1,0:T(8,128)S(1)} %get-tuple-element.73), channel_id=1, source_target_pairs={{0,16},{4,20},{8,24},{12,28},{16,0},{20,4},{24,8},{28,12},{1,17},{... | collective-permute-start | bytes 786440 | tf_op jit(solution)/shard_map/ppermute | solution.py:542
  23.8 1.5 %collective-permute-start.5 = (f32[4,128,128]{2,1,0:T(8,128)S(1)}, f32[4,128,128]{2,1,0:T(8,128)S(1)}, u32[]{:S(2)}, u32[]{:S(2)}) collective-permute-start(f32[4,128,128]{2,1,0:T(8,128)S(1)} %get-tuple-element.74), channel_id=1, source_target_pairs={{0,8},{4,12},{8,0},{12,4},{16,24},{20,28},{24,16},{28,20},{1,9},{5... | collective-permute-start | bytes 786440 | tf_op jit(solution)/shard_map/ppermute | solution.py:542
  25.3 6.2 %intra_1.1 = (bf16[16,256,128]{2,1,0:T(8,128)(2,1)S(1)}, bf16[16,256,128]{2,1,0:T(8,128)(2,1)S(1)}, bf16[16,256,256]{2,1,0:T(8,128)(2,1)S(1)}, f32[16,256,128]{2,1,0:T(8,128)S(1)}) custom-call(f32[16,512]{1,0:T(8,128)S(1)} %copy-done, bf16[2,16,256,128]{3,2,1,0:T(8,128)(2,1)S(1)} %get-tuple-element.64.kh, ...), custom_call_target="tpu_custom_call" | custom-call | flops 1073741824 | bytes 10485760 | tf_op jit(solution)/shard_map/intra_1/pallas_call | solution.py:230
  31.6 0.7 earlier_enter.1
  32.4 1.9 %collective-permute-done.6.recv_ref = f32[8,128,128]{2,1,0:T(8,128)S(1)} collective-permute-done((f32[8,128,128]{2,1,0:T(8,128)S(1)}, f32[8,128,128]{2,1,0:T(8,128)S(1)}, u32[]{:S(2)}, u32[]{:S(2)}) %collective-permute-start.6) | collective-permute-done | bytes 524320 | tf_op jit(solution)/shard_map/ppermute | solution.py:542
  34.3 4.3 %attend.1 = (f32[16,256,128]{2,1,0:T(8,128)S(1)}, f32[16,256,128]{2,1,0:T(8,128)S(1)}, f32[2,512]{1,0:T(2,128)S(1)}) custom-call(s32[4]{0:T(128)S(1)} %pad_add_fusion.1.place_ref, f32[16,512]{1,0:T(8,128)S(1)} %copy-done, f32[16,128]{1,0:T(8,128)S(1)} %copy-done.1, f32[8,128,128]{2,1,0:T(8,128)S(1)} %get-tuple-element.79.keep_ref, ...), custom_call_target="tpu_custom_call" | custom-call | flops 536870912 | bytes 16777216 | tf_op jit(solution)/shard_map/attend/pallas_call | solution.py:293
  38.6 1.6 %collective-permute-start.7 = (f32[2,512]{1,0:T(2,128)S(1)}, f32[2,512]{1,0:T(2,128)S(1)}, u32[]{:S(2)}, u32[]{:S(2)}) collective-permute-start(f32[2,512]{1,0:T(2,128)S(1)} %get-tuple-element.85), channel_id=1, source_target_pairs={{0,1},{1,0},{2,3},{3,2},{4,5},{5,4},{6,7},{7,6},{8,9},{9,8},{10,11... | collective-permute-start | bytes 12296 | tf_op jit(solution)/shard_map/ppermute | solution.py:542
  40.2 2.0 %collective-permute-done.7 = f32[2,512]{1,0:T(2,128)S(1)} collective-permute-done((f32[2,512]{1,0:T(2,128)S(1)}, f32[2,512]{1,0:T(2,128)S(1)}, u32[]{:S(2)}, u32[]{:S(2)}) %collective-permute-start.7) | collective-permute-done | bytes 4128 | tf_op jit(solution)/shard_map/ppermute | solution.py:542
  42.2 2.6 %collective-permute-start.8 = (f32[2,512]{1,0:T(2,128)S(1)}, f32[2,512]{1,0:T(2,128)S(1)}, u32[]{:S(2)}, u32[]{:S(2)}) collective-permute-start(f32[2,512]{1,0:T(2,128)S(1)} %add.19), channel_id=1, source_target_pairs={{0,2},{1,3},{2,0},{3,1},{4,6},{5,7},{6,4},{7,5},{8,10},{9,11},{10,... | collective-permute-start | bytes 12296 | tf_op jit(solution)/shard_map/ppermute | solution.py:542
  44.8 1.9 %collective-permute-done.8 = f32[2,512]{1,0:T(2,128)S(1)} collective-permute-done((f32[2,512]{1,0:T(2,128)S(1)}, f32[2,512]{1,0:T(2,128)S(1)}, u32[]{:S(2)}, u32[]{:S(2)}) %collective-permute-start.8) | collective-permute-done | bytes 4128 | tf_op jit(solution)/shard_map/ppermute | solution.py:542
  46.7 3.5 %norm_grad.1 = (bf16[16,256,128]{2,1,0:T(8,128)(2,1)S(1)}, bf16[16,256,128]{2,1,0:T(8,128)(2,1)S(1)}, f32[8,128,128]{2,1,0:T(8,128)S(1)}, f32[8,128,128]{2,1,0:T(8,128)S(1)}, f32[16,128,128]{2,1,0:T(8,128)S(1)}) custom-call(s32[4]{0:T(128)S(1)} %pad_add_fusion.1.place_ref, f32[16,512]{1,0:T(8,128)S(1)} %copy-done, f32[16,128]{1,0:T(8,128)S(1)} %copy-done.1, ...), custom_call_target="tpu_custom_call" | custom-call | flops 268435456 | bytes 14680064 | tf_op jit(solution)/shard_map/norm_grad/pallas_call | solution.py:352
  50.4 1.7 %collective-permute-done.9.refs_2_ = f32[8,128,128]{2,1,0:T(8,128)S(1)} collective-permute-done((f32[8,128,128]{2,1,0:T(8,128)S(1)}, f32[8,128,128]{2,1,0:T(8,128)S(1)}, u32[]{:S(2)}, u32[]{:S(2)}) %collective-permute-start.9) | collective-permute-done | bytes 524320 | tf_op jit(solution)/shard_map/ppermute | solution.py:542
  52.2 0.6 later_total.1
  52.8 1.0 %collective-permute-start.10 = (f32[4,128,128]{2,1,0:T(8,128)S(1)}, f32[4,128,128]{2,1,0:T(8,128)S(1)}, u32[]{:S(2)}, u32[]{:S(2)}) collective-permute-start(f32[4,128,128]{2,1,0:T(8,128)S(1)} %get-tuple-element.90.refs_1_), channel_id=1, source_target_pairs={{0,8},{4,12},{8,0},{12,4},{16,24},{20,28},{24,16},{28,20},{1,9},{5... | collective-permute-start | bytes 786440 | tf_op jit(solution)/shard_map/ppermute | solution.py:542
  53.8 0.5 collective-permute-start.11
  54.3 10.8 %grad_query.1 = (bf16[512,16,128]{2,1,0:T(8,128)(2,1)}, bf16[2,16,256,256]{3,2,1,0:T(8,128)(2,1)S(1)}) custom-call(s32[4]{0:T(128)S(1)} %pad_add_fusion.1.place_ref, f32[16,512]{1,0:T(8,128)S(1)} %copy-done, f32[8,128,128]{2,1,0:T(8,128)S(1)} %get-tuple-element.79.keep_ref, f32[8,128,128]{2,1,0:T(8,128)S(1)} %collective-permute-done.6.recv_ref, ...), custom_call_target="tpu_custom_call" | custom-call | flops 1610612736 | bytes 12582912 | tf_op jit(solution)/shard_map/grad_query/pallas_call | solution.py:445
  65.2 0.6 later_next.1
  65.8 1.6 %collective-permute-start.12 = (f32[4,128,128]{2,1,0:T(8,128)S(1)}, f32[4,128,128]{2,1,0:T(8,128)S(1)}, u32[]{:S(2)}, u32[]{:S(2)}) collective-permute-start(f32[4,128,128]{2,1,0:T(8,128)S(1)} %get-tuple-element.98), channel_id=1, source_target_pairs={{0,16},{4,20},{8,24},{12,28},{16,0},{20,4},{24,8},{28,12},{1,17},{... | collective-permute-start | bytes 786440 | tf_op jit(solution)/shard_map/ppermute | solution.py:542
  67.3 1.1 %collective-permute-start.13 = (f32[4,128,128]{2,1,0:T(8,128)S(1)}, f32[4,128,128]{2,1,0:T(8,128)S(1)}, u32[]{:S(2)}, u32[]{:S(2)}) collective-permute-start(f32[4,128,128]{2,1,0:T(8,128)S(1)} %get-tuple-element.99), channel_id=1, source_target_pairs={{0,8},{4,12},{8,0},{12,4},{16,24},{20,28},{24,16},{28,20},{1,9},{5... | collective-permute-start | bytes 786440 | tf_op jit(solution)/shard_map/ppermute | solution.py:542
  68.4 5.0 %grad_key_value.1 = (f32[2,16,256,128]{3,2,1,0:T(8,128)S(1)}, f32[2,16,256,128]{3,2,1,0:T(8,128)S(1)}) custom-call(f32[16,512]{1,0:T(8,128)S(1)} %copy-done, bf16[2,16,256,256]{3,2,1,0:T(8,128)(2,1)S(1)} %get-tuple-element.95.gs_ref, bf16[16,256,256]{2,1,0:T(8,128)(2,1)S(1)} %get-tuple-element.100.w0, bf16[16,256,256]{2,1,0:T(8,128)(2,1)S(1)} %get-tuple-element.101.w1, ...), custom_call_target="tpu_custom_call" | custom-call | flops 1610612736 | bytes 31457280 | tf_op jit(solution)/shard_map/grad_key_value/pallas_call | solution.py:480
  73.6 1.2 %collective-permute-done.13.refs_6_ = f32[4,128,128]{2,1,0:T(8,128)S(1)} collective-permute-done((f32[4,128,128]{2,1,0:T(8,128)S(1)}, f32[4,128,128]{2,1,0:T(8,128)S(1)}, u32[]{:S(2)}, u32[]{:S(2)}) %collective-permute-start.13) | collective-permute-done | bytes 262176 | tf_op jit(solution)/shard_map/ppermute | solution.py:542
  74.9 0.7 later_enter.1
  75.6 3.7 %normed_rows.1 = bf16[512,16,128]{2,1,0:T(8,128)(2,1)} custom-call(f32[16,128]{1,0:T(8,128)S(1)} %copy-done.1, f32[2,512]{1,0:T(2,128)S(1)} %add.20.sums_ref, f32[16,256,128]{2,1,0:T(8,128)S(1)} %get-tuple-element.86.att0, f32[16,256,128]{2,1,0:T(8,128)S(1)} %get-tuple-element.87.att1), custom_call_target="tpu_custom_call" | custom-call | flops 3145728 | bytes 6291456 | tf_op jit(solution)/shard_map/normed_rows/pallas_call | solution.py:401
  79.4 10.1 %finish.1 = (bf16[512,16,128]{2,1,0:T(8,128)(2,1)}, bf16[512,16,128]{2,1,0:T(8,128)(2,1)}) custom-call(s32[4]{0:T(128)S(1)} %pad_add_fusion.1.place_ref, f32[16,512]{1,0:T(8,128)S(1)} %copy-done, f32[8,128,128]{2,1,0:T(8,128)S(1)} %get-tuple-element.110.keep_ref, f32[8,128,128]{2,1,0:T(8,128)S(1)} %collective-permute-done.14.recv_ref, ...), custom_call_target="tpu_custom_call" | custom-call | flops 1073741824 | bytes 16777216 | tf_op jit(solution)/shard_map/finish/pallas_call | solution.py:523
  (22 shorter events, 0.8 us)
Async XLA Ops:
  0.7 13.8 %copy-start = (f32[16,512]{1,0:T(8,128)S(1)}, f32[16,512]{1,0:T(8,128)}, u32[]{:S(2)}) copy-start(f32[16,512]{1,0:T(8,128)} %ld_ref.13) | copy-start | bytes 98308
  7.4 2.1 %collective-permute-start = (f32[8,136,128]{2,1,0:T(8,128)S(1)}, f32[8,136,128]{2,1,0:T(8,128)S(1)}, u32[]{:S(2)}, u32[]{:S(2)}) collective-permute-start(f32[8,136,128]{2,1,0:T(8,128)S(1)} %get-tuple-element.60), channel_id=1, source_target_pairs={{0,4},{4,0},{8,12},{12,8},{16,20},{20,16},{24,28},{28,24},{1,5},{5... | collective-permute-start | bytes 1671176 | tf_op jit(solution)/shard_map/ppermute | solution.py:542
  10.1 11.2 %collective-permute-start.1 = (f32[4,136,128]{2,1,0:T(8,128)S(1)}, f32[4,136,128]{2,1,0:T(8,128)S(1)}, u32[]{:S(2)}, u32[]{:S(2)}) collective-permute-start(f32[4,136,128]{2,1,0:T(8,128)S(1)} %get-tuple-element.62.refs_4_), channel_id=1, source_target_pairs={{0,8},{4,12},{8,0},{12,4},{16,24},{20,28},{24,16},{28,20},{1,9},{5... | collective-permute-start | bytes 835592 | tf_op jit(solution)/shard_map/ppermute | solution.py:542
  13.0 8.3 %collective-permute-start.2 = (f32[4,128,128]{2,1,0:T(8,128)S(1)}, f32[4,128,128]{2,1,0:T(8,128)S(1)}, u32[]{:S(2)}, u32[]{:S(2)}) collective-permute-start(f32[4,128,128]{2,1,0:T(8,128)S(1)} %get-tuple-element.63.refs_5_), channel_id=1, source_target_pairs={{0,16},{4,20},{8,24},{12,28},{16,0},{20,4},{24,8},{28,12},{1,17},{... | collective-permute-start | bytes 786440 | tf_op jit(solution)/shard_map/ppermute | solution.py:542
  14.5 6.7 %collective-permute-start.3 = (f32[8,128]{1,0:T(8,128)S(1)}, f32[8,128]{1,0:T(8,128)S(1)}, u32[]{:S(2)}, u32[]{:S(2)}) collective-permute-start(f32[8,128]{1,0:T(8,128)S(1)} %get-tuple-element.61.refs_2_), channel_id=1, source_target_pairs={{0,24},{4,28},{8,16},{12,20},{16,8},{20,12},{24,0},{28,4},{1,25},{... | collective-permute-start | bytes 12296 | tf_op jit(solution)/shard_map/ppermute | solution.py:542
  21.9 9.7 %collective-permute-start.4 = (f32[4,128,128]{2,1,0:T(8,128)S(1)}, f32[4,128,128]{2,1,0:T(8,128)S(1)}, u32[]{:S(2)}, u32[]{:S(2)}) collective-permute-start(f32[4,128,128]{2,1,0:T(8,128)S(1)} %get-tuple-element.73), channel_id=1, source_target_pairs={{0,16},{4,20},{8,24},{12,28},{16,0},{20,4},{24,8},{28,12},{1,17},{... | collective-permute-start | bytes 786440 | tf_op jit(solution)/shard_map/ppermute | solution.py:542
  23.8 7.8 %collective-permute-start.5 = (f32[4,128,128]{2,1,0:T(8,128)S(1)}, f32[4,128,128]{2,1,0:T(8,128)S(1)}, u32[]{:S(2)}, u32[]{:S(2)}) collective-permute-start(f32[4,128,128]{2,1,0:T(8,128)S(1)} %get-tuple-element.74), channel_id=1, source_target_pairs={{0,8},{4,12},{8,0},{12,4},{16,24},{20,28},{24,16},{28,20},{1,9},{5... | collective-permute-start | bytes 786440 | tf_op jit(solution)/shard_map/ppermute | solution.py:542
  31.6 2.7 %copy-start.1 = (f32[16,128]{1,0:T(8,128)S(1)}, f32[16,128]{1,0:T(8,128)}, u32[]{:S(2)}) copy-start(f32[16,128]{1,0:T(8,128)} %gain_ref.4) | copy-start | bytes 24580
  32.3 2.0 %collective-permute-start.6 = (f32[8,128,128]{2,1,0:T(8,128)S(1)}, f32[8,128,128]{2,1,0:T(8,128)S(1)}, u32[]{:S(2)}, u32[]{:S(2)}) collective-permute-start(f32[8,128,128]{2,1,0:T(8,128)S(1)} %get-tuple-element.80), channel_id=1, source_target_pairs={{0,4},{4,0},{8,12},{12,8},{16,20},{20,16},{24,28},{28,24},{1,5},{5... | collective-permute-start | bytes 1572872 | tf_op jit(solution)/shard_map/ppermute | solution.py:542
  38.6 3.6 %collective-permute-start.7 = (f32[2,512]{1,0:T(2,128)S(1)}, f32[2,512]{1,0:T(2,128)S(1)}, u32[]{:S(2)}, u32[]{:S(2)}) collective-permute-start(f32[2,512]{1,0:T(2,128)S(1)} %get-tuple-element.85), channel_id=1, source_target_pairs={{0,1},{1,0},{2,3},{3,2},{4,5},{5,4},{6,7},{7,6},{8,9},{9,8},{10,11... | collective-permute-start | bytes 12296 | tf_op jit(solution)/shard_map/ppermute | solution.py:542
  42.2 4.5 %collective-permute-start.8 = (f32[2,512]{1,0:T(2,128)S(1)}, f32[2,512]{1,0:T(2,128)S(1)}, u32[]{:S(2)}, u32[]{:S(2)}) collective-permute-start(f32[2,512]{1,0:T(2,128)S(1)} %add.19), channel_id=1, source_target_pairs={{0,2},{1,3},{2,0},{3,1},{4,6},{5,7},{6,4},{7,5},{8,10},{9,11},{10,... | collective-permute-start | bytes 12296 | tf_op jit(solution)/shard_map/ppermute | solution.py:542
  50.2 2.0 %collective-permute-start.9 = (f32[8,128,128]{2,1,0:T(8,128)S(1)}, f32[8,128,128]{2,1,0:T(8,128)S(1)}, u32[]{:S(2)}, u32[]{:S(2)}) collective-permute-start(f32[8,128,128]{2,1,0:T(8,128)S(1)} %get-tuple-element.89), channel_id=1, source_target_pairs={{0,4},{4,0},{8,12},{12,8},{16,20},{20,16},{24,28},{28,24},{1,5},{5... | collective-permute-start | bytes 1572872 | tf_op jit(solution)/shard_map/ppermute | solution.py:542
  52.8 12.4 %collective-permute-start.10 = (f32[4,128,128]{2,1,0:T(8,128)S(1)}, f32[4,128,128]{2,1,0:T(8,128)S(1)}, u32[]{:S(2)}, u32[]{:S(2)}) collective-permute-start(f32[4,128,128]{2,1,0:T(8,128)S(1)} %get-tuple-element.90.refs_1_), channel_id=1, source_target_pairs={{0,8},{4,12},{8,0},{12,4},{16,24},{20,28},{24,16},{28,20},{1,9},{5... | collective-permute-start | bytes 786440 | tf_op jit(solution)/shard_map/ppermute | solution.py:542
  53.8 11.4 %collective-permute-start.11 = (f32[4,128,128]{2,1,0:T(8,128)S(1)}, f32[4,128,128]{2,1,0:T(8,128)S(1)}, u32[]{:S(2)}, u32[]{:S(2)}) collective-permute-start(f32[4,128,128]{2,1,0:T(8,128)S(1)} %get-tuple-element.91.refs_2_), channel_id=1, source_target_pairs={{0,16},{4,20},{8,24},{12,28},{16,0},{20,4},{24,8},{28,12},{1,17},{... | collective-permute-start | bytes 786440 | tf_op jit(solution)/shard_map/ppermute | solution.py:542
  65.8 7.9 %collective-permute-start.12 = (f32[4,128,128]{2,1,0:T(8,128)S(1)}, f32[4,128,128]{2,1,0:T(8,128)S(1)}, u32[]{:S(2)}, u32[]{:S(2)}) collective-permute-start(f32[4,128,128]{2,1,0:T(8,128)S(1)} %get-tuple-element.98), channel_id=1, source_target_pairs={{0,16},{4,20},{8,24},{12,28},{16,0},{20,4},{24,8},{28,12},{1,17},{... | collective-permute-start | bytes 786440 | tf_op jit(solution)/shard_map/ppermute | solution.py:542
  67.3 7.5 %collective-permute-start.13 = (f32[4,128,128]{2,1,0:T(8,128)S(1)}, f32[4,128,128]{2,1,0:T(8,128)S(1)}, u32[]{:S(2)}, u32[]{:S(2)}) collective-permute-start(f32[4,128,128]{2,1,0:T(8,128)S(1)} %get-tuple-element.99), channel_id=1, source_target_pairs={{0,8},{4,12},{8,0},{12,4},{16,24},{20,28},{24,16},{28,20},{1,9},{5... | collective-permute-start | bytes 786440 | tf_op jit(solution)/shard_map/ppermute | solution.py:542
  75.6 3.8 %collective-permute-start.14 = (f32[8,128,128]{2,1,0:T(8,128)S(1)}, f32[8,128,128]{2,1,0:T(8,128)S(1)}, u32[]{:S(2)}, u32[]{:S(2)}) collective-permute-start(f32[8,128,128]{2,1,0:T(8,128)S(1)} %get-tuple-element.107), channel_id=1, source_target_pairs={{0,4},{4,0},{8,12},{12,8},{16,20},{20,16},{24,28},{28,24},{1,5},{5... | collective-permute-start | bytes 1572872 | tf_op jit(solution)/shard_map/ppermute | solution.py:542

commit v4 on v3

--- a/solution.py
+++ b/solution.py
@@ -15,7 +15,7 @@
 MIB = 1024 * 1024
 NEAR = pl.BlockSpec(memory_space=pltpu.VMEM)
 FAR = pl.BlockSpec(memory_space=pl.ANY)
-SCALARS = pl.BlockSpec(memory_space=pltpu.SMEM)
+LOWER, UPPER, LATE, RIGHT, LOW = range(5)
 
 
 def in_vmem(*shape, kind=F32):
@@ -78,23 +78,21 @@
     )
 
 
-def decay_matrix(row, columns):
-    size = row.shape[1]
-    lower = lax.broadcasted_iota(jnp.int32, (size, size), 0) >= lax.broadcasted_iota(
-        jnp.int32, (size, size), 1
-    )
-    both = jnp.concatenate([columns] * (size // HD), axis=1)
-    return jnp.exp(jnp.where(lower, both - row, -jnp.inf))
-
-
-def to_rows(dst, block):
-    tok, heads, dim = block.shape
-    dst[...] = block[...].astype(F32).reshape(tok * heads, dim)
-
-
-def from_rows(rows, block):
-    tok, heads, dim = block.shape
-    block[...] = rows[...].reshape(tok, heads, dim).astype(BF16)
+def causal(table, row, columns):
+    half = row.shape[1] // 2
+    lower = lax.broadcasted_iota(jnp.int32, (half, half), 0) >= lax.broadcasted_iota(
+        jnp.int32, (half, half), 1
+    )
+    quarters = []
+    for t in range(2):
+        for s in range(t + 1):
+            gap = columns[t * half : (t + 1) * half] - row[:, s * half : (s + 1) * half]
+            if t == s:
+                gap = jnp.where(lower, gap, -jnp.inf)
+            part = table[t * half : (t + 1) * half, s * half : (s + 1) * half]
+            quarters.append((part * jnp.exp(gap)).astype(BF16))
+    top = jnp.concatenate([quarters[0], jnp.zeros_like(quarters[0])], axis=1)
+    return jnp.concatenate([top, jnp.concatenate(quarters[1:], axis=1)], axis=0)
 
 
 def transposed_dot(a, b):
@@ -109,13 +107,71 @@
     lax.fori_loop(0, heads, step, 0, unroll=unroll)
 
 
-def head_rows(ref, head, heads, tok):
-    return ref[pl.ds(head, tok, stride=heads), :]
+def turn_tiles(tiles):
+    count = len(tiles)
+    at = lax.broadcasted_iota(jnp.int32, tiles[0].shape, 0)
+    turned = [tile if i == 0 else pltpu.roll(tile, i, 0) for i, tile in enumerate(tiles)]
+    reach = 1
+    while reach < count:
+        odd = (at & reach) != 0
+        turned = [
+            jnp.where(odd, turned[(n + reach) % count], turned[n]) for n in range(count)
+        ]
+        reach *= 2
+    picked = [turned[-j % count] for j in range(count)]
+    return [tile if j == 0 else pltpu.roll(tile, count - j, 0) for j, tile in enumerate(picked)]
+
+
+def to_heads(dst, block):
+    tok, heads, _ = block.shape
+
+    def step(group, carry):
+        at = pl.multiple_of(group * 2 * TILE, 2 * TILE)
+        tokens = block[pl.ds(at, 2 * TILE)].astype(F32)
+        for first in range(0, heads, TILE):
+            halves = [
+                turn_tiles([tokens[base + i, first : first + TILE] for i in range(TILE)])
+                for base in (0, TILE)
+            ]
+            for j in range(TILE):
+                both = jnp.concatenate([halves[0][j], halves[1][j]], axis=0)
+                dst[first + j, pl.ds(at, 2 * TILE)] = both.astype(BF16)
+        return carry
+
+    lax.fori_loop(0, tok // (2 * TILE), step, 0, unroll=2)
+
+
+def from_heads(block, src, start, tok):
+    heads = src.shape[0]
+
+    def step(group, carry):
+        at = pl.multiple_of(group * TILE, TILE)
+        parts = [
+            turn_tiles([src[first + i, pl.ds(start + at, TILE)] for i in range(TILE)])
+            for first in range(0, heads, TILE)
+        ]
+        for j in range(TILE):
+            block[at + j] = jnp.concatenate([part[j] for part in parts], axis=0).astype(BF16)
+        return carry
+
+    lax.fori_loop(0, tok // TILE, step, 0, unroll=2)
+
+
+def is_set(place_ref, which):
+    return place_ref[which : which + 1] > 0.5
+
+
+def split_halves(place_ref, whole, own_ref, send_ref):
+    half = own_ref.shape[0]
+    mine = is_set(place_ref, LOWER)
+    for i in range(half):
+        own_ref[i, :HD] = jnp.where(mine, whole[i], whole[half + i])
+        send_ref[i, :HD] = jnp.where(mine, whole[half + i], whole[i])
 
 
 def state_kernel(
     place_ref, ld_hbm, k_hbm, v_hbm, own_ref, send_ref, first_ref, kh, vh,
-    ld_ref, k_raw, v_raw, kx, vx, cum, acc, decay, sems,
+    ld_ref, k_raw, v_raw, cum, acc, decay, sems,
 ):
     heads, tok = ld_ref.shape
     half = heads // 2
@@ -136,21 +192,17 @@
     for b in range(2):
         for c in range(per_block):
             at = pl.ds((b * per_block + c) * CHUNK, CHUNK)
-            rows = pl.ds(c * CHUNK * heads, CHUNK * heads)
+            here = pl.ds(c * CHUNK, CHUNK)
             which = 2 * (b * per_block + c) + 1
             copies[which].wait()
-            to_rows(kx.at[rows], k_raw.at[at])
+            to_heads(kh.at[b, :, here], k_raw.at[at])
             copies[which + 1].wait()
-            to_rows(vx.at[rows], v_raw.at[at])
+            to_heads(vh.at[b, :, here], v_raw.at[at])
 
         def one(h, b=b):
             row = cum[b, pl.ds(h, 1), :]
             scale = jnp.exp(row[:, BLOCK - 1 :] - row)
-            key = head_rows(kx, h, heads, BLOCK)
-            value = head_rows(vx, h, heads, BLOCK).astype(BF16)
-            kh[b, h] = key.astype(BF16)
-            vh[b, h] = value
-            state = dot((key.T * scale).astype(BF16), value)
+            state = dot((kh[b, h].astype(F32).T * scale).astype(BF16), vh[b, h])
             if b == 0:
                 first_ref[h] = state
             else:
@@ -158,12 +210,14 @@
 
         each_head(heads, 4, one)
 
-    core = place_ref[0]
-    own_ref[:, :HD] = acc[pl.ds(core * half, half)]
-    send_ref[:, :HD] = acc[pl.ds((1 - core) * half, half)]
+    split_halves(place_ref, acc, own_ref, send_ref)
+    mine = is_set(place_ref, LOWER)
     for i in range(half):
-        for ref, base in ((own_ref, core * half), (send_ref, (1 - core) * half)):
-            ref[i, HD:] = jnp.broadcast_to(decay[pl.ds(base + i, 1), :], (TILE, HD))
+        lower, upper = decay[i : i + 1], decay[half + i : half + i + 1]
+        for ref, row in (
+            (own_ref, jnp.where(mine, lower, upper)), (send_ref, jnp.where(mine, upper, lower)),
+        ):
+            ref[i, HD:] = jnp.broadcast_to(row, (TILE, HD))
 
 
 def local_state(place, log_decay, key_rows, value_rows):
@@ -172,7 +226,7 @@
     by_head = in_vmem(2, heads, BLOCK, dim, kind=BF16)
     return pl.pallas_call(
         state_kernel,
-        in_specs=[SCALARS, FAR, FAR, FAR],
+        in_specs=[NEAR, FAR, FAR, FAR],
         out_specs=[NEAR] * 5,
         out_shape=[
             in_vmem(half, dim + TILE, dim), in_vmem(half, dim + TILE, dim),
@@ -182,14 +236,12 @@
             pltpu.VMEM((heads, tok), F32),
             pltpu.VMEM((tok, heads, dim), BF16),
             pltpu.VMEM((tok, heads, dim), BF16),
-            pltpu.VMEM((BLOCK * heads, dim), F32),
-            pltpu.VMEM((BLOCK * heads, dim), F32),
             pltpu.VMEM((2, heads, BLOCK), F32),
             pltpu.VMEM((heads, dim, dim), F32),
             pltpu.VMEM((heads, dim), F32),
             pltpu.SemaphoreType.DMA((2 * (tok // CHUNK) + 1,)),
         ],
-        compiler_params=params(16),
+        compiler_params=params(8),
         cost_estimate=cost(2 * tok * heads * dim * dim, 8 * tok * heads * dim),
         name="local_state",
     )(place, *far(log_decay, key_rows, value_rows))
@@ -199,7 +251,7 @@
     tok, heads, dim = query_rows.shape
 
     def kernel(ld_ref, kh, vh, first_ref, q_hbm, o_hbm, qh, oh, w_ref, inner_ref,
-               q_raw, o_raw, qx, ox, cum, sems):
+               q_raw, o_raw, cum, sems):
         at = pl.ds(index * BLOCK, BLOCK)
         copy_q = pltpu.make_async_copy(q_hbm.at[at], q_raw, sems.at[0])
         copy_o = pltpu.make_async_copy(o_hbm.at[at], o_raw, sems.at[1])
@@ -207,17 +259,15 @@
         copy_o.start()
         cum[...] = block_cum(ld_ref[:, index * BLOCK : (index + 1) * BLOCK])
         copy_q.wait()
-        to_rows(qx, q_raw)
+        to_heads(qh, q_raw)
         copy_o.wait()
-        to_rows(ox, o_raw)
+        to_heads(oh, o_raw)
 
         def one(h):
-            query = head_rows(qx, h, heads, BLOCK).astype(BF16)
-            qh[h] = query
-            oh[h] = head_rows(ox, h, heads, BLOCK).astype(BF16)
+            query = qh[h]
             row = cum[pl.ds(h, 1), :]
             columns = as_columns(row)
-            weights = (dot_rows(query, kh[index, h]) * decay_matrix(row, columns)).astype(BF16)
+            weights = causal(dot_rows(query, kh[index, h]), row, columns)
             w_ref[h] = weights
             inner = dot(weights, vh[index, h])
             if index:
@@ -237,12 +287,10 @@
         scratch_shapes=[
             pltpu.VMEM((BLOCK, heads, dim), BF16),
             pltpu.VMEM((BLOCK, heads, dim), BF16),
-            pltpu.VMEM((BLOCK * heads, dim), F32),
-            pltpu.VMEM((BLOCK * heads, dim), F32),
             pltpu.VMEM((heads, BLOCK), F32),
             pltpu.SemaphoreType.DMA((2,)),
         ],
-        compiler_params=params(10),
+        compiler_params=params(6),
         cost_estimate=cost(
             2 * heads * BLOCK * BLOCK * dim * 4, 20 * heads * BLOCK * dim, heads * BLOCK * BLOCK
         ),
@@ -250,9 +298,9 @@
     )(log_decay, *near(kh, vh, first), *far(query_rows, output_grad))
 
 
-def whole_state(core, keep_ref, recv_ref, head):
+def whole_state(place_ref, keep_ref, recv_ref, head):
     half = keep_ref.shape[0]
-    mine = (head // half) == core
+    mine = place_ref[pl.ds(head // half, 1)] > 0.5
     return jnp.where(mine, keep_ref[head % half], recv_ref[head % half])
 
 
@@ -266,10 +314,10 @@
     products[...] = jnp.zeros_like(products)
 
     def one(h):
-        state = whole_state(place_ref[0], keep_ref, recv_ref, h)
+        state = whole_state(place_ref, keep_ref, recv_ref, h)
         gain = gain_ref[pl.ds(h, 1), :]
         for b, (q, o, inner, att) in enumerate(((q0, o0, inner0, att0), (q1, o1, inner1, att1))):
-            columns = jnp.exp(as_columns(cum[b, pl.ds(h, 1), :]))
+            columns = as_columns(jnp.exp(cum[b, pl.ds(h, 1), :]))
             attended = inner[h] + columns * times_state(q[h], state)
             att[h] = attended
             squares[b] += attended * attended
@@ -292,7 +340,7 @@
     by_head = in_vmem(heads, BLOCK, dim)
     return pl.pallas_call(
         attend_kernel,
-        in_specs=[SCALARS] + [NEAR] * 10,
+        in_specs=[NEAR] + [NEAR] * 10,
         out_specs=[NEAR] * 3,
         out_shape=[by_head, by_head, in_vmem(2, tok)],
         scratch_shapes=[
@@ -318,7 +366,6 @@
     g0, g1, own_ref, send_ref, second_ref, cum, scales, acc,
 ):
     heads = ld_ref.shape[0]
-    half = heads // 2
     for b in range(2):
         cum[b] = block_cum(ld_ref[:, b * BLOCK : (b + 1) * BLOCK])
         inv, mean = inverse_rms(sums_ref, b)
@@ -339,9 +386,7 @@
         acc[h] = ends[0] + first_decay * ends[1]
 
     each_head(heads, 2, one)
-    core = place_ref[0]
-    own_ref[...] = acc[pl.ds(core * half, half)]
-    send_ref[...] = acc[pl.ds((1 - core) * half, half)]
+    split_halves(place_ref, acc, own_ref, send_ref)
 
 
 def norm_grad(place, log_decay, gain, sums, parts):
@@ -351,7 +396,7 @@
     by_head = in_vmem(heads, BLOCK, dim, kind=BF16)
     return pl.pallas_call(
         norm_grad_kernel,
-        in_specs=[SCALARS] + [NEAR] * 9,
+        in_specs=[NEAR] + [NEAR] * 9,
         out_specs=[NEAR] * 5,
         out_shape=[
             by_head, by_head, in_vmem(half, dim, dim), in_vmem(half, dim, dim),
@@ -386,12 +431,12 @@
         att = (att0, att1)[b]
 
         def one(h):
-            rows[pl.ds(h, BLOCK, stride=heads), :] = att[h] * inv * gain_ref[pl.ds(h, 1), :]
+            rows[h] = att[h] * inv * gain_ref[pl.ds(h, 1), :]
 
         each_head(heads, 2, one)
 
     on_block(work)
-    from_rows(rows, out_ref)
+    from_heads(out_ref, rows, 0, BLOCK)
 
 
 def normed_rows(gain, sums, att0, att1):
@@ -404,7 +449,7 @@
         in_specs=[NEAR] * 4,
         out_specs=spec,
         out_shape=shape,
-        scratch_shapes=[pltpu.VMEM((BLOCK * heads, dim), F32)],
+        scratch_shapes=[pltpu.VMEM((heads, BLOCK, dim), F32)],
         compiler_params=params(7),
         cost_estimate=cost(3 * heads * tok * dim, 6 * heads * tok * dim),
         name="normed_rows",
@@ -424,18 +469,18 @@
         def one(h):
             row = cum[b, pl.ds(h, 1), :]
             columns = as_columns(row)
-            scores = (dot_rows(g[h], vh[b, h]) * decay_matrix(row, columns)).astype(BF16)
+            scores = causal(dot_rows(g[h], vh[b, h]), row, columns)
             gs_ref[b, h] = scores
-            state = whole_state(place_ref[0], keep_ref, recv_ref, h)
+            state = whole_state(place_ref, keep_ref, recv_ref, h)
             if b:
                 state = jnp.exp(cum[0, pl.ds(h, 1), :][:, BLOCK - 1 :]) * state + first_ref[h]
             grad = dot(scores, kh[b, h]) + jnp.exp(columns) * times_state_t(g[h], state)
-            rows[pl.ds(h, BLOCK, stride=heads), :] = grad
+            rows[h] = grad
 
         each_head(heads, 2, one)
 
     on_block(work)
-    from_rows(rows, out_ref)
+    from_heads(out_ref, rows, 0, BLOCK)
 
 
 def grad_query(place, log_decay, keep, recv, first, kh, vh, g0, g1):
@@ -445,10 +490,10 @@
     return pl.pallas_call(
         grad_q_kernel,
         grid=(2,),
-        in_specs=[SCALARS] + [NEAR] * 8,
+        in_specs=[NEAR] + [NEAR] * 8,
         out_specs=[spec, NEAR],
         out_shape=[shape, in_vmem(2, heads, BLOCK, BLOCK, kind=BF16)],
-        scratch_shapes=[pltpu.VMEM((2, heads, BLOCK), F32), pltpu.VMEM((BLOCK * heads, dim), F32)],
+        scratch_shapes=[pltpu.VMEM((2, heads, BLOCK), F32), pltpu.VMEM((heads, BLOCK, dim), F32)],
         compiler_params=params(8),
         cost_estimate=cost(
             4 * heads * tok * dim * (BLOCK + dim), 12 * heads * tok * dim, heads * tok * BLOCK
@@ -491,45 +536,51 @@
 
 def finish_kernel(
     place_ref, ld_ref, keep_ref, recv_ref, kh, vh, dk, dv, out_k, out_v, cum, rows_k, rows_v,
+    raw_k, raw_v, sems,
 ):
     heads = ld_ref.shape[0]
-
-    def work(b):
-        for x in range(2):
-            cum[x] = block_cum(ld_ref[:, x * BLOCK : (x + 1) * BLOCK])
-
-        def one(h):
+    for x in range(2):
+        cum[x] = block_cum(ld_ref[:, x * BLOCK : (x + 1) * BLOCK])
+    copies = []
+    for b in range(2):
+
+        def one(h, b=b):
             row = cum[b, pl.ds(h, 1), :]
             left = row[:, BLOCK - 1 :] - row
             if b == 0:
                 left = left + cum[1, pl.ds(h, 1), :][:, BLOCK - 1 :]
             columns = as_columns(jnp.exp(left))
-            state = whole_state(place_ref[0], keep_ref, recv_ref, h)
-            at = pl.ds(h, BLOCK, stride=heads)
-            rows_k[at, :] = dk[b, h] + columns * times_state_t(vh[b, h], state)
-            rows_v[at, :] = dv[b, h] + columns * times_state(kh[b, h], state)
+            state = whole_state(place_ref, keep_ref, recv_ref, h)
+            rows_k[h] = dk[b, h] + columns * times_state_t(vh[b, h], state)
+            rows_v[h] = dv[b, h] + columns * times_state(kh[b, h], state)
 
         each_head(heads, 2, one)
-
-    on_block(work)
-    from_rows(rows_k, out_k)
-    from_rows(rows_v, out_v)
+        for start in range(0, BLOCK, CHUNK):
+            at = pl.ds(b * BLOCK + start, CHUNK)
+            for rows, raw, out in ((rows_k, raw_k, out_k), (rows_v, raw_v, out_v)):
+                from_heads(raw.at[at], rows, start, CHUNK)
+                copies.append(pltpu.make_async_copy(raw.at[at], out.at[at], sems.at[len(copies)]))
+                copies[-1].start()
+    for copy in copies:
+        copy.wait()
 
 
 def finish(place, log_decay, keep, recv, kh, vh, dk, dv):
     heads, tok = log_decay.shape
     dim = HD
-    spec, shape = raw_output(heads, tok)
+    shape = jax.ShapeDtypeStruct((tok, heads, dim), BF16)
     return pl.pallas_call(
         finish_kernel,
-        grid=(2,),
-        in_specs=[SCALARS] + [NEAR] * 7,
-        out_specs=[spec, spec],
+        in_specs=[NEAR] * 8,
+        out_specs=[FAR, FAR],
         out_shape=[shape, shape],
         scratch_shapes=[
             pltpu.VMEM((2, heads, BLOCK), F32),
-            pltpu.VMEM((BLOCK * heads, dim), F32),
-            pltpu.VMEM((BLOCK * heads, dim), F32),
+            pltpu.VMEM((heads, BLOCK, dim), F32),
+            pltpu.VMEM((heads, BLOCK, dim), F32),
+            pltpu.VMEM((tok, heads, dim), BF16),
+            pltpu.VMEM((tok, heads, dim), BF16),
+            pltpu.SemaphoreType.DMA((2 * (tok // CHUNK),)),
         ],
         compiler_params=params(12),
         cost_estimate=cost(8 * heads * tok * dim * dim, 16 * heads * tok * dim),
@@ -544,12 +595,12 @@
 
 def mix(body, place, arrays, shapes, name):
     def kernel(place_ref, *refs):
-        bits = [place_ref[at] == 1 for at in range(1, 4)]
+        bits = [is_set(place_ref, which) for which in (LATE, RIGHT, LOW)]
         body(bits, refs[: len(arrays)], refs[len(arrays) :])
 
     return pl.pallas_call(
         kernel,
-        in_specs=[SCALARS] + [NEAR] * len(arrays),
+        in_specs=[NEAR] + [NEAR] * len(arrays),
         out_specs=[NEAR] * len(shapes),
         out_shape=[in_vmem(*shape) for shape in shapes],
         compiler_params=params(4),
@@ -742,10 +793,15 @@
 
 def on_device(query_rows, key_rows, value_rows, output_grad, norm_gain, log_decay):
     mine = lax.axis_index("seq")
-    bits = jnp.stack([(mine >> at) % 2 for at in range(3)])
-    core = bits[:1]
-    ahead = jnp.concatenate([core, bits]).astype(jnp.int32)
-    behind = jnp.concatenate([core, 1 - bits]).astype(jnp.int32)
+    core, *chip = ((mine >> at) % 2 for at in range(3))
+    no = jnp.zeros_like(core)
+    ahead, behind = (
+        jnp.broadcast_to(jnp.stack(marks).astype(F32)[:, None], (TILE, HD))
+        for marks in (
+            (1 - core, core, core, *chip, no, no, no),
+            (1 - core, core, 1 - core, *(1 - bit for bit in chip), no, no, no),
+        )
+    )
     table = [None]
 
     def entering(own, send, backward, tasks):

time: 89.6 us -> 98.4 us (1.098)
  local copies, waits for them, and re-layouts: 0.01 us -> 15.9 us
  Pallas kernels: 60.7 us -> 54.4 us
  waiting for transfers between devices: 10.7 us -> 9.61 us
    unnamed x4 -> x64, local copies, waits for them, and re-layouts: 0.01 us -> 15.6 us
    pallas_call x11, Pallas kernels: 39.1 us -> 34.7 us  [the longest x1 10.8 us: grad_query(): pl.pallas_call(grad_q_kernel, grid=(2,), in_specs=[NEAR] + [NEAR] * 8, ou...]
    pallas_call x1, Pallas kernels: 3.71 us -> 2.56 us  [normed_rows(): pl.pallas_call(normed_kernel, grid=(2,), in_specs=[NEAR] * 4, out_specs=s...]
    ppermute x15, waiting for transfers between devices: 10.7 us -> 9.61 us  [swap(): return lax.ppermute(value, axis, [(i, i ^ bit) for i in range(count)])]
  transfers between devices with their start and end apart: 15 -> 15, of which waited for: 8 -> 5; matrix products, arithmetic and copies ran while one was open for 0% -> 0% of each run, Pallas kernels for 36% -> 31%
where the time goes in v4:
time: 98.4 us; the launch traced here: 97.9 us
  Pallas kernels  54.4 us (55%)
  starting transfers between devices  17.1 us (17%)
  local copies, waits for them, and re-layouts  15.9 us (16%)
  waiting for transfers between devices  9.61 us (10%)
    ppermute x15, starting transfers between devices, swap(): return lax.ppermute(value, axis, [(i, i ^ bit) for i in range(count)])  17.1 us
    unnamed x64, local copies, waits for them, and re-layouts  15.6 us
    pallas_call x2, Pallas kernels, intra(): pl.pallas_call(kernel, in_specs=[NEAR] * 4 + [FAR, FAR], out_specs=[NEAR]...  12 us
    pallas_call x1, Pallas kernels, grad_query(): pl.pallas_call(grad_q_kernel, grid=(2,), in_specs=[NEAR] + [NEAR] * 8, ou...  10.8 us
    ppermute x15, waiting for transfers between devices, swap(): return lax.ppermute(value, axis, [(i, i ^ bit) for i in range(count)])  9.61 us
    pallas_call x1, Pallas kernels, finish(): pl.pallas_call(finish_kernel, in_specs=[NEAR] * 8, out_specs=[FAR, FAR],...  7.84 us
    pallas_call x1, Pallas kernels, local_state(): pl.pallas_call(state_kernel, in_specs=[NEAR, FAR, FAR, FAR], out_specs=[N...  5.76 us
    pallas_call x1, Pallas kernels, grad_key_value(): pl.pallas_call(grad_kv_kernel, in_specs=[NEAR] * 11, out_specs=[NEAR] * 2...  5.06 us
  transfers between devices with their start and end apart: 15, of which 5 were waited for; matrix products, arithmetic and copies ran while one was open for 0% of the time, Pallas kernels for 31%

profile of v4, /device:TPU:0, one launch (start us, length us, event | category | flops | bytes accessed | tf_op | source)
XLA Modules:
  0.0 97.9 jit_solution(3270786597631623260)
XLA Ops:
  0.8 5.8 %local_state.1 = (f32[8,136,128]{2,1,0:T(8,128)S(1)}, f32[8,136,128]{2,1,0:T(8,128)S(1)}, f32[16,128,128]{2,1,0:T(8,128)S(1)}, bf16[2,16,256,128]{3,2,1,0:T(8,128)(2,1)S(1)}, bf16[2,16,256,128]{3,2,1,0:T(8,128)(2,1)S(1)}) custom-call(f32[8,128]{1,0:T(8,128)S(1)} %broadcast_in_dim.5.place_ref, f32[16,512]{1,0:T(8,128)} %ld_ref.13, ...), custom_call_target="tpu_custom_call" | custom-call | flops 268435456 | bytes 8388608 | tf_op jit(solution)/shard_map/local_state/pallas_call | solution.py:227
  7.1 1.6 %collective-permute-done.refs_1_.refs_2_ = f32[8,136,128]{2,1,0:T(8,128)S(1)} collective-permute-done((f32[8,136,128]{2,1,0:T(8,128)S(1)}, f32[8,136,128]{2,1,0:T(8,128)S(1)}, u32[]{:S(2)}, u32[]{:S(2)}) %collective-permute-start) | collective-permute-done | bytes 557088 | tf_op jit(solution)/shard_map/ppermute | solution.py:593
  8.8 2.9 %collective-permute-start.1 = (f32[4,136,128]{2,1,0:T(8,128)S(1)}, f32[4,136,128]{2,1,0:T(8,128)S(1)}, u32[]{:S(2)}, u32[]{:S(2)}) collective-permute-start(f32[4,136,128]{2,1,0:T(8,128)S(1)} %get-tuple-element.62.refs_4_), channel_id=1, source_target_pairs={{0,8},{4,12},{8,0},{12,4},{16,24},{20,28},{24,16},{28,20},{1,9},{5... | collective-permute-start | bytes 835592 | tf_op jit(solution)/shard_map/ppermute | solution.py:593
  11.7 1.5 %collective-permute-start.2 = (f32[4,128,128]{2,1,0:T(8,128)S(1)}, f32[4,128,128]{2,1,0:T(8,128)S(1)}, u32[]{:S(2)}, u32[]{:S(2)}) collective-permute-start(f32[4,128,128]{2,1,0:T(8,128)S(1)} %get-tuple-element.63.refs_5_), channel_id=1, source_target_pairs={{0,16},{4,20},{8,24},{12,28},{16,0},{20,4},{24,8},{28,12},{1,17},{... | collective-permute-start | bytes 786440 | tf_op jit(solution)/shard_map/ppermute | solution.py:593
  13.3 6.4 %intra_0.1 = (bf16[16,256,128]{2,1,0:T(8,128)(2,1)S(1)}, bf16[16,256,128]{2,1,0:T(8,128)(2,1)S(1)}, bf16[16,256,256]{2,1,0:T(8,128)(2,1)S(1)}, f32[16,256,128]{2,1,0:T(8,128)S(1)}) custom-call(f32[16,512]{1,0:T(8,128)S(1)} %copy-done.17, bf16[2,16,256,128]{3,2,1,0:T(8,128)(2,1)S(1)} %get-tuple-element.64.kh, ...), custom_call_target="tpu_custom_call" | custom-call | flops 1073741824 | bytes 10485760 | tf_op jit(solution)/shard_map/intra_0/pallas_call | solution.py:280
  19.7 1.3 %copy-done.18 = bf16[16,256,256]{2,1,0:T(8,128)(2,1)} copy-done((bf16[16,256,256]{2,1,0:T(8,128)(2,1)}, bf16[16,256,256]{2,1,0:T(8,128)(2,1)S(1)}, u32[]{:S(2)}) %copy-start.18) | copy-done | bytes 2097176
  21.1 2.0 %collective-permute-start.4 = (f32[4,128,128]{2,1,0:T(8,128)S(1)}, f32[4,128,128]{2,1,0:T(8,128)S(1)}, u32[]{:S(2)}, u32[]{:S(2)}) collective-permute-start(f32[4,128,128]{2,1,0:T(8,128)S(1)} %get-tuple-element.73), channel_id=1, source_target_pairs={{0,16},{4,20},{8,24},{12,28},{16,0},{20,4},{24,8},{28,12},{1,17},{... | collective-permute-start | bytes 786440 | tf_op jit(solution)/shard_map/ppermute | solution.py:593
  23.2 1.5 %collective-permute-start.5 = (f32[4,128,128]{2,1,0:T(8,128)S(1)}, f32[4,128,128]{2,1,0:T(8,128)S(1)}, u32[]{:S(2)}, u32[]{:S(2)}) collective-permute-start(f32[4,128,128]{2,1,0:T(8,128)S(1)} %get-tuple-element.74), channel_id=1, source_target_pairs={{0,8},{4,12},{8,0},{12,4},{16,24},{20,28},{24,16},{28,20},{1,9},{5... | collective-permute-start | bytes 786440 | tf_op jit(solution)/shard_map/ppermute | solution.py:593
  24.7 5.6 %intra_1.1 = (bf16[16,256,128]{2,1,0:T(8,128)(2,1)S(1)}, bf16[16,256,128]{2,1,0:T(8,128)(2,1)S(1)}, bf16[16,256,256]{2,1,0:T(8,128)(2,1)S(1)}, f32[16,256,128]{2,1,0:T(8,128)S(1)}) custom-call(f32[16,512]{1,0:T(8,128)S(1)} %copy-done.17, bf16[2,16,256,128]{3,2,1,0:T(8,128)(2,1)S(1)} %get-tuple-element.64.kh, ...), custom_call_target="tpu_custom_call" | custom-call | flops 1073741824 | bytes 10485760 | tf_op jit(solution)/shard_map/intra_1/pallas_call | solution.py:280
  30.3 1.4 %copy-done.20 = bf16[16,256,256]{2,1,0:T(8,128)(2,1)} copy-done((bf16[16,256,256]{2,1,0:T(8,128)(2,1)}, bf16[16,256,256]{2,1,0:T(8,128)(2,1)S(1)}, u32[]{:S(2)}) %copy-start.20) | copy-done | bytes 2097176
  32.0 1.9 %collective-permute-done.6.recv_ref = f32[8,128,128]{2,1,0:T(8,128)S(1)} collective-permute-done((f32[8,128,128]{2,1,0:T(8,128)S(1)}, f32[8,128,128]{2,1,0:T(8,128)S(1)}, u32[]{:S(2)}, u32[]{:S(2)}) %collective-permute-start.6) | collective-permute-done | bytes 524320 | tf_op jit(solution)/shard_map/ppermute | solution.py:593
  33.9 3.7 %attend.1 = (f32[16,256,128]{2,1,0:T(8,128)S(1)}, f32[16,256,128]{2,1,0:T(8,128)S(1)}, f32[2,512]{1,0:T(2,128)S(1)}) custom-call(f32[8,128]{1,0:T(8,128)S(1)} %broadcast_in_dim.5.place_ref, f32[16,512]{1,0:T(8,128)S(1)} %copy-done.17, f32[16,128]{1,0:T(8,128)S(1)} %copy-done.31, f32[8,128,128]{2,1,0:T(8,128)S(1)} %get-tuple-element.79.keep_ref, ...), custom_call_target="tpu_custom_call" | custom-call | flops 536870912 | bytes 16777216 | tf_op jit(solution)/shard_map/attend/pallas_call | solution.py:341
  37.6 1.6 %collective-permute-start.7 = (f32[2,512]{1,0:T(2,128)S(1)}, f32[2,512]{1,0:T(2,128)S(1)}, u32[]{:S(2)}, u32[]{:S(2)}) collective-permute-start(f32[2,512]{1,0:T(2,128)S(1)} %get-tuple-element.85), channel_id=1, source_target_pairs={{0,1},{1,0},{2,3},{3,2},{4,5},{5,4},{6,7},{7,6},{8,9},{9,8},{10,11... | collective-permute-start | bytes 12296 | tf_op jit(solution)/shard_map/ppermute | solution.py:593
  39.3 2.0 %collective-permute-done.7 = f32[2,512]{1,0:T(2,128)S(1)} collective-permute-done((f32[2,512]{1,0:T(2,128)S(1)}, f32[2,512]{1,0:T(2,128)S(1)}, u32[]{:S(2)}, u32[]{:S(2)}) %collective-permute-start.7) | collective-permute-done | bytes 4128 | tf_op jit(solution)/shard_map/ppermute | solution.py:593
  41.3 2.6 %collective-permute-start.8 = (f32[2,512]{1,0:T(2,128)S(1)}, f32[2,512]{1,0:T(2,128)S(1)}, u32[]{:S(2)}, u32[]{:S(2)}) collective-permute-start(f32[2,512]{1,0:T(2,128)S(1)} %add.19), channel_id=1, source_target_pairs={{0,2},{1,3},{2,0},{3,1},{4,6},{5,7},{6,4},{7,5},{8,10},{9,11},{10,... | collective-permute-start | bytes 12296 | tf_op jit(solution)/shard_map/ppermute | solution.py:593
  43.9 1.9 %collective-permute-done.8 = f32[2,512]{1,0:T(2,128)S(1)} collective-permute-done((f32[2,512]{1,0:T(2,128)S(1)}, f32[2,512]{1,0:T(2,128)S(1)}, u32[]{:S(2)}, u32[]{:S(2)}) %collective-permute-start.8) | collective-permute-done | bytes 4128 | tf_op jit(solution)/shard_map/ppermute | solution.py:593
  45.8 3.7 %norm_grad.1 = (bf16[16,256,128]{2,1,0:T(8,128)(2,1)S(1)}, bf16[16,256,128]{2,1,0:T(8,128)(2,1)S(1)}, f32[8,128,128]{2,1,0:T(8,128)S(1)}, f32[8,128,128]{2,1,0:T(8,128)}, f32[16,128,128]{2,1,0:T(8,128)S(1)}) custom-call(f32[8,128]{1,0:T(8,128)S(1)} %broadcast_in_dim.5.place_ref, f32[16,512]{1,0:T(8,128)S(1)} %copy-done.17, f32[16,128]{1,0:T(8,128)S(1)} %copy-done.31, ...), custom_call_target="tpu_custom_call" | custom-call | flops 268435456 | bytes 14680064 | tf_op jit(solution)/shard_map/norm_grad/pallas_call | solution.py:397
  50.5 1.0 %copy-done.14 = bf16[16,256,128]{2,1,0:T(8,128)(2,1)} copy-done((bf16[16,256,128]{2,1,0:T(8,128)(2,1)}, bf16[16,256,128]{2,1,0:T(8,128)(2,1)S(1)}, u32[]{:S(2)}) %copy-start.14) | copy-done | bytes 1048600
  53.5 2.2 %collective-permute-done.9.refs_2_ = f32[8,128,128]{2,1,0:T(8,128)} collective-permute-done((f32[8,128,128]{2,1,0:T(8,128)}, f32[8,128,128]{2,1,0:T(8,128)}, u32[]{:S(2)}, u32[]{:S(2)}) %collective-permute-start.9) | collective-permute-done | bytes 524320 | tf_op jit(solution)/shard_map/ppermute | solution.py:593
  55.7 1.0 %copy-done.23 = f32[8,128,128]{2,1,0:T(8,128)S(1)} copy-done((f32[8,128,128]{2,1,0:T(8,128)S(1)}, f32[8,128,128]{2,1,0:T(8,128)}, u32[]{:S(2)}) %copy-start.23) | copy-done | bytes 524312
  56.7 1.1 %later_total.1 = (f32[4,128,128]{2,1,0:T(8,128)S(1)}, f32[4,128,128]{2,1,0:T(8,128)S(1)}) custom-call(f32[8,128]{1,0:T(8,128)S(1)} %broadcast_in_dim.4.place_ref, f32[5,8,128]{2,1,0:T(8,128)S(1)} %get-tuple-element.72.refs_0_, f32[8,128,128]{2,1,0:T(8,128)S(1)} %copy-done.23, f32[8,128,128]{2,1,0:T(8,128)} %collective-permute-done.9.refs_2_), custom_call_target="tpu_custom_call" | custom-call | flops 524288 | bytes 2097152 | tf_op jit(solution)/shard_map/later_total/pallas_call | solution.py:601
  58.6 1.6 %copy-done.1 = bf16[2,16,256,128]{3,2,1,0:T(8,128)(2,1)S(1)} copy-done((bf16[2,16,256,128]{3,2,1,0:T(8,128)(2,1)S(1)}, bf16[2,16,256,128]{3,2,1,0:T(8,128)(2,1)}, u32[]{:S(2)}) %copy-start.1) | copy-done | bytes 2097176
  60.2 1.2 %copy-done.12 = bf16[16,256,128]{2,1,0:T(8,128)(2,1)S(1)} copy-done((bf16[16,256,128]{2,1,0:T(8,128)(2,1)S(1)}, bf16[16,256,128]{2,1,0:T(8,128)(2,1)}, u32[]{:S(2)}) %copy-start.12) | copy-done | bytes 1048600
  61.5 1.2 %copy-done.15 = bf16[16,256,128]{2,1,0:T(8,128)(2,1)S(1)} copy-done((bf16[16,256,128]{2,1,0:T(8,128)(2,1)S(1)}, bf16[16,256,128]{2,1,0:T(8,128)(2,1)}, u32[]{:S(2)}) %copy-start.15) | copy-done | bytes 1048600
  64.8 10.8 %grad_query.1 = (bf16[512,16,128]{2,1,0:T(8,128)(2,1)}, bf16[2,16,256,256]{3,2,1,0:T(8,128)(2,1)S(1)}) custom-call(f32[8,128]{1,0:T(8,128)S(1)} %broadcast_in_dim.5.place_ref, f32[16,512]{1,0:T(8,128)S(1)} %copy-done.17, f32[8,128,128]{2,1,0:T(8,128)S(1)} %copy-done.26, f32[8,128,128]{2,1,0:T(8,128)S(1)} %copy-done.28, ...), custom_call_target="tpu_custom_call" | custom-call | flops 1610612736 | bytes 12582912 | tf_op jit(solution)/shard_map/grad_query/pallas_call | solution.py:490
  75.6 1.9 %collective-permute-start.12 = (f32[4,128,128]{2,1,0:T(8,128)S(1)}, f32[4,128,128]{2,1,0:T(8,128)S(1)}, u32[]{:S(2)}, u32[]{:S(2)}) collective-permute-start(f32[4,128,128]{2,1,0:T(8,128)S(1)} %get-tuple-element.98), channel_id=1, source_target_pairs={{0,16},{4,20},{8,24},{12,28},{16,0},{20,4},{24,8},{28,12},{1,17},{... | collective-permute-start | bytes 786440 | tf_op jit(solution)/shard_map/ppermute | solution.py:593
  77.5 1.5 %collective-permute-start.13 = (f32[4,128,128]{2,1,0:T(8,128)S(1)}, f32[4,128,128]{2,1,0:T(8,128)S(1)}, u32[]{:S(2)}, u32[]{:S(2)}) collective-permute-start(f32[4,128,128]{2,1,0:T(8,128)S(1)} %get-tuple-element.99), channel_id=1, source_target_pairs={{0,8},{4,12},{8,0},{12,4},{16,24},{20,28},{24,16},{28,20},{1,9},{5... | collective-permute-start | bytes 786440 | tf_op jit(solution)/shard_map/ppermute | solution.py:593
  79.1 1.6 %copy-done.21 = bf16[16,256,256]{2,1,0:T(8,128)(2,1)S(1)} copy-done((bf16[16,256,256]{2,1,0:T(8,128)(2,1)S(1)}, bf16[16,256,256]{2,1,0:T(8,128)(2,1)}, u32[]{:S(2)}) %copy-start.21) | copy-done | bytes 2097176
  80.7 5.1 %grad_key_value.1 = (f32[2,16,256,128]{3,2,1,0:T(8,128)S(1)}, f32[2,16,256,128]{3,2,1,0:T(8,128)S(1)}) custom-call(f32[16,512]{1,0:T(8,128)S(1)} %copy-done.17, bf16[2,16,256,256]{3,2,1,0:T(8,128)(2,1)S(1)} %get-tuple-element.95.gs_ref, bf16[16,256,256]{2,1,0:T(8,128)(2,1)S(1)} %copy-done.19, bf16[16,256,256]{2,1,0:T(8,128)(2,1)S(1)} %copy-done.21, ...), custom_call_target="tpu_custom_call" | custom-call | flops 1610612736 | bytes 31457280 | tf_op jit(solution)/shard_map/grad_key_value/pallas_call | solution.py:525
  85.8 1.4 %later_enter.1 = (f32[8,128,128]{2,1,0:T(8,128)S(1)}, f32[8,128,128]{2,1,0:T(8,128)S(1)}) custom-call(f32[8,128]{1,0:T(8,128)S(1)} %broadcast_in_dim.4.place_ref, f32[5,8,128]{2,1,0:T(8,128)S(1)} %get-tuple-element.72.refs_0_, f32[8,128,128]{2,1,0:T(8,128)S(1)} %copy-done.24, f32[8,128,128]{2,1,0:T(8,128)} %collective-permute-done.9.refs_2_, ...), custom_call_target="tpu_custom_call" | custom-call | flops 524288 | bytes 2097152 | tf_op jit(solution)/shard_map/later_enter/pallas_call | solution.py:601
  87.5 2.6 %normed_rows.1 = bf16[512,16,128]{2,1,0:T(8,128)(2,1)} custom-call(f32[16,128]{1,0:T(8,128)S(1)} %copy-done.31, f32[2,512]{1,0:T(2,128)S(1)} %add.20.sums_ref, f32[16,256,128]{2,1,0:T(8,128)S(1)} %copy-done.8, f32[16,256,128]{2,1,0:T(8,128)S(1)} %copy-done.10), custom_call_target="tpu_custom_call" | custom-call | flops 3145728 | bytes 6291456 | tf_op jit(solution)/shard_map/normed_rows/pallas_call | solution.py:446
  90.1 7.8 %finish.1 = (bf16[512,16,128]{2,1,0:T(8,128)(2,1)}, bf16[512,16,128]{2,1,0:T(8,128)(2,1)}) custom-call(f32[8,128]{1,0:T(8,128)S(1)} %broadcast_in_dim.5.place_ref, f32[16,512]{1,0:T(8,128)S(1)} %copy-done.17, f32[8,128,128]{2,1,0:T(8,128)S(1)} %get-tuple-element.110.keep_ref, f32[8,128,128]{2,1,0:T(8,128)S(1)} %collective-permute-done.14.recv_ref, ...), custom_call_target="tpu_custom_call" | custom-call | flops 1073741824 | bytes 16777216 | tf_op jit(solution)/shard_map/finish/pallas_call | solution.py:572
  (86 shorter events, 7.4 us)
Async XLA Ops:
  0.8 12.4 %copy-start.17 = (f32[16,512]{1,0:T(8,128)S(1)}, f32[16,512]{1,0:T(8,128)}, u32[]{:S(2)}) copy-start(f32[16,512]{1,0:T(8,128)} %ld_ref.13) | copy-start | bytes 98308
  6.6 18.1 %copy-start = (bf16[2,16,256,128]{3,2,1,0:T(8,128)(2,1)}, bf16[2,16,256,128]{3,2,1,0:T(8,128)(2,1)S(1)}, u32[]{:S(2)}) copy-start(bf16[2,16,256,128]{3,2,1,0:T(8,128)(2,1)S(1)} %get-tuple-element.65.vh) | copy-start | bytes 6291460
  6.6 2.1 %collective-permute-start = (f32[8,136,128]{2,1,0:T(8,128)S(1)}, f32[8,136,128]{2,1,0:T(8,128)S(1)}, u32[]{:S(2)}, u32[]{:S(2)}) collective-permute-start(f32[8,136,128]{2,1,0:T(8,128)S(1)} %get-tuple-element.60), channel_id=1, source_target_pairs={{0,4},{4,0},{8,12},{12,8},{16,20},{20,16},{24,28},{28,24},{1,5},{5... | collective-permute-start | bytes 1671176 | tf_op jit(solution)/shard_map/ppermute | solution.py:593
  8.8 12.2 %collective-permute-start.1 = (f32[4,136,128]{2,1,0:T(8,128)S(1)}, f32[4,136,128]{2,1,0:T(8,128)S(1)}, u32[]{:S(2)}, u32[]{:S(2)}) collective-permute-start(f32[4,136,128]{2,1,0:T(8,128)S(1)} %get-tuple-element.62.refs_4_), channel_id=1, source_target_pairs={{0,8},{4,12},{8,0},{12,4},{16,24},{20,28},{24,16},{28,20},{1,9},{5... | collective-permute-start | bytes 835592 | tf_op jit(solution)/shard_map/ppermute | solution.py:593
  11.7 9.3 %collective-permute-start.2 = (f32[4,128,128]{2,1,0:T(8,128)S(1)}, f32[4,128,128]{2,1,0:T(8,128)S(1)}, u32[]{:S(2)}, u32[]{:S(2)}) collective-permute-start(f32[4,128,128]{2,1,0:T(8,128)S(1)} %get-tuple-element.63.refs_5_), channel_id=1, source_target_pairs={{0,16},{4,20},{8,24},{12,28},{16,0},{20,4},{24,8},{28,12},{1,17},{... | collective-permute-start | bytes 786440 | tf_op jit(solution)/shard_map/ppermute | solution.py:593
  13.3 7.8 %collective-permute-start.3 = (f32[8,128]{1,0:T(8,128)S(1)}, f32[8,128]{1,0:T(8,128)S(1)}, u32[]{:S(2)}, u32[]{:S(2)}) collective-permute-start(f32[8,128]{1,0:T(8,128)S(1)} %get-tuple-element.61.refs_2_), channel_id=1, source_target_pairs={{0,24},{4,28},{8,16},{12,20},{16,8},{20,12},{24,0},{28,4},{1,25},{... | collective-permute-start | bytes 12296 | tf_op jit(solution)/shard_map/ppermute | solution.py:593
  21.0 24.8 %copy-start.3 = (bf16[16,256,128]{2,1,0:T(8,128)(2,1)}, bf16[16,256,128]{2,1,0:T(8,128)(2,1)S(1)}, u32[]{:S(2)}) copy-start(bf16[16,256,128]{2,1,0:T(8,128)(2,1)S(1)} %get-tuple-element.81.q0) | copy-start | bytes 3145732
  21.1 10.6 %collective-permute-start.4 = (f32[4,128,128]{2,1,0:T(8,128)S(1)}, f32[4,128,128]{2,1,0:T(8,128)S(1)}, u32[]{:S(2)}, u32[]{:S(2)}) collective-permute-start(f32[4,128,128]{2,1,0:T(8,128)S(1)} %get-tuple-element.73), channel_id=1, source_target_pairs={{0,16},{4,20},{8,24},{12,28},{16,0},{20,4},{24,8},{28,12},{1,17},{... | collective-permute-start | bytes 786440 | tf_op jit(solution)/shard_map/ppermute | solution.py:593
  23.2 8.5 %collective-permute-start.5 = (f32[4,128,128]{2,1,0:T(8,128)S(1)}, f32[4,128,128]{2,1,0:T(8,128)S(1)}, u32[]{:S(2)}, u32[]{:S(2)}) collective-permute-start(f32[4,128,128]{2,1,0:T(8,128)S(1)} %get-tuple-element.74), channel_id=1, source_target_pairs={{0,8},{4,12},{8,0},{12,4},{16,24},{20,28},{24,16},{28,20},{1,9},{5... | collective-permute-start | bytes 786440 | tf_op jit(solution)/shard_map/ppermute | solution.py:593
  31.7 14.2 %copy-start.5 = (bf16[16,256,128]{2,1,0:T(8,128)(2,1)}, bf16[16,256,128]{2,1,0:T(8,128)(2,1)S(1)}, u32[]{:S(2)}) copy-start(bf16[16,256,128]{2,1,0:T(8,128)(2,1)S(1)} %get-tuple-element.82.q1) | copy-start | bytes 3145732
  31.9 5.7 %copy-start.25 = (f32[8,128,128]{2,1,0:T(8,128)}, f32[8,128,128]{2,1,0:T(8,128)S(1)}, u32[]{:S(2)}) copy-start(f32[8,128,128]{2,1,0:T(8,128)S(1)} %get-tuple-element.79.keep_ref) | copy-start | bytes 1572868
  31.9 2.0 %collective-permute-start.6 = (f32[8,128,128]{2,1,0:T(8,128)S(1)}, f32[8,128,128]{2,1,0:T(8,128)S(1)}, u32[]{:S(2)}, u32[]{:S(2)}) collective-permute-start(f32[8,128,128]{2,1,0:T(8,128)S(1)} %get-tuple-element.80), channel_id=1, source_target_pairs={{0,4},{4,0},{8,12},{12,8},{16,20},{20,16},{24,28},{28,24},{1,5},{5... | collective-permute-start | bytes 1572872 | tf_op jit(solution)/shard_map/ppermute | solution.py:593
  33.9 3.7 %copy-start.27 = (f32[8,128,128]{2,1,0:T(8,128)}, f32[8,128,128]{2,1,0:T(8,128)S(1)}, u32[]{:S(2)}) copy-start(f32[8,128,128]{2,1,0:T(8,128)S(1)} %collective-permute-done.6.recv_ref) | copy-start | bytes 1572868
  37.6 11.9 %copy-start.7 = (f32[16,256,128]{2,1,0:T(8,128)}, f32[16,256,128]{2,1,0:T(8,128)S(1)}, u32[]{:S(2)}) copy-start(f32[16,256,128]{2,1,0:T(8,128)S(1)} %get-tuple-element.86.att0) | copy-start | bytes 6291460
  37.6 11.9 %copy-start.9 = (f32[16,256,128]{2,1,0:T(8,128)}, f32[16,256,128]{2,1,0:T(8,128)S(1)}, u32[]{:S(2)}) copy-start(f32[16,256,128]{2,1,0:T(8,128)S(1)} %get-tuple-element.87.att1) | copy-start | bytes 6291460
  37.6 3.7 %collective-permute-start.7 = (f32[2,512]{1,0:T(2,128)S(1)}, f32[2,512]{1,0:T(2,128)S(1)}, u32[]{:S(2)}, u32[]{:S(2)}) collective-permute-start(f32[2,512]{1,0:T(2,128)S(1)} %get-tuple-element.85), channel_id=1, source_target_pairs={{0,1},{1,0},{2,3},{3,2},{4,5},{5,4},{6,7},{7,6},{8,9},{9,8},{10,11... | collective-permute-start | bytes 12296 | tf_op jit(solution)/shard_map/ppermute | solution.py:593
  41.3 4.5 %collective-permute-start.8 = (f32[2,512]{1,0:T(2,128)S(1)}, f32[2,512]{1,0:T(2,128)S(1)}, u32[]{:S(2)}, u32[]{:S(2)}) collective-permute-start(f32[2,512]{1,0:T(2,128)S(1)} %add.19), channel_id=1, source_target_pairs={{0,2},{1,3},{2,0},{3,1},{4,6},{5,7},{6,4},{7,5},{8,10},{9,11},{10,... | collective-permute-start | bytes 12296 | tf_op jit(solution)/shard_map/ppermute | solution.py:593
  53.4 2.3 %collective-permute-start.9 = (f32[8,128,128]{2,1,0:T(8,128)}, f32[8,128,128]{2,1,0:T(8,128)}, u32[]{:S(2)}, u32[]{:S(2)}) collective-permute-start(f32[8,128,128]{2,1,0:T(8,128)} %get-tuple-element.89), channel_id=1, source_target_pairs={{0,4},{4,0},{8,12},{12,8},{16,20},{20,16},{24,28},{28,24},{1,5},{5... | collective-permute-start | bytes 1572872 | tf_op jit(solution)/shard_map/ppermute | solution.py:593
  57.9 17.7 %collective-permute-start.10 = (f32[4,128,128]{2,1,0:T(8,128)S(1)}, f32[4,128,128]{2,1,0:T(8,128)S(1)}, u32[]{:S(2)}, u32[]{:S(2)}) collective-permute-start(f32[4,128,128]{2,1,0:T(8,128)S(1)} %get-tuple-element.90.refs_1_), channel_id=1, source_target_pairs={{0,8},{4,12},{8,0},{12,4},{16,24},{20,28},{24,16},{28,20},{1,9},{5... | collective-permute-start | bytes 786440 | tf_op jit(solution)/shard_map/ppermute | solution.py:593
  58.4 17.1 %collective-permute-start.11 = (f32[4,128,128]{2,1,0:T(8,128)S(1)}, f32[4,128,128]{2,1,0:T(8,128)S(1)}, u32[]{:S(2)}, u32[]{:S(2)}) collective-permute-start(f32[4,128,128]{2,1,0:T(8,128)S(1)} %get-tuple-element.91.refs_2_), channel_id=1, source_target_pairs={{0,16},{4,20},{8,24},{12,28},{16,0},{20,4},{24,8},{28,12},{1,17},{... | collective-permute-start | bytes 786440 | tf_op jit(solution)/shard_map/ppermute | solution.py:593
  64.8 14.3 %copy-start.2 = (bf16[2,16,256,128]{3,2,1,0:T(8,128)(2,1)S(1)}, bf16[2,16,256,128]{3,2,1,0:T(8,128)(2,1)}, u32[]{:S(2)}) copy-start(bf16[2,16,256,128]{3,2,1,0:T(8,128)(2,1)} %copy-done) | copy-start | bytes 6291460
  64.8 14.3 %copy-start.4 = (bf16[16,256,128]{2,1,0:T(8,128)(2,1)S(1)}, bf16[16,256,128]{2,1,0:T(8,128)(2,1)}, u32[]{:S(2)}) copy-start(bf16[16,256,128]{2,1,0:T(8,128)(2,1)} %copy-done.3) | copy-start | bytes 3145732
  64.8 14.3 %copy-start.6 = (bf16[16,256,128]{2,1,0:T(8,128)(2,1)S(1)}, bf16[16,256,128]{2,1,0:T(8,128)(2,1)}, u32[]{:S(2)}) copy-start(bf16[16,256,128]{2,1,0:T(8,128)(2,1)} %copy-done.5) | copy-start | bytes 3145732
  64.8 14.3 %copy-start.13 = (bf16[16,256,128]{2,1,0:T(8,128)(2,1)S(1)}, bf16[16,256,128]{2,1,0:T(8,128)(2,1)}, u32[]{:S(2)}) copy-start(bf16[16,256,128]{2,1,0:T(8,128)(2,1)} %copy-done.11) | copy-start | bytes 3145732
  64.8 14.3 %copy-start.16 = (bf16[16,256,128]{2,1,0:T(8,128)(2,1)S(1)}, bf16[16,256,128]{2,1,0:T(8,128)(2,1)}, u32[]{:S(2)}) copy-start(bf16[16,256,128]{2,1,0:T(8,128)(2,1)} %copy-done.14) | copy-start | bytes 3145732
  64.8 14.3 %copy-start.19 = (bf16[16,256,256]{2,1,0:T(8,128)(2,1)S(1)}, bf16[16,256,256]{2,1,0:T(8,128)(2,1)}, u32[]{:S(2)}) copy-start(bf16[16,256,256]{2,1,0:T(8,128)(2,1)} %copy-done.18) | copy-start | bytes 6291460
  64.8 14.3 %copy-start.30 = (f32[16,128,128]{2,1,0:T(8,128)S(1)}, f32[16,128,128]{2,1,0:T(8,128)}, u32[]{:S(2)}) copy-start(f32[16,128,128]{2,1,0:T(8,128)} %copy-done.29) | copy-start | bytes 3145732
  75.6 10.1 %collective-permute-start.12 = (f32[4,128,128]{2,1,0:T(8,128)S(1)}, f32[4,128,128]{2,1,0:T(8,128)S(1)}, u32[]{:S(2)}, u32[]{:S(2)}) collective-permute-start(f32[4,128,128]{2,1,0:T(8,128)S(1)} %get-tuple-element.98), channel_id=1, source_target_pairs={{0,16},{4,20},{8,24},{12,28},{16,0},{20,4},{24,8},{28,12},{1,17},{... | collective-permute-start | bytes 786440 | tf_op jit(solution)/shard_map/ppermute | solution.py:593
  77.5 8.2 %collective-permute-start.13 = (f32[4,128,128]{2,1,0:T(8,128)S(1)}, f32[4,128,128]{2,1,0:T(8,128)S(1)}, u32[]{:S(2)}, u32[]{:S(2)}) collective-permute-start(f32[4,128,128]{2,1,0:T(8,128)S(1)} %get-tuple-element.99), channel_id=1, source_target_pairs={{0,8},{4,12},{8,0},{12,4},{16,24},{20,28},{24,16},{28,20},{1,9},{5... | collective-permute-start | bytes 786440 | tf_op jit(solution)/shard_map/ppermute | solution.py:593
  80.7 5.1 %copy-start.24 = (f32[8,128,128]{2,1,0:T(8,128)S(1)}, f32[8,128,128]{2,1,0:T(8,128)}, u32[]{:S(2)}) copy-start(f32[8,128,128]{2,1,0:T(8,128)} %copy-done.22) | copy-start | bytes 1572868
  80.7 6.6 %copy-start.10 = (f32[16,256,128]{2,1,0:T(8,128)S(1)}, f32[16,256,128]{2,1,0:T(8,128)}, u32[]{:S(2)}) copy-start(f32[16,256,128]{2,1,0:T(8,128)} %copy-done.9) | copy-start | bytes 6291460
  87.2 2.9 %collective-permute-start.14 = (f32[8,128,128]{2,1,0:T(8,128)S(1)}, f32[8,128,128]{2,1,0:T(8,128)S(1)}, u32[]{:S(2)}, u32[]{:S(2)}) collective-permute-start(f32[8,128,128]{2,1,0:T(8,128)S(1)} %get-tuple-element.107), channel_id=1, source_target_pairs={{0,4},{4,0},{8,12},{12,8},{16,20},{20,16},{24,28},{28,24},{1,5},{5... | collective-permute-start | bytes 1572872 | tf_op jit(solution)/shard_map/ppermute | solution.py:593
  (15 other events, 19.2 us)

commit v5 on v4

--- a/solution.py
+++ b/solution.py
@@ -593,9 +593,9 @@
     return lax.ppermute(value, axis, [(i, i ^ bit) for i in range(count)])
 
 
-def mix(body, place, arrays, shapes, name):
+def mix(body, backward, place, arrays, shapes, name):
     def kernel(place_ref, *refs):
-        bits = [is_set(place_ref, which) for which in (LATE, RIGHT, LOW)]
+        bits = [is_set(place_ref, which) != backward for which in (LATE, RIGHT, LOW)]
         body(bits, refs[: len(arrays)], refs[len(arrays) :])
 
     return pl.pallas_call(
@@ -606,7 +606,7 @@
         compiler_params=params(4),
         cost_estimate=cost(4 * 8 * HD * HD, 16 * 8 * HD * HD),
         name=name,
-    )(place, *arrays)
+    )(place, *near(*arrays))
 
 
 OWN, PARTNER, CHIP, ROW, CORNER = range(5)
@@ -703,7 +703,7 @@
         sent[h] = jnp.where(late, enter, after)
 
 
-def entering_quad(own, send, table, place, tasks, name):
+def entering_quad(own, send, table, place, backward, tasks):
     def work(stage, after, before=()):
         if stage not in tasks:
             return before
@@ -711,36 +711,37 @@
         outputs.extend(run(after))
         return lax.optimization_barrier((before, outputs[-1]))[0]
 
+    name = "later" if backward else "earlier"
     half = own.shape[0]
     quarter = half // 2
     states, wide = (quarter, HD, HD), (quarter, HD + TILE, HD)
     got = swap(send, "seq", 1)
     if table is None:
         first, second, chip = mix(
-            mix_total_first, place, (own, got), (wide, states, (half, HD)), name + "_total"
+            mix_total_first, backward, place, (own, got), (wide, states, (half, HD)), name + "_total"
         )
     else:
         first, second = mix(
-            mix_total_again, place, (table, own, got), (states, states), name + "_total"
+            mix_total_again, backward, place, (table, own, got), (states, states), name + "_total"
         )
     one_a, one_b = swap(first, "seq", 2), swap(second, "seq", 4)
     if table is None:
         corner = swap(chip, "seq", 6)
         one_a, one_b, corner = work(1, second, (one_a, one_b, corner))
         next_a, next_b, table = mix(
-            mix_next_first, place, (own, got, chip, corner, first, second, one_a, one_b),
+            mix_next_first, backward, place, (own, got, chip, corner, first, second, one_a, one_b),
             (states, states, (5, half, HD)), name + "_next",
         )
     else:
         one_a, one_b = work(1, second, (one_a, one_b))
         next_a, next_b = mix(
-            mix_next_again, place, (table, first, second, one_a, one_b), (states, states),
+            mix_next_again, backward, place, (table, first, second, one_a, one_b), (states, states),
             name + "_next",
         )
     two_a, two_b = swap(next_a, "seq", 4), swap(next_b, "seq", 2)
     two_a, two_b = work(2, next_b, (two_a, two_b))
     kept, sent = mix(
-        mix_enter, place, (table, own, got, one_a, one_b, two_a, two_b),
+        mix_enter, backward, place, (table, own, got, one_a, one_b, two_a, two_b),
         ((half, HD, HD), (half, HD, HD)), name + "_enter",
     )
     received = swap(sent, "seq", 1)
@@ -773,16 +774,31 @@
     return kept, lax.dynamic_slice_in_dim(total, (1 - core) * half, half)
 
 
+def add(first, second):
+    def kernel(first_ref, second_ref, out_ref):
+        out_ref[...] = first_ref[...] + second_ref[...]
+
+    return pl.pallas_call(
+        kernel,
+        in_specs=[NEAR, NEAR],
+        out_specs=NEAR,
+        out_shape=in_vmem(*first.shape),
+        compiler_params=params(2),
+        name="add",
+    )(*near(first, second))
+
+
 def sum_over_heads(value):
     count = lax.axis_size("head")
     reach = 1
     while 2 * reach <= count and count % (2 * reach) == 0:
-        value = value + swap(value, "head", reach)
+        value = add(value, swap(value, "head", reach))
         reach *= 2
     part = value
     for shift in range(1, count // reach):
-        value = value + lax.ppermute(
-            part, "head", [(i, (i + shift * reach) % count) for i in range(count)]
+        value = add(
+            value,
+            lax.ppermute(part, "head", [(i, (i + shift * reach) % count) for i in range(count)]),
         )
     return value
 
@@ -793,27 +809,20 @@
 
 def on_device(query_rows, key_rows, value_rows, output_grad, norm_gain, log_decay):
     mine = lax.axis_index("seq")
-    core, *chip = ((mine >> at) % 2 for at in range(3))
-    no = jnp.zeros_like(core)
-    ahead, behind = (
-        jnp.broadcast_to(jnp.stack(marks).astype(F32)[:, None], (TILE, HD))
-        for marks in (
-            (1 - core, core, core, *chip, no, no, no),
-            (1 - core, core, 1 - core, *(1 - bit for bit in chip), no, no, no),
-        )
-    )
+    bits = [(mine >> at) % 2 for at in range(3)]
+    marks = [1 - bits[0], bits[0], *bits] + [jnp.zeros_like(mine)] * (TILE - 5)
+    place = jnp.broadcast_to(jnp.stack(marks).astype(F32)[:, None], (TILE, HD))
     table = [None]
 
     def entering(own, send, backward, tasks):
         if lax.axis_size("seq") != 8:
             return entering_any(own, send, jnp.sum(log_decay, axis=1), backward, tasks)
         kept, received, table[0] = entering_quad(
-            own, send, table[0], behind if backward else ahead, tasks,
-            "later" if backward else "earlier",
+            own, send, table[0], place, backward, tasks
         )
         return kept, received
 
-    own, send, first, kh, vh = local_state(ahead, log_decay, key_rows, value_rows)
+    own, send, first, kh, vh = local_state(place, log_decay, key_rows, value_rows)
 
     def forward_task(index):
         return lambda earlier: intra(
@@ -827,17 +836,17 @@
     q0, o0, w0, inner0 = in_0
     q1, o1, w1, inner1 = in_1
     att0, att1, sums = attend(
-        ahead, log_decay, norm_gain, keep, recv, (q0, q1, o0, o1, inner0, inner1)
+        place, log_decay, norm_gain, keep, recv, (q0, q1, o0, o1, inner0, inner1)
     )
     sums = sum_over_heads(sums)
     g0, g1, grad_own, grad_send, second = norm_grad(
-        ahead, log_decay, norm_gain, sums, (q0, q1, o0, o1, att0, att1)
+        place, log_decay, norm_gain, sums, (q0, q1, o0, o1, att0, att1)
     )
     queries, pairs, norms = [], [], []
 
     def query_task(earlier):
         return grad_query(
-            ahead, log_decay, keep, recv, follows(first, earlier), kh, vh, g0, g1
+            place, log_decay, keep, recv, follows(first, earlier), kh, vh, g0, g1
         )
 
     def pair_task(earlier):
@@ -851,7 +860,7 @@
     grad_keep, grad_recv = entering(
         grad_own, grad_send, True, {1: (query_task, queries), 2: (pair_task, pairs), 3: (norm_task, norms)}
     )
-    grad_k, grad_v = finish(ahead, log_decay, grad_keep, grad_recv, kh, vh, *pairs)
+    grad_k, grad_v = finish(place, log_decay, grad_keep, grad_recv, kh, vh, *pairs)
     return norms[0], queries[0], grad_k, grad_v
 
 

time: 98.4 us -> 81.1 us (0.82)
  local copies, waits for them, and re-layouts: 15.9 us -> 0.17 us
  Pallas kernels: 54.4 us -> 51.5 us
  waiting for transfers between devices: 9.61 us -> 11.6 us
    unnamed x64 -> x4, local copies, waits for them, and re-layouts: 15.6 us -> 0.01 us
    pallas_call x6, Pallas kernels: 2.93 us -> 0.68 us  [mix(): pl.pallas_call(kernel, in_specs=[NEAR] + [NEAR] * len(arrays), out_specs=...]
    ppermute x15, waiting for transfers between devices: 9.61 us -> 11.6 us  [swap(): return lax.ppermute(value, axis, [(i, i ^ bit) for i in range(count)])]
  transfers between devices with their start and end apart: 15 -> 15, of which waited for: 5 -> 9; matrix products, arithmetic and copies ran while one was open for 0% -> 0% of each run, Pallas kernels for 31% -> 38%
where the time goes in v5:
time: 81.1 us; the launch traced here: 80.9 us
  Pallas kernels  51.5 us (64%)
  starting transfers between devices  16.8 us (21%)
  waiting for transfers between devices  11.6 us (14%)
    ppermute x15, starting transfers between devices, swap(): return lax.ppermute(value, axis, [(i, i ^ bit) for i in range(count)])  16.8 us
    pallas_call x2, Pallas kernels, intra(): pl.pallas_call(kernel, in_specs=[NEAR] * 4 + [FAR, FAR], out_specs=[NEAR]...  12 us
    ppermute x15, waiting for transfers between devices, swap(): return lax.ppermute(value, axis, [(i, i ^ bit) for i in range(count)])  11.6 us
    pallas_call x1, Pallas kernels, grad_query(): pl.pallas_call(grad_q_kernel, grid=(2,), in_specs=[NEAR] + [NEAR] * 8, ou...  10.7 us
    pallas_call x1, Pallas kernels, finish(): pl.pallas_call(finish_kernel, in_specs=[NEAR] * 8, out_specs=[FAR, FAR],...  7.98 us
    pallas_call x1, Pallas kernels, local_state(): pl.pallas_call(state_kernel, in_specs=[NEAR, FAR, FAR, FAR], out_specs=[N...  5.76 us
    pallas_call x1, Pallas kernels, grad_key_value(): pl.pallas_call(grad_kv_kernel, in_specs=[NEAR] * 11, out_specs=[NEAR] * 2...  5.08 us
    pallas_call x1, Pallas kernels, attend(): pl.pallas_call(attend_kernel, in_specs=[NEAR] + [NEAR] * 10, out_specs=[N...  3.73 us
  transfers between devices with their start and end apart: 15, of which 9 were waited for; matrix products, arithmetic and copies ran while one was open for 0% of the time, Pallas kernels for 38%

profile of v5, /device:TPU:0, one launch (start us, length us, event | category | flops | bytes accessed | tf_op | source)
XLA Modules:
  0.0 80.9 jit_solution(9220267880273963180)
XLA Ops:
  0.8 5.8 %local_state.1 = (f32[8,136,128]{2,1,0:T(8,128)S(1)}, f32[8,136,128]{2,1,0:T(8,128)S(1)}, f32[16,128,128]{2,1,0:T(8,128)S(1)}, bf16[2,16,256,128]{3,2,1,0:T(8,128)(2,1)S(1)}, bf16[2,16,256,128]{3,2,1,0:T(8,128)(2,1)S(1)}) custom-call(f32[8,128]{1,0:T(8,128)S(1)} %broadcast_in_dim.2.place_ref, f32[16,512]{1,0:T(8,128)} %ld_ref.13, ...), custom_call_target="tpu_custom_call" | custom-call | flops 268435456 | bytes 8388608 | tf_op jit(solution)/shard_map/local_state/pallas_call | solution.py:227
  6.6 0.5 collective-permute-start
  7.1 1.6 %collective-permute-done.refs_1_.refs_2_ = f32[8,136,128]{2,1,0:T(8,128)S(1)} collective-permute-done((f32[8,136,128]{2,1,0:T(8,128)S(1)}, f32[8,136,128]{2,1,0:T(8,128)S(1)}, u32[]{:S(2)}, u32[]{:S(2)}) %collective-permute-start) | collective-permute-done | bytes 557088 | tf_op jit(solution)/shard_map/ppermute | solution.py:593
  8.7 0.1 earlier_total.1
  8.8 2.9 %collective-permute-start.1 = (f32[4,136,128]{2,1,0:T(8,128)S(1)}, f32[4,136,128]{2,1,0:T(8,128)S(1)}, u32[]{:S(2)}, u32[]{:S(2)}) collective-permute-start(f32[4,136,128]{2,1,0:T(8,128)S(1)} %get-tuple-element.62.refs_4_), channel_id=1, source_target_pairs={{0,8},{4,12},{8,0},{12,4},{16,24},{20,28},{24,16},{28,20},{1,9},{5... | collective-permute-start | bytes 835592 | tf_op jit(solution)/shard_map/ppermute | solution.py:593
  11.7 1.5 %collective-permute-start.2 = (f32[4,128,128]{2,1,0:T(8,128)S(1)}, f32[4,128,128]{2,1,0:T(8,128)S(1)}, u32[]{:S(2)}, u32[]{:S(2)}) collective-permute-start(f32[4,128,128]{2,1,0:T(8,128)S(1)} %get-tuple-element.63.refs_5_), channel_id=1, source_target_pairs={{0,16},{4,20},{8,24},{12,28},{16,0},{20,4},{24,8},{28,12},{1,17},{... | collective-permute-start | bytes 786440 | tf_op jit(solution)/shard_map/ppermute | solution.py:593
  13.3 6.4 %intra_0.1 = (bf16[16,256,128]{2,1,0:T(8,128)(2,1)S(1)}, bf16[16,256,128]{2,1,0:T(8,128)(2,1)S(1)}, bf16[16,256,256]{2,1,0:T(8,128)(2,1)S(1)}, f32[16,256,128]{2,1,0:T(8,128)S(1)}) custom-call(f32[16,512]{1,0:T(8,128)S(1)} %copy-done, bf16[2,16,256,128]{3,2,1,0:T(8,128)(2,1)S(1)} %get-tuple-element.64.kh, ...), custom_call_target="tpu_custom_call" | custom-call | flops 1073741824 | bytes 10485760 | tf_op jit(solution)/shard_map/intra_0/pallas_call | solution.py:280
  19.7 0.3 collective-permute-done.3.refs_3_
  20.1 1.7 %collective-permute-start.4 = (f32[4,128,128]{2,1,0:T(8,128)S(1)}, f32[4,128,128]{2,1,0:T(8,128)S(1)}, u32[]{:S(2)}, u32[]{:S(2)}) collective-permute-start(f32[4,128,128]{2,1,0:T(8,128)S(1)} %get-tuple-element.73), channel_id=1, source_target_pairs={{0,16},{4,20},{8,24},{12,28},{16,0},{20,4},{24,8},{28,12},{1,17},{... | collective-permute-start | bytes 786440 | tf_op jit(solution)/shard_map/ppermute | solution.py:593
  21.8 1.5 %collective-permute-start.5 = (f32[4,128,128]{2,1,0:T(8,128)S(1)}, f32[4,128,128]{2,1,0:T(8,128)S(1)}, u32[]{:S(2)}, u32[]{:S(2)}) collective-permute-start(f32[4,128,128]{2,1,0:T(8,128)S(1)} %get-tuple-element.74), channel_id=1, source_target_pairs={{0,8},{4,12},{8,0},{12,4},{16,24},{20,28},{24,16},{28,20},{1,9},{5... | collective-permute-start | bytes 786440 | tf_op jit(solution)/shard_map/ppermute | solution.py:593
  23.3 5.6 %intra_1.1 = (bf16[16,256,128]{2,1,0:T(8,128)(2,1)S(1)}, bf16[16,256,128]{2,1,0:T(8,128)(2,1)S(1)}, bf16[16,256,256]{2,1,0:T(8,128)(2,1)S(1)}, f32[16,256,128]{2,1,0:T(8,128)S(1)}) custom-call(f32[16,512]{1,0:T(8,128)S(1)} %copy-done, bf16[2,16,256,128]{3,2,1,0:T(8,128)(2,1)S(1)} %get-tuple-element.64.kh, ...), custom_call_target="tpu_custom_call" | custom-call | flops 1073741824 | bytes 10485760 | tf_op jit(solution)/shard_map/intra_1/pallas_call | solution.py:280
  29.0 0.1 collective-permute-done.5.refs_6_
  29.1 0.2 earlier_enter.1
  29.3 1.9 %collective-permute-done.6.recv_ref = f32[8,128,128]{2,1,0:T(8,128)S(1)} collective-permute-done((f32[8,128,128]{2,1,0:T(8,128)S(1)}, f32[8,128,128]{2,1,0:T(8,128)S(1)}, u32[]{:S(2)}, u32[]{:S(2)}) %collective-permute-start.6) | collective-permute-done | bytes 524320 | tf_op jit(solution)/shard_map/ppermute | solution.py:593
  31.2 3.7 %attend.1 = (f32[16,256,128]{2,1,0:T(8,128)S(1)}, f32[16,256,128]{2,1,0:T(8,128)S(1)}, f32[2,512]{1,0:T(2,128)S(1)}) custom-call(f32[8,128]{1,0:T(8,128)S(1)} %broadcast_in_dim.2.place_ref, f32[16,512]{1,0:T(8,128)S(1)} %copy-done, f32[16,128]{1,0:T(8,128)S(1)} %copy-done.1, f32[8,128,128]{2,1,0:T(8,128)S(1)} %get-tuple-element.79.keep_ref, ...), custom_call_target="tpu_custom_call" | custom-call | flops 536870912 | bytes 16777216 | tf_op jit(solution)/shard_map/attend/pallas_call | solution.py:341
  34.9 1.6 %collective-permute-start.7 = (f32[2,512]{1,0:T(2,128)S(1)}, f32[2,512]{1,0:T(2,128)S(1)}, u32[]{:S(2)}, u32[]{:S(2)}) collective-permute-start(f32[2,512]{1,0:T(2,128)S(1)} %get-tuple-element.85.first_ref), channel_id=1, source_target_pairs={{0,1},{1,0},{2,3},{3,2},{4,5},{5,4},{6,7},{7,6},{8,9},{9,8},{10,11... | collective-permute-start | bytes 12296 | tf_op jit(solution)/shard_map/ppermute | solution.py:593
  36.5 2.0 %collective-permute-done.7.second_ref = f32[2,512]{1,0:T(2,128)S(1)} collective-permute-done((f32[2,512]{1,0:T(2,128)S(1)}, f32[2,512]{1,0:T(2,128)S(1)}, u32[]{:S(2)}, u32[]{:S(2)}) %collective-permute-start.7) | collective-permute-done | bytes 4128 | tf_op jit(solution)/shard_map/ppermute | solution.py:593
  38.6 2.6 %collective-permute-start.8 = (f32[2,512]{1,0:T(2,128)S(1)}, f32[2,512]{1,0:T(2,128)S(1)}, u32[]{:S(2)}, u32[]{:S(2)}) collective-permute-start(f32[2,512]{1,0:T(2,128)S(1)} %add.15.first_ref), channel_id=1, source_target_pairs={{0,2},{1,3},{2,0},{3,1},{4,6},{5,7},{6,4},{7,5},{8,10},{9,11},{10,... | collective-permute-start | bytes 12296 | tf_op jit(solution)/shard_map/ppermute | solution.py:593
  41.2 1.9 %collective-permute-done.8.second_ref = f32[2,512]{1,0:T(2,128)S(1)} collective-permute-done((f32[2,512]{1,0:T(2,128)S(1)}, f32[2,512]{1,0:T(2,128)S(1)}, u32[]{:S(2)}, u32[]{:S(2)}) %collective-permute-start.8) | collective-permute-done | bytes 4128 | tf_op jit(solution)/shard_map/ppermute | solution.py:593
  43.1 3.0 %norm_grad.1 = (bf16[16,256,128]{2,1,0:T(8,128)(2,1)S(1)}, bf16[16,256,128]{2,1,0:T(8,128)(2,1)S(1)}, f32[8,128,128]{2,1,0:T(8,128)S(1)}, f32[8,128,128]{2,1,0:T(8,128)S(1)}, f32[16,128,128]{2,1,0:T(8,128)S(1)}) custom-call(f32[8,128]{1,0:T(8,128)S(1)} %broadcast_in_dim.2.place_ref, f32[16,512]{1,0:T(8,128)S(1)} %copy-done, f32[16,128]{1,0:T(8,128)S(1)} %copy-done.1, ...), custom_call_target="tpu_custom_call" | custom-call | flops 268435456 | bytes 14680064 | tf_op jit(solution)/shard_map/norm_grad/pallas_call | solution.py:397
  46.1 1.9 %collective-permute-done.9.refs_2_ = f32[8,128,128]{2,1,0:T(8,128)S(1)} collective-permute-done((f32[8,128,128]{2,1,0:T(8,128)S(1)}, f32[8,128,128]{2,1,0:T(8,128)S(1)}, u32[]{:S(2)}, u32[]{:S(2)}) %collective-permute-start.9) | collective-permute-done | bytes 524320 | tf_op jit(solution)/shard_map/ppermute | solution.py:593
  48.1 1.6 %collective-permute-start.10 = (f32[4,128,128]{2,1,0:T(8,128)S(1)}, f32[4,128,128]{2,1,0:T(8,128)S(1)}, u32[]{:S(2)}, u32[]{:S(2)}) collective-permute-start(f32[4,128,128]{2,1,0:T(8,128)S(1)} %get-tuple-element.90.refs_1_), channel_id=1, source_target_pairs={{0,8},{4,12},{8,0},{12,4},{16,24},{20,28},{24,16},{28,20},{1,9},{5... | collective-permute-start | bytes 786440 | tf_op jit(solution)/shard_map/ppermute | solution.py:593
  49.7 0.5 collective-permute-start.11
  50.2 10.7 %grad_query.1 = (bf16[512,16,128]{2,1,0:T(8,128)(2,1)}, bf16[2,16,256,256]{3,2,1,0:T(8,128)(2,1)S(1)}) custom-call(f32[8,128]{1,0:T(8,128)S(1)} %broadcast_in_dim.2.place_ref, f32[16,512]{1,0:T(8,128)S(1)} %copy-done, f32[8,128,128]{2,1,0:T(8,128)S(1)} %get-tuple-element.79.keep_ref, f32[8,128,128]{2,1,0:T(8,128)S(1)} %collective-permute-done.6.recv_ref, ...), custom_call_target="tpu_custom_call" | custom-call | flops 1610612736 | bytes 12582912 | tf_op jit(solution)/shard_map/grad_query/pallas_call | solution.py:490
  61.0 1.6 %collective-permute-start.12 = (f32[4,128,128]{2,1,0:T(8,128)S(1)}, f32[4,128,128]{2,1,0:T(8,128)S(1)}, u32[]{:S(2)}, u32[]{:S(2)}) collective-permute-start(f32[4,128,128]{2,1,0:T(8,128)S(1)} %get-tuple-element.98), channel_id=1, source_target_pairs={{0,16},{4,20},{8,24},{12,28},{16,0},{20,4},{24,8},{28,12},{1,17},{... | collective-permute-start | bytes 786440 | tf_op jit(solution)/shard_map/ppermute | solution.py:593
  62.6 0.5 collective-permute-start.13
  63.1 5.1 %grad_key_value.1 = (f32[2,16,256,128]{3,2,1,0:T(8,128)S(1)}, f32[2,16,256,128]{3,2,1,0:T(8,128)S(1)}) custom-call(f32[16,512]{1,0:T(8,128)S(1)} %copy-done, bf16[2,16,256,256]{3,2,1,0:T(8,128)(2,1)S(1)} %get-tuple-element.95.gs_ref, bf16[16,256,256]{2,1,0:T(8,128)(2,1)S(1)} %get-tuple-element.100.w0, bf16[16,256,256]{2,1,0:T(8,128)(2,1)S(1)} %get-tuple-element.101.w1, ...), custom_call_target="tpu_custom_call" | custom-call | flops 1610612736 | bytes 31457280 | tf_op jit(solution)/shard_map/grad_key_value/pallas_call | solution.py:525
  68.2 0.6 collective-permute-done.12.refs_5_
  68.8 1.2 %collective-permute-done.13.refs_6_ = f32[4,128,128]{2,1,0:T(8,128)S(1)} collective-permute-done((f32[4,128,128]{2,1,0:T(8,128)S(1)}, f32[4,128,128]{2,1,0:T(8,128)S(1)}, u32[]{:S(2)}, u32[]{:S(2)}) %collective-permute-start.13) | collective-permute-done | bytes 262176 | tf_op jit(solution)/shard_map/ppermute | solution.py:593
  70.1 0.2 later_enter.1
  70.3 2.6 %normed_rows.1 = bf16[512,16,128]{2,1,0:T(8,128)(2,1)} custom-call(f32[16,128]{1,0:T(8,128)S(1)} %copy-done.1, f32[2,512]{1,0:T(2,128)S(1)} %add.16.sums_ref, f32[16,256,128]{2,1,0:T(8,128)S(1)} %get-tuple-element.86.att0, f32[16,256,128]{2,1,0:T(8,128)S(1)} %get-tuple-element.87.att1), custom_call_target="tpu_custom_call" | custom-call | flops 3145728 | bytes 6291456 | tf_op jit(solution)/shard_map/normed_rows/pallas_call | solution.py:446
  72.9 8.0 %finish.1 = (bf16[512,16,128]{2,1,0:T(8,128)(2,1)}, bf16[512,16,128]{2,1,0:T(8,128)(2,1)}) custom-call(f32[8,128]{1,0:T(8,128)S(1)} %broadcast_in_dim.2.place_ref, f32[16,512]{1,0:T(8,128)S(1)} %copy-done, f32[8,128,128]{2,1,0:T(8,128)S(1)} %get-tuple-element.110.keep_ref, f32[8,128,128]{2,1,0:T(8,128)S(1)} %collective-permute-done.14.recv_ref, ...), custom_call_target="tpu_custom_call" | custom-call | flops 1073741824 | bytes 16777216 | tf_op jit(solution)/shard_map/finish/pallas_call | solution.py:572
  (23 shorter events, 0.7 us)
Async XLA Ops:
  0.8 12.4 %copy-start = (f32[16,512]{1,0:T(8,128)S(1)}, f32[16,512]{1,0:T(8,128)}, u32[]{:S(2)}) copy-start(f32[16,512]{1,0:T(8,128)} %ld_ref.13) | copy-start | bytes 98308
  6.6 2.1 %collective-permute-start = (f32[8,136,128]{2,1,0:T(8,128)S(1)}, f32[8,136,128]{2,1,0:T(8,128)S(1)}, u32[]{:S(2)}, u32[]{:S(2)}) collective-permute-start(f32[8,136,128]{2,1,0:T(8,128)S(1)} %get-tuple-element.60), channel_id=1, source_target_pairs={{0,4},{4,0},{8,12},{12,8},{16,20},{20,16},{24,28},{28,24},{1,5},{5... | collective-permute-start | bytes 1671176 | tf_op jit(solution)/shard_map/ppermute | solution.py:593
  8.8 11.2 %collective-permute-start.1 = (f32[4,136,128]{2,1,0:T(8,128)S(1)}, f32[4,136,128]{2,1,0:T(8,128)S(1)}, u32[]{:S(2)}, u32[]{:S(2)}) collective-permute-start(f32[4,136,128]{2,1,0:T(8,128)S(1)} %get-tuple-element.62.refs_4_), channel_id=1, source_target_pairs={{0,8},{4,12},{8,0},{12,4},{16,24},{20,28},{24,16},{28,20},{1,9},{5... | collective-permute-start | bytes 835592 | tf_op jit(solution)/shard_map/ppermute | solution.py:593
  11.7 8.3 %collective-permute-start.2 = (f32[4,128,128]{2,1,0:T(8,128)S(1)}, f32[4,128,128]{2,1,0:T(8,128)S(1)}, u32[]{:S(2)}, u32[]{:S(2)}) collective-permute-start(f32[4,128,128]{2,1,0:T(8,128)S(1)} %get-tuple-element.63.refs_5_), channel_id=1, source_target_pairs={{0,16},{4,20},{8,24},{12,28},{16,0},{20,4},{24,8},{28,12},{1,17},{... | collective-permute-start | bytes 786440 | tf_op jit(solution)/shard_map/ppermute | solution.py:593
  13.2 6.7 %collective-permute-start.3 = (f32[8,128]{1,0:T(8,128)S(1)}, f32[8,128]{1,0:T(8,128)S(1)}, u32[]{:S(2)}, u32[]{:S(2)}) collective-permute-start(f32[8,128]{1,0:T(8,128)S(1)} %get-tuple-element.61.refs_2_), channel_id=1, source_target_pairs={{0,24},{4,28},{8,16},{12,20},{16,8},{20,12},{24,0},{28,4},{1,25},{... | collective-permute-start | bytes 12296 | tf_op jit(solution)/shard_map/ppermute | solution.py:593
  20.1 8.9 %collective-permute-start.4 = (f32[4,128,128]{2,1,0:T(8,128)S(1)}, f32[4,128,128]{2,1,0:T(8,128)S(1)}, u32[]{:S(2)}, u32[]{:S(2)}) collective-permute-start(f32[4,128,128]{2,1,0:T(8,128)S(1)} %get-tuple-element.73), channel_id=1, source_target_pairs={{0,16},{4,20},{8,24},{12,28},{16,0},{20,4},{24,8},{28,12},{1,17},{... | collective-permute-start | bytes 786440 | tf_op jit(solution)/shard_map/ppermute | solution.py:593
  21.8 7.2 %collective-permute-start.5 = (f32[4,128,128]{2,1,0:T(8,128)S(1)}, f32[4,128,128]{2,1,0:T(8,128)S(1)}, u32[]{:S(2)}, u32[]{:S(2)}) collective-permute-start(f32[4,128,128]{2,1,0:T(8,128)S(1)} %get-tuple-element.74), channel_id=1, source_target_pairs={{0,8},{4,12},{8,0},{12,4},{16,24},{20,28},{24,16},{28,20},{1,9},{5... | collective-permute-start | bytes 786440 | tf_op jit(solution)/shard_map/ppermute | solution.py:593
  28.9 2.3 %copy-start.1 = (f32[16,128]{1,0:T(8,128)S(1)}, f32[16,128]{1,0:T(8,128)}, u32[]{:S(2)}) copy-start(f32[16,128]{1,0:T(8,128)} %gain_ref.4) | copy-start | bytes 24580
  29.2 2.0 %collective-permute-start.6 = (f32[8,128,128]{2,1,0:T(8,128)S(1)}, f32[8,128,128]{2,1,0:T(8,128)S(1)}, u32[]{:S(2)}, u32[]{:S(2)}) collective-permute-start(f32[8,128,128]{2,1,0:T(8,128)S(1)} %get-tuple-element.80), channel_id=1, source_target_pairs={{0,4},{4,0},{8,12},{12,8},{16,20},{20,16},{24,28},{28,24},{1,5},{5... | collective-permute-start | bytes 1572872 | tf_op jit(solution)/shard_map/ppermute | solution.py:593
  34.9 3.6 %collective-permute-start.7 = (f32[2,512]{1,0:T(2,128)S(1)}, f32[2,512]{1,0:T(2,128)S(1)}, u32[]{:S(2)}, u32[]{:S(2)}) collective-permute-start(f32[2,512]{1,0:T(2,128)S(1)} %get-tuple-element.85.first_ref), channel_id=1, source_target_pairs={{0,1},{1,0},{2,3},{3,2},{4,5},{5,4},{6,7},{7,6},{8,9},{9,8},{10,11... | collective-permute-start | bytes 12296 | tf_op jit(solution)/shard_map/ppermute | solution.py:593
  38.6 4.5 %collective-permute-start.8 = (f32[2,512]{1,0:T(2,128)S(1)}, f32[2,512]{1,0:T(2,128)S(1)}, u32[]{:S(2)}, u32[]{:S(2)}) collective-permute-start(f32[2,512]{1,0:T(2,128)S(1)} %add.15.first_ref), channel_id=1, source_target_pairs={{0,2},{1,3},{2,0},{3,1},{4,6},{5,7},{6,4},{7,5},{8,10},{9,11},{10,... | collective-permute-start | bytes 12296 | tf_op jit(solution)/shard_map/ppermute | solution.py:593
  46.1 2.0 %collective-permute-start.9 = (f32[8,128,128]{2,1,0:T(8,128)S(1)}, f32[8,128,128]{2,1,0:T(8,128)S(1)}, u32[]{:S(2)}, u32[]{:S(2)}) collective-permute-start(f32[8,128,128]{2,1,0:T(8,128)S(1)} %get-tuple-element.89), channel_id=1, source_target_pairs={{0,4},{4,0},{8,12},{12,8},{16,20},{20,16},{24,28},{28,24},{1,5},{5... | collective-permute-start | bytes 1572872 | tf_op jit(solution)/shard_map/ppermute | solution.py:593
  48.1 12.8 %collective-permute-start.10 = (f32[4,128,128]{2,1,0:T(8,128)S(1)}, f32[4,128,128]{2,1,0:T(8,128)S(1)}, u32[]{:S(2)}, u32[]{:S(2)}) collective-permute-start(f32[4,128,128]{2,1,0:T(8,128)S(1)} %get-tuple-element.90.refs_1_), channel_id=1, source_target_pairs={{0,8},{4,12},{8,0},{12,4},{16,24},{20,28},{24,16},{28,20},{1,9},{5... | collective-permute-start | bytes 786440 | tf_op jit(solution)/shard_map/ppermute | solution.py:593
  49.7 11.2 %collective-permute-start.11 = (f32[4,128,128]{2,1,0:T(8,128)S(1)}, f32[4,128,128]{2,1,0:T(8,128)S(1)}, u32[]{:S(2)}, u32[]{:S(2)}) collective-permute-start(f32[4,128,128]{2,1,0:T(8,128)S(1)} %get-tuple-element.91.refs_2_), channel_id=1, source_target_pairs={{0,16},{4,20},{8,24},{12,28},{16,0},{20,4},{24,8},{28,12},{1,17},{... | collective-permute-start | bytes 786440 | tf_op jit(solution)/shard_map/ppermute | solution.py:593
  61.0 7.9 %collective-permute-start.12 = (f32[4,128,128]{2,1,0:T(8,128)S(1)}, f32[4,128,128]{2,1,0:T(8,128)S(1)}, u32[]{:S(2)}, u32[]{:S(2)}) collective-permute-start(f32[4,128,128]{2,1,0:T(8,128)S(1)} %get-tuple-element.98), channel_id=1, source_target_pairs={{0,16},{4,20},{8,24},{12,28},{16,0},{20,4},{24,8},{28,12},{1,17},{... | collective-permute-start | bytes 786440 | tf_op jit(solution)/shard_map/ppermute | solution.py:593
  62.6 7.5 %collective-permute-start.13 = (f32[4,128,128]{2,1,0:T(8,128)S(1)}, f32[4,128,128]{2,1,0:T(8,128)S(1)}, u32[]{:S(2)}, u32[]{:S(2)}) collective-permute-start(f32[4,128,128]{2,1,0:T(8,128)S(1)} %get-tuple-element.99), channel_id=1, source_target_pairs={{0,8},{4,12},{8,0},{12,4},{16,24},{20,28},{24,16},{28,20},{1,9},{5... | collective-permute-start | bytes 786440 | tf_op jit(solution)/shard_map/ppermute | solution.py:593
  70.2 2.7 %collective-permute-start.14 = (f32[8,128,128]{2,1,0:T(8,128)S(1)}, f32[8,128,128]{2,1,0:T(8,128)S(1)}, u32[]{:S(2)}, u32[]{:S(2)}) collective-permute-start(f32[8,128,128]{2,1,0:T(8,128)S(1)} %get-tuple-element.107), channel_id=1, source_target_pairs={{0,4},{4,0},{8,12},{12,8},{16,20},{20,16},{24,28},{28,24},{1,5},{5... | collective-permute-start | bytes 1572872 | tf_op jit(solution)/shard_map/ppermute | solution.py:593

commit v6 on v5

--- a/solution.py
+++ b/solution.py
@@ -78,21 +78,26 @@
     )
 
 
-def causal(table, row, columns):
+def decay_quarters(row, columns):
     half = row.shape[1] // 2
     lower = lax.broadcasted_iota(jnp.int32, (half, half), 0) >= lax.broadcasted_iota(
         jnp.int32, (half, half), 1
     )
     quarters = []
-    for t in range(2):
-        for s in range(t + 1):
-            gap = columns[t * half : (t + 1) * half] - row[:, s * half : (s + 1) * half]
-            if t == s:
-                gap = jnp.where(lower, gap, -jnp.inf)
-            part = table[t * half : (t + 1) * half, s * half : (s + 1) * half]
-            quarters.append((part * jnp.exp(gap)).astype(BF16))
-    top = jnp.concatenate([quarters[0], jnp.zeros_like(quarters[0])], axis=1)
-    return jnp.concatenate([top, jnp.concatenate(quarters[1:], axis=1)], axis=0)
+    for t, s in ((0, 0), (1, 0), (1, 1)):
+        gap = columns[t * half : (t + 1) * half] - row[:, s * half : (s + 1) * half]
+        quarters.append(jnp.exp(jnp.where(lower, gap, -jnp.inf) if t == s else gap))
+    return quarters
+
+
+def causal(table, quarters):
+    half = table.shape[0] // 2
+    first, second, third = (
+        (table[t * half : (t + 1) * half, s * half : (s + 1) * half] * quarter).astype(BF16)
+        for (t, s), quarter in zip(((0, 0), (1, 0), (1, 1)), quarters)
+    )
+    top = jnp.concatenate([first, jnp.zeros_like(first)], axis=1)
+    return jnp.concatenate([top, jnp.concatenate([second, third], axis=1)], axis=0)
 
 
 def transposed_dot(a, b):
@@ -250,7 +255,8 @@
 def intra(index, log_decay, kh, vh, first, query_rows, output_grad):
     tok, heads, dim = query_rows.shape
 
-    def kernel(ld_ref, kh, vh, first_ref, q_hbm, o_hbm, qh, oh, w_ref, inner_ref,
+    def kernel(ld_ref, kh, vh, first_ref, q_hbm, o_hbm,
+               qh, oh, w_ref, decays_ref, columns_ref, inner_ref,
                q_raw, o_raw, cum, sems):
         at = pl.ds(index * BLOCK, BLOCK)
         copy_q = pltpu.make_async_copy(q_hbm.at[at], q_raw, sems.at[0])
@@ -267,11 +273,16 @@
             query = qh[h]
             row = cum[pl.ds(h, 1), :]
             columns = as_columns(row)
-            weights = causal(dot_rows(query, kh[index, h]), row, columns)
+            quarters = decay_quarters(row, columns)
+            for at, quarter in enumerate(quarters):
+                decays_ref[h, at] = quarter
+            weights = causal(dot_rows(query, kh[index, h]), quarters)
             w_ref[h] = weights
             inner = dot(weights, vh[index, h])
+            columns = jnp.exp(columns)
+            columns_ref[h] = columns
             if index:
-                inner += jnp.exp(columns) * times_state(query, first_ref[h])
+                inner += columns * times_state(query, first_ref[h])
             inner_ref[h] = inner
 
         each_head(heads, 2, one)
@@ -280,9 +291,11 @@
     return pl.pallas_call(
         kernel,
         in_specs=[NEAR] * 4 + [FAR, FAR],
-        out_specs=[NEAR] * 4,
+        out_specs=[NEAR] * 6,
         out_shape=[
-            by_head, by_head, in_vmem(heads, BLOCK, BLOCK, kind=BF16), in_vmem(heads, BLOCK, dim),
+            by_head, by_head, in_vmem(heads, BLOCK, BLOCK, kind=BF16),
+            in_vmem(heads, 3, BLOCK // 2, BLOCK // 2), in_vmem(heads, BLOCK, dim),
+            in_vmem(heads, BLOCK, dim),
         ],
         scratch_shapes=[
             pltpu.VMEM((BLOCK, heads, dim), BF16),
@@ -305,25 +318,25 @@
 
 
 def attend_kernel(
-    place_ref, ld_ref, gain_ref, keep_ref, recv_ref, q0, q1, o0, o1, inner0, inner1,
-    att0, att1, sums_ref, cum, squares, products,
+    place_ref, gain_ref, keep_ref, recv_ref, q0, q1, o0, o1, columns0, columns1, inner0, inner1,
+    att0, att1, sums_ref, squares, products,
 ):
-    cum[0] = block_cum(ld_ref[:, :BLOCK])
-    cum[1] = cum[0, :, BLOCK - 1 :] + block_cum(ld_ref[:, BLOCK:])
+    heads = gain_ref.shape[0]
     squares[...] = jnp.zeros_like(squares)
     products[...] = jnp.zeros_like(products)
 
     def one(h):
         state = whole_state(place_ref, keep_ref, recv_ref, h)
         gain = gain_ref[pl.ds(h, 1), :]
-        for b, (q, o, inner, att) in enumerate(((q0, o0, inner0, att0), (q1, o1, inner1, att1))):
-            columns = as_columns(jnp.exp(cum[b, pl.ds(h, 1), :]))
-            attended = inner[h] + columns * times_state(q[h], state)
+        blocks = ((q0, o0, columns0, inner0, att0), (q1, o1, columns1, inner1, att1))
+        for b, (q, o, columns, inner, att) in enumerate(blocks):
+            attended = inner[h] + columns[h] * times_state(q[h], state)
             att[h] = attended
             squares[b] += attended * attended
             products[b] += gain * o[h].astype(F32) * attended
-
-    each_head(ld_ref.shape[0], 2, one)
+            state = columns[h, BLOCK - 1 :] * state
+
+    each_head(heads, 2, one)
     ones = jnp.ones((8, HD), F32)
     for b in range(2):
         for at, total in enumerate((squares, products)):
@@ -334,24 +347,74 @@
             sums_ref[at : at + 1, b * BLOCK : (b + 1) * BLOCK] = line[:1]
 
 
-def attend(place, log_decay, gain, keep, recv, parts):
-    heads, tok = log_decay.shape
-    dim = HD
+def attend(place, gain, keep, recv, parts):
+    heads, dim = gain.shape
+    tok = 2 * BLOCK
     by_head = in_vmem(heads, BLOCK, dim)
     return pl.pallas_call(
         attend_kernel,
-        in_specs=[NEAR] + [NEAR] * 10,
+        in_specs=[NEAR] * 12,
         out_specs=[NEAR] * 3,
         out_shape=[by_head, by_head, in_vmem(2, tok)],
-        scratch_shapes=[
-            pltpu.VMEM((2, heads, BLOCK), F32),
-            pltpu.VMEM((2, BLOCK, dim), F32),
-            pltpu.VMEM((2, BLOCK, dim), F32),
-        ],
+        scratch_shapes=[pltpu.VMEM((2, BLOCK, dim), F32), pltpu.VMEM((2, BLOCK, dim), F32)],
         compiler_params=params(6),
         cost_estimate=cost(4 * heads * tok * dim * dim, 16 * heads * tok * dim),
         name="attend",
-    )(place, log_decay, gain, *near(keep, recv, *parts))
+    )(place, gain, *near(keep, recv, *parts))
+
+
+def queries_kernel(ld_ref, q0, q1, out_ref, ends_ref, cum):
+    heads = ld_ref.shape[0]
+    for b in range(2):
+        cum[b] = jnp.exp(block_cum(ld_ref[:, b * BLOCK : (b + 1) * BLOCK]))
+        ends_ref[b] = jnp.broadcast_to(cum[b, :, BLOCK - 1 :], (heads, HD))
+
+    def one(h):
+        for b, q in enumerate((q0, q1)):
+            out_ref[b, h] = (q[h].astype(F32).T * cum[b, pl.ds(h, 1), :]).astype(BF16)
+
+    each_head(heads, 2, one)
+
+
+def scaled_queries(log_decay, q0, q1):
+    heads, tok = log_decay.shape
+    return pl.pallas_call(
+        queries_kernel,
+        in_specs=[NEAR] * 3,
+        out_specs=[NEAR] * 2,
+        out_shape=[in_vmem(2, heads, HD, BLOCK, kind=BF16), in_vmem(2, heads, HD)],
+        scratch_shapes=[pltpu.VMEM((2, heads, BLOCK), F32)],
+        compiler_params=params(4),
+        cost_estimate=cost(2 * heads * tok * HD, 4 * heads * tok * HD),
+        name="scaled_queries",
+    )(log_decay, *near(q0, q1))
+
+
+def remaining_kernel(ld_ref, out_ref, cum):
+    heads = ld_ref.shape[0]
+    for b in range(2):
+        total = block_cum(ld_ref[:, b * BLOCK : (b + 1) * BLOCK])
+        cum[b] = jnp.exp(total[:, BLOCK - 1 :] - total)
+
+    def one(h):
+        for b in range(2):
+            out_ref[b, h] = as_columns(cum[b, pl.ds(h, 1), :])
+
+    each_head(heads, 2, one)
+
+
+def remaining_decay(log_decay):
+    heads, tok = log_decay.shape
+    return pl.pallas_call(
+        remaining_kernel,
+        in_specs=[NEAR],
+        out_specs=NEAR,
+        out_shape=in_vmem(2, heads, BLOCK, HD),
+        scratch_shapes=[pltpu.VMEM((2, heads, BLOCK), F32)],
+        compiler_params=params(4),
+        cost_estimate=cost(heads * tok * HD, 4 * heads * tok * HD),
+        name="remaining_decay",
+    )(log_decay)
 
 
 def inverse_rms(sums_ref, b):
@@ -362,55 +425,50 @@
 
 
 def norm_grad_kernel(
-    place_ref, ld_ref, gain_ref, sums_ref, q0, q1, o0, o1, att0, att1,
-    g0, g1, own_ref, send_ref, second_ref, cum, scales, acc,
+    place_ref, ends_ref, gain_ref, sums_ref, queries_ref, o0, o1, att0, att1,
+    g0, g1, own_ref, send_ref, second_ref, scales, acc,
 ):
-    heads = ld_ref.shape[0]
     for b in range(2):
-        cum[b] = block_cum(ld_ref[:, b * BLOCK : (b + 1) * BLOCK])
         inv, mean = inverse_rms(sums_ref, b)
         scales[b, 0] = as_columns(inv)
         scales[b, 1] = as_columns(inv * inv * mean)
 
     def one(h):
         gain = gain_ref[pl.ds(h, 1), :]
-        ends = []
-        for b, (q, o, att, g) in enumerate(((q0, o0, att0, g0), (q1, o1, att1, g1))):
+        starts = []
+        for b, (o, att, g) in enumerate(((o0, att0, g0), (o1, att1, g1))):
             grad = gain * o[h].astype(F32) * scales[b, 0] - att[h] * scales[b, 1]
             grad = grad.astype(BF16)
             g[h] = grad
-            queries = q[h].astype(F32).T * jnp.exp(cum[b, pl.ds(h, 1), :])
-            ends.append(dot(queries.astype(BF16), grad))
-        second_ref[h] = ends[1]
-        first_decay = jnp.exp(cum[0, pl.ds(h, 1), :][:, BLOCK - 1 :])
-        acc[h] = ends[0] + first_decay * ends[1]
-
-    each_head(heads, 2, one)
+            starts.append(dot(queries_ref[b, h], grad))
+        second_ref[h] = starts[1]
+        acc[h] = starts[0] + ends_ref[0, pl.ds(h, 1)] * starts[1]
+
+    each_head(gain_ref.shape[0], 2, one)
     split_halves(place_ref, acc, own_ref, send_ref)
 
 
-def norm_grad(place, log_decay, gain, sums, parts):
-    heads, tok = log_decay.shape
-    dim = HD
+def norm_grad(place, ends, gain, sums, parts):
+    heads, dim = gain.shape
+    tok = 2 * BLOCK
     half = heads // 2
     by_head = in_vmem(heads, BLOCK, dim, kind=BF16)
     return pl.pallas_call(
         norm_grad_kernel,
-        in_specs=[NEAR] + [NEAR] * 9,
+        in_specs=[NEAR] * 9,
         out_specs=[NEAR] * 5,
         out_shape=[
             by_head, by_head, in_vmem(half, dim, dim), in_vmem(half, dim, dim),
             in_vmem(heads, dim, dim),
         ],
         scratch_shapes=[
-            pltpu.VMEM((2, heads, BLOCK), F32),
             pltpu.VMEM((2, 2, BLOCK, dim), F32),
             pltpu.VMEM((heads, dim, dim), F32),
         ],
         compiler_params=params(6),
         cost_estimate=cost(2 * heads * tok * dim * dim, 14 * heads * tok * dim),
         name="norm_grad",
-    )(place, log_decay, gain, sums, *near(*parts))
+    )(place, ends, gain, sums, *near(*parts))
 
 
 def on_block(work):
@@ -457,25 +515,22 @@
 
 
 def grad_q_kernel(
-    place_ref, ld_ref, keep_ref, recv_ref, first_ref, kh, vh, g0, g1, out_ref, gs_ref, cum, rows,
+    place_ref, ends_ref, keep_ref, recv_ref, first_ref, kh, vh, g0, g1, decays0, decays1,
+    columns0, columns1, out_ref, gs_ref, rows,
 ):
-    heads = ld_ref.shape[0]
+    heads = ends_ref.shape[1]
 
     def work(b):
-        g = (g0, g1)[b]
-        for x in range(2):
-            cum[x] = block_cum(ld_ref[:, x * BLOCK : (x + 1) * BLOCK])
+        g, decays, columns = ((g0, decays0, columns0), (g1, decays1, columns1))[b]
 
         def one(h):
-            row = cum[b, pl.ds(h, 1), :]
-            columns = as_columns(row)
-            scores = causal(dot_rows(g[h], vh[b, h]), row, columns)
+            quarters = [decays[h, at] for at in range(3)]
+            scores = causal(dot_rows(g[h], vh[b, h]), quarters)
             gs_ref[b, h] = scores
             state = whole_state(place_ref, keep_ref, recv_ref, h)
             if b:
-                state = jnp.exp(cum[0, pl.ds(h, 1), :][:, BLOCK - 1 :]) * state + first_ref[h]
-            grad = dot(scores, kh[b, h]) + jnp.exp(columns) * times_state_t(g[h], state)
-            rows[h] = grad
+                state = ends_ref[0, pl.ds(h, 1)] * state + first_ref[h]
+            rows[h] = dot(scores, kh[b, h]) + columns[h] * times_state_t(g[h], state)
 
         each_head(heads, 2, one)
 
@@ -483,74 +538,66 @@
     from_heads(out_ref, rows, 0, BLOCK)
 
 
-def grad_query(place, log_decay, keep, recv, first, kh, vh, g0, g1):
-    heads, tok = log_decay.shape
-    dim = HD
+def grad_query(place, ends, keep, recv, first, parts):
+    _, heads, dim = ends.shape
+    tok = 2 * BLOCK
     spec, shape = raw_output(heads, tok)
     return pl.pallas_call(
         grad_q_kernel,
         grid=(2,),
-        in_specs=[NEAR] + [NEAR] * 8,
+        in_specs=[NEAR] * 13,
         out_specs=[spec, NEAR],
         out_shape=[shape, in_vmem(2, heads, BLOCK, BLOCK, kind=BF16)],
-        scratch_shapes=[pltpu.VMEM((2, heads, BLOCK), F32), pltpu.VMEM((heads, BLOCK, dim), F32)],
+        scratch_shapes=[pltpu.VMEM((heads, BLOCK, dim), F32)],
         compiler_params=params(8),
         cost_estimate=cost(
             4 * heads * tok * dim * (BLOCK + dim), 12 * heads * tok * dim, heads * tok * BLOCK
         ),
         name="grad_query",
-    )(place, log_decay, *near(keep, recv, first, kh, vh, g0, g1))
+    )(place, ends, *near(keep, recv, first, *parts))
 
 
 def grad_kv_kernel(
-    ld_ref, gs_ref, w0, w1, q0, q1, kh, vh, g0, g1, second_ref, dk, dv, cum,
+    gs_ref, w0, w1, q0, q1, kh, vh, g0, g1, remaining_ref, second_ref, dk, dv,
 ):
-    cum[...] = block_cum(ld_ref[:, :BLOCK])
-
     def one(h):
-        row = cum[pl.ds(h, 1), :]
-        columns = as_columns(jnp.exp(row[:, BLOCK - 1 :] - row))
+        columns = remaining_ref[0, h]
         state = second_ref[h]
         dk[0, h] = transposed_dot(gs_ref[0, h], q0[h]) + columns * times_state_t(vh[0, h], state)
         dv[0, h] = transposed_dot(w0[h], g0[h]) + columns * times_state(kh[0, h], state)
         dk[1, h] = transposed_dot(gs_ref[1, h], q1[h])
         dv[1, h] = transposed_dot(w1[h], g1[h])
 
-    each_head(ld_ref.shape[0], 2, one)
-
-
-def grad_key_value(log_decay, gs, w0, w1, q0, q1, kh, vh, g0, g1, second):
-    heads, tok = log_decay.shape
-    dim = HD
+    each_head(gs_ref.shape[1], 2, one)
+
+
+def grad_key_value(*arrays):
+    _, heads, _, dim = arrays[5].shape
+    tok = 2 * BLOCK
     return pl.pallas_call(
         grad_kv_kernel,
         in_specs=[NEAR] * 11,
         out_specs=[NEAR] * 2,
         out_shape=[in_vmem(2, heads, BLOCK, dim)] * 2,
-        scratch_shapes=[pltpu.VMEM((heads, BLOCK), F32)],
         compiler_params=params(4),
         cost_estimate=cost(4 * heads * tok * dim * (BLOCK + dim), 30 * heads * tok * dim),
         name="grad_key_value",
-    )(log_decay, *near(gs, w0, w1, q0, q1, kh, vh, g0, g1, second))
+    )(*near(*arrays))
 
 
 def finish_kernel(
-    place_ref, ld_ref, keep_ref, recv_ref, kh, vh, dk, dv, out_k, out_v, cum, rows_k, rows_v,
-    raw_k, raw_v, sems,
+    place_ref, ends_ref, keep_ref, recv_ref, kh, vh, remaining_ref, dk, dv, out_k, out_v,
+    rows_k, rows_v, raw_k, raw_v, sems,
 ):
-    heads = ld_ref.shape[0]
-    for x in range(2):
-        cum[x] = block_cum(ld_ref[:, x * BLOCK : (x + 1) * BLOCK])
+    heads = ends_ref.shape[1]
     copies = []
     for b in range(2):
 
         def one(h, b=b):
-            row = cum[b, pl.ds(h, 1), :]
-            left = row[:, BLOCK - 1 :] - row
+            columns = remaining_ref[b, h]
+            state = whole_state(place_ref, keep_ref, recv_ref, h)
             if b == 0:
-                left = left + cum[1, pl.ds(h, 1), :][:, BLOCK - 1 :]
-            columns = as_columns(jnp.exp(left))
-            state = whole_state(place_ref, keep_ref, recv_ref, h)
+                state = ends_ref[1, pl.ds(h, 1)] * state
             rows_k[h] = dk[b, h] + columns * times_state_t(vh[b, h], state)
             rows_v[h] = dv[b, h] + columns * times_state(kh[b, h], state)
 
@@ -565,17 +612,16 @@
         copy.wait()
 
 
-def finish(place, log_decay, keep, recv, kh, vh, dk, dv):
-    heads, tok = log_decay.shape
-    dim = HD
+def finish(place, ends, keep, recv, kh, vh, remaining, dk, dv):
+    _, heads, dim = ends.shape
+    tok = 2 * BLOCK
     shape = jax.ShapeDtypeStruct((tok, heads, dim), BF16)
     return pl.pallas_call(
         finish_kernel,
-        in_specs=[NEAR] * 8,
+        in_specs=[NEAR] * 9,
         out_specs=[FAR, FAR],
         out_shape=[shape, shape],
         scratch_shapes=[
-            pltpu.VMEM((2, heads, BLOCK), F32),
             pltpu.VMEM((heads, BLOCK, dim), F32),
             pltpu.VMEM((heads, BLOCK, dim), F32),
             pltpu.VMEM((tok, heads, dim), BF16),
@@ -585,7 +631,7 @@
         compiler_params=params(12),
         cost_estimate=cost(8 * heads * tok * dim * dim, 16 * heads * tok * dim),
         name="finish",
-    )(place, log_decay, *near(keep, recv, kh, vh, dk, dv))
+    )(place, ends, *near(keep, recv, kh, vh, remaining, dk, dv))
 
 
 def swap(value, axis, bit):
@@ -788,19 +834,26 @@
     )(*near(first, second))
 
 
-def sum_over_heads(value):
+def sum_over_heads(value, tasks):
+    tasks = list(tasks)
+    results = []
     count = lax.axis_size("head")
     reach = 1
     while 2 * reach <= count and count % (2 * reach) == 0:
-        value = add(value, swap(value, "head", reach))
+        got = swap(value, "head", reach)
+        if tasks:
+            results.append(tasks.pop(0)(value))
+            got = follows(got, results[-1])
+        value = add(value, got)
         reach *= 2
+    results += [task(value) for task in tasks]
     part = value
     for shift in range(1, count // reach):
         value = add(
             value,
             lax.ppermute(part, "head", [(i, (i + shift * reach) % count) for i in range(count)]),
         )
-    return value
+    return value, results
 
 
 def follows(value, earlier):
@@ -833,25 +886,32 @@
     keep, recv = entering(
         own, send, False, {1: (forward_task(0), in_0), 2: (forward_task(1), in_1)}
     )
-    q0, o0, w0, inner0 = in_0
-    q1, o1, w1, inner1 = in_1
+    q0, o0, w0, decays0, columns0, inner0 = in_0
+    q1, o1, w1, decays1, columns1, inner1 = in_1
     att0, att1, sums = attend(
-        place, log_decay, norm_gain, keep, recv, (q0, q1, o0, o1, inner0, inner1)
-    )
-    sums = sum_over_heads(sums)
+        place, norm_gain, keep, recv, (q0, q1, o0, o1, columns0, columns1, inner0, inner1)
+    )
+    sums, ((scaled, ends), remaining) = sum_over_heads(
+        sums,
+        (
+            lambda earlier: scaled_queries(log_decay, follows(q0, earlier), q1),
+            lambda earlier: remaining_decay(follows(log_decay, earlier)),
+        ),
+    )
     g0, g1, grad_own, grad_send, second = norm_grad(
-        place, log_decay, norm_gain, sums, (q0, q1, o0, o1, att0, att1)
+        place, ends, norm_gain, sums, (scaled, o0, o1, att0, att1)
     )
     queries, pairs, norms = [], [], []
 
     def query_task(earlier):
         return grad_query(
-            place, log_decay, keep, recv, follows(first, earlier), kh, vh, g0, g1
+            place, ends, keep, recv, follows(first, earlier),
+            (kh, vh, g0, g1, decays0, decays1, columns0, columns1),
         )
 
     def pair_task(earlier):
         return grad_key_value(
-            log_decay, queries[1], w0, w1, q0, q1, kh, vh, g0, g1, follows(second, earlier)
+            queries[1], w0, w1, q0, q1, kh, vh, g0, g1, remaining, follows(second, earlier)
         )
 
     def norm_task(earlier):
@@ -860,7 +920,7 @@
     grad_keep, grad_recv = entering(
         grad_own, grad_send, True, {1: (query_task, queries), 2: (pair_task, pairs), 3: (norm_task, norms)}
     )
-    grad_k, grad_v = finish(place, log_decay, grad_keep, grad_recv, kh, vh, *pairs)
+    grad_k, grad_v = finish(place, ends, grad_keep, grad_recv, kh, vh, remaining, *pairs)
     return norms[0], queries[0], grad_k, grad_v
 
 

time: 81.1 us -> 78.3 us (0.965)
  waiting for transfers between devices: 11.6 us -> 8.44 us
    ppermute x15, waiting for transfers between devices: 11.6 us -> 8.44 us  [swap(): return lax.ppermute(value, axis, [(i, i ^ bit) for i in range(count)])]
    pallas_call x4 -> x6, Pallas kernels: 25.4 us -> 26 us  [the longest x1 8.95 us: grad_query(): pl.pallas_call(grad_q_kernel, grid=(2,), in_specs=[NEAR] * 13, out_specs=...]
  transfers between devices with their start and end apart: 15 -> 15, of which waited for: 9 -> 8; matrix products, arithmetic and copies ran while one was open for 0% -> 0% of each run, Pallas kernels for 38% -> 41%
where the time goes in v6:
time: 78.3 us; the launch traced here: 78.1 us
  Pallas kernels  51.9 us (66%)
  starting transfers between devices  16.8 us (21%)
  waiting for transfers between devices  8.44 us (11%)
  between operations  0.81 us (1%)
    ppermute x15, starting transfers between devices, swap(): return lax.ppermute(value, axis, [(i, i ^ bit) for i in range(count)])  16.8 us
    pallas_call x2, Pallas kernels, intra(): pl.pallas_call(kernel, in_specs=[NEAR] * 4 + [FAR, FAR], out_specs=[NEAR]...  12 us
    pallas_call x1, Pallas kernels, grad_query(): pl.pallas_call(grad_q_kernel, grid=(2,), in_specs=[NEAR] * 13, out_specs=...  8.95 us
    ppermute x15, waiting for transfers between devices, swap(): return lax.ppermute(value, axis, [(i, i ^ bit) for i in range(count)])  8.44 us
    pallas_call x1, Pallas kernels, finish(): pl.pallas_call(finish_kernel, in_specs=[NEAR] * 9, out_specs=[FAR, FAR],...  7.49 us
    pallas_call x1, Pallas kernels, local_state(): pl.pallas_call(state_kernel, in_specs=[NEAR, FAR, FAR, FAR], out_specs=[N...  5.76 us
    pallas_call x1, Pallas kernels, grad_key_value(): pl.pallas_call(grad_kv_kernel, in_specs=[NEAR] * 11, out_specs=[NEAR] * 2...  4.83 us
    pallas_call x1, Pallas kernels, attend(): pl.pallas_call(attend_kernel, in_specs=[NEAR] * 12, out_specs=[NEAR] * 3,...  3.34 us
  transfers between devices with their start and end apart: 15, of which 8 were waited for; matrix products, arithmetic and copies ran while one was open for 0% of the time, Pallas kernels for 41%

profile of v6, /device:TPU:0, one launch (start us, length us, event | category | flops | bytes accessed | tf_op | source)
XLA Modules:
  0.0 78.1 jit_solution(3787295259433143851)
XLA Ops:
  0.8 5.8 %local_state.1 = (f32[8,136,128]{2,1,0:T(8,128)S(1)}, f32[8,136,128]{2,1,0:T(8,128)S(1)}, f32[16,128,128]{2,1,0:T(8,128)S(1)}, bf16[2,16,256,128]{3,2,1,0:T(8,128)(2,1)S(1)}, bf16[2,16,256,128]{3,2,1,0:T(8,128)(2,1)S(1)}) custom-call(f32[8,128]{1,0:T(8,128)S(1)} %broadcast_in_dim.2.place_ref, f32[16,512]{1,0:T(8,128)} %ld_ref.6, ...), custom_call_target="tpu_custom_call" | custom-call | flops 268435456 | bytes 8388608 | tf_op jit(solution)/shard_map/local_state/pallas_call | solution.py:232
  6.6 0.5 collective-permute-start
  7.1 1.6 %collective-permute-done.refs_1_.refs_2_ = f32[8,136,128]{2,1,0:T(8,128)S(1)} collective-permute-done((f32[8,136,128]{2,1,0:T(8,128)S(1)}, f32[8,136,128]{2,1,0:T(8,128)S(1)}, u32[]{:S(2)}, u32[]{:S(2)}) %collective-permute-start) | collective-permute-done | bytes 557088 | tf_op jit(solution)/shard_map/ppermute | solution.py:639
  8.7 0.1 earlier_total.1
  8.8 2.9 %collective-permute-start.1 = (f32[4,136,128]{2,1,0:T(8,128)S(1)}, f32[4,136,128]{2,1,0:T(8,128)S(1)}, u32[]{:S(2)}, u32[]{:S(2)}) collective-permute-start(f32[4,136,128]{2,1,0:T(8,128)S(1)} %get-tuple-element.72.refs_4_), channel_id=1, source_target_pairs={{0,8},{4,12},{8,0},{12,4},{16,24},{20,28},{24,16},{28,20},{1,9},{5... | collective-permute-start | bytes 835592 | tf_op jit(solution)/shard_map/ppermute | solution.py:639
  11.7 1.5 %collective-permute-start.2 = (f32[4,128,128]{2,1,0:T(8,128)S(1)}, f32[4,128,128]{2,1,0:T(8,128)S(1)}, u32[]{:S(2)}, u32[]{:S(2)}) collective-permute-start(f32[4,128,128]{2,1,0:T(8,128)S(1)} %get-tuple-element.73.refs_5_), channel_id=1, source_target_pairs={{0,16},{4,20},{8,24},{12,28},{16,0},{20,4},{24,8},{28,12},{1,17},{... | collective-permute-start | bytes 786440 | tf_op jit(solution)/shard_map/ppermute | solution.py:639
  13.3 6.4 %intra_0.1 = (bf16[16,256,128]{2,1,0:T(8,128)(2,1)S(1)}, bf16[16,256,128]{2,1,0:T(8,128)(2,1)S(1)}, bf16[16,256,256]{2,1,0:T(8,128)(2,1)S(1)}, f32[16,3,128,128]...) custom-call(f32[16,512]{1,0:T(8,128)S(1)} %copy-done, ...), custom_call_target="tpu_custom_call" | custom-call | flops 1073741824 | bytes 10485760 | tf_op jit(solution)/shard_map/intra_0/pallas_call | solution.py:291
  19.7 0.3 collective-permute-done.3.refs_3_
  20.1 1.7 %collective-permute-start.4 = (f32[4,128,128]{2,1,0:T(8,128)S(1)}, f32[4,128,128]{2,1,0:T(8,128)S(1)}, u32[]{:S(2)}, u32[]{:S(2)}) collective-permute-start(f32[4,128,128]{2,1,0:T(8,128)S(1)} %get-tuple-element.84), channel_id=1, source_target_pairs={{0,16},{4,20},{8,24},{12,28},{16,0},{20,4},{24,8},{28,12},{1,17},{... | collective-permute-start | bytes 786440 | tf_op jit(solution)/shard_map/ppermute | solution.py:639
  21.8 1.5 %collective-permute-start.5 = (f32[4,128,128]{2,1,0:T(8,128)S(1)}, f32[4,128,128]{2,1,0:T(8,128)S(1)}, u32[]{:S(2)}, u32[]{:S(2)}) collective-permute-start(f32[4,128,128]{2,1,0:T(8,128)S(1)} %get-tuple-element.85), channel_id=1, source_target_pairs={{0,8},{4,12},{8,0},{12,4},{16,24},{20,28},{24,16},{28,20},{1,9},{5... | collective-permute-start | bytes 786440 | tf_op jit(solution)/shard_map/ppermute | solution.py:639
  23.3 5.6 %intra_1.1 = (bf16[16,256,128]{2,1,0:T(8,128)(2,1)S(1)}, bf16[16,256,128]{2,1,0:T(8,128)(2,1)S(1)}, bf16[16,256,256]{2,1,0:T(8,128)(2,1)S(1)}, f32[16,3,128,128]...) custom-call(f32[16,512]{1,0:T(8,128)S(1)} %copy-done, ...), custom_call_target="tpu_custom_call" | custom-call | flops 1073741824 | bytes 10485760 | tf_op jit(solution)/shard_map/intra_1/pallas_call | solution.py:291
  29.0 0.2 earlier_enter.1
  29.3 1.9 %collective-permute-done.6.recv_ref = f32[8,128,128]{2,1,0:T(8,128)S(1)} collective-permute-done((f32[8,128,128]{2,1,0:T(8,128)S(1)}, f32[8,128,128]{2,1,0:T(8,128)S(1)}, u32[]{:S(2)}, u32[]{:S(2)}) %collective-permute-start.6) | collective-permute-done | bytes 524320 | tf_op jit(solution)/shard_map/ppermute | solution.py:639
  31.2 3.3 %attend.1 = (f32[16,256,128]{2,1,0:T(8,128)S(1)}, f32[16,256,128]{2,1,0:T(8,128)S(1)}, f32[2,512]{1,0:T(2,128)S(1)}) custom-call(f32[8,128]{1,0:T(8,128)S(1)} %broadcast_in_dim.2.place_ref, f32[16,128]{1,0:T(8,128)S(1)} %copy-done.1, f32[8,128,128]{2,1,0:T(8,128)S(1)} %get-tuple-element.90.keep_ref, f32[8,128,128]{2,1,0:T(8,128)S(1)} %collective-permute-done.6.recv_ref, ...), custom_call_target="tpu_custom_call" | custom-call | flops 536870912 | bytes 16777216 | tf_op jit(solution)/shard_map/attend/pallas_call | solution.py:354
  34.6 1.6 %collective-permute-start.7 = (f32[2,512]{1,0:T(2,128)S(1)}, f32[2,512]{1,0:T(2,128)S(1)}, u32[]{:S(2)}, u32[]{:S(2)}) collective-permute-start(f32[2,512]{1,0:T(2,128)S(1)} %get-tuple-element.97.first_ref), channel_id=1, source_target_pairs={{0,1},{1,0},{2,3},{3,2},{4,5},{5,4},{6,7},{7,6},{8,9},{9,8},{10,11... | collective-permute-start | bytes 12296 | tf_op jit(solution)/shard_map/ppermute | solution.py:639
  36.1 1.5 %scaled_queries.1 = (bf16[2,16,128,256]{3,2,1,0:T(8,128)(2,1)S(1)}, f32[2,16,128]{2,1,0:T(8,128)S(1)}) custom-call(f32[16,512]{1,0:T(8,128)S(1)} %copy-done, bf16[16,256,128]{2,1,0:T(8,128)(2,1)S(1)} %get-tuple-element.98.q0, bf16[16,256,128]{2,1,0:T(8,128)(2,1)S(1)} %get-tuple-element.92.q1), custom_call_target="tpu_custom_call" | custom-call | flops 2097152 | bytes 4194304 | tf_op jit(solution)/shard_map/scaled_queries/pallas_call | solution.py:381
  37.7 0.5 collective-permute-done.7.second_ref
  38.2 2.6 %collective-permute-start.8 = (f32[2,512]{1,0:T(2,128)S(1)}, f32[2,512]{1,0:T(2,128)S(1)}, u32[]{:S(2)}, u32[]{:S(2)}) collective-permute-start(f32[2,512]{1,0:T(2,128)S(1)} %add.15.first_ref), channel_id=1, source_target_pairs={{0,2},{1,3},{2,0},{3,1},{4,6},{5,7},{6,4},{7,5},{8,10},{9,11},{10,... | collective-permute-start | bytes 12296 | tf_op jit(solution)/shard_map/ppermute | solution.py:639
  40.8 2.0 %remaining_decay.1.remaining_ref = f32[2,16,256,128]{3,2,1,0:T(8,128)S(1)} custom-call(f32[16,512]{1,0:T(8,128)S(1)} %copy-done), custom_call_target="tpu_custom_call" | custom-call | flops 1048576 | bytes 4194304 | tf_op jit(solution)/shard_map/remaining_decay/pallas_call | solution.py:408
  42.8 2.7 %norm_grad.1 = (bf16[16,256,128]{2,1,0:T(8,128)(2,1)S(1)}, bf16[16,256,128]{2,1,0:T(8,128)(2,1)S(1)}, f32[8,128,128]{2,1,0:T(8,128)S(1)}, f32[8,128,128]{2,1,0:T(8,128)S(1)}, f32[16,128,128]{2,1,0:T(8,128)S(1)}) custom-call(f32[8,128]{1,0:T(8,128)S(1)} %broadcast_in_dim.2.place_ref, f32[2,16,128]{2,1,0:T(8,128)S(1)} %get-tuple-element.99.ends_ref, ...), custom_call_target="tpu_custom_call" | custom-call | flops 268435456 | bytes 14680064 | tf_op jit(solution)/shard_map/norm_grad/pallas_call | solution.py:456
  45.6 1.9 %collective-permute-done.9.refs_2_ = f32[8,128,128]{2,1,0:T(8,128)S(1)} collective-permute-done((f32[8,128,128]{2,1,0:T(8,128)S(1)}, f32[8,128,128]{2,1,0:T(8,128)S(1)}, u32[]{:S(2)}, u32[]{:S(2)}) %collective-permute-start.9) | collective-permute-done | bytes 524320 | tf_op jit(solution)/shard_map/ppermute | solution.py:639
  47.6 1.6 %collective-permute-start.10 = (f32[4,128,128]{2,1,0:T(8,128)S(1)}, f32[4,128,128]{2,1,0:T(8,128)S(1)}, u32[]{:S(2)}, u32[]{:S(2)}) collective-permute-start(f32[4,128,128]{2,1,0:T(8,128)S(1)} %get-tuple-element.108.refs_1_), channel_id=1, source_target_pairs={{0,8},{4,12},{8,0},{12,4},{16,24},{20,28},{24,16},{28,20},{1,9},{5... | collective-permute-start | bytes 786440 | tf_op jit(solution)/shard_map/ppermute | solution.py:639
  49.1 0.5 collective-permute-start.11
  49.7 8.9 %grad_query.1 = (bf16[512,16,128]{2,1,0:T(8,128)(2,1)}, bf16[2,16,256,256]{3,2,1,0:T(8,128)(2,1)S(1)}) custom-call(f32[8,128]{1,0:T(8,128)S(1)} %broadcast_in_dim.2.place_ref, f32[2,16,128]{2,1,0:T(8,128)S(1)} %get-tuple-element.99.ends_ref, f32[8,128,128]{2,1,0:T(8,128)S(1)} %get-tuple-element.90.keep_ref, ...), custom_call_target="tpu_custom_call" | custom-call | flops 1610612736 | bytes 12582912 | tf_op jit(solution)/shard_map/grad_query/pallas_call | solution.py:545
  58.7 1.6 %collective-permute-start.12 = (f32[4,128,128]{2,1,0:T(8,128)S(1)}, f32[4,128,128]{2,1,0:T(8,128)S(1)}, u32[]{:S(2)}, u32[]{:S(2)}) collective-permute-start(f32[4,128,128]{2,1,0:T(8,128)S(1)} %get-tuple-element.118), channel_id=1, source_target_pairs={{0,16},{4,20},{8,24},{12,28},{16,0},{20,4},{24,8},{28,12},{1,17},{... | collective-permute-start | bytes 786440 | tf_op jit(solution)/shard_map/ppermute | solution.py:639
  60.3 0.5 collective-permute-start.13
  60.8 4.8 %grad_key_value.1 = (f32[2,16,256,128]{3,2,1,0:T(8,128)S(1)}, f32[2,16,256,128]{3,2,1,0:T(8,128)S(1)}) custom-call(bf16[2,16,256,256]{3,2,1,0:T(8,128)(2,1)S(1)} %get-tuple-element.115.gs_ref, bf16[16,256,256]{2,1,0:T(8,128)(2,1)S(1)} %get-tuple-element.120.w0, bf16[16,256,256]{2,1,0:T(8,128)(2,1)S(1)} %get-tuple-element.121.w1, ...), custom_call_target="tpu_custom_call" | custom-call | flops 1610612736 | bytes 31457280 | tf_op jit(solution)/shard_map/grad_key_value/pallas_call | solution.py:577
  65.6 0.9 %collective-permute-done.12.refs_5_ = f32[4,128,128]{2,1,0:T(8,128)S(1)} collective-permute-done((f32[4,128,128]{2,1,0:T(8,128)S(1)}, f32[4,128,128]{2,1,0:T(8,128)S(1)}, u32[]{:S(2)}, u32[]{:S(2)}) %collective-permute-start.12) | collective-permute-done | bytes 262176 | tf_op jit(solution)/shard_map/ppermute | solution.py:639
  66.5 1.2 %collective-permute-done.13.refs_6_ = f32[4,128,128]{2,1,0:T(8,128)S(1)} collective-permute-done((f32[4,128,128]{2,1,0:T(8,128)S(1)}, f32[4,128,128]{2,1,0:T(8,128)S(1)}, u32[]{:S(2)}, u32[]{:S(2)}) %collective-permute-start.13) | collective-permute-done | bytes 262176 | tf_op jit(solution)/shard_map/ppermute | solution.py:639
  67.8 0.2 later_enter.1
  68.0 2.6 %normed_rows.1 = bf16[512,16,128]{2,1,0:T(8,128)(2,1)} custom-call(f32[16,128]{1,0:T(8,128)S(1)} %copy-done.1, f32[2,512]{1,0:T(2,128)S(1)} %add.16.sums_ref, f32[16,256,128]{2,1,0:T(8,128)S(1)} %get-tuple-element.104.att0, f32[16,256,128]{2,1,0:T(8,128)S(1)} %get-tuple-element.105.att1), custom_call_target="tpu_custom_call" | custom-call | flops 3145728 | bytes 6291456 | tf_op jit(solution)/shard_map/normed_rows/pallas_call | solution.py:504
  70.6 7.5 %finish.1 = (bf16[512,16,128]{2,1,0:T(8,128)(2,1)}, bf16[512,16,128]{2,1,0:T(8,128)(2,1)}) custom-call(f32[8,128]{1,0:T(8,128)S(1)} %broadcast_in_dim.2.place_ref, f32[2,16,128]{2,1,0:T(8,128)S(1)} %get-tuple-element.99.ends_ref, f32[8,128,128]{2,1,0:T(8,128)S(1)} %get-tuple-element.130.keep_ref, f32[8,128,128]{2,1,0:T(8,128)S(1)} %collective-permute-done.14.recv_ref, ...), custom_call_target="tpu_custom_call" | custom-call | flops 1073741824 | bytes 16777216 | tf_op jit(solution)/shard_map/finish/pallas_call | solution.py:619
  (25 shorter events, 0.8 us)
Async XLA Ops:
  0.8 12.4 %copy-start = (f32[16,512]{1,0:T(8,128)S(1)}, f32[16,512]{1,0:T(8,128)}, u32[]{:S(2)}) copy-start(f32[16,512]{1,0:T(8,128)} %ld_ref.6) | copy-start | bytes 98308
  6.6 2.1 %collective-permute-start = (f32[8,136,128]{2,1,0:T(8,128)S(1)}, f32[8,136,128]{2,1,0:T(8,128)S(1)}, u32[]{:S(2)}, u32[]{:S(2)}) collective-permute-start(f32[8,136,128]{2,1,0:T(8,128)S(1)} %get-tuple-element.70), channel_id=1, source_target_pairs={{0,4},{4,0},{8,12},{12,8},{16,20},{20,16},{24,28},{28,24},{1,5},{5... | collective-permute-start | bytes 1671176 | tf_op jit(solution)/shard_map/ppermute | solution.py:639
  8.8 11.2 %collective-permute-start.1 = (f32[4,136,128]{2,1,0:T(8,128)S(1)}, f32[4,136,128]{2,1,0:T(8,128)S(1)}, u32[]{:S(2)}, u32[]{:S(2)}) collective-permute-start(f32[4,136,128]{2,1,0:T(8,128)S(1)} %get-tuple-element.72.refs_4_), channel_id=1, source_target_pairs={{0,8},{4,12},{8,0},{12,4},{16,24},{20,28},{24,16},{28,20},{1,9},{5... | collective-permute-start | bytes 835592 | tf_op jit(solution)/shard_map/ppermute | solution.py:639
  11.7 8.3 %collective-permute-start.2 = (f32[4,128,128]{2,1,0:T(8,128)S(1)}, f32[4,128,128]{2,1,0:T(8,128)S(1)}, u32[]{:S(2)}, u32[]{:S(2)}) collective-permute-start(f32[4,128,128]{2,1,0:T(8,128)S(1)} %get-tuple-element.73.refs_5_), channel_id=1, source_target_pairs={{0,16},{4,20},{8,24},{12,28},{16,0},{20,4},{24,8},{28,12},{1,17},{... | collective-permute-start | bytes 786440 | tf_op jit(solution)/shard_map/ppermute | solution.py:639
  13.2 6.7 %collective-permute-start.3 = (f32[8,128]{1,0:T(8,128)S(1)}, f32[8,128]{1,0:T(8,128)S(1)}, u32[]{:S(2)}, u32[]{:S(2)}) collective-permute-start(f32[8,128]{1,0:T(8,128)S(1)} %get-tuple-element.71.refs_2_), channel_id=1, source_target_pairs={{0,24},{4,28},{8,16},{12,20},{16,8},{20,12},{24,0},{28,4},{1,25},{... | collective-permute-start | bytes 12296 | tf_op jit(solution)/shard_map/ppermute | solution.py:639
  20.1 8.9 %collective-permute-start.4 = (f32[4,128,128]{2,1,0:T(8,128)S(1)}, f32[4,128,128]{2,1,0:T(8,128)S(1)}, u32[]{:S(2)}, u32[]{:S(2)}) collective-permute-start(f32[4,128,128]{2,1,0:T(8,128)S(1)} %get-tuple-element.84), channel_id=1, source_target_pairs={{0,16},{4,20},{8,24},{12,28},{16,0},{20,4},{24,8},{28,12},{1,17},{... | collective-permute-start | bytes 786440 | tf_op jit(solution)/shard_map/ppermute | solution.py:639
  21.8 7.2 %collective-permute-start.5 = (f32[4,128,128]{2,1,0:T(8,128)S(1)}, f32[4,128,128]{2,1,0:T(8,128)S(1)}, u32[]{:S(2)}, u32[]{:S(2)}) collective-permute-start(f32[4,128,128]{2,1,0:T(8,128)S(1)} %get-tuple-element.85), channel_id=1, source_target_pairs={{0,8},{4,12},{8,0},{12,4},{16,24},{20,28},{24,16},{28,20},{1,9},{5... | collective-permute-start | bytes 786440 | tf_op jit(solution)/shard_map/ppermute | solution.py:639
  28.9 2.3 %copy-start.1 = (f32[16,128]{1,0:T(8,128)S(1)}, f32[16,128]{1,0:T(8,128)}, u32[]{:S(2)}) copy-start(f32[16,128]{1,0:T(8,128)} %gain_ref.4) | copy-start | bytes 24580
  29.2 2.0 %collective-permute-start.6 = (f32[8,128,128]{2,1,0:T(8,128)S(1)}, f32[8,128,128]{2,1,0:T(8,128)S(1)}, u32[]{:S(2)}, u32[]{:S(2)}) collective-permute-start(f32[8,128,128]{2,1,0:T(8,128)S(1)} %get-tuple-element.91), channel_id=1, source_target_pairs={{0,4},{4,0},{8,12},{12,8},{16,20},{20,16},{24,28},{28,24},{1,5},{5... | collective-permute-start | bytes 1572872 | tf_op jit(solution)/shard_map/ppermute | solution.py:639
  34.6 3.6 %collective-permute-start.7 = (f32[2,512]{1,0:T(2,128)S(1)}, f32[2,512]{1,0:T(2,128)S(1)}, u32[]{:S(2)}, u32[]{:S(2)}) collective-permute-start(f32[2,512]{1,0:T(2,128)S(1)} %get-tuple-element.97.first_ref), channel_id=1, source_target_pairs={{0,1},{1,0},{2,3},{3,2},{4,5},{5,4},{6,7},{7,6},{8,9},{9,8},{10,11... | collective-permute-start | bytes 12296 | tf_op jit(solution)/shard_map/ppermute | solution.py:639
  38.2 4.6 %collective-permute-start.8 = (f32[2,512]{1,0:T(2,128)S(1)}, f32[2,512]{1,0:T(2,128)S(1)}, u32[]{:S(2)}, u32[]{:S(2)}) collective-permute-start(f32[2,512]{1,0:T(2,128)S(1)} %add.15.first_ref), channel_id=1, source_target_pairs={{0,2},{1,3},{2,0},{3,1},{4,6},{5,7},{6,4},{7,5},{8,10},{9,11},{10,... | collective-permute-start | bytes 12296 | tf_op jit(solution)/shard_map/ppermute | solution.py:639
  45.5 2.0 %collective-permute-start.9 = (f32[8,128,128]{2,1,0:T(8,128)S(1)}, f32[8,128,128]{2,1,0:T(8,128)S(1)}, u32[]{:S(2)}, u32[]{:S(2)}) collective-permute-start(f32[8,128,128]{2,1,0:T(8,128)S(1)} %get-tuple-element.107), channel_id=1, source_target_pairs={{0,4},{4,0},{8,12},{12,8},{16,20},{20,16},{24,28},{28,24},{1,5},{5... | collective-permute-start | bytes 1572872 | tf_op jit(solution)/shard_map/ppermute | solution.py:639
  47.6 11.0 %collective-permute-start.10 = (f32[4,128,128]{2,1,0:T(8,128)S(1)}, f32[4,128,128]{2,1,0:T(8,128)S(1)}, u32[]{:S(2)}, u32[]{:S(2)}) collective-permute-start(f32[4,128,128]{2,1,0:T(8,128)S(1)} %get-tuple-element.108.refs_1_), channel_id=1, source_target_pairs={{0,8},{4,12},{8,0},{12,4},{16,24},{20,28},{24,16},{28,20},{1,9},{5... | collective-permute-start | bytes 786440 | tf_op jit(solution)/shard_map/ppermute | solution.py:639
  49.1 9.5 %collective-permute-start.11 = (f32[4,128,128]{2,1,0:T(8,128)S(1)}, f32[4,128,128]{2,1,0:T(8,128)S(1)}, u32[]{:S(2)}, u32[]{:S(2)}) collective-permute-start(f32[4,128,128]{2,1,0:T(8,128)S(1)} %get-tuple-element.109.refs_2_), channel_id=1, source_target_pairs={{0,16},{4,20},{8,24},{12,28},{16,0},{20,4},{24,8},{28,12},{1,17},{... | collective-permute-start | bytes 786440 | tf_op jit(solution)/shard_map/ppermute | solution.py:639
  58.7 7.9 %collective-permute-start.12 = (f32[4,128,128]{2,1,0:T(8,128)S(1)}, f32[4,128,128]{2,1,0:T(8,128)S(1)}, u32[]{:S(2)}, u32[]{:S(2)}) collective-permute-start(f32[4,128,128]{2,1,0:T(8,128)S(1)} %get-tuple-element.118), channel_id=1, source_target_pairs={{0,16},{4,20},{8,24},{12,28},{16,0},{20,4},{24,8},{28,12},{1,17},{... | collective-permute-start | bytes 786440 | tf_op jit(solution)/shard_map/ppermute | solution.py:639
  60.3 7.5 %collective-permute-start.13 = (f32[4,128,128]{2,1,0:T(8,128)S(1)}, f32[4,128,128]{2,1,0:T(8,128)S(1)}, u32[]{:S(2)}, u32[]{:S(2)}) collective-permute-start(f32[4,128,128]{2,1,0:T(8,128)S(1)} %get-tuple-element.119), channel_id=1, source_target_pairs={{0,8},{4,12},{8,0},{12,4},{16,24},{20,28},{24,16},{28,20},{1,9},{5... | collective-permute-start | bytes 786440 | tf_op jit(solution)/shard_map/ppermute | solution.py:639
  68.0 2.7 %collective-permute-start.14 = (f32[8,128,128]{2,1,0:T(8,128)S(1)}, f32[8,128,128]{2,1,0:T(8,128)S(1)}, u32[]{:S(2)}, u32[]{:S(2)}) collective-permute-start(f32[8,128,128]{2,1,0:T(8,128)S(1)} %get-tuple-element.127), channel_id=1, source_target_pairs={{0,4},{4,0},{8,12},{12,8},{16,20},{20,16},{24,28},{28,24},{1,5},{5... | collective-permute-start | bytes 1572872 | tf_op jit(solution)/shard_map/ppermute | solution.py:639

commit v7 on v6

--- a/solution.py
+++ b/solution.py
@@ -336,7 +336,7 @@
             products[b] += gain * o[h].astype(F32) * attended
             state = columns[h, BLOCK - 1 :] * state
 
-    each_head(heads, 2, one)
+    each_head(heads, 4, one)
     ones = jnp.ones((8, HD), F32)
     for b in range(2):
         for at, total in enumerate((squares, products)):
@@ -516,40 +516,34 @@
 
 def grad_q_kernel(
     place_ref, ends_ref, keep_ref, recv_ref, first_ref, kh, vh, g0, g1, decays0, decays1,
-    columns0, columns1, out_ref, gs_ref, rows,
+    columns0, columns1, rows, gs_ref,
 ):
     heads = ends_ref.shape[1]
-
-    def work(b):
-        g, decays, columns = ((g0, decays0, columns0), (g1, decays1, columns1))[b]
-
-        def one(h):
+    for b, (g, decays, columns) in enumerate(((g0, decays0, columns0), (g1, decays1, columns1))):
+
+        def one(h, b=b, g=g, decays=decays, columns=columns):
             quarters = [decays[h, at] for at in range(3)]
             scores = causal(dot_rows(g[h], vh[b, h]), quarters)
             gs_ref[b, h] = scores
             state = whole_state(place_ref, keep_ref, recv_ref, h)
             if b:
                 state = ends_ref[0, pl.ds(h, 1)] * state + first_ref[h]
-            rows[h] = dot(scores, kh[b, h]) + columns[h] * times_state_t(g[h], state)
-
-        each_head(heads, 2, one)
-
-    on_block(work)
-    from_heads(out_ref, rows, 0, BLOCK)
+            rows[b, h] = dot(scores, kh[b, h]) + columns[h] * times_state_t(g[h], state)
+
+        each_head(heads, 4, one)
 
 
 def grad_query(place, ends, keep, recv, first, parts):
     _, heads, dim = ends.shape
     tok = 2 * BLOCK
-    spec, shape = raw_output(heads, tok)
     return pl.pallas_call(
         grad_q_kernel,
-        grid=(2,),
         in_specs=[NEAR] * 13,
-        out_specs=[spec, NEAR],
-        out_shape=[shape, in_vmem(2, heads, BLOCK, BLOCK, kind=BF16)],
-        scratch_shapes=[pltpu.VMEM((heads, BLOCK, dim), F32)],
-        compiler_params=params(8),
+        out_specs=[NEAR, NEAR],
+        out_shape=[
+            in_vmem(2, heads, BLOCK, dim), in_vmem(2, heads, BLOCK, BLOCK, kind=BF16),
+        ],
+        compiler_params=params(4),
         cost_estimate=cost(
             4 * heads * tok * dim * (BLOCK + dim), 12 * heads * tok * dim, heads * tok * BLOCK
         ),
@@ -558,8 +552,18 @@
 
 
 def grad_kv_kernel(
-    gs_ref, w0, w1, q0, q1, kh, vh, g0, g1, remaining_ref, second_ref, dk, dv,
+    gs_ref, w0, w1, q0, q1, kh, vh, g0, g1, remaining_ref, second_ref, rows, dk, dv, out_q,
+    raw, sems,
 ):
+    heads = gs_ref.shape[1]
+    copies = []
+    for b in range(2):
+        for start in range(0, BLOCK, CHUNK):
+            at = pl.ds(b * BLOCK + start, CHUNK)
+            from_heads(raw.at[at], rows.at[b], start, CHUNK)
+            copies.append(pltpu.make_async_copy(raw.at[at], out_q.at[at], sems.at[len(copies)]))
+            copies[-1].start()
+
     def one(h):
         columns = remaining_ref[0, h]
         state = second_ref[h]
@@ -568,7 +572,9 @@
         dk[1, h] = transposed_dot(gs_ref[1, h], q1[h])
         dv[1, h] = transposed_dot(w1[h], g1[h])
 
-    each_head(gs_ref.shape[1], 2, one)
+    each_head(heads, 2, one)
+    for copy in copies:
+        copy.wait()
 
 
 def grad_key_value(*arrays):
@@ -576,10 +582,15 @@
     tok = 2 * BLOCK
     return pl.pallas_call(
         grad_kv_kernel,
-        in_specs=[NEAR] * 11,
-        out_specs=[NEAR] * 2,
-        out_shape=[in_vmem(2, heads, BLOCK, dim)] * 2,
-        compiler_params=params(4),
+        in_specs=[NEAR] * 12,
+        out_specs=[NEAR, NEAR, FAR],
+        out_shape=[in_vmem(2, heads, BLOCK, dim)] * 2
+        + [jax.ShapeDtypeStruct((tok, heads, dim), BF16)],
+        scratch_shapes=[
+            pltpu.VMEM((tok, heads, dim), BF16),
+            pltpu.SemaphoreType.DMA((tok // CHUNK,)),
+        ],
+        compiler_params=params(6),
         cost_estimate=cost(4 * heads * tok * dim * (BLOCK + dim), 30 * heads * tok * dim),
         name="grad_key_value",
     )(*near(*arrays))
@@ -598,10 +609,17 @@
             state = whole_state(place_ref, keep_ref, recv_ref, h)
             if b == 0:
                 state = ends_ref[1, pl.ds(h, 1)] * state
-            rows_k[h] = dk[b, h] + columns * times_state_t(vh[b, h], state)
-            rows_v[h] = dv[b, h] + columns * times_state(kh[b, h], state)
-
-        each_head(heads, 2, one)
+            state = state.astype(BF16)
+            none = jnp.zeros_like(state)
+            both = jnp.concatenate(
+                [jnp.concatenate([state.T, none], axis=1), jnp.concatenate([none, state], axis=1)],
+                axis=0,
+            )
+            carried = dot(jnp.concatenate([vh[b, h], kh[b, h]], axis=1), both)
+            rows_k[h] = dk[b, h] + columns * carried[:, :HD]
+            rows_v[h] = dv[b, h] + columns * carried[:, HD:]
+
+        each_head(heads, 4, one)
         for start in range(0, BLOCK, CHUNK):
             at = pl.ds(b * BLOCK + start, CHUNK)
             for rows, raw, out in ((rows_k, raw_k, out_k), (rows_v, raw_v, out_v)):
@@ -911,7 +929,8 @@
 
     def pair_task(earlier):
         return grad_key_value(
-            queries[1], w0, w1, q0, q1, kh, vh, g0, g1, remaining, follows(second, earlier)
+            queries[1], w0, w1, q0, q1, kh, vh, g0, g1, remaining, follows(second, earlier),
+            queries[0],
         )
 
     def norm_task(earlier):
@@ -920,8 +939,9 @@
     grad_keep, grad_recv = entering(
         grad_own, grad_send, True, {1: (query_task, queries), 2: (pair_task, pairs), 3: (norm_task, norms)}
     )
-    grad_k, grad_v = finish(place, ends, grad_keep, grad_recv, kh, vh, remaining, *pairs)
-    return norms[0], queries[0], grad_k, grad_v
+    dk, dv, grad_q = pairs
+    grad_k, grad_v = finish(place, ends, grad_keep, grad_recv, kh, vh, remaining, dk, dv)
+    return norms[0], grad_q, grad_k, grad_v
 
 
 def solution(mesh):

time: 78.3 us -> 73 us (0.932)
  Pallas kernels: 51.9 us -> 47.2 us
  starting transfers between devices: 16.8 us -> 15.8 us
    pallas_call x2, Pallas kernels: 13.8 us -> 11.4 us  [the longest x1 5.83 us: grad_key_value(): pl.pallas_call(grad_kv_kernel, in_specs=[NEAR] * 12, out_specs=[NEAR, NEA...]
    pallas_call x1, Pallas kernels: 7.49 us -> 5.9 us  [finish(): pl.pallas_call(finish_kernel, in_specs=[NEAR] * 9, out_specs=[FAR, FAR],...]
    ppermute x15, starting transfers between devices: 16.8 us -> 15.8 us  [swap(): return lax.ppermute(value, axis, [(i, i ^ bit) for i in range(count)])]
  transfers between devices with their start and end apart: 15 -> 15, of which waited for: 8 -> 10; matrix products, arithmetic and copies ran while one was open for 0% -> 0% of each run, Pallas kernels for 41% -> 41%
where the time goes in v7:
time: 73 us; the launch traced here: 72.8 us
  Pallas kernels  47.2 us (65%)
  starting transfers between devices  15.8 us (22%)
  waiting for transfers between devices  8.84 us (12%)
  between operations  0.82 us (1%)
    ppermute x15, starting transfers between devices, swap(): return lax.ppermute(value, axis, [(i, i ^ bit) for i in range(count)])  15.8 us
    pallas_call x2, Pallas kernels, intra(): pl.pallas_call(kernel, in_specs=[NEAR] * 4 + [FAR, FAR], out_specs=[NEAR]...  12 us
    ppermute x15, waiting for transfers between devices, swap(): return lax.ppermute(value, axis, [(i, i ^ bit) for i in range(count)])  8.84 us
    pallas_call x1, Pallas kernels, finish(): pl.pallas_call(finish_kernel, in_specs=[NEAR] * 9, out_specs=[FAR, FAR],...  5.9 us
    pallas_call x1, Pallas kernels, grad_key_value(): pl.pallas_call(grad_kv_kernel, in_specs=[NEAR] * 12, out_specs=[NEAR, NEA...  5.83 us
    pallas_call x1, Pallas kernels, local_state(): pl.pallas_call(state_kernel, in_specs=[NEAR, FAR, FAR, FAR], out_specs=[N...  5.76 us
    pallas_call x1, Pallas kernels, grad_query(): pl.pallas_call(grad_q_kernel, in_specs=[NEAR] * 13, out_specs=[NEAR, NEAR...  5.59 us
    pallas_call x1, Pallas kernels, norm_grad(): pl.pallas_call(norm_grad_kernel, in_specs=[NEAR] * 9, out_specs=[NEAR] *...  2.7 us
  transfers between devices with their start and end apart: 15, of which 10 were waited for; matrix products, arithmetic and copies ran while one was open for 0% of the time, Pallas kernels for 41%

profile of v7, /device:TPU:0, one launch (start us, length us, event | category | flops | bytes accessed | tf_op | source)
XLA Modules:
  0.0 72.8 jit_solution(10678203437912412510)
XLA Ops:
  0.8 5.8 %local_state.1 = (f32[8,136,128]{2,1,0:T(8,128)S(1)}, f32[8,136,128]{2,1,0:T(8,128)S(1)}, f32[16,128,128]{2,1,0:T(8,128)S(1)}, bf16[2,16,256,128]{3,2,1,0:T(8,128)(2,1)S(1)}, bf16[2,16,256,128]{3,2,1,0:T(8,128)(2,1)S(1)}) custom-call(f32[8,128]{1,0:T(8,128)S(1)} %broadcast_in_dim.2.place_ref, f32[16,512]{1,0:T(8,128)} %ld_ref.6, ...), custom_call_target="tpu_custom_call" | custom-call | flops 268435456 | bytes 8388608 | tf_op jit(solution)/shard_map/local_state/pallas_call | solution.py:232
  6.6 0.5 collective-permute-start
  7.1 1.6 %collective-permute-done.refs_1_.refs_2_ = f32[8,136,128]{2,1,0:T(8,128)S(1)} collective-permute-done((f32[8,136,128]{2,1,0:T(8,128)S(1)}, f32[8,136,128]{2,1,0:T(8,128)S(1)}, u32[]{:S(2)}, u32[]{:S(2)}) %collective-permute-start) | collective-permute-done | bytes 557088 | tf_op jit(solution)/shard_map/ppermute | solution.py:657
  8.8 2.9 %collective-permute-start.1 = (f32[4,136,128]{2,1,0:T(8,128)S(1)}, f32[4,136,128]{2,1,0:T(8,128)S(1)}, u32[]{:S(2)}, u32[]{:S(2)}) collective-permute-start(f32[4,136,128]{2,1,0:T(8,128)S(1)} %get-tuple-element.73.refs_4_), channel_id=1, source_target_pairs={{0,8},{4,12},{8,0},{12,4},{16,24},{20,28},{24,16},{28,20},{1,9},{5... | collective-permute-start | bytes 835592 | tf_op jit(solution)/shard_map/ppermute | solution.py:657
  11.7 1.5 %collective-permute-start.2 = (f32[4,128,128]{2,1,0:T(8,128)S(1)}, f32[4,128,128]{2,1,0:T(8,128)S(1)}, u32[]{:S(2)}, u32[]{:S(2)}) collective-permute-start(f32[4,128,128]{2,1,0:T(8,128)S(1)} %get-tuple-element.74.refs_5_), channel_id=1, source_target_pairs={{0,16},{4,20},{8,24},{12,28},{16,0},{20,4},{24,8},{28,12},{1,17},{... | collective-permute-start | bytes 786440 | tf_op jit(solution)/shard_map/ppermute | solution.py:657
  13.3 6.4 %intra_0.1 = (bf16[16,256,128]{2,1,0:T(8,128)(2,1)S(1)}, bf16[16,256,128]{2,1,0:T(8,128)(2,1)S(1)}, bf16[16,256,256]{2,1,0:T(8,128)(2,1)S(1)}, f32[16,3,128,128]...) custom-call(f32[16,512]{1,0:T(8,128)S(1)} %copy-done, ...), custom_call_target="tpu_custom_call" | custom-call | flops 1073741824 | bytes 10485760 | tf_op jit(solution)/shard_map/intra_0/pallas_call | solution.py:291
  19.7 0.3 collective-permute-done.3.refs_3_
  20.1 1.7 %collective-permute-start.4 = (f32[4,128,128]{2,1,0:T(8,128)S(1)}, f32[4,128,128]{2,1,0:T(8,128)S(1)}, u32[]{:S(2)}, u32[]{:S(2)}) collective-permute-start(f32[4,128,128]{2,1,0:T(8,128)S(1)} %get-tuple-element.85), channel_id=1, source_target_pairs={{0,16},{4,20},{8,24},{12,28},{16,0},{20,4},{24,8},{28,12},{1,17},{... | collective-permute-start | bytes 786440 | tf_op jit(solution)/shard_map/ppermute | solution.py:657
  21.8 1.5 %collective-permute-start.5 = (f32[4,128,128]{2,1,0:T(8,128)S(1)}, f32[4,128,128]{2,1,0:T(8,128)S(1)}, u32[]{:S(2)}, u32[]{:S(2)}) collective-permute-start(f32[4,128,128]{2,1,0:T(8,128)S(1)} %get-tuple-element.86), channel_id=1, source_target_pairs={{0,8},{4,12},{8,0},{12,4},{16,24},{20,28},{24,16},{28,20},{1,9},{5... | collective-permute-start | bytes 786440 | tf_op jit(solution)/shard_map/ppermute | solution.py:657
  23.3 5.6 %intra_1.1 = (bf16[16,256,128]{2,1,0:T(8,128)(2,1)S(1)}, bf16[16,256,128]{2,1,0:T(8,128)(2,1)S(1)}, bf16[16,256,256]{2,1,0:T(8,128)(2,1)S(1)}, f32[16,3,128,128]...) custom-call(f32[16,512]{1,0:T(8,128)S(1)} %copy-done, ...), custom_call_target="tpu_custom_call" | custom-call | flops 1073741824 | bytes 10485760 | tf_op jit(solution)/shard_map/intra_1/pallas_call | solution.py:291
  29.0 0.2 earlier_enter.1
  29.3 1.9 %collective-permute-done.6.recv_ref = f32[8,128,128]{2,1,0:T(8,128)S(1)} collective-permute-done((f32[8,128,128]{2,1,0:T(8,128)S(1)}, f32[8,128,128]{2,1,0:T(8,128)S(1)}, u32[]{:S(2)}, u32[]{:S(2)}) %collective-permute-start.6) | collective-permute-done | bytes 524320 | tf_op jit(solution)/shard_map/ppermute | solution.py:657
  31.2 2.7 %attend.1 = (f32[16,256,128]{2,1,0:T(8,128)S(1)}, f32[16,256,128]{2,1,0:T(8,128)S(1)}, f32[2,512]{1,0:T(2,128)S(1)}) custom-call(f32[8,128]{1,0:T(8,128)S(1)} %broadcast_in_dim.2.place_ref, f32[16,128]{1,0:T(8,128)S(1)} %copy-done.1, f32[8,128,128]{2,1,0:T(8,128)S(1)} %get-tuple-element.91.keep_ref, f32[8,128,128]{2,1,0:T(8,128)S(1)} %collective-permute-done.6.recv_ref, ...), custom_call_target="tpu_custom_call" | custom-call | flops 536870912 | bytes 16777216 | tf_op jit(solution)/shard_map/attend/pallas_call | solution.py:354
  33.9 1.6 %collective-permute-start.7 = (f32[2,512]{1,0:T(2,128)S(1)}, f32[2,512]{1,0:T(2,128)S(1)}, u32[]{:S(2)}, u32[]{:S(2)}) collective-permute-start(f32[2,512]{1,0:T(2,128)S(1)} %get-tuple-element.98.first_ref), channel_id=1, source_target_pairs={{0,1},{1,0},{2,3},{3,2},{4,5},{5,4},{6,7},{7,6},{8,9},{9,8},{10,11... | collective-permute-start | bytes 12296 | tf_op jit(solution)/shard_map/ppermute | solution.py:657
  35.5 1.5 %scaled_queries.1 = (bf16[2,16,128,256]{3,2,1,0:T(8,128)(2,1)S(1)}, f32[2,16,128]{2,1,0:T(8,128)S(1)}) custom-call(f32[16,512]{1,0:T(8,128)S(1)} %copy-done, bf16[16,256,128]{2,1,0:T(8,128)(2,1)S(1)} %get-tuple-element.99.q0, bf16[16,256,128]{2,1,0:T(8,128)(2,1)S(1)} %get-tuple-element.93.q1), custom_call_target="tpu_custom_call" | custom-call | flops 2097152 | bytes 4194304 | tf_op jit(solution)/shard_map/scaled_queries/pallas_call | solution.py:381
  37.0 0.5 collective-permute-done.7.second_ref
  37.5 2.6 %collective-permute-start.8 = (f32[2,512]{1,0:T(2,128)S(1)}, f32[2,512]{1,0:T(2,128)S(1)}, u32[]{:S(2)}, u32[]{:S(2)}) collective-permute-start(f32[2,512]{1,0:T(2,128)S(1)} %add.15.first_ref), channel_id=1, source_target_pairs={{0,2},{1,3},{2,0},{3,1},{4,6},{5,7},{6,4},{7,5},{8,10},{9,11},{10,... | collective-permute-start | bytes 12296 | tf_op jit(solution)/shard_map/ppermute | solution.py:657
  40.1 2.0 %remaining_decay.1.remaining_ref = f32[2,16,256,128]{3,2,1,0:T(8,128)S(1)} custom-call(f32[16,512]{1,0:T(8,128)S(1)} %copy-done), custom_call_target="tpu_custom_call" | custom-call | flops 1048576 | bytes 4194304 | tf_op jit(solution)/shard_map/remaining_decay/pallas_call | solution.py:408
  42.1 2.7 %norm_grad.1 = (bf16[16,256,128]{2,1,0:T(8,128)(2,1)S(1)}, bf16[16,256,128]{2,1,0:T(8,128)(2,1)S(1)}, f32[8,128,128]{2,1,0:T(8,128)S(1)}, f32[8,128,128]{2,1,0:T(8,128)S(1)}, f32[16,128,128]{2,1,0:T(8,128)S(1)}) custom-call(f32[8,128]{1,0:T(8,128)S(1)} %broadcast_in_dim.2.place_ref, f32[2,16,128]{2,1,0:T(8,128)S(1)} %get-tuple-element.100.ends_ref, ...), custom_call_target="tpu_custom_call" | custom-call | flops 268435456 | bytes 14680064 | tf_op jit(solution)/shard_map/norm_grad/pallas_call | solution.py:456
  44.9 1.9 %collective-permute-done.9.refs_2_ = f32[8,128,128]{2,1,0:T(8,128)S(1)} collective-permute-done((f32[8,128,128]{2,1,0:T(8,128)S(1)}, f32[8,128,128]{2,1,0:T(8,128)S(1)}, u32[]{:S(2)}, u32[]{:S(2)}) %collective-permute-start.9) | collective-permute-done | bytes 524320 | tf_op jit(solution)/shard_map/ppermute | solution.py:657
  46.8 1.6 %collective-permute-start.10 = (f32[4,128,128]{2,1,0:T(8,128)S(1)}, f32[4,128,128]{2,1,0:T(8,128)S(1)}, u32[]{:S(2)}, u32[]{:S(2)}) collective-permute-start(f32[4,128,128]{2,1,0:T(8,128)S(1)} %get-tuple-element.109.refs_1_), channel_id=1, source_target_pairs={{0,8},{4,12},{8,0},{12,4},{16,24},{20,28},{24,16},{28,20},{1,9},{5... | collective-permute-start | bytes 786440 | tf_op jit(solution)/shard_map/ppermute | solution.py:657
  48.4 0.5 collective-permute-start.11
  48.9 5.6 %grad_query.1 = (f32[2,16,256,128]{3,2,1,0:T(8,128)S(1)}, bf16[2,16,256,256]{3,2,1,0:T(8,128)(2,1)S(1)}) custom-call(f32[8,128]{1,0:T(8,128)S(1)} %broadcast_in_dim.2.place_ref, f32[2,16,128]{2,1,0:T(8,128)S(1)} %get-tuple-element.100.ends_ref, f32[8,128,128]{2,1,0:T(8,128)S(1)} %get-tuple-element.91.keep_ref, ...), custom_call_target="tpu_custom_call" | custom-call | flops 1610612736 | bytes 12582912 | tf_op jit(solution)/shard_map/grad_query/pallas_call | solution.py:539
  54.5 0.7 %collective-permute-done.10.refs_3_ = f32[4,128,128]{2,1,0:T(8,128)S(1)} collective-permute-done((f32[4,128,128]{2,1,0:T(8,128)S(1)}, f32[4,128,128]{2,1,0:T(8,128)S(1)}, u32[]{:S(2)}, u32[]{:S(2)}) %collective-permute-start.10) | collective-permute-done | bytes 262176 | tf_op jit(solution)/shard_map/ppermute | solution.py:657
  55.3 1.2 %collective-permute-done.11.refs_4_ = f32[4,128,128]{2,1,0:T(8,128)S(1)} collective-permute-done((f32[4,128,128]{2,1,0:T(8,128)S(1)}, f32[4,128,128]{2,1,0:T(8,128)S(1)}, u32[]{:S(2)}, u32[]{:S(2)}) %collective-permute-start.11) | collective-permute-done | bytes 262176 | tf_op jit(solution)/shard_map/ppermute | solution.py:657
  56.6 0.6 collective-permute-start.12
  57.1 0.5 collective-permute-start.13
  57.7 5.8 %grad_key_value.1 = (f32[2,16,256,128]{3,2,1,0:T(8,128)S(1)}, f32[2,16,256,128]{3,2,1,0:T(8,128)S(1)}, bf16[512,16,128]{2,1,0:T(8,128)(2,1)}) custom-call(bf16[2,16,256,256]{3,2,1,0:T(8,128)(2,1)S(1)} %get-tuple-element.116.gs_ref, bf16[16,256,256]{2,1,0:T(8,128)(2,1)S(1)} %get-tuple-element.121.w0, bf16[16,256,256]{2,1,0:T(8,128)(2,1)S(1)} %get-tuple-element.122.w1, ...), custom_call_target="tpu_custom_call" | custom-call | flops 1610612736 | bytes 31457280 | tf_op jit(solution)/shard_map/grad_key_value/pallas_call | solution.py:583
  63.5 0.3 collective-permute-done.12.refs_5_
  63.8 0.2 collective-permute-done.13.refs_6_
  64.3 2.6 %normed_rows.1 = bf16[512,16,128]{2,1,0:T(8,128)(2,1)} custom-call(f32[16,128]{1,0:T(8,128)S(1)} %copy-done.1, f32[2,512]{1,0:T(2,128)S(1)} %add.16.sums_ref, f32[16,256,128]{2,1,0:T(8,128)S(1)} %get-tuple-element.105.att0, f32[16,256,128]{2,1,0:T(8,128)S(1)} %get-tuple-element.106.att1), custom_call_target="tpu_custom_call" | custom-call | flops 3145728 | bytes 6291456 | tf_op jit(solution)/shard_map/normed_rows/pallas_call | solution.py:504
  66.9 5.9 %finish.1 = (bf16[512,16,128]{2,1,0:T(8,128)(2,1)}, bf16[512,16,128]{2,1,0:T(8,128)(2,1)}) custom-call(f32[8,128]{1,0:T(8,128)S(1)} %broadcast_in_dim.2.place_ref, f32[2,16,128]{2,1,0:T(8,128)S(1)} %get-tuple-element.100.ends_ref, f32[8,128,128]{2,1,0:T(8,128)S(1)} %get-tuple-element.131.keep_ref, f32[8,128,128]{2,1,0:T(8,128)S(1)} %collective-permute-done.14.recv_ref, ...), custom_call_target="tpu_custom_call" | custom-call | flops 1073741824 | bytes 16777216 | tf_op jit(solution)/shard_map/finish/pallas_call | solution.py:637
  (25 shorter events, 1.0 us)
Async XLA Ops:
  0.8 12.4 %copy-start = (f32[16,512]{1,0:T(8,128)S(1)}, f32[16,512]{1,0:T(8,128)}, u32[]{:S(2)}) copy-start(f32[16,512]{1,0:T(8,128)} %ld_ref.6) | copy-start | bytes 98308
  6.6 2.1 %collective-permute-start = (f32[8,136,128]{2,1,0:T(8,128)S(1)}, f32[8,136,128]{2,1,0:T(8,128)S(1)}, u32[]{:S(2)}, u32[]{:S(2)}) collective-permute-start(f32[8,136,128]{2,1,0:T(8,128)S(1)} %get-tuple-element.71), channel_id=1, source_target_pairs={{0,4},{4,0},{8,12},{12,8},{16,20},{20,16},{24,28},{28,24},{1,5},{5... | collective-permute-start | bytes 1671176 | tf_op jit(solution)/shard_map/ppermute | solution.py:657
  8.8 11.2 %collective-permute-start.1 = (f32[4,136,128]{2,1,0:T(8,128)S(1)}, f32[4,136,128]{2,1,0:T(8,128)S(1)}, u32[]{:S(2)}, u32[]{:S(2)}) collective-permute-start(f32[4,136,128]{2,1,0:T(8,128)S(1)} %get-tuple-element.73.refs_4_), channel_id=1, source_target_pairs={{0,8},{4,12},{8,0},{12,4},{16,24},{20,28},{24,16},{28,20},{1,9},{5... | collective-permute-start | bytes 835592 | tf_op jit(solution)/shard_map/ppermute | solution.py:657
  11.7 8.3 %collective-permute-start.2 = (f32[4,128,128]{2,1,0:T(8,128)S(1)}, f32[4,128,128]{2,1,0:T(8,128)S(1)}, u32[]{:S(2)}, u32[]{:S(2)}) collective-permute-start(f32[4,128,128]{2,1,0:T(8,128)S(1)} %get-tuple-element.74.refs_5_), channel_id=1, source_target_pairs={{0,16},{4,20},{8,24},{12,28},{16,0},{20,4},{24,8},{28,12},{1,17},{... | collective-permute-start | bytes 786440 | tf_op jit(solution)/shard_map/ppermute | solution.py:657
  13.2 6.7 %collective-permute-start.3 = (f32[8,128]{1,0:T(8,128)S(1)}, f32[8,128]{1,0:T(8,128)S(1)}, u32[]{:S(2)}, u32[]{:S(2)}) collective-permute-start(f32[8,128]{1,0:T(8,128)S(1)} %get-tuple-element.72.refs_2_), channel_id=1, source_target_pairs={{0,24},{4,28},{8,16},{12,20},{16,8},{20,12},{24,0},{28,4},{1,25},{... | collective-permute-start | bytes 12296 | tf_op jit(solution)/shard_map/ppermute | solution.py:657
  20.1 8.9 %collective-permute-start.4 = (f32[4,128,128]{2,1,0:T(8,128)S(1)}, f32[4,128,128]{2,1,0:T(8,128)S(1)}, u32[]{:S(2)}, u32[]{:S(2)}) collective-permute-start(f32[4,128,128]{2,1,0:T(8,128)S(1)} %get-tuple-element.85), channel_id=1, source_target_pairs={{0,16},{4,20},{8,24},{12,28},{16,0},{20,4},{24,8},{28,12},{1,17},{... | collective-permute-start | bytes 786440 | tf_op jit(solution)/shard_map/ppermute | solution.py:657
  21.8 7.2 %collective-permute-start.5 = (f32[4,128,128]{2,1,0:T(8,128)S(1)}, f32[4,128,128]{2,1,0:T(8,128)S(1)}, u32[]{:S(2)}, u32[]{:S(2)}) collective-permute-start(f32[4,128,128]{2,1,0:T(8,128)S(1)} %get-tuple-element.86), channel_id=1, source_target_pairs={{0,8},{4,12},{8,0},{12,4},{16,24},{20,28},{24,16},{28,20},{1,9},{5... | collective-permute-start | bytes 786440 | tf_op jit(solution)/shard_map/ppermute | solution.py:657
  28.9 2.3 %copy-start.1 = (f32[16,128]{1,0:T(8,128)S(1)}, f32[16,128]{1,0:T(8,128)}, u32[]{:S(2)}) copy-start(f32[16,128]{1,0:T(8,128)} %gain_ref.4) | copy-start | bytes 24580
  29.2 2.0 %collective-permute-start.6 = (f32[8,128,128]{2,1,0:T(8,128)S(1)}, f32[8,128,128]{2,1,0:T(8,128)S(1)}, u32[]{:S(2)}, u32[]{:S(2)}) collective-permute-start(f32[8,128,128]{2,1,0:T(8,128)S(1)} %get-tuple-element.92), channel_id=1, source_target_pairs={{0,4},{4,0},{8,12},{12,8},{16,20},{20,16},{24,28},{28,24},{1,5},{5... | collective-permute-start | bytes 1572872 | tf_op jit(solution)/shard_map/ppermute | solution.py:657
  33.9 3.6 %collective-permute-start.7 = (f32[2,512]{1,0:T(2,128)S(1)}, f32[2,512]{1,0:T(2,128)S(1)}, u32[]{:S(2)}, u32[]{:S(2)}) collective-permute-start(f32[2,512]{1,0:T(2,128)S(1)} %get-tuple-element.98.first_ref), channel_id=1, source_target_pairs={{0,1},{1,0},{2,3},{3,2},{4,5},{5,4},{6,7},{7,6},{8,9},{9,8},{10,11... | collective-permute-start | bytes 12296 | tf_op jit(solution)/shard_map/ppermute | solution.py:657
  37.5 4.6 %collective-permute-start.8 = (f32[2,512]{1,0:T(2,128)S(1)}, f32[2,512]{1,0:T(2,128)S(1)}, u32[]{:S(2)}, u32[]{:S(2)}) collective-permute-start(f32[2,512]{1,0:T(2,128)S(1)} %add.15.first_ref), channel_id=1, source_target_pairs={{0,2},{1,3},{2,0},{3,1},{4,6},{5,7},{6,4},{7,5},{8,10},{9,11},{10,... | collective-permute-start | bytes 12296 | tf_op jit(solution)/shard_map/ppermute | solution.py:657
  44.8 2.0 %collective-permute-start.9 = (f32[8,128,128]{2,1,0:T(8,128)S(1)}, f32[8,128,128]{2,1,0:T(8,128)S(1)}, u32[]{:S(2)}, u32[]{:S(2)}) collective-permute-start(f32[8,128,128]{2,1,0:T(8,128)S(1)} %get-tuple-element.108), channel_id=1, source_target_pairs={{0,4},{4,0},{8,12},{12,8},{16,20},{20,16},{24,28},{28,24},{1,5},{5... | collective-permute-start | bytes 1572872 | tf_op jit(solution)/shard_map/ppermute | solution.py:657
  46.8 8.4 %collective-permute-start.10 = (f32[4,128,128]{2,1,0:T(8,128)S(1)}, f32[4,128,128]{2,1,0:T(8,128)S(1)}, u32[]{:S(2)}, u32[]{:S(2)}) collective-permute-start(f32[4,128,128]{2,1,0:T(8,128)S(1)} %get-tuple-element.109.refs_1_), channel_id=1, source_target_pairs={{0,8},{4,12},{8,0},{12,4},{16,24},{20,28},{24,16},{28,20},{1,9},{5... | collective-permute-start | bytes 786440 | tf_op jit(solution)/shard_map/ppermute | solution.py:657
  48.4 8.1 %collective-permute-start.11 = (f32[4,128,128]{2,1,0:T(8,128)S(1)}, f32[4,128,128]{2,1,0:T(8,128)S(1)}, u32[]{:S(2)}, u32[]{:S(2)}) collective-permute-start(f32[4,128,128]{2,1,0:T(8,128)S(1)} %get-tuple-element.110.refs_2_), channel_id=1, source_target_pairs={{0,16},{4,20},{8,24},{12,28},{16,0},{20,4},{24,8},{28,12},{1,17},{... | collective-permute-start | bytes 786440 | tf_op jit(solution)/shard_map/ppermute | solution.py:657
  56.6 7.3 %collective-permute-start.12 = (f32[4,128,128]{2,1,0:T(8,128)S(1)}, f32[4,128,128]{2,1,0:T(8,128)S(1)}, u32[]{:S(2)}, u32[]{:S(2)}) collective-permute-start(f32[4,128,128]{2,1,0:T(8,128)S(1)} %get-tuple-element.119), channel_id=1, source_target_pairs={{0,16},{4,20},{8,24},{12,28},{16,0},{20,4},{24,8},{28,12},{1,17},{... | collective-permute-start | bytes 786440 | tf_op jit(solution)/shard_map/ppermute | solution.py:657
  57.1 6.9 %collective-permute-start.13 = (f32[4,128,128]{2,1,0:T(8,128)S(1)}, f32[4,128,128]{2,1,0:T(8,128)S(1)}, u32[]{:S(2)}, u32[]{:S(2)}) collective-permute-start(f32[4,128,128]{2,1,0:T(8,128)S(1)} %get-tuple-element.120), channel_id=1, source_target_pairs={{0,8},{4,12},{8,0},{12,4},{16,24},{20,28},{24,16},{28,20},{1,9},{5... | collective-permute-start | bytes 786440 | tf_op jit(solution)/shard_map/ppermute | solution.py:657
  64.2 2.7 %collective-permute-start.14 = (f32[8,128,128]{2,1,0:T(8,128)S(1)}, f32[8,128,128]{2,1,0:T(8,128)S(1)}, u32[]{:S(2)}, u32[]{:S(2)}) collective-permute-start(f32[8,128,128]{2,1,0:T(8,128)S(1)} %get-tuple-element.129), channel_id=1, source_target_pairs={{0,4},{4,0},{8,12},{12,8},{16,20},{20,16},{24,28},{28,24},{1,5},{5... | collective-permute-start | bytes 1572872 | tf_op jit(solution)/shard_map/ppermute | solution.py:657

commit v8 on v7

--- a/solution.py
+++ b/solution.py
@@ -654,12 +654,14 @@
 
 def swap(value, axis, bit):
     count = lax.axis_size(axis)
-    return lax.ppermute(value, axis, [(i, i ^ bit) for i in range(count)])
+    bits = bit if isinstance(bit, tuple) else (bit, bit)
+    return lax.ppermute(value, axis, [(i, i ^ bits[i % 2]) for i in range(count)])
 
 
 def mix(body, backward, place, arrays, shapes, name):
     def kernel(place_ref, *refs):
         bits = [is_set(place_ref, which) != backward for which in (LATE, RIGHT, LOW)]
+        bits.append(is_set(place_ref, UPPER))
         body(bits, refs[: len(arrays)], refs[len(arrays) :])
 
     return pl.pallas_call(
@@ -676,29 +678,23 @@
 OWN, PARTNER, CHIP, ROW, CORNER = range(5)
 
 
-def mix_total(bits, own, got, d_own, d_got, first, second):
+def mix_total(bits, own, got, d_own, d_got, out):
     late = bits[0]
-    quarter = first.shape[0]
-    for h in range(2 * quarter):
-        total = jnp.where(late, 1.0, d_got(h)) * own[h, :HD] + jnp.where(late, d_own(h), 1.0) * got[h, :HD]
-        if h < quarter:
-            first[h, :HD] = total
-        else:
-            second[h - quarter] = total
+    for h in range(out.shape[0]):
+        scale_own, scale_got = jnp.where(late, 1.0, d_got(h)), jnp.where(late, d_own(h), 1.0)
+        out[h, :HD] = scale_own * own[h, :HD] + scale_got * got[h, :HD]
 
 
 def mix_total_first(bits, arrays, outputs):
     own, got = arrays
-    first, second, chip = outputs
-    quarter = first.shape[0]
+    total, chip = outputs
     d_own = lambda h: own[h, HD : HD + 1]
     d_got = lambda h: got[h, HD : HD + 1]
-    mix_total(bits, own, got, d_own, d_got, first, second)
-    for h in range(2 * quarter):
-        whole = d_own(h) * d_got(h)
-        chip[h : h + 1] = whole
-        place = HD + (TILE // 2) * (h // quarter)
-        first[h % quarter, place : place + TILE // 2] = jnp.broadcast_to(whole, (TILE // 2, HD))
+    mix_total(bits, own, got, d_own, d_got, total)
+    for h in range(total.shape[0]):
+        both = d_own(h) * d_got(h)
+        chip[h : h + 1] = both
+        total[h, HD:] = jnp.broadcast_to(both, (TILE, HD))
 
 
 def mix_total_again(bits, arrays, outputs):
@@ -707,64 +703,67 @@
     mix_total(bits, own, got, decay(OWN), decay(PARTNER), *outputs)
 
 
-def mix_next(bits, decay, totals, gots, outputs):
-    _, right, low = bits
-    quarter = totals[1].shape[0]
-    for i in range(quarter):
-        h = i
-        scale_total = jnp.where(right, 1.0, decay(ROW, h))
-        scale_got = jnp.where(right, decay(CHIP, h), 1.0)
-        outputs[0][i] = scale_total * totals[0][i, :HD] + scale_got * gots[0][i, :HD]
-        h = quarter + i
-        scale_total = jnp.where(low & right, 0.0, 1.0)
-        corner = jnp.where(right, 1.0, decay(CHIP, h) * decay(CORNER, h))
-        scale_got = jnp.where(low, corner, 0.0)
-        outputs[1][i] = scale_total * totals[1][i] + scale_got * gots[1][i]
+def mix_next(bits, chip, corner, row, total, one, out):
+    _, right, low, by_column = bits
+    for h in range(out.shape[0]):
+        scale_total = jnp.where(
+            by_column, jnp.where(low & right, 0.0, 1.0), jnp.where(right, 1.0, row(h))
+        )
+        scale_one = jnp.where(
+            by_column,
+            jnp.where(low, jnp.where(right, 1.0, chip(h) * corner(h)), 0.0),
+            jnp.where(right, chip(h), 1.0),
+        )
+        out[h, :HD] = scale_total * total[h, :HD] + scale_one * one[h, :HD]
 
 
 def mix_next_first(bits, arrays, outputs):
-    own, got, chip, corner, first, second, one_a, one_b = arrays
-    table = outputs[2]
-    quarter = second.shape[0]
-    for h in range(2 * quarter):
-        place = HD + (TILE // 2) * (h // quarter)
-        table[OWN, h : h + 1] = own[h, HD : HD + 1]
-        table[PARTNER, h : h + 1] = got[h, HD : HD + 1]
-        table[ROW, h : h + 1] = one_a[h % quarter, place : place + 1]
-    table[CHIP] = chip[...]
-    table[CORNER] = corner[...]
-    decay = lambda which, h: table[which, h : h + 1]
-    mix_next(bits, decay, (first, second), (one_a, one_b), outputs[:2])
+    chip, corner, total, one = arrays
+    (out,) = outputs
+    lines = lambda ref: lambda h: ref[h : h + 1]
+    mix_next(bits, lines(chip), lines(corner), lambda h: one[h, HD : HD + 1], total, one, out)
+    out[:, HD:] = total[:, HD:]
 
 
 def mix_next_again(bits, arrays, outputs):
-    table, first, second, one_a, one_b = arrays
-    decay = lambda which, h: table[which, h : h + 1]
-    mix_next(bits, decay, (first, second), (one_a, one_b), outputs)
-
-
-def mix_enter(bits, arrays, outputs):
-    table, own, got, one_a, one_b, two_a, two_b = arrays
-    kept, sent = outputs
-    late, right, low = bits
-    quarter = one_b.shape[0]
-    decay = lambda which, h: table[which, h : h + 1]
-    for h in range(2 * quarter):
-        i = h % quarter
-        row = jnp.where(right, decay(ROW, h), 1.0)
-        if h < quarter:
-            one, two = one_a[i, :HD], two_a[i]
-            scale_one = jnp.where(right, 1.0, 0.0)
-            scale_two = jnp.where(low, row, 0.0)
-        else:
-            one, two = one_b[i], two_b[i]
-            scale_one = jnp.where(low, jnp.where(right, row, decay(CORNER, h)), 0.0)
-            scale_two = jnp.where(low | right, 1.0, 0.0)
-        enter = scale_one * one + scale_two * two
-        after = jnp.where(late, decay(PARTNER, h), decay(OWN, h)) * enter
+    table, total, one = arrays
+    decay = lambda which: lambda h: table[which, h : h + 1]
+    mix_next(bits, decay(CHIP), decay(CORNER), decay(ROW), total, one, *outputs)
+
+
+def mix_enter(bits, table, own, got, one, two, kept, sent):
+    late, right, low, by_column = bits
+    for h in range(kept.shape[0]):
+        decay = lambda which: table[which, h : h + 1]
+        row = jnp.where(right, decay(ROW), 1.0)
+        scale_one = jnp.where(
+            by_column,
+            jnp.where(low, jnp.where(right, row, decay(CORNER)), 0.0),
+            jnp.where(right, 1.0, 0.0),
+        )
+        scale_two = jnp.where(
+            by_column, jnp.where(low | right, 1.0, 0.0), jnp.where(low, row, 0.0)
+        )
+        enter = scale_one * one[h, :HD] + scale_two * two[h, :HD]
+        after = jnp.where(late, decay(PARTNER), decay(OWN)) * enter
         after += jnp.where(late, got[h, :HD], own[h, :HD])
         kept[h] = jnp.where(late, after, enter)
         sent[h] = jnp.where(late, enter, after)
+
+
+def mix_enter_first(bits, arrays, outputs):
+    own, got, chip, corner, one, two = arrays
+    kept, sent, table = outputs
+    for h in range(kept.shape[0]):
+        at, line = slice(h, h + 1), slice(HD, HD + 1)
+        table[OWN, at], table[PARTNER, at] = own[h, line], got[h, line]
+        table[ROW, at] = jnp.where(bits[3], two[h, line], one[h, line])
+    table[CHIP], table[CORNER] = chip[...], corner[...]
+    mix_enter(bits, table, own, got, one, two, kept, sent)
+
+
+def mix_enter_again(bits, arrays, outputs):
+    mix_enter(bits, *arrays, *outputs)
 
 
 def entering_quad(own, send, table, place, backward, tasks):
@@ -777,37 +776,36 @@
 
     name = "later" if backward else "earlier"
     half = own.shape[0]
-    quarter = half // 2
-    states, wide = (quarter, HD, HD), (quarter, HD + TILE, HD)
+    states, wide = (half, HD, HD), (half, HD + TILE, HD)
     got = swap(send, "seq", 1)
     if table is None:
-        first, second, chip = mix(
-            mix_total_first, backward, place, (own, got), (wide, states, (half, HD)), name + "_total"
+        total, chip = mix(
+            mix_total_first, backward, place, (own, got), (wide, (half, HD)), name + "_total"
+        )
+        one, corner = swap(total, "seq", (2, 4)), swap(chip, "seq", 6)
+        one, corner = work(1, total, (one, corner))
+        (after,) = mix(
+            mix_next_first, backward, place, (chip, corner, total, one), (wide,), name + "_next"
         )
     else:
-        first, second = mix(
-            mix_total_again, backward, place, (table, own, got), (states, states), name + "_total"
-        )
-    one_a, one_b = swap(first, "seq", 2), swap(second, "seq", 4)
+        (total,) = mix(
+            mix_total_again, backward, place, (table, own, got), (states,), name + "_total"
+        )
+        one = work(1, total, swap(total, "seq", (2, 4)))
+        (after,) = mix(
+            mix_next_again, backward, place, (table, total, one), (states,), name + "_next"
+        )
+    two = work(2, after, swap(after, "seq", (4, 2)))
     if table is None:
-        corner = swap(chip, "seq", 6)
-        one_a, one_b, corner = work(1, second, (one_a, one_b, corner))
-        next_a, next_b, table = mix(
-            mix_next_first, backward, place, (own, got, chip, corner, first, second, one_a, one_b),
-            (states, states, (5, half, HD)), name + "_next",
+        kept, sent, table = mix(
+            mix_enter_first, backward, place, (own, got, chip, corner, one, two),
+            (states, states, (5, half, HD)), name + "_enter",
         )
     else:
-        one_a, one_b = work(1, second, (one_a, one_b))
-        next_a, next_b = mix(
-            mix_next_again, backward, place, (table, first, second, one_a, one_b), (states, states),
-            name + "_next",
-        )
-    two_a, two_b = swap(next_a, "seq", 4), swap(next_b, "seq", 2)
-    two_a, two_b = work(2, next_b, (two_a, two_b))
-    kept, sent = mix(
-        mix_enter, backward, place, (table, own, got, one_a, one_b, two_a, two_b),
-        ((half, HD, HD), (half, HD, HD)), name + "_enter",
-    )
+        kept, sent = mix(
+            mix_enter_again, backward, place, (table, own, got, one, two), (states, states),
+            name + "_enter",
+        )
     received = swap(sent, "seq", 1)
     work(3, sent)
     return kept, received, table

time: 73 us -> 75.8 us (1.038)
  waiting for transfers between devices: 8.84 us -> 15.4 us
  starting transfers between devices: 15.8 us -> 12 us
    ppermute x15 -> x11, waiting for transfers between devices: 8.84 us -> 15.4 us  [swap(): lax.ppermute(value, axis, [(i, i ^ bits[i % 2]) for i in range(count)])]
    ppermute x15 -> x11, starting transfers between devices: 15.8 us -> 12 us  [swap(): lax.ppermute(value, axis, [(i, i ^ bits[i % 2]) for i in range(count)])]
  transfers between devices with their start and end apart: 15 -> 11, of which waited for: 10 -> 8; matrix products, arithmetic and copies ran while one was open for 0% -> 0% of each run, Pallas kernels for 41% -> 39%
where the time goes in v8:
time: 75.8 us; the launch traced here: 75.6 us
  Pallas kernels  47.2 us (62%)
  waiting for transfers between devices  15.4 us (20%)
  starting transfers between devices  12 us (16%)
  between operations  0.81 us (1%)
    ppermute x11, waiting for transfers between devices, swap(): lax.ppermute(value, axis, [(i, i ^ bits[i % 2]) for i in range(count)])  15.4 us
    ppermute x11, starting transfers between devices, swap(): lax.ppermute(value, axis, [(i, i ^ bits[i % 2]) for i in range(count)])  12 us
    pallas_call x2, Pallas kernels, intra(): pl.pallas_call(kernel, in_specs=[NEAR] * 4 + [FAR, FAR], out_specs=[NEAR]...  12 us
    pallas_call x1, Pallas kernels, finish(): pl.pallas_call(finish_kernel, in_specs=[NEAR] * 9, out_specs=[FAR, FAR],...  5.91 us
    pallas_call x1, Pallas kernels, grad_key_value(): pl.pallas_call(grad_kv_kernel, in_specs=[NEAR] * 12, out_specs=[NEAR, NEA...  5.83 us
    pallas_call x1, Pallas kernels, local_state(): pl.pallas_call(state_kernel, in_specs=[NEAR, FAR, FAR, FAR], out_specs=[N...  5.76 us
    pallas_call x1, Pallas kernels, grad_query(): pl.pallas_call(grad_q_kernel, in_specs=[NEAR] * 13, out_specs=[NEAR, NEAR...  5.59 us
    pallas_call x1, Pallas kernels, norm_grad(): pl.pallas_call(norm_grad_kernel, in_specs=[NEAR] * 9, out_specs=[NEAR] *...  2.64 us
  transfers between devices with their start and end apart: 11, of which 8 were waited for; matrix products, arithmetic and copies ran while one was open for 0% of the time, Pallas kernels for 39%

profile of v8, /device:TPU:0, one launch (start us, length us, event | category | flops | bytes accessed | tf_op | source)
XLA Modules:
  0.0 75.6 jit_solution(8545535955736055814)
XLA Ops:
  0.7 0.1 stack.23
  0.8 5.8 %local_state.1 = (f32[8,136,128]{2,1,0:T(8,128)S(1)}, f32[8,136,128]{2,1,0:T(8,128)S(1)}, f32[16,128,128]{2,1,0:T(8,128)S(1)}, bf16[2,16,256,128]{3,2,1,0:T(8,128)(2,1)S(1)}, bf16[2,16,256,128]{3,2,1,0:T(8,128)(2,1)S(1)}) custom-call(f32[8,128]{1,0:T(8,128)S(1)} %broadcast_in_dim.2.place_ref, f32[16,512]{1,0:T(8,128)} %ld_ref.6, ...), custom_call_target="tpu_custom_call" | custom-call | flops 268435456 | bytes 8388608 | tf_op jit(solution)/shard_map/local_state/pallas_call | solution.py:232
  6.6 0.5 collective-permute-start
  7.1 1.6 %collective-permute-done.refs_1_ = f32[8,136,128]{2,1,0:T(8,128)S(1)} collective-permute-done((f32[8,136,128]{2,1,0:T(8,128)S(1)}, f32[8,136,128]{2,1,0:T(8,128)S(1)}, u32[]{:S(2)}, u32[]{:S(2)}) %collective-permute-start) | collective-permute-done | bytes 557088 | tf_op jit(solution)/shard_map/ppermute | solution.py:658
  8.8 2.9 %collective-permute-start.1 = (f32[8,136,128]{2,1,0:T(8,128)S(1)}, f32[8,136,128]{2,1,0:T(8,128)S(1)}, u32[]{:S(2)}, u32[]{:S(2)}) collective-permute-start(f32[8,136,128]{2,1,0:T(8,128)S(1)} %get-tuple-element.62.refs_2_), channel_id=1, source_target_pairs={{0,8},{4,20},{8,0},{12,28},{16,24},{20,4},{24,16},{28,12},{1,9},{5... | collective-permute-start | bytes 1671176 | tf_op jit(solution)/shard_map/ppermute | solution.py:658
  11.7 1.5 %collective-permute-start.2 = (f32[8,128]{1,0:T(8,128)S(1)}, f32[8,128]{1,0:T(8,128)S(1)}, u32[]{:S(2)}, u32[]{:S(2)}) collective-permute-start(f32[8,128]{1,0:T(8,128)S(1)} %get-tuple-element.61.refs_0_.refs_2_), channel_id=1, source_target_pairs={{0,24},{4,28},{8,16},{12,20},{16,8},{20,12},{24,0},{28,4},{1,25},{... | collective-permute-start | bytes 12296 | tf_op jit(solution)/shard_map/ppermute | solution.py:658
  13.2 6.4 %intra_0.1 = (bf16[16,256,128]{2,1,0:T(8,128)(2,1)S(1)}, bf16[16,256,128]{2,1,0:T(8,128)(2,1)S(1)}, bf16[16,256,256]{2,1,0:T(8,128)(2,1)S(1)}, f32[16,3,128,128]...) custom-call(f32[16,512]{1,0:T(8,128)S(1)} %copy-done, ...), custom_call_target="tpu_custom_call" | custom-call | flops 1073741824 | bytes 10485760 | tf_op jit(solution)/shard_map/intra_0/pallas_call | solution.py:291
  19.6 1.2 %collective-permute-done.2.refs_1_.refs_3_ = f32[8,128]{1,0:T(8,128)S(1)} collective-permute-done((f32[8,128]{1,0:T(8,128)S(1)}, f32[8,128]{1,0:T(8,128)S(1)}, u32[]{:S(2)}, u32[]{:S(2)}) %collective-permute-start.2) | collective-permute-done | bytes 4128 | tf_op jit(solution)/shard_map/ppermute | solution.py:658
  20.8 0.1 earlier_next.1
  20.9 0.6 collective-permute-start.3
  21.5 5.6 %intra_1.1 = (bf16[16,256,128]{2,1,0:T(8,128)(2,1)S(1)}, bf16[16,256,128]{2,1,0:T(8,128)(2,1)S(1)}, bf16[16,256,256]{2,1,0:T(8,128)(2,1)S(1)}, f32[16,3,128,128]...) custom-call(f32[16,512]{1,0:T(8,128)S(1)} %copy-done, ...), custom_call_target="tpu_custom_call" | custom-call | flops 1073741824 | bytes 10485760 | tf_op jit(solution)/shard_map/intra_1/pallas_call | solution.py:291
  27.1 3.4 %collective-permute-done.3.refs_5_ = f32[8,136,128]{2,1,0:T(8,128)S(1)} collective-permute-done((f32[8,136,128]{2,1,0:T(8,128)S(1)}, f32[8,136,128]{2,1,0:T(8,128)S(1)}, u32[]{:S(2)}, u32[]{:S(2)}) %collective-permute-start.3) | collective-permute-done | bytes 557088 | tf_op jit(solution)/shard_map/ppermute | solution.py:658
  30.5 0.2 earlier_enter.1
  30.8 1.9 %collective-permute-done.4.recv_ref = f32[8,128,128]{2,1,0:T(8,128)S(1)} collective-permute-done((f32[8,128,128]{2,1,0:T(8,128)S(1)}, f32[8,128,128]{2,1,0:T(8,128)S(1)}, u32[]{:S(2)}, u32[]{:S(2)}) %collective-permute-start.4) | collective-permute-done | bytes 524320 | tf_op jit(solution)/shard_map/ppermute | solution.py:658
  32.7 2.6 %attend.1 = (f32[16,256,128]{2,1,0:T(8,128)S(1)}, f32[16,256,128]{2,1,0:T(8,128)S(1)}, f32[2,512]{1,0:T(2,128)S(1)}) custom-call(f32[8,128]{1,0:T(8,128)S(1)} %broadcast_in_dim.2.place_ref, f32[16,128]{1,0:T(8,128)S(1)} %copy-done.1, f32[8,128,128]{2,1,0:T(8,128)S(1)} %get-tuple-element.75.keep_ref, f32[8,128,128]{2,1,0:T(8,128)S(1)} %collective-permute-done.4.recv_ref, ...), custom_call_target="tpu_custom_call" | custom-call | flops 536870912 | bytes 16777216 | tf_op jit(solution)/shard_map/attend/pallas_call | solution.py:354
  35.3 1.6 %collective-permute-start.5 = (f32[2,512]{1,0:T(2,128)S(1)}, f32[2,512]{1,0:T(2,128)S(1)}, u32[]{:S(2)}, u32[]{:S(2)}) collective-permute-start(f32[2,512]{1,0:T(2,128)S(1)} %get-tuple-element.82.first_ref), channel_id=1, source_target_pairs={{0,1},{1,0},{2,3},{3,2},{4,5},{5,4},{6,7},{7,6},{8,9},{9,8},{10,11... | collective-permute-start | bytes 12296 | tf_op jit(solution)/shard_map/ppermute | solution.py:658
  36.9 1.5 %scaled_queries.1 = (bf16[2,16,128,256]{3,2,1,0:T(8,128)(2,1)S(1)}, f32[2,16,128]{2,1,0:T(8,128)S(1)}) custom-call(f32[16,512]{1,0:T(8,128)S(1)} %copy-done, bf16[16,256,128]{2,1,0:T(8,128)(2,1)S(1)} %get-tuple-element.83.q0, bf16[16,256,128]{2,1,0:T(8,128)(2,1)S(1)} %get-tuple-element.77.q1), custom_call_target="tpu_custom_call" | custom-call | flops 2097152 | bytes 4194304 | tf_op jit(solution)/shard_map/scaled_queries/pallas_call | solution.py:381
  38.4 0.5 collective-permute-done.5.second_ref
  39.0 2.6 %collective-permute-start.6 = (f32[2,512]{1,0:T(2,128)S(1)}, f32[2,512]{1,0:T(2,128)S(1)}, u32[]{:S(2)}, u32[]{:S(2)}) collective-permute-start(f32[2,512]{1,0:T(2,128)S(1)} %add.15.first_ref), channel_id=1, source_target_pairs={{0,2},{1,3},{2,0},{3,1},{4,6},{5,7},{6,4},{7,5},{8,10},{9,11},{10,... | collective-permute-start | bytes 12296 | tf_op jit(solution)/shard_map/ppermute | solution.py:658
  41.5 2.0 %remaining_decay.1.remaining_ref = f32[2,16,256,128]{3,2,1,0:T(8,128)S(1)} custom-call(f32[16,512]{1,0:T(8,128)S(1)} %copy-done), custom_call_target="tpu_custom_call" | custom-call | flops 1048576 | bytes 4194304 | tf_op jit(solution)/shard_map/remaining_decay/pallas_call | solution.py:408
  43.6 2.6 %norm_grad.1 = (bf16[16,256,128]{2,1,0:T(8,128)(2,1)S(1)}, bf16[16,256,128]{2,1,0:T(8,128)(2,1)S(1)}, f32[8,128,128]{2,1,0:T(8,128)S(1)}, f32[8,128,128]{2,1,0:T(8,128)S(1)}, f32[16,128,128]{2,1,0:T(8,128)S(1)}) custom-call(f32[8,128]{1,0:T(8,128)S(1)} %broadcast_in_dim.2.place_ref, f32[2,16,128]{2,1,0:T(8,128)S(1)} %get-tuple-element.84.ends_ref, ...), custom_call_target="tpu_custom_call" | custom-call | flops 268435456 | bytes 14680064 | tf_op jit(solution)/shard_map/norm_grad/pallas_call | solution.py:456
  46.3 1.9 %collective-permute-done.7.refs_2_ = f32[8,128,128]{2,1,0:T(8,128)S(1)} collective-permute-done((f32[8,128,128]{2,1,0:T(8,128)S(1)}, f32[8,128,128]{2,1,0:T(8,128)S(1)}, u32[]{:S(2)}, u32[]{:S(2)}) %collective-permute-start.7) | collective-permute-done | bytes 524320 | tf_op jit(solution)/shard_map/ppermute | solution.py:658
  48.3 1.6 %collective-permute-start.8 = (f32[8,128,128]{2,1,0:T(8,128)S(1)}, f32[8,128,128]{2,1,0:T(8,128)S(1)}, u32[]{:S(2)}, u32[]{:S(2)}) collective-permute-start(f32[8,128,128]{2,1,0:T(8,128)S(1)} %later_total.1.refs_1_), channel_id=1, source_target_pairs={{0,8},{4,20},{8,0},{12,28},{16,24},{20,4},{24,16},{28,12},{1,9},{5... | collective-permute-start | bytes 1572872 | tf_op jit(solution)/shard_map/ppermute | solution.py:658
  49.8 5.6 %grad_query.1 = (f32[2,16,256,128]{3,2,1,0:T(8,128)S(1)}, bf16[2,16,256,256]{3,2,1,0:T(8,128)(2,1)S(1)}) custom-call(f32[8,128]{1,0:T(8,128)S(1)} %broadcast_in_dim.2.place_ref, f32[2,16,128]{2,1,0:T(8,128)S(1)} %get-tuple-element.84.ends_ref, f32[8,128,128]{2,1,0:T(8,128)S(1)} %get-tuple-element.75.keep_ref, ...), custom_call_target="tpu_custom_call" | custom-call | flops 1610612736 | bytes 12582912 | tf_op jit(solution)/shard_map/grad_query/pallas_call | solution.py:539
  55.4 2.1 %collective-permute-done.8.refs_2_.refs_3_ = f32[8,128,128]{2,1,0:T(8,128)S(1)} collective-permute-done((f32[8,128,128]{2,1,0:T(8,128)S(1)}, f32[8,128,128]{2,1,0:T(8,128)S(1)}, u32[]{:S(2)}, u32[]{:S(2)}) %collective-permute-start.8) | collective-permute-done | bytes 524320 | tf_op jit(solution)/shard_map/ppermute | solution.py:658
  57.5 0.1 later_next.1
  57.6 0.6 collective-permute-start.9
  58.2 5.8 %grad_key_value.1 = (f32[2,16,256,128]{3,2,1,0:T(8,128)S(1)}, f32[2,16,256,128]{3,2,1,0:T(8,128)S(1)}, bf16[512,16,128]{2,1,0:T(8,128)(2,1)}) custom-call(bf16[2,16,256,256]{3,2,1,0:T(8,128)(2,1)S(1)} %get-tuple-element.98.gs_ref, bf16[16,256,256]{2,1,0:T(8,128)(2,1)S(1)} %get-tuple-element.100.w0, bf16[16,256,256]{2,1,0:T(8,128)(2,1)S(1)} %get-tuple-element.101.w1, ...), custom_call_target="tpu_custom_call" | custom-call | flops 1610612736 | bytes 31457280 | tf_op jit(solution)/shard_map/grad_key_value/pallas_call | solution.py:583
  64.0 2.8 %collective-permute-done.9.refs_4_ = f32[8,128,128]{2,1,0:T(8,128)S(1)} collective-permute-done((f32[8,128,128]{2,1,0:T(8,128)S(1)}, f32[8,128,128]{2,1,0:T(8,128)S(1)}, u32[]{:S(2)}, u32[]{:S(2)}) %collective-permute-start.9) | collective-permute-done | bytes 524320 | tf_op jit(solution)/shard_map/ppermute | solution.py:658
  66.8 0.2 later_enter.1
  67.1 2.6 %normed_rows.1 = bf16[512,16,128]{2,1,0:T(8,128)(2,1)} custom-call(f32[16,128]{1,0:T(8,128)S(1)} %copy-done.1, f32[2,512]{1,0:T(2,128)S(1)} %add.16.sums_ref, f32[16,256,128]{2,1,0:T(8,128)S(1)} %get-tuple-element.89.att0, f32[16,256,128]{2,1,0:T(8,128)S(1)} %get-tuple-element.90.att1), custom_call_target="tpu_custom_call" | custom-call | flops 3145728 | bytes 6291456 | tf_op jit(solution)/shard_map/normed_rows/pallas_call | solution.py:504
  69.7 5.9 %finish.1 = (bf16[512,16,128]{2,1,0:T(8,128)(2,1)}, bf16[512,16,128]{2,1,0:T(8,128)(2,1)}) custom-call(f32[8,128]{1,0:T(8,128)S(1)} %broadcast_in_dim.2.place_ref, f32[2,16,128]{2,1,0:T(8,128)S(1)} %get-tuple-element.84.ends_ref, f32[8,128,128]{2,1,0:T(8,128)S(1)} %get-tuple-element.109.keep_ref, f32[8,128,128]{2,1,0:T(8,128)S(1)} %collective-permute-done.10.recv_ref, ...), custom_call_target="tpu_custom_call" | custom-call | flops 1073741824 | bytes 16777216 | tf_op jit(solution)/shard_map/finish/pallas_call | solution.py:637
  (17 shorter events, 0.5 us)
Async XLA Ops:
  0.8 12.4 %copy-start = (f32[16,512]{1,0:T(8,128)S(1)}, f32[16,512]{1,0:T(8,128)}, u32[]{:S(2)}) copy-start(f32[16,512]{1,0:T(8,128)} %ld_ref.6) | copy-start | bytes 98308
  6.6 2.1 %collective-permute-start = (f32[8,136,128]{2,1,0:T(8,128)S(1)}, f32[8,136,128]{2,1,0:T(8,128)S(1)}, u32[]{:S(2)}, u32[]{:S(2)}) collective-permute-start(f32[8,136,128]{2,1,0:T(8,128)S(1)} %get-tuple-element.60), channel_id=1, source_target_pairs={{0,4},{4,0},{8,12},{12,8},{16,20},{20,16},{24,28},{28,24},{1,5},{5... | collective-permute-start | bytes 1671176 | tf_op jit(solution)/shard_map/ppermute | solution.py:658
  8.8 12.0 %collective-permute-start.1 = (f32[8,136,128]{2,1,0:T(8,128)S(1)}, f32[8,136,128]{2,1,0:T(8,128)S(1)}, u32[]{:S(2)}, u32[]{:S(2)}) collective-permute-start(f32[8,136,128]{2,1,0:T(8,128)S(1)} %get-tuple-element.62.refs_2_), channel_id=1, source_target_pairs={{0,8},{4,20},{8,0},{12,28},{16,24},{20,4},{24,16},{28,12},{1,9},{5... | collective-permute-start | bytes 1671176 | tf_op jit(solution)/shard_map/ppermute | solution.py:658
  11.7 9.1 %collective-permute-start.2 = (f32[8,128]{1,0:T(8,128)S(1)}, f32[8,128]{1,0:T(8,128)S(1)}, u32[]{:S(2)}, u32[]{:S(2)}) collective-permute-start(f32[8,128]{1,0:T(8,128)S(1)} %get-tuple-element.61.refs_0_.refs_2_), channel_id=1, source_target_pairs={{0,24},{4,28},{8,16},{12,20},{16,8},{20,12},{24,0},{28,4},{1,25},{... | collective-permute-start | bytes 12296 | tf_op jit(solution)/shard_map/ppermute | solution.py:658
  20.9 9.6 %collective-permute-start.3 = (f32[8,136,128]{2,1,0:T(8,128)S(1)}, f32[8,136,128]{2,1,0:T(8,128)S(1)}, u32[]{:S(2)}, u32[]{:S(2)}) collective-permute-start(f32[8,136,128]{2,1,0:T(8,128)S(1)} %earlier_next.1), channel_id=1, source_target_pairs={{0,16},{4,12},{8,24},{12,4},{16,0},{20,28},{24,8},{28,20},{1,17},{... | collective-permute-start | bytes 1671176 | tf_op jit(solution)/shard_map/ppermute | solution.py:658
  27.1 5.6 %copy-start.1 = (f32[16,128]{1,0:T(8,128)S(1)}, f32[16,128]{1,0:T(8,128)}, u32[]{:S(2)}) copy-start(f32[16,128]{1,0:T(8,128)} %gain_ref.4) | copy-start | bytes 24580
  30.7 2.0 %collective-permute-start.4 = (f32[8,128,128]{2,1,0:T(8,128)S(1)}, f32[8,128,128]{2,1,0:T(8,128)S(1)}, u32[]{:S(2)}, u32[]{:S(2)}) collective-permute-start(f32[8,128,128]{2,1,0:T(8,128)S(1)} %get-tuple-element.76), channel_id=1, source_target_pairs={{0,4},{4,0},{8,12},{12,8},{16,20},{20,16},{24,28},{28,24},{1,5},{5... | collective-permute-start | bytes 1572872 | tf_op jit(solution)/shard_map/ppermute | solution.py:658
  35.3 3.6 %collective-permute-start.5 = (f32[2,512]{1,0:T(2,128)S(1)}, f32[2,512]{1,0:T(2,128)S(1)}, u32[]{:S(2)}, u32[]{:S(2)}) collective-permute-start(f32[2,512]{1,0:T(2,128)S(1)} %get-tuple-element.82.first_ref), channel_id=1, source_target_pairs={{0,1},{1,0},{2,3},{3,2},{4,5},{5,4},{6,7},{7,6},{8,9},{9,8},{10,11... | collective-permute-start | bytes 12296 | tf_op jit(solution)/shard_map/ppermute | solution.py:658
  39.0 4.6 %collective-permute-start.6 = (f32[2,512]{1,0:T(2,128)S(1)}, f32[2,512]{1,0:T(2,128)S(1)}, u32[]{:S(2)}, u32[]{:S(2)}) collective-permute-start(f32[2,512]{1,0:T(2,128)S(1)} %add.15.first_ref), channel_id=1, source_target_pairs={{0,2},{1,3},{2,0},{3,1},{4,6},{5,7},{6,4},{7,5},{8,10},{9,11},{10,... | collective-permute-start | bytes 12296 | tf_op jit(solution)/shard_map/ppermute | solution.py:658
  46.2 2.0 %collective-permute-start.7 = (f32[8,128,128]{2,1,0:T(8,128)S(1)}, f32[8,128,128]{2,1,0:T(8,128)S(1)}, u32[]{:S(2)}, u32[]{:S(2)}) collective-permute-start(f32[8,128,128]{2,1,0:T(8,128)S(1)} %get-tuple-element.92), channel_id=1, source_target_pairs={{0,4},{4,0},{8,12},{12,8},{16,20},{20,16},{24,28},{28,24},{1,5},{5... | collective-permute-start | bytes 1572872 | tf_op jit(solution)/shard_map/ppermute | solution.py:658
  48.3 9.2 %collective-permute-start.8 = (f32[8,128,128]{2,1,0:T(8,128)S(1)}, f32[8,128,128]{2,1,0:T(8,128)S(1)}, u32[]{:S(2)}, u32[]{:S(2)}) collective-permute-start(f32[8,128,128]{2,1,0:T(8,128)S(1)} %later_total.1.refs_1_), channel_id=1, source_target_pairs={{0,8},{4,20},{8,0},{12,28},{16,24},{20,4},{24,16},{28,12},{1,9},{5... | collective-permute-start | bytes 1572872 | tf_op jit(solution)/shard_map/ppermute | solution.py:658
  57.6 9.2 %collective-permute-start.9 = (f32[8,128,128]{2,1,0:T(8,128)S(1)}, f32[8,128,128]{2,1,0:T(8,128)S(1)}, u32[]{:S(2)}, u32[]{:S(2)}) collective-permute-start(f32[8,128,128]{2,1,0:T(8,128)S(1)} %later_next.1), channel_id=1, source_target_pairs={{0,16},{4,12},{8,24},{12,4},{16,0},{20,28},{24,8},{28,20},{1,17},{... | collective-permute-start | bytes 1572872 | tf_op jit(solution)/shard_map/ppermute | solution.py:658
  67.0 2.7 %collective-permute-start.10 = (f32[8,128,128]{2,1,0:T(8,128)S(1)}, f32[8,128,128]{2,1,0:T(8,128)S(1)}, u32[]{:S(2)}, u32[]{:S(2)}) collective-permute-start(f32[8,128,128]{2,1,0:T(8,128)S(1)} %get-tuple-element.107), channel_id=1, source_target_pairs={{0,4},{4,0},{8,12},{12,8},{16,20},{20,16},{24,28},{28,24},{1,5},{5... | collective-permute-start | bytes 1572872 | tf_op jit(solution)/shard_map/ppermute | solution.py:658

commit v9 on v7

v9 whole, which is shorter than its diff:
```python
import functools

import jax
import jax.numpy as jnp
from jax import lax
from jax.experimental import pallas as pl
from jax.experimental.pallas import tpu as pltpu
from jax.sharding import PartitionSpec as P

HEAD_TOTAL = 64
HD = 128
BLOCK = 256
CHUNK = 128
TILE = 8
F32 = jnp.float32
BF16 = jnp.bfloat16
MIB = 1024 * 1024
NEAR = pl.BlockSpec(memory_space=pltpu.VMEM)
FAR = pl.BlockSpec(memory_space=pl.ANY)
LOWER, UPPER, LATE, RIGHT, LOW = range(5)


def in_vmem(*shape, kind=F32):
    return pltpu.VMEM(shape, kind)


def near(*arrays):
    return [pltpu.with_memory_space_constraint(array, pltpu.VMEM) for array in arrays]


def far(*arrays):
    return [pltpu.with_memory_space_constraint(array, pltpu.HBM) for array in arrays]


def params(mib):
    return pltpu.CompilerParams(vmem_limit_bytes=mib * MIB)


def cost(flops, moved, exps=0):
    return pl.CostEstimate(flops=flops, bytes_accessed=moved, transcendentals=exps)


def block_cum(log_decay):
    size = log_decay.shape[1]
    upper = lax.broadcasted_iota(jnp.int32, (size, size), 0) <= lax.broadcasted_iota(
        jnp.int32, (size, size), 1
    )
    return jnp.dot(
        log_decay,
        jnp.where(upper, 1.0, 0.0).astype(F32),
        precision=lax.Precision.HIGHEST,
        preferred_element_type=F32,
    )


def as_columns(row):
    return jnp.broadcast_to(row, (HD, row.shape[1])).T


def dot(a, b):
    return jnp.dot(a, b, preferred_element_type=F32)


def dot_rows(a, b):
    return lax.dot_general(a, b, (((1,), (1,)), ((), ())), preferred_element_type=F32)


def two_parts(matrix):
    high = matrix.astype(BF16)
    return high, (matrix - high.astype(F32)).astype(BF16)


def times_state(rows, state):
    return dot(jnp.concatenate([rows, rows], axis=1), jnp.concatenate(two_parts(state), axis=0))


def times_state_t(rows, state):
    return dot_rows(
        jnp.concatenate([rows, rows], axis=1), jnp.concatenate(two_parts(state), axis=1)
    )


def decay_quarters(row, columns):
    half = row.shape[1] // 2
    lower = lax.broadcasted_iota(jnp.int32, (half, half), 0) >= lax.broadcasted_iota(
        jnp.int32, (half, half), 1
    )
    quarters = []
    for t, s in ((0, 0), (1, 0), (1, 1)):
        gap = columns[t * half : (t + 1) * half] - row[:, s * half : (s + 1) * half]
        quarters.append(jnp.exp(jnp.where(lower, gap, -jnp.inf) if t == s else gap))
    return quarters


def causal(table, quarters):
    half = table.shape[0] // 2
    first, second, third = (
        (table[t * half : (t + 1) * half, s * half : (s + 1) * half] * quarter).astype(BF16)
        for (t, s), quarter in zip(((0, 0), (1, 0), (1, 1)), quarters)
    )
    top = jnp.concatenate([first, jnp.zeros_like(first)], axis=1)
    return jnp.concatenate([top, jnp.concatenate([second, third], axis=1)], axis=0)


def transposed_dot(a, b):
    return lax.dot_general(a, b, (((0,), (0,)), ((), ())), preferred_element_type=F32)


def each_head(heads, unroll, body):
    def step(h, carry):
        body(h)
        return carry

    lax.fori_loop(0, heads, step, 0, unroll=unroll)


def each_half(half, unroll, body):
    for part in range(2):
        each_head(half, unroll, lambda i, part=part: body(part, i, part * half + i))


def turn_tiles(tiles):
    count = len(tiles)
    at = lax.broadcasted_iota(jnp.int32, tiles[0].shape, 0)
    turned = [tile if i == 0 else pltpu.roll(tile, i, 0) for i, tile in enumerate(tiles)]
    reach = 1
    while reach < count:
        odd = (at & reach) != 0
        turned = [
            jnp.where(odd, turned[(n + reach) % count], turned[n]) for n in range(count)
        ]
        reach *= 2
    picked = [turned[-j % count] for j in range(count)]
    return [tile if j == 0 else pltpu.roll(tile, count - j, 0) for j, tile in enumerate(picked)]


def is_upper(place_ref):
    return jnp.max(place_ref[UPPER : UPPER + 1]) > 0.5


def to_heads(dst, block, upper):
    tok, heads, _ = block.shape

    def step(group, carry):
        at = pl.multiple_of(group * 2 * TILE, 2 * TILE)
        tokens = block[pl.ds(at, 2 * TILE)].astype(F32)
        for first in range(0, heads, TILE):
            halves = [
                turn_tiles([tokens[base + i, first : first + TILE] for i in range(TILE)])
                for base in (0, TILE)
            ]
            local = jnp.where(upper, heads - TILE - first, first)
            for j in range(TILE):
                both = jnp.concatenate([halves[0][j], halves[1][j]], axis=0)
                dst[local + j, pl.ds(at, 2 * TILE)] = both.astype(BF16)
        return carry

    lax.fori_loop(0, tok // (2 * TILE), step, 0, unroll=2)


def from_heads(block, src, start, tok, upper):
    heads = src.shape[0]

    def step(group, carry):
        at = pl.multiple_of(group * TILE, TILE)
        parts = []
        for first in range(0, heads, TILE):
            local = jnp.where(upper, heads - TILE - first, first)
            parts.append(turn_tiles([src[local + i, pl.ds(start + at, TILE)] for i in range(TILE)]))
        for j in range(TILE):
            block[at + j] = jnp.concatenate([part[j] for part in parts], axis=0).astype(BF16)
        return carry

    lax.fori_loop(0, tok // TILE, step, 0, unroll=2)


def is_set(place_ref, which):
    return place_ref[which : which + 1] > 0.5


def in_local_order(place_ref, rows):
    half = rows.shape[0] // 2
    lower, upper = rows[:half], rows[half:]
    mine = jnp.broadcast_to(place_ref[LOWER : LOWER + 1, :1], lower.shape) > 0.5
    return jnp.concatenate(
        [jnp.where(mine, lower, upper), jnp.where(mine, upper, lower)], axis=0
    )


def half_states(part, kh, vh, cum, b, out, first=None):
    half = kh.shape[1] // 2

    def one(i):
        h = part * half + i
        row = cum[b, pl.ds(h, 1), :]
        scale = jnp.exp(row[:, BLOCK - 1 :] - row)
        state = dot((kh[b, h].astype(F32).T * scale).astype(BF16), vh[b, h])
        if first is not None:
            state += jnp.exp(row[:, BLOCK - 1 :]) * first[i]
        out[i, :HD] = state

    each_head(half, 4, one)


def add_decays(out, decay, part):
    half = out.shape[0]
    for i in range(half):
        out[i, HD:] = jnp.broadcast_to(decay[part * half + i : part * half + i + 1], (TILE, HD))


def state_kernel(
    place_ref, gain_hbm, ld_hbm, k_hbm, v_hbm, send_ref, first_ref, kh, vh, cum, ld_ref, decay,
    gain_ref, gain_raw, ld_raw, k_raw, v_raw, sems,
):
    heads, tok = ld_ref.shape
    per_block = BLOCK // CHUNK
    copies = [pltpu.make_async_copy(ld_hbm, ld_raw, sems.at[0])]
    for c in range(tok // CHUNK):
        at = pl.ds(c * CHUNK, CHUNK)
        copies.append(pltpu.make_async_copy(k_hbm.at[at], k_raw.at[at], sems.at[2 * c + 1]))
        copies.append(pltpu.make_async_copy(v_hbm.at[at], v_raw.at[at], sems.at[2 * c + 2]))
    copies.append(pltpu.make_async_copy(gain_hbm, gain_raw, sems.at[len(copies)]))
    for copy in copies:
        copy.start()
    upper = is_upper(place_ref)
    copies[0].wait()
    ld_ref[...] = in_local_order(place_ref, ld_raw[...])
    for b in range(2):
        cum[b] = block_cum(ld_ref[:, b * BLOCK : (b + 1) * BLOCK])
    ends = cum[0, :, BLOCK - 1 :] + cum[1, :, BLOCK - 1 :]
    decay[...] = jnp.broadcast_to(jnp.exp(ends), decay.shape)

    for b in range(2):
        for c in range(per_block):
            at = pl.ds((b * per_block + c) * CHUNK, CHUNK)
            here = pl.ds(c * CHUNK, CHUNK)
            which = 2 * (b * per_block + c) + 1
            copies[which].wait()
            to_heads(kh.at[b, :, here], k_raw.at[at], upper)
            copies[which + 1].wait()
            to_heads(vh.at[b, :, here], v_raw.at[at], upper)
        if b == 0:
            half_states(1, kh, vh, cum, 0, first_ref)
        else:
            half_states(1, kh, vh, cum, 1, send_ref, first_ref)
    add_decays(send_ref, decay, 1)
    copies[-1].wait()
    gain_ref[...] = in_local_order(place_ref, gain_raw[...])


def state_to_send(place, gain, log_decay, key_rows, value_rows):
    tok, heads, dim = key_rows.shape
    half = heads // 2
    by_head = in_vmem(2, heads, BLOCK, dim, kind=BF16)
    return pl.pallas_call(
        state_kernel,
        in_specs=[NEAR, FAR, FAR, FAR, FAR],
        out_specs=[NEAR] * 8,
        out_shape=[
            in_vmem(half, dim + TILE, dim), in_vmem(half, dim, dim), by_head, by_head,
            in_vmem(2, heads, BLOCK), in_vmem(heads, tok), in_vmem(heads, dim), in_vmem(heads, dim),
        ],
        scratch_shapes=[
            pltpu.VMEM((heads, dim), F32),
            pltpu.VMEM((heads, tok), F32),
            pltpu.VMEM((tok, heads, dim), BF16),
            pltpu.VMEM((tok, heads, dim), BF16),
            pltpu.SemaphoreType.DMA((2 * (tok // CHUNK) + 2,)),
        ],
        compiler_params=params(8),
        cost_estimate=cost(tok * heads * dim * dim, 8 * tok * heads * dim),
        name="state_to_send",
    )(place, *far(gain, log_decay, key_rows, value_rows))


def own_state_kernel(kh, vh, cum, decay, own_ref, first_ref):
    half_states(0, kh, vh, cum, 0, first_ref)
    half_states(0, kh, vh, cum, 1, own_ref, first_ref)
    add_decays(own_ref, decay, 0)


def own_state(kh, vh, cum, decay):
    _, heads, tok, dim = kh.shape
    half = heads // 2
    return pl.pallas_call(
        own_state_kernel,
        in_specs=[NEAR] * 4,
        out_specs=[NEAR] * 2,
        out_shape=[in_vmem(half, dim + TILE, dim), in_vmem(half, dim, dim)],
        compiler_params=params(4),
        cost_estimate=cost(2 * tok * heads * dim * dim, 4 * tok * heads * dim),
        name="own_state",
    )(*near(kh, vh, cum, decay))


def intra(index, place, cum, kh, vh, first_own, first_send, query_rows, output_grad):
    tok, heads, dim = query_rows.shape

    def kernel(place_ref, cum, kh, vh, first_own, first_send, q_hbm, o_hbm,
               qh, oh, w_ref, decays_ref, columns_ref, inner_ref,
               q_raw, o_raw, sems):
        at = pl.ds(index * BLOCK, BLOCK)
        copy_q = pltpu.make_async_copy(q_hbm.at[at], q_raw, sems.at[0])
        copy_o = pltpu.make_async_copy(o_hbm.at[at], o_raw, sems.at[1])
        copy_q.start()
        copy_o.start()
        upper = is_upper(place_ref)
        copy_q.wait()
        to_heads(qh, q_raw, upper)
        copy_o.wait()
        to_heads(oh, o_raw, upper)

        def one(part, i, h):
            query = qh[h]
            row = cum[index, pl.ds(h, 1), :]
            columns = as_columns(row)
            quarters = decay_quarters(row, columns)
            for at, quarter in enumerate(quarters):
                decays_ref[h, at] = quarter
            weights = causal(dot_rows(query, kh[index, h]), quarters)
            w_ref[h] = weights
            inner = dot(weights, vh[index, h])
            columns = jnp.exp(columns)
            columns_ref[h] = columns
            if index:
                inner += columns * times_state(query, (first_own, first_send)[part][i])
            inner_ref[h] = inner

        each_half(heads // 2, 2, one)

    by_head = in_vmem(heads, BLOCK, dim, kind=BF16)
    return pl.pallas_call(
        kernel,
        in_specs=[NEAR] * 6 + [FAR, FAR],
        out_specs=[NEAR] * 6,
        out_shape=[
            by_head, by_head, in_vmem(heads, BLOCK, BLOCK, kind=BF16),
            in_vmem(heads, 3, BLOCK // 2, BLOCK // 2), in_vmem(heads, BLOCK, dim),
            in_vmem(heads, BLOCK, dim),
        ],
        scratch_shapes=[
            pltpu.VMEM((BLOCK, heads, dim), BF16),
            pltpu.VMEM((BLOCK, heads, dim), BF16),
            pltpu.SemaphoreType.DMA((2,)),
        ],
        compiler_params=params(6),
        cost_estimate=cost(
            2 * heads * BLOCK * BLOCK * dim * 4, 20 * heads * BLOCK * dim, heads * BLOCK * BLOCK
        ),
        name=f"intra_{index}",
    )(place, *near(cum, kh, vh, first_own, first_send), *far(query_rows, output_grad))


def attend_kernel(part, *refs):
    gain_ref, state_ref, q0, q1, o0, o1, columns0, columns1, inner0, inner1 = refs[:10]
    half = state_ref.shape[0]
    if part:
        before, att0, att1, sums_ref, partial = refs[10:]
        partial[...] = before[...]
    else:
        att0, att1, partial = refs[10:]
        partial[...] = jnp.zeros_like(partial)

    def one(i):
        h = part * half + i
        state = state_ref[i]
        gain = gain_ref[pl.ds(h, 1), :]
        blocks = ((q0, o0, columns0, inner0, att0), (q1, o1, columns1, inner1, att1))
        for b, (q, o, columns, inner, att) in enumerate(blocks):
            attended = inner[h] + columns[h] * times_state(q[h], state)
            att[i] = attended
            partial[0, b] += attended * attended
            partial[1, b] += gain * o[h].astype(F32) * attended
            state = columns[h, BLOCK - 1 :] * state

    each_head(half, 4, one)
    if part:
        ones = jnp.ones((8, HD), F32)
        for b in range(2):
            for at in range(2):
                line = lax.dot_general(
                    ones, partial[at, b], (((1,), (1,)), ((), ())),
                    precision=lax.Precision.HIGHEST, preferred_element_type=F32,
                )
                sums_ref[at : at + 1, b * BLOCK : (b + 1) * BLOCK] = line[:1]


def attend(part, gain, state, arrays, before=()):
    heads, dim = gain.shape
    tok = 2 * BLOCK
    half = heads // 2
    by_head = in_vmem(half, BLOCK, dim)
    partial = (2, 2, BLOCK, dim)
    return pl.pallas_call(
        functools.partial(attend_kernel, part),
        in_specs=[NEAR] * (10 + part),
        out_specs=[NEAR] * 3,
        out_shape=[by_head, by_head, in_vmem(2, tok) if part else in_vmem(*partial)],
        scratch_shapes=[pltpu.VMEM(partial, F32)] * part,
        compiler_params=params(6),
        cost_estimate=cost(2 * heads * tok * dim * dim, 8 * heads * tok * dim),
        name=f"attend_{part}",
    )(*near(gain, state, *arrays, *before))


def scaled_queries(cum, q0, q1):
    _, heads, _ = cum.shape

    def kernel(cum_ref, q0, q1, out_ref, ends_ref):
        for b in range(2):
            ends_ref[b] = jnp.broadcast_to(jnp.exp(cum_ref[b, :, BLOCK - 1 :]), (heads, HD))

        def one(h):
            for b, q in enumerate((q0, q1)):
                scale = jnp.exp(cum_ref[b, pl.ds(h, 1), :])
                out_ref[b, h] = (q[h].astype(F32).T * scale).astype(BF16)

        each_head(heads, 2, one)

    return pl.pallas_call(
        kernel,
        in_specs=[NEAR] * 3,
        out_specs=[NEAR] * 2,
        out_shape=[in_vmem(2, heads, HD, BLOCK, kind=BF16), in_vmem(2, heads, HD)],
        compiler_params=params(4),
        cost_estimate=cost(4 * heads * BLOCK * HD, 8 * heads * BLOCK * HD),
        name="scaled_queries",
    )(*near(cum, q0, q1))


def remaining_decay(cum):
    _, heads, _ = cum.shape

    def kernel(cum_ref, out_ref):
        def one(h):
            for b in range(2):
                row = cum_ref[b, pl.ds(h, 1), :]
                out_ref[b, h] = as_columns(jnp.exp(row[:, BLOCK - 1 :] - row))

        each_head(heads, 2, one)

    return pl.pallas_call(
        kernel,
        in_specs=[NEAR],
        out_specs=NEAR,
        out_shape=in_vmem(2, heads, BLOCK, HD),
        compiler_params=params(4),
        cost_estimate=cost(2 * heads * BLOCK * HD, 8 * heads * BLOCK * HD),
        name="remaining_decay",
    )(*near(cum))


def inverse_rms(sums_ref, b):
    at = slice(b * BLOCK, (b + 1) * BLOCK)
    inv = lax.rsqrt(sums_ref[0:1, at] / (HEAD_TOTAL * HD) + 1e-06)
    mean = sums_ref[1:2, at] * inv / (HEAD_TOTAL * HD)
    return inv, mean


def norm_grad(part, ends, gain, sums, scaled, arrays):
    heads, dim = gain.shape
    tok = 2 * BLOCK
    half = heads // 2

    def kernel(ends_ref, gain_ref, sums_ref, queries_ref, o0, o1, att0, att1,
               out_ref, second_ref, g0, g1, scales):
        for b in range(2):
            inv, mean = inverse_rms(sums_ref, b)
            scales[b, 0] = as_columns(inv)
            scales[b, 1] = as_columns(inv * inv * mean)

        def one(i):
            h = part * half + i
            line = gain_ref[pl.ds(h, 1), :]
            starts = []
            for b, (o, att, g) in enumerate(((o0, att0, g0), (o1, att1, g1))):
                grad = line * o[h].astype(F32) * scales[b, 0] - att[i] * scales[b, 1]
                grad = grad.astype(BF16)
                g[i] = grad
                starts.append(dot(queries_ref[b, h], grad))
            second_ref[i] = starts[1]
            out_ref[i] = starts[0] + ends_ref[0, pl.ds(h, 1)] * starts[1]

        each_head(half, 4, one)

    by_head = in_vmem(half, BLOCK, dim, kind=BF16)
    return pl.pallas_call(
        kernel,
        in_specs=[NEAR] * 8,
        out_specs=[NEAR] * 4,
        out_shape=[in_vmem(half, dim, dim), in_vmem(half, dim, dim), by_head, by_head],
        scratch_shapes=[pltpu.VMEM((2, 2, BLOCK, dim), F32)],
        compiler_params=params(4),
        cost_estimate=cost(heads * tok * dim * dim, 7 * heads * tok * dim),
        name=f"norm_grad_{part}",
    )(*near(ends, gain, sums, scaled, *arrays))


def on_block(work):
    for index in range(2):
        pl.when(pl.program_id(0) == index)(lambda index=index: work(index))


def raw_output(heads, tok):
    spec = pl.BlockSpec((BLOCK, heads, HD), lambda i: (i, 0, 0))
    return spec, jax.ShapeDtypeStruct((tok, heads, HD), BF16)


def normed_kernel(place_ref, gain_ref, sums_ref, own0, own1, other0, other1, out_ref, rows):
    upper = is_upper(place_ref)

    def work(b):
        inv = as_columns(inverse_rms(sums_ref, b)[0])
        halves = ((own0, other0), (own1, other1))[b]

        def one(part, i, h):
            rows[h] = halves[part][i] * inv * gain_ref[pl.ds(h, 1), :]

        each_half(own0.shape[0], 4, one)

    on_block(work)
    from_heads(out_ref, rows, 0, BLOCK, upper)


def normed_rows(place, gain, sums, arrays):
    heads, dim = gain.shape
    tok = 2 * BLOCK
    spec, shape = raw_output(heads, tok)
    return pl.pallas_call(
        normed_kernel,
        grid=(2,),
        in_specs=[NEAR] * 7,
        out_specs=spec,
        out_shape=shape,
        scratch_shapes=[pltpu.VMEM((heads, BLOCK, dim), F32)],
        compiler_params=params(7),
        cost_estimate=cost(3 * heads * tok * dim, 6 * heads * tok * dim),
        name="normed_rows",
    )(place, *near(gain, sums, *arrays))


def grad_q_kernel(
    ends_ref, keep_ref, recv_ref, first_own, first_send, kh, vh, own0, own1, other0, other1,
    decays0, decays1, columns0, columns1, rows, gs_ref,
):
    blocks = (((own0, other0), decays0, columns0), ((own1, other1), decays1, columns1))
    for b, (g, decays, columns) in enumerate(blocks):

        def one(part, i, h, b=b, g=g, decays=decays, columns=columns):
            grad = g[part][i]
            scores = causal(dot_rows(grad, vh[b, h]), [decays[h, at] for at in range(3)])
            gs_ref[b, h] = scores
            state = (keep_ref, recv_ref)[part][i]
            if b:
                state = ends_ref[0, pl.ds(h, 1)] * state + (first_own, first_send)[part][i]
            rows[b, h] = dot(scores, kh[b, h]) + columns[h] * times_state_t(grad, state)

        each_half(keep_ref.shape[0], 4, one)


def grad_query(ends, arrays):
    _, heads, dim = ends.shape
    tok = 2 * BLOCK
    return pl.pallas_call(
        grad_q_kernel,
        in_specs=[NEAR] * 15,
        out_specs=[NEAR, NEAR],
        out_shape=[
            in_vmem(2, heads, BLOCK, dim), in_vmem(2, heads, BLOCK, BLOCK, kind=BF16),
        ],
        compiler_params=params(4),
        cost_estimate=cost(
            4 * heads * tok * dim * (BLOCK + dim), 12 * heads * tok * dim, heads * tok * BLOCK
        ),
        name="grad_query",
    )(*near(ends, *arrays))


def grad_kv_kernel(
    place_ref, gs_ref, w0, w1, q0, q1, kh, vh, own0, own1, other0, other1, remaining_ref,
    second_own, second_send, rows, dk, dv, out_q, raw, sems,
):
    upper = is_upper(place_ref)
    copies = []
    for b in range(2):
        for start in range(0, BLOCK, CHUNK):
            at = pl.ds(b * BLOCK + start, CHUNK)
            from_heads(raw.at[at], rows.at[b], start, CHUNK, upper)
            copies.append(pltpu.make_async_copy(raw.at[at], out_q.at[at], sems.at[len(copies)]))
            copies[-1].start()

    def one(part, i, h):
        columns = remaining_ref[0, h]
        state = (second_own, second_send)[part][i]
        g0, g1 = ((own0, own1), (other0, other1))[part]
        dk[0, h] = transposed_dot(gs_ref[0, h], q0[h]) + columns * times_state_t(vh[0, h], state)
        dv[0, h] = transposed_dot(w0[h], g0[i]) + columns * times_state(kh[0, h], state)
        dk[1, h] = transposed_dot(gs_ref[1, h], q1[h])
        dv[1, h] = transposed_dot(w1[h], g1[i])

    each_half(second_own.shape[0], 2, one)
    for copy in copies:
        copy.wait()


def grad_key_value(*arrays):
    _, heads, _, dim = arrays[6].shape
    tok = 2 * BLOCK
    return pl.pallas_call(
        grad_kv_kernel,
        in_specs=[NEAR] * 16,
        out_specs=[NEAR, NEAR, FAR],
        out_shape=[in_vmem(2, heads, BLOCK, dim)] * 2
        + [jax.ShapeDtypeStruct((tok, heads, dim), BF16)],
        scratch_shapes=[
            pltpu.VMEM((tok, heads, dim), BF16),
            pltpu.SemaphoreType.DMA((tok // CHUNK,)),
        ],
        compiler_params=params(6),
        cost_estimate=cost(4 * heads * tok * dim * (BLOCK + dim), 30 * heads * tok * dim),
        name="grad_key_value",
    )(*near(*arrays))


def finish_rows(part, b, ends_ref, state_ref, kh, vh, remaining_ref, dk, dv, rows_k, rows_v):
    half = state_ref.shape[0]

    def one(i):
        h = part * half + i
        columns = remaining_ref[b, h]
        state = state_ref[i]
        if b == 0:
            state = ends_ref[1, pl.ds(h, 1)] * state
        state = state.astype(BF16)
        none = jnp.zeros_like(state)
        both = jnp.concatenate(
            [jnp.concatenate([state.T, none], axis=1), jnp.concatenate([none, state], axis=1)],
            axis=0,
        )
        carried = dot(jnp.concatenate([vh[b, h], kh[b, h]], axis=1), both)
        rows_k[b, h] = dk[b, h] + columns * carried[:, :HD]
        rows_v[b, h] = dv[b, h] + columns * carried[:, HD:]

    each_head(half, 4, one)


def finish_own_kernel(*refs):
    for b in range(2):
        finish_rows(0, b, *refs)


def finish_other_kernel(
    place_ref, old_k, old_v, ends_ref, state_ref, kh, vh, remaining_ref, dk, dv,
    out_k, out_v, rows_k, rows_v, raw_k, raw_v, sems,
):
    upper = is_upper(place_ref)
    copies = []
    for b in range(2):
        finish_rows(1, b, ends_ref, state_ref, kh, vh, remaining_ref, dk, dv, rows_k, rows_v)
        for start in range(0, BLOCK, CHUNK):
            at = pl.ds(b * BLOCK + start, CHUNK)
            for rows, raw, out in ((rows_k, raw_k, out_k), (rows_v, raw_v, out_v)):
                from_heads(raw.at[at], rows.at[b], start, CHUNK, upper)
                copies.append(pltpu.make_async_copy(raw.at[at], out.at[at], sems.at[len(copies)]))
                copies[-1].start()
    for copy in copies:
        copy.wait()


def finish_own(ends, keep, arrays):
    _, heads, dim = ends.shape
    tok = 2 * BLOCK
    return pl.pallas_call(
        finish_own_kernel,
        in_specs=[NEAR] * 7,
        out_specs=[NEAR, NEAR],
        out_shape=[in_vmem(2, heads, BLOCK, dim)] * 2,
        compiler_params=params(4),
        cost_estimate=cost(4 * heads * tok * dim * dim, 8 * heads * tok * dim),
        name="finish_own",
    )(*near(ends, keep, *arrays))


def finish_other(place, rows, ends, recv, arrays):
    _, heads, dim = ends.shape
    tok = 2 * BLOCK
    shape = jax.ShapeDtypeStruct((tok, heads, dim), BF16)
    return pl.pallas_call(
        finish_other_kernel,
        in_specs=[NEAR] * 10,
        out_specs=[FAR, FAR, NEAR, NEAR],
        out_shape=[shape, shape] + [in_vmem(2, heads, BLOCK, dim)] * 2,
        input_output_aliases={1: 2, 2: 3},
        scratch_shapes=[
            pltpu.VMEM((tok, heads, dim), BF16),
            pltpu.VMEM((tok, heads, dim), BF16),
            pltpu.SemaphoreType.DMA((2 * (tok // CHUNK),)),
        ],
        compiler_params=params(8),
        cost_estimate=cost(4 * heads * tok * dim * dim, 8 * heads * tok * dim),
        name="finish_other",
    )(*near(place, *rows, ends, recv, *arrays))[:2]


def follows(value, earlier):
    return lax.optimization_barrier((value, earlier))[0]


def swap(value, axis, bit):
    count = lax.axis_size(axis)
    return lax.ppermute(value, axis, [(i, i ^ bit) for i in range(count)])


def mix(body, backward, place, arrays, shapes, name):
    def kernel(place_ref, *refs):
        bits = [is_set(place_ref, which) != backward for which in (LATE, RIGHT, LOW)]
        body(bits, refs[: len(arrays)], refs[len(arrays) :])

    return pl.pallas_call(
        kernel,
        in_specs=[NEAR] + [NEAR] * len(arrays),
        out_specs=[NEAR] * len(shapes),
        out_shape=[in_vmem(*shape) for shape in shapes],
        compiler_params=params(4),
        cost_estimate=cost(4 * 8 * HD * HD, 16 * 8 * HD * HD),
        name=name,
    )(place, *near(*arrays))


OWN, PARTNER, CHIP, ROW, CORNER = range(5)


def mix_total(bits, own, got, d_own, d_got, first, second):
    late = bits[0]
    quarter = first.shape[0]
    for h in range(2 * quarter):
        total = jnp.where(late, 1.0, d_got(h)) * own[h, :HD] + jnp.where(late, d_own(h), 1.0) * got[h, :HD]
        if h < quarter:
            first[h, :HD] = total
        else:
            second[h - quarter] = total


def mix_total_first(bits, arrays, outputs):
    own, got = arrays
    first, second, chip = outputs
    quarter = first.shape[0]
    d_own = lambda h: own[h, HD : HD + 1]
    d_got = lambda h: got[h, HD : HD + 1]
    mix_total(bits, own, got, d_own, d_got, first, second)
    for h in range(2 * quarter):
        whole = d_own(h) * d_got(h)
        chip[h : h + 1] = whole
        place = HD + (TILE // 2) * (h // quarter)
        first[h % quarter, place : place + TILE // 2] = jnp.broadcast_to(whole, (TILE // 2, HD))


def mix_total_again(bits, arrays, outputs):
    table, own, got = arrays
    decay = lambda which: lambda h: table[which, h : h + 1]
    mix_total(bits, own, got, decay(OWN), decay(PARTNER), *outputs)


def mix_next(bits, decay, totals, gots, outputs):
    _, right, low = bits
    quarter = totals[1].shape[0]
    for i in range(quarter):
        h = i
        scale_total = jnp.where(right, 1.0, decay(ROW, h))
        scale_got = jnp.where(right, decay(CHIP, h), 1.0)
        outputs[0][i] = scale_total * totals[0][i, :HD] + scale_got * gots[0][i, :HD]
        h = quarter + i
        scale_total = jnp.where(low & right, 0.0, 1.0)
        corner = jnp.where(right, 1.0, decay(CHIP, h) * decay(CORNER, h))
        scale_got = jnp.where(low, corner, 0.0)
        outputs[1][i] = scale_total * totals[1][i] + scale_got * gots[1][i]


def mix_next_first(bits, arrays, outputs):
    own, got, chip, corner, first, second, one_a, one_b = arrays
    table = outputs[2]
    quarter = second.shape[0]
    for h in range(2 * quarter):
        place = HD + (TILE // 2) * (h // quarter)
        table[OWN, h : h + 1] = own[h, HD : HD + 1]
        table[PARTNER, h : h + 1] = got[h, HD : HD + 1]
        table[ROW, h : h + 1] = one_a[h % quarter, place : place + 1]
    table[CHIP] = chip[...]
    table[CORNER] = corner[...]
    decay = lambda which, h: table[which, h : h + 1]
    mix_next(bits, decay, (first, second), (one_a, one_b), outputs[:2])


def mix_next_again(bits, arrays, outputs):
    table, first, second, one_a, one_b = arrays
    decay = lambda which, h: table[which, h : h + 1]
    mix_next(bits, decay, (first, second), (one_a, one_b), outputs)


def mix_enter(bits, arrays, outputs):
    table, own, got, one_a, one_b, two_a, two_b = arrays
    kept, sent = outputs
    late, right, low = bits
    quarter = one_b.shape[0]
    decay = lambda which, h: table[which, h : h + 1]
    for h in range(2 * quarter):
        i = h % quarter
        row = jnp.where(right, decay(ROW, h), 1.0)
        if h < quarter:
            one, two = one_a[i, :HD], two_a[i]
            scale_one = jnp.where(right, 1.0, 0.0)
            scale_two = jnp.where(low, row, 0.0)
        else:
            one, two = one_b[i], two_b[i]
            scale_one = jnp.where(low, jnp.where(right, row, decay(CORNER, h)), 0.0)
            scale_two = jnp.where(low | right, 1.0, 0.0)
        enter = scale_one * one + scale_two * two
        after = jnp.where(late, decay(PARTNER, h), decay(OWN, h)) * enter
        after += jnp.where(late, got[h, :HD], own[h, :HD])
        kept[h] = jnp.where(late, after, enter)
        sent[h] = jnp.where(late, enter, after)


def entering_quad(send, own_task, table, place, backward, tasks):
    def work(stage, after, before=()):
        if stage not in tasks:
            return before
        run, outputs = tasks[stage]
        outputs.extend(run(after))
        return lax.optimization_barrier((before, outputs[-1]))[0]

    name = "later" if backward else "earlier"
    half = send.shape[0]
    quarter = half // 2
    states, wide = (quarter, HD, HD), (quarter, HD + TILE, HD)
    got = swap(send, "seq", 1)
    own = own_task(send)
    if table is None:
        first, second, chip = mix(
            mix_total_first, backward, place, (own, got), (wide, states, (half, HD)), name + "_total"
        )
    else:
        first, second = mix(
            mix_total_again, backward, place, (table, own, got), (states, states), name + "_total"
        )
    one_a, one_b = swap(first, "seq", 2), swap(second, "seq", 4)
    if table is None:
        corner = swap(chip, "seq", 6)
        one_a, one_b, corner = work(1, second, (one_a, one_b, corner))
        next_a, next_b, table = mix(
            mix_next_first, backward, place, (own, got, chip, corner, first, second, one_a, one_b),
            (states, states, (5, half, HD)), name + "_next",
        )
    else:
        one_a, one_b = work(1, second, (one_a, one_b))
        next_a, next_b = mix(
            mix_next_again, backward, place, (table, first, second, one_a, one_b), (states, states),
            name + "_next",
        )
    two_a, two_b = swap(next_a, "seq", 4), swap(next_b, "seq", 2)
    two_a, two_b = work(2, next_b, (two_a, two_b))
    kept, sent = mix(
        mix_enter, backward, place, (table, own, got, one_a, one_b, two_a, two_b),
        ((half, HD, HD), (half, HD, HD)), name + "_enter",
    )
    received = swap(sent, "seq", 1)
    received = follows(received, tasks[3](follows(kept, sent)))
    return kept, received, table


def entering_any(send, own_task, log_total, backward, tasks):
    own = own_task(send)
    for stage in (1, 2):
        run, outputs = tasks[stage]
        outputs.extend(run(send))
    count, mine = lax.axis_size("seq"), lax.axis_index("seq")
    core = mine % 2
    own, send = own[:, :HD], send[:, :HD]
    half = own.shape[0]
    in_order = jnp.where(
        core == 0, jnp.concatenate([own, send], axis=0), jnp.concatenate([send, own], axis=0)
    )
    states = lax.all_gather(in_order, "seq")
    decays = jnp.exp(lax.all_gather(log_total, "seq"))
    place = mine
    if backward:
        states, decays, place = states[::-1], decays[::-1], count - 1 - mine

    def step(at, total):
        longer = decays[at][:, None, None] * total + states[at]
        return jnp.where(at < place, longer, total)

    total = lax.fori_loop(0, count - 1, step, jnp.zeros_like(in_order))
    kept = lax.dynamic_slice_in_dim(total, core * half, half)
    tasks[3](kept)
    return kept, lax.dynamic_slice_in_dim(total, (1 - core) * half, half)


def add(first, second):
    def kernel(first_ref, second_ref, out_ref):
        out_ref[...] = first_ref[...] + second_ref[...]

    return pl.pallas_call(
        kernel,
        in_specs=[NEAR, NEAR],
        out_specs=NEAR,
        out_shape=in_vmem(*first.shape),
        compiler_params=params(2),
        name="add",
    )(*near(first, second))


def sum_over_heads(value, tasks):
    tasks = list(tasks)
    results = []
    count = lax.axis_size("head")
    reach = 1
    while 2 * reach <= count and count % (2 * reach) == 0:
        got = swap(value, "head", reach)
        if tasks:
            results.append(tasks.pop(0)(value))
            got = follows(got, results[-1])
        value = add(value, got)
        reach *= 2
    results += [task(value) for task in tasks]
    part = value
    for shift in range(1, count // reach):
        value = add(
            value,
            lax.ppermute(part, "head", [(i, (i + shift * reach) % count) for i in range(count)]),
        )
    return value, results


def on_device(query_rows, key_rows, value_rows, output_grad, norm_gain, log_decay):
    mine = lax.axis_index("seq")
    bits = [(mine >> at) % 2 for at in range(3)]
    marks = [1 - bits[0], bits[0], *bits] + [jnp.zeros_like(mine)] * (TILE - 5)
    place = jnp.broadcast_to(jnp.stack(marks).astype(F32)[:, None], (TILE, HD))
    table = [None]

    def entering(send, own_task, backward, tasks):
        if lax.axis_size("seq") != 8:
            log_total = jnp.sum(log_decay, axis=1)
            return entering_any(send, own_task, log_total, backward, tasks)
        kept, received, table[0] = entering_quad(
            send, own_task, table[0], place, backward, tasks
        )
        return kept, received

    send, first_send, kh, vh, cum, _, decay, gain = state_to_send(
        place, norm_gain, log_decay, key_rows, value_rows
    )
    firsts, in_0, in_1, begun = [], [], [], []

    def own_task(earlier):
        own, first = own_state(follows(kh, earlier), vh, cum, decay)
        firsts.extend((first, first_send))
        return own

    def forward_task(index):
        return lambda earlier: intra(
            index, place, follows(cum, earlier), kh, vh, *firsts, query_rows, output_grad
        )

    def parts():
        q0, o0, _, _, columns0, inner0 = in_0
        q1, o1, _, _, columns1, inner1 = in_1
        return q0, q1, o0, o1, columns0, columns1, inner0, inner1

    def attend_task(kept):
        begun.extend(attend(0, gain, kept, parts()))
        return begun[-1]

    keep, recv = entering(
        send, own_task, False, {1: (forward_task(0), in_0), 2: (forward_task(1), in_1), 3: attend_task}
    )
    q0, o0, w0, decays0, columns0, _ = in_0
    q1, o1, w1, decays1, columns1, _ = in_1
    own_att = begun[:2]
    *other_att, sums = attend(1, gain, recv, parts(), begun[2:])
    sums, ((scaled, ends), remaining) = sum_over_heads(
        sums,
        (
            lambda earlier: scaled_queries(cum, follows(q0, earlier), q1),
            lambda earlier: remaining_decay(follows(cum, earlier)),
        ),
    )
    grad_send, second_send, *other_g = norm_grad(1, ends, gain, sums, scaled, (o0, o1, *other_att))
    own_g, seconds, queries, pairs, norms, rows = [], [], [], [], [], []

    def own_grad_task(earlier):
        own, second, *grads = norm_grad(
            0, ends, gain, follows(sums, earlier), scaled, (o0, o1, *own_att)
        )
        own_g.extend(grads)
        seconds.extend((second, second_send))
        return own

    def query_task(earlier):
        made = grad_query(
            follows(ends, earlier),
            (keep, recv, *firsts, kh, vh, *own_g, *other_g, decays0, decays1, columns0, columns1),
        )
        norms.append(
            normed_rows(place, gain, follows(sums, made[-1]), (*own_att, *other_att))
        )
        return *made, norms[0]

    def pair_task(earlier):
        return grad_key_value(
            place, queries[1], w0, w1, q0, q1, kh, vh, *own_g, *other_g, remaining,
            follows(seconds[0], earlier), seconds[1], queries[0],
        )

    def finish_task(kept):
        rows.extend(finish_own(ends, kept, (kh, vh, remaining, *pairs[:2])))
        return rows[-1]

    _, grad_recv = entering(
        grad_send, own_grad_task, True,
        {1: (query_task, queries), 2: (pair_task, pairs), 3: finish_task},
    )
    grad_k, grad_v = finish_other(
        place, rows, ends, grad_recv, (kh, vh, remaining, *pairs[:2])
    )
    return norms[0], pairs[2], grad_k, grad_v


def solution(mesh):
    rows = P("seq", "head", None)
    return jax.shard_map(
        on_device,
        mesh=mesh,
        in_specs=(rows, rows, rows, rows, P("head", None), P("head", "seq")),
        out_specs=(rows, rows, rows, rows),
        check_vma=False,
    )
```

time: 73 us -> 70.1 us (0.960)
  waiting for transfers between devices: 8.84 us -> 4.18 us
  starting transfers between devices: 15.8 us -> 16.9 us
    ppermute x15, waiting for transfers between devices: 8.84 us -> 4.18 us  [swap(): return lax.ppermute(value, axis, [(i, i ^ bit) for i in range(count)])]
    ppermute x15, starting transfers between devices: 15.8 us -> 16.9 us  [swap(): return lax.ppermute(value, axis, [(i, i ^ bit) for i in range(count)])]
    pallas_call x11 -> x15, Pallas kernels: 46.5 us -> 47.2 us  [the longest x2 12.2 us: intra(): pl.pallas_call(kernel, in_specs=[NEAR] * 6 + [FAR, FAR], out_specs=[NEAR]...]
  transfers between devices with their start and end apart: 15 -> 15, of which waited for: 10 -> 7; matrix products, arithmetic and copies ran while one was open for 0% -> 0% of each run, Pallas kernels for 41% -> 50%
where the time goes in v9:
time: 70.1 us; the launch traced here: 70 us
  Pallas kernels  47.9 us (68%)
  starting transfers between devices  16.9 us (24%)
  waiting for transfers between devices  4.18 us (6%)
  between operations  0.86 us (1%)
    ppermute x15, starting transfers between devices, swap(): return lax.ppermute(value, axis, [(i, i ^ bit) for i in range(count)])  16.9 us
    pallas_call x2, Pallas kernels, intra(): pl.pallas_call(kernel, in_specs=[NEAR] * 6 + [FAR, FAR], out_specs=[NEAR]...  12.2 us
    pallas_call x1, Pallas kernels, grad_key_value(): pl.pallas_call(grad_kv_kernel, in_specs=[NEAR] * 16, out_specs=[NEAR, NEA...  5.95 us
    pallas_call x1, Pallas kernels, grad_query(): pl.pallas_call(grad_q_kernel, in_specs=[NEAR] * 15, out_specs=[NEAR, NEAR...  5.61 us
    pallas_call x1, Pallas kernels, state_to_send(): pl.pallas_call(state_kernel, in_specs=[NEAR, FAR, FAR, FAR, FAR], out_spe...  5.13 us
    pallas_call x1, Pallas kernels, finish_other(): pl.pallas_call(finish_other_kernel, in_specs=[NEAR] * 10, out_specs=[FAR,...  4.33 us
    ppermute x15, waiting for transfers between devices, swap(): return lax.ppermute(value, axis, [(i, i ^ bit) for i in range(count)])  4.18 us
    pallas_call x2, Pallas kernels, attend(): pl.pallas_call(functools.partial(attend_kernel, part), in_specs=[NEAR] *...  2.85 us
  transfers between devices with their start and end apart: 15, of which 7 were waited for; matrix products, arithmetic and copies ran while one was open for 0% of the time, Pallas kernels for 50%

profile of v9, /device:TPU:0, one launch (start us, length us, event | category | flops | bytes accessed | tf_op | source)
XLA Modules:
  0.0 70.0 jit_solution(14062158640065993229)
XLA Ops:
  0.8 5.1 %state_to_send.1 = (f32[8,136,128]{2,1,0:T(8,128)S(1)}, f32[8,128,128]{2,1,0:T(8,128)S(1)}, bf16[2,16,256,128]{3,2,1,0:T(8,128)(2,1)S(1)}, bf16[2,16,256,128]{3,...) custom-call(f32[8,128]{1,0:T(8,128)S(1)} %broadcast_in_dim.2.place_r, ...), custom_call_target="tpu_custom_call" | custom-call | flops 134217728 | bytes 8388608 | tf_op jit(solution)/shard_map/state_to_send/pallas_call | solution.py:255
  6.0 0.5 collective-permute-start
  6.5 1.3 %own_state.1 = (f32[8,136,128]{2,1,0:T(8,128)S(1)}, f32[8,128,128]{2,1,0:T(8,128)S(1)}) custom-call(bf16[2,16,256,128]{3,2,1,0:T(8,128)(2,1)S(1)} %get-tuple-element.91.kh.refs_2_, bf16[2,16,256,128]{3,2,1,0:T(8,128)(2,1)S(1)} %get-tuple-element.92.vh.refs_3_, f32[2,16,256]{2,1,0:T(8,128)S(1)} %get-tuple-element.128.cum.cum_ref, ...), custom_call_target="tpu_custom_call" | custom-call | flops 134217728 | bytes 2097152 | tf_op jit(solution)/shard_map/own_state/pallas_call | solution.py:285
  7.8 0.3 collective-permute-done.refs_1_.refs_2_
  8.1 2.9 %collective-permute-start.1 = (f32[4,136,128]{2,1,0:T(8,128)S(1)}, f32[4,136,128]{2,1,0:T(8,128)S(1)}, u32[]{:S(2)}, u32[]{:S(2)}) collective-permute-start(f32[4,136,128]{2,1,0:T(8,128)S(1)} %get-tuple-element.97.refs_4_), channel_id=1, source_target_pairs={{0,8},{4,12},{8,0},{12,4},{16,24},{20,28},{24,16},{28,20},{1,9},{5... | collective-permute-start | bytes 835592 | tf_op jit(solution)/shard_map/ppermute | solution.py:711
  11.1 1.5 %collective-permute-start.2 = (f32[4,128,128]{2,1,0:T(8,128)S(1)}, f32[4,128,128]{2,1,0:T(8,128)S(1)}, u32[]{:S(2)}, u32[]{:S(2)}) collective-permute-start(f32[4,128,128]{2,1,0:T(8,128)S(1)} %get-tuple-element.98.refs_5_), channel_id=1, source_target_pairs={{0,16},{4,20},{8,24},{12,28},{16,0},{20,4},{24,8},{28,12},{1,17},{... | collective-permute-start | bytes 786440 | tf_op jit(solution)/shard_map/ppermute | solution.py:711
  12.6 6.5 %intra_0.1 = (bf16[16,256,128]{2,1,0:T(8,128)(2,1)S(1)}, bf16[16,256,128]{2,1,0:T(8,128)(2,1)S(1)}, bf16[16,256,256]{2,1,0:T(8,128)(2,1)S(1)}, f32[16,3,128,128]...) custom-call(f32[8,128]{1,0:T(8,128)S(1)} %broadcast_in_dim.2.place_ref, ...), custom_call_target="tpu_custom_call" | custom-call | flops 1073741824 | bytes 10485760 | tf_op jit(solution)/shard_map/intra_0/pallas_call | solution.py:332
  19.4 1.8 %collective-permute-start.4 = (f32[4,128,128]{2,1,0:T(8,128)S(1)}, f32[4,128,128]{2,1,0:T(8,128)S(1)}, u32[]{:S(2)}, u32[]{:S(2)}) collective-permute-start(f32[4,128,128]{2,1,0:T(8,128)S(1)} %get-tuple-element.107), channel_id=1, source_target_pairs={{0,16},{4,20},{8,24},{12,28},{16,0},{20,4},{24,8},{28,12},{1,17},{... | collective-permute-start | bytes 786440 | tf_op jit(solution)/shard_map/ppermute | solution.py:711
  21.2 1.5 %collective-permute-start.5 = (f32[4,128,128]{2,1,0:T(8,128)S(1)}, f32[4,128,128]{2,1,0:T(8,128)S(1)}, u32[]{:S(2)}, u32[]{:S(2)}) collective-permute-start(f32[4,128,128]{2,1,0:T(8,128)S(1)} %get-tuple-element.108), channel_id=1, source_target_pairs={{0,8},{4,12},{8,0},{12,4},{16,24},{20,28},{24,16},{28,20},{1,9},{5... | collective-permute-start | bytes 786440 | tf_op jit(solution)/shard_map/ppermute | solution.py:711
  22.7 5.8 %intra_1.1 = (bf16[16,256,128]{2,1,0:T(8,128)(2,1)S(1)}, bf16[16,256,128]{2,1,0:T(8,128)(2,1)S(1)}, bf16[16,256,256]{2,1,0:T(8,128)(2,1)S(1)}, f32[16,3,128,128]...) custom-call(f32[8,128]{1,0:T(8,128)S(1)} %broadcast_in_dim.2.place_ref, ...), custom_call_target="tpu_custom_call" | custom-call | flops 1073741824 | bytes 10485760 | tf_op jit(solution)/shard_map/intra_1/pallas_call | solution.py:332
  28.8 1.2 %attend_0.1 = (f32[8,256,128]{2,1,0:T(8,128)S(1)}, f32[8,256,128]{2,1,0:T(8,128)S(1)}, f32[2,2,256,128]{3,2,1,0:T(8,128)S(1)}) custom-call(f32[16,128]{1,0:T(8,128)S(1)} %get-tuple-element.88.refs_0_.gain_ref, f32[8,128,128]{2,1,0:T(8,128)S(1)} %get-tuple-element.114.refs_1_.keep_ref, bf16[16,256,128]{2,1,0:T(8,128)(2,1)S(1)} %get-tuple-element.124.refs_2_.q0, ...), custom_call_target="tpu_custom_call" | custom-call | flops 268435456 | bytes 8388608 | tf_op jit(solution)/shard_map/attend_0/pallas_call | solution.py:394
  30.0 0.7 collective-permute-done.6.refs_1_.recv_ref
  30.7 1.6 %attend_1.1 = (f32[8,256,128]{2,1,0:T(8,128)S(1)}, f32[8,256,128]{2,1,0:T(8,128)S(1)}, f32[2,512]{1,0:T(2,128)S(1)}) custom-call(f32[16,128]{1,0:T(8,128)S(1)} %get-tuple-element.88.refs_0_.gain_ref, f32[8,128,128]{2,1,0:T(8,128)S(1)} %collective-permute-done.6.refs_1_.recv_ref, bf16[16,256,128]{2,1,0:T(8,128)(2,1)S(1)} %get-tuple-element.124.refs_2_.q0, ...), custom_call_target="tpu_custom_call" | custom-call | flops 268435456 | bytes 8388608 | tf_op jit(solution)/shard_map/attend_1/pallas_call | solution.py:394
  32.3 1.6 %collective-permute-start.7 = (f32[2,512]{1,0:T(2,128)S(1)}, f32[2,512]{1,0:T(2,128)S(1)}, u32[]{:S(2)}, u32[]{:S(2)}) collective-permute-start(f32[2,512]{1,0:T(2,128)S(1)} %get-tuple-element.123.first_ref), channel_id=1, source_target_pairs={{0,1},{1,0},{2,3},{3,2},{4,5},{5,4},{6,7},{7,6},{8,9},{9,8},{10,11... | collective-permute-start | bytes 12296 | tf_op jit(solution)/shard_map/ppermute | solution.py:711
  33.9 1.2 %scaled_queries.1 = (bf16[2,16,128,256]{3,2,1,0:T(8,128)(2,1)S(1)}, f32[2,16,128]{2,1,0:T(8,128)S(1)}) custom-call(f32[2,16,256]{2,1,0:T(8,128)S(1)} %get-tuple-element.128.cum.cum_ref, bf16[16,256,128]{2,1,0:T(8,128)(2,1)S(1)} %get-tuple-element.124.refs_2_.q0, bf16[16,256,128]{2,1,0:T(8,128)(2,1)S(1)} %get-tuple-element.116.refs_3_.q1), custom_call_target="tpu_custom_call" | custom-call | flops 2097152 | bytes 4194304 | tf_op jit(solution)/shard_map/scaled_queries/pallas_call | solution.py:420
  35.1 0.8 %collective-permute-done.7.second_ref = f32[2,512]{1,0:T(2,128)S(1)} collective-permute-done((f32[2,512]{1,0:T(2,128)S(1)}, f32[2,512]{1,0:T(2,128)S(1)}, u32[]{:S(2)}, u32[]{:S(2)}) %collective-permute-start.7) | collective-permute-done | bytes 4128 | tf_op jit(solution)/shard_map/ppermute | solution.py:711
  35.9 2.6 %collective-permute-start.8 = (f32[2,512]{1,0:T(2,128)S(1)}, f32[2,512]{1,0:T(2,128)S(1)}, u32[]{:S(2)}, u32[]{:S(2)}) collective-permute-start(f32[2,512]{1,0:T(2,128)S(1)} %add.15.first_ref), channel_id=1, source_target_pairs={{0,2},{1,3},{2,0},{3,1},{4,6},{5,7},{6,4},{7,5},{8,10},{9,11},{10,... | collective-permute-start | bytes 12296 | tf_op jit(solution)/shard_map/ppermute | solution.py:711
  38.5 2.2 %remaining_decay.1.remaining_ref.refs_4_ = f32[2,16,256,128]{3,2,1,0:T(8,128)S(1)} custom-call(f32[2,16,256]{2,1,0:T(8,128)S(1)} %get-tuple-element.128.cum.cum_ref), custom_call_target="tpu_custom_call" | custom-call | flops 1048576 | bytes 4194304 | tf_op jit(solution)/shard_map/remaining_decay/pallas_call | solution.py:442
  40.8 1.1 %norm_grad_1.1 = (f32[8,128,128]{2,1,0:T(8,128)S(1)}, f32[8,128,128]{2,1,0:T(8,128)S(1)}, bf16[8,256,128]{2,1,0:T(8,128)(2,1)S(1)}, bf16[8,256,128]{2,1,0:T(8,128)(2,1)S(1)}) custom-call(f32[2,16,128]{2,1,0:T(8,128)S(1)} %get-tuple-element.138.ends_ref.refs_0_, f32[16,128]{1,0:T(8,128)S(1)} %get-tuple-element.88.refs_0_.gain_ref, ...), custom_call_target="tpu_custom_call" | custom-call | flops 134217728 | bytes 7340032 | tf_op jit(solution)/shard_map/norm_grad_1/pallas_call | solution.py:487
  42.0 1.1 %norm_grad_0.1 = (f32[8,128,128]{2,1,0:T(8,128)S(1)}, f32[8,128,128]{2,1,0:T(8,128)S(1)}, bf16[8,256,128]{2,1,0:T(8,128)(2,1)S(1)}, bf16[8,256,128]{2,1,0:T(8,128)(2,1)S(1)}) custom-call(f32[2,16,128]{2,1,0:T(8,128)S(1)} %get-tuple-element.138.ends_ref.refs_0_, f32[16,128]{1,0:T(8,128)S(1)} %get-tuple-element.88.refs_0_.gain_ref, ...), custom_call_target="tpu_custom_call" | custom-call | flops 134217728 | bytes 7340032 | tf_op jit(solution)/shard_map/norm_grad_0/pallas_call | solution.py:487
  43.1 0.7 %collective-permute-done.9.refs_2_ = f32[8,128,128]{2,1,0:T(8,128)S(1)} collective-permute-done((f32[8,128,128]{2,1,0:T(8,128)S(1)}, f32[8,128,128]{2,1,0:T(8,128)S(1)}, u32[]{:S(2)}, u32[]{:S(2)}) %collective-permute-start.9) | collective-permute-done | bytes 524320 | tf_op jit(solution)/shard_map/ppermute | solution.py:711
  44.0 1.5 %collective-permute-start.10 = (f32[4,128,128]{2,1,0:T(8,128)S(1)}, f32[4,128,128]{2,1,0:T(8,128)S(1)}, u32[]{:S(2)}, u32[]{:S(2)}) collective-permute-start(f32[4,128,128]{2,1,0:T(8,128)S(1)} %get-tuple-element.150.refs_1_), channel_id=1, source_target_pairs={{0,8},{4,12},{8,0},{12,4},{16,24},{20,28},{24,16},{28,20},{1,9},{5... | collective-permute-start | bytes 786440 | tf_op jit(solution)/shard_map/ppermute | solution.py:711
  45.5 0.5 collective-permute-start.11
  46.0 5.6 %grad_query.1 = (f32[2,16,256,128]{3,2,1,0:T(8,128)S(1)}, bf16[2,16,256,256]{3,2,1,0:T(8,128)(2,1)S(1)}) custom-call(f32[2,16,128]{2,1,0:T(8,128)S(1)} %get-tuple-element.138.ends_ref.refs_0_, f32[8,128,128]{2,1,0:T(8,128)S(1)} %get-tuple-element.114.refs_1_.keep_ref, f32[8,128,128]{2,1,0:T(8,128)S(1)} %collective-permute-done.6.refs_1_.recv_ref, ...), custom_call_target="tpu_custom_call" | custom-call | flops 1610612736 | bytes 12582912 | tf_op jit(solution)/shard_map/grad_query/pallas_call | solution.py:564
  51.6 2.7 %normed_rows.1 = bf16[512,16,128]{2,1,0:T(8,128)(2,1)} custom-call(f32[8,128]{1,0:T(8,128)S(1)} %broadcast_in_dim.2.place_ref, f32[16,128]{1,0:T(8,128)S(1)} %get-tuple-element.88.refs_0_.gain_ref, f32[2,512]{1,0:T(2,128)S(1)} %add.16.sums_ref, f32[8,256,128]{2,1,0:T(8,128)S(1)} %get-tuple-element.134.att0.own0, ...), custom_call_target="tpu_custom_call" | custom-call | flops 3145728 | bytes 6291456 | tf_op jit(solution)/shard_map/normed_rows/pallas_call | solution.py:529
  54.4 1.6 %collective-permute-start.12 = (f32[4,128,128]{2,1,0:T(8,128)S(1)}, f32[4,128,128]{2,1,0:T(8,128)S(1)}, u32[]{:S(2)}, u32[]{:S(2)}) collective-permute-start(f32[4,128,128]{2,1,0:T(8,128)S(1)} %get-tuple-element.158), channel_id=1, source_target_pairs={{0,16},{4,20},{8,24},{12,28},{16,0},{20,4},{24,8},{28,12},{1,17},{... | collective-permute-start | bytes 786440 | tf_op jit(solution)/shard_map/ppermute | solution.py:711
  56.0 0.6 collective-permute-start.13
  56.6 6.0 %grad_key_value.1 = (f32[2,16,256,128]{3,2,1,0:T(8,128)S(1)}, f32[2,16,256,128]{3,2,1,0:T(8,128)S(1)}, bf16[512,16,128]{2,1,0:T(8,128)(2,1)}) custom-call(f32[8,128]{1,0:T(8,128)S(1)} %broadcast_in_dim.2.place_ref, bf16[2,16,256,256]{3,2,1,0:T(8,128)(2,1)S(1)} %get-tuple-element.145.gs_ref, bf16[16,256,256]{2,1,0:T(8,128)(2,1)S(1)} %get-tuple-element.147.w0, ...), custom_call_target="tpu_custom_call" | custom-call | flops 1610612736 | bytes 31457280 | tf_op jit(solution)/shard_map/grad_key_value/pallas_call | solution.py:609
  62.6 0.9 %collective-permute-done.13.refs_6_ = f32[4,128,128]{2,1,0:T(8,128)S(1)} collective-permute-done((f32[4,128,128]{2,1,0:T(8,128)S(1)}, f32[4,128,128]{2,1,0:T(8,128)S(1)}, u32[]{:S(2)}, u32[]{:S(2)}) %collective-permute-start.13) | collective-permute-done | bytes 262176 | tf_op jit(solution)/shard_map/ppermute | solution.py:711
  63.8 1.5 %finish_own.1 = (f32[2,16,256,128]{3,2,1,0:T(8,128)S(1)}, f32[2,16,256,128]{3,2,1,0:T(8,128)S(1)}) custom-call(f32[2,16,128]{2,1,0:T(8,128)S(1)} %get-tuple-element.138.ends_ref.refs_0_, f32[8,128,128]{2,1,0:T(8,128)S(1)} %get-tuple-element.161.refs_1_, bf16[2,16,256,128]{3,2,1,0:T(8,128)(2,1)S(1)} %get-tuple-element.91.kh.refs_2_, ...), custom_call_target="tpu_custom_call" | custom-call | flops 536870912 | bytes 8388608 | tf_op jit(solution)/shard_map/finish_own/pallas_call | solution.py:673
  65.2 0.4 collective-permute-done.14.state_ref
  65.7 4.3 %finish_other.1 = (bf16[512,16,128]{2,1,0:T(8,128)(2,1)}, bf16[512,16,128]{2,1,0:T(8,128)(2,1)}, f32[2,16,256,128]{3,2,1,0:T(8,128)S(1)}, f32[2,16,256,128]{3,2,1,0:T(8,128)S(1)}) custom-call(f32[8,128]{1,0:T(8,128)S(1)} %broadcast_in_dim.2.place_ref, ...), custom_call_target="tpu_custom_call", output_to_operand_aliasing={{2}: (1, {}), {3}: (2, {})} | custom-call | flops 536870912 | bytes 8388608 | tf_op jit(solution)/shard_map/finish_other/pallas_call | solution.py:688
  (25 shorter events, 1.4 us)
Async XLA Ops:
  6.0 2.1 %collective-permute-start = (f32[8,136,128]{2,1,0:T(8,128)S(1)}, f32[8,136,128]{2,1,0:T(8,128)S(1)}, u32[]{:S(2)}, u32[]{:S(2)}) collective-permute-start(f32[8,136,128]{2,1,0:T(8,128)S(1)} %get-tuple-element.90), channel_id=1, source_target_pairs={{0,4},{4,0},{8,12},{12,8},{16,20},{20,16},{24,28},{28,24},{1,5},{5... | collective-permute-start | bytes 1671176 | tf_op jit(solution)/shard_map/ppermute | solution.py:711
  8.1 11.2 %collective-permute-start.1 = (f32[4,136,128]{2,1,0:T(8,128)S(1)}, f32[4,136,128]{2,1,0:T(8,128)S(1)}, u32[]{:S(2)}, u32[]{:S(2)}) collective-permute-start(f32[4,136,128]{2,1,0:T(8,128)S(1)} %get-tuple-element.97.refs_4_), channel_id=1, source_target_pairs={{0,8},{4,12},{8,0},{12,4},{16,24},{20,28},{24,16},{28,20},{1,9},{5... | collective-permute-start | bytes 835592 | tf_op jit(solution)/shard_map/ppermute | solution.py:711
  11.1 8.3 %collective-permute-start.2 = (f32[4,128,128]{2,1,0:T(8,128)S(1)}, f32[4,128,128]{2,1,0:T(8,128)S(1)}, u32[]{:S(2)}, u32[]{:S(2)}) collective-permute-start(f32[4,128,128]{2,1,0:T(8,128)S(1)} %get-tuple-element.98.refs_5_), channel_id=1, source_target_pairs={{0,16},{4,20},{8,24},{12,28},{16,0},{20,4},{24,8},{28,12},{1,17},{... | collective-permute-start | bytes 786440 | tf_op jit(solution)/shard_map/ppermute | solution.py:711
  12.6 6.7 %collective-permute-start.3 = (f32[8,128]{1,0:T(8,128)S(1)}, f32[8,128]{1,0:T(8,128)S(1)}, u32[]{:S(2)}, u32[]{:S(2)}) collective-permute-start(f32[8,128]{1,0:T(8,128)S(1)} %get-tuple-element.96.refs_2_), channel_id=1, source_target_pairs={{0,24},{4,28},{8,16},{12,20},{16,8},{20,12},{24,0},{28,4},{1,25},{... | collective-permute-start | bytes 12296 | tf_op jit(solution)/shard_map/ppermute | solution.py:711
  19.4 9.1 %collective-permute-start.4 = (f32[4,128,128]{2,1,0:T(8,128)S(1)}, f32[4,128,128]{2,1,0:T(8,128)S(1)}, u32[]{:S(2)}, u32[]{:S(2)}) collective-permute-start(f32[4,128,128]{2,1,0:T(8,128)S(1)} %get-tuple-element.107), channel_id=1, source_target_pairs={{0,16},{4,20},{8,24},{12,28},{16,0},{20,4},{24,8},{28,12},{1,17},{... | collective-permute-start | bytes 786440 | tf_op jit(solution)/shard_map/ppermute | solution.py:711
  21.2 7.3 %collective-permute-start.5 = (f32[4,128,128]{2,1,0:T(8,128)S(1)}, f32[4,128,128]{2,1,0:T(8,128)S(1)}, u32[]{:S(2)}, u32[]{:S(2)}) collective-permute-start(f32[4,128,128]{2,1,0:T(8,128)S(1)} %get-tuple-element.108), channel_id=1, source_target_pairs={{0,8},{4,12},{8,0},{12,4},{16,24},{20,28},{24,16},{28,20},{1,9},{5... | collective-permute-start | bytes 786440 | tf_op jit(solution)/shard_map/ppermute | solution.py:711
  28.7 2.0 %collective-permute-start.6 = (f32[8,128,128]{2,1,0:T(8,128)S(1)}, f32[8,128,128]{2,1,0:T(8,128)S(1)}, u32[]{:S(2)}, u32[]{:S(2)}) collective-permute-start(f32[8,128,128]{2,1,0:T(8,128)S(1)} %get-tuple-element.113), channel_id=1, source_target_pairs={{0,4},{4,0},{8,12},{12,8},{16,20},{20,16},{24,28},{28,24},{1,5},{5... | collective-permute-start | bytes 1572872 | tf_op jit(solution)/shard_map/ppermute | solution.py:711
  32.3 3.6 %collective-permute-start.7 = (f32[2,512]{1,0:T(2,128)S(1)}, f32[2,512]{1,0:T(2,128)S(1)}, u32[]{:S(2)}, u32[]{:S(2)}) collective-permute-start(f32[2,512]{1,0:T(2,128)S(1)} %get-tuple-element.123.first_ref), channel_id=1, source_target_pairs={{0,1},{1,0},{2,3},{3,2},{4,5},{5,4},{6,7},{7,6},{8,9},{9,8},{10,11... | collective-permute-start | bytes 12296 | tf_op jit(solution)/shard_map/ppermute | solution.py:711
  35.9 4.8 %collective-permute-start.8 = (f32[2,512]{1,0:T(2,128)S(1)}, f32[2,512]{1,0:T(2,128)S(1)}, u32[]{:S(2)}, u32[]{:S(2)}) collective-permute-start(f32[2,512]{1,0:T(2,128)S(1)} %add.15.first_ref), channel_id=1, source_target_pairs={{0,2},{1,3},{2,0},{3,1},{4,6},{5,7},{6,4},{7,5},{8,10},{9,11},{10,... | collective-permute-start | bytes 12296 | tf_op jit(solution)/shard_map/ppermute | solution.py:711
  41.9 2.0 %collective-permute-start.9 = (f32[8,128,128]{2,1,0:T(8,128)S(1)}, f32[8,128,128]{2,1,0:T(8,128)S(1)}, u32[]{:S(2)}, u32[]{:S(2)}) collective-permute-start(f32[8,128,128]{2,1,0:T(8,128)S(1)} %get-tuple-element.132), channel_id=1, source_target_pairs={{0,4},{4,0},{8,12},{12,8},{16,20},{20,16},{24,28},{28,24},{1,5},{5... | collective-permute-start | bytes 1572872 | tf_op jit(solution)/shard_map/ppermute | solution.py:711
  44.0 10.3 %collective-permute-start.10 = (f32[4,128,128]{2,1,0:T(8,128)S(1)}, f32[4,128,128]{2,1,0:T(8,128)S(1)}, u32[]{:S(2)}, u32[]{:S(2)}) collective-permute-start(f32[4,128,128]{2,1,0:T(8,128)S(1)} %get-tuple-element.150.refs_1_), channel_id=1, source_target_pairs={{0,8},{4,12},{8,0},{12,4},{16,24},{20,28},{24,16},{28,20},{1,9},{5... | collective-permute-start | bytes 786440 | tf_op jit(solution)/shard_map/ppermute | solution.py:711
  45.5 8.8 %collective-permute-start.11 = (f32[4,128,128]{2,1,0:T(8,128)S(1)}, f32[4,128,128]{2,1,0:T(8,128)S(1)}, u32[]{:S(2)}, u32[]{:S(2)}) collective-permute-start(f32[4,128,128]{2,1,0:T(8,128)S(1)} %get-tuple-element.137.refs_2_), channel_id=1, source_target_pairs={{0,16},{4,20},{8,24},{12,28},{16,0},{20,4},{24,8},{28,12},{1,17},{... | collective-permute-start | bytes 786440 | tf_op jit(solution)/shard_map/ppermute | solution.py:711
  54.4 8.2 %collective-permute-start.12 = (f32[4,128,128]{2,1,0:T(8,128)S(1)}, f32[4,128,128]{2,1,0:T(8,128)S(1)}, u32[]{:S(2)}, u32[]{:S(2)}) collective-permute-start(f32[4,128,128]{2,1,0:T(8,128)S(1)} %get-tuple-element.158), channel_id=1, source_target_pairs={{0,16},{4,20},{8,24},{12,28},{16,0},{20,4},{24,8},{28,12},{1,17},{... | collective-permute-start | bytes 786440 | tf_op jit(solution)/shard_map/ppermute | solution.py:711
  56.0 7.5 %collective-permute-start.13 = (f32[4,128,128]{2,1,0:T(8,128)S(1)}, f32[4,128,128]{2,1,0:T(8,128)S(1)}, u32[]{:S(2)}, u32[]{:S(2)}) collective-permute-start(f32[4,128,128]{2,1,0:T(8,128)S(1)} %get-tuple-element.153), channel_id=1, source_target_pairs={{0,8},{4,12},{8,0},{12,4},{16,24},{20,28},{24,16},{28,20},{1,9},{5... | collective-permute-start | bytes 786440 | tf_op jit(solution)/shard_map/ppermute | solution.py:711
  63.7 2.0 %collective-permute-start.14 = (f32[8,128,128]{2,1,0:T(8,128)S(1)}, f32[8,128,128]{2,1,0:T(8,128)S(1)}, u32[]{:S(2)}, u32[]{:S(2)}) collective-permute-start(f32[8,128,128]{2,1,0:T(8,128)S(1)} %get-tuple-element.166), channel_id=1, source_target_pairs={{0,4},{4,0},{8,12},{12,8},{16,20},{20,16},{24,28},{28,24},{1,5},{5... | collective-permute-start | bytes 1572872 | tf_op jit(solution)/shard_map/ppermute | solution.py:711

commit v10 on v9

--- a/solution.py
+++ b/solution.py
@@ -273,41 +273,55 @@
     )(place, *far(gain, log_decay, key_rows, value_rows))
 
 
-def own_state_kernel(kh, vh, cum, decay, own_ref, first_ref):
+def fetch_block(index, arrays, blocks, sems):
+    copies = [
+        pltpu.make_async_copy(array.at[pl.ds(index * BLOCK, BLOCK)], block, sems.at[at])
+        for at, (array, block) in enumerate(zip(arrays, blocks))
+    ]
+    for copy in copies:
+        copy.start()
+    return copies
+
+
+def own_state_kernel(
+    kh, vh, cum, decay, q_hbm, o_hbm, own_ref, first_ref, q_raw, o_raw, sems
+):
+    copies = fetch_block(0, (q_hbm, o_hbm), (q_raw, o_raw), sems)
     half_states(0, kh, vh, cum, 0, first_ref)
     half_states(0, kh, vh, cum, 1, own_ref, first_ref)
     add_decays(own_ref, decay, 0)
-
-
-def own_state(kh, vh, cum, decay):
+    for copy in copies:
+        copy.wait()
+
+
+def own_state(kh, vh, cum, decay, query_rows, output_grad):
     _, heads, tok, dim = kh.shape
     half = heads // 2
+    raw = in_vmem(BLOCK, heads, dim, kind=BF16)
     return pl.pallas_call(
         own_state_kernel,
-        in_specs=[NEAR] * 4,
-        out_specs=[NEAR] * 2,
-        out_shape=[in_vmem(half, dim + TILE, dim), in_vmem(half, dim, dim)],
+        in_specs=[NEAR] * 4 + [FAR, FAR],
+        out_specs=[NEAR] * 4,
+        out_shape=[in_vmem(half, dim + TILE, dim), in_vmem(half, dim, dim), raw, raw],
+        scratch_shapes=[pltpu.SemaphoreType.DMA((2,))],
         compiler_params=params(4),
         cost_estimate=cost(2 * tok * heads * dim * dim, 4 * tok * heads * dim),
         name="own_state",
-    )(*near(kh, vh, cum, decay))
-
-
-def intra(index, place, cum, kh, vh, first_own, first_send, query_rows, output_grad):
+    )(*near(kh, vh, cum, decay), *far(query_rows, output_grad))
+
+
+def intra(index, place, cum, kh, vh, first_own, first_send, raw, query_rows, output_grad):
     tok, heads, dim = query_rows.shape
-
-    def kernel(place_ref, cum, kh, vh, first_own, first_send, q_hbm, o_hbm,
-               qh, oh, w_ref, decays_ref, columns_ref, inner_ref,
-               q_raw, o_raw, sems):
-        at = pl.ds(index * BLOCK, BLOCK)
-        copy_q = pltpu.make_async_copy(q_hbm.at[at], q_raw, sems.at[0])
-        copy_o = pltpu.make_async_copy(o_hbm.at[at], o_raw, sems.at[1])
-        copy_q.start()
-        copy_o.start()
+    ahead = index == 0
+
+    def kernel(place_ref, cum, kh, vh, first_own, first_send, q_raw, o_raw, *refs):
+        if ahead:
+            q_hbm, o_hbm, *refs = refs
+            *refs, q_next, o_next, sems = refs
+            copies = fetch_block(1, (q_hbm, o_hbm), (q_next, o_next), sems)
+        qh, oh, w_ref, decays_ref, columns_ref, inner_ref = refs
         upper = is_upper(place_ref)
-        copy_q.wait()
         to_heads(qh, q_raw, upper)
-        copy_o.wait()
         to_heads(oh, o_raw, upper)
 
         def one(part, i, h):
@@ -326,29 +340,32 @@
                 inner += columns * times_state(query, (first_own, first_send)[part][i])
             inner_ref[h] = inner
 
-        each_half(heads // 2, 2, one)
+        each_half(heads // 2, 4, one)
+        if ahead:
+            for copy in copies:
+                copy.wait()
 
     by_head = in_vmem(heads, BLOCK, dim, kind=BF16)
     return pl.pallas_call(
         kernel,
-        in_specs=[NEAR] * 6 + [FAR, FAR],
-        out_specs=[NEAR] * 6,
+        in_specs=[NEAR] * 8 + [FAR, FAR] * ahead,
+        out_specs=[NEAR] * (6 + 2 * ahead),
         out_shape=[
             by_head, by_head, in_vmem(heads, BLOCK, BLOCK, kind=BF16),
             in_vmem(heads, 3, BLOCK // 2, BLOCK // 2), in_vmem(heads, BLOCK, dim),
             in_vmem(heads, BLOCK, dim),
-        ],
-        scratch_shapes=[
-            pltpu.VMEM((BLOCK, heads, dim), BF16),
-            pltpu.VMEM((BLOCK, heads, dim), BF16),
-            pltpu.SemaphoreType.DMA((2,)),
-        ],
-        compiler_params=params(6),
+        ]
+        + [in_vmem(BLOCK, heads, dim, kind=BF16)] * (2 * ahead),
+        scratch_shapes=[pltpu.SemaphoreType.DMA((2,))] * ahead,
+        compiler_params=params(4),
         cost_estimate=cost(
             2 * heads * BLOCK * BLOCK * dim * 4, 20 * heads * BLOCK * dim, heads * BLOCK * BLOCK
         ),
         name=f"intra_{index}",
-    )(place, *near(cum, kh, vh, first_own, first_send), *far(query_rows, output_grad))
+    )(
+        *near(place, cum, kh, vh, first_own, first_send, *raw),
+        *(far(query_rows, output_grad) if ahead else ()),
+    )
 
 
 def attend_kernel(part, *refs):
@@ -415,7 +432,7 @@
                 scale = jnp.exp(cum_ref[b, pl.ds(h, 1), :])
                 out_ref[b, h] = (q[h].astype(F32).T * scale).astype(BF16)
 
-        each_head(heads, 2, one)
+        each_head(heads, 4, one)
 
     return pl.pallas_call(
         kernel,
@@ -437,7 +454,7 @@
                 row = cum_ref[b, pl.ds(h, 1), :]
                 out_ref[b, h] = as_columns(jnp.exp(row[:, BLOCK - 1 :] - row))
 
-        each_head(heads, 2, one)
+        each_head(heads, 4, one)
 
     return pl.pallas_call(
         kernel,
@@ -496,53 +513,27 @@
     )(*near(ends, gain, sums, scaled, *arrays))
 
 
-def on_block(work):
-    for index in range(2):
-        pl.when(pl.program_id(0) == index)(lambda index=index: work(index))
-
-
-def raw_output(heads, tok):
-    spec = pl.BlockSpec((BLOCK, heads, HD), lambda i: (i, 0, 0))
-    return spec, jax.ShapeDtypeStruct((tok, heads, HD), BF16)
-
-
-def normed_kernel(place_ref, gain_ref, sums_ref, own0, own1, other0, other1, out_ref, rows):
-    upper = is_upper(place_ref)
-
-    def work(b):
-        inv = as_columns(inverse_rms(sums_ref, b)[0])
-        halves = ((own0, other0), (own1, other1))[b]
-
-        def one(part, i, h):
-            rows[h] = halves[part][i] * inv * gain_ref[pl.ds(h, 1), :]
-
-        each_half(own0.shape[0], 4, one)
-
-    on_block(work)
-    from_heads(out_ref, rows, 0, BLOCK, upper)
-
-
-def normed_rows(place, gain, sums, arrays):
-    heads, dim = gain.shape
-    tok = 2 * BLOCK
-    spec, shape = raw_output(heads, tok)
-    return pl.pallas_call(
-        normed_kernel,
-        grid=(2,),
-        in_specs=[NEAR] * 7,
-        out_specs=spec,
-        out_shape=shape,
-        scratch_shapes=[pltpu.VMEM((heads, BLOCK, dim), F32)],
-        compiler_params=params(7),
-        cost_estimate=cost(3 * heads * tok * dim, 6 * heads * tok * dim),
-        name="normed_rows",
-    )(place, *near(gain, sums, *arrays))
+def normed_block(b, place_ref, gain_ref, sums_ref, halves, rows, raw):
+    inv = as_columns(inverse_rms(sums_ref, b)[0])
+
+    def one(part, i, h):
+        rows[b, h] = halves[part][i] * inv * gain_ref[pl.ds(h, 1), :]
+
+    each_half(halves[0].shape[0], 4, one)
+    from_heads(raw, rows.at[b], 0, BLOCK, is_upper(place_ref))
 
 
 def grad_q_kernel(
+    place_ref, gain_ref, sums_ref, att_own0, att_own1, att_other0, att_other1,
     ends_ref, keep_ref, recv_ref, first_own, first_send, kh, vh, own0, own1, other0, other1,
-    decays0, decays1, columns0, columns1, rows, gs_ref,
+    decays0, decays1, columns0, columns1, rows, gs_ref, out_normed, raw, sems,
 ):
+    copies = []
+    for b, halves in enumerate(((att_own0, att_other0), (att_own1, att_other1))):
+        at = pl.ds(b * BLOCK, BLOCK)
+        normed_block(b, place_ref, gain_ref, sums_ref, halves, rows, raw.at[at])
+        copies.append(pltpu.make_async_copy(raw.at[at], out_normed.at[at], sems.at[b]))
+        copies[-1].start()
     blocks = (((own0, other0), decays0, columns0), ((own1, other1), decays1, columns1))
     for b, (g, decays, columns) in enumerate(blocks):
 
@@ -556,24 +547,31 @@
             rows[b, h] = dot(scores, kh[b, h]) + columns[h] * times_state_t(grad, state)
 
         each_half(keep_ref.shape[0], 4, one)
-
-
-def grad_query(ends, arrays):
+    for copy in copies:
+        copy.wait()
+
+
+def grad_query(place, gain, sums, att, ends, arrays):
     _, heads, dim = ends.shape
     tok = 2 * BLOCK
     return pl.pallas_call(
         grad_q_kernel,
-        in_specs=[NEAR] * 15,
-        out_specs=[NEAR, NEAR],
+        in_specs=[NEAR] * 22,
+        out_specs=[NEAR, NEAR, FAR],
         out_shape=[
             in_vmem(2, heads, BLOCK, dim), in_vmem(2, heads, BLOCK, BLOCK, kind=BF16),
+            jax.ShapeDtypeStruct((tok, heads, dim), BF16),
         ],
-        compiler_params=params(4),
+        scratch_shapes=[
+            pltpu.VMEM((tok, heads, dim), BF16),
+            pltpu.SemaphoreType.DMA((2,)),
+        ],
+        compiler_params=params(6),
         cost_estimate=cost(
             4 * heads * tok * dim * (BLOCK + dim), 12 * heads * tok * dim, heads * tok * BLOCK
         ),
         name="grad_query",
-    )(*near(ends, *arrays))
+    )(*near(place, gain, sums, *att, ends, *arrays))
 
 
 def grad_kv_kernel(
@@ -657,10 +655,10 @@
     copies = []
     for b in range(2):
         finish_rows(1, b, ends_ref, state_ref, kh, vh, remaining_ref, dk, dv, rows_k, rows_v)
-        for start in range(0, BLOCK, CHUNK):
-            at = pl.ds(b * BLOCK + start, CHUNK)
+        for start in range(0, BLOCK, CHUNK // 2):
+            at = pl.ds(b * BLOCK + start, CHUNK // 2)
             for rows, raw, out in ((rows_k, raw_k, out_k), (rows_v, raw_v, out_v)):
-                from_heads(raw.at[at], rows.at[b], start, CHUNK, upper)
+                from_heads(raw.at[at], rows.at[b], start, CHUNK // 2, upper)
                 copies.append(pltpu.make_async_copy(raw.at[at], out.at[at], sems.at[len(copies)]))
                 copies[-1].start()
     for copy in copies:
@@ -694,7 +692,7 @@
         scratch_shapes=[
             pltpu.VMEM((tok, heads, dim), BF16),
             pltpu.VMEM((tok, heads, dim), BF16),
-            pltpu.SemaphoreType.DMA((2 * (tok // CHUNK),)),
+            pltpu.SemaphoreType.DMA((4 * (tok // CHUNK),)),
         ],
         compiler_params=params(8),
         cost_estimate=cost(4 * heads * tok * dim * dim, 8 * heads * tok * dim),
@@ -827,7 +825,7 @@
             return before
         run, outputs = tasks[stage]
         outputs.extend(run(after))
-        return lax.optimization_barrier((before, outputs[-1]))[0]
+        return lax.optimization_barrier((before, outputs[0]))[0]
 
     name = "later" if backward else "earlier"
     half = send.shape[0]
@@ -951,17 +949,29 @@
     send, first_send, kh, vh, cum, _, decay, gain = state_to_send(
         place, norm_gain, log_decay, key_rows, value_rows
     )
-    firsts, in_0, in_1, begun = [], [], [], []
+    firsts, raws, in_0, in_1, begun = [], [], [], [], []
 
     def own_task(earlier):
-        own, first = own_state(follows(kh, earlier), vh, cum, decay)
+        own, first, *raw = own_state(
+            follows(kh, earlier), vh, cum, decay, query_rows, output_grad
+        )
         firsts.extend((first, first_send))
+        raws.append(raw)
         return own
 
     def forward_task(index):
-        return lambda earlier: intra(
-            index, place, follows(cum, earlier), kh, vh, *firsts, query_rows, output_grad
-        )
+        def task(earlier):
+            *made, q_next, o_next = [
+                *intra(
+                    index, place, follows(cum, earlier), kh, vh, *firsts, raws[-1],
+                    query_rows, output_grad,
+                ),
+                *raws[-1] * index,
+            ]
+            raws.append([q_next, o_next])
+            return made
+
+        return task
 
     def parts():
         q0, o0, _, _, columns0, inner0 = in_0
@@ -987,7 +997,7 @@
         ),
     )
     grad_send, second_send, *other_g = norm_grad(1, ends, gain, sums, scaled, (o0, o1, *other_att))
-    own_g, seconds, queries, pairs, norms, rows = [], [], [], [], [], []
+    own_g, seconds, queries, pairs, rows = [], [], [], [], []
 
     def own_grad_task(earlier):
         own, second, *grads = norm_grad(
@@ -998,14 +1008,10 @@
         return own
 
     def query_task(earlier):
-        made = grad_query(
-            follows(ends, earlier),
+        return grad_query(
+            place, gain, sums, (*own_att, *other_att), follows(ends, earlier),
             (keep, recv, *firsts, kh, vh, *own_g, *other_g, decays0, decays1, columns0, columns1),
         )
-        norms.append(
-            normed_rows(place, gain, follows(sums, made[-1]), (*own_att, *other_att))
-        )
-        return *made, norms[0]
 
     def pair_task(earlier):
         return grad_key_value(
@@ -1024,7 +1030,7 @@
     grad_k, grad_v = finish_other(
         place, rows, ends, grad_recv, (kh, vh, remaining, *pairs[:2])
     )
-    return norms[0], pairs[2], grad_k, grad_v
+    return queries[2], pairs[2], grad_k, grad_v
 
 
 def solution(mesh):

time: 70.1 us -> 67.9 us (0.969)
  Pallas kernels: 47.9 us -> 42.2 us
  waiting for transfers between devices: 4.18 us -> 8.7 us
  starting transfers between devices: 16.9 us -> 15.6 us
    pallas_call x5 -> x4, Pallas kernels: 21.8 us -> 16.7 us  [the longest x2 7.69 us: intra(): pl.pallas_call(kernel, in_specs=[NEAR] * 8 + [FAR, FAR] * ahead, out_spec...]
    ppermute x15, waiting for transfers between devices: 4.18 us -> 8.7 us  [swap(): return lax.ppermute(value, axis, [(i, i ^ bit) for i in range(count)])]
    ppermute x15, starting transfers between devices: 16.9 us -> 15.6 us  [swap(): return lax.ppermute(value, axis, [(i, i ^ bit) for i in range(count)])]
  transfers between devices with their start and end apart: 15 -> 15, of which waited for: 7 -> 9; matrix products, arithmetic and copies ran while one was open for 0% -> 0% of each run, Pallas kernels for 50% -> 43%
where the time goes in v10:
time: 67.9 us; the launch traced here: 67.7 us
  Pallas kernels  42.2 us (62%)
  starting transfers between devices  15.6 us (23%)
  waiting for transfers between devices  8.7 us (13%)
  between operations  1 us (1%)
    ppermute x15, starting transfers between devices, swap(): return lax.ppermute(value, axis, [(i, i ^ bit) for i in range(count)])  15.6 us
    ppermute x15, waiting for transfers between devices, swap(): return lax.ppermute(value, axis, [(i, i ^ bit) for i in range(count)])  8.7 us
    pallas_call x2, Pallas kernels, intra(): pl.pallas_call(kernel, in_specs=[NEAR] * 8 + [FAR, FAR] * ahead, out_spec...  7.69 us
    pallas_call x1, Pallas kernels, grad_query(): pl.pallas_call(grad_q_kernel, in_specs=[NEAR] * 22, out_specs=[NEAR, NEAR...  7.41 us
    pallas_call x1, Pallas kernels, grad_key_value(): pl.pallas_call(grad_kv_kernel, in_specs=[NEAR] * 16, out_specs=[NEAR, NEA...  6.17 us
    pallas_call x1, Pallas kernels, state_to_send(): pl.pallas_call(state_kernel, in_specs=[NEAR, FAR, FAR, FAR, FAR], out_spe...  5.12 us
    pallas_call x1, Pallas kernels, finish_other(): pl.pallas_call(finish_other_kernel, in_specs=[NEAR] * 10, out_specs=[FAR,...  4.3 us
    pallas_call x2, Pallas kernels, attend(): pl.pallas_call(functools.partial(attend_kernel, part), in_specs=[NEAR] *...  2.91 us
  transfers between devices with their start and end apart: 15, of which 9 were waited for; matrix products, arithmetic and copies ran while one was open for 0% of the time, Pallas kernels for 43%

profile of v10, /device:TPU:0, one launch (start us, length us, event | category | flops | bytes accessed | tf_op | source)
XLA Modules:
  0.0 67.7 jit_solution(18310787018216455915)
XLA Ops:
  0.8 5.1 %state_to_send.1 = (f32[8,136,128]{2,1,0:T(8,128)S(1)}, f32[8,128,128]{2,1,0:T(8,128)S(1)}, bf16[2,16,256,128]{3,2,1,0:T(8,128)(2,1)S(1)}, bf16[2,16,256,128]{3,...) custom-call(f32[8,128]{1,0:T(8,128)S(1)} %broadcast_in_dim.2.place_r, ...), custom_call_target="tpu_custom_call" | custom-call | flops 134217728 | bytes 8388608 | tf_op jit(solution)/shard_map/state_to_send/pallas_call | solution.py:255
  6.0 0.5 collective-permute-start
  6.5 1.6 %own_state.1 = (f32[8,136,128]{2,1,0:T(8,128)S(1)}, f32[8,128,128]{2,1,0:T(8,128)S(1)}, bf16[256,16,128]{2,1,0:T(8,128)(2,1)S(1)}, bf16[256,16,128]{2,1,0:T(8,128)(2,1)S(1)}) custom-call(bf16[2,16,256,128]{3,2,1,0:T(8,128)(2,1)S(1)} %get-tuple-element.95.kh.refs_2_, bf16[2,16,256,128]{3,2,1,0:T(8,128)(2,1)S(1)} %get-tuple-element.96.vh.refs_3_, ...), custom_call_target="tpu_custom_call" | custom-call | flops 134217728 | bytes 2097152 | tf_op jit(solution)/shard_map/own_state/pallas_call | solution.py:301
  8.2 2.9 %collective-permute-start.1 = (f32[4,136,128]{2,1,0:T(8,128)S(1)}, f32[4,136,128]{2,1,0:T(8,128)S(1)}, u32[]{:S(2)}, u32[]{:S(2)}) collective-permute-start(f32[4,136,128]{2,1,0:T(8,128)S(1)} %get-tuple-element.101.refs_4_), channel_id=1, source_target_pairs={{0,8},{4,12},{8,0},{12,4},{16,24},{20,28},{24,16},{28,20},{1,9},{5... | collective-permute-start | bytes 835592 | tf_op jit(solution)/shard_map/ppermute | solution.py:709
  11.1 1.5 %collective-permute-start.2 = (f32[4,128,128]{2,1,0:T(8,128)S(1)}, f32[4,128,128]{2,1,0:T(8,128)S(1)}, u32[]{:S(2)}, u32[]{:S(2)}) collective-permute-start(f32[4,128,128]{2,1,0:T(8,128)S(1)} %get-tuple-element.102.refs_5_), channel_id=1, source_target_pairs={{0,16},{4,20},{8,24},{12,28},{16,0},{20,4},{24,8},{28,12},{1,17},{... | collective-permute-start | bytes 786440 | tf_op jit(solution)/shard_map/ppermute | solution.py:709
  12.6 3.8 %intra_0.1 = (bf16[16,256,128]{2,1,0:T(8,128)(2,1)S(1)}, bf16[16,256,128]{2,1,0:T(8,128)(2,1)S(1)}, bf16[16,256,256]{2,1,0:T(8,128)(2,1)S(1)}, f32[16,3,128,128]...) custom-call(f32[8,128]{1,0:T(8,128)S(1)} %broadcast_in_dim.2.place_r, ...), custom_call_target="tpu_custom_call" | custom-call | flops 1073741824 | bytes 10485760 | tf_op jit(solution)/shard_map/intra_0/pallas_call | solution.py:349
  16.4 2.9 %collective-permute-done.3.refs_3_ = f32[8,128]{1,0:T(8,128)S(1)} collective-permute-done((f32[8,128]{1,0:T(8,128)S(1)}, f32[8,128]{1,0:T(8,128)S(1)}, u32[]{:S(2)}, u32[]{:S(2)}) %collective-permute-start.3) | collective-permute-done | bytes 4128 | tf_op jit(solution)/shard_map/ppermute | solution.py:709
  19.4 1.5 %collective-permute-start.4 = (f32[4,128,128]{2,1,0:T(8,128)S(1)}, f32[4,128,128]{2,1,0:T(8,128)S(1)}, u32[]{:S(2)}, u32[]{:S(2)}) collective-permute-start(f32[4,128,128]{2,1,0:T(8,128)S(1)} %get-tuple-element.113), channel_id=1, source_target_pairs={{0,16},{4,20},{8,24},{12,28},{16,0},{20,4},{24,8},{28,12},{1,17},{... | collective-permute-start | bytes 786440 | tf_op jit(solution)/shard_map/ppermute | solution.py:709
  20.9 0.6 collective-permute-start.5
  21.5 3.9 %intra_1.1 = (bf16[16,256,128]{2,1,0:T(8,128)(2,1)S(1)}, bf16[16,256,128]{2,1,0:T(8,128)(2,1)S(1)}, bf16[16,256,256]{2,1,0:T(8,128)(2,1)S(1)}, f32[16,3,128,128]...) custom-call(f32[8,128]{1,0:T(8,128)S(1)} %broadcast_in_dim.2.place_ref, ...), custom_call_target="tpu_custom_call" | custom-call | flops 1073741824 | bytes 10485760 | tf_op jit(solution)/shard_map/intra_1/pallas_call | solution.py:349
  25.4 1.3 %collective-permute-done.4.refs_5_ = f32[4,128,128]{2,1,0:T(8,128)S(1)} collective-permute-done((f32[4,128,128]{2,1,0:T(8,128)S(1)}, f32[4,128,128]{2,1,0:T(8,128)S(1)}, u32[]{:S(2)}, u32[]{:S(2)}) %collective-permute-start.4) | collective-permute-done | bytes 262176 | tf_op jit(solution)/shard_map/ppermute | solution.py:709
  26.7 1.1 %collective-permute-done.5.refs_6_ = f32[4,128,128]{2,1,0:T(8,128)S(1)} collective-permute-done((f32[4,128,128]{2,1,0:T(8,128)S(1)}, f32[4,128,128]{2,1,0:T(8,128)S(1)}, u32[]{:S(2)}, u32[]{:S(2)}) %collective-permute-start.5) | collective-permute-done | bytes 262176 | tf_op jit(solution)/shard_map/ppermute | solution.py:709
  28.1 1.3 %attend_0.1 = (f32[8,256,128]{2,1,0:T(8,128)S(1)}, f32[8,256,128]{2,1,0:T(8,128)S(1)}, f32[2,2,256,128]{3,2,1,0:T(8,128)S(1)}) custom-call(f32[16,128]{1,0:T(8,128)S(1)} %get-tuple-element.92.refs_0_.gain_ref, f32[8,128,128]{2,1,0:T(8,128)S(1)} %get-tuple-element.122.refs_1_.keep_ref, bf16[16,256,128]{2,1,0:T(8,128)(2,1)S(1)} %get-tuple-element.132.refs_2_.q0, ...), custom_call_target="tpu_custom_call" | custom-call | flops 268435456 | bytes 8388608 | tf_op jit(solution)/shard_map/attend_0/pallas_call | solution.py:411
  29.4 0.6 collective-permute-done.6.refs_1_.recv_ref
  30.0 1.7 %attend_1.1 = (f32[8,256,128]{2,1,0:T(8,128)S(1)}, f32[8,256,128]{2,1,0:T(8,128)S(1)}, f32[2,512]{1,0:T(2,128)S(1)}) custom-call(f32[16,128]{1,0:T(8,128)S(1)} %get-tuple-element.92.refs_0_.gain_ref, f32[8,128,128]{2,1,0:T(8,128)S(1)} %collective-permute-done.6.refs_1_.recv_ref, bf16[16,256,128]{2,1,0:T(8,128)(2,1)S(1)} %get-tuple-element.132.refs_2_.q0, ...), custom_call_target="tpu_custom_call" | custom-call | flops 268435456 | bytes 8388608 | tf_op jit(solution)/shard_map/attend_1/pallas_call | solution.py:411
  31.6 1.6 %collective-permute-start.7 = (f32[2,512]{1,0:T(2,128)S(1)}, f32[2,512]{1,0:T(2,128)S(1)}, u32[]{:S(2)}, u32[]{:S(2)}) collective-permute-start(f32[2,512]{1,0:T(2,128)S(1)} %get-tuple-element.131.first_ref), channel_id=1, source_target_pairs={{0,1},{1,0},{2,3},{3,2},{4,5},{5,4},{6,7},{7,6},{8,9},{9,8},{10,11... | collective-permute-start | bytes 12296 | tf_op jit(solution)/shard_map/ppermute | solution.py:709
  33.2 0.9 %scaled_queries.1 = (bf16[2,16,128,256]{3,2,1,0:T(8,128)(2,1)S(1)}, f32[2,16,128]{2,1,0:T(8,128)S(1)}) custom-call(f32[2,16,256]{2,1,0:T(8,128)S(1)} %get-tuple-element.136.cum.cum_ref, bf16[16,256,128]{2,1,0:T(8,128)(2,1)S(1)} %get-tuple-element.132.refs_2_.q0, bf16[16,256,128]{2,1,0:T(8,128)(2,1)S(1)} %get-tuple-element.118.refs_3_.q1), custom_call_target="tpu_custom_call" | custom-call | flops 2097152 | bytes 4194304 | tf_op jit(solution)/shard_map/scaled_queries/pallas_call | solution.py:437
  34.1 1.1 %collective-permute-done.7.second_ref = f32[2,512]{1,0:T(2,128)S(1)} collective-permute-done((f32[2,512]{1,0:T(2,128)S(1)}, f32[2,512]{1,0:T(2,128)S(1)}, u32[]{:S(2)}, u32[]{:S(2)}) %collective-permute-start.7) | collective-permute-done | bytes 4128 | tf_op jit(solution)/shard_map/ppermute | solution.py:709
  35.3 2.6 %collective-permute-start.8 = (f32[2,512]{1,0:T(2,128)S(1)}, f32[2,512]{1,0:T(2,128)S(1)}, u32[]{:S(2)}, u32[]{:S(2)}) collective-permute-start(f32[2,512]{1,0:T(2,128)S(1)} %add.15.first_ref), channel_id=1, source_target_pairs={{0,2},{1,3},{2,0},{3,1},{4,6},{5,7},{6,4},{7,5},{8,10},{9,11},{10,... | collective-permute-start | bytes 12296 | tf_op jit(solution)/shard_map/ppermute | solution.py:709
  37.8 1.6 %remaining_decay.1.remaining_ref.refs_4_ = f32[2,16,256,128]{3,2,1,0:T(8,128)S(1)} custom-call(f32[2,16,256]{2,1,0:T(8,128)S(1)} %get-tuple-element.136.cum.cum_ref), custom_call_target="tpu_custom_call" | custom-call | flops 1048576 | bytes 4194304 | tf_op jit(solution)/shard_map/remaining_decay/pallas_call | solution.py:459
  39.8 1.1 %norm_grad_1.1 = (f32[8,128,128]{2,1,0:T(8,128)S(1)}, f32[8,128,128]{2,1,0:T(8,128)S(1)}, bf16[8,256,128]{2,1,0:T(8,128)(2,1)S(1)}, bf16[8,256,128]{2,1,0:T(8,128)(2,1)S(1)}) custom-call(f32[2,16,128]{2,1,0:T(8,128)S(1)} %get-tuple-element.146.ends_ref.refs_0_, f32[16,128]{1,0:T(8,128)S(1)} %get-tuple-element.92.refs_0_.gain_ref, ...), custom_call_target="tpu_custom_call" | custom-call | flops 134217728 | bytes 7340032 | tf_op jit(solution)/shard_map/norm_grad_1/pallas_call | solution.py:504
  41.0 1.2 %norm_grad_0.1 = (f32[8,128,128]{2,1,0:T(8,128)S(1)}, f32[8,128,128]{2,1,0:T(8,128)S(1)}, bf16[8,256,128]{2,1,0:T(8,128)(2,1)S(1)}, bf16[8,256,128]{2,1,0:T(8,128)(2,1)S(1)}) custom-call(f32[2,16,128]{2,1,0:T(8,128)S(1)} %get-tuple-element.146.ends_ref.refs_0_, f32[16,128]{1,0:T(8,128)S(1)} %get-tuple-element.92.refs_0_.gain_ref, ...), custom_call_target="tpu_custom_call" | custom-call | flops 134217728 | bytes 7340032 | tf_op jit(solution)/shard_map/norm_grad_0/pallas_call | solution.py:504
  42.2 0.7 %collective-permute-done.9.refs_2_ = f32[8,128,128]{2,1,0:T(8,128)S(1)} collective-permute-done((f32[8,128,128]{2,1,0:T(8,128)S(1)}, f32[8,128,128]{2,1,0:T(8,128)S(1)}, u32[]{:S(2)}, u32[]{:S(2)}) %collective-permute-start.9) | collective-permute-done | bytes 524320 | tf_op jit(solution)/shard_map/ppermute | solution.py:709
  43.0 1.0 %collective-permute-start.10 = (f32[4,128,128]{2,1,0:T(8,128)S(1)}, f32[4,128,128]{2,1,0:T(8,128)S(1)}, u32[]{:S(2)}, u32[]{:S(2)}) collective-permute-start(f32[4,128,128]{2,1,0:T(8,128)S(1)} %get-tuple-element.158.refs_1_), channel_id=1, source_target_pairs={{0,8},{4,12},{8,0},{12,4},{16,24},{20,28},{24,16},{28,20},{1,9},{5... | collective-permute-start | bytes 786440 | tf_op jit(solution)/shard_map/ppermute | solution.py:709
  44.0 1.3 %collective-permute-start.11 = (f32[4,128,128]{2,1,0:T(8,128)S(1)}, f32[4,128,128]{2,1,0:T(8,128)S(1)}, u32[]{:S(2)}, u32[]{:S(2)}) collective-permute-start(f32[4,128,128]{2,1,0:T(8,128)S(1)} %get-tuple-element.145.refs_2_), channel_id=1, source_target_pairs={{0,16},{4,20},{8,24},{12,28},{16,0},{20,4},{24,8},{28,12},{1,17},{... | collective-permute-start | bytes 786440 | tf_op jit(solution)/shard_map/ppermute | solution.py:709
  45.2 7.4 %grad_query.1 = (f32[2,16,256,128]{3,2,1,0:T(8,128)S(1)}, bf16[2,16,256,256]{3,2,1,0:T(8,128)(2,1)S(1)}, bf16[512,16,128]{2,1,0:T(8,128)(2,1)}) custom-call(f32[8,128]{1,0:T(8,128)S(1)} %broadcast_in_dim.2.place_ref, f32[16,128]{1,0:T(8,128)S(1)} %get-tuple-element.92.refs_0_.gain_ref, f32[2,512]{1,0:T(2,128)S(1)} %add.16.sums_ref, ...), custom_call_target="tpu_custom_call" | custom-call | flops 1610612736 | bytes 12582912 | tf_op jit(solution)/shard_map/grad_query/pallas_call | solution.py:557
  52.7 0.8 %collective-permute-start.12 = (f32[4,128,128]{2,1,0:T(8,128)S(1)}, f32[4,128,128]{2,1,0:T(8,128)S(1)}, u32[]{:S(2)}, u32[]{:S(2)}) collective-permute-start(f32[4,128,128]{2,1,0:T(8,128)S(1)} %get-tuple-element.166), channel_id=1, source_target_pairs={{0,16},{4,20},{8,24},{12,28},{16,0},{20,4},{24,8},{28,12},{1,17},{... | collective-permute-start | bytes 786440 | tf_op jit(solution)/shard_map/ppermute | solution.py:709
  53.6 1.1 %collective-permute-start.13 = (f32[4,128,128]{2,1,0:T(8,128)S(1)}, f32[4,128,128]{2,1,0:T(8,128)S(1)}, u32[]{:S(2)}, u32[]{:S(2)}) collective-permute-start(f32[4,128,128]{2,1,0:T(8,128)S(1)} %get-tuple-element.162), channel_id=1, source_target_pairs={{0,8},{4,12},{8,0},{12,4},{16,24},{20,28},{24,16},{28,20},{1,9},{5... | collective-permute-start | bytes 786440 | tf_op jit(solution)/shard_map/ppermute | solution.py:709
  54.7 6.2 %grad_key_value.1 = (f32[2,16,256,128]{3,2,1,0:T(8,128)S(1)}, f32[2,16,256,128]{3,2,1,0:T(8,128)S(1)}, bf16[512,16,128]{2,1,0:T(8,128)(2,1)}) custom-call(f32[8,128]{1,0:T(8,128)S(1)} %broadcast_in_dim.2.place_ref, bf16[2,16,256,256]{3,2,1,0:T(8,128)(2,1)S(1)} %get-tuple-element.154.gs_ref, bf16[16,256,256]{2,1,0:T(8,128)(2,1)S(1)} %get-tuple-element.155.w0, ...), custom_call_target="tpu_custom_call" | custom-call | flops 1610612736 | bytes 31457280 | tf_op jit(solution)/shard_map/grad_key_value/pallas_call | solution.py:607
  61.4 1.5 %finish_own.1 = (f32[2,16,256,128]{3,2,1,0:T(8,128)S(1)}, f32[2,16,256,128]{3,2,1,0:T(8,128)S(1)}) custom-call(f32[2,16,128]{2,1,0:T(8,128)S(1)} %get-tuple-element.146.ends_ref.refs_0_, f32[8,128,128]{2,1,0:T(8,128)S(1)} %get-tuple-element.170.refs_1_, bf16[2,16,256,128]{3,2,1,0:T(8,128)(2,1)S(1)} %get-tuple-element.95.kh.refs_2_, ...), custom_call_target="tpu_custom_call" | custom-call | flops 536870912 | bytes 8388608 | tf_op jit(solution)/shard_map/finish_own/pallas_call | solution.py:671
  62.8 0.4 collective-permute-done.14.state_ref
  63.3 4.3 %finish_other.1 = (bf16[512,16,128]{2,1,0:T(8,128)(2,1)}, bf16[512,16,128]{2,1,0:T(8,128)(2,1)}, f32[2,16,256,128]{3,2,1,0:T(8,128)S(1)}, f32[2,16,256,128]{3,2,1,0:T(8,128)S(1)}) custom-call(f32[8,128]{1,0:T(8,128)S(1)} %broadcast_in_dim.2.place_ref, ...), custom_call_target="tpu_custom_call", output_to_operand_aliasing={{2}: (1, {}), {3}: (2, {})} | custom-call | flops 536870912 | bytes 8388608 | tf_op jit(solution)/shard_map/finish_other/pallas_call | solution.py:686
  (24 shorter events, 1.6 us)
Async XLA Ops:
  6.0 2.1 %collective-permute-start = (f32[8,136,128]{2,1,0:T(8,128)S(1)}, f32[8,136,128]{2,1,0:T(8,128)S(1)}, u32[]{:S(2)}, u32[]{:S(2)}) collective-permute-start(f32[8,136,128]{2,1,0:T(8,128)S(1)} %get-tuple-element.94), channel_id=1, source_target_pairs={{0,4},{4,0},{8,12},{12,8},{16,20},{20,16},{24,28},{28,24},{1,5},{5... | collective-permute-start | bytes 1671176 | tf_op jit(solution)/shard_map/ppermute | solution.py:709
  8.2 11.2 %collective-permute-start.1 = (f32[4,136,128]{2,1,0:T(8,128)S(1)}, f32[4,136,128]{2,1,0:T(8,128)S(1)}, u32[]{:S(2)}, u32[]{:S(2)}) collective-permute-start(f32[4,136,128]{2,1,0:T(8,128)S(1)} %get-tuple-element.101.refs_4_), channel_id=1, source_target_pairs={{0,8},{4,12},{8,0},{12,4},{16,24},{20,28},{24,16},{28,20},{1,9},{5... | collective-permute-start | bytes 835592 | tf_op jit(solution)/shard_map/ppermute | solution.py:709
  11.1 8.3 %collective-permute-start.2 = (f32[4,128,128]{2,1,0:T(8,128)S(1)}, f32[4,128,128]{2,1,0:T(8,128)S(1)}, u32[]{:S(2)}, u32[]{:S(2)}) collective-permute-start(f32[4,128,128]{2,1,0:T(8,128)S(1)} %get-tuple-element.102.refs_5_), channel_id=1, source_target_pairs={{0,16},{4,20},{8,24},{12,28},{16,0},{20,4},{24,8},{28,12},{1,17},{... | collective-permute-start | bytes 786440 | tf_op jit(solution)/shard_map/ppermute | solution.py:709
  12.6 6.7 %collective-permute-start.3 = (f32[8,128]{1,0:T(8,128)S(1)}, f32[8,128]{1,0:T(8,128)S(1)}, u32[]{:S(2)}, u32[]{:S(2)}) collective-permute-start(f32[8,128]{1,0:T(8,128)S(1)} %get-tuple-element.100.refs_2_), channel_id=1, source_target_pairs={{0,24},{4,28},{8,16},{12,20},{16,8},{20,12},{24,0},{28,4},{1,25},{... | collective-permute-start | bytes 12296 | tf_op jit(solution)/shard_map/ppermute | solution.py:709
  19.4 7.3 %collective-permute-start.4 = (f32[4,128,128]{2,1,0:T(8,128)S(1)}, f32[4,128,128]{2,1,0:T(8,128)S(1)}, u32[]{:S(2)}, u32[]{:S(2)}) collective-permute-start(f32[4,128,128]{2,1,0:T(8,128)S(1)} %get-tuple-element.113), channel_id=1, source_target_pairs={{0,16},{4,20},{8,24},{12,28},{16,0},{20,4},{24,8},{28,12},{1,17},{... | collective-permute-start | bytes 786440 | tf_op jit(solution)/shard_map/ppermute | solution.py:709
  20.9 6.9 %collective-permute-start.5 = (f32[4,128,128]{2,1,0:T(8,128)S(1)}, f32[4,128,128]{2,1,0:T(8,128)S(1)}, u32[]{:S(2)}, u32[]{:S(2)}) collective-permute-start(f32[4,128,128]{2,1,0:T(8,128)S(1)} %get-tuple-element.114), channel_id=1, source_target_pairs={{0,8},{4,12},{8,0},{12,4},{16,24},{20,28},{24,16},{28,20},{1,9},{5... | collective-permute-start | bytes 786440 | tf_op jit(solution)/shard_map/ppermute | solution.py:709
  28.0 2.0 %collective-permute-start.6 = (f32[8,128,128]{2,1,0:T(8,128)S(1)}, f32[8,128,128]{2,1,0:T(8,128)S(1)}, u32[]{:S(2)}, u32[]{:S(2)}) collective-permute-start(f32[8,128,128]{2,1,0:T(8,128)S(1)} %get-tuple-element.121), channel_id=1, source_target_pairs={{0,4},{4,0},{8,12},{12,8},{16,20},{20,16},{24,28},{28,24},{1,5},{5... | collective-permute-start | bytes 1572872 | tf_op jit(solution)/shard_map/ppermute | solution.py:709
  31.6 3.6 %collective-permute-start.7 = (f32[2,512]{1,0:T(2,128)S(1)}, f32[2,512]{1,0:T(2,128)S(1)}, u32[]{:S(2)}, u32[]{:S(2)}) collective-permute-start(f32[2,512]{1,0:T(2,128)S(1)} %get-tuple-element.131.first_ref), channel_id=1, source_target_pairs={{0,1},{1,0},{2,3},{3,2},{4,5},{5,4},{6,7},{7,6},{8,9},{9,8},{10,11... | collective-permute-start | bytes 12296 | tf_op jit(solution)/shard_map/ppermute | solution.py:709
  35.3 4.5 %collective-permute-start.8 = (f32[2,512]{1,0:T(2,128)S(1)}, f32[2,512]{1,0:T(2,128)S(1)}, u32[]{:S(2)}, u32[]{:S(2)}) collective-permute-start(f32[2,512]{1,0:T(2,128)S(1)} %add.15.first_ref), channel_id=1, source_target_pairs={{0,2},{1,3},{2,0},{3,1},{4,6},{5,7},{6,4},{7,5},{8,10},{9,11},{10,... | collective-permute-start | bytes 12296 | tf_op jit(solution)/shard_map/ppermute | solution.py:709
  40.9 2.0 %collective-permute-start.9 = (f32[8,128,128]{2,1,0:T(8,128)S(1)}, f32[8,128,128]{2,1,0:T(8,128)S(1)}, u32[]{:S(2)}, u32[]{:S(2)}) collective-permute-start(f32[8,128,128]{2,1,0:T(8,128)S(1)} %get-tuple-element.142), channel_id=1, source_target_pairs={{0,4},{4,0},{8,12},{12,8},{16,20},{20,16},{24,28},{28,24},{1,5},{5... | collective-permute-start | bytes 1572872 | tf_op jit(solution)/shard_map/ppermute | solution.py:709
  43.0 9.6 %collective-permute-start.10 = (f32[4,128,128]{2,1,0:T(8,128)S(1)}, f32[4,128,128]{2,1,0:T(8,128)S(1)}, u32[]{:S(2)}, u32[]{:S(2)}) collective-permute-start(f32[4,128,128]{2,1,0:T(8,128)S(1)} %get-tuple-element.158.refs_1_), channel_id=1, source_target_pairs={{0,8},{4,12},{8,0},{12,4},{16,24},{20,28},{24,16},{28,20},{1,9},{5... | collective-permute-start | bytes 786440 | tf_op jit(solution)/shard_map/ppermute | solution.py:709
  44.0 8.7 %collective-permute-start.11 = (f32[4,128,128]{2,1,0:T(8,128)S(1)}, f32[4,128,128]{2,1,0:T(8,128)S(1)}, u32[]{:S(2)}, u32[]{:S(2)}) collective-permute-start(f32[4,128,128]{2,1,0:T(8,128)S(1)} %get-tuple-element.145.refs_2_), channel_id=1, source_target_pairs={{0,16},{4,20},{8,24},{12,28},{16,0},{20,4},{24,8},{28,12},{1,17},{... | collective-permute-start | bytes 786440 | tf_op jit(solution)/shard_map/ppermute | solution.py:709
  52.7 8.1 %collective-permute-start.12 = (f32[4,128,128]{2,1,0:T(8,128)S(1)}, f32[4,128,128]{2,1,0:T(8,128)S(1)}, u32[]{:S(2)}, u32[]{:S(2)}) collective-permute-start(f32[4,128,128]{2,1,0:T(8,128)S(1)} %get-tuple-element.166), channel_id=1, source_target_pairs={{0,16},{4,20},{8,24},{12,28},{16,0},{20,4},{24,8},{28,12},{1,17},{... | collective-permute-start | bytes 786440 | tf_op jit(solution)/shard_map/ppermute | solution.py:709
  53.6 7.5 %collective-permute-start.13 = (f32[4,128,128]{2,1,0:T(8,128)S(1)}, f32[4,128,128]{2,1,0:T(8,128)S(1)}, u32[]{:S(2)}, u32[]{:S(2)}) collective-permute-start(f32[4,128,128]{2,1,0:T(8,128)S(1)} %get-tuple-element.162), channel_id=1, source_target_pairs={{0,8},{4,12},{8,0},{12,4},{16,24},{20,28},{24,16},{28,20},{1,9},{5... | collective-permute-start | bytes 786440 | tf_op jit(solution)/shard_map/ppermute | solution.py:709
  61.3 2.0 %collective-permute-start.14 = (f32[8,128,128]{2,1,0:T(8,128)S(1)}, f32[8,128,128]{2,1,0:T(8,128)S(1)}, u32[]{:S(2)}, u32[]{:S(2)}) collective-permute-start(f32[8,128,128]{2,1,0:T(8,128)S(1)} %get-tuple-element.174), channel_id=1, source_target_pairs={{0,4},{4,0},{8,12},{12,8},{16,20},{20,16},{24,28},{28,24},{1,5},{5... | collective-permute-start | bytes 1572872 | tf_op jit(solution)/shard_map/ppermute | solution.py:709

commit v11 on v10

--- a/solution.py
+++ b/solution.py
@@ -155,7 +155,7 @@
                 dst[local + j, pl.ds(at, 2 * TILE)] = both.astype(BF16)
         return carry
 
-    lax.fori_loop(0, tok // (2 * TILE), step, 0, unroll=2)
+    lax.fori_loop(0, tok // (2 * TILE), step, 0, unroll=4)
 
 
 def from_heads(block, src, start, tok, upper):
@@ -171,7 +171,7 @@
             block[at + j] = jnp.concatenate([part[j] for part in parts], axis=0).astype(BF16)
         return carry
 
-    lax.fori_loop(0, tok // TILE, step, 0, unroll=2)
+    lax.fori_loop(0, tok // TILE, step, 0, unroll=4)
 
 
 def is_set(place_ref, which):
@@ -332,7 +332,7 @@
             for at, quarter in enumerate(quarters):
                 decays_ref[h, at] = quarter
             weights = causal(dot_rows(query, kh[index, h]), quarters)
-            w_ref[h] = weights
+            w_ref[h] = weights.T
             inner = dot(weights, vh[index, h])
             columns = jnp.exp(columns)
             columns_ref[h] = columns
@@ -592,9 +592,9 @@
         state = (second_own, second_send)[part][i]
         g0, g1 = ((own0, own1), (other0, other1))[part]
         dk[0, h] = transposed_dot(gs_ref[0, h], q0[h]) + columns * times_state_t(vh[0, h], state)
-        dv[0, h] = transposed_dot(w0[h], g0[i]) + columns * times_state(kh[0, h], state)
+        dv[0, h] = dot(w0[h], g0[i]) + columns * times_state(kh[0, h], state)
         dk[1, h] = transposed_dot(gs_ref[1, h], q1[h])
-        dv[1, h] = transposed_dot(w1[h], g1[i])
+        dv[1, h] = dot(w1[h], g1[i])
 
     each_half(second_own.shape[0], 2, one)
     for copy in copies:
@@ -759,25 +759,35 @@
     mix_total(bits, own, got, decay(OWN), decay(PARTNER), *outputs)
 
 
-def mix_next(bits, decay, totals, gots, outputs):
+def mix_next_row(bits, chip, row, total, got, out):
+    right = bits[1]
+    for i in range(out.shape[0]):
+        scale_total = jnp.where(right, 1.0, row(i))
+        scale_got = jnp.where(right, chip(i), 1.0)
+        out[i] = scale_total * total[i, :HD] + scale_got * got[i, :HD]
+
+
+def mix_next_column(bits, chip, corner, total, got, out):
     _, right, low = bits
-    quarter = totals[1].shape[0]
-    for i in range(quarter):
-        h = i
-        scale_total = jnp.where(right, 1.0, decay(ROW, h))
-        scale_got = jnp.where(right, decay(CHIP, h), 1.0)
-        outputs[0][i] = scale_total * totals[0][i, :HD] + scale_got * gots[0][i, :HD]
-        h = quarter + i
+    for i in range(out.shape[0]):
         scale_total = jnp.where(low & right, 0.0, 1.0)
-        corner = jnp.where(right, 1.0, decay(CHIP, h) * decay(CORNER, h))
-        scale_got = jnp.where(low, corner, 0.0)
-        outputs[1][i] = scale_total * totals[1][i] + scale_got * gots[1][i]
-
-
-def mix_next_first(bits, arrays, outputs):
-    own, got, chip, corner, first, second, one_a, one_b = arrays
-    table = outputs[2]
-    quarter = second.shape[0]
+        scale_got = jnp.where(low, jnp.where(right, 1.0, chip(i) * corner(i)), 0.0)
+        out[i] = scale_total * total[i] + scale_got * got[i]
+
+
+def lines(ref, first=0):
+    return lambda i: ref[first + i : first + i + 1]
+
+
+def mix_next_row_first(bits, arrays, outputs):
+    chip, total, got = arrays
+    mix_next_row(bits, lines(chip), lambda i: got[i, HD : HD + 1], total, got, *outputs)
+
+
+def mix_next_column_first(bits, arrays, outputs):
+    own, got, chip, corner, one_a, total, one_b = arrays
+    out, table = outputs
+    quarter = total.shape[0]
     for h in range(2 * quarter):
         place = HD + (TILE // 2) * (h // quarter)
         table[OWN, h : h + 1] = own[h, HD : HD + 1]
@@ -785,14 +795,19 @@
         table[ROW, h : h + 1] = one_a[h % quarter, place : place + 1]
     table[CHIP] = chip[...]
     table[CORNER] = corner[...]
-    decay = lambda which, h: table[which, h : h + 1]
-    mix_next(bits, decay, (first, second), (one_a, one_b), outputs[:2])
-
-
-def mix_next_again(bits, arrays, outputs):
-    table, first, second, one_a, one_b = arrays
-    decay = lambda which, h: table[which, h : h + 1]
-    mix_next(bits, decay, (first, second), (one_a, one_b), outputs)
+    mix_next_column(bits, lines(chip, quarter), lines(corner, quarter), total, one_b, out)
+
+
+def mix_next_row_again(bits, arrays, outputs):
+    table, total, got = arrays
+    mix_next_row(bits, lines(table.at[CHIP]), lines(table.at[ROW]), total, got, *outputs)
+
+
+def mix_next_column_again(bits, arrays, outputs):
+    table, total, got = arrays
+    quarter = total.shape[0]
+    chip, corner = (lines(table.at[which], quarter) for which in (CHIP, CORNER))
+    mix_next_column(bits, chip, corner, total, got, *outputs)
 
 
 def mix_enter(bits, arrays, outputs):
@@ -845,15 +860,23 @@
     if table is None:
         corner = swap(chip, "seq", 6)
         one_a, one_b, corner = work(1, second, (one_a, one_b, corner))
-        next_a, next_b, table = mix(
-            mix_next_first, backward, place, (own, got, chip, corner, first, second, one_a, one_b),
-            (states, states, (5, half, HD)), name + "_next",
+        (next_a,) = mix(
+            mix_next_row_first, backward, place, (chip, first, one_a), (states,), name + "_row"
+        )
+        one_b, corner = follows((one_b, corner), next_a)
+        next_b, table = mix(
+            mix_next_column_first, backward, place,
+            (own, got, chip, corner, one_a, second, one_b), (states, (5, half, HD)),
+            name + "_column",
         )
     else:
         one_a, one_b = work(1, second, (one_a, one_b))
-        next_a, next_b = mix(
-            mix_next_again, backward, place, (table, first, second, one_a, one_b), (states, states),
-            name + "_next",
+        (next_a,) = mix(
+            mix_next_row_again, backward, place, (table, first, one_a), (states,), name + "_row"
+        )
+        (next_b,) = mix(
+            mix_next_column_again, backward, place, (table, second, follows(one_b, next_a)),
+            (states,), name + "_column",
         )
     two_a, two_b = swap(next_a, "seq", 4), swap(next_b, "seq", 2)
     two_a, two_b = work(2, next_b, (two_a, two_b))

time: 67.9 us -> 67.4 us (level)
  Pallas kernels: 42.2 us -> 41.5 us
where the time goes in v11:
time: 67.4 us; the launch traced here: 67.2 us
  Pallas kernels  41.5 us (62%)
  starting transfers between devices  15.6 us (23%)
  waiting for transfers between devices  8.92 us (13%)
  between operations  1.02 us (2%)
    ppermute x15, starting transfers between devices, swap(): return lax.ppermute(value, axis, [(i, i ^ bit) for i in range(count)])  15.6 us
    ppermute x15, waiting for transfers between devices, swap(): return lax.ppermute(value, axis, [(i, i ^ bit) for i in range(count)])  8.92 us
    pallas_call x2, Pallas kernels, intra(): pl.pallas_call(kernel, in_specs=[NEAR] * 8 + [FAR, FAR] * ahead, out_spec...  7.6 us
    pallas_call x1, Pallas kernels, grad_query(): pl.pallas_call(grad_q_kernel, in_specs=[NEAR] * 22, out_specs=[NEAR, NEAR...  7.25 us
    pallas_call x1, Pallas kernels, grad_key_value(): pl.pallas_call(grad_kv_kernel, in_specs=[NEAR] * 16, out_specs=[NEAR, NEA...  6 us
    pallas_call x1, Pallas kernels, state_to_send(): pl.pallas_call(state_kernel, in_specs=[NEAR, FAR, FAR, FAR, FAR], out_spe...  5.04 us
    pallas_call x1, Pallas kernels, finish_other(): pl.pallas_call(finish_other_kernel, in_specs=[NEAR] * 10, out_specs=[FAR,...  4.06 us
    pallas_call x2, Pallas kernels, attend(): pl.pallas_call(functools.partial(attend_kernel, part), in_specs=[NEAR] *...  2.9 us
  transfers between devices with their start and end apart: 15, of which 9 were waited for; matrix products, arithmetic and copies ran while one was open for 0% of the time, Pallas kernels for 43%

profile of v11, /device:TPU:0, one launch (start us, length us, event | category | flops | bytes accessed | tf_op | source)
XLA Modules:
  0.0 67.2 jit_solution(5914773916115775662)
XLA Ops:
  0.8 5.0 %state_to_send.1 = (f32[8,136,128]{2,1,0:T(8,128)S(1)}, f32[8,128,128]{2,1,0:T(8,128)S(1)}, bf16[2,16,256,128]{3,2,1,0:T(8,128)(2,1)S(1)}, bf16[2,16,256,128]{3,...) custom-call(f32[8,128]{1,0:T(8,128)S(1)} %broadcast_in_dim.2.place_r, ...), custom_call_target="tpu_custom_call" | custom-call | flops 134217728 | bytes 8388608 | tf_op jit(solution)/shard_map/state_to_send/pallas_call | solution.py:255
  5.9 0.5 collective-permute-start
  6.4 1.6 %own_state.1 = (f32[8,136,128]{2,1,0:T(8,128)S(1)}, f32[8,128,128]{2,1,0:T(8,128)S(1)}, bf16[256,16,128]{2,1,0:T(8,128)(2,1)S(1)}, bf16[256,16,128]{2,1,0:T(8,128)(2,1)S(1)}) custom-call(bf16[2,16,256,128]{3,2,1,0:T(8,128)(2,1)S(1)} %get-tuple-element.95.kh.refs_2_, bf16[2,16,256,128]{3,2,1,0:T(8,128)(2,1)S(1)} %get-tuple-element.96.vh.refs_3_, ...), custom_call_target="tpu_custom_call" | custom-call | flops 134217728 | bytes 2097152 | tf_op jit(solution)/shard_map/own_state/pallas_call | solution.py:301
  8.1 2.9 %collective-permute-start.1 = (f32[4,136,128]{2,1,0:T(8,128)S(1)}, f32[4,136,128]{2,1,0:T(8,128)S(1)}, u32[]{:S(2)}, u32[]{:S(2)}) collective-permute-start(f32[4,136,128]{2,1,0:T(8,128)S(1)} %get-tuple-element.101.refs_1_), channel_id=1, source_target_pairs={{0,8},{4,12},{8,0},{12,4},{16,24},{20,28},{24,16},{28,20},{1,9},{5... | collective-permute-start | bytes 835592 | tf_op jit(solution)/shard_map/ppermute | solution.py:709
  11.0 1.5 %collective-permute-start.2 = (f32[4,128,128]{2,1,0:T(8,128)S(1)}, f32[4,128,128]{2,1,0:T(8,128)S(1)}, u32[]{:S(2)}, u32[]{:S(2)}) collective-permute-start(f32[4,128,128]{2,1,0:T(8,128)S(1)} %get-tuple-element.102.refs_5_), channel_id=1, source_target_pairs={{0,16},{4,20},{8,24},{12,28},{16,0},{20,4},{24,8},{28,12},{1,17},{... | collective-permute-start | bytes 786440 | tf_op jit(solution)/shard_map/ppermute | solution.py:709
  12.5 3.7 %intra_0.1 = (bf16[16,256,128]{2,1,0:T(8,128)(2,1)S(1)}, bf16[16,256,128]{2,1,0:T(8,128)(2,1)S(1)}, bf16[16,256,256]{2,1,0:T(8,128)(2,1)S(1)}, f32[16,3,128,128]...) custom-call(f32[8,128]{1,0:T(8,128)S(1)} %broadcast_in_dim.2.place_r, ...), custom_call_target="tpu_custom_call" | custom-call | flops 1073741824 | bytes 10485760 | tf_op jit(solution)/shard_map/intra_0/pallas_call | solution.py:349
  16.3 3.0 %collective-permute-done.3.refs_3_ = f32[8,128]{1,0:T(8,128)S(1)} collective-permute-done((f32[8,128]{1,0:T(8,128)S(1)}, f32[8,128]{1,0:T(8,128)S(1)}, u32[]{:S(2)}, u32[]{:S(2)}) %collective-permute-start.3) | collective-permute-done | bytes 4128 | tf_op jit(solution)/shard_map/ppermute | solution.py:709
  19.4 1.6 %collective-permute-start.5 = (f32[4,128,128]{2,1,0:T(8,128)S(1)}, f32[4,128,128]{2,1,0:T(8,128)S(1)}, u32[]{:S(2)}, u32[]{:S(2)}) collective-permute-start(f32[4,128,128]{2,1,0:T(8,128)S(1)} %get-tuple-element.115), channel_id=1, source_target_pairs={{0,8},{4,12},{8,0},{12,4},{16,24},{20,28},{24,16},{28,20},{1,9},{5... | collective-permute-start | bytes 786440 | tf_op jit(solution)/shard_map/ppermute | solution.py:709
  20.9 0.5 collective-permute-start.4
  21.4 3.9 %intra_1.1 = (bf16[16,256,128]{2,1,0:T(8,128)(2,1)S(1)}, bf16[16,256,128]{2,1,0:T(8,128)(2,1)S(1)}, bf16[16,256,256]{2,1,0:T(8,128)(2,1)S(1)}, f32[16,3,128,128]...) custom-call(f32[8,128]{1,0:T(8,128)S(1)} %broadcast_in_dim.2.place_ref, ...), custom_call_target="tpu_custom_call" | custom-call | flops 1073741824 | bytes 10485760 | tf_op jit(solution)/shard_map/intra_1/pallas_call | solution.py:349
  25.3 1.4 %collective-permute-done.5.refs_6_ = f32[4,128,128]{2,1,0:T(8,128)S(1)} collective-permute-done((f32[4,128,128]{2,1,0:T(8,128)S(1)}, f32[4,128,128]{2,1,0:T(8,128)S(1)}, u32[]{:S(2)}, u32[]{:S(2)}) %collective-permute-start.5) | collective-permute-done | bytes 262176 | tf_op jit(solution)/shard_map/ppermute | solution.py:709
  26.6 1.2 %collective-permute-done.4.refs_5_ = f32[4,128,128]{2,1,0:T(8,128)S(1)} collective-permute-done((f32[4,128,128]{2,1,0:T(8,128)S(1)}, f32[4,128,128]{2,1,0:T(8,128)S(1)}, u32[]{:S(2)}, u32[]{:S(2)}) %collective-permute-start.4) | collective-permute-done | bytes 262176 | tf_op jit(solution)/shard_map/ppermute | solution.py:709
  28.1 1.3 %attend_0.1 = (f32[8,256,128]{2,1,0:T(8,128)S(1)}, f32[8,256,128]{2,1,0:T(8,128)S(1)}, f32[2,2,256,128]{3,2,1,0:T(8,128)S(1)}) custom-call(f32[16,128]{1,0:T(8,128)S(1)} %get-tuple-element.92.refs_0_.gain_ref, f32[8,128,128]{2,1,0:T(8,128)S(1)} %get-tuple-element.123.refs_1_.keep_ref, bf16[16,256,128]{2,1,0:T(8,128)(2,1)S(1)} %get-tuple-element.133.refs_2_.q0, ...), custom_call_target="tpu_custom_call" | custom-call | flops 268435456 | bytes 8388608 | tf_op jit(solution)/shard_map/attend_0/pallas_call | solution.py:411
  29.4 0.6 collective-permute-done.6.refs_1_.recv_ref
  30.0 1.6 %attend_1.1 = (f32[8,256,128]{2,1,0:T(8,128)S(1)}, f32[8,256,128]{2,1,0:T(8,128)S(1)}, f32[2,512]{1,0:T(2,128)S(1)}) custom-call(f32[16,128]{1,0:T(8,128)S(1)} %get-tuple-element.92.refs_0_.gain_ref, f32[8,128,128]{2,1,0:T(8,128)S(1)} %collective-permute-done.6.refs_1_.recv_ref, bf16[16,256,128]{2,1,0:T(8,128)(2,1)S(1)} %get-tuple-element.133.refs_2_.q0, ...), custom_call_target="tpu_custom_call" | custom-call | flops 268435456 | bytes 8388608 | tf_op jit(solution)/shard_map/attend_1/pallas_call | solution.py:411
  31.6 1.6 %collective-permute-start.7 = (f32[2,512]{1,0:T(2,128)S(1)}, f32[2,512]{1,0:T(2,128)S(1)}, u32[]{:S(2)}, u32[]{:S(2)}) collective-permute-start(f32[2,512]{1,0:T(2,128)S(1)} %get-tuple-element.132.first_ref), channel_id=1, source_target_pairs={{0,1},{1,0},{2,3},{3,2},{4,5},{5,4},{6,7},{7,6},{8,9},{9,8},{10,11... | collective-permute-start | bytes 12296 | tf_op jit(solution)/shard_map/ppermute | solution.py:709
  33.2 0.9 %scaled_queries.1 = (bf16[2,16,128,256]{3,2,1,0:T(8,128)(2,1)S(1)}, f32[2,16,128]{2,1,0:T(8,128)S(1)}) custom-call(f32[2,16,256]{2,1,0:T(8,128)S(1)} %get-tuple-element.137.cum.cum_ref, bf16[16,256,128]{2,1,0:T(8,128)(2,1)S(1)} %get-tuple-element.133.refs_2_.q0, bf16[16,256,128]{2,1,0:T(8,128)(2,1)S(1)} %get-tuple-element.119.refs_3_.q1), custom_call_target="tpu_custom_call" | custom-call | flops 2097152 | bytes 4194304 | tf_op jit(solution)/shard_map/scaled_queries/pallas_call | solution.py:437
  34.2 1.1 %collective-permute-done.7.second_ref = f32[2,512]{1,0:T(2,128)S(1)} collective-permute-done((f32[2,512]{1,0:T(2,128)S(1)}, f32[2,512]{1,0:T(2,128)S(1)}, u32[]{:S(2)}, u32[]{:S(2)}) %collective-permute-start.7) | collective-permute-done | bytes 4128 | tf_op jit(solution)/shard_map/ppermute | solution.py:709
  35.3 2.6 %collective-permute-start.8 = (f32[2,512]{1,0:T(2,128)S(1)}, f32[2,512]{1,0:T(2,128)S(1)}, u32[]{:S(2)}, u32[]{:S(2)}) collective-permute-start(f32[2,512]{1,0:T(2,128)S(1)} %add.15.first_ref), channel_id=1, source_target_pairs={{0,2},{1,3},{2,0},{3,1},{4,6},{5,7},{6,4},{7,5},{8,10},{9,11},{10,... | collective-permute-start | bytes 12296 | tf_op jit(solution)/shard_map/ppermute | solution.py:709
  37.9 1.6 %remaining_decay.1.remaining_ref.refs_4_ = f32[2,16,256,128]{3,2,1,0:T(8,128)S(1)} custom-call(f32[2,16,256]{2,1,0:T(8,128)S(1)} %get-tuple-element.137.cum.cum_ref), custom_call_target="tpu_custom_call" | custom-call | flops 1048576 | bytes 4194304 | tf_op jit(solution)/shard_map/remaining_decay/pallas_call | solution.py:459
  39.8 1.1 %norm_grad_1.1 = (f32[8,128,128]{2,1,0:T(8,128)S(1)}, f32[8,128,128]{2,1,0:T(8,128)S(1)}, bf16[8,256,128]{2,1,0:T(8,128)(2,1)S(1)}, bf16[8,256,128]{2,1,0:T(8,128)(2,1)S(1)}) custom-call(f32[2,16,128]{2,1,0:T(8,128)S(1)} %get-tuple-element.147.ends_ref.refs_0_, f32[16,128]{1,0:T(8,128)S(1)} %get-tuple-element.92.refs_0_.gain_ref, ...), custom_call_target="tpu_custom_call" | custom-call | flops 134217728 | bytes 7340032 | tf_op jit(solution)/shard_map/norm_grad_1/pallas_call | solution.py:504
  41.0 1.2 %norm_grad_0.1 = (f32[8,128,128]{2,1,0:T(8,128)S(1)}, f32[8,128,128]{2,1,0:T(8,128)S(1)}, bf16[8,256,128]{2,1,0:T(8,128)(2,1)S(1)}, bf16[8,256,128]{2,1,0:T(8,128)(2,1)S(1)}) custom-call(f32[2,16,128]{2,1,0:T(8,128)S(1)} %get-tuple-element.147.ends_ref.refs_0_, f32[16,128]{1,0:T(8,128)S(1)} %get-tuple-element.92.refs_0_.gain_ref, ...), custom_call_target="tpu_custom_call" | custom-call | flops 134217728 | bytes 7340032 | tf_op jit(solution)/shard_map/norm_grad_0/pallas_call | solution.py:504
  42.2 0.7 %collective-permute-done.9.refs_2_ = f32[8,128,128]{2,1,0:T(8,128)S(1)} collective-permute-done((f32[8,128,128]{2,1,0:T(8,128)S(1)}, f32[8,128,128]{2,1,0:T(8,128)S(1)}, u32[]{:S(2)}, u32[]{:S(2)}) %collective-permute-start.9) | collective-permute-done | bytes 524320 | tf_op jit(solution)/shard_map/ppermute | solution.py:709
  43.0 0.6 collective-permute-start.10
  43.6 1.4 %collective-permute-start.11 = (f32[4,128,128]{2,1,0:T(8,128)S(1)}, f32[4,128,128]{2,1,0:T(8,128)S(1)}, u32[]{:S(2)}, u32[]{:S(2)}) collective-permute-start(f32[4,128,128]{2,1,0:T(8,128)S(1)} %get-tuple-element.146.refs_1_), channel_id=1, source_target_pairs={{0,16},{4,20},{8,24},{12,28},{16,0},{20,4},{24,8},{28,12},{1,17},{... | collective-permute-start | bytes 786440 | tf_op jit(solution)/shard_map/ppermute | solution.py:709
  45.0 7.3 %grad_query.1 = (f32[2,16,256,128]{3,2,1,0:T(8,128)S(1)}, bf16[2,16,256,256]{3,2,1,0:T(8,128)(2,1)S(1)}, bf16[512,16,128]{2,1,0:T(8,128)(2,1)}) custom-call(f32[8,128]{1,0:T(8,128)S(1)} %broadcast_in_dim.2.place_ref, f32[16,128]{1,0:T(8,128)S(1)} %get-tuple-element.92.refs_0_.gain_ref, f32[2,512]{1,0:T(2,128)S(1)} %add.16.sums_ref, ...), custom_call_target="tpu_custom_call" | custom-call | flops 1610612736 | bytes 12582912 | tf_op jit(solution)/shard_map/grad_query/pallas_call | solution.py:557
  52.4 1.0 %collective-permute-start.13 = (f32[4,128,128]{2,1,0:T(8,128)S(1)}, f32[4,128,128]{2,1,0:T(8,128)S(1)}, u32[]{:S(2)}, u32[]{:S(2)}) collective-permute-start(f32[4,128,128]{2,1,0:T(8,128)S(1)} %later_column.1), channel_id=1, source_target_pairs={{0,8},{4,12},{8,0},{12,4},{16,24},{20,28},{24,16},{28,20},{1,9},{5... | collective-permute-start | bytes 786440 | tf_op jit(solution)/shard_map/ppermute | solution.py:709
  53.3 1.2 %collective-permute-start.12 = (f32[4,128,128]{2,1,0:T(8,128)S(1)}, f32[4,128,128]{2,1,0:T(8,128)S(1)}, u32[]{:S(2)}, u32[]{:S(2)}) collective-permute-start(f32[4,128,128]{2,1,0:T(8,128)S(1)} %later_row.1), channel_id=1, source_target_pairs={{0,16},{4,20},{8,24},{12,28},{16,0},{20,4},{24,8},{28,12},{1,17},{... | collective-permute-start | bytes 786440 | tf_op jit(solution)/shard_map/ppermute | solution.py:709
  54.6 6.0 %grad_key_value.1 = (f32[2,16,256,128]{3,2,1,0:T(8,128)S(1)}, f32[2,16,256,128]{3,2,1,0:T(8,128)S(1)}, bf16[512,16,128]{2,1,0:T(8,128)(2,1)}) custom-call(f32[8,128]{1,0:T(8,128)S(1)} %broadcast_in_dim.2.place_ref, bf16[2,16,256,256]{3,2,1,0:T(8,128)(2,1)S(1)} %get-tuple-element.155.gs_ref, bf16[16,256,256]{2,1,0:T(8,128)(2,1)S(1)} %get-tuple-element.156.w0, ...), custom_call_target="tpu_custom_call" | custom-call | flops 1610612736 | bytes 31457280 | tf_op jit(solution)/shard_map/grad_key_value/pallas_call | solution.py:607
  61.1 1.5 %finish_own.1 = (f32[2,16,256,128]{3,2,1,0:T(8,128)S(1)}, f32[2,16,256,128]{3,2,1,0:T(8,128)S(1)}) custom-call(f32[2,16,128]{2,1,0:T(8,128)S(1)} %get-tuple-element.147.ends_ref.refs_0_, f32[8,128,128]{2,1,0:T(8,128)S(1)} %get-tuple-element.170.refs_1_, bf16[2,16,256,128]{3,2,1,0:T(8,128)(2,1)S(1)} %get-tuple-element.95.kh.refs_2_, ...), custom_call_target="tpu_custom_call" | custom-call | flops 536870912 | bytes 8388608 | tf_op jit(solution)/shard_map/finish_own/pallas_call | solution.py:671
  62.5 0.4 collective-permute-done.14.state_ref
  63.0 4.1 %finish_other.1 = (bf16[512,16,128]{2,1,0:T(8,128)(2,1)}, bf16[512,16,128]{2,1,0:T(8,128)(2,1)}, f32[2,16,256,128]{3,2,1,0:T(8,128)S(1)}, f32[2,16,256,128]{3,2,1,0:T(8,128)S(1)}) custom-call(f32[8,128]{1,0:T(8,128)S(1)} %broadcast_in_dim.2.place_ref, ...), custom_call_target="tpu_custom_call", output_to_operand_aliasing={{2}: (1, {}), {3}: (2, {})} | custom-call | flops 536870912 | bytes 8388608 | tf_op jit(solution)/shard_map/finish_other/pallas_call | solution.py:686
  (26 shorter events, 1.6 us)
Async XLA Ops:
  5.9 2.1 %collective-permute-start = (f32[8,136,128]{2,1,0:T(8,128)S(1)}, f32[8,136,128]{2,1,0:T(8,128)S(1)}, u32[]{:S(2)}, u32[]{:S(2)}) collective-permute-start(f32[8,136,128]{2,1,0:T(8,128)S(1)} %get-tuple-element.94), channel_id=1, source_target_pairs={{0,4},{4,0},{8,12},{12,8},{16,20},{20,16},{24,28},{28,24},{1,5},{5... | collective-permute-start | bytes 1671176 | tf_op jit(solution)/shard_map/ppermute | solution.py:709
  8.1 11.2 %collective-permute-start.1 = (f32[4,136,128]{2,1,0:T(8,128)S(1)}, f32[4,136,128]{2,1,0:T(8,128)S(1)}, u32[]{:S(2)}, u32[]{:S(2)}) collective-permute-start(f32[4,136,128]{2,1,0:T(8,128)S(1)} %get-tuple-element.101.refs_1_), channel_id=1, source_target_pairs={{0,8},{4,12},{8,0},{12,4},{16,24},{20,28},{24,16},{28,20},{1,9},{5... | collective-permute-start | bytes 835592 | tf_op jit(solution)/shard_map/ppermute | solution.py:709
  11.0 8.3 %collective-permute-start.2 = (f32[4,128,128]{2,1,0:T(8,128)S(1)}, f32[4,128,128]{2,1,0:T(8,128)S(1)}, u32[]{:S(2)}, u32[]{:S(2)}) collective-permute-start(f32[4,128,128]{2,1,0:T(8,128)S(1)} %get-tuple-element.102.refs_5_), channel_id=1, source_target_pairs={{0,16},{4,20},{8,24},{12,28},{16,0},{20,4},{24,8},{28,12},{1,17},{... | collective-permute-start | bytes 786440 | tf_op jit(solution)/shard_map/ppermute | solution.py:709
  12.5 6.7 %collective-permute-start.3 = (f32[8,128]{1,0:T(8,128)S(1)}, f32[8,128]{1,0:T(8,128)S(1)}, u32[]{:S(2)}, u32[]{:S(2)}) collective-permute-start(f32[8,128]{1,0:T(8,128)S(1)} %get-tuple-element.100.refs_0_.refs_2_), channel_id=1, source_target_pairs={{0,24},{4,28},{8,16},{12,20},{16,8},{20,12},{24,0},{28,4},{1,25},{... | collective-permute-start | bytes 12296 | tf_op jit(solution)/shard_map/ppermute | solution.py:709
  19.4 7.3 %collective-permute-start.5 = (f32[4,128,128]{2,1,0:T(8,128)S(1)}, f32[4,128,128]{2,1,0:T(8,128)S(1)}, u32[]{:S(2)}, u32[]{:S(2)}) collective-permute-start(f32[4,128,128]{2,1,0:T(8,128)S(1)} %get-tuple-element.115), channel_id=1, source_target_pairs={{0,8},{4,12},{8,0},{12,4},{16,24},{20,28},{24,16},{28,20},{1,9},{5... | collective-permute-start | bytes 786440 | tf_op jit(solution)/shard_map/ppermute | solution.py:709
  20.9 6.9 %collective-permute-start.4 = (f32[4,128,128]{2,1,0:T(8,128)S(1)}, f32[4,128,128]{2,1,0:T(8,128)S(1)}, u32[]{:S(2)}, u32[]{:S(2)}) collective-permute-start(f32[4,128,128]{2,1,0:T(8,128)S(1)} %earlier_row.1), channel_id=1, source_target_pairs={{0,16},{4,20},{8,24},{12,28},{16,0},{20,4},{24,8},{28,12},{1,17},{... | collective-permute-start | bytes 786440 | tf_op jit(solution)/shard_map/ppermute | solution.py:709
  28.0 2.0 %collective-permute-start.6 = (f32[8,128,128]{2,1,0:T(8,128)S(1)}, f32[8,128,128]{2,1,0:T(8,128)S(1)}, u32[]{:S(2)}, u32[]{:S(2)}) collective-permute-start(f32[8,128,128]{2,1,0:T(8,128)S(1)} %get-tuple-element.122), channel_id=1, source_target_pairs={{0,4},{4,0},{8,12},{12,8},{16,20},{20,16},{24,28},{28,24},{1,5},{5... | collective-permute-start | bytes 1572872 | tf_op jit(solution)/shard_map/ppermute | solution.py:709
  31.6 3.6 %collective-permute-start.7 = (f32[2,512]{1,0:T(2,128)S(1)}, f32[2,512]{1,0:T(2,128)S(1)}, u32[]{:S(2)}, u32[]{:S(2)}) collective-permute-start(f32[2,512]{1,0:T(2,128)S(1)} %get-tuple-element.132.first_ref), channel_id=1, source_target_pairs={{0,1},{1,0},{2,3},{3,2},{4,5},{5,4},{6,7},{7,6},{8,9},{9,8},{10,11... | collective-permute-start | bytes 12296 | tf_op jit(solution)/shard_map/ppermute | solution.py:709
  35.3 4.5 %collective-permute-start.8 = (f32[2,512]{1,0:T(2,128)S(1)}, f32[2,512]{1,0:T(2,128)S(1)}, u32[]{:S(2)}, u32[]{:S(2)}) collective-permute-start(f32[2,512]{1,0:T(2,128)S(1)} %add.15.first_ref), channel_id=1, source_target_pairs={{0,2},{1,3},{2,0},{3,1},{4,6},{5,7},{6,4},{7,5},{8,10},{9,11},{10,... | collective-permute-start | bytes 12296 | tf_op jit(solution)/shard_map/ppermute | solution.py:709
  40.9 2.0 %collective-permute-start.9 = (f32[8,128,128]{2,1,0:T(8,128)S(1)}, f32[8,128,128]{2,1,0:T(8,128)S(1)}, u32[]{:S(2)}, u32[]{:S(2)}) collective-permute-start(f32[8,128,128]{2,1,0:T(8,128)S(1)} %get-tuple-element.143), channel_id=1, source_target_pairs={{0,4},{4,0},{8,12},{12,8},{16,20},{20,16},{24,28},{28,24},{1,5},{5... | collective-permute-start | bytes 1572872 | tf_op jit(solution)/shard_map/ppermute | solution.py:709
  43.0 9.2 %collective-permute-start.10 = (f32[4,128,128]{2,1,0:T(8,128)S(1)}, f32[4,128,128]{2,1,0:T(8,128)S(1)}, u32[]{:S(2)}, u32[]{:S(2)}) collective-permute-start(f32[4,128,128]{2,1,0:T(8,128)S(1)} %get-tuple-element.159.refs_1_), channel_id=1, source_target_pairs={{0,8},{4,12},{8,0},{12,4},{16,24},{20,28},{24,16},{28,20},{1,9},{5... | collective-permute-start | bytes 786440 | tf_op jit(solution)/shard_map/ppermute | solution.py:709
  43.6 8.6 %collective-permute-start.11 = (f32[4,128,128]{2,1,0:T(8,128)S(1)}, f32[4,128,128]{2,1,0:T(8,128)S(1)}, u32[]{:S(2)}, u32[]{:S(2)}) collective-permute-start(f32[4,128,128]{2,1,0:T(8,128)S(1)} %get-tuple-element.146.refs_1_), channel_id=1, source_target_pairs={{0,16},{4,20},{8,24},{12,28},{16,0},{20,4},{24,8},{28,12},{1,17},{... | collective-permute-start | bytes 786440 | tf_op jit(solution)/shard_map/ppermute | solution.py:709
  52.4 8.2 %collective-permute-start.13 = (f32[4,128,128]{2,1,0:T(8,128)S(1)}, f32[4,128,128]{2,1,0:T(8,128)S(1)}, u32[]{:S(2)}, u32[]{:S(2)}) collective-permute-start(f32[4,128,128]{2,1,0:T(8,128)S(1)} %later_column.1), channel_id=1, source_target_pairs={{0,8},{4,12},{8,0},{12,4},{16,24},{20,28},{24,16},{28,20},{1,9},{5... | collective-permute-start | bytes 786440 | tf_op jit(solution)/shard_map/ppermute | solution.py:709
  53.3 7.5 %collective-permute-start.12 = (f32[4,128,128]{2,1,0:T(8,128)S(1)}, f32[4,128,128]{2,1,0:T(8,128)S(1)}, u32[]{:S(2)}, u32[]{:S(2)}) collective-permute-start(f32[4,128,128]{2,1,0:T(8,128)S(1)} %later_row.1), channel_id=1, source_target_pairs={{0,16},{4,20},{8,24},{12,28},{16,0},{20,4},{24,8},{28,12},{1,17},{... | collective-permute-start | bytes 786440 | tf_op jit(solution)/shard_map/ppermute | solution.py:709
  61.0 2.0 %collective-permute-start.14 = (f32[8,128,128]{2,1,0:T(8,128)S(1)}, f32[8,128,128]{2,1,0:T(8,128)S(1)}, u32[]{:S(2)}, u32[]{:S(2)}) collective-permute-start(f32[8,128,128]{2,1,0:T(8,128)S(1)} %get-tuple-element.174), channel_id=1, source_target_pairs={{0,4},{4,0},{8,12},{12,8},{16,20},{20,16},{24,28},{28,24},{1,5},{5... | collective-permute-start | bytes 1572872 | tf_op jit(solution)/shard_map/ppermute | solution.py:709

commit v12 on v11

--- a/solution.py
+++ b/solution.py
@@ -220,7 +220,8 @@
         copies.append(pltpu.make_async_copy(k_hbm.at[at], k_raw.at[at], sems.at[2 * c + 1]))
         copies.append(pltpu.make_async_copy(v_hbm.at[at], v_raw.at[at], sems.at[2 * c + 2]))
     copies.append(pltpu.make_async_copy(gain_hbm, gain_raw, sems.at[len(copies)]))
-    for copy in copies:
+    early = 1 + 2 * per_block
+    for copy in copies[:early]:
         copy.start()
     upper = is_upper(place_ref)
     copies[0].wait()
@@ -236,6 +237,9 @@
             here = pl.ds(c * CHUNK, CHUNK)
             which = 2 * (b * per_block + c) + 1
             copies[which].wait()
+            if which == 1:
+                for copy in copies[early:]:
+                    copy.start()
             to_heads(kh.at[b, :, here], k_raw.at[at], upper)
             copies[which + 1].wait()
             to_heads(vh.at[b, :, here], v_raw.at[at], upper)
@@ -739,18 +743,74 @@
             second[h - quarter] = total
 
 
-def mix_total_first(bits, arrays, outputs):
+def chosen(bits, values, at):
+    _, right, low = bits
+    upper, lower = (
+        jnp.where(right, values[at ^ base ^ 1], values[at ^ base]) for base in (0, 2)
+    )
+    return jnp.where(low, lower, upper)
+
+
+PIECE = 32
+
+
+def mix_blocks(bits, arrays, outputs):
     own, got = arrays
-    first, second, chip = outputs
-    quarter = first.shape[0]
-    d_own = lambda h: own[h, HD : HD + 1]
-    d_got = lambda h: got[h, HD : HD + 1]
-    mix_total(bits, own, got, d_own, d_got, first, second)
-    for h in range(2 * quarter):
-        whole = d_own(h) * d_got(h)
-        chip[h : h + 1] = whole
-        place = HD + (TILE // 2) * (h // quarter)
-        first[h % quarter, place : place + TILE // 2] = jnp.broadcast_to(whole, (TILE // 2, HD))
+    *blocks, total, table = outputs
+    late = bits[0]
+    half = total.shape[0]
+    heads = half // 4
+    for h in range(half):
+        d_own, d_got = own[h, HD : HD + 1], got[h, HD : HD + 1]
+        scale_own, scale_got = jnp.where(late, 1.0, d_got), jnp.where(late, d_own, 1.0)
+        total[h] = scale_own * own[h, :HD] + scale_got * got[h, :HD]
+        table[OWN, h : h + 1], table[PARTNER, h : h + 1] = d_own, d_got
+        table[CHIP, h : h + 1] = d_own * d_got
+    for at, block in enumerate(blocks):
+        for i in range(heads):
+            for piece in range(0, HD, PIECE):
+                rows = pl.ds(piece, PIECE)
+                states = [total[heads * chip + i, rows] for chip in range(4)]
+                block[i, rows] = chosen(bits, states, at)
+            block[i, HD:] = table[CHIP]
+
+
+def mix_scan(bits, arrays, outputs):
+    old, *gots = arrays
+    *blocks, table = outputs
+    heads = gots[0].shape[0]
+    for i in range(heads):
+        decays = []
+        for got in gots:
+            lines = [got[i, HD + heads * chip + i : HD + heads * chip + i + 1] for chip in range(4)]
+            decays.append(chosen(bits, lines, 0))
+        decays = [chosen(bits, decays, chip) for chip in range(4)]
+        for piece in range(0, HD, PIECE):
+            rows = pl.ds(piece, PIECE)
+            states = [got[i, rows] for got in gots]
+            enter = [jnp.zeros((PIECE, HD), F32)]
+            for chip in range(3):
+                enter.append(decays[chip] * enter[-1] + chosen(bits, states, chip))
+            for at, block in enumerate(blocks):
+                block[i, rows] = chosen(bits, enter, at)
+    for which in (OWN, PARTNER, CHIP):
+        table[which] = old[which]
+    table[ROW], table[CORNER] = gots[1][0, HD:], gots[3][0, HD:]
+
+
+def mix_enter_first(bits, arrays, outputs):
+    table, own, got, *blocks = arrays
+    kept, sent = outputs
+    late = bits[0]
+    heads = blocks[0].shape[0]
+    for h in range(kept.shape[0]):
+        scale = jnp.where(late, table[PARTNER, h : h + 1], table[OWN, h : h + 1])
+        for piece in range(0, HD, PIECE):
+            rows = pl.ds(piece, PIECE)
+            enter = chosen(bits, [block[h % heads, rows] for block in blocks], h // heads)
+            after = scale * enter + jnp.where(late, got[h, rows], own[h, rows])
+            kept[h, rows] = jnp.where(late, after, enter)
+            sent[h, rows] = jnp.where(late, enter, after)
 
 
 def mix_total_again(bits, arrays, outputs):
@@ -777,25 +837,6 @@
 
 def lines(ref, first=0):
     return lambda i: ref[first + i : first + i + 1]
-
-
-def mix_next_row_first(bits, arrays, outputs):
-    chip, total, got = arrays
-    mix_next_row(bits, lines(chip), lambda i: got[i, HD : HD + 1], total, got, *outputs)
-
-
-def mix_next_column_first(bits, arrays, outputs):
-    own, got, chip, corner, one_a, total, one_b = arrays
-    out, table = outputs
-    quarter = total.shape[0]
-    for h in range(2 * quarter):
-        place = HD + (TILE // 2) * (h // quarter)
-        table[OWN, h : h + 1] = own[h, HD : HD + 1]
-        table[PARTNER, h : h + 1] = got[h, HD : HD + 1]
-        table[ROW, h : h + 1] = one_a[h % quarter, place : place + 1]
-    table[CHIP] = chip[...]
-    table[CORNER] = corner[...]
-    mix_next_column(bits, lines(chip, quarter), lines(corner, quarter), total, one_b, out)
 
 
 def mix_next_row_again(bits, arrays, outputs):
@@ -835,55 +876,43 @@
 
 
 def entering_quad(send, own_task, table, place, backward, tasks):
-    def work(stage, after, before=()):
-        if stage not in tasks:
-            return before
+    def work(stage, after, before):
         run, outputs = tasks[stage]
         outputs.extend(run(after))
-        return lax.optimization_barrier((before, outputs[0]))[0]
-
-    name = "later" if backward else "earlier"
+        return follows(before, outputs[0])
+
     half = send.shape[0]
-    quarter = half // 2
-    states, wide = (quarter, HD, HD), (quarter, HD + TILE, HD)
+    whole, part = (half, HD, HD), (half // 2, HD, HD)
     got = swap(send, "seq", 1)
     own = own_task(send)
-    if table is None:
-        first, second, chip = mix(
-            mix_total_first, backward, place, (own, got), (wide, states, (half, HD)), name + "_total"
+    run = lambda body, arrays, shapes, name: mix(body, backward, place, arrays, shapes, name)
+    if not backward:
+        heads = half // 4
+        wide, block = (heads, HD + TILE, HD), (heads, HD, HD)
+        *blocks, total, table = run(
+            mix_blocks, (own, got), [wide] * 4 + [whole, (3, half, HD)], "earlier_blocks"
+        )
+        gots = [swap(blocks[at], "seq", 2 * at) for at in (1, 2, 3)]
+        gots = work(1, total, gots)
+        *blocks, table = run(
+            mix_scan, (table, blocks[0], *gots), [block] * 4 + [(5, half, HD)], "earlier_scan"
+        )
+        gots = [swap(blocks[at], "seq", 2 * at) for at in (1, 2, 3)]
+        gots = work(2, blocks[0], gots)
+        kept, sent = run(
+            mix_enter_first, (table, own, got, blocks[0], *gots), [whole] * 2, "earlier_enter"
         )
     else:
-        first, second = mix(
-            mix_total_again, backward, place, (table, own, got), (states, states), name + "_total"
+        first, second = run(mix_total_again, (table, own, got), [part] * 2, "later_total")
+        one_a, one_b = swap(first, "seq", 2), swap(second, "seq", 4)
+        one_a, one_b = work(1, second, (one_a, one_b))
+        (next_a,) = run(mix_next_row_again, (table, first, one_a), [part], "later_row")
+        (next_b,) = run(mix_next_column_again, (table, second, one_b), [part], "later_column")
+        two_a, two_b = swap(next_a, "seq", 4), swap(next_b, "seq", 2)
+        two_a, two_b = work(2, next_b, (two_a, two_b))
+        kept, sent = run(
+            mix_enter, (table, own, got, one_a, one_b, two_a, two_b), [whole] * 2, "later_enter"
         )
-    one_a, one_b = swap(first, "seq", 2), swap(second, "seq", 4)
-    if table is None:
-        corner = swap(chip, "seq", 6)
-        one_a, one_b, corner = work(1, second, (one_a, one_b, corner))
-        (next_a,) = mix(
-            mix_next_row_first, backward, place, (chip, first, one_a), (states,), name + "_row"
-        )
-        one_b, corner = follows((one_b, corner), next_a)
-        next_b, table = mix(
-            mix_next_column_first, backward, place,
-            (own, got, chip, corner, one_a, second, one_b), (states, (5, half, HD)),
-            name + "_column",
-        )
-    else:
-        one_a, one_b = work(1, second, (one_a, one_b))
-        (next_a,) = mix(
-            mix_next_row_again, backward, place, (table, first, one_a), (states,), name + "_row"
-        )
-        (next_b,) = mix(
-            mix_next_column_again, backward, place, (table, second, follows(one_b, next_a)),
-            (states,), name + "_column",
-        )
-    two_a, two_b = swap(next_a, "seq", 4), swap(next_b, "seq", 2)
-    two_a, two_b = work(2, next_b, (two_a, two_b))
-    kept, sent = mix(
-        mix_enter, backward, place, (table, own, got, one_a, one_b, two_a, two_b),
-        ((half, HD, HD), (half, HD, HD)), name + "_enter",
-    )
     received = swap(sent, "seq", 1)
     received = follows(received, tasks[3](follows(kept, sent)))
     return kept, received, table

time: 67.4 us -> 69 us (1.024)
  starting transfers between devices: 15.6 us -> 17 us
  Pallas kernels: 41.5 us -> 42.3 us
    ppermute x15 -> x16, starting transfers between devices: 15.6 us -> 17 us  [swap(): return lax.ppermute(value, axis, [(i, i ^ bit) for i in range(count)])]
    pallas_call x8 -> x7, Pallas kernels: 0.73 us -> 1.57 us  [mix(): pl.pallas_call(kernel, in_specs=[NEAR] + [NEAR] * len(arrays), out_specs=...]
    ppermute x15 -> x16, waiting for transfers between devices: 8.92 us -> 8.3 us  [swap(): return lax.ppermute(value, axis, [(i, i ^ bit) for i in range(count)])]
  transfers between devices with their start and end apart: 15 -> 16, of which waited for: 9 -> 9; matrix products, arithmetic and copies ran while one was open for 0% -> 0% of each run, Pallas kernels for 43% -> 42%
where the time goes in v12:
time: 69 us; the launch traced here: 68.9 us
  Pallas kernels  42.3 us (61%)
  starting transfers between devices  17 us (25%)
  waiting for transfers between devices  8.3 us (12%)
  between operations  1.01 us (1%)
    ppermute x16, starting transfers between devices, swap(): return lax.ppermute(value, axis, [(i, i ^ bit) for i in range(count)])  17 us
    ppermute x16, waiting for transfers between devices, swap(): return lax.ppermute(value, axis, [(i, i ^ bit) for i in range(count)])  8.3 us
    pallas_call x2, Pallas kernels, intra(): pl.pallas_call(kernel, in_specs=[NEAR] * 8 + [FAR, FAR] * ahead, out_spec...  7.6 us
    pallas_call x1, Pallas kernels, grad_query(): pl.pallas_call(grad_q_kernel, in_specs=[NEAR] * 22, out_specs=[NEAR, NEAR...  7.45 us
    pallas_call x1, Pallas kernels, grad_key_value(): pl.pallas_call(grad_kv_kernel, in_specs=[NEAR] * 16, out_specs=[NEAR, NEA...  5.83 us
    pallas_call x1, Pallas kernels, state_to_send(): pl.pallas_call(state_kernel, in_specs=[NEAR, FAR, FAR, FAR, FAR], out_spe...  5.04 us
    pallas_call x1, Pallas kernels, finish_other(): pl.pallas_call(finish_other_kernel, in_specs=[NEAR] * 10, out_specs=[FAR,...  4.06 us
    pallas_call x2, Pallas kernels, attend(): pl.pallas_call(functools.partial(attend_kernel, part), in_specs=[NEAR] *...  2.91 us
  transfers between devices with their start and end apart: 16, of which 9 were waited for; matrix products, arithmetic and copies ran while one was open for 0% of the time, Pallas kernels for 42%

profile of v12, /device:TPU:0, one launch (start us, length us, event | category | flops | bytes accessed | tf_op | source)
XLA Modules:
  0.0 68.9 jit_solution(11716945643468698507)
XLA Ops:
  0.8 5.0 %state_to_send.1 = (f32[8,136,128]{2,1,0:T(8,128)S(1)}, f32[8,128,128]{2,1,0:T(8,128)S(1)}, bf16[2,16,256,128]{3,2,1,0:T(8,128)(2,1)S(1)}, bf16[2,16,256,128]{3,...) custom-call(f32[8,128]{1,0:T(8,128)S(1)} %broadcast_in_dim.2.place_r, ...), custom_call_target="tpu_custom_call" | custom-call | flops 134217728 | bytes 8388608 | tf_op jit(solution)/shard_map/state_to_send/pallas_call | solution.py:259
  6.4 1.6 %own_state.1 = (f32[8,136,128]{2,1,0:T(8,128)S(1)}, f32[8,128,128]{2,1,0:T(8,128)S(1)}, bf16[256,16,128]{2,1,0:T(8,128)(2,1)S(1)}, bf16[256,16,128]{2,1,0:T(8,128)(2,1)S(1)}) custom-call(bf16[2,16,256,128]{3,2,1,0:T(8,128)(2,1)S(1)} %get-tuple-element.97.kh.refs_2_, bf16[2,16,256,128]{3,2,1,0:T(8,128)(2,1)S(1)} %get-tuple-element.98.vh.refs_3_, ...), custom_call_target="tpu_custom_call" | custom-call | flops 134217728 | bytes 2097152 | tf_op jit(solution)/shard_map/own_state/pallas_call | solution.py:305
  8.0 0.9 %earlier_blocks.1 = (f32[2,136,128]{2,1,0:T(8,128)S(1)}, f32[2,136,128]{2,1,0:T(8,128)S(1)}, f32[2,136,128]{2,1,0:T(8,128)S(1)}, f32[2,136,128]{2,1,0:T(8,128)S(...) custom-call(f32[8,128]{1,0:T(8,128)S(1)} %broadcast_in_dim.2.place_ref, ...), custom_call_target="tpu_custom_call" | custom-call | flops 524288 | bytes 2097152 | tf_op jit(solution)/shard_map/earlier_blocks/pallas_call | solution.py:721
  8.9 2.9 %collective-permute-start.1 = (f32[2,136,128]{2,1,0:T(8,128)S(1)}, f32[2,136,128]{2,1,0:T(8,128)S(1)}, u32[]{:S(2)}, u32[]{:S(2)}) collective-permute-start(f32[2,136,128]{2,1,0:T(8,128)S(1)} %get-tuple-element.104), channel_id=1, source_target_pairs={{0,8},{4,12},{8,0},{12,4},{16,24},{20,28},{24,16},{28,20},{1,9},{5... | collective-permute-start | bytes 417800 | tf_op jit(solution)/shard_map/ppermute | solution.py:713
  11.7 1.5 %collective-permute-start.2 = (f32[2,136,128]{2,1,0:T(8,128)S(1)}, f32[2,136,128]{2,1,0:T(8,128)S(1)}, u32[]{:S(2)}, u32[]{:S(2)}) collective-permute-start(f32[2,136,128]{2,1,0:T(8,128)S(1)} %get-tuple-element.105), channel_id=1, source_target_pairs={{0,16},{4,20},{8,24},{12,28},{16,0},{20,4},{24,8},{28,12},{1,17},{... | collective-permute-start | bytes 417800 | tf_op jit(solution)/shard_map/ppermute | solution.py:713
  13.3 3.7 %intra_0.1 = (bf16[16,256,128]{2,1,0:T(8,128)(2,1)S(1)}, bf16[16,256,128]{2,1,0:T(8,128)(2,1)S(1)}, bf16[16,256,256]{2,1,0:T(8,128)(2,1)S(1)}, f32[16,3,128,128]...) custom-call(f32[8,128]{1,0:T(8,128)S(1)} %broadcast_in_dim.2.place_r, ...), custom_call_target="tpu_custom_call" | custom-call | flops 1073741824 | bytes 10485760 | tf_op jit(solution)/shard_map/intra_0/pallas_call | solution.py:353
  17.0 3.1 %collective-permute-done.2.refs_3_ = f32[2,136,128]{2,1,0:T(8,128)S(1)} collective-permute-done((f32[2,136,128]{2,1,0:T(8,128)S(1)}, f32[2,136,128]{2,1,0:T(8,128)S(1)}, u32[]{:S(2)}, u32[]{:S(2)}) %collective-permute-start.2) | collective-permute-done | bytes 139296 | tf_op jit(solution)/shard_map/ppermute | solution.py:713
  20.3 1.3 %collective-permute-start.4 = (f32[2,128,128]{2,1,0:T(8,128)S(1)}, f32[2,128,128]{2,1,0:T(8,128)S(1)}, u32[]{:S(2)}, u32[]{:S(2)}) collective-permute-start(f32[2,128,128]{2,1,0:T(8,128)S(1)} %get-tuple-element.117), channel_id=1, source_target_pairs={{0,8},{4,12},{8,0},{12,4},{16,24},{20,28},{24,16},{28,20},{1,9},{5... | collective-permute-start | bytes 393224 | tf_op jit(solution)/shard_map/ppermute | solution.py:713
  21.6 0.8 %collective-permute-start.5 = (f32[2,128,128]{2,1,0:T(8,128)S(1)}, f32[2,128,128]{2,1,0:T(8,128)S(1)}, u32[]{:S(2)}, u32[]{:S(2)}) collective-permute-start(f32[2,128,128]{2,1,0:T(8,128)S(1)} %get-tuple-element.118), channel_id=1, source_target_pairs={{0,16},{4,20},{8,24},{12,28},{16,0},{20,4},{24,8},{28,12},{1,17},{... | collective-permute-start | bytes 393224 | tf_op jit(solution)/shard_map/ppermute | solution.py:713
  22.4 1.4 %collective-permute-start.6 = (f32[2,128,128]{2,1,0:T(8,128)S(1)}, f32[2,128,128]{2,1,0:T(8,128)S(1)}, u32[]{:S(2)}, u32[]{:S(2)}) collective-permute-start(f32[2,128,128]{2,1,0:T(8,128)S(1)} %get-tuple-element.119), channel_id=1, source_target_pairs={{0,24},{4,28},{8,16},{12,20},{16,8},{20,12},{24,0},{28,4},{1,25},{... | collective-permute-start | bytes 393224 | tf_op jit(solution)/shard_map/ppermute | solution.py:713
  23.8 3.9 %intra_1.1 = (bf16[16,256,128]{2,1,0:T(8,128)(2,1)S(1)}, bf16[16,256,128]{2,1,0:T(8,128)(2,1)S(1)}, bf16[16,256,256]{2,1,0:T(8,128)(2,1)S(1)}, f32[16,3,128,128]...) custom-call(f32[8,128]{1,0:T(8,128)S(1)} %broadcast_in_dim.2.place_ref, ...), custom_call_target="tpu_custom_call" | custom-call | flops 1073741824 | bytes 10485760 | tf_op jit(solution)/shard_map/intra_1/pallas_call | solution.py:353
  27.7 1.1 %collective-permute-done.5.refs_5_ = f32[2,128,128]{2,1,0:T(8,128)S(1)} collective-permute-done((f32[2,128,128]{2,1,0:T(8,128)S(1)}, f32[2,128,128]{2,1,0:T(8,128)S(1)}, u32[]{:S(2)}, u32[]{:S(2)}) %collective-permute-start.5) | collective-permute-done | bytes 131104 | tf_op jit(solution)/shard_map/ppermute | solution.py:713
  29.1 1.3 %attend_0.1 = (f32[8,256,128]{2,1,0:T(8,128)S(1)}, f32[8,256,128]{2,1,0:T(8,128)S(1)}, f32[2,2,256,128]{3,2,1,0:T(8,128)S(1)}) custom-call(f32[16,128]{1,0:T(8,128)S(1)} %get-tuple-element.94.refs_0_.gain_ref, f32[8,128,128]{2,1,0:T(8,128)S(1)} %get-tuple-element.128.refs_1_.keep_ref, bf16[16,256,128]{2,1,0:T(8,128)(2,1)S(1)} %get-tuple-element.138.refs_2_.q0, ...), custom_call_target="tpu_custom_call" | custom-call | flops 268435456 | bytes 8388608 | tf_op jit(solution)/shard_map/attend_0/pallas_call | solution.py:415
  30.4 0.6 collective-permute-done.7.refs_1_.recv_ref
  31.0 1.6 %attend_1.1 = (f32[8,256,128]{2,1,0:T(8,128)S(1)}, f32[8,256,128]{2,1,0:T(8,128)S(1)}, f32[2,512]{1,0:T(2,128)S(1)}) custom-call(f32[16,128]{1,0:T(8,128)S(1)} %get-tuple-element.94.refs_0_.gain_ref, f32[8,128,128]{2,1,0:T(8,128)S(1)} %collective-permute-done.7.refs_1_.recv_ref, bf16[16,256,128]{2,1,0:T(8,128)(2,1)S(1)} %get-tuple-element.138.refs_2_.q0, ...), custom_call_target="tpu_custom_call" | custom-call | flops 268435456 | bytes 8388608 | tf_op jit(solution)/shard_map/attend_1/pallas_call | solution.py:415
  32.6 1.6 %collective-permute-start.8 = (f32[2,512]{1,0:T(2,128)S(1)}, f32[2,512]{1,0:T(2,128)S(1)}, u32[]{:S(2)}, u32[]{:S(2)}) collective-permute-start(f32[2,512]{1,0:T(2,128)S(1)} %get-tuple-element.137.first_ref), channel_id=1, source_target_pairs={{0,1},{1,0},{2,3},{3,2},{4,5},{5,4},{6,7},{7,6},{8,9},{9,8},{10,11... | collective-permute-start | bytes 12296 | tf_op jit(solution)/shard_map/ppermute | solution.py:713
  34.2 0.9 %scaled_queries.1 = (bf16[2,16,128,256]{3,2,1,0:T(8,128)(2,1)S(1)}, f32[2,16,128]{2,1,0:T(8,128)S(1)}) custom-call(f32[2,16,256]{2,1,0:T(8,128)S(1)} %get-tuple-element.142.cum.cum_ref, bf16[16,256,128]{2,1,0:T(8,128)(2,1)S(1)} %get-tuple-element.138.refs_2_.q0, bf16[16,256,128]{2,1,0:T(8,128)(2,1)S(1)} %get-tuple-element.123.refs_3_.q1), custom_call_target="tpu_custom_call" | custom-call | flops 2097152 | bytes 4194304 | tf_op jit(solution)/shard_map/scaled_queries/pallas_call | solution.py:441
  35.2 1.1 %collective-permute-done.8.second_ref = f32[2,512]{1,0:T(2,128)S(1)} collective-permute-done((f32[2,512]{1,0:T(2,128)S(1)}, f32[2,512]{1,0:T(2,128)S(1)}, u32[]{:S(2)}, u32[]{:S(2)}) %collective-permute-start.8) | collective-permute-done | bytes 4128 | tf_op jit(solution)/shard_map/ppermute | solution.py:713
  36.3 2.6 %collective-permute-start.9 = (f32[2,512]{1,0:T(2,128)S(1)}, f32[2,512]{1,0:T(2,128)S(1)}, u32[]{:S(2)}, u32[]{:S(2)}) collective-permute-start(f32[2,512]{1,0:T(2,128)S(1)} %add.15.first_ref), channel_id=1, source_target_pairs={{0,2},{1,3},{2,0},{3,1},{4,6},{5,7},{6,4},{7,5},{8,10},{9,11},{10,... | collective-permute-start | bytes 12296 | tf_op jit(solution)/shard_map/ppermute | solution.py:713
  38.9 1.6 %remaining_decay.1.remaining_ref.refs_4_ = f32[2,16,256,128]{3,2,1,0:T(8,128)S(1)} custom-call(f32[2,16,256]{2,1,0:T(8,128)S(1)} %get-tuple-element.142.cum.cum_ref), custom_call_target="tpu_custom_call" | custom-call | flops 1048576 | bytes 4194304 | tf_op jit(solution)/shard_map/remaining_decay/pallas_call | solution.py:463
  40.8 1.1 %norm_grad_1.1 = (f32[8,128,128]{2,1,0:T(8,128)S(1)}, f32[8,128,128]{2,1,0:T(8,128)S(1)}, bf16[8,256,128]{2,1,0:T(8,128)(2,1)S(1)}, bf16[8,256,128]{2,1,0:T(8,128)(2,1)S(1)}) custom-call(f32[2,16,128]{2,1,0:T(8,128)S(1)} %get-tuple-element.152.ends_ref.refs_0_, f32[16,128]{1,0:T(8,128)S(1)} %get-tuple-element.94.refs_0_.gain_ref, ...), custom_call_target="tpu_custom_call" | custom-call | flops 134217728 | bytes 7340032 | tf_op jit(solution)/shard_map/norm_grad_1/pallas_call | solution.py:508
  42.0 1.2 %norm_grad_0.1 = (f32[8,128,128]{2,1,0:T(8,128)S(1)}, f32[8,128,128]{2,1,0:T(8,128)S(1)}, bf16[8,256,128]{2,1,0:T(8,128)(2,1)S(1)}, bf16[8,256,128]{2,1,0:T(8,128)(2,1)S(1)}) custom-call(f32[2,16,128]{2,1,0:T(8,128)S(1)} %get-tuple-element.152.ends_ref.refs_0_, f32[16,128]{1,0:T(8,128)S(1)} %get-tuple-element.94.refs_0_.gain_ref, ...), custom_call_target="tpu_custom_call" | custom-call | flops 134217728 | bytes 7340032 | tf_op jit(solution)/shard_map/norm_grad_0/pallas_call | solution.py:508
  43.2 0.7 %collective-permute-done.10.refs_2_ = f32[8,128,128]{2,1,0:T(8,128)S(1)} collective-permute-done((f32[8,128,128]{2,1,0:T(8,128)S(1)}, f32[8,128,128]{2,1,0:T(8,128)S(1)}, u32[]{:S(2)}, u32[]{:S(2)}) %collective-permute-start.10) | collective-permute-done | bytes 524320 | tf_op jit(solution)/shard_map/ppermute | solution.py:713
  44.0 1.3 %collective-permute-start.11 = (f32[4,128,128]{2,1,0:T(8,128)S(1)}, f32[4,128,128]{2,1,0:T(8,128)S(1)}, u32[]{:S(2)}, u32[]{:S(2)}) collective-permute-start(f32[4,128,128]{2,1,0:T(8,128)S(1)} %get-tuple-element.164.refs_1_), channel_id=1, source_target_pairs={{0,8},{4,12},{8,0},{12,4},{16,24},{20,28},{24,16},{28,20},{1,9},{5... | collective-permute-start | bytes 786440 | tf_op jit(solution)/shard_map/ppermute | solution.py:713
  45.3 1.0 %collective-permute-start.12 = (f32[4,128,128]{2,1,0:T(8,128)S(1)}, f32[4,128,128]{2,1,0:T(8,128)S(1)}, u32[]{:S(2)}, u32[]{:S(2)}) collective-permute-start(f32[4,128,128]{2,1,0:T(8,128)S(1)} %get-tuple-element.151.refs_1_), channel_id=1, source_target_pairs={{0,16},{4,20},{8,24},{12,28},{16,0},{20,4},{24,8},{28,12},{1,17},{... | collective-permute-start | bytes 786440 | tf_op jit(solution)/shard_map/ppermute | solution.py:713
  46.3 7.4 %grad_query.1 = (f32[2,16,256,128]{3,2,1,0:T(8,128)S(1)}, bf16[2,16,256,256]{3,2,1,0:T(8,128)(2,1)S(1)}, bf16[512,16,128]{2,1,0:T(8,128)(2,1)}) custom-call(f32[8,128]{1,0:T(8,128)S(1)} %broadcast_in_dim.2.place_ref, f32[16,128]{1,0:T(8,128)S(1)} %get-tuple-element.94.refs_0_.gain_ref, f32[2,512]{1,0:T(2,128)S(1)} %add.16.sums_ref, ...), custom_call_target="tpu_custom_call" | custom-call | flops 1610612736 | bytes 12582912 | tf_op jit(solution)/shard_map/grad_query/pallas_call | solution.py:561
  53.8 1.1 %collective-permute-start.13 = (f32[4,128,128]{2,1,0:T(8,128)S(1)}, f32[4,128,128]{2,1,0:T(8,128)S(1)}, u32[]{:S(2)}, u32[]{:S(2)}) collective-permute-start(f32[4,128,128]{2,1,0:T(8,128)S(1)} %later_row.1), channel_id=1, source_target_pairs={{0,16},{4,20},{8,24},{12,28},{16,0},{20,4},{24,8},{28,12},{1,17},{... | collective-permute-start | bytes 786440 | tf_op jit(solution)/shard_map/ppermute | solution.py:713
  55.0 0.8 %collective-permute-start.14 = (f32[4,128,128]{2,1,0:T(8,128)S(1)}, f32[4,128,128]{2,1,0:T(8,128)S(1)}, u32[]{:S(2)}, u32[]{:S(2)}) collective-permute-start(f32[4,128,128]{2,1,0:T(8,128)S(1)} %later_column.1), channel_id=1, source_target_pairs={{0,8},{4,12},{8,0},{12,4},{16,24},{20,28},{24,16},{28,20},{1,9},{5... | collective-permute-start | bytes 786440 | tf_op jit(solution)/shard_map/ppermute | solution.py:713
  55.8 5.8 %grad_key_value.1 = (f32[2,16,256,128]{3,2,1,0:T(8,128)S(1)}, f32[2,16,256,128]{3,2,1,0:T(8,128)S(1)}, bf16[512,16,128]{2,1,0:T(8,128)(2,1)}) custom-call(f32[8,128]{1,0:T(8,128)S(1)} %broadcast_in_dim.2.place_ref, bf16[2,16,256,256]{3,2,1,0:T(8,128)(2,1)S(1)} %get-tuple-element.160.gs_ref, bf16[16,256,256]{2,1,0:T(8,128)(2,1)S(1)} %get-tuple-element.161.w0, ...), custom_call_target="tpu_custom_call" | custom-call | flops 1610612736 | bytes 31457280 | tf_op jit(solution)/shard_map/grad_key_value/pallas_call | solution.py:611
  61.7 0.8 %collective-permute-done.14.refs_6_ = f32[4,128,128]{2,1,0:T(8,128)S(1)} collective-permute-done((f32[4,128,128]{2,1,0:T(8,128)S(1)}, f32[4,128,128]{2,1,0:T(8,128)S(1)}, u32[]{:S(2)}, u32[]{:S(2)}) %collective-permute-start.14) | collective-permute-done | bytes 262176 | tf_op jit(solution)/shard_map/ppermute | solution.py:713
  62.7 1.4 %finish_own.1 = (f32[2,16,256,128]{3,2,1,0:T(8,128)S(1)}, f32[2,16,256,128]{3,2,1,0:T(8,128)S(1)}) custom-call(f32[2,16,128]{2,1,0:T(8,128)S(1)} %get-tuple-element.152.ends_ref.refs_0_, f32[8,128,128]{2,1,0:T(8,128)S(1)} %get-tuple-element.174.refs_1_, bf16[2,16,256,128]{3,2,1,0:T(8,128)(2,1)S(1)} %get-tuple-element.97.kh.refs_2_, ...), custom_call_target="tpu_custom_call" | custom-call | flops 536870912 | bytes 8388608 | tf_op jit(solution)/shard_map/finish_own/pallas_call | solution.py:675
  64.6 4.1 %finish_other.1 = (bf16[512,16,128]{2,1,0:T(8,128)(2,1)}, bf16[512,16,128]{2,1,0:T(8,128)(2,1)}, f32[2,16,256,128]{3,2,1,0:T(8,128)S(1)}, f32[2,16,256,128]{3,2,1,0:T(8,128)S(1)}) custom-call(f32[8,128]{1,0:T(8,128)S(1)} %broadcast_in_dim.2.place_ref, ...), custom_call_target="tpu_custom_call", output_to_operand_aliasing={{2}: (1, {}), {3}: (2, {})} | custom-call | flops 536870912 | bytes 8388608 | tf_op jit(solution)/shard_map/finish_other/pallas_call | solution.py:690
  (27 shorter events, 2.4 us)
Async XLA Ops:
  5.9 2.1 %collective-permute-start = (f32[8,136,128]{2,1,0:T(8,128)S(1)}, f32[8,136,128]{2,1,0:T(8,128)S(1)}, u32[]{:S(2)}, u32[]{:S(2)}) collective-permute-start(f32[8,136,128]{2,1,0:T(8,128)S(1)} %get-tuple-element.96), channel_id=1, source_target_pairs={{0,4},{4,0},{8,12},{12,8},{16,20},{20,16},{24,28},{28,24},{1,5},{5... | collective-permute-start | bytes 1671176 | tf_op jit(solution)/shard_map/ppermute | solution.py:713
  8.9 8.1 %collective-permute-start.1 = (f32[2,136,128]{2,1,0:T(8,128)S(1)}, f32[2,136,128]{2,1,0:T(8,128)S(1)}, u32[]{:S(2)}, u32[]{:S(2)}) collective-permute-start(f32[2,136,128]{2,1,0:T(8,128)S(1)} %get-tuple-element.104), channel_id=1, source_target_pairs={{0,8},{4,12},{8,0},{12,4},{16,24},{20,28},{24,16},{28,20},{1,9},{5... | collective-permute-start | bytes 417800 | tf_op jit(solution)/shard_map/ppermute | solution.py:713
  11.7 8.4 %collective-permute-start.2 = (f32[2,136,128]{2,1,0:T(8,128)S(1)}, f32[2,136,128]{2,1,0:T(8,128)S(1)}, u32[]{:S(2)}, u32[]{:S(2)}) collective-permute-start(f32[2,136,128]{2,1,0:T(8,128)S(1)} %get-tuple-element.105), channel_id=1, source_target_pairs={{0,16},{4,20},{8,24},{12,28},{16,0},{20,4},{24,8},{28,12},{1,17},{... | collective-permute-start | bytes 417800 | tf_op jit(solution)/shard_map/ppermute | solution.py:713
  13.2 6.9 %collective-permute-start.3 = (f32[2,136,128]{2,1,0:T(8,128)S(1)}, f32[2,136,128]{2,1,0:T(8,128)S(1)}, u32[]{:S(2)}, u32[]{:S(2)}) collective-permute-start(f32[2,136,128]{2,1,0:T(8,128)S(1)} %get-tuple-element.106), channel_id=1, source_target_pairs={{0,24},{4,28},{8,16},{12,20},{16,8},{20,12},{24,0},{28,4},{1,25},{... | collective-permute-start | bytes 417800 | tf_op jit(solution)/shard_map/ppermute | solution.py:713
  20.3 7.4 %collective-permute-start.4 = (f32[2,128,128]{2,1,0:T(8,128)S(1)}, f32[2,128,128]{2,1,0:T(8,128)S(1)}, u32[]{:S(2)}, u32[]{:S(2)}) collective-permute-start(f32[2,128,128]{2,1,0:T(8,128)S(1)} %get-tuple-element.117), channel_id=1, source_target_pairs={{0,8},{4,12},{8,0},{12,4},{16,24},{20,28},{24,16},{28,20},{1,9},{5... | collective-permute-start | bytes 393224 | tf_op jit(solution)/shard_map/ppermute | solution.py:713
  21.6 7.2 %collective-permute-start.5 = (f32[2,128,128]{2,1,0:T(8,128)S(1)}, f32[2,128,128]{2,1,0:T(8,128)S(1)}, u32[]{:S(2)}, u32[]{:S(2)}) collective-permute-start(f32[2,128,128]{2,1,0:T(8,128)S(1)} %get-tuple-element.118), channel_id=1, source_target_pairs={{0,16},{4,20},{8,24},{12,28},{16,0},{20,4},{24,8},{28,12},{1,17},{... | collective-permute-start | bytes 393224 | tf_op jit(solution)/shard_map/ppermute | solution.py:713
  22.4 6.4 %collective-permute-start.6 = (f32[2,128,128]{2,1,0:T(8,128)S(1)}, f32[2,128,128]{2,1,0:T(8,128)S(1)}, u32[]{:S(2)}, u32[]{:S(2)}) collective-permute-start(f32[2,128,128]{2,1,0:T(8,128)S(1)} %get-tuple-element.119), channel_id=1, source_target_pairs={{0,24},{4,28},{8,16},{12,20},{16,8},{20,12},{24,0},{28,4},{1,25},{... | collective-permute-start | bytes 393224 | tf_op jit(solution)/shard_map/ppermute | solution.py:713
  29.0 2.0 %collective-permute-start.7 = (f32[8,128,128]{2,1,0:T(8,128)S(1)}, f32[8,128,128]{2,1,0:T(8,128)S(1)}, u32[]{:S(2)}, u32[]{:S(2)}) collective-permute-start(f32[8,128,128]{2,1,0:T(8,128)S(1)} %get-tuple-element.127), channel_id=1, source_target_pairs={{0,4},{4,0},{8,12},{12,8},{16,20},{20,16},{24,28},{28,24},{1,5},{5... | collective-permute-start | bytes 1572872 | tf_op jit(solution)/shard_map/ppermute | solution.py:713
  32.6 3.6 %collective-permute-start.8 = (f32[2,512]{1,0:T(2,128)S(1)}, f32[2,512]{1,0:T(2,128)S(1)}, u32[]{:S(2)}, u32[]{:S(2)}) collective-permute-start(f32[2,512]{1,0:T(2,128)S(1)} %get-tuple-element.137.first_ref), channel_id=1, source_target_pairs={{0,1},{1,0},{2,3},{3,2},{4,5},{5,4},{6,7},{7,6},{8,9},{9,8},{10,11... | collective-permute-start | bytes 12296 | tf_op jit(solution)/shard_map/ppermute | solution.py:713
  36.3 4.5 %collective-permute-start.9 = (f32[2,512]{1,0:T(2,128)S(1)}, f32[2,512]{1,0:T(2,128)S(1)}, u32[]{:S(2)}, u32[]{:S(2)}) collective-permute-start(f32[2,512]{1,0:T(2,128)S(1)} %add.15.first_ref), channel_id=1, source_target_pairs={{0,2},{1,3},{2,0},{3,1},{4,6},{5,7},{6,4},{7,5},{8,10},{9,11},{10,... | collective-permute-start | bytes 12296 | tf_op jit(solution)/shard_map/ppermute | solution.py:713
  41.9 2.0 %collective-permute-start.10 = (f32[8,128,128]{2,1,0:T(8,128)S(1)}, f32[8,128,128]{2,1,0:T(8,128)S(1)}, u32[]{:S(2)}, u32[]{:S(2)}) collective-permute-start(f32[8,128,128]{2,1,0:T(8,128)S(1)} %get-tuple-element.148), channel_id=1, source_target_pairs={{0,4},{4,0},{8,12},{12,8},{16,20},{20,16},{24,28},{28,24},{1,5},{5... | collective-permute-start | bytes 1572872 | tf_op jit(solution)/shard_map/ppermute | solution.py:713
  44.0 9.7 %collective-permute-start.11 = (f32[4,128,128]{2,1,0:T(8,128)S(1)}, f32[4,128,128]{2,1,0:T(8,128)S(1)}, u32[]{:S(2)}, u32[]{:S(2)}) collective-permute-start(f32[4,128,128]{2,1,0:T(8,128)S(1)} %get-tuple-element.164.refs_1_), channel_id=1, source_target_pairs={{0,8},{4,12},{8,0},{12,4},{16,24},{20,28},{24,16},{28,20},{1,9},{5... | collective-permute-start | bytes 786440 | tf_op jit(solution)/shard_map/ppermute | solution.py:713
  45.3 8.4 %collective-permute-start.12 = (f32[4,128,128]{2,1,0:T(8,128)S(1)}, f32[4,128,128]{2,1,0:T(8,128)S(1)}, u32[]{:S(2)}, u32[]{:S(2)}) collective-permute-start(f32[4,128,128]{2,1,0:T(8,128)S(1)} %get-tuple-element.151.refs_1_), channel_id=1, source_target_pairs={{0,16},{4,20},{8,24},{12,28},{16,0},{20,4},{24,8},{28,12},{1,17},{... | collective-permute-start | bytes 786440 | tf_op jit(solution)/shard_map/ppermute | solution.py:713
  53.8 7.9 %collective-permute-start.13 = (f32[4,128,128]{2,1,0:T(8,128)S(1)}, f32[4,128,128]{2,1,0:T(8,128)S(1)}, u32[]{:S(2)}, u32[]{:S(2)}) collective-permute-start(f32[4,128,128]{2,1,0:T(8,128)S(1)} %later_row.1), channel_id=1, source_target_pairs={{0,16},{4,20},{8,24},{12,28},{16,0},{20,4},{24,8},{28,12},{1,17},{... | collective-permute-start | bytes 786440 | tf_op jit(solution)/shard_map/ppermute | solution.py:713
  55.0 7.5 %collective-permute-start.14 = (f32[4,128,128]{2,1,0:T(8,128)S(1)}, f32[4,128,128]{2,1,0:T(8,128)S(1)}, u32[]{:S(2)}, u32[]{:S(2)}) collective-permute-start(f32[4,128,128]{2,1,0:T(8,128)S(1)} %later_column.1), channel_id=1, source_target_pairs={{0,8},{4,12},{8,0},{12,4},{16,24},{20,28},{24,16},{28,20},{1,9},{5... | collective-permute-start | bytes 786440 | tf_op jit(solution)/shard_map/ppermute | solution.py:713
  62.7 2.0 %collective-permute-start.15 = (f32[8,128,128]{2,1,0:T(8,128)S(1)}, f32[8,128,128]{2,1,0:T(8,128)S(1)}, u32[]{:S(2)}, u32[]{:S(2)}) collective-permute-start(f32[8,128,128]{2,1,0:T(8,128)S(1)} %get-tuple-element.178), channel_id=1, source_target_pairs={{0,4},{4,0},{8,12},{12,8},{16,20},{20,16},{24,28},{28,24},{1,5},{5... | collective-permute-start | bytes 1572872 | tf_op jit(solution)/shard_map/ppermute | solution.py:713

commit v13 on v11

--- a/solution.py
+++ b/solution.py
@@ -199,7 +199,7 @@
             state += jnp.exp(row[:, BLOCK - 1 :]) * first[i]
         out[i, :HD] = state
 
-    each_head(half, 4, one)
+    each_head(half, 8, one)
 
 
 def add_decays(out, decay, part):
@@ -390,7 +390,7 @@
             partial[1, b] += gain * o[h].astype(F32) * attended
             state = columns[h, BLOCK - 1 :] * state
 
-    each_head(half, 4, one)
+    each_head(half, 8, one)
     if part:
         ones = jnp.ones((8, HD), F32)
         for b in range(2):
@@ -498,7 +498,7 @@
             second_ref[i] = starts[1]
             out_ref[i] = starts[0] + ends_ref[0, pl.ds(h, 1)] * starts[1]
 
-        each_head(half, 4, one)
+        each_head(half, 8, one)
 
     by_head = in_vmem(half, BLOCK, dim, kind=BF16)
     return pl.pallas_call(
@@ -546,7 +546,7 @@
                 state = ends_ref[0, pl.ds(h, 1)] * state + (first_own, first_send)[part][i]
             rows[b, h] = dot(scores, kh[b, h]) + columns[h] * times_state_t(grad, state)
 
-        each_half(keep_ref.shape[0], 4, one)
+        each_half(keep_ref.shape[0], 8, one)
     for copy in copies:
         copy.wait()
 
@@ -596,7 +596,7 @@
         dk[1, h] = transposed_dot(gs_ref[1, h], q1[h])
         dv[1, h] = dot(w1[h], g1[i])
 
-    each_half(second_own.shape[0], 2, one)
+    each_half(second_own.shape[0], 4, one)
     for copy in copies:
         copy.wait()
 
@@ -639,7 +639,7 @@
         rows_k[b, h] = dk[b, h] + columns * carried[:, :HD]
         rows_v[b, h] = dv[b, h] + columns * carried[:, HD:]
 
-    each_head(half, 4, one)
+    each_head(half, 8, one)
 
 
 def finish_own_kernel(*refs):

time: 67.4 us -> 66.7 us (0.990)
  Pallas kernels: 41.5 us -> 38.4 us
  waiting for transfers between devices: 8.92 us -> 11.7 us
    ppermute x15, waiting for transfers between devices: 8.92 us -> 11.7 us  [swap(): return lax.ppermute(value, axis, [(i, i ^ bit) for i in range(count)])]
    pallas_call x1, Pallas kernels: 6 us -> 5.07 us  [grad_key_value(): pl.pallas_call(grad_kv_kernel, in_specs=[NEAR] * 16, out_specs=[NEAR, NEA...]
    pallas_call x2, Pallas kernels: 2.31 us -> 1.63 us  [norm_grad(): pl.pallas_call(kernel, in_specs=[NEAR] * 8, out_specs=[NEAR] * 4, out_sha...]
  transfers between devices with their start and end apart: 15 -> 15, of which waited for: 9 -> 10; matrix products, arithmetic and copies ran while one was open for 0% -> 0% of each run, Pallas kernels for 43% -> 41%
where the time goes in v13:
time: 66.7 us; the launch traced here: 66.5 us
  Pallas kernels  38.4 us (58%)
  starting transfers between devices  15.3 us (23%)
  waiting for transfers between devices  11.7 us (18%)
  between operations  1.01 us (2%)
    ppermute x15, starting transfers between devices, swap(): return lax.ppermute(value, axis, [(i, i ^ bit) for i in range(count)])  15.3 us
    ppermute x15, waiting for transfers between devices, swap(): return lax.ppermute(value, axis, [(i, i ^ bit) for i in range(count)])  11.7 us
    pallas_call x2, Pallas kernels, intra(): pl.pallas_call(kernel, in_specs=[NEAR] * 8 + [FAR, FAR] * ahead, out_spec...  7.59 us
    pallas_call x1, Pallas kernels, grad_query(): pl.pallas_call(grad_q_kernel, in_specs=[NEAR] * 22, out_specs=[NEAR, NEAR...  7.04 us
    pallas_call x1, Pallas kernels, grad_key_value(): pl.pallas_call(grad_kv_kernel, in_specs=[NEAR] * 16, out_specs=[NEAR, NEA...  5.07 us
    pallas_call x1, Pallas kernels, state_to_send(): pl.pallas_call(state_kernel, in_specs=[NEAR, FAR, FAR, FAR, FAR], out_spe...  4.61 us
    pallas_call x1, Pallas kernels, finish_other(): pl.pallas_call(finish_other_kernel, in_specs=[NEAR] * 10, out_specs=[FAR,...  3.5 us
    pallas_call x2, Pallas kernels, attend(): pl.pallas_call(functools.partial(attend_kernel, part), in_specs=[NEAR] *...  2.85 us
  transfers between devices with their start and end apart: 15, of which 10 were waited for; matrix products, arithmetic and copies ran while one was open for 0% of the time, Pallas kernels for 41%

profile of v13, /device:TPU:0, one launch (start us, length us, event | category | flops | bytes accessed | tf_op | source)
XLA Modules:
  0.0 66.5 jit_solution(14334515490518106988)
XLA Ops:
  0.8 4.6 %state_to_send.1 = (f32[8,136,128]{2,1,0:T(8,128)S(1)}, f32[8,128,128]{2,1,0:T(8,128)S(1)}, bf16[2,16,256,128]{3,2,1,0:T(8,128)(2,1)S(1)}, bf16[2,16,256,128]{3,...) custom-call(f32[8,128]{1,0:T(8,128)S(1)} %broadcast_in_dim.2.place_r, ...), custom_call_target="tpu_custom_call" | custom-call | flops 134217728 | bytes 8388608 | tf_op jit(solution)/shard_map/state_to_send/pallas_call | solution.py:255
  6.0 2.0 %own_state.1 = (f32[8,136,128]{2,1,0:T(8,128)S(1)}, f32[8,128,128]{2,1,0:T(8,128)S(1)}, bf16[256,16,128]{2,1,0:T(8,128)(2,1)S(1)}, bf16[256,16,128]{2,1,0:T(8,128)(2,1)S(1)}) custom-call(bf16[2,16,256,128]{3,2,1,0:T(8,128)(2,1)S(1)} %get-tuple-element.95.kh.refs_2_, bf16[2,16,256,128]{3,2,1,0:T(8,128)(2,1)S(1)} %get-tuple-element.96.vh.refs_3_, ...), custom_call_target="tpu_custom_call" | custom-call | flops 134217728 | bytes 2097152 | tf_op jit(solution)/shard_map/own_state/pallas_call | solution.py:301
  8.0 2.6 %collective-permute-start.1 = (f32[4,136,128]{2,1,0:T(8,128)S(1)}, f32[4,136,128]{2,1,0:T(8,128)S(1)}, u32[]{:S(2)}, u32[]{:S(2)}) collective-permute-start(f32[4,136,128]{2,1,0:T(8,128)S(1)} %get-tuple-element.101.refs_1_), channel_id=1, source_target_pairs={{0,8},{4,12},{8,0},{12,4},{16,24},{20,28},{24,16},{28,20},{1,9},{5... | collective-permute-start | bytes 835592 | tf_op jit(solution)/shard_map/ppermute | solution.py:709
  10.6 1.5 %collective-permute-start.2 = (f32[4,128,128]{2,1,0:T(8,128)S(1)}, f32[4,128,128]{2,1,0:T(8,128)S(1)}, u32[]{:S(2)}, u32[]{:S(2)}) collective-permute-start(f32[4,128,128]{2,1,0:T(8,128)S(1)} %get-tuple-element.102.refs_5_), channel_id=1, source_target_pairs={{0,16},{4,20},{8,24},{12,28},{16,0},{20,4},{24,8},{28,12},{1,17},{... | collective-permute-start | bytes 786440 | tf_op jit(solution)/shard_map/ppermute | solution.py:709
  12.2 3.7 %intra_0.1 = (bf16[16,256,128]{2,1,0:T(8,128)(2,1)S(1)}, bf16[16,256,128]{2,1,0:T(8,128)(2,1)S(1)}, bf16[16,256,256]{2,1,0:T(8,128)(2,1)S(1)}, f32[16,3,128,128]...) custom-call(f32[8,128]{1,0:T(8,128)S(1)} %broadcast_in_dim.2.place_r, ...), custom_call_target="tpu_custom_call" | custom-call | flops 1073741824 | bytes 10485760 | tf_op jit(solution)/shard_map/intra_0/pallas_call | solution.py:349
  15.9 3.3 %collective-permute-done.3.refs_3_ = f32[8,128]{1,0:T(8,128)S(1)} collective-permute-done((f32[8,128]{1,0:T(8,128)S(1)}, f32[8,128]{1,0:T(8,128)S(1)}, u32[]{:S(2)}, u32[]{:S(2)}) %collective-permute-start.3) | collective-permute-done | bytes 4128 | tf_op jit(solution)/shard_map/ppermute | solution.py:709
  19.3 1.6 %collective-permute-start.5 = (f32[4,128,128]{2,1,0:T(8,128)S(1)}, f32[4,128,128]{2,1,0:T(8,128)S(1)}, u32[]{:S(2)}, u32[]{:S(2)}) collective-permute-start(f32[4,128,128]{2,1,0:T(8,128)S(1)} %get-tuple-element.115), channel_id=1, source_target_pairs={{0,8},{4,12},{8,0},{12,4},{16,24},{20,28},{24,16},{28,20},{1,9},{5... | collective-permute-start | bytes 786440 | tf_op jit(solution)/shard_map/ppermute | solution.py:709
  21.4 3.8 %intra_1.1 = (bf16[16,256,128]{2,1,0:T(8,128)(2,1)S(1)}, bf16[16,256,128]{2,1,0:T(8,128)(2,1)S(1)}, bf16[16,256,256]{2,1,0:T(8,128)(2,1)S(1)}, f32[16,3,128,128]...) custom-call(f32[8,128]{1,0:T(8,128)S(1)} %broadcast_in_dim.2.place_ref, ...), custom_call_target="tpu_custom_call" | custom-call | flops 1073741824 | bytes 10485760 | tf_op jit(solution)/shard_map/intra_1/pallas_call | solution.py:349
  25.2 1.8 %collective-permute-done.5.refs_6_ = f32[4,128,128]{2,1,0:T(8,128)S(1)} collective-permute-done((f32[4,128,128]{2,1,0:T(8,128)S(1)}, f32[4,128,128]{2,1,0:T(8,128)S(1)}, u32[]{:S(2)}, u32[]{:S(2)}) %collective-permute-start.5) | collective-permute-done | bytes 262176 | tf_op jit(solution)/shard_map/ppermute | solution.py:709
  27.0 1.2 %collective-permute-done.4.refs_5_ = f32[4,128,128]{2,1,0:T(8,128)S(1)} collective-permute-done((f32[4,128,128]{2,1,0:T(8,128)S(1)}, f32[4,128,128]{2,1,0:T(8,128)S(1)}, u32[]{:S(2)}, u32[]{:S(2)}) %collective-permute-start.4) | collective-permute-done | bytes 262176 | tf_op jit(solution)/shard_map/ppermute | solution.py:709
  28.5 1.2 %attend_0.1 = (f32[8,256,128]{2,1,0:T(8,128)S(1)}, f32[8,256,128]{2,1,0:T(8,128)S(1)}, f32[2,2,256,128]{3,2,1,0:T(8,128)S(1)}) custom-call(f32[16,128]{1,0:T(8,128)S(1)} %get-tuple-element.92.refs_0_.gain_ref, f32[8,128,128]{2,1,0:T(8,128)S(1)} %get-tuple-element.123.refs_1_.keep_ref, bf16[16,256,128]{2,1,0:T(8,128)(2,1)S(1)} %get-tuple-element.133.refs_2_.q0, ...), custom_call_target="tpu_custom_call" | custom-call | flops 268435456 | bytes 8388608 | tf_op jit(solution)/shard_map/attend_0/pallas_call | solution.py:411
  29.7 0.7 %collective-permute-done.6.refs_1_.recv_ref = f32[8,128,128]{2,1,0:T(8,128)S(1)} collective-permute-done((f32[8,128,128]{2,1,0:T(8,128)S(1)}, f32[8,128,128]{2,1,0:T(8,128)S(1)}, u32[]{:S(2)}, u32[]{:S(2)}) %collective-permute-start.6) | collective-permute-done | bytes 524320 | tf_op jit(solution)/shard_map/ppermute | solution.py:709
  30.4 1.7 %attend_1.1 = (f32[8,256,128]{2,1,0:T(8,128)S(1)}, f32[8,256,128]{2,1,0:T(8,128)S(1)}, f32[2,512]{1,0:T(2,128)S(1)}) custom-call(f32[16,128]{1,0:T(8,128)S(1)} %get-tuple-element.92.refs_0_.gain_ref, f32[8,128,128]{2,1,0:T(8,128)S(1)} %collective-permute-done.6.refs_1_.recv_ref, bf16[16,256,128]{2,1,0:T(8,128)(2,1)S(1)} %get-tuple-element.133.refs_2_.q0, ...), custom_call_target="tpu_custom_call" | custom-call | flops 268435456 | bytes 8388608 | tf_op jit(solution)/shard_map/attend_1/pallas_call | solution.py:411
  32.1 1.6 %collective-permute-start.7 = (f32[2,512]{1,0:T(2,128)S(1)}, f32[2,512]{1,0:T(2,128)S(1)}, u32[]{:S(2)}, u32[]{:S(2)}) collective-permute-start(f32[2,512]{1,0:T(2,128)S(1)} %get-tuple-element.132.first_ref), channel_id=1, source_target_pairs={{0,1},{1,0},{2,3},{3,2},{4,5},{5,4},{6,7},{7,6},{8,9},{9,8},{10,11... | collective-permute-start | bytes 12296 | tf_op jit(solution)/shard_map/ppermute | solution.py:709
  33.7 0.9 %scaled_queries.1 = (bf16[2,16,128,256]{3,2,1,0:T(8,128)(2,1)S(1)}, f32[2,16,128]{2,1,0:T(8,128)S(1)}) custom-call(f32[2,16,256]{2,1,0:T(8,128)S(1)} %get-tuple-element.137.cum.cum_ref, bf16[16,256,128]{2,1,0:T(8,128)(2,1)S(1)} %get-tuple-element.133.refs_2_.q0, bf16[16,256,128]{2,1,0:T(8,128)(2,1)S(1)} %get-tuple-element.119.refs_3_.q1), custom_call_target="tpu_custom_call" | custom-call | flops 2097152 | bytes 4194304 | tf_op jit(solution)/shard_map/scaled_queries/pallas_call | solution.py:437
  34.6 1.1 %collective-permute-done.7.second_ref = f32[2,512]{1,0:T(2,128)S(1)} collective-permute-done((f32[2,512]{1,0:T(2,128)S(1)}, f32[2,512]{1,0:T(2,128)S(1)}, u32[]{:S(2)}, u32[]{:S(2)}) %collective-permute-start.7) | collective-permute-done | bytes 4128 | tf_op jit(solution)/shard_map/ppermute | solution.py:709
  35.7 2.6 %collective-permute-start.8 = (f32[2,512]{1,0:T(2,128)S(1)}, f32[2,512]{1,0:T(2,128)S(1)}, u32[]{:S(2)}, u32[]{:S(2)}) collective-permute-start(f32[2,512]{1,0:T(2,128)S(1)} %add.15.first_ref), channel_id=1, source_target_pairs={{0,2},{1,3},{2,0},{3,1},{4,6},{5,7},{6,4},{7,5},{8,10},{9,11},{10,... | collective-permute-start | bytes 12296 | tf_op jit(solution)/shard_map/ppermute | solution.py:709
  38.3 1.6 %remaining_decay.1.remaining_ref.refs_4_ = f32[2,16,256,128]{3,2,1,0:T(8,128)S(1)} custom-call(f32[2,16,256]{2,1,0:T(8,128)S(1)} %get-tuple-element.137.cum.cum_ref), custom_call_target="tpu_custom_call" | custom-call | flops 1048576 | bytes 4194304 | tf_op jit(solution)/shard_map/remaining_decay/pallas_call | solution.py:459
  40.2 0.8 %norm_grad_1.1 = (f32[8,128,128]{2,1,0:T(8,128)S(1)}, f32[8,128,128]{2,1,0:T(8,128)S(1)}, bf16[8,256,128]{2,1,0:T(8,128)(2,1)S(1)}, bf16[8,256,128]{2,1,0:T(8,128)(2,1)S(1)}) custom-call(f32[2,16,128]{2,1,0:T(8,128)S(1)} %get-tuple-element.147.ends_ref.refs_0_, f32[16,128]{1,0:T(8,128)S(1)} %get-tuple-element.92.refs_0_.gain_ref, ...), custom_call_target="tpu_custom_call" | custom-call | flops 134217728 | bytes 7340032 | tf_op jit(solution)/shard_map/norm_grad_1/pallas_call | solution.py:504
  41.1 0.8 %norm_grad_0.1 = (f32[8,128,128]{2,1,0:T(8,128)S(1)}, f32[8,128,128]{2,1,0:T(8,128)S(1)}, bf16[8,256,128]{2,1,0:T(8,128)(2,1)S(1)}, bf16[8,256,128]{2,1,0:T(8,128)(2,1)S(1)}) custom-call(f32[2,16,128]{2,1,0:T(8,128)S(1)} %get-tuple-element.147.ends_ref.refs_0_, f32[16,128]{1,0:T(8,128)S(1)} %get-tuple-element.92.refs_0_.gain_ref, ...), custom_call_target="tpu_custom_call" | custom-call | flops 134217728 | bytes 7340032 | tf_op jit(solution)/shard_map/norm_grad_0/pallas_call | solution.py:504
  41.9 1.1 %collective-permute-done.9.refs_2_ = f32[8,128,128]{2,1,0:T(8,128)S(1)} collective-permute-done((f32[8,128,128]{2,1,0:T(8,128)S(1)}, f32[8,128,128]{2,1,0:T(8,128)S(1)}, u32[]{:S(2)}, u32[]{:S(2)}) %collective-permute-start.9) | collective-permute-done | bytes 524320 | tf_op jit(solution)/shard_map/ppermute | solution.py:709
  43.1 0.6 collective-permute-start.10
  43.7 1.4 %collective-permute-start.11 = (f32[4,128,128]{2,1,0:T(8,128)S(1)}, f32[4,128,128]{2,1,0:T(8,128)S(1)}, u32[]{:S(2)}, u32[]{:S(2)}) collective-permute-start(f32[4,128,128]{2,1,0:T(8,128)S(1)} %get-tuple-element.146.refs_1_), channel_id=1, source_target_pairs={{0,16},{4,20},{8,24},{12,28},{16,0},{20,4},{24,8},{28,12},{1,17},{... | collective-permute-start | bytes 786440 | tf_op jit(solution)/shard_map/ppermute | solution.py:709
  45.1 7.0 %grad_query.1 = (f32[2,16,256,128]{3,2,1,0:T(8,128)S(1)}, bf16[2,16,256,256]{3,2,1,0:T(8,128)(2,1)S(1)}, bf16[512,16,128]{2,1,0:T(8,128)(2,1)}) custom-call(f32[8,128]{1,0:T(8,128)S(1)} %broadcast_in_dim.2.place_ref, f32[16,128]{1,0:T(8,128)S(1)} %get-tuple-element.92.refs_0_.gain_ref, f32[2,512]{1,0:T(2,128)S(1)} %add.16.sums_ref, ...), custom_call_target="tpu_custom_call" | custom-call | flops 1610612736 | bytes 12582912 | tf_op jit(solution)/shard_map/grad_query/pallas_call | solution.py:557
  52.3 1.2 %collective-permute-start.13 = (f32[4,128,128]{2,1,0:T(8,128)S(1)}, f32[4,128,128]{2,1,0:T(8,128)S(1)}, u32[]{:S(2)}, u32[]{:S(2)}) collective-permute-start(f32[4,128,128]{2,1,0:T(8,128)S(1)} %later_column.1), channel_id=1, source_target_pairs={{0,8},{4,12},{8,0},{12,4},{16,24},{20,28},{24,16},{28,20},{1,9},{5... | collective-permute-start | bytes 786440 | tf_op jit(solution)/shard_map/ppermute | solution.py:709
  53.4 1.0 %collective-permute-start.12 = (f32[4,128,128]{2,1,0:T(8,128)S(1)}, f32[4,128,128]{2,1,0:T(8,128)S(1)}, u32[]{:S(2)}, u32[]{:S(2)}) collective-permute-start(f32[4,128,128]{2,1,0:T(8,128)S(1)} %later_row.1), channel_id=1, source_target_pairs={{0,16},{4,20},{8,24},{12,28},{16,0},{20,4},{24,8},{28,12},{1,17},{... | collective-permute-start | bytes 786440 | tf_op jit(solution)/shard_map/ppermute | solution.py:709
  54.5 5.1 %grad_key_value.1 = (f32[2,16,256,128]{3,2,1,0:T(8,128)S(1)}, f32[2,16,256,128]{3,2,1,0:T(8,128)S(1)}, bf16[512,16,128]{2,1,0:T(8,128)(2,1)}) custom-call(f32[8,128]{1,0:T(8,128)S(1)} %broadcast_in_dim.2.place_ref, bf16[2,16,256,256]{3,2,1,0:T(8,128)(2,1)S(1)} %get-tuple-element.155.gs_ref, bf16[16,256,256]{2,1,0:T(8,128)(2,1)S(1)} %get-tuple-element.156.w0, ...), custom_call_target="tpu_custom_call" | custom-call | flops 1610612736 | bytes 31457280 | tf_op jit(solution)/shard_map/grad_key_value/pallas_call | solution.py:607
  59.5 0.6 collective-permute-done.13.refs_6_
  60.1 0.6 collective-permute-done.12.refs_5_
  61.0 0.8 %finish_own.1 = (f32[2,16,256,128]{3,2,1,0:T(8,128)S(1)}, f32[2,16,256,128]{3,2,1,0:T(8,128)S(1)}) custom-call(f32[2,16,128]{2,1,0:T(8,128)S(1)} %get-tuple-element.147.ends_ref.refs_0_, f32[8,128,128]{2,1,0:T(8,128)S(1)} %get-tuple-element.170.refs_1_, bf16[2,16,256,128]{3,2,1,0:T(8,128)(2,1)S(1)} %get-tuple-element.95.kh.refs_2_, ...), custom_call_target="tpu_custom_call" | custom-call | flops 536870912 | bytes 8388608 | tf_op jit(solution)/shard_map/finish_own/pallas_call | solution.py:671
  61.8 1.1 %collective-permute-done.14.state_ref = f32[8,128,128]{2,1,0:T(8,128)S(1)} collective-permute-done((f32[8,128,128]{2,1,0:T(8,128)S(1)}, f32[8,128,128]{2,1,0:T(8,128)S(1)}, u32[]{:S(2)}, u32[]{:S(2)}) %collective-permute-start.14) | collective-permute-done | bytes 524320 | tf_op jit(solution)/shard_map/ppermute | solution.py:709
  62.9 3.5 %finish_other.1 = (bf16[512,16,128]{2,1,0:T(8,128)(2,1)}, bf16[512,16,128]{2,1,0:T(8,128)(2,1)}, f32[2,16,256,128]{3,2,1,0:T(8,128)S(1)}, f32[2,16,256,128]{3,2,1,0:T(8,128)S(1)}) custom-call(f32[8,128]{1,0:T(8,128)S(1)} %broadcast_in_dim.2.place_ref, ...), custom_call_target="tpu_custom_call", output_to_operand_aliasing={{2}: (1, {}), {3}: (2, {})} | custom-call | flops 536870912 | bytes 8388608 | tf_op jit(solution)/shard_map/finish_other/pallas_call | solution.py:686
  (26 shorter events, 2.4 us)
Async XLA Ops:
  5.5 2.5 %collective-permute-start = (f32[8,136,128]{2,1,0:T(8,128)S(1)}, f32[8,136,128]{2,1,0:T(8,128)S(1)}, u32[]{:S(2)}, u32[]{:S(2)}) collective-permute-start(f32[8,136,128]{2,1,0:T(8,128)S(1)} %get-tuple-element.94), channel_id=1, source_target_pairs={{0,4},{4,0},{8,12},{12,8},{16,20},{20,16},{24,28},{28,24},{1,5},{5... | collective-permute-start | bytes 1671176 | tf_op jit(solution)/shard_map/ppermute | solution.py:709
  8.0 11.2 %collective-permute-start.1 = (f32[4,136,128]{2,1,0:T(8,128)S(1)}, f32[4,136,128]{2,1,0:T(8,128)S(1)}, u32[]{:S(2)}, u32[]{:S(2)}) collective-permute-start(f32[4,136,128]{2,1,0:T(8,128)S(1)} %get-tuple-element.101.refs_1_), channel_id=1, source_target_pairs={{0,8},{4,12},{8,0},{12,4},{16,24},{20,28},{24,16},{28,20},{1,9},{5... | collective-permute-start | bytes 835592 | tf_op jit(solution)/shard_map/ppermute | solution.py:709
  10.6 8.6 %collective-permute-start.2 = (f32[4,128,128]{2,1,0:T(8,128)S(1)}, f32[4,128,128]{2,1,0:T(8,128)S(1)}, u32[]{:S(2)}, u32[]{:S(2)}) collective-permute-start(f32[4,128,128]{2,1,0:T(8,128)S(1)} %get-tuple-element.102.refs_5_), channel_id=1, source_target_pairs={{0,16},{4,20},{8,24},{12,28},{16,0},{20,4},{24,8},{28,12},{1,17},{... | collective-permute-start | bytes 786440 | tf_op jit(solution)/shard_map/ppermute | solution.py:709
  12.1 7.1 %collective-permute-start.3 = (f32[8,128]{1,0:T(8,128)S(1)}, f32[8,128]{1,0:T(8,128)S(1)}, u32[]{:S(2)}, u32[]{:S(2)}) collective-permute-start(f32[8,128]{1,0:T(8,128)S(1)} %get-tuple-element.100.refs_0_.refs_2_), channel_id=1, source_target_pairs={{0,24},{4,28},{8,16},{12,20},{16,8},{20,12},{24,0},{28,4},{1,25},{... | collective-permute-start | bytes 12296 | tf_op jit(solution)/shard_map/ppermute | solution.py:709
  19.3 7.7 %collective-permute-start.5 = (f32[4,128,128]{2,1,0:T(8,128)S(1)}, f32[4,128,128]{2,1,0:T(8,128)S(1)}, u32[]{:S(2)}, u32[]{:S(2)}) collective-permute-start(f32[4,128,128]{2,1,0:T(8,128)S(1)} %get-tuple-element.115), channel_id=1, source_target_pairs={{0,8},{4,12},{8,0},{12,4},{16,24},{20,28},{24,16},{28,20},{1,9},{5... | collective-permute-start | bytes 786440 | tf_op jit(solution)/shard_map/ppermute | solution.py:709
  20.9 7.4 %collective-permute-start.4 = (f32[4,128,128]{2,1,0:T(8,128)S(1)}, f32[4,128,128]{2,1,0:T(8,128)S(1)}, u32[]{:S(2)}, u32[]{:S(2)}) collective-permute-start(f32[4,128,128]{2,1,0:T(8,128)S(1)} %earlier_row.1), channel_id=1, source_target_pairs={{0,16},{4,20},{8,24},{12,28},{16,0},{20,4},{24,8},{28,12},{1,17},{... | collective-permute-start | bytes 786440 | tf_op jit(solution)/shard_map/ppermute | solution.py:709
  28.4 2.0 %collective-permute-start.6 = (f32[8,128,128]{2,1,0:T(8,128)S(1)}, f32[8,128,128]{2,1,0:T(8,128)S(1)}, u32[]{:S(2)}, u32[]{:S(2)}) collective-permute-start(f32[8,128,128]{2,1,0:T(8,128)S(1)} %get-tuple-element.122), channel_id=1, source_target_pairs={{0,4},{4,0},{8,12},{12,8},{16,20},{20,16},{24,28},{28,24},{1,5},{5... | collective-permute-start | bytes 1572872 | tf_op jit(solution)/shard_map/ppermute | solution.py:709
  32.1 3.6 %collective-permute-start.7 = (f32[2,512]{1,0:T(2,128)S(1)}, f32[2,512]{1,0:T(2,128)S(1)}, u32[]{:S(2)}, u32[]{:S(2)}) collective-permute-start(f32[2,512]{1,0:T(2,128)S(1)} %get-tuple-element.132.first_ref), channel_id=1, source_target_pairs={{0,1},{1,0},{2,3},{3,2},{4,5},{5,4},{6,7},{7,6},{8,9},{9,8},{10,11... | collective-permute-start | bytes 12296 | tf_op jit(solution)/shard_map/ppermute | solution.py:709
  35.7 4.5 %collective-permute-start.8 = (f32[2,512]{1,0:T(2,128)S(1)}, f32[2,512]{1,0:T(2,128)S(1)}, u32[]{:S(2)}, u32[]{:S(2)}) collective-permute-start(f32[2,512]{1,0:T(2,128)S(1)} %add.15.first_ref), channel_id=1, source_target_pairs={{0,2},{1,3},{2,0},{3,1},{4,6},{5,7},{6,4},{7,5},{8,10},{9,11},{10,... | collective-permute-start | bytes 12296 | tf_op jit(solution)/shard_map/ppermute | solution.py:709
  41.0 2.0 %collective-permute-start.9 = (f32[8,128,128]{2,1,0:T(8,128)S(1)}, f32[8,128,128]{2,1,0:T(8,128)S(1)}, u32[]{:S(2)}, u32[]{:S(2)}) collective-permute-start(f32[8,128,128]{2,1,0:T(8,128)S(1)} %get-tuple-element.143), channel_id=1, source_target_pairs={{0,4},{4,0},{8,12},{12,8},{16,20},{20,16},{24,28},{28,24},{1,5},{5... | collective-permute-start | bytes 1572872 | tf_op jit(solution)/shard_map/ppermute | solution.py:709
  43.1 9.0 %collective-permute-start.10 = (f32[4,128,128]{2,1,0:T(8,128)S(1)}, f32[4,128,128]{2,1,0:T(8,128)S(1)}, u32[]{:S(2)}, u32[]{:S(2)}) collective-permute-start(f32[4,128,128]{2,1,0:T(8,128)S(1)} %get-tuple-element.159.refs_1_), channel_id=1, source_target_pairs={{0,8},{4,12},{8,0},{12,4},{16,24},{20,28},{24,16},{28,20},{1,9},{5... | collective-permute-start | bytes 786440 | tf_op jit(solution)/shard_map/ppermute | solution.py:709
  43.7 8.5 %collective-permute-start.11 = (f32[4,128,128]{2,1,0:T(8,128)S(1)}, f32[4,128,128]{2,1,0:T(8,128)S(1)}, u32[]{:S(2)}, u32[]{:S(2)}) collective-permute-start(f32[4,128,128]{2,1,0:T(8,128)S(1)} %get-tuple-element.146.refs_1_), channel_id=1, source_target_pairs={{0,16},{4,20},{8,24},{12,28},{16,0},{20,4},{24,8},{28,12},{1,17},{... | collective-permute-start | bytes 786440 | tf_op jit(solution)/shard_map/ppermute | solution.py:709
  52.3 7.9 %collective-permute-start.13 = (f32[4,128,128]{2,1,0:T(8,128)S(1)}, f32[4,128,128]{2,1,0:T(8,128)S(1)}, u32[]{:S(2)}, u32[]{:S(2)}) collective-permute-start(f32[4,128,128]{2,1,0:T(8,128)S(1)} %later_column.1), channel_id=1, source_target_pairs={{0,8},{4,12},{8,0},{12,4},{16,24},{20,28},{24,16},{28,20},{1,9},{5... | collective-permute-start | bytes 786440 | tf_op jit(solution)/shard_map/ppermute | solution.py:709
  53.4 7.3 %collective-permute-start.12 = (f32[4,128,128]{2,1,0:T(8,128)S(1)}, f32[4,128,128]{2,1,0:T(8,128)S(1)}, u32[]{:S(2)}, u32[]{:S(2)}) collective-permute-start(f32[4,128,128]{2,1,0:T(8,128)S(1)} %later_row.1), channel_id=1, source_target_pairs={{0,16},{4,20},{8,24},{12,28},{16,0},{20,4},{24,8},{28,12},{1,17},{... | collective-permute-start | bytes 786440 | tf_op jit(solution)/shard_map/ppermute | solution.py:709
  60.9 2.0 %collective-permute-start.14 = (f32[8,128,128]{2,1,0:T(8,128)S(1)}, f32[8,128,128]{2,1,0:T(8,128)S(1)}, u32[]{:S(2)}, u32[]{:S(2)}) collective-permute-start(f32[8,128,128]{2,1,0:T(8,128)S(1)} %get-tuple-element.174), channel_id=1, source_target_pairs={{0,4},{4,0},{8,12},{12,8},{16,20},{20,16},{24,28},{28,24},{1,5},{5... | collective-permute-start | bytes 1572872 | tf_op jit(solution)/shard_map/ppermute | solution.py:709

commit v14 on v13

--- a/solution.py
+++ b/solution.py
@@ -187,7 +187,7 @@
     )
 
 
-def half_states(part, kh, vh, cum, b, out, first=None):
+def half_states(part, kh, vh, cum, b, out, first=None, unroll=8):
     half = kh.shape[1] // 2
 
     def one(i):
@@ -199,7 +199,7 @@
             state += jnp.exp(row[:, BLOCK - 1 :]) * first[i]
         out[i, :HD] = state
 
-    each_head(half, 8, one)
+    each_head(half, unroll, one)
 
 
 def add_decays(out, decay, part):
@@ -287,8 +287,8 @@
     kh, vh, cum, decay, q_hbm, o_hbm, own_ref, first_ref, q_raw, o_raw, sems
 ):
     copies = fetch_block(0, (q_hbm, o_hbm), (q_raw, o_raw), sems)
-    half_states(0, kh, vh, cum, 0, first_ref)
-    half_states(0, kh, vh, cum, 1, own_ref, first_ref)
+    half_states(0, kh, vh, cum, 0, first_ref, unroll=4)
+    half_states(0, kh, vh, cum, 1, own_ref, first_ref, unroll=4)
     add_decays(own_ref, decay, 0)
     for copy in copies:
         copy.wait()
@@ -524,16 +524,9 @@
 
 
 def grad_q_kernel(
-    place_ref, gain_ref, sums_ref, att_own0, att_own1, att_other0, att_other1,
     ends_ref, keep_ref, recv_ref, first_own, first_send, kh, vh, own0, own1, other0, other1,
-    decays0, decays1, columns0, columns1, rows, gs_ref, out_normed, raw, sems,
+    decays0, decays1, columns0, columns1, rows, gs_ref,
 ):
-    copies = []
-    for b, halves in enumerate(((att_own0, att_other0), (att_own1, att_other1))):
-        at = pl.ds(b * BLOCK, BLOCK)
-        normed_block(b, place_ref, gain_ref, sums_ref, halves, rows, raw.at[at])
-        copies.append(pltpu.make_async_copy(raw.at[at], out_normed.at[at], sems.at[b]))
-        copies[-1].start()
     blocks = (((own0, other0), decays0, columns0), ((own1, other1), decays1, columns1))
     for b, (g, decays, columns) in enumerate(blocks):
 
@@ -547,45 +540,37 @@
             rows[b, h] = dot(scores, kh[b, h]) + columns[h] * times_state_t(grad, state)
 
         each_half(keep_ref.shape[0], 8, one)
-    for copy in copies:
-        copy.wait()
-
-
-def grad_query(place, gain, sums, att, ends, arrays):
+
+
+def grad_query(ends, arrays):
     _, heads, dim = ends.shape
     tok = 2 * BLOCK
     return pl.pallas_call(
         grad_q_kernel,
-        in_specs=[NEAR] * 22,
-        out_specs=[NEAR, NEAR, FAR],
+        in_specs=[NEAR] * 15,
+        out_specs=[NEAR, NEAR],
         out_shape=[
             in_vmem(2, heads, BLOCK, dim), in_vmem(2, heads, BLOCK, BLOCK, kind=BF16),
-            jax.ShapeDtypeStruct((tok, heads, dim), BF16),
         ],
-        scratch_shapes=[
-            pltpu.VMEM((tok, heads, dim), BF16),
-            pltpu.SemaphoreType.DMA((2,)),
-        ],
-        compiler_params=params(6),
+        compiler_params=params(4),
         cost_estimate=cost(
             4 * heads * tok * dim * (BLOCK + dim), 12 * heads * tok * dim, heads * tok * BLOCK
         ),
         name="grad_query",
-    )(*near(place, gain, sums, *att, ends, *arrays))
+    )(*near(ends, *arrays))
 
 
 def grad_kv_kernel(
-    place_ref, gs_ref, w0, w1, q0, q1, kh, vh, own0, own1, other0, other1, remaining_ref,
-    second_own, second_send, rows, dk, dv, out_q, raw, sems,
+    place_ref, gain_ref, sums_ref, att_own0, att_own1, att_other0, att_other1,
+    gs_ref, w0, w1, q0, q1, kh, vh, own0, own1, other0, other1, remaining_ref,
+    second_own, second_send, dk, dv, out_normed, raw, sems,
 ):
-    upper = is_upper(place_ref)
     copies = []
-    for b in range(2):
-        for start in range(0, BLOCK, CHUNK):
-            at = pl.ds(b * BLOCK + start, CHUNK)
-            from_heads(raw.at[at], rows.at[b], start, CHUNK, upper)
-            copies.append(pltpu.make_async_copy(raw.at[at], out_q.at[at], sems.at[len(copies)]))
-            copies[-1].start()
+    for b, halves in enumerate(((att_own0, att_other0), (att_own1, att_other1))):
+        at = pl.ds(b * BLOCK, BLOCK)
+        normed_block(b, place_ref, gain_ref, sums_ref, halves, dk, raw.at[at])
+        copies.append(pltpu.make_async_copy(raw.at[at], out_normed.at[at], sems.at[b]))
+        copies[-1].start()
 
     def one(part, i, h):
         columns = remaining_ref[0, h]
@@ -601,23 +586,23 @@
         copy.wait()
 
 
-def grad_key_value(*arrays):
-    _, heads, _, dim = arrays[6].shape
+def grad_key_value(place, gain, sums, att, arrays):
+    heads, dim = gain.shape
     tok = 2 * BLOCK
     return pl.pallas_call(
         grad_kv_kernel,
-        in_specs=[NEAR] * 16,
+        in_specs=[NEAR] * 21,
         out_specs=[NEAR, NEAR, FAR],
         out_shape=[in_vmem(2, heads, BLOCK, dim)] * 2
         + [jax.ShapeDtypeStruct((tok, heads, dim), BF16)],
         scratch_shapes=[
             pltpu.VMEM((tok, heads, dim), BF16),
-            pltpu.SemaphoreType.DMA((tok // CHUNK,)),
+            pltpu.SemaphoreType.DMA((2,)),
         ],
         compiler_params=params(6),
         cost_estimate=cost(4 * heads * tok * dim * (BLOCK + dim), 30 * heads * tok * dim),
         name="grad_key_value",
-    )(*near(*arrays))
+    )(*near(place, gain, sums, *att, *arrays))
 
 
 def finish_rows(part, b, ends_ref, state_ref, kh, vh, remaining_ref, dk, dv, rows_k, rows_v):
@@ -642,9 +627,20 @@
     each_head(half, 8, one)
 
 
-def finish_own_kernel(*refs):
+def finish_own_kernel(place_ref, query_rows, *refs):
+    *refs, out_q, raw, sems = refs
+    upper = is_upper(place_ref)
+    copies = []
+    for b in range(2):
+        for start in range(0, BLOCK, CHUNK):
+            at = pl.ds(b * BLOCK + start, CHUNK)
+            from_heads(raw.at[at], query_rows.at[b], start, CHUNK, upper)
+            copies.append(pltpu.make_async_copy(raw.at[at], out_q.at[at], sems.at[len(copies)]))
+            copies[-1].start()
     for b in range(2):
         finish_rows(0, b, *refs)
+    for copy in copies:
+        copy.wait()
 
 
 def finish_other_kernel(
@@ -665,18 +661,23 @@
         copy.wait()
 
 
-def finish_own(ends, keep, arrays):
+def finish_own(place, query_rows, ends, keep, arrays):
     _, heads, dim = ends.shape
     tok = 2 * BLOCK
     return pl.pallas_call(
         finish_own_kernel,
-        in_specs=[NEAR] * 7,
-        out_specs=[NEAR, NEAR],
-        out_shape=[in_vmem(2, heads, BLOCK, dim)] * 2,
-        compiler_params=params(4),
+        in_specs=[NEAR] * 9,
+        out_specs=[NEAR, NEAR, FAR],
+        out_shape=[in_vmem(2, heads, BLOCK, dim)] * 2
+        + [jax.ShapeDtypeStruct((tok, heads, dim), BF16)],
+        scratch_shapes=[
+            pltpu.VMEM((tok, heads, dim), BF16),
+            pltpu.SemaphoreType.DMA((tok // CHUNK,)),
+        ],
+        compiler_params=params(6),
         cost_estimate=cost(4 * heads * tok * dim * dim, 8 * heads * tok * dim),
         name="finish_own",
-    )(*near(ends, keep, *arrays))
+    )(*near(place, query_rows, ends, keep, *arrays))
 
 
 def finish_other(place, rows, ends, recv, arrays):
@@ -1032,28 +1033,31 @@
 
     def query_task(earlier):
         return grad_query(
-            place, gain, sums, (*own_att, *other_att), follows(ends, earlier),
+            follows(ends, earlier),
             (keep, recv, *firsts, kh, vh, *own_g, *other_g, decays0, decays1, columns0, columns1),
         )
 
     def pair_task(earlier):
         return grad_key_value(
-            place, queries[1], w0, w1, q0, q1, kh, vh, *own_g, *other_g, remaining,
-            follows(seconds[0], earlier), seconds[1], queries[0],
+            place, gain, sums, (*own_att, *other_att),
+            (
+                queries[1], w0, w1, q0, q1, kh, vh, *own_g, *other_g, remaining,
+                follows(seconds[0], earlier), seconds[1],
+            ),
         )
 
     def finish_task(kept):
-        rows.extend(finish_own(ends, kept, (kh, vh, remaining, *pairs[:2])))
-        return rows[-1]
+        rows.extend(finish_own(place, queries[0], ends, kept, (kh, vh, remaining, *pairs[:2])))
+        return rows[0]
 
     _, grad_recv = entering(
         grad_send, own_grad_task, True,
         {1: (query_task, queries), 2: (pair_task, pairs), 3: finish_task},
     )
     grad_k, grad_v = finish_other(
-        place, rows, ends, grad_recv, (kh, vh, remaining, *pairs[:2])
-    )
-    return queries[2], pairs[2], grad_k, grad_v
+        place, rows[:2], ends, grad_recv, (kh, vh, remaining, *pairs[:2])
+    )
+    return pairs[2], rows[2], grad_k, grad_v
 
 
 def solution(mesh):

time: 66.7 us -> 66.3 us (level)
  Pallas kernels: 38.4 us -> 37.7 us
  transfers between devices with their start and end apart: 15 -> 15, of which waited for: 10 -> 10; matrix products, arithmetic and copies ran while one was open for 0% -> 0% of each run, Pallas kernels for 41% -> 40%
where the time goes in v14:
time: 66.3 us; the launch traced here: 66.1 us
  Pallas kernels  37.7 us (57%)
  starting transfers between devices  15.7 us (24%)
  waiting for transfers between devices  11.5 us (17%)
  between operations  0.99 us (1%)
    ppermute x15, starting transfers between devices, swap(): return lax.ppermute(value, axis, [(i, i ^ bit) for i in range(count)])  15.7 us
    ppermute x15, waiting for transfers between devices, swap(): return lax.ppermute(value, axis, [(i, i ^ bit) for i in range(count)])  11.5 us
    pallas_call x2, Pallas kernels, intra(): pl.pallas_call(kernel, in_specs=[NEAR] * 8 + [FAR, FAR] * ahead, out_spec...  7.57 us
    pallas_call x1, Pallas kernels, grad_key_value(): pl.pallas_call(grad_kv_kernel, in_specs=[NEAR] * 21, out_specs=[NEAR, NEA...  5.72 us
    pallas_call x1, Pallas kernels, state_to_send(): pl.pallas_call(state_kernel, in_specs=[NEAR, FAR, FAR, FAR, FAR], out_spe...  4.6 us
    pallas_call x1, Pallas kernels, grad_query(): pl.pallas_call(grad_q_kernel, in_specs=[NEAR] * 15, out_specs=[NEAR, NEAR...  4.35 us
    pallas_call x1, Pallas kernels, finish_other(): pl.pallas_call(finish_other_kernel, in_specs=[NEAR] * 10, out_specs=[FAR,...  3.67 us
    pallas_call x2, Pallas kernels, attend(): pl.pallas_call(functools.partial(attend_kernel, part), in_specs=[NEAR] *...  2.7 us
  transfers between devices with their start and end apart: 15, of which 10 were waited for; matrix products, arithmetic and copies ran while one was open for 0% of the time, Pallas kernels for 40%

profile of v14, /device:TPU:0, one launch (start us, length us, event | category | flops | bytes accessed | tf_op | source)
XLA Modules:
  0.0 66.1 jit_solution(576939443212694486)
XLA Ops:
  0.8 4.6 %state_to_send.1 = (f32[8,136,128]{2,1,0:T(8,128)S(1)}, f32[8,128,128]{2,1,0:T(8,128)S(1)}, bf16[2,16,256,128]{3,2,1,0:T(8,128)(2,1)S(1)}, bf16[2,16,256,128]{3,...) custom-call(f32[8,128]{1,0:T(8,128)S(1)} %broadcast_in_dim.2.place_r, ...), custom_call_target="tpu_custom_call" | custom-call | flops 134217728 | bytes 8388608 | tf_op jit(solution)/shard_map/state_to_send/pallas_call | solution.py:255
  5.4 0.5 collective-permute-start
  6.0 1.6 %own_state.1 = (f32[8,136,128]{2,1,0:T(8,128)S(1)}, f32[8,128,128]{2,1,0:T(8,128)S(1)}, bf16[256,16,128]{2,1,0:T(8,128)(2,1)S(1)}, bf16[256,16,128]{2,1,0:T(8,128)(2,1)S(1)}) custom-call(bf16[2,16,256,128]{3,2,1,0:T(8,128)(2,1)S(1)} %get-tuple-element.95.kh.refs_2_, bf16[2,16,256,128]{3,2,1,0:T(8,128)(2,1)S(1)} %get-tuple-element.96.vh.refs_3_, ...), custom_call_target="tpu_custom_call" | custom-call | flops 134217728 | bytes 2097152 | tf_op jit(solution)/shard_map/own_state/pallas_call | solution.py:301
  7.7 2.9 %collective-permute-start.1 = (f32[4,136,128]{2,1,0:T(8,128)S(1)}, f32[4,136,128]{2,1,0:T(8,128)S(1)}, u32[]{:S(2)}, u32[]{:S(2)}) collective-permute-start(f32[4,136,128]{2,1,0:T(8,128)S(1)} %get-tuple-element.101.refs_1_), channel_id=1, source_target_pairs={{0,8},{4,12},{8,0},{12,4},{16,24},{20,28},{24,16},{28,20},{1,9},{5... | collective-permute-start | bytes 835592 | tf_op jit(solution)/shard_map/ppermute | solution.py:710
  10.6 1.5 %collective-permute-start.2 = (f32[4,128,128]{2,1,0:T(8,128)S(1)}, f32[4,128,128]{2,1,0:T(8,128)S(1)}, u32[]{:S(2)}, u32[]{:S(2)}) collective-permute-start(f32[4,128,128]{2,1,0:T(8,128)S(1)} %get-tuple-element.102.refs_5_), channel_id=1, source_target_pairs={{0,16},{4,20},{8,24},{12,28},{16,0},{20,4},{24,8},{28,12},{1,17},{... | collective-permute-start | bytes 786440 | tf_op jit(solution)/shard_map/ppermute | solution.py:710
  12.1 3.7 %intra_0.1 = (bf16[16,256,128]{2,1,0:T(8,128)(2,1)S(1)}, bf16[16,256,128]{2,1,0:T(8,128)(2,1)S(1)}, bf16[16,256,256]{2,1,0:T(8,128)(2,1)S(1)}, f32[16,3,128,128]...) custom-call(f32[8,128]{1,0:T(8,128)S(1)} %broadcast_in_dim.2.place_r, ...), custom_call_target="tpu_custom_call" | custom-call | flops 1073741824 | bytes 10485760 | tf_op jit(solution)/shard_map/intra_0/pallas_call | solution.py:349
  15.9 3.0 %collective-permute-done.3.refs_3_ = f32[8,128]{1,0:T(8,128)S(1)} collective-permute-done((f32[8,128]{1,0:T(8,128)S(1)}, f32[8,128]{1,0:T(8,128)S(1)}, u32[]{:S(2)}, u32[]{:S(2)}) %collective-permute-start.3) | collective-permute-done | bytes 4128 | tf_op jit(solution)/shard_map/ppermute | solution.py:710
  18.9 1.6 %collective-permute-start.5 = (f32[4,128,128]{2,1,0:T(8,128)S(1)}, f32[4,128,128]{2,1,0:T(8,128)S(1)}, u32[]{:S(2)}, u32[]{:S(2)}) collective-permute-start(f32[4,128,128]{2,1,0:T(8,128)S(1)} %get-tuple-element.115), channel_id=1, source_target_pairs={{0,8},{4,12},{8,0},{12,4},{16,24},{20,28},{24,16},{28,20},{1,9},{5... | collective-permute-start | bytes 786440 | tf_op jit(solution)/shard_map/ppermute | solution.py:710
  20.5 0.5 collective-permute-start.4
  21.0 3.8 %intra_1.1 = (bf16[16,256,128]{2,1,0:T(8,128)(2,1)S(1)}, bf16[16,256,128]{2,1,0:T(8,128)(2,1)S(1)}, bf16[16,256,256]{2,1,0:T(8,128)(2,1)S(1)}, f32[16,3,128,128]...) custom-call(f32[8,128]{1,0:T(8,128)S(1)} %broadcast_in_dim.2.place_ref, ...), custom_call_target="tpu_custom_call" | custom-call | flops 1073741824 | bytes 10485760 | tf_op jit(solution)/shard_map/intra_1/pallas_call | solution.py:349
  24.8 1.4 %collective-permute-done.5.refs_6_ = f32[4,128,128]{2,1,0:T(8,128)S(1)} collective-permute-done((f32[4,128,128]{2,1,0:T(8,128)S(1)}, f32[4,128,128]{2,1,0:T(8,128)S(1)}, u32[]{:S(2)}, u32[]{:S(2)}) %collective-permute-start.5) | collective-permute-done | bytes 262176 | tf_op jit(solution)/shard_map/ppermute | solution.py:710
  26.2 1.2 %collective-permute-done.4.refs_5_ = f32[4,128,128]{2,1,0:T(8,128)S(1)} collective-permute-done((f32[4,128,128]{2,1,0:T(8,128)S(1)}, f32[4,128,128]{2,1,0:T(8,128)S(1)}, u32[]{:S(2)}, u32[]{:S(2)}) %collective-permute-start.4) | collective-permute-done | bytes 262176 | tf_op jit(solution)/shard_map/ppermute | solution.py:710
  27.7 1.1 %attend_0.1 = (f32[8,256,128]{2,1,0:T(8,128)S(1)}, f32[8,256,128]{2,1,0:T(8,128)S(1)}, f32[2,2,256,128]{3,2,1,0:T(8,128)S(1)}) custom-call(f32[16,128]{1,0:T(8,128)S(1)} %get-tuple-element.92.refs_0_.gain_ref, f32[8,128,128]{2,1,0:T(8,128)S(1)} %get-tuple-element.123.refs_1_.keep_ref, bf16[16,256,128]{2,1,0:T(8,128)(2,1)S(1)} %get-tuple-element.133.refs_2_.q0, ...), custom_call_target="tpu_custom_call" | custom-call | flops 268435456 | bytes 8388608 | tf_op jit(solution)/shard_map/attend_0/pallas_call | solution.py:411
  28.8 0.8 %collective-permute-done.6.refs_1_.recv_ref = f32[8,128,128]{2,1,0:T(8,128)S(1)} collective-permute-done((f32[8,128,128]{2,1,0:T(8,128)S(1)}, f32[8,128,128]{2,1,0:T(8,128)S(1)}, u32[]{:S(2)}, u32[]{:S(2)}) %collective-permute-start.6) | collective-permute-done | bytes 524320 | tf_op jit(solution)/shard_map/ppermute | solution.py:710
  29.6 1.6 %attend_1.1 = (f32[8,256,128]{2,1,0:T(8,128)S(1)}, f32[8,256,128]{2,1,0:T(8,128)S(1)}, f32[2,512]{1,0:T(2,128)S(1)}) custom-call(f32[16,128]{1,0:T(8,128)S(1)} %get-tuple-element.92.refs_0_.gain_ref, f32[8,128,128]{2,1,0:T(8,128)S(1)} %collective-permute-done.6.refs_1_.recv_ref, bf16[16,256,128]{2,1,0:T(8,128)(2,1)S(1)} %get-tuple-element.133.refs_2_.q0, ...), custom_call_target="tpu_custom_call" | custom-call | flops 268435456 | bytes 8388608 | tf_op jit(solution)/shard_map/attend_1/pallas_call | solution.py:411
  31.2 1.6 %collective-permute-start.7 = (f32[2,512]{1,0:T(2,128)S(1)}, f32[2,512]{1,0:T(2,128)S(1)}, u32[]{:S(2)}, u32[]{:S(2)}) collective-permute-start(f32[2,512]{1,0:T(2,128)S(1)} %get-tuple-element.132.first_ref), channel_id=1, source_target_pairs={{0,1},{1,0},{2,3},{3,2},{4,5},{5,4},{6,7},{7,6},{8,9},{9,8},{10,11... | collective-permute-start | bytes 12296 | tf_op jit(solution)/shard_map/ppermute | solution.py:710
  32.8 0.9 %scaled_queries.1 = (bf16[2,16,128,256]{3,2,1,0:T(8,128)(2,1)S(1)}, f32[2,16,128]{2,1,0:T(8,128)S(1)}) custom-call(f32[2,16,256]{2,1,0:T(8,128)S(1)} %get-tuple-element.137.cum.cum_ref, bf16[16,256,128]{2,1,0:T(8,128)(2,1)S(1)} %get-tuple-element.133.refs_2_.q0, bf16[16,256,128]{2,1,0:T(8,128)(2,1)S(1)} %get-tuple-element.119.refs_3_.q1), custom_call_target="tpu_custom_call" | custom-call | flops 2097152 | bytes 4194304 | tf_op jit(solution)/shard_map/scaled_queries/pallas_call | solution.py:437
  33.7 1.1 %collective-permute-done.7.second_ref = f32[2,512]{1,0:T(2,128)S(1)} collective-permute-done((f32[2,512]{1,0:T(2,128)S(1)}, f32[2,512]{1,0:T(2,128)S(1)}, u32[]{:S(2)}, u32[]{:S(2)}) %collective-permute-start.7) | collective-permute-done | bytes 4128 | tf_op jit(solution)/shard_map/ppermute | solution.py:710
  34.8 2.6 %collective-permute-start.8 = (f32[2,512]{1,0:T(2,128)S(1)}, f32[2,512]{1,0:T(2,128)S(1)}, u32[]{:S(2)}, u32[]{:S(2)}) collective-permute-start(f32[2,512]{1,0:T(2,128)S(1)} %add.15.first_ref), channel_id=1, source_target_pairs={{0,2},{1,3},{2,0},{3,1},{4,6},{5,7},{6,4},{7,5},{8,10},{9,11},{10,... | collective-permute-start | bytes 12296 | tf_op jit(solution)/shard_map/ppermute | solution.py:710
  37.4 1.8 %remaining_decay.1.remaining_ref.refs_4_ = f32[2,16,256,128]{3,2,1,0:T(8,128)S(1)} custom-call(f32[2,16,256]{2,1,0:T(8,128)S(1)} %get-tuple-element.137.cum.cum_ref), custom_call_target="tpu_custom_call" | custom-call | flops 1048576 | bytes 4194304 | tf_op jit(solution)/shard_map/remaining_decay/pallas_call | solution.py:459
  39.3 0.8 %norm_grad_1.1 = (f32[8,128,128]{2,1,0:T(8,128)S(1)}, f32[8,128,128]{2,1,0:T(8,128)S(1)}, bf16[8,256,128]{2,1,0:T(8,128)(2,1)S(1)}, bf16[8,256,128]{2,1,0:T(8,128)(2,1)S(1)}) custom-call(f32[2,16,128]{2,1,0:T(8,128)S(1)} %get-tuple-element.147.ends_ref.refs_0_, f32[16,128]{1,0:T(8,128)S(1)} %get-tuple-element.92.refs_0_.gain_ref, ...), custom_call_target="tpu_custom_call" | custom-call | flops 134217728 | bytes 7340032 | tf_op jit(solution)/shard_map/norm_grad_1/pallas_call | solution.py:504
  40.2 0.7 %norm_grad_0.1 = (f32[8,128,128]{2,1,0:T(8,128)S(1)}, f32[8,128,128]{2,1,0:T(8,128)S(1)}, bf16[8,256,128]{2,1,0:T(8,128)(2,1)S(1)}, bf16[8,256,128]{2,1,0:T(8,128)(2,1)S(1)}) custom-call(f32[2,16,128]{2,1,0:T(8,128)S(1)} %get-tuple-element.147.ends_ref.refs_0_, f32[16,128]{1,0:T(8,128)S(1)} %get-tuple-element.92.refs_0_.gain_ref, ...), custom_call_target="tpu_custom_call" | custom-call | flops 134217728 | bytes 7340032 | tf_op jit(solution)/shard_map/norm_grad_0/pallas_call | solution.py:504
  40.9 1.2 %collective-permute-done.9.refs_2_ = f32[8,128,128]{2,1,0:T(8,128)S(1)} collective-permute-done((f32[8,128,128]{2,1,0:T(8,128)S(1)}, f32[8,128,128]{2,1,0:T(8,128)S(1)}, u32[]{:S(2)}, u32[]{:S(2)}) %collective-permute-start.9) | collective-permute-done | bytes 524320 | tf_op jit(solution)/shard_map/ppermute | solution.py:710
  42.2 0.6 collective-permute-start.10
  42.8 1.4 %collective-permute-start.11 = (f32[4,128,128]{2,1,0:T(8,128)S(1)}, f32[4,128,128]{2,1,0:T(8,128)S(1)}, u32[]{:S(2)}, u32[]{:S(2)}) collective-permute-start(f32[4,128,128]{2,1,0:T(8,128)S(1)} %get-tuple-element.146.refs_1_), channel_id=1, source_target_pairs={{0,16},{4,20},{8,24},{12,28},{16,0},{20,4},{24,8},{28,12},{1,17},{... | collective-permute-start | bytes 786440 | tf_op jit(solution)/shard_map/ppermute | solution.py:710
  44.1 4.3 %grad_query.1 = (f32[2,16,256,128]{3,2,1,0:T(8,128)S(1)}, bf16[2,16,256,256]{3,2,1,0:T(8,128)(2,1)S(1)}) custom-call(f32[2,16,128]{2,1,0:T(8,128)S(1)} %get-tuple-element.147.ends_ref.refs_0_, f32[8,128,128]{2,1,0:T(8,128)S(1)} %get-tuple-element.123.refs_1_.keep_ref, f32[8,128,128]{2,1,0:T(8,128)S(1)} %collective-permute-done.6.refs_1_.recv_ref, ...), custom_call_target="tpu_custom_call" | custom-call | flops 1610612736 | bytes 12582912 | tf_op jit(solution)/shard_map/grad_query/pallas_call | solution.py:548
  48.5 2.1 %collective-permute-done.10.refs_2_.refs_3_ = f32[4,128,128]{2,1,0:T(8,128)S(1)} collective-permute-done((f32[4,128,128]{2,1,0:T(8,128)S(1)}, f32[4,128,128]{2,1,0:T(8,128)S(1)}, u32[]{:S(2)}, u32[]{:S(2)}) %collective-permute-start.10) | collective-permute-done | bytes 262176 | tf_op jit(solution)/shard_map/ppermute | solution.py:710
  51.0 1.6 %collective-permute-start.13 = (f32[4,128,128]{2,1,0:T(8,128)S(1)}, f32[4,128,128]{2,1,0:T(8,128)S(1)}, u32[]{:S(2)}, u32[]{:S(2)}) collective-permute-start(f32[4,128,128]{2,1,0:T(8,128)S(1)} %later_column.1), channel_id=1, source_target_pairs={{0,8},{4,12},{8,0},{12,4},{16,24},{20,28},{24,16},{28,20},{1,9},{5... | collective-permute-start | bytes 786440 | tf_op jit(solution)/shard_map/ppermute | solution.py:710
  52.5 0.8 %collective-permute-start.12 = (f32[4,128,128]{2,1,0:T(8,128)S(1)}, f32[4,128,128]{2,1,0:T(8,128)S(1)}, u32[]{:S(2)}, u32[]{:S(2)}) collective-permute-start(f32[4,128,128]{2,1,0:T(8,128)S(1)} %later_row.1), channel_id=1, source_target_pairs={{0,16},{4,20},{8,24},{12,28},{16,0},{20,4},{24,8},{28,12},{1,17},{... | collective-permute-start | bytes 786440 | tf_op jit(solution)/shard_map/ppermute | solution.py:710
  53.3 5.7 %grad_key_value.1 = (f32[2,16,256,128]{3,2,1,0:T(8,128)S(1)}, f32[2,16,256,128]{3,2,1,0:T(8,128)S(1)}, bf16[512,16,128]{2,1,0:T(8,128)(2,1)}) custom-call(f32[8,128]{1,0:T(8,128)S(1)} %broadcast_in_dim.2.place_ref, f32[16,128]{1,0:T(8,128)S(1)} %get-tuple-element.92.refs_0_.gain_ref, f32[2,512]{1,0:T(2,128)S(1)} %add.16.sums_ref, ...), custom_call_target="tpu_custom_call" | custom-call | flops 1610612736 | bytes 31457280 | tf_op jit(solution)/shard_map/grad_key_value/pallas_call | solution.py:592
  59.7 2.6 %finish_own.1 = (f32[2,16,256,128]{3,2,1,0:T(8,128)S(1)}, f32[2,16,256,128]{3,2,1,0:T(8,128)S(1)}, bf16[512,16,128]{2,1,0:T(8,128)(2,1)}) custom-call(f32[8,128]{1,0:T(8,128)S(1)} %broadcast_in_dim.2.place_ref, f32[2,16,256,128]{3,2,1,0:T(8,128)S(1)} %get-tuple-element.159.query_rows, f32[2,16,128]{2,1,0:T(8,128)S(1)} %get-tuple-element.147.ends_ref.refs_0_, ...), custom_call_target="tpu_custom_call" | custom-call | flops 536870912 | bytes 8388608 | tf_op jit(solution)/shard_map/finish_own/pallas_call | solution.py:667
  62.3 3.7 %finish_other.1 = (bf16[512,16,128]{2,1,0:T(8,128)(2,1)}, bf16[512,16,128]{2,1,0:T(8,128)(2,1)}, f32[2,16,256,128]{3,2,1,0:T(8,128)S(1)}, f32[2,16,256,128]{3,2,1,0:T(8,128)S(1)}) custom-call(f32[8,128]{1,0:T(8,128)S(1)} %broadcast_in_dim.2.place_ref, ...), custom_call_target="tpu_custom_call", output_to_operand_aliasing={{2}: (1, {}), {3}: (2, {})} | custom-call | flops 536870912 | bytes 8388608 | tf_op jit(solution)/shard_map/finish_other/pallas_call | solution.py:687
  (26 shorter events, 1.9 us)
Async XLA Ops:
  5.4 2.1 %collective-permute-start = (f32[8,136,128]{2,1,0:T(8,128)S(1)}, f32[8,136,128]{2,1,0:T(8,128)S(1)}, u32[]{:S(2)}, u32[]{:S(2)}) collective-permute-start(f32[8,136,128]{2,1,0:T(8,128)S(1)} %get-tuple-element.94), channel_id=1, source_target_pairs={{0,4},{4,0},{8,12},{12,8},{16,20},{20,16},{24,28},{28,24},{1,5},{5... | collective-permute-start | bytes 1671176 | tf_op jit(solution)/shard_map/ppermute | solution.py:710
  7.7 11.2 %collective-permute-start.1 = (f32[4,136,128]{2,1,0:T(8,128)S(1)}, f32[4,136,128]{2,1,0:T(8,128)S(1)}, u32[]{:S(2)}, u32[]{:S(2)}) collective-permute-start(f32[4,136,128]{2,1,0:T(8,128)S(1)} %get-tuple-element.101.refs_1_), channel_id=1, source_target_pairs={{0,8},{4,12},{8,0},{12,4},{16,24},{20,28},{24,16},{28,20},{1,9},{5... | collective-permute-start | bytes 835592 | tf_op jit(solution)/shard_map/ppermute | solution.py:710
  10.6 8.2 %collective-permute-start.2 = (f32[4,128,128]{2,1,0:T(8,128)S(1)}, f32[4,128,128]{2,1,0:T(8,128)S(1)}, u32[]{:S(2)}, u32[]{:S(2)}) collective-permute-start(f32[4,128,128]{2,1,0:T(8,128)S(1)} %get-tuple-element.102.refs_5_), channel_id=1, source_target_pairs={{0,16},{4,20},{8,24},{12,28},{16,0},{20,4},{24,8},{28,12},{1,17},{... | collective-permute-start | bytes 786440 | tf_op jit(solution)/shard_map/ppermute | solution.py:710
  12.1 6.7 %collective-permute-start.3 = (f32[8,128]{1,0:T(8,128)S(1)}, f32[8,128]{1,0:T(8,128)S(1)}, u32[]{:S(2)}, u32[]{:S(2)}) collective-permute-start(f32[8,128]{1,0:T(8,128)S(1)} %get-tuple-element.100.refs_0_.refs_2_), channel_id=1, source_target_pairs={{0,24},{4,28},{8,16},{12,20},{16,8},{20,12},{24,0},{28,4},{1,25},{... | collective-permute-start | bytes 12296 | tf_op jit(solution)/shard_map/ppermute | solution.py:710
  18.9 7.3 %collective-permute-start.5 = (f32[4,128,128]{2,1,0:T(8,128)S(1)}, f32[4,128,128]{2,1,0:T(8,128)S(1)}, u32[]{:S(2)}, u32[]{:S(2)}) collective-permute-start(f32[4,128,128]{2,1,0:T(8,128)S(1)} %get-tuple-element.115), channel_id=1, source_target_pairs={{0,8},{4,12},{8,0},{12,4},{16,24},{20,28},{24,16},{28,20},{1,9},{5... | collective-permute-start | bytes 786440 | tf_op jit(solution)/shard_map/ppermute | solution.py:710
  20.5 6.9 %collective-permute-start.4 = (f32[4,128,128]{2,1,0:T(8,128)S(1)}, f32[4,128,128]{2,1,0:T(8,128)S(1)}, u32[]{:S(2)}, u32[]{:S(2)}) collective-permute-start(f32[4,128,128]{2,1,0:T(8,128)S(1)} %earlier_row.1), channel_id=1, source_target_pairs={{0,16},{4,20},{8,24},{12,28},{16,0},{20,4},{24,8},{28,12},{1,17},{... | collective-permute-start | bytes 786440 | tf_op jit(solution)/shard_map/ppermute | solution.py:710
  27.6 2.0 %collective-permute-start.6 = (f32[8,128,128]{2,1,0:T(8,128)S(1)}, f32[8,128,128]{2,1,0:T(8,128)S(1)}, u32[]{:S(2)}, u32[]{:S(2)}) collective-permute-start(f32[8,128,128]{2,1,0:T(8,128)S(1)} %get-tuple-element.122), channel_id=1, source_target_pairs={{0,4},{4,0},{8,12},{12,8},{16,20},{20,16},{24,28},{28,24},{1,5},{5... | collective-permute-start | bytes 1572872 | tf_op jit(solution)/shard_map/ppermute | solution.py:710
  31.2 3.6 %collective-permute-start.7 = (f32[2,512]{1,0:T(2,128)S(1)}, f32[2,512]{1,0:T(2,128)S(1)}, u32[]{:S(2)}, u32[]{:S(2)}) collective-permute-start(f32[2,512]{1,0:T(2,128)S(1)} %get-tuple-element.132.first_ref), channel_id=1, source_target_pairs={{0,1},{1,0},{2,3},{3,2},{4,5},{5,4},{6,7},{7,6},{8,9},{9,8},{10,11... | collective-permute-start | bytes 12296 | tf_op jit(solution)/shard_map/ppermute | solution.py:710
  34.8 4.5 %collective-permute-start.8 = (f32[2,512]{1,0:T(2,128)S(1)}, f32[2,512]{1,0:T(2,128)S(1)}, u32[]{:S(2)}, u32[]{:S(2)}) collective-permute-start(f32[2,512]{1,0:T(2,128)S(1)} %add.15.first_ref), channel_id=1, source_target_pairs={{0,2},{1,3},{2,0},{3,1},{4,6},{5,7},{6,4},{7,5},{8,10},{9,11},{10,... | collective-permute-start | bytes 12296 | tf_op jit(solution)/shard_map/ppermute | solution.py:710
  40.1 2.0 %collective-permute-start.9 = (f32[8,128,128]{2,1,0:T(8,128)S(1)}, f32[8,128,128]{2,1,0:T(8,128)S(1)}, u32[]{:S(2)}, u32[]{:S(2)}) collective-permute-start(f32[8,128,128]{2,1,0:T(8,128)S(1)} %get-tuple-element.143), channel_id=1, source_target_pairs={{0,4},{4,0},{8,12},{12,8},{16,20},{20,16},{24,28},{28,24},{1,5},{5... | collective-permute-start | bytes 1572872 | tf_op jit(solution)/shard_map/ppermute | solution.py:710
  42.2 8.4 %collective-permute-start.10 = (f32[4,128,128]{2,1,0:T(8,128)S(1)}, f32[4,128,128]{2,1,0:T(8,128)S(1)}, u32[]{:S(2)}, u32[]{:S(2)}) collective-permute-start(f32[4,128,128]{2,1,0:T(8,128)S(1)} %get-tuple-element.158.refs_1_), channel_id=1, source_target_pairs={{0,8},{4,12},{8,0},{12,4},{16,24},{20,28},{24,16},{28,20},{1,9},{5... | collective-permute-start | bytes 786440 | tf_op jit(solution)/shard_map/ppermute | solution.py:710
  42.8 8.1 %collective-permute-start.11 = (f32[4,128,128]{2,1,0:T(8,128)S(1)}, f32[4,128,128]{2,1,0:T(8,128)S(1)}, u32[]{:S(2)}, u32[]{:S(2)}) collective-permute-start(f32[4,128,128]{2,1,0:T(8,128)S(1)} %get-tuple-element.146.refs_1_), channel_id=1, source_target_pairs={{0,16},{4,20},{8,24},{12,28},{16,0},{20,4},{24,8},{28,12},{1,17},{... | collective-permute-start | bytes 786440 | tf_op jit(solution)/shard_map/ppermute | solution.py:710
  51.0 8.1 %collective-permute-start.13 = (f32[4,128,128]{2,1,0:T(8,128)S(1)}, f32[4,128,128]{2,1,0:T(8,128)S(1)}, u32[]{:S(2)}, u32[]{:S(2)}) collective-permute-start(f32[4,128,128]{2,1,0:T(8,128)S(1)} %later_column.1), channel_id=1, source_target_pairs={{0,8},{4,12},{8,0},{12,4},{16,24},{20,28},{24,16},{28,20},{1,9},{5... | collective-permute-start | bytes 786440 | tf_op jit(solution)/shard_map/ppermute | solution.py:710
  52.5 6.9 %collective-permute-start.12 = (f32[4,128,128]{2,1,0:T(8,128)S(1)}, f32[4,128,128]{2,1,0:T(8,128)S(1)}, u32[]{:S(2)}, u32[]{:S(2)}) collective-permute-start(f32[4,128,128]{2,1,0:T(8,128)S(1)} %later_row.1), channel_id=1, source_target_pairs={{0,16},{4,20},{8,24},{12,28},{16,0},{20,4},{24,8},{28,12},{1,17},{... | collective-permute-start | bytes 786440 | tf_op jit(solution)/shard_map/ppermute | solution.py:710
  59.6 2.6 %collective-permute-start.14 = (f32[8,128,128]{2,1,0:T(8,128)S(1)}, f32[8,128,128]{2,1,0:T(8,128)S(1)}, u32[]{:S(2)}, u32[]{:S(2)}) collective-permute-start(f32[8,128,128]{2,1,0:T(8,128)S(1)} %get-tuple-element.174), channel_id=1, source_target_pairs={{0,4},{4,0},{8,12},{12,8},{16,20},{20,16},{24,28},{28,24},{1,5},{5... | collective-permute-start | bytes 1572872 | tf_op jit(solution)/shard_map/ppermute | solution.py:710

commit v15 on v14

--- a/solution.py
+++ b/solution.py
@@ -524,9 +524,11 @@
 
 
 def grad_q_kernel(
-    ends_ref, keep_ref, recv_ref, first_own, first_send, kh, vh, own0, own1, other0, other1,
-    decays0, decays1, columns0, columns1, rows, gs_ref,
+    place_ref, ends_ref, keep_ref, recv_ref, first_own, first_send, kh, vh, own0, own1, other0,
+    other1, decays0, decays1, columns0, columns1, gs_ref, out_q, rows, raw, sems,
 ):
+    upper = is_upper(place_ref)
+    copies = []
     blocks = (((own0, other0), decays0, columns0), ((own1, other1), decays1, columns1))
     for b, (g, decays, columns) in enumerate(blocks):
 
@@ -537,27 +539,40 @@
             state = (keep_ref, recv_ref)[part][i]
             if b:
                 state = ends_ref[0, pl.ds(h, 1)] * state + (first_own, first_send)[part][i]
-            rows[b, h] = dot(scores, kh[b, h]) + columns[h] * times_state_t(grad, state)
+            rows[h] = dot(scores, kh[b, h]) + columns[h] * times_state_t(grad, state)
 
         each_half(keep_ref.shape[0], 8, one)
-
-
-def grad_query(ends, arrays):
+        for start in range(0, BLOCK, CHUNK):
+            at = pl.ds(b * BLOCK + start, CHUNK)
+            from_heads(raw.at[at], rows, start, CHUNK, upper)
+            copies.append(pltpu.make_async_copy(raw.at[at], out_q.at[at], sems.at[len(copies)]))
+            copies[-1].start()
+    for copy in copies:
+        copy.wait()
+
+
+def grad_query(place, ends, arrays):
     _, heads, dim = ends.shape
     tok = 2 * BLOCK
     return pl.pallas_call(
         grad_q_kernel,
-        in_specs=[NEAR] * 15,
-        out_specs=[NEAR, NEAR],
+        in_specs=[NEAR] * 16,
+        out_specs=[NEAR, FAR],
         out_shape=[
-            in_vmem(2, heads, BLOCK, dim), in_vmem(2, heads, BLOCK, BLOCK, kind=BF16),
+            in_vmem(2, heads, BLOCK, BLOCK, kind=BF16),
+            jax.ShapeDtypeStruct((tok, heads, dim), BF16),
         ],
-        compiler_params=params(4),
+        scratch_shapes=[
+            pltpu.VMEM((heads, BLOCK, dim), F32),
+            pltpu.VMEM((tok, heads, dim), BF16),
+            pltpu.SemaphoreType.DMA((tok // CHUNK,)),
+        ],
+        compiler_params=params(8),
         cost_estimate=cost(
             4 * heads * tok * dim * (BLOCK + dim), 12 * heads * tok * dim, heads * tok * BLOCK
         ),
         name="grad_query",
-    )(*near(ends, *arrays))
+    )(*near(place, ends, *arrays))
 
 
 def grad_kv_kernel(
@@ -627,20 +642,9 @@
     each_head(half, 8, one)
 
 
-def finish_own_kernel(place_ref, query_rows, *refs):
-    *refs, out_q, raw, sems = refs
-    upper = is_upper(place_ref)
-    copies = []
-    for b in range(2):
-        for start in range(0, BLOCK, CHUNK):
-            at = pl.ds(b * BLOCK + start, CHUNK)
-            from_heads(raw.at[at], query_rows.at[b], start, CHUNK, upper)
-            copies.append(pltpu.make_async_copy(raw.at[at], out_q.at[at], sems.at[len(copies)]))
-            copies[-1].start()
+def finish_own_kernel(*refs):
     for b in range(2):
         finish_rows(0, b, *refs)
-    for copy in copies:
-        copy.wait()
 
 
 def finish_other_kernel(
@@ -661,23 +665,18 @@
         copy.wait()
 
 
-def finish_own(place, query_rows, ends, keep, arrays):
+def finish_own(ends, keep, arrays):
     _, heads, dim = ends.shape
     tok = 2 * BLOCK
     return pl.pallas_call(
         finish_own_kernel,
-        in_specs=[NEAR] * 9,
-        out_specs=[NEAR, NEAR, FAR],
-        out_shape=[in_vmem(2, heads, BLOCK, dim)] * 2
-        + [jax.ShapeDtypeStruct((tok, heads, dim), BF16)],
-        scratch_shapes=[
-            pltpu.VMEM((tok, heads, dim), BF16),
-            pltpu.SemaphoreType.DMA((tok // CHUNK,)),
-        ],
-        compiler_params=params(6),
+        in_specs=[NEAR] * 7,
+        out_specs=[NEAR, NEAR],
+        out_shape=[in_vmem(2, heads, BLOCK, dim)] * 2,
+        compiler_params=params(4),
         cost_estimate=cost(4 * heads * tok * dim * dim, 8 * heads * tok * dim),
         name="finish_own",
-    )(*near(place, query_rows, ends, keep, *arrays))
+    )(*near(ends, keep, *arrays))
 
 
 def finish_other(place, rows, ends, recv, arrays):
@@ -1033,7 +1032,7 @@
 
     def query_task(earlier):
         return grad_query(
-            follows(ends, earlier),
+            place, follows(ends, earlier),
             (keep, recv, *firsts, kh, vh, *own_g, *other_g, decays0, decays1, columns0, columns1),
         )
 
@@ -1041,13 +1040,13 @@
         return grad_key_value(
             place, gain, sums, (*own_att, *other_att),
             (
-                queries[1], w0, w1, q0, q1, kh, vh, *own_g, *other_g, remaining,
+                queries[0], w0, w1, q0, q1, kh, vh, *own_g, *other_g, remaining,
                 follows(seconds[0], earlier), seconds[1],
             ),
         )
 
     def finish_task(kept):
-        rows.extend(finish_own(place, queries[0], ends, kept, (kh, vh, remaining, *pairs[:2])))
+        rows.extend(finish_own(ends, kept, (kh, vh, remaining, *pairs[:2])))
         return rows[0]
 
     _, grad_recv = entering(
@@ -1055,9 +1054,9 @@
         {1: (query_task, queries), 2: (pair_task, pairs), 3: finish_task},
     )
     grad_k, grad_v = finish_other(
-        place, rows[:2], ends, grad_recv, (kh, vh, remaining, *pairs[:2])
-    )
-    return pairs[2], rows[2], grad_k, grad_v
+        place, rows, ends, grad_recv, (kh, vh, remaining, *pairs[:2])
+    )
+    return pairs[2], queries[1], grad_k, grad_v
 
 
 def solution(mesh):

time: 66.3 us -> 65.6 us (0.989)
  waiting for transfers between devices: 11.5 us -> 10.5 us
    ppermute x15, waiting for transfers between devices: 11.5 us -> 10.5 us  [swap(): return lax.ppermute(value, axis, [(i, i ^ bit) for i in range(count)])]
  transfers between devices with their start and end apart: 15 -> 15, of which waited for: 10 -> 11; matrix products, arithmetic and copies ran while one was open for 0% -> 0% of each run, Pallas kernels for 40% -> 41%
where the time goes in v15:
time: 65.6 us; the launch traced here: 65.5 us
  Pallas kernels  38.1 us (58%)
  starting transfers between devices  15.7 us (24%)
  waiting for transfers between devices  10.5 us (16%)
  between operations  0.99 us (2%)
    ppermute x15, starting transfers between devices, swap(): return lax.ppermute(value, axis, [(i, i ^ bit) for i in range(count)])  15.7 us
    ppermute x15, waiting for transfers between devices, swap(): return lax.ppermute(value, axis, [(i, i ^ bit) for i in range(count)])  10.5 us
    pallas_call x2, Pallas kernels, intra(): pl.pallas_call(kernel, in_specs=[NEAR] * 8 + [FAR, FAR] * ahead, out_spec...  7.62 us
    pallas_call x1, Pallas kernels, grad_query(): pl.pallas_call(grad_q_kernel, in_specs=[NEAR] * 16, out_specs=[NEAR, FAR]...  6.25 us
    pallas_call x1, Pallas kernels, grad_key_value(): pl.pallas_call(grad_kv_kernel, in_specs=[NEAR] * 21, out_specs=[NEAR, NEA...  5.77 us
    pallas_call x1, Pallas kernels, state_to_send(): pl.pallas_call(state_kernel, in_specs=[NEAR, FAR, FAR, FAR, FAR], out_spe...  4.61 us
    pallas_call x1, Pallas kernels, finish_other(): pl.pallas_call(finish_other_kernel, in_specs=[NEAR] * 10, out_specs=[FAR,...  3.66 us
    pallas_call x2, Pallas kernels, attend(): pl.pallas_call(functools.partial(attend_kernel, part), in_specs=[NEAR] *...  2.64 us
  transfers between devices with their start and end apart: 15, of which 11 were waited for; matrix products, arithmetic and copies ran while one was open for 0% of the time, Pallas kernels for 41%

profile of v15, /device:TPU:0, one launch (start us, length us, event | category | flops | bytes accessed | tf_op | source)
XLA Modules:
  0.0 65.5 jit_solution(5937206154756301171)
XLA Ops:
  0.8 4.6 %state_to_send.1 = (f32[8,136,128]{2,1,0:T(8,128)S(1)}, f32[8,128,128]{2,1,0:T(8,128)S(1)}, bf16[2,16,256,128]{3,2,1,0:T(8,128)(2,1)S(1)}, bf16[2,16,256,128]{3,...) custom-call(f32[8,128]{1,0:T(8,128)S(1)} %broadcast_in_dim.2.place_r, ...), custom_call_target="tpu_custom_call" | custom-call | flops 134217728 | bytes 8388608 | tf_op jit(solution)/shard_map/state_to_send/pallas_call | solution.py:255
  5.4 0.5 collective-permute-start
  6.0 1.6 %own_state.1 = (f32[8,136,128]{2,1,0:T(8,128)S(1)}, f32[8,128,128]{2,1,0:T(8,128)S(1)}, bf16[256,16,128]{2,1,0:T(8,128)(2,1)S(1)}, bf16[256,16,128]{2,1,0:T(8,128)(2,1)S(1)}) custom-call(bf16[2,16,256,128]{3,2,1,0:T(8,128)(2,1)S(1)} %get-tuple-element.94.kh.refs_2_, bf16[2,16,256,128]{3,2,1,0:T(8,128)(2,1)S(1)} %get-tuple-element.95.vh.refs_3_, ...), custom_call_target="tpu_custom_call" | custom-call | flops 134217728 | bytes 2097152 | tf_op jit(solution)/shard_map/own_state/pallas_call | solution.py:301
  7.7 2.9 %collective-permute-start.1 = (f32[4,136,128]{2,1,0:T(8,128)S(1)}, f32[4,136,128]{2,1,0:T(8,128)S(1)}, u32[]{:S(2)}, u32[]{:S(2)}) collective-permute-start(f32[4,136,128]{2,1,0:T(8,128)S(1)} %get-tuple-element.100.refs_1_), channel_id=1, source_target_pairs={{0,8},{4,12},{8,0},{12,4},{16,24},{20,28},{24,16},{28,20},{1,9},{5... | collective-permute-start | bytes 835592 | tf_op jit(solution)/shard_map/ppermute | solution.py:709
  10.6 1.5 %collective-permute-start.2 = (f32[4,128,128]{2,1,0:T(8,128)S(1)}, f32[4,128,128]{2,1,0:T(8,128)S(1)}, u32[]{:S(2)}, u32[]{:S(2)}) collective-permute-start(f32[4,128,128]{2,1,0:T(8,128)S(1)} %get-tuple-element.101.refs_5_), channel_id=1, source_target_pairs={{0,16},{4,20},{8,24},{12,28},{16,0},{20,4},{24,8},{28,12},{1,17},{... | collective-permute-start | bytes 786440 | tf_op jit(solution)/shard_map/ppermute | solution.py:709
  12.1 3.8 %intra_0.1 = (bf16[16,256,128]{2,1,0:T(8,128)(2,1)S(1)}, bf16[16,256,128]{2,1,0:T(8,128)(2,1)S(1)}, bf16[16,256,256]{2,1,0:T(8,128)(2,1)S(1)}, f32[16,3,128,128]...) custom-call(f32[8,128]{1,0:T(8,128)S(1)} %broadcast_in_dim.2.place_r, ...), custom_call_target="tpu_custom_call" | custom-call | flops 1073741824 | bytes 10485760 | tf_op jit(solution)/shard_map/intra_0/pallas_call | solution.py:349
  15.9 2.9 %collective-permute-done.3.refs_3_ = f32[8,128]{1,0:T(8,128)S(1)} collective-permute-done((f32[8,128]{1,0:T(8,128)S(1)}, f32[8,128]{1,0:T(8,128)S(1)}, u32[]{:S(2)}, u32[]{:S(2)}) %collective-permute-start.3) | collective-permute-done | bytes 4128 | tf_op jit(solution)/shard_map/ppermute | solution.py:709
  18.9 1.6 %collective-permute-start.5 = (f32[4,128,128]{2,1,0:T(8,128)S(1)}, f32[4,128,128]{2,1,0:T(8,128)S(1)}, u32[]{:S(2)}, u32[]{:S(2)}) collective-permute-start(f32[4,128,128]{2,1,0:T(8,128)S(1)} %get-tuple-element.114), channel_id=1, source_target_pairs={{0,8},{4,12},{8,0},{12,4},{16,24},{20,28},{24,16},{28,20},{1,9},{5... | collective-permute-start | bytes 786440 | tf_op jit(solution)/shard_map/ppermute | solution.py:709
  20.5 0.5 collective-permute-start.4
  21.0 3.9 %intra_1.1 = (bf16[16,256,128]{2,1,0:T(8,128)(2,1)S(1)}, bf16[16,256,128]{2,1,0:T(8,128)(2,1)S(1)}, bf16[16,256,256]{2,1,0:T(8,128)(2,1)S(1)}, f32[16,3,128,128]...) custom-call(f32[8,128]{1,0:T(8,128)S(1)} %broadcast_in_dim.2.place_ref, ...), custom_call_target="tpu_custom_call" | custom-call | flops 1073741824 | bytes 10485760 | tf_op jit(solution)/shard_map/intra_1/pallas_call | solution.py:349
  24.9 1.4 %collective-permute-done.5.refs_6_ = f32[4,128,128]{2,1,0:T(8,128)S(1)} collective-permute-done((f32[4,128,128]{2,1,0:T(8,128)S(1)}, f32[4,128,128]{2,1,0:T(8,128)S(1)}, u32[]{:S(2)}, u32[]{:S(2)}) %collective-permute-start.5) | collective-permute-done | bytes 262176 | tf_op jit(solution)/shard_map/ppermute | solution.py:709
  26.2 1.2 %collective-permute-done.4.refs_5_ = f32[4,128,128]{2,1,0:T(8,128)S(1)} collective-permute-done((f32[4,128,128]{2,1,0:T(8,128)S(1)}, f32[4,128,128]{2,1,0:T(8,128)S(1)}, u32[]{:S(2)}, u32[]{:S(2)}) %collective-permute-start.4) | collective-permute-done | bytes 262176 | tf_op jit(solution)/shard_map/ppermute | solution.py:709
  27.7 1.0 %attend_0.1 = (f32[8,256,128]{2,1,0:T(8,128)S(1)}, f32[8,256,128]{2,1,0:T(8,128)S(1)}, f32[2,2,256,128]{3,2,1,0:T(8,128)S(1)}) custom-call(f32[16,128]{1,0:T(8,128)S(1)} %get-tuple-element.91.refs_0_.gain_ref, f32[8,128,128]{2,1,0:T(8,128)S(1)} %get-tuple-element.122.refs_1_.keep_ref, bf16[16,256,128]{2,1,0:T(8,128)(2,1)S(1)} %get-tuple-element.132.refs_2_.q0, ...), custom_call_target="tpu_custom_call" | custom-call | flops 268435456 | bytes 8388608 | tf_op jit(solution)/shard_map/attend_0/pallas_call | solution.py:411
  28.7 0.9 %collective-permute-done.6.refs_1_.recv_ref = f32[8,128,128]{2,1,0:T(8,128)S(1)} collective-permute-done((f32[8,128,128]{2,1,0:T(8,128)S(1)}, f32[8,128,128]{2,1,0:T(8,128)S(1)}, u32[]{:S(2)}, u32[]{:S(2)}) %collective-permute-start.6) | collective-permute-done | bytes 524320 | tf_op jit(solution)/shard_map/ppermute | solution.py:709
  29.6 1.6 %attend_1.1 = (f32[8,256,128]{2,1,0:T(8,128)S(1)}, f32[8,256,128]{2,1,0:T(8,128)S(1)}, f32[2,512]{1,0:T(2,128)S(1)}) custom-call(f32[16,128]{1,0:T(8,128)S(1)} %get-tuple-element.91.refs_0_.gain_ref, f32[8,128,128]{2,1,0:T(8,128)S(1)} %collective-permute-done.6.refs_1_.recv_ref, bf16[16,256,128]{2,1,0:T(8,128)(2,1)S(1)} %get-tuple-element.132.refs_2_.q0, ...), custom_call_target="tpu_custom_call" | custom-call | flops 268435456 | bytes 8388608 | tf_op jit(solution)/shard_map/attend_1/pallas_call | solution.py:411
  31.2 1.6 %collective-permute-start.7 = (f32[2,512]{1,0:T(2,128)S(1)}, f32[2,512]{1,0:T(2,128)S(1)}, u32[]{:S(2)}, u32[]{:S(2)}) collective-permute-start(f32[2,512]{1,0:T(2,128)S(1)} %get-tuple-element.131.first_ref), channel_id=1, source_target_pairs={{0,1},{1,0},{2,3},{3,2},{4,5},{5,4},{6,7},{7,6},{8,9},{9,8},{10,11... | collective-permute-start | bytes 12296 | tf_op jit(solution)/shard_map/ppermute | solution.py:709
  32.8 0.9 %scaled_queries.1 = (bf16[2,16,128,256]{3,2,1,0:T(8,128)(2,1)S(1)}, f32[2,16,128]{2,1,0:T(8,128)S(1)}) custom-call(f32[2,16,256]{2,1,0:T(8,128)S(1)} %get-tuple-element.136.cum.cum_ref, bf16[16,256,128]{2,1,0:T(8,128)(2,1)S(1)} %get-tuple-element.132.refs_2_.q0, bf16[16,256,128]{2,1,0:T(8,128)(2,1)S(1)} %get-tuple-element.118.refs_3_.q1), custom_call_target="tpu_custom_call" | custom-call | flops 2097152 | bytes 4194304 | tf_op jit(solution)/shard_map/scaled_queries/pallas_call | solution.py:437
  33.7 1.1 %collective-permute-done.7.second_ref = f32[2,512]{1,0:T(2,128)S(1)} collective-permute-done((f32[2,512]{1,0:T(2,128)S(1)}, f32[2,512]{1,0:T(2,128)S(1)}, u32[]{:S(2)}, u32[]{:S(2)}) %collective-permute-start.7) | collective-permute-done | bytes 4128 | tf_op jit(solution)/shard_map/ppermute | solution.py:709
  34.9 2.6 %collective-permute-start.8 = (f32[2,512]{1,0:T(2,128)S(1)}, f32[2,512]{1,0:T(2,128)S(1)}, u32[]{:S(2)}, u32[]{:S(2)}) collective-permute-start(f32[2,512]{1,0:T(2,128)S(1)} %add.15.first_ref), channel_id=1, source_target_pairs={{0,2},{1,3},{2,0},{3,1},{4,6},{5,7},{6,4},{7,5},{8,10},{9,11},{10,... | collective-permute-start | bytes 12296 | tf_op jit(solution)/shard_map/ppermute | solution.py:709
  37.4 1.8 %remaining_decay.1.remaining_ref.refs_4_ = f32[2,16,256,128]{3,2,1,0:T(8,128)S(1)} custom-call(f32[2,16,256]{2,1,0:T(8,128)S(1)} %get-tuple-element.136.cum.cum_ref), custom_call_target="tpu_custom_call" | custom-call | flops 1048576 | bytes 4194304 | tf_op jit(solution)/shard_map/remaining_decay/pallas_call | solution.py:459
  39.4 0.8 %norm_grad_1.1 = (f32[8,128,128]{2,1,0:T(8,128)S(1)}, f32[8,128,128]{2,1,0:T(8,128)S(1)}, bf16[8,256,128]{2,1,0:T(8,128)(2,1)S(1)}, bf16[8,256,128]{2,1,0:T(8,128)(2,1)S(1)}) custom-call(f32[2,16,128]{2,1,0:T(8,128)S(1)} %get-tuple-element.146.ends_ref.refs_0_, f32[16,128]{1,0:T(8,128)S(1)} %get-tuple-element.91.refs_0_.gain_ref, ...), custom_call_target="tpu_custom_call" | custom-call | flops 134217728 | bytes 7340032 | tf_op jit(solution)/shard_map/norm_grad_1/pallas_call | solution.py:504
  40.3 0.8 %norm_grad_0.1 = (f32[8,128,128]{2,1,0:T(8,128)S(1)}, f32[8,128,128]{2,1,0:T(8,128)S(1)}, bf16[8,256,128]{2,1,0:T(8,128)(2,1)S(1)}, bf16[8,256,128]{2,1,0:T(8,128)(2,1)S(1)}) custom-call(f32[2,16,128]{2,1,0:T(8,128)S(1)} %get-tuple-element.146.ends_ref.refs_0_, f32[16,128]{1,0:T(8,128)S(1)} %get-tuple-element.91.refs_0_.gain_ref, ...), custom_call_target="tpu_custom_call" | custom-call | flops 134217728 | bytes 7340032 | tf_op jit(solution)/shard_map/norm_grad_0/pallas_call | solution.py:504
  41.1 1.1 %collective-permute-done.9.refs_2_ = f32[8,128,128]{2,1,0:T(8,128)S(1)} collective-permute-done((f32[8,128,128]{2,1,0:T(8,128)S(1)}, f32[8,128,128]{2,1,0:T(8,128)S(1)}, u32[]{:S(2)}, u32[]{:S(2)}) %collective-permute-start.9) | collective-permute-done | bytes 524320 | tf_op jit(solution)/shard_map/ppermute | solution.py:709
  42.3 0.6 collective-permute-start.10
  42.9 1.4 %collective-permute-start.11 = (f32[4,128,128]{2,1,0:T(8,128)S(1)}, f32[4,128,128]{2,1,0:T(8,128)S(1)}, u32[]{:S(2)}, u32[]{:S(2)}) collective-permute-start(f32[4,128,128]{2,1,0:T(8,128)S(1)} %get-tuple-element.145.refs_1_), channel_id=1, source_target_pairs={{0,16},{4,20},{8,24},{12,28},{16,0},{20,4},{24,8},{28,12},{1,17},{... | collective-permute-start | bytes 786440 | tf_op jit(solution)/shard_map/ppermute | solution.py:709
  44.2 6.2 %grad_query.1 = (bf16[2,16,256,256]{3,2,1,0:T(8,128)(2,1)S(1)}, bf16[512,16,128]{2,1,0:T(8,128)(2,1)}) custom-call(f32[8,128]{1,0:T(8,128)S(1)} %broadcast_in_dim.2.place_ref, f32[2,16,128]{2,1,0:T(8,128)S(1)} %get-tuple-element.146.ends_ref.refs_0_, f32[8,128,128]{2,1,0:T(8,128)S(1)} %get-tuple-element.122.refs_1_.keep_ref, ...), custom_call_target="tpu_custom_call" | custom-call | flops 1610612736 | bytes 12582912 | tf_op jit(solution)/shard_map/grad_query/pallas_call | solution.py:557
  51.0 1.6 %collective-permute-start.13 = (f32[4,128,128]{2,1,0:T(8,128)S(1)}, f32[4,128,128]{2,1,0:T(8,128)S(1)}, u32[]{:S(2)}, u32[]{:S(2)}) collective-permute-start(f32[4,128,128]{2,1,0:T(8,128)S(1)} %later_column.1), channel_id=1, source_target_pairs={{0,8},{4,12},{8,0},{12,4},{16,24},{20,28},{24,16},{28,20},{1,9},{5... | collective-permute-start | bytes 786440 | tf_op jit(solution)/shard_map/ppermute | solution.py:709
  52.6 0.8 %collective-permute-start.12 = (f32[4,128,128]{2,1,0:T(8,128)S(1)}, f32[4,128,128]{2,1,0:T(8,128)S(1)}, u32[]{:S(2)}, u32[]{:S(2)}) collective-permute-start(f32[4,128,128]{2,1,0:T(8,128)S(1)} %later_row.1), channel_id=1, source_target_pairs={{0,16},{4,20},{8,24},{12,28},{16,0},{20,4},{24,8},{28,12},{1,17},{... | collective-permute-start | bytes 786440 | tf_op jit(solution)/shard_map/ppermute | solution.py:709
  53.3 5.8 %grad_key_value.1 = (f32[2,16,256,128]{3,2,1,0:T(8,128)S(1)}, f32[2,16,256,128]{3,2,1,0:T(8,128)S(1)}, bf16[512,16,128]{2,1,0:T(8,128)(2,1)}) custom-call(f32[8,128]{1,0:T(8,128)S(1)} %broadcast_in_dim.2.place_ref, f32[16,128]{1,0:T(8,128)S(1)} %get-tuple-element.91.refs_0_.gain_ref, f32[2,512]{1,0:T(2,128)S(1)} %add.16.sums_ref, ...), custom_call_target="tpu_custom_call" | custom-call | flops 1610612736 | bytes 31457280 | tf_op jit(solution)/shard_map/grad_key_value/pallas_call | solution.py:607
  59.8 0.9 %finish_own.1 = (f32[2,16,256,128]{3,2,1,0:T(8,128)S(1)}, f32[2,16,256,128]{3,2,1,0:T(8,128)S(1)}) custom-call(f32[2,16,128]{2,1,0:T(8,128)S(1)} %get-tuple-element.146.ends_ref.refs_0_, f32[8,128,128]{2,1,0:T(8,128)S(1)} %get-tuple-element.168.refs_1_, bf16[2,16,256,128]{3,2,1,0:T(8,128)(2,1)S(1)} %get-tuple-element.94.kh.refs_2_, ...), custom_call_target="tpu_custom_call" | custom-call | flops 536870912 | bytes 8388608 | tf_op jit(solution)/shard_map/finish_own/pallas_call | solution.py:671
  60.7 1.0 %collective-permute-done.14.state_ref = f32[8,128,128]{2,1,0:T(8,128)S(1)} collective-permute-done((f32[8,128,128]{2,1,0:T(8,128)S(1)}, f32[8,128,128]{2,1,0:T(8,128)S(1)}, u32[]{:S(2)}, u32[]{:S(2)}) %collective-permute-start.14) | collective-permute-done | bytes 524320 | tf_op jit(solution)/shard_map/ppermute | solution.py:709
  61.7 3.7 %finish_other.1 = (bf16[512,16,128]{2,1,0:T(8,128)(2,1)}, bf16[512,16,128]{2,1,0:T(8,128)(2,1)}, f32[2,16,256,128]{3,2,1,0:T(8,128)S(1)}, f32[2,16,256,128]{3,2,1,0:T(8,128)S(1)}) custom-call(f32[8,128]{1,0:T(8,128)S(1)} %broadcast_in_dim.2.place_ref, ...), custom_call_target="tpu_custom_call", output_to_operand_aliasing={{2}: (1, {}), {3}: (2, {})} | custom-call | flops 536870912 | bytes 8388608 | tf_op jit(solution)/shard_map/finish_other/pallas_call | solution.py:686
  (26 shorter events, 2.1 us)
Async XLA Ops:
  5.4 2.1 %collective-permute-start = (f32[8,136,128]{2,1,0:T(8,128)S(1)}, f32[8,136,128]{2,1,0:T(8,128)S(1)}, u32[]{:S(2)}, u32[]{:S(2)}) collective-permute-start(f32[8,136,128]{2,1,0:T(8,128)S(1)} %get-tuple-element.93), channel_id=1, source_target_pairs={{0,4},{4,0},{8,12},{12,8},{16,20},{20,16},{24,28},{28,24},{1,5},{5... | collective-permute-start | bytes 1671176 | tf_op jit(solution)/shard_map/ppermute | solution.py:709
  7.7 11.2 %collective-permute-start.1 = (f32[4,136,128]{2,1,0:T(8,128)S(1)}, f32[4,136,128]{2,1,0:T(8,128)S(1)}, u32[]{:S(2)}, u32[]{:S(2)}) collective-permute-start(f32[4,136,128]{2,1,0:T(8,128)S(1)} %get-tuple-element.100.refs_1_), channel_id=1, source_target_pairs={{0,8},{4,12},{8,0},{12,4},{16,24},{20,28},{24,16},{28,20},{1,9},{5... | collective-permute-start | bytes 835592 | tf_op jit(solution)/shard_map/ppermute | solution.py:709
  10.6 8.2 %collective-permute-start.2 = (f32[4,128,128]{2,1,0:T(8,128)S(1)}, f32[4,128,128]{2,1,0:T(8,128)S(1)}, u32[]{:S(2)}, u32[]{:S(2)}) collective-permute-start(f32[4,128,128]{2,1,0:T(8,128)S(1)} %get-tuple-element.101.refs_5_), channel_id=1, source_target_pairs={{0,16},{4,20},{8,24},{12,28},{16,0},{20,4},{24,8},{28,12},{1,17},{... | collective-permute-start | bytes 786440 | tf_op jit(solution)/shard_map/ppermute | solution.py:709
  12.1 6.7 %collective-permute-start.3 = (f32[8,128]{1,0:T(8,128)S(1)}, f32[8,128]{1,0:T(8,128)S(1)}, u32[]{:S(2)}, u32[]{:S(2)}) collective-permute-start(f32[8,128]{1,0:T(8,128)S(1)} %get-tuple-element.99.refs_0_.refs_2_), channel_id=1, source_target_pairs={{0,24},{4,28},{8,16},{12,20},{16,8},{20,12},{24,0},{28,4},{1,25},{... | collective-permute-start | bytes 12296 | tf_op jit(solution)/shard_map/ppermute | solution.py:709
  18.9 7.3 %collective-permute-start.5 = (f32[4,128,128]{2,1,0:T(8,128)S(1)}, f32[4,128,128]{2,1,0:T(8,128)S(1)}, u32[]{:S(2)}, u32[]{:S(2)}) collective-permute-start(f32[4,128,128]{2,1,0:T(8,128)S(1)} %get-tuple-element.114), channel_id=1, source_target_pairs={{0,8},{4,12},{8,0},{12,4},{16,24},{20,28},{24,16},{28,20},{1,9},{5... | collective-permute-start | bytes 786440 | tf_op jit(solution)/shard_map/ppermute | solution.py:709
  20.5 6.9 %collective-permute-start.4 = (f32[4,128,128]{2,1,0:T(8,128)S(1)}, f32[4,128,128]{2,1,0:T(8,128)S(1)}, u32[]{:S(2)}, u32[]{:S(2)}) collective-permute-start(f32[4,128,128]{2,1,0:T(8,128)S(1)} %earlier_row.1), channel_id=1, source_target_pairs={{0,16},{4,20},{8,24},{12,28},{16,0},{20,4},{24,8},{28,12},{1,17},{... | collective-permute-start | bytes 786440 | tf_op jit(solution)/shard_map/ppermute | solution.py:709
  27.6 2.0 %collective-permute-start.6 = (f32[8,128,128]{2,1,0:T(8,128)S(1)}, f32[8,128,128]{2,1,0:T(8,128)S(1)}, u32[]{:S(2)}, u32[]{:S(2)}) collective-permute-start(f32[8,128,128]{2,1,0:T(8,128)S(1)} %get-tuple-element.121), channel_id=1, source_target_pairs={{0,4},{4,0},{8,12},{12,8},{16,20},{20,16},{24,28},{28,24},{1,5},{5... | collective-permute-start | bytes 1572872 | tf_op jit(solution)/shard_map/ppermute | solution.py:709
  31.2 3.6 %collective-permute-start.7 = (f32[2,512]{1,0:T(2,128)S(1)}, f32[2,512]{1,0:T(2,128)S(1)}, u32[]{:S(2)}, u32[]{:S(2)}) collective-permute-start(f32[2,512]{1,0:T(2,128)S(1)} %get-tuple-element.131.first_ref), channel_id=1, source_target_pairs={{0,1},{1,0},{2,3},{3,2},{4,5},{5,4},{6,7},{7,6},{8,9},{9,8},{10,11... | collective-permute-start | bytes 12296 | tf_op jit(solution)/shard_map/ppermute | solution.py:709
  34.9 4.5 %collective-permute-start.8 = (f32[2,512]{1,0:T(2,128)S(1)}, f32[2,512]{1,0:T(2,128)S(1)}, u32[]{:S(2)}, u32[]{:S(2)}) collective-permute-start(f32[2,512]{1,0:T(2,128)S(1)} %add.15.first_ref), channel_id=1, source_target_pairs={{0,2},{1,3},{2,0},{3,1},{4,6},{5,7},{6,4},{7,5},{8,10},{9,11},{10,... | collective-permute-start | bytes 12296 | tf_op jit(solution)/shard_map/ppermute | solution.py:709
  40.2 2.0 %collective-permute-start.9 = (f32[8,128,128]{2,1,0:T(8,128)S(1)}, f32[8,128,128]{2,1,0:T(8,128)S(1)}, u32[]{:S(2)}, u32[]{:S(2)}) collective-permute-start(f32[8,128,128]{2,1,0:T(8,128)S(1)} %get-tuple-element.142), channel_id=1, source_target_pairs={{0,4},{4,0},{8,12},{12,8},{16,20},{20,16},{24,28},{28,24},{1,5},{5... | collective-permute-start | bytes 1572872 | tf_op jit(solution)/shard_map/ppermute | solution.py:709
  42.3 8.4 %collective-permute-start.10 = (f32[4,128,128]{2,1,0:T(8,128)S(1)}, f32[4,128,128]{2,1,0:T(8,128)S(1)}, u32[]{:S(2)}, u32[]{:S(2)}) collective-permute-start(f32[4,128,128]{2,1,0:T(8,128)S(1)} %get-tuple-element.157.refs_1_), channel_id=1, source_target_pairs={{0,8},{4,12},{8,0},{12,4},{16,24},{20,28},{24,16},{28,20},{1,9},{5... | collective-permute-start | bytes 786440 | tf_op jit(solution)/shard_map/ppermute | solution.py:709
  42.9 8.1 %collective-permute-start.11 = (f32[4,128,128]{2,1,0:T(8,128)S(1)}, f32[4,128,128]{2,1,0:T(8,128)S(1)}, u32[]{:S(2)}, u32[]{:S(2)}) collective-permute-start(f32[4,128,128]{2,1,0:T(8,128)S(1)} %get-tuple-element.145.refs_1_), channel_id=1, source_target_pairs={{0,16},{4,20},{8,24},{12,28},{16,0},{20,4},{24,8},{28,12},{1,17},{... | collective-permute-start | bytes 786440 | tf_op jit(solution)/shard_map/ppermute | solution.py:709
  51.0 8.1 %collective-permute-start.13 = (f32[4,128,128]{2,1,0:T(8,128)S(1)}, f32[4,128,128]{2,1,0:T(8,128)S(1)}, u32[]{:S(2)}, u32[]{:S(2)}) collective-permute-start(f32[4,128,128]{2,1,0:T(8,128)S(1)} %later_column.1), channel_id=1, source_target_pairs={{0,8},{4,12},{8,0},{12,4},{16,24},{20,28},{24,16},{28,20},{1,9},{5... | collective-permute-start | bytes 786440 | tf_op jit(solution)/shard_map/ppermute | solution.py:709
  52.6 6.9 %collective-permute-start.12 = (f32[4,128,128]{2,1,0:T(8,128)S(1)}, f32[4,128,128]{2,1,0:T(8,128)S(1)}, u32[]{:S(2)}, u32[]{:S(2)}) collective-permute-start(f32[4,128,128]{2,1,0:T(8,128)S(1)} %later_row.1), channel_id=1, source_target_pairs={{0,16},{4,20},{8,24},{12,28},{16,0},{20,4},{24,8},{28,12},{1,17},{... | collective-permute-start | bytes 786440 | tf_op jit(solution)/shard_map/ppermute | solution.py:709
  59.7 2.0 %collective-permute-start.14 = (f32[8,128,128]{2,1,0:T(8,128)S(1)}, f32[8,128,128]{2,1,0:T(8,128)S(1)}, u32[]{:S(2)}, u32[]{:S(2)}) collective-permute-start(f32[8,128,128]{2,1,0:T(8,128)S(1)} %get-tuple-element.172), channel_id=1, source_target_pairs={{0,4},{4,0},{8,12},{12,8},{16,20},{20,16},{24,28},{28,24},{1,5},{5... | collective-permute-start | bytes 1572872 | tf_op jit(solution)/shard_map/ppermute | solution.py:709

commit v16 on v15

--- a/solution.py
+++ b/solution.py
@@ -392,14 +392,13 @@
 
     each_head(half, 8, one)
     if part:
-        ones = jnp.ones((8, HD), F32)
-        for b in range(2):
-            for at in range(2):
-                line = lax.dot_general(
-                    ones, partial[at, b], (((1,), (1,)), ((), ())),
-                    precision=lax.Precision.HIGHEST, preferred_element_type=F32,
-                )
-                sums_ref[at : at + 1, b * BLOCK : (b + 1) * BLOCK] = line[:1]
+        totals = partial[...].reshape(4 * BLOCK, HD)
+        high, rest = two_parts(totals)
+        low = (totals - high.astype(F32) - rest.astype(F32)).astype(BF16)
+        parts = jnp.concatenate([high, rest, low], axis=1)
+        line = dot_rows(jnp.ones((2 * TILE, 3 * HD), BF16), parts)
+        for at in range(2):
+            sums_ref[at : at + 1] = line[:1, at * 2 * BLOCK : (at + 1) * 2 * BLOCK]
 
 
 def attend(part, gain, state, arrays, before=()):

time: 65.6 us -> 65.4 us (level)
  no operation moved by 1% of the time
where the time goes in v16:
time: 65.4 us; the launch traced here: 65.2 us
  Pallas kernels  37.8 us (58%)
  starting transfers between devices  15.7 us (24%)
  waiting for transfers between devices  10.5 us (16%)
  between operations  0.99 us (2%)
    ppermute x15, starting transfers between devices, swap(): return lax.ppermute(value, axis, [(i, i ^ bit) for i in range(count)])  15.7 us
    ppermute x15, waiting for transfers between devices, swap(): return lax.ppermute(value, axis, [(i, i ^ bit) for i in range(count)])  10.5 us
    pallas_call x2, Pallas kernels, intra(): pl.pallas_call(kernel, in_specs=[NEAR] * 8 + [FAR, FAR] * ahead, out_spec...  7.62 us
    pallas_call x1, Pallas kernels, grad_query(): pl.pallas_call(grad_q_kernel, in_specs=[NEAR] * 16, out_specs=[NEAR, FAR]...  6.25 us
    pallas_call x1, Pallas kernels, grad_key_value(): pl.pallas_call(grad_kv_kernel, in_specs=[NEAR] * 21, out_specs=[NEAR, NEA...  5.77 us
    pallas_call x1, Pallas kernels, state_to_send(): pl.pallas_call(state_kernel, in_specs=[NEAR, FAR, FAR, FAR, FAR], out_spe...  4.61 us
    pallas_call x1, Pallas kernels, finish_other(): pl.pallas_call(finish_other_kernel, in_specs=[NEAR] * 10, out_specs=[FAR,...  3.67 us
    pallas_call x2, Pallas kernels, attend(): pl.pallas_call(functools.partial(attend_kernel, part), in_specs=[NEAR] *...  2.39 us
  transfers between devices with their start and end apart: 15, of which 11 were waited for; matrix products, arithmetic and copies ran while one was open for 0% of the time, Pallas kernels for 41%

profile of v16, /device:TPU:0, one launch (start us, length us, event | category | flops | bytes accessed | tf_op | source)
XLA Modules:
  0.0 65.2 jit_solution(6947522015187194235)
XLA Ops:
  0.8 4.6 %state_to_send.1 = (f32[8,136,128]{2,1,0:T(8,128)S(1)}, f32[8,128,128]{2,1,0:T(8,128)S(1)}, bf16[2,16,256,128]{3,2,1,0:T(8,128)(2,1)S(1)}, bf16[2,16,256,128]{3,...) custom-call(f32[8,128]{1,0:T(8,128)S(1)} %broadcast_in_dim.2.place_r, ...), custom_call_target="tpu_custom_call" | custom-call | flops 134217728 | bytes 8388608 | tf_op jit(solution)/shard_map/state_to_send/pallas_call | solution.py:255
  5.4 0.5 collective-permute-start
  6.0 1.6 %own_state.1 = (f32[8,136,128]{2,1,0:T(8,128)S(1)}, f32[8,128,128]{2,1,0:T(8,128)S(1)}, bf16[256,16,128]{2,1,0:T(8,128)(2,1)S(1)}, bf16[256,16,128]{2,1,0:T(8,128)(2,1)S(1)}) custom-call(bf16[2,16,256,128]{3,2,1,0:T(8,128)(2,1)S(1)} %get-tuple-element.94.kh.refs_2_, bf16[2,16,256,128]{3,2,1,0:T(8,128)(2,1)S(1)} %get-tuple-element.95.vh.refs_3_, ...), custom_call_target="tpu_custom_call" | custom-call | flops 134217728 | bytes 2097152 | tf_op jit(solution)/shard_map/own_state/pallas_call | solution.py:301
  7.7 2.9 %collective-permute-start.1 = (f32[4,136,128]{2,1,0:T(8,128)S(1)}, f32[4,136,128]{2,1,0:T(8,128)S(1)}, u32[]{:S(2)}, u32[]{:S(2)}) collective-permute-start(f32[4,136,128]{2,1,0:T(8,128)S(1)} %get-tuple-element.100.refs_1_), channel_id=1, source_target_pairs={{0,8},{4,12},{8,0},{12,4},{16,24},{20,28},{24,16},{28,20},{1,9},{5... | collective-permute-start | bytes 835592 | tf_op jit(solution)/shard_map/ppermute | solution.py:708
  10.6 1.5 %collective-permute-start.2 = (f32[4,128,128]{2,1,0:T(8,128)S(1)}, f32[4,128,128]{2,1,0:T(8,128)S(1)}, u32[]{:S(2)}, u32[]{:S(2)}) collective-permute-start(f32[4,128,128]{2,1,0:T(8,128)S(1)} %get-tuple-element.101.refs_5_), channel_id=1, source_target_pairs={{0,16},{4,20},{8,24},{12,28},{16,0},{20,4},{24,8},{28,12},{1,17},{... | collective-permute-start | bytes 786440 | tf_op jit(solution)/shard_map/ppermute | solution.py:708
  12.1 3.8 %intra_0.1 = (bf16[16,256,128]{2,1,0:T(8,128)(2,1)S(1)}, bf16[16,256,128]{2,1,0:T(8,128)(2,1)S(1)}, bf16[16,256,256]{2,1,0:T(8,128)(2,1)S(1)}, f32[16,3,128,128]...) custom-call(f32[8,128]{1,0:T(8,128)S(1)} %broadcast_in_dim.2.place_r, ...), custom_call_target="tpu_custom_call" | custom-call | flops 1073741824 | bytes 10485760 | tf_op jit(solution)/shard_map/intra_0/pallas_call | solution.py:349
  15.9 2.9 %collective-permute-done.3.refs_3_ = f32[8,128]{1,0:T(8,128)S(1)} collective-permute-done((f32[8,128]{1,0:T(8,128)S(1)}, f32[8,128]{1,0:T(8,128)S(1)}, u32[]{:S(2)}, u32[]{:S(2)}) %collective-permute-start.3) | collective-permute-done | bytes 4128 | tf_op jit(solution)/shard_map/ppermute | solution.py:708
  18.9 1.6 %collective-permute-start.5 = (f32[4,128,128]{2,1,0:T(8,128)S(1)}, f32[4,128,128]{2,1,0:T(8,128)S(1)}, u32[]{:S(2)}, u32[]{:S(2)}) collective-permute-start(f32[4,128,128]{2,1,0:T(8,128)S(1)} %get-tuple-element.114), channel_id=1, source_target_pairs={{0,8},{4,12},{8,0},{12,4},{16,24},{20,28},{24,16},{28,20},{1,9},{5... | collective-permute-start | bytes 786440 | tf_op jit(solution)/shard_map/ppermute | solution.py:708
  20.5 0.5 collective-permute-start.4
  21.0 3.9 %intra_1.1 = (bf16[16,256,128]{2,1,0:T(8,128)(2,1)S(1)}, bf16[16,256,128]{2,1,0:T(8,128)(2,1)S(1)}, bf16[16,256,256]{2,1,0:T(8,128)(2,1)S(1)}, f32[16,3,128,128]...) custom-call(f32[8,128]{1,0:T(8,128)S(1)} %broadcast_in_dim.2.place_ref, ...), custom_call_target="tpu_custom_call" | custom-call | flops 1073741824 | bytes 10485760 | tf_op jit(solution)/shard_map/intra_1/pallas_call | solution.py:349
  24.9 1.4 %collective-permute-done.5.refs_6_ = f32[4,128,128]{2,1,0:T(8,128)S(1)} collective-permute-done((f32[4,128,128]{2,1,0:T(8,128)S(1)}, f32[4,128,128]{2,1,0:T(8,128)S(1)}, u32[]{:S(2)}, u32[]{:S(2)}) %collective-permute-start.5) | collective-permute-done | bytes 262176 | tf_op jit(solution)/shard_map/ppermute | solution.py:708
  26.2 1.2 %collective-permute-done.4.refs_5_ = f32[4,128,128]{2,1,0:T(8,128)S(1)} collective-permute-done((f32[4,128,128]{2,1,0:T(8,128)S(1)}, f32[4,128,128]{2,1,0:T(8,128)S(1)}, u32[]{:S(2)}, u32[]{:S(2)}) %collective-permute-start.4) | collective-permute-done | bytes 262176 | tf_op jit(solution)/shard_map/ppermute | solution.py:708
  27.7 1.0 %attend_0.1 = (f32[8,256,128]{2,1,0:T(8,128)S(1)}, f32[8,256,128]{2,1,0:T(8,128)S(1)}, f32[2,2,256,128]{3,2,1,0:T(8,128)S(1)}) custom-call(f32[16,128]{1,0:T(8,128)S(1)} %get-tuple-element.91.refs_0_.gain_ref, f32[8,128,128]{2,1,0:T(8,128)S(1)} %get-tuple-element.122.refs_1_.keep_ref, bf16[16,256,128]{2,1,0:T(8,128)(2,1)S(1)} %get-tuple-element.132.refs_2_.q0, ...), custom_call_target="tpu_custom_call" | custom-call | flops 268435456 | bytes 8388608 | tf_op jit(solution)/shard_map/attend_0/pallas_call | solution.py:410
  28.7 0.9 %collective-permute-done.6.refs_1_.recv_ref = f32[8,128,128]{2,1,0:T(8,128)S(1)} collective-permute-done((f32[8,128,128]{2,1,0:T(8,128)S(1)}, f32[8,128,128]{2,1,0:T(8,128)S(1)}, u32[]{:S(2)}, u32[]{:S(2)}) %collective-permute-start.6) | collective-permute-done | bytes 524320 | tf_op jit(solution)/shard_map/ppermute | solution.py:708
  29.6 1.4 %attend_1.1 = (f32[8,256,128]{2,1,0:T(8,128)S(1)}, f32[8,256,128]{2,1,0:T(8,128)S(1)}, f32[2,512]{1,0:T(2,128)S(1)}) custom-call(f32[16,128]{1,0:T(8,128)S(1)} %get-tuple-element.91.refs_0_.gain_ref, f32[8,128,128]{2,1,0:T(8,128)S(1)} %collective-permute-done.6.refs_1_.recv_ref, bf16[16,256,128]{2,1,0:T(8,128)(2,1)S(1)} %get-tuple-element.132.refs_2_.q0, ...), custom_call_target="tpu_custom_call" | custom-call | flops 268435456 | bytes 8388608 | tf_op jit(solution)/shard_map/attend_1/pallas_call | solution.py:410
  31.0 1.6 %collective-permute-start.7 = (f32[2,512]{1,0:T(2,128)S(1)}, f32[2,512]{1,0:T(2,128)S(1)}, u32[]{:S(2)}, u32[]{:S(2)}) collective-permute-start(f32[2,512]{1,0:T(2,128)S(1)} %get-tuple-element.131.first_ref), channel_id=1, source_target_pairs={{0,1},{1,0},{2,3},{3,2},{4,5},{5,4},{6,7},{7,6},{8,9},{9,8},{10,11... | collective-permute-start | bytes 12296 | tf_op jit(solution)/shard_map/ppermute | solution.py:708
  32.6 0.9 %scaled_queries.1 = (bf16[2,16,128,256]{3,2,1,0:T(8,128)(2,1)S(1)}, f32[2,16,128]{2,1,0:T(8,128)S(1)}) custom-call(f32[2,16,256]{2,1,0:T(8,128)S(1)} %get-tuple-element.136.cum.cum_ref, bf16[16,256,128]{2,1,0:T(8,128)(2,1)S(1)} %get-tuple-element.132.refs_2_.q0, bf16[16,256,128]{2,1,0:T(8,128)(2,1)S(1)} %get-tuple-element.118.refs_3_.q1), custom_call_target="tpu_custom_call" | custom-call | flops 2097152 | bytes 4194304 | tf_op jit(solution)/shard_map/scaled_queries/pallas_call | solution.py:436
  33.5 1.1 %collective-permute-done.7.second_ref = f32[2,512]{1,0:T(2,128)S(1)} collective-permute-done((f32[2,512]{1,0:T(2,128)S(1)}, f32[2,512]{1,0:T(2,128)S(1)}, u32[]{:S(2)}, u32[]{:S(2)}) %collective-permute-start.7) | collective-permute-done | bytes 4128 | tf_op jit(solution)/shard_map/ppermute | solution.py:708
  34.6 2.6 %collective-permute-start.8 = (f32[2,512]{1,0:T(2,128)S(1)}, f32[2,512]{1,0:T(2,128)S(1)}, u32[]{:S(2)}, u32[]{:S(2)}) collective-permute-start(f32[2,512]{1,0:T(2,128)S(1)} %add.15.first_ref), channel_id=1, source_target_pairs={{0,2},{1,3},{2,0},{3,1},{4,6},{5,7},{6,4},{7,5},{8,10},{9,11},{10,... | collective-permute-start | bytes 12296 | tf_op jit(solution)/shard_map/ppermute | solution.py:708
  37.2 1.8 %remaining_decay.1.remaining_ref.refs_4_ = f32[2,16,256,128]{3,2,1,0:T(8,128)S(1)} custom-call(f32[2,16,256]{2,1,0:T(8,128)S(1)} %get-tuple-element.136.cum.cum_ref), custom_call_target="tpu_custom_call" | custom-call | flops 1048576 | bytes 4194304 | tf_op jit(solution)/shard_map/remaining_decay/pallas_call | solution.py:458
  39.1 0.8 %norm_grad_1.1 = (f32[8,128,128]{2,1,0:T(8,128)S(1)}, f32[8,128,128]{2,1,0:T(8,128)S(1)}, bf16[8,256,128]{2,1,0:T(8,128)(2,1)S(1)}, bf16[8,256,128]{2,1,0:T(8,128)(2,1)S(1)}) custom-call(f32[2,16,128]{2,1,0:T(8,128)S(1)} %get-tuple-element.146.ends_ref.refs_0_, f32[16,128]{1,0:T(8,128)S(1)} %get-tuple-element.91.refs_0_.gain_ref, ...), custom_call_target="tpu_custom_call" | custom-call | flops 134217728 | bytes 7340032 | tf_op jit(solution)/shard_map/norm_grad_1/pallas_call | solution.py:503
  40.0 0.8 %norm_grad_0.1 = (f32[8,128,128]{2,1,0:T(8,128)S(1)}, f32[8,128,128]{2,1,0:T(8,128)S(1)}, bf16[8,256,128]{2,1,0:T(8,128)(2,1)S(1)}, bf16[8,256,128]{2,1,0:T(8,128)(2,1)S(1)}) custom-call(f32[2,16,128]{2,1,0:T(8,128)S(1)} %get-tuple-element.146.ends_ref.refs_0_, f32[16,128]{1,0:T(8,128)S(1)} %get-tuple-element.91.refs_0_.gain_ref, ...), custom_call_target="tpu_custom_call" | custom-call | flops 134217728 | bytes 7340032 | tf_op jit(solution)/shard_map/norm_grad_0/pallas_call | solution.py:503
  40.8 1.1 %collective-permute-done.9.refs_2_ = f32[8,128,128]{2,1,0:T(8,128)S(1)} collective-permute-done((f32[8,128,128]{2,1,0:T(8,128)S(1)}, f32[8,128,128]{2,1,0:T(8,128)S(1)}, u32[]{:S(2)}, u32[]{:S(2)}) %collective-permute-start.9) | collective-permute-done | bytes 524320 | tf_op jit(solution)/shard_map/ppermute | solution.py:708
  42.0 0.6 collective-permute-start.10
  42.6 1.4 %collective-permute-start.11 = (f32[4,128,128]{2,1,0:T(8,128)S(1)}, f32[4,128,128]{2,1,0:T(8,128)S(1)}, u32[]{:S(2)}, u32[]{:S(2)}) collective-permute-start(f32[4,128,128]{2,1,0:T(8,128)S(1)} %get-tuple-element.145.refs_1_), channel_id=1, source_target_pairs={{0,16},{4,20},{8,24},{12,28},{16,0},{20,4},{24,8},{28,12},{1,17},{... | collective-permute-start | bytes 786440 | tf_op jit(solution)/shard_map/ppermute | solution.py:708
  44.0 6.2 %grad_query.1 = (bf16[2,16,256,256]{3,2,1,0:T(8,128)(2,1)S(1)}, bf16[512,16,128]{2,1,0:T(8,128)(2,1)}) custom-call(f32[8,128]{1,0:T(8,128)S(1)} %broadcast_in_dim.2.place_ref, f32[2,16,128]{2,1,0:T(8,128)S(1)} %get-tuple-element.146.ends_ref.refs_0_, f32[8,128,128]{2,1,0:T(8,128)S(1)} %get-tuple-element.122.refs_1_.keep_ref, ...), custom_call_target="tpu_custom_call" | custom-call | flops 1610612736 | bytes 12582912 | tf_op jit(solution)/shard_map/grad_query/pallas_call | solution.py:556
  50.7 1.6 %collective-permute-start.13 = (f32[4,128,128]{2,1,0:T(8,128)S(1)}, f32[4,128,128]{2,1,0:T(8,128)S(1)}, u32[]{:S(2)}, u32[]{:S(2)}) collective-permute-start(f32[4,128,128]{2,1,0:T(8,128)S(1)} %later_column.1), channel_id=1, source_target_pairs={{0,8},{4,12},{8,0},{12,4},{16,24},{20,28},{24,16},{28,20},{1,9},{5... | collective-permute-start | bytes 786440 | tf_op jit(solution)/shard_map/ppermute | solution.py:708
  52.3 0.8 %collective-permute-start.12 = (f32[4,128,128]{2,1,0:T(8,128)S(1)}, f32[4,128,128]{2,1,0:T(8,128)S(1)}, u32[]{:S(2)}, u32[]{:S(2)}) collective-permute-start(f32[4,128,128]{2,1,0:T(8,128)S(1)} %later_row.1), channel_id=1, source_target_pairs={{0,16},{4,20},{8,24},{12,28},{16,0},{20,4},{24,8},{28,12},{1,17},{... | collective-permute-start | bytes 786440 | tf_op jit(solution)/shard_map/ppermute | solution.py:708
  53.1 5.8 %grad_key_value.1 = (f32[2,16,256,128]{3,2,1,0:T(8,128)S(1)}, f32[2,16,256,128]{3,2,1,0:T(8,128)S(1)}, bf16[512,16,128]{2,1,0:T(8,128)(2,1)}) custom-call(f32[8,128]{1,0:T(8,128)S(1)} %broadcast_in_dim.2.place_ref, f32[16,128]{1,0:T(8,128)S(1)} %get-tuple-element.91.refs_0_.gain_ref, f32[2,512]{1,0:T(2,128)S(1)} %add.16.sums_ref, ...), custom_call_target="tpu_custom_call" | custom-call | flops 1610612736 | bytes 31457280 | tf_op jit(solution)/shard_map/grad_key_value/pallas_call | solution.py:606
  59.5 0.9 %finish_own.1 = (f32[2,16,256,128]{3,2,1,0:T(8,128)S(1)}, f32[2,16,256,128]{3,2,1,0:T(8,128)S(1)}) custom-call(f32[2,16,128]{2,1,0:T(8,128)S(1)} %get-tuple-element.146.ends_ref.refs_0_, f32[8,128,128]{2,1,0:T(8,128)S(1)} %get-tuple-element.168.refs_1_, bf16[2,16,256,128]{3,2,1,0:T(8,128)(2,1)S(1)} %get-tuple-element.94.kh.refs_2_, ...), custom_call_target="tpu_custom_call" | custom-call | flops 536870912 | bytes 8388608 | tf_op jit(solution)/shard_map/finish_own/pallas_call | solution.py:670
  60.4 1.0 %collective-permute-done.14.state_ref = f32[8,128,128]{2,1,0:T(8,128)S(1)} collective-permute-done((f32[8,128,128]{2,1,0:T(8,128)S(1)}, f32[8,128,128]{2,1,0:T(8,128)S(1)}, u32[]{:S(2)}, u32[]{:S(2)}) %collective-permute-start.14) | collective-permute-done | bytes 524320 | tf_op jit(solution)/shard_map/ppermute | solution.py:708
  61.4 3.7 %finish_other.1 = (bf16[512,16,128]{2,1,0:T(8,128)(2,1)}, bf16[512,16,128]{2,1,0:T(8,128)(2,1)}, f32[2,16,256,128]{3,2,1,0:T(8,128)S(1)}, f32[2,16,256,128]{3,2,1,0:T(8,128)S(1)}) custom-call(f32[8,128]{1,0:T(8,128)S(1)} %broadcast_in_dim.2.place_ref, ...), custom_call_target="tpu_custom_call", output_to_operand_aliasing={{2}: (1, {}), {3}: (2, {})} | custom-call | flops 536870912 | bytes 8388608 | tf_op jit(solution)/shard_map/finish_other/pallas_call | solution.py:685
  (26 shorter events, 2.1 us)
Async XLA Ops:
  5.4 2.1 %collective-permute-start = (f32[8,136,128]{2,1,0:T(8,128)S(1)}, f32[8,136,128]{2,1,0:T(8,128)S(1)}, u32[]{:S(2)}, u32[]{:S(2)}) collective-permute-start(f32[8,136,128]{2,1,0:T(8,128)S(1)} %get-tuple-element.93), channel_id=1, source_target_pairs={{0,4},{4,0},{8,12},{12,8},{16,20},{20,16},{24,28},{28,24},{1,5},{5... | collective-permute-start | bytes 1671176 | tf_op jit(solution)/shard_map/ppermute | solution.py:708
  7.7 11.2 %collective-permute-start.1 = (f32[4,136,128]{2,1,0:T(8,128)S(1)}, f32[4,136,128]{2,1,0:T(8,128)S(1)}, u32[]{:S(2)}, u32[]{:S(2)}) collective-permute-start(f32[4,136,128]{2,1,0:T(8,128)S(1)} %get-tuple-element.100.refs_1_), channel_id=1, source_target_pairs={{0,8},{4,12},{8,0},{12,4},{16,24},{20,28},{24,16},{28,20},{1,9},{5... | collective-permute-start | bytes 835592 | tf_op jit(solution)/shard_map/ppermute | solution.py:708
  10.6 8.2 %collective-permute-start.2 = (f32[4,128,128]{2,1,0:T(8,128)S(1)}, f32[4,128,128]{2,1,0:T(8,128)S(1)}, u32[]{:S(2)}, u32[]{:S(2)}) collective-permute-start(f32[4,128,128]{2,1,0:T(8,128)S(1)} %get-tuple-element.101.refs_5_), channel_id=1, source_target_pairs={{0,16},{4,20},{8,24},{12,28},{16,0},{20,4},{24,8},{28,12},{1,17},{... | collective-permute-start | bytes 786440 | tf_op jit(solution)/shard_map/ppermute | solution.py:708
  12.1 6.7 %collective-permute-start.3 = (f32[8,128]{1,0:T(8,128)S(1)}, f32[8,128]{1,0:T(8,128)S(1)}, u32[]{:S(2)}, u32[]{:S(2)}) collective-permute-start(f32[8,128]{1,0:T(8,128)S(1)} %get-tuple-element.99.refs_0_.refs_2_), channel_id=1, source_target_pairs={{0,24},{4,28},{8,16},{12,20},{16,8},{20,12},{24,0},{28,4},{1,25},{... | collective-permute-start | bytes 12296 | tf_op jit(solution)/shard_map/ppermute | solution.py:708
  18.9 7.3 %collective-permute-start.5 = (f32[4,128,128]{2,1,0:T(8,128)S(1)}, f32[4,128,128]{2,1,0:T(8,128)S(1)}, u32[]{:S(2)}, u32[]{:S(2)}) collective-permute-start(f32[4,128,128]{2,1,0:T(8,128)S(1)} %get-tuple-element.114), channel_id=1, source_target_pairs={{0,8},{4,12},{8,0},{12,4},{16,24},{20,28},{24,16},{28,20},{1,9},{5... | collective-permute-start | bytes 786440 | tf_op jit(solution)/shard_map/ppermute | solution.py:708
  20.5 6.9 %collective-permute-start.4 = (f32[4,128,128]{2,1,0:T(8,128)S(1)}, f32[4,128,128]{2,1,0:T(8,128)S(1)}, u32[]{:S(2)}, u32[]{:S(2)}) collective-permute-start(f32[4,128,128]{2,1,0:T(8,128)S(1)} %earlier_row.1), channel_id=1, source_target_pairs={{0,16},{4,20},{8,24},{12,28},{16,0},{20,4},{24,8},{28,12},{1,17},{... | collective-permute-start | bytes 786440 | tf_op jit(solution)/shard_map/ppermute | solution.py:708
  27.6 2.0 %collective-permute-start.6 = (f32[8,128,128]{2,1,0:T(8,128)S(1)}, f32[8,128,128]{2,1,0:T(8,128)S(1)}, u32[]{:S(2)}, u32[]{:S(2)}) collective-permute-start(f32[8,128,128]{2,1,0:T(8,128)S(1)} %get-tuple-element.121), channel_id=1, source_target_pairs={{0,4},{4,0},{8,12},{12,8},{16,20},{20,16},{24,28},{28,24},{1,5},{5... | collective-permute-start | bytes 1572872 | tf_op jit(solution)/shard_map/ppermute | solution.py:708
  31.0 3.6 %collective-permute-start.7 = (f32[2,512]{1,0:T(2,128)S(1)}, f32[2,512]{1,0:T(2,128)S(1)}, u32[]{:S(2)}, u32[]{:S(2)}) collective-permute-start(f32[2,512]{1,0:T(2,128)S(1)} %get-tuple-element.131.first_ref), channel_id=1, source_target_pairs={{0,1},{1,0},{2,3},{3,2},{4,5},{5,4},{6,7},{7,6},{8,9},{9,8},{10,11... | collective-permute-start | bytes 12296 | tf_op jit(solution)/shard_map/ppermute | solution.py:708
  34.6 4.5 %collective-permute-start.8 = (f32[2,512]{1,0:T(2,128)S(1)}, f32[2,512]{1,0:T(2,128)S(1)}, u32[]{:S(2)}, u32[]{:S(2)}) collective-permute-start(f32[2,512]{1,0:T(2,128)S(1)} %add.15.first_ref), channel_id=1, source_target_pairs={{0,2},{1,3},{2,0},{3,1},{4,6},{5,7},{6,4},{7,5},{8,10},{9,11},{10,... | collective-permute-start | bytes 12296 | tf_op jit(solution)/shard_map/ppermute | solution.py:708
  39.9 2.0 %collective-permute-start.9 = (f32[8,128,128]{2,1,0:T(8,128)S(1)}, f32[8,128,128]{2,1,0:T(8,128)S(1)}, u32[]{:S(2)}, u32[]{:S(2)}) collective-permute-start(f32[8,128,128]{2,1,0:T(8,128)S(1)} %get-tuple-element.142), channel_id=1, source_target_pairs={{0,4},{4,0},{8,12},{12,8},{16,20},{20,16},{24,28},{28,24},{1,5},{5... | collective-permute-start | bytes 1572872 | tf_op jit(solution)/shard_map/ppermute | solution.py:708
  42.0 8.4 %collective-permute-start.10 = (f32[4,128,128]{2,1,0:T(8,128)S(1)}, f32[4,128,128]{2,1,0:T(8,128)S(1)}, u32[]{:S(2)}, u32[]{:S(2)}) collective-permute-start(f32[4,128,128]{2,1,0:T(8,128)S(1)} %get-tuple-element.157.refs_1_), channel_id=1, source_target_pairs={{0,8},{4,12},{8,0},{12,4},{16,24},{20,28},{24,16},{28,20},{1,9},{5... | collective-permute-start | bytes 786440 | tf_op jit(solution)/shard_map/ppermute | solution.py:708
  42.6 8.1 %collective-permute-start.11 = (f32[4,128,128]{2,1,0:T(8,128)S(1)}, f32[4,128,128]{2,1,0:T(8,128)S(1)}, u32[]{:S(2)}, u32[]{:S(2)}) collective-permute-start(f32[4,128,128]{2,1,0:T(8,128)S(1)} %get-tuple-element.145.refs_1_), channel_id=1, source_target_pairs={{0,16},{4,20},{8,24},{12,28},{16,0},{20,4},{24,8},{28,12},{1,17},{... | collective-permute-start | bytes 786440 | tf_op jit(solution)/shard_map/ppermute | solution.py:708
  50.7 8.1 %collective-permute-start.13 = (f32[4,128,128]{2,1,0:T(8,128)S(1)}, f32[4,128,128]{2,1,0:T(8,128)S(1)}, u32[]{:S(2)}, u32[]{:S(2)}) collective-permute-start(f32[4,128,128]{2,1,0:T(8,128)S(1)} %later_column.1), channel_id=1, source_target_pairs={{0,8},{4,12},{8,0},{12,4},{16,24},{20,28},{24,16},{28,20},{1,9},{5... | collective-permute-start | bytes 786440 | tf_op jit(solution)/shard_map/ppermute | solution.py:708
  52.3 6.9 %collective-permute-start.12 = (f32[4,128,128]{2,1,0:T(8,128)S(1)}, f32[4,128,128]{2,1,0:T(8,128)S(1)}, u32[]{:S(2)}, u32[]{:S(2)}) collective-permute-start(f32[4,128,128]{2,1,0:T(8,128)S(1)} %later_row.1), channel_id=1, source_target_pairs={{0,16},{4,20},{8,24},{12,28},{16,0},{20,4},{24,8},{28,12},{1,17},{... | collective-permute-start | bytes 786440 | tf_op jit(solution)/shard_map/ppermute | solution.py:708
  59.4 2.0 %collective-permute-start.14 = (f32[8,128,128]{2,1,0:T(8,128)S(1)}, f32[8,128,128]{2,1,0:T(8,128)S(1)}, u32[]{:S(2)}, u32[]{:S(2)}) collective-permute-start(f32[8,128,128]{2,1,0:T(8,128)S(1)} %get-tuple-element.172), channel_id=1, source_target_pairs={{0,4},{4,0},{8,12},{12,8},{16,20},{20,16},{24,28},{28,24},{1,5},{5... | collective-permute-start | bytes 1572872 | tf_op jit(solution)/shard_map/ppermute | solution.py:708

commit v17 on v16

--- a/solution.py
+++ b/solution.py
@@ -45,12 +45,10 @@
     upper = lax.broadcasted_iota(jnp.int32, (size, size), 0) <= lax.broadcasted_iota(
         jnp.int32, (size, size), 1
     )
-    return jnp.dot(
-        log_decay,
-        jnp.where(upper, 1.0, 0.0).astype(F32),
-        precision=lax.Precision.HIGHEST,
-        preferred_element_type=F32,
-    )
+    high, rest = two_parts(log_decay)
+    low = (log_decay - high.astype(F32) - rest.astype(F32)).astype(BF16)
+    ones = jnp.where(upper, 1.0, 0.0).astype(BF16)
+    return dot(jnp.concatenate([high, rest, low], axis=1), jnp.concatenate([ones] * 3, axis=0))
 
 
 def as_columns(row):

time: 65.4 us -> 65.3 us (level)
  no operation moved by 1% of the time
where the time goes in v17:
time: 65.3 us; the launch traced here: 65.1 us
  Pallas kernels  37.7 us (58%)
  starting transfers between devices  15.7 us (24%)
  waiting for transfers between devices  10.5 us (16%)
  between operations  0.99 us (2%)
    ppermute x15, starting transfers between devices, swap(): return lax.ppermute(value, axis, [(i, i ^ bit) for i in range(count)])  15.7 us
    ppermute x15, waiting for transfers between devices, swap(): return lax.ppermute(value, axis, [(i, i ^ bit) for i in range(count)])  10.5 us
    pallas_call x2, Pallas kernels, intra(): pl.pallas_call(kernel, in_specs=[NEAR] * 8 + [FAR, FAR] * ahead, out_spec...  7.61 us
    pallas_call x1, Pallas kernels, grad_query(): pl.pallas_call(grad_q_kernel, in_specs=[NEAR] * 16, out_specs=[NEAR, FAR]...  6.25 us
    pallas_call x1, Pallas kernels, grad_key_value(): pl.pallas_call(grad_kv_kernel, in_specs=[NEAR] * 21, out_specs=[NEAR, NEA...  5.77 us
    pallas_call x1, Pallas kernels, state_to_send(): pl.pallas_call(state_kernel, in_specs=[NEAR, FAR, FAR, FAR, FAR], out_spe...  4.5 us
    pallas_call x1, Pallas kernels, finish_other(): pl.pallas_call(finish_other_kernel, in_specs=[NEAR] * 10, out_specs=[FAR,...  3.67 us
    pallas_call x2, Pallas kernels, attend(): pl.pallas_call(functools.partial(attend_kernel, part), in_specs=[NEAR] *...  2.39 us
  transfers between devices with their start and end apart: 15, of which 11 were waited for; matrix products, arithmetic and copies ran while one was open for 0% of the time, Pallas kernels for 41%

profile of v17, /device:TPU:0, one launch (start us, length us, event | category | flops | bytes accessed | tf_op | source)
XLA Modules:
  0.0 65.1 jit_solution(14393259145807931287)
XLA Ops:
  0.8 4.5 %state_to_send.1 = (f32[8,136,128]{2,1,0:T(8,128)S(1)}, f32[8,128,128]{2,1,0:T(8,128)S(1)}, bf16[2,16,256,128]{3,2,1,0:T(8,128)(2,1)S(1)}, bf16[2,16,256,128]{3,...) custom-call(f32[8,128]{1,0:T(8,128)S(1)} %broadcast_in_dim.2.place_r, ...), custom_call_target="tpu_custom_call" | custom-call | flops 134217728 | bytes 8388608 | tf_op jit(solution)/shard_map/state_to_send/pallas_call | solution.py:253
  5.3 0.5 collective-permute-start
  5.9 1.6 %own_state.1 = (f32[8,136,128]{2,1,0:T(8,128)S(1)}, f32[8,128,128]{2,1,0:T(8,128)S(1)}, bf16[256,16,128]{2,1,0:T(8,128)(2,1)S(1)}, bf16[256,16,128]{2,1,0:T(8,128)(2,1)S(1)}) custom-call(bf16[2,16,256,128]{3,2,1,0:T(8,128)(2,1)S(1)} %get-tuple-element.94.kh.refs_2_, bf16[2,16,256,128]{3,2,1,0:T(8,128)(2,1)S(1)} %get-tuple-element.95.vh.refs_3_, ...), custom_call_target="tpu_custom_call" | custom-call | flops 134217728 | bytes 2097152 | tf_op jit(solution)/shard_map/own_state/pallas_call | solution.py:299
  7.6 2.9 %collective-permute-start.1 = (f32[4,136,128]{2,1,0:T(8,128)S(1)}, f32[4,136,128]{2,1,0:T(8,128)S(1)}, u32[]{:S(2)}, u32[]{:S(2)}) collective-permute-start(f32[4,136,128]{2,1,0:T(8,128)S(1)} %get-tuple-element.100.refs_1_), channel_id=1, source_target_pairs={{0,8},{4,12},{8,0},{12,4},{16,24},{20,28},{24,16},{28,20},{1,9},{5... | collective-permute-start | bytes 835592 | tf_op jit(solution)/shard_map/ppermute | solution.py:706
  10.5 1.5 %collective-permute-start.2 = (f32[4,128,128]{2,1,0:T(8,128)S(1)}, f32[4,128,128]{2,1,0:T(8,128)S(1)}, u32[]{:S(2)}, u32[]{:S(2)}) collective-permute-start(f32[4,128,128]{2,1,0:T(8,128)S(1)} %get-tuple-element.101.refs_5_), channel_id=1, source_target_pairs={{0,16},{4,20},{8,24},{12,28},{16,0},{20,4},{24,8},{28,12},{1,17},{... | collective-permute-start | bytes 786440 | tf_op jit(solution)/shard_map/ppermute | solution.py:706
  12.0 3.8 %intra_0.1 = (bf16[16,256,128]{2,1,0:T(8,128)(2,1)S(1)}, bf16[16,256,128]{2,1,0:T(8,128)(2,1)S(1)}, bf16[16,256,256]{2,1,0:T(8,128)(2,1)S(1)}, f32[16,3,128,128]...) custom-call(f32[8,128]{1,0:T(8,128)S(1)} %broadcast_in_dim.2.place_r, ...), custom_call_target="tpu_custom_call" | custom-call | flops 1073741824 | bytes 10485760 | tf_op jit(solution)/shard_map/intra_0/pallas_call | solution.py:347
  15.8 2.9 %collective-permute-done.3.refs_3_ = f32[8,128]{1,0:T(8,128)S(1)} collective-permute-done((f32[8,128]{1,0:T(8,128)S(1)}, f32[8,128]{1,0:T(8,128)S(1)}, u32[]{:S(2)}, u32[]{:S(2)}) %collective-permute-start.3) | collective-permute-done | bytes 4128 | tf_op jit(solution)/shard_map/ppermute | solution.py:706
  18.8 1.6 %collective-permute-start.5 = (f32[4,128,128]{2,1,0:T(8,128)S(1)}, f32[4,128,128]{2,1,0:T(8,128)S(1)}, u32[]{:S(2)}, u32[]{:S(2)}) collective-permute-start(f32[4,128,128]{2,1,0:T(8,128)S(1)} %get-tuple-element.114), channel_id=1, source_target_pairs={{0,8},{4,12},{8,0},{12,4},{16,24},{20,28},{24,16},{28,20},{1,9},{5... | collective-permute-start | bytes 786440 | tf_op jit(solution)/shard_map/ppermute | solution.py:706
  20.4 0.5 collective-permute-start.4
  20.9 3.9 %intra_1.1 = (bf16[16,256,128]{2,1,0:T(8,128)(2,1)S(1)}, bf16[16,256,128]{2,1,0:T(8,128)(2,1)S(1)}, bf16[16,256,256]{2,1,0:T(8,128)(2,1)S(1)}, f32[16,3,128,128]...) custom-call(f32[8,128]{1,0:T(8,128)S(1)} %broadcast_in_dim.2.place_ref, ...), custom_call_target="tpu_custom_call" | custom-call | flops 1073741824 | bytes 10485760 | tf_op jit(solution)/shard_map/intra_1/pallas_call | solution.py:347
  24.8 1.4 %collective-permute-done.5.refs_6_ = f32[4,128,128]{2,1,0:T(8,128)S(1)} collective-permute-done((f32[4,128,128]{2,1,0:T(8,128)S(1)}, f32[4,128,128]{2,1,0:T(8,128)S(1)}, u32[]{:S(2)}, u32[]{:S(2)}) %collective-permute-start.5) | collective-permute-done | bytes 262176 | tf_op jit(solution)/shard_map/ppermute | solution.py:706
  26.1 1.2 %collective-permute-done.4.refs_5_ = f32[4,128,128]{2,1,0:T(8,128)S(1)} collective-permute-done((f32[4,128,128]{2,1,0:T(8,128)S(1)}, f32[4,128,128]{2,1,0:T(8,128)S(1)}, u32[]{:S(2)}, u32[]{:S(2)}) %collective-permute-start.4) | collective-permute-done | bytes 262176 | tf_op jit(solution)/shard_map/ppermute | solution.py:706
  27.6 1.0 %attend_0.1 = (f32[8,256,128]{2,1,0:T(8,128)S(1)}, f32[8,256,128]{2,1,0:T(8,128)S(1)}, f32[2,2,256,128]{3,2,1,0:T(8,128)S(1)}) custom-call(f32[16,128]{1,0:T(8,128)S(1)} %get-tuple-element.91.refs_0_.gain_ref, f32[8,128,128]{2,1,0:T(8,128)S(1)} %get-tuple-element.122.refs_1_.keep_ref, bf16[16,256,128]{2,1,0:T(8,128)(2,1)S(1)} %get-tuple-element.132.refs_2_.q0, ...), custom_call_target="tpu_custom_call" | custom-call | flops 268435456 | bytes 8388608 | tf_op jit(solution)/shard_map/attend_0/pallas_call | solution.py:408
  28.6 0.9 %collective-permute-done.6.refs_1_.recv_ref = f32[8,128,128]{2,1,0:T(8,128)S(1)} collective-permute-done((f32[8,128,128]{2,1,0:T(8,128)S(1)}, f32[8,128,128]{2,1,0:T(8,128)S(1)}, u32[]{:S(2)}, u32[]{:S(2)}) %collective-permute-start.6) | collective-permute-done | bytes 524320 | tf_op jit(solution)/shard_map/ppermute | solution.py:706
  29.5 1.4 %attend_1.1 = (f32[8,256,128]{2,1,0:T(8,128)S(1)}, f32[8,256,128]{2,1,0:T(8,128)S(1)}, f32[2,512]{1,0:T(2,128)S(1)}) custom-call(f32[16,128]{1,0:T(8,128)S(1)} %get-tuple-element.91.refs_0_.gain_ref, f32[8,128,128]{2,1,0:T(8,128)S(1)} %collective-permute-done.6.refs_1_.recv_ref, bf16[16,256,128]{2,1,0:T(8,128)(2,1)S(1)} %get-tuple-element.132.refs_2_.q0, ...), custom_call_target="tpu_custom_call" | custom-call | flops 268435456 | bytes 8388608 | tf_op jit(solution)/shard_map/attend_1/pallas_call | solution.py:408
  30.9 1.6 %collective-permute-start.7 = (f32[2,512]{1,0:T(2,128)S(1)}, f32[2,512]{1,0:T(2,128)S(1)}, u32[]{:S(2)}, u32[]{:S(2)}) collective-permute-start(f32[2,512]{1,0:T(2,128)S(1)} %get-tuple-element.131.first_ref), channel_id=1, source_target_pairs={{0,1},{1,0},{2,3},{3,2},{4,5},{5,4},{6,7},{7,6},{8,9},{9,8},{10,11... | collective-permute-start | bytes 12296 | tf_op jit(solution)/shard_map/ppermute | solution.py:706
  32.5 0.9 %scaled_queries.1 = (bf16[2,16,128,256]{3,2,1,0:T(8,128)(2,1)S(1)}, f32[2,16,128]{2,1,0:T(8,128)S(1)}) custom-call(f32[2,16,256]{2,1,0:T(8,128)S(1)} %get-tuple-element.136.cum.cum_ref, bf16[16,256,128]{2,1,0:T(8,128)(2,1)S(1)} %get-tuple-element.132.refs_2_.q0, bf16[16,256,128]{2,1,0:T(8,128)(2,1)S(1)} %get-tuple-element.118.refs_3_.q1), custom_call_target="tpu_custom_call" | custom-call | flops 2097152 | bytes 4194304 | tf_op jit(solution)/shard_map/scaled_queries/pallas_call | solution.py:434
  33.4 1.1 %collective-permute-done.7.second_ref = f32[2,512]{1,0:T(2,128)S(1)} collective-permute-done((f32[2,512]{1,0:T(2,128)S(1)}, f32[2,512]{1,0:T(2,128)S(1)}, u32[]{:S(2)}, u32[]{:S(2)}) %collective-permute-start.7) | collective-permute-done | bytes 4128 | tf_op jit(solution)/shard_map/ppermute | solution.py:706
  34.5 2.6 %collective-permute-start.8 = (f32[2,512]{1,0:T(2,128)S(1)}, f32[2,512]{1,0:T(2,128)S(1)}, u32[]{:S(2)}, u32[]{:S(2)}) collective-permute-start(f32[2,512]{1,0:T(2,128)S(1)} %add.15.first_ref), channel_id=1, source_target_pairs={{0,2},{1,3},{2,0},{3,1},{4,6},{5,7},{6,4},{7,5},{8,10},{9,11},{10,... | collective-permute-start | bytes 12296 | tf_op jit(solution)/shard_map/ppermute | solution.py:706
  37.1 1.8 %remaining_decay.1.remaining_ref.refs_4_ = f32[2,16,256,128]{3,2,1,0:T(8,128)S(1)} custom-call(f32[2,16,256]{2,1,0:T(8,128)S(1)} %get-tuple-element.136.cum.cum_ref), custom_call_target="tpu_custom_call" | custom-call | flops 1048576 | bytes 4194304 | tf_op jit(solution)/shard_map/remaining_decay/pallas_call | solution.py:456
  39.0 0.8 %norm_grad_1.1 = (f32[8,128,128]{2,1,0:T(8,128)S(1)}, f32[8,128,128]{2,1,0:T(8,128)S(1)}, bf16[8,256,128]{2,1,0:T(8,128)(2,1)S(1)}, bf16[8,256,128]{2,1,0:T(8,128)(2,1)S(1)}) custom-call(f32[2,16,128]{2,1,0:T(8,128)S(1)} %get-tuple-element.146.ends_ref.refs_0_, f32[16,128]{1,0:T(8,128)S(1)} %get-tuple-element.91.refs_0_.gain_ref, ...), custom_call_target="tpu_custom_call" | custom-call | flops 134217728 | bytes 7340032 | tf_op jit(solution)/shard_map/norm_grad_1/pallas_call | solution.py:501
  39.9 0.8 %norm_grad_0.1 = (f32[8,128,128]{2,1,0:T(8,128)S(1)}, f32[8,128,128]{2,1,0:T(8,128)S(1)}, bf16[8,256,128]{2,1,0:T(8,128)(2,1)S(1)}, bf16[8,256,128]{2,1,0:T(8,128)(2,1)S(1)}) custom-call(f32[2,16,128]{2,1,0:T(8,128)S(1)} %get-tuple-element.146.ends_ref.refs_0_, f32[16,128]{1,0:T(8,128)S(1)} %get-tuple-element.91.refs_0_.gain_ref, ...), custom_call_target="tpu_custom_call" | custom-call | flops 134217728 | bytes 7340032 | tf_op jit(solution)/shard_map/norm_grad_0/pallas_call | solution.py:501
  40.7 1.1 %collective-permute-done.9.refs_2_ = f32[8,128,128]{2,1,0:T(8,128)S(1)} collective-permute-done((f32[8,128,128]{2,1,0:T(8,128)S(1)}, f32[8,128,128]{2,1,0:T(8,128)S(1)}, u32[]{:S(2)}, u32[]{:S(2)}) %collective-permute-start.9) | collective-permute-done | bytes 524320 | tf_op jit(solution)/shard_map/ppermute | solution.py:706
  41.9 0.6 collective-permute-start.10
  42.5 1.4 %collective-permute-start.11 = (f32[4,128,128]{2,1,0:T(8,128)S(1)}, f32[4,128,128]{2,1,0:T(8,128)S(1)}, u32[]{:S(2)}, u32[]{:S(2)}) collective-permute-start(f32[4,128,128]{2,1,0:T(8,128)S(1)} %get-tuple-element.145.refs_1_), channel_id=1, source_target_pairs={{0,16},{4,20},{8,24},{12,28},{16,0},{20,4},{24,8},{28,12},{1,17},{... | collective-permute-start | bytes 786440 | tf_op jit(solution)/shard_map/ppermute | solution.py:706
  43.9 6.2 %grad_query.1 = (bf16[2,16,256,256]{3,2,1,0:T(8,128)(2,1)S(1)}, bf16[512,16,128]{2,1,0:T(8,128)(2,1)}) custom-call(f32[8,128]{1,0:T(8,128)S(1)} %broadcast_in_dim.2.place_ref, f32[2,16,128]{2,1,0:T(8,128)S(1)} %get-tuple-element.146.ends_ref.refs_0_, f32[8,128,128]{2,1,0:T(8,128)S(1)} %get-tuple-element.122.refs_1_.keep_ref, ...), custom_call_target="tpu_custom_call" | custom-call | flops 1610612736 | bytes 12582912 | tf_op jit(solution)/shard_map/grad_query/pallas_call | solution.py:554
  50.7 1.6 %collective-permute-start.13 = (f32[4,128,128]{2,1,0:T(8,128)S(1)}, f32[4,128,128]{2,1,0:T(8,128)S(1)}, u32[]{:S(2)}, u32[]{:S(2)}) collective-permute-start(f32[4,128,128]{2,1,0:T(8,128)S(1)} %later_column.1), channel_id=1, source_target_pairs={{0,8},{4,12},{8,0},{12,4},{16,24},{20,28},{24,16},{28,20},{1,9},{5... | collective-permute-start | bytes 786440 | tf_op jit(solution)/shard_map/ppermute | solution.py:706
  52.2 0.8 %collective-permute-start.12 = (f32[4,128,128]{2,1,0:T(8,128)S(1)}, f32[4,128,128]{2,1,0:T(8,128)S(1)}, u32[]{:S(2)}, u32[]{:S(2)}) collective-permute-start(f32[4,128,128]{2,1,0:T(8,128)S(1)} %later_row.1), channel_id=1, source_target_pairs={{0,16},{4,20},{8,24},{12,28},{16,0},{20,4},{24,8},{28,12},{1,17},{... | collective-permute-start | bytes 786440 | tf_op jit(solution)/shard_map/ppermute | solution.py:706
  53.0 5.8 %grad_key_value.1 = (f32[2,16,256,128]{3,2,1,0:T(8,128)S(1)}, f32[2,16,256,128]{3,2,1,0:T(8,128)S(1)}, bf16[512,16,128]{2,1,0:T(8,128)(2,1)}) custom-call(f32[8,128]{1,0:T(8,128)S(1)} %broadcast_in_dim.2.place_ref, f32[16,128]{1,0:T(8,128)S(1)} %get-tuple-element.91.refs_0_.gain_ref, f32[2,512]{1,0:T(2,128)S(1)} %add.16.sums_ref, ...), custom_call_target="tpu_custom_call" | custom-call | flops 1610612736 | bytes 31457280 | tf_op jit(solution)/shard_map/grad_key_value/pallas_call | solution.py:604
  59.4 0.9 %finish_own.1 = (f32[2,16,256,128]{3,2,1,0:T(8,128)S(1)}, f32[2,16,256,128]{3,2,1,0:T(8,128)S(1)}) custom-call(f32[2,16,128]{2,1,0:T(8,128)S(1)} %get-tuple-element.146.ends_ref.refs_0_, f32[8,128,128]{2,1,0:T(8,128)S(1)} %get-tuple-element.168.refs_1_, bf16[2,16,256,128]{3,2,1,0:T(8,128)(2,1)S(1)} %get-tuple-element.94.kh.refs_2_, ...), custom_call_target="tpu_custom_call" | custom-call | flops 536870912 | bytes 8388608 | tf_op jit(solution)/shard_map/finish_own/pallas_call | solution.py:668
  60.3 1.0 %collective-permute-done.14.state_ref = f32[8,128,128]{2,1,0:T(8,128)S(1)} collective-permute-done((f32[8,128,128]{2,1,0:T(8,128)S(1)}, f32[8,128,128]{2,1,0:T(8,128)S(1)}, u32[]{:S(2)}, u32[]{:S(2)}) %collective-permute-start.14) | collective-permute-done | bytes 524320 | tf_op jit(solution)/shard_map/ppermute | solution.py:706
  61.3 3.7 %finish_other.1 = (bf16[512,16,128]{2,1,0:T(8,128)(2,1)}, bf16[512,16,128]{2,1,0:T(8,128)(2,1)}, f32[2,16,256,128]{3,2,1,0:T(8,128)S(1)}, f32[2,16,256,128]{3,2,1,0:T(8,128)S(1)}) custom-call(f32[8,128]{1,0:T(8,128)S(1)} %broadcast_in_dim.2.place_ref, ...), custom_call_target="tpu_custom_call", output_to_operand_aliasing={{2}: (1, {}), {3}: (2, {})} | custom-call | flops 536870912 | bytes 8388608 | tf_op jit(solution)/shard_map/finish_other/pallas_call | solution.py:683
  (26 shorter events, 2.1 us)
Async XLA Ops:
  5.3 2.1 %collective-permute-start = (f32[8,136,128]{2,1,0:T(8,128)S(1)}, f32[8,136,128]{2,1,0:T(8,128)S(1)}, u32[]{:S(2)}, u32[]{:S(2)}) collective-permute-start(f32[8,136,128]{2,1,0:T(8,128)S(1)} %get-tuple-element.93), channel_id=1, source_target_pairs={{0,4},{4,0},{8,12},{12,8},{16,20},{20,16},{24,28},{28,24},{1,5},{5... | collective-permute-start | bytes 1671176 | tf_op jit(solution)/shard_map/ppermute | solution.py:706
  7.6 11.2 %collective-permute-start.1 = (f32[4,136,128]{2,1,0:T(8,128)S(1)}, f32[4,136,128]{2,1,0:T(8,128)S(1)}, u32[]{:S(2)}, u32[]{:S(2)}) collective-permute-start(f32[4,136,128]{2,1,0:T(8,128)S(1)} %get-tuple-element.100.refs_1_), channel_id=1, source_target_pairs={{0,8},{4,12},{8,0},{12,4},{16,24},{20,28},{24,16},{28,20},{1,9},{5... | collective-permute-start | bytes 835592 | tf_op jit(solution)/shard_map/ppermute | solution.py:706
  10.5 8.2 %collective-permute-start.2 = (f32[4,128,128]{2,1,0:T(8,128)S(1)}, f32[4,128,128]{2,1,0:T(8,128)S(1)}, u32[]{:S(2)}, u32[]{:S(2)}) collective-permute-start(f32[4,128,128]{2,1,0:T(8,128)S(1)} %get-tuple-element.101.refs_5_), channel_id=1, source_target_pairs={{0,16},{4,20},{8,24},{12,28},{16,0},{20,4},{24,8},{28,12},{1,17},{... | collective-permute-start | bytes 786440 | tf_op jit(solution)/shard_map/ppermute | solution.py:706
  12.0 6.7 %collective-permute-start.3 = (f32[8,128]{1,0:T(8,128)S(1)}, f32[8,128]{1,0:T(8,128)S(1)}, u32[]{:S(2)}, u32[]{:S(2)}) collective-permute-start(f32[8,128]{1,0:T(8,128)S(1)} %get-tuple-element.99.refs_0_.refs_2_), channel_id=1, source_target_pairs={{0,24},{4,28},{8,16},{12,20},{16,8},{20,12},{24,0},{28,4},{1,25},{... | collective-permute-start | bytes 12296 | tf_op jit(solution)/shard_map/ppermute | solution.py:706
  18.8 7.3 %collective-permute-start.5 = (f32[4,128,128]{2,1,0:T(8,128)S(1)}, f32[4,128,128]{2,1,0:T(8,128)S(1)}, u32[]{:S(2)}, u32[]{:S(2)}) collective-permute-start(f32[4,128,128]{2,1,0:T(8,128)S(1)} %get-tuple-element.114), channel_id=1, source_target_pairs={{0,8},{4,12},{8,0},{12,4},{16,24},{20,28},{24,16},{28,20},{1,9},{5... | collective-permute-start | bytes 786440 | tf_op jit(solution)/shard_map/ppermute | solution.py:706
  20.4 6.9 %collective-permute-start.4 = (f32[4,128,128]{2,1,0:T(8,128)S(1)}, f32[4,128,128]{2,1,0:T(8,128)S(1)}, u32[]{:S(2)}, u32[]{:S(2)}) collective-permute-start(f32[4,128,128]{2,1,0:T(8,128)S(1)} %earlier_row.1), channel_id=1, source_target_pairs={{0,16},{4,20},{8,24},{12,28},{16,0},{20,4},{24,8},{28,12},{1,17},{... | collective-permute-start | bytes 786440 | tf_op jit(solution)/shard_map/ppermute | solution.py:706
  27.5 2.0 %collective-permute-start.6 = (f32[8,128,128]{2,1,0:T(8,128)S(1)}, f32[8,128,128]{2,1,0:T(8,128)S(1)}, u32[]{:S(2)}, u32[]{:S(2)}) collective-permute-start(f32[8,128,128]{2,1,0:T(8,128)S(1)} %get-tuple-element.121), channel_id=1, source_target_pairs={{0,4},{4,0},{8,12},{12,8},{16,20},{20,16},{24,28},{28,24},{1,5},{5... | collective-permute-start | bytes 1572872 | tf_op jit(solution)/shard_map/ppermute | solution.py:706
  30.9 3.6 %collective-permute-start.7 = (f32[2,512]{1,0:T(2,128)S(1)}, f32[2,512]{1,0:T(2,128)S(1)}, u32[]{:S(2)}, u32[]{:S(2)}) collective-permute-start(f32[2,512]{1,0:T(2,128)S(1)} %get-tuple-element.131.first_ref), channel_id=1, source_target_pairs={{0,1},{1,0},{2,3},{3,2},{4,5},{5,4},{6,7},{7,6},{8,9},{9,8},{10,11... | collective-permute-start | bytes 12296 | tf_op jit(solution)/shard_map/ppermute | solution.py:706
  34.5 4.5 %collective-permute-start.8 = (f32[2,512]{1,0:T(2,128)S(1)}, f32[2,512]{1,0:T(2,128)S(1)}, u32[]{:S(2)}, u32[]{:S(2)}) collective-permute-start(f32[2,512]{1,0:T(2,128)S(1)} %add.15.first_ref), channel_id=1, source_target_pairs={{0,2},{1,3},{2,0},{3,1},{4,6},{5,7},{6,4},{7,5},{8,10},{9,11},{10,... | collective-permute-start | bytes 12296 | tf_op jit(solution)/shard_map/ppermute | solution.py:706
  39.8 2.0 %collective-permute-start.9 = (f32[8,128,128]{2,1,0:T(8,128)S(1)}, f32[8,128,128]{2,1,0:T(8,128)S(1)}, u32[]{:S(2)}, u32[]{:S(2)}) collective-permute-start(f32[8,128,128]{2,1,0:T(8,128)S(1)} %get-tuple-element.142), channel_id=1, source_target_pairs={{0,4},{4,0},{8,12},{12,8},{16,20},{20,16},{24,28},{28,24},{1,5},{5... | collective-permute-start | bytes 1572872 | tf_op jit(solution)/shard_map/ppermute | solution.py:706
  41.9 8.4 %collective-permute-start.10 = (f32[4,128,128]{2,1,0:T(8,128)S(1)}, f32[4,128,128]{2,1,0:T(8,128)S(1)}, u32[]{:S(2)}, u32[]{:S(2)}) collective-permute-start(f32[4,128,128]{2,1,0:T(8,128)S(1)} %get-tuple-element.157.refs_1_), channel_id=1, source_target_pairs={{0,8},{4,12},{8,0},{12,4},{16,24},{20,28},{24,16},{28,20},{1,9},{5... | collective-permute-start | bytes 786440 | tf_op jit(solution)/shard_map/ppermute | solution.py:706
  42.5 8.1 %collective-permute-start.11 = (f32[4,128,128]{2,1,0:T(8,128)S(1)}, f32[4,128,128]{2,1,0:T(8,128)S(1)}, u32[]{:S(2)}, u32[]{:S(2)}) collective-permute-start(f32[4,128,128]{2,1,0:T(8,128)S(1)} %get-tuple-element.145.refs_1_), channel_id=1, source_target_pairs={{0,16},{4,20},{8,24},{12,28},{16,0},{20,4},{24,8},{28,12},{1,17},{... | collective-permute-start | bytes 786440 | tf_op jit(solution)/shard_map/ppermute | solution.py:706
  50.7 8.1 %collective-permute-start.13 = (f32[4,128,128]{2,1,0:T(8,128)S(1)}, f32[4,128,128]{2,1,0:T(8,128)S(1)}, u32[]{:S(2)}, u32[]{:S(2)}) collective-permute-start(f32[4,128,128]{2,1,0:T(8,128)S(1)} %later_column.1), channel_id=1, source_target_pairs={{0,8},{4,12},{8,0},{12,4},{16,24},{20,28},{24,16},{28,20},{1,9},{5... | collective-permute-start | bytes 786440 | tf_op jit(solution)/shard_map/ppermute | solution.py:706
  52.2 6.9 %collective-permute-start.12 = (f32[4,128,128]{2,1,0:T(8,128)S(1)}, f32[4,128,128]{2,1,0:T(8,128)S(1)}, u32[]{:S(2)}, u32[]{:S(2)}) collective-permute-start(f32[4,128,128]{2,1,0:T(8,128)S(1)} %later_row.1), channel_id=1, source_target_pairs={{0,16},{4,20},{8,24},{12,28},{16,0},{20,4},{24,8},{28,12},{1,17},{... | collective-permute-start | bytes 786440 | tf_op jit(solution)/shard_map/ppermute | solution.py:706
  59.3 2.0 %collective-permute-start.14 = (f32[8,128,128]{2,1,0:T(8,128)S(1)}, f32[8,128,128]{2,1,0:T(8,128)S(1)}, u32[]{:S(2)}, u32[]{:S(2)}) collective-permute-start(f32[8,128,128]{2,1,0:T(8,128)S(1)} %get-tuple-element.172), channel_id=1, source_target_pairs={{0,4},{4,0},{8,12},{12,8},{16,20},{20,16},{24,28},{28,24},{1,5},{5... | collective-permute-start | bytes 1572872 | tf_op jit(solution)/shard_map/ppermute | solution.py:706
